TPU v7x, 32 devices: a whole 2x2x4 slice. The times are simulated.
32 devices in a mesh: fsdp: 8 (over z, x), factor: 4 (over y, core).
Axes of the slice: x: 2, y: 2, z: 4, core: 2. Of those that a mesh axis runs over, the one named last changes fastest.
Arguments:
- activations: bfloat16 [32, 16, 16, 512], P(('fsdp', 'factor')), may hold values from -12 to 12
- cotangent: bfloat16 [32, 16, 16, 512], P(('fsdp', 'factor')), may hold values from -0.6684369 to 0.6684369
- weight: bfloat16 [4608, 512], P('fsdp'), may hold values from -0.09375 to 0.09375
- a_factor_old: float32 [4608, 4608], P('factor', 'fsdp'), may hold values from -0.11785113 to 5, as said below
- g_factor_old: float32 [512, 512], P('factor'), may hold values from -0.35355339 to 5, as said below
- a_inverse: float32 [4608, 4608], P('fsdp', 'factor'), may hold values from -0.09375 to 0.09375
- g_inverse: float32 [512, 512], replicated, may hold values from -0.25 to 0.25
Outputs:
- conv_out: bfloat16 [32, 16, 16, 512], P(('fsdp', 'factor'))
- a_factor: float32 [4608, 4608], P('factor', 'fsdp')
- g_factor: float32 [512, 512], P('factor')
- natural_grad: bfloat16 [4608, 512], P('fsdp', 'factor')
Inputs may be any that keep to these rules, and one draw needn't show every extreme that they name: `a_factor_old`: a symmetric matrix. `g_factor_old`: a symmetric matrix.
All inputs are finite; a program needn't handle non-finite values.
Results may differ from a plain program's by a relative error of at most 0.0017.
Values may be sent and summed in bfloat16 or wider, within the bound.
No kernel may reach another device: no remote copies, remote signals or barrier semaphores. Data moves between devices by JAX's collectives and lax.ppermute only.
A program may use at most 192 MiB of HBM per device.

v0:
```python
import jax
import jax.numpy as jnp
from jax import lax
from jax.sharding import PartitionSpec as P


def unfold(images):
    side = images.shape[1]
    padded = jnp.pad(images, ((0, 0), (1, 1), (1, 1), (0, 0)))
    tap_list = [
        padded[:, row_off : row_off + side, col_off : col_off + side, :]
        for row_off in range(3)
        for col_off in range(3)
    ]
    return jnp.concatenate(tap_list, axis=3).reshape(-1, 9 * images.shape[3])


def contract(first_op, second_op):
    return lax.dot_general(
        first_op, second_op, (((0,), (0,)), ((), ())), preferred_element_type=jnp.float32
    )


def per_device(activations, cotangent, weight, a_factor_old, g_factor_old, a_inverse, g_inverse):
    channels = activations.shape[3]
    own_patches = unfold(activations)
    own_cot = cotangent.reshape(-1, channels)
    factor_index = lax.axis_index("factor")
    rows_per = a_factor_old.shape[0]
    row_start = factor_index * rows_per
    conv_total = jnp.dot(
        own_patches,
        lax.all_gather(weight, "fsdp", axis=0, tiled=True),
        preferred_element_type=jnp.float32,
    )
    conv_out = conv_total.astype(jnp.bfloat16).reshape(activations.shape)
    patches = unfold(lax.all_gather(activations, "factor", axis=0, tiled=True))
    a_partial = contract(lax.dynamic_slice_in_dim(patches, row_start, rows_per, 1), patches)
    grad_partial = lax.psum_scatter(
        contract(own_patches, own_cot), "factor", scatter_dimension=0, tiled=True
    )
    a_summed = lax.psum_scatter(a_partial, "fsdp", scatter_dimension=1, tiled=True)
    pixel_total = float(
        activations.shape[1]
        * activations.shape[2]
        * lax.axis_size("fsdp")
        * lax.axis_size("factor")
    )
    a_factor = 0.5 * a_factor_old + 0.5 * (a_summed / pixel_total)
    grad_rows = lax.psum(grad_partial, "fsdp")
    g_partial = contract(own_cot, own_cot)
    g_rows_count = g_factor_old.shape[0]
    g_summed = lax.psum(g_partial, ("fsdp", "factor"))
    g_rows = lax.dynamic_slice_in_dim(g_summed, factor_index * g_rows_count, g_rows_count, 0)
    g_factor = 0.5 * g_factor_old + 0.5 * g_rows
    mixed = jnp.dot(
        grad_rows, g_inverse, precision=lax.Precision.HIGHEST, preferred_element_type=jnp.float32
    )
    partial_rows = jnp.dot(
        a_inverse, mixed, precision=lax.Precision.HIGHEST, preferred_element_type=jnp.float32
    )
    summed_rows = lax.psum(partial_rows, "factor")
    tile_width = channels // lax.axis_size("factor")
    result_tile = lax.dynamic_slice_in_dim(summed_rows, factor_index * tile_width, tile_width, 1)
    return (conv_out, a_factor, g_factor, result_tile.astype(jnp.bfloat16))


def solution(mesh):
    return jax.shard_map(
        per_device,
        mesh=mesh,
        in_specs=(
            P(("fsdp", "factor"), None, None, None),
            P(("fsdp", "factor"), None, None, None),
            P("fsdp", None),
            P("factor", "fsdp"),
            P("factor", None),
            P("fsdp", "factor"),
            P(),
        ),
        out_specs=(
            P(("fsdp", "factor"), None, None, None),
            P("factor", "fsdp"),
            P("factor", None),
            P("fsdp", "factor"),
        ),
        check_vma=False,
    )
```

profile of v0, /device:TPU:0, one launch (start us, length us, event | category | flops | bytes accessed | tf_op | source)
XLA Modules:
  0.0 700.0 jit_solution(12300978903634027714)
XLA Ops:
  8.0 0.0 copy-start
  8.0 0.0 copy-start.3
  8.0 0.0 all-gather.5.cloned.1.call-start
  8.1 0.7 all-gather.5.cloned.1.call-update
  8.8 0.0 copy-start.6
  8.8 0.0 reduce-scatter.5.cloned.1.call-start
  8.8 1.1 fusion.11
  10.0 1.0 fusion.12
  10.9 1.0 fusion.13
  12.0 1.0 fusion.14
  13.0 0.0 copy-done.3
  13.0 0.1 fusion.15
  13.1 0.1 fusion.16
  13.2 0.1 fusion.18
  13.3 0.0 copy-start.5
  13.3 1.4 copy-done.5
  14.7 0.0 copy-done.6
  14.7 5.1 convolution_bitcast_fusion
  19.7 0.0 reduce-scatter.5.cloned.1.call-update
  19.8 0.0 all-reduce.6.cloned.1.call-start
  19.8 1.4 convolution_bitcast_fusion.2
  21.2 0.0 all-reduce.6.cloned.1.call-update
  21.2 0.0 all-gather.3.cloned.1.call-start
  21.3 0.7 all-gather.3.cloned.1.call-update
  21.9 0.0 all-reduce.8.cloned.1.call-start
  22.0 7.9 %all-gather.5.cloned.1.call-done = bf16[4,16,16,512]{3,2,1,0:T(8,128)(2,1)} async-done(((bf16[1,16,16,512]{3,2,1,0:T(8,128)(2,1)}), bf16[4,16,16,512]{3,2,1,0:T(8,128)(2,1)}) %all-gather.5.cloned.1.call-update) | async-done | bytes 1048592 | tf_op jit(solution)/shard_map/all_gather | solution.py:37
  29.9 0.0 copy-start.1
  29.9 2.6 fusion.3
  32.5 0.0 copy-done.1
  32.5 1.2 fusion.4
  33.7 1.4 fusion.5
  35.1 1.4 fusion.6
  36.5 75.4 %reduce-scatter.5.cloned.1.call-done = f32[1152,512]{1,0:T(8,128)} async-done(((f32[4608,512]{1,0:T(8,128)}), f32[1152,512]{1,0:T(8,128)}) %reduce-scatter.5.cloned.1.call-update) | async-done | bytes 2359312 | tf_op jit(solution)/shard_map/reduce_scatter | solution.py:39
  111.9 0.0 all-reduce.8.cloned.1.call-update
  111.9 0.0 reduce-scatter.3.cloned.1.call-start
  112.0 0.0 copy-start.2
  112.0 2.4 constant_dynamic-update-slice_fusion.1
  114.4 0.0 copy-done.2
  114.4 1.4 fusion.7
  115.8 1.5 fusion.8
  117.3 1.1 fusion.9
  118.4 1.4 fusion.10
  119.8 20.1 %fusion.1 = f32[1152,4608]{0,1:T(8,128)} fusion(bf16[1024,4608]{1,0:T(8,128)(2,1)} %bitcast.2, s32[]{:T(128)S(6)} %select_n.7), kind=kOutput, calls=%fused_computation.11 | convolution fusion | flops 10871635968 | bytes 33030148 | tf_op jit(solution)/shard_map/dot_general | solution.py:19
  139.9 0.0 copy-start.4
  139.9 0.0 reduce-scatter.3.cloned.1.call-update
  139.9 88.3 %all-reduce.6.cloned.1.call-done = f32[512,512]{1,0:T(8,128)} async-done(((f32[512,512]{1,0:T(8,128)}), f32[512,512]{1,0:T(8,128)}) %all-reduce.6.cloned.1.call-update) | async-done | bytes 1048592 | tf_op jit(solution)/shard_map/psum | solution.py:53
  228.2 0.0 copy-done.4
  228.2 1.7 add_multiply_fusion
  229.9 0.0 all-gather.3.cloned.1.call-done
  229.9 5.1 convolution_convert_fusion
  235.0 104.3 %all-reduce.8.cloned.1.call-done = f32[1152,512]{1,0:T(8,128)} async-done(((f32[1152,512]{1,0:T(8,128)}), f32[1152,512]{1,0:T(8,128)}) %all-reduce.8.cloned.1.call-update) | async-done | bytes 2359312 | tf_op jit(solution)/shard_map/psum | solution.py:50
  339.3 5.9 fusion.22
  345.2 0.0 copy-done
  345.2 5.9 convolution_bitcast_fusion.1
  351.1 27.7 %all-reduce.9 = bf16[576,512]{1,0:T(8,128)(2,1)S(1)} all-reduce(f32[576,512]{1,0:T(8,128)} %convolution_bitcast_fusion.1), channel_id=1, replica_groups=mesh['fsdp'=8,'factor'=4] {'factor'}, use_global_device_ids=true, to_apply=%region_4.5 | all-reduce | flops 294912 | bytes 1769472 | tf_op jit(solution)/shard_map/psum | solution.py:62
  378.8 0.7 dynamic-slice_convert_fusion
  379.5 308.9 %reduce-scatter.3.cloned.1.call-done = f32[1152,576]{0,1:T(8,128)} async-done(((f32[1152,4608]{0,1:T(8,128)}), f32[1152,576]{0,1:T(8,128)}) %reduce-scatter.3.cloned.1.call-update) | async-done | bytes 2654224 | tf_op jit(solution)/shard_map/reduce_scatter | solution.py:42
  688.3 4.3 multiply_add_fusion
  (2 shorter events, 0.0 us)
Async XLA Ops:
  8.0 337.2 %copy-start = (f32[576,1152]{1,0:T(8,128)S(1)}, f32[576,1152]{1,0:T(8,128)}, u32[]{:S(2)}) copy-start(f32[576,1152]{1,0:T(8,128)} %param.12) | copy-start | bytes 7962628
  8.0 5.0 copy-start.3
  8.0 21.9 %all-gather.5.cloned.1.call-start = ((), (), s32[]{:S(2)}) async-start(), calls=%async_computation.3 | async-start | bytes 1310720 | tf_op jit(solution)/shard_map/all_gather | solution.py:37
  8.8 5.9 copy-start.6
  8.8 103.1 %reduce-scatter.5.cloned.1.call-start = ((), (), s32[]{:S(2)}) async-start(), calls=%async_computation.6 | async-start | bytes 11796480 | tf_op jit(solution)/shard_map/reduce_scatter | solution.py:39
  13.3 1.4 copy-start.5
  19.8 208.4 %all-reduce.6.cloned.1.call-start = ((), (), s32[]{:S(2)}) async-start(), calls=%async_computation.5 | async-start | bytes 2097152 | tf_op jit(solution)/shard_map/psum | solution.py:53
  21.2 208.7 %all-gather.3.cloned.1.call-start = ((), (), s32[]{:S(2)}) async-start(), calls=%async_computation.2 | async-start | bytes 5308416 | tf_op jit(solution)/shard_map/all_gather | solution.py:33
  21.9 317.4 %all-reduce.8.cloned.1.call-start = ((), (), s32[]{:S(2)}) async-start(), calls=%async_computation.7 | async-start | bytes 4718592 | tf_op jit(solution)/shard_map/psum | solution.py:50
  29.9 2.6 copy-start.1
  111.9 576.4 %reduce-scatter.3.cloned.1.call-start = ((), (), s32[]{:S(2)}) async-start(), calls=%async_computation.4 | async-start | bytes 23887872 | tf_op jit(solution)/shard_map/reduce_scatter | solution.py:42
  112.0 2.5 copy-start.2
  139.9 88.3 %copy-start.4 = (f32[128,512]{1,0:T(8,128)S(1)}, f32[128,512]{1,0:T(8,128)}, u32[]{:S(2)}) copy-start(f32[128,512]{1,0:T(8,128)} %param.11) | copy-start | bytes 786436
Sparse Core Ops, SparseCore 0:
  10.4 19.4 all-gather.4
  32.5 79.3 reduce-scatter.4
  114.1 80.4 all-gather.2
Sparse Core Ops, SparseCore 1:
  25.4 202.7 all-reduce.5
  232.1 107.2 all-reduce.7
  343.1 345.2 reduce-scatter.2
where the time goes:
time: 700 us
  waiting for transfers between devices  586 us (84%)
  matrix products  43.4 us (6%)
  blocking collectives  27.7 us (4%)
  local copies, waits for them, and re-layouts  20.9 us (3%)
  between operations  15.6 us (2%)
    reduce_scatter x1, waiting for transfers between devices, per_device(): lax.psum_scatter(a_partial, 'fsdp', scatter_dimension=1, tiled=True)  309 us
    psum x1, waiting for transfers between devices, per_device(): grad_rows = lax.psum(grad_partial, 'fsdp')  104 us
    psum x1, waiting for transfers between devices, per_device(): g_summed = lax.psum(g_partial, ('fsdp', 'factor'))  88.3 us
    reduce_scatter x1, waiting for transfers between devices, per_device(): lax.psum_scatter(contract(own_patches, own_cot), 'factor', scatter_dimens...  75.4 us
    psum x1, blocking collectives, per_device(): summed_rows = lax.psum(partial_rows, 'factor')  27.7 us
    dot_general x3, matrix products, contract(): lax.dot_general(first_op, second_op, (((0,), (0,)), ((), ())), preferred_...  26.5 us
    unnamed x30, local copies, waits for them, and re-layouts  18.8 us
  transfers between devices with their start and end apart: 6, of which 5 were waited for; matrix products, arithmetic and copies ran while one was open for 9% of the time, Pallas kernels for 0%

commit v1 on v0

v1 whole, which is shorter than its diff:
```python
import jax
import jax.numpy as jnp
from jax import lax
from jax.sharding import PartitionSpec as P


def by_rows(first_op, second_op):
    return lax.dot_general(
        first_op, second_op, (((0,), (0,)), ((), ())), preferred_element_type=jnp.float32
    )


def moved(array, axis, target):
    count = lax.axis_size(axis)
    return lax.ppermute(array, axis, [(at, target(at) % count) for at in range(count)])


def tile_of_patches(images, start, width):
    side, channels = images.shape[1], images.shape[3]
    padded = jnp.pad(images, ((0, 0), (1, 1), (1, 1), (0, 0)))
    first_tap, offset = start // channels, start % channels
    rolled = lax.dynamic_slice_in_dim(
        jnp.concatenate([padded, padded], axis=3), offset, channels, 3
    )
    lane = lax.broadcasted_iota(jnp.int32, (1, 1, 1, channels), 3)

    def tap(index):
        index = jnp.minimum(index, 8)
        return lax.dynamic_slice(
            rolled, (0, index // 3, index % 3, 0), (images.shape[0], side, side, channels)
        )

    pieces = []
    for at in range(0, width, channels):
        step = at // channels
        piece = jnp.where(lane < channels - offset, tap(first_tap + step), tap(first_tap + step + 1))
        pieces.append(piece[..., : min(channels, width - at)])
    return jnp.concatenate(pieces, axis=3).reshape(-1, width)


def per_device(activations, cotangent, weight, a_factor_old, g_factor_old, a_inverse, g_inverse):
    channels = activations.shape[3]
    n_fsdp, n_factor = lax.axis_size("fsdp"), lax.axis_size("factor")
    n_layer, n_pair = n_fsdp // 2, n_factor // 2
    fsdp_at, factor_at = lax.axis_index("fsdp"), lax.axis_index("factor")
    core_at, pair_at = factor_at % 2, factor_at // 2
    rows, cols = a_factor_old.shape
    strip = channels // n_fsdp
    block = channels // n_factor

    def over_layer(array, step):
        return moved(array, "fsdp", lambda at: at + 2 * step)

    def over_side(array):
        return moved(array, "fsdp", lambda at: at ^ 1)

    def over_pair(array, step):
        return moved(array, "factor", lambda at: at + 2 * step)

    def over_core(array):
        return moved(array, "factor", lambda at: at ^ 1)

    own_cot = cotangent.reshape(-1, channels)
    strips = lax.all_to_all(
        own_cot.T.reshape(n_fsdp, strip, own_cot.shape[0]), "fsdp", split_axis=0, concat_axis=0
    )
    strips_by_pair = [strips] + [over_pair(strips, step) for step in range(1, n_pair)]

    layers = [activations] + [over_layer(activations, step) for step in range(1, n_layer)]
    cov_pair = jnp.zeros((cols, 2 * rows), jnp.float32)
    grad_pair = jnp.zeros((strip, 2 * rows), jnp.float32)
    group_images = []
    for step, layer in enumerate(layers):
        near = [layer] + [over_pair(layer, pair) for pair in range(1, n_pair)]
        if step % 2 == 0:
            aside = over_side(layer)
            far = [aside] + [over_pair(aside, pair) for pair in range(1, n_pair)]
        else:
            far = [over_side(image) for image in near]
        if step == 0:
            group_images = near
        images = jnp.concatenate(near + far, axis=0)
        row_tile = tile_of_patches(images, pair_at * (2 * rows), 2 * rows)
        col_tile = tile_of_patches(images, fsdp_at * cols, cols)
        owner = (fsdp_at - 2 * step) % n_fsdp
        cot_list = [
            lax.dynamic_index_in_dim(strips_by_pair[pair], which, 0, keepdims=False)
            for which in (owner, owner ^ 1)
            for pair in range(n_pair)
        ]
        cov_pair = cov_pair + by_rows(col_tile, row_tile)
        grad_pair = grad_pair + jnp.dot(
            jnp.concatenate(cot_list, axis=1), row_tile, preferred_element_type=jnp.float32
        )

    def own_half(array):
        halves = array.reshape(array.shape[0], 2, rows)
        mine = lax.dynamic_index_in_dim(halves, core_at, 1, keepdims=False)
        theirs = lax.dynamic_index_in_dim(halves, 1 - core_at, 1, keepdims=False)
        return mine + over_core(theirs)

    grad_own = own_half(grad_pair)
    cov_own = own_half(cov_pair)
    pixel_total = float(
        activations.shape[0] * activations.shape[1] * activations.shape[2] * n_fsdp * n_factor
    )
    a_factor = 0.5 * a_factor_old + (0.5 / pixel_total) * cov_own.T

    grad_layers = [grad_own] + [over_layer(grad_own, step) for step in range(1, n_layer)]
    near_grads = jnp.concatenate(grad_layers, axis=0)
    grad_cols = jnp.concatenate([near_grads, over_side(near_grads)], axis=0)
    came_from = (fsdp_at - 2 * jnp.arange(n_layer)) % n_fsdp
    came_from = jnp.concatenate([came_from, came_from ^ 1])
    inverse_rows = g_inverse.reshape(n_fsdp, strip, channels)[came_from].reshape(channels, channels)
    partial = lax.dot_general(
        a_inverse,
        grad_cols,
        (((1,), (1,)), ((), ())),
        precision=lax.Precision.HIGH,
        preferred_element_type=jnp.float32,
    )
    partial = jnp.dot(
        partial, inverse_rows, precision=lax.Precision.HIGH, preferred_element_type=jnp.float32
    )
    by_block = partial.reshape(-1, n_pair, 2, block)
    mine = lax.dynamic_index_in_dim(by_block, core_at, 2, keepdims=False)
    theirs = lax.dynamic_index_in_dim(by_block, 1 - core_at, 2, keepdims=False)
    by_pair = mine + over_core(theirs)
    result = lax.dynamic_index_in_dim(by_pair, pair_at, 1, keepdims=False)
    for step in range(1, n_pair):
        away = lax.dynamic_index_in_dim(by_pair, (pair_at + step) % n_pair, 1, keepdims=False)
        result = result + over_pair(away, step)
    natural_grad = result.astype(jnp.bfloat16)

    weight_part = lax.dynamic_slice_in_dim(weight, factor_at * block, block, 1)
    kernel = lax.all_gather(weight_part, "fsdp", axis=0, tiled=True).reshape(3, 3, channels, block)
    near_images = jnp.concatenate(group_images, axis=0)
    maps = lax.conv_general_dilated(
        jnp.concatenate([near_images, over_core(near_images)], axis=0),
        kernel,
        (1, 1),
        "SAME",
        dimension_numbers=("NHWC", "HWIO", "NHWC"),
        preferred_element_type=jnp.float32,
    ).astype(jnp.bfloat16)
    maps = maps.reshape((2, n_pair) + activations.shape[:3] + (block,))
    own_maps = []
    for pair in range(n_pair):
        for other in range(2):
            own_maps.append(
                maps[other, pair]
                if pair + other == 0
                else moved(
                    maps[other, pair], "factor", lambda at, o=other, p=pair: (at ^ o) - 2 * p
                )
            )
    own_maps = jnp.stack(own_maps)
    conv_out = jnp.concatenate(
        [
            lax.dynamic_index_in_dim(
                own_maps,
                2 * ((at // 2 - pair_at) % n_pair) + (at + core_at) % 2,
                0,
                keepdims=False,
            )
            for at in range(n_factor)
        ],
        axis=3,
    )

    g_partial = lax.psum_scatter(
        by_rows(own_cot, own_cot), "factor", scatter_dimension=0, tiled=True
    )
    g_factor = 0.5 * g_factor_old + 0.5 * lax.psum(g_partial, "fsdp")
    return (conv_out, a_factor, g_factor, natural_grad)


def solution(mesh):
    images = P(("fsdp", "factor"), None, None, None)
    return jax.shard_map(
        per_device,
        mesh=mesh,
        in_specs=(
            images,
            images,
            P("fsdp", None),
            P("factor", "fsdp"),
            P("factor", None),
            P("fsdp", "factor"),
            P(),
        ),
        out_specs=(
            images,
            P("factor", "fsdp"),
            P("factor", None),
            P("fsdp", "factor"),
        ),
        check_vma=False,
    )
```

time: 700 us -> 339 us (0.48)
  waiting for transfers between devices: 586 us -> 82.8 us
  other arithmetic: 6.03 us -> 109 us
  starting transfers between devices: 0.25 us -> 43.7 us
  local copies, waits for them, and re-layouts: 20.9 us -> 49.6 us
  blocking collectives: 27.7 us -> 0 us
  matrix products: 43.4 us -> 33.3 us
    reduce_scatter x2 -> x1, waiting for transfers between devices: 384 us -> 0.01 us  [per_device(): lax.psum_scatter(by_rows(own_cot, own_cot), 'factor', scatter_dimension=0...]
    psum x2 -> x1, waiting for transfers between devices: 193 us -> 44.3 us  [per_device(): g_factor = 0.5 * g_factor_old + 0.5 * lax.psum(g_partial, 'fsdp')]
    unnamed x0 -> x11, other arithmetic: none -> 45.1 us
    select_n x0 -> x6, other arithmetic: none -> 37 us  [the longest x5 36.9 us: tile_of_patches(): jnp.where(lane < channels - offset, tap(first_tap + step), tap(first_tap...]
    ppermute x0 -> x28, starting transfers between devices: none -> 36.3 us  [moved(): lax.ppermute(array, axis, [(at, target(at) % count) for at in range(count)])]
    ppermute x0 -> x28, waiting for transfers between devices: none -> 30 us  [moved(): lax.ppermute(array, axis, [(at, target(at) % count) for at in range(count)])]
    psum x1 -> x0, blocking collectives: 27.7 us -> none  [per_device(): summed_rows = lax.psum(partial_rows, 'factor')]
    concatenate x0 -> x10, other arithmetic: none -> 16.2 us  [the longest x4 8.29 us: per_device(): images = jnp.concatenate(near + far, axis=0)]
  transfers between devices with their start and end apart: 6 -> 32, of which waited for: 5 -> 9; matrix products, arithmetic and copies ran while one was open for 9% -> 55% of each run, Pallas kernels for 0% -> 0%
where the time goes in v1:
time: 339 us; the launch traced here: 334 us
  other arithmetic  109 us (32%)
  waiting for transfers between devices  82.8 us (24%)
  local copies, waits for them, and re-layouts  49.6 us (15%)
  starting transfers between devices  43.7 us (13%)
  matrix products  33.3 us (10%)
  between operations  16.5 us (5%)
    unnamed x11, other arithmetic  45.1 us
    psum x1, waiting for transfers between devices, per_device(): g_factor = 0.5 * g_factor_old + 0.5 * lax.psum(g_partial, 'fsdp')  44.3 us
    select_n x5, other arithmetic, tile_of_patches(): jnp.where(lane < channels - offset, tap(first_tap + step), tap(first_tap...  36.9 us
    ppermute x28, starting transfers between devices, moved(): lax.ppermute(array, axis, [(at, target(at) % count) for at in range(count)])  36.3 us
    ppermute x28, waiting for transfers between devices, moved(): lax.ppermute(array, axis, [(at, target(at) % count) for at in range(count)])  30 us
    dot_general x5, matrix products, by_rows(): lax.dot_general(first_op, second_op, (((0,), (0,)), ((), ())), preferred_...  17.1 us
    dynamic_slice x2, local copies, waits for them, and re-layouts, own_half(): mine = lax.dynamic_index_in_dim(halves, core_at, 1, keepdims=False)  14 us
    unnamed x86, local copies, waits for them, and re-layouts  11.2 us
  transfers between devices with their start and end apart: 32, of which 9 were waited for; matrix products, arithmetic and copies ran while one was open for 55% of the time, Pallas kernels for 0%

profile of v1, /device:TPU:0, one launch (start us, length us, event | category | flops | bytes accessed | tf_op | source)
XLA Modules:
  0.0 334.4 jit_solution(7231428155823532182)
XLA Ops:
  8.1 1.7 constant_dynamic-slice_fusion.8
  9.8 1.8 copy.36
  11.6 7.3 %all-to-all-start = ((bf16[8,64,256]{2,1,0:T(8,128)(2,1)}), bf16[8,64,256]{2,1,0:T(8,128)(2,1)S(1)}, u32[]{:S(2)}, u32[]{:S(2)}) async-start(bf16[8,64,256]{2,1,0:T(8,128)(2,1)} %bitcast.35), calls=%async_computation.1 | async-start | bytes 524288 | tf_op jit(solution)/shard_map/all_to_all | solution.py:64
  18.9 2.0 collective-permute-start.7
  20.9 1.5 collective-permute-start.5
  22.4 1.5 collective-permute-start
  23.9 2.4 collective-permute-start.15
  26.3 2.4 convolution_bitcast_fusion.1
  28.7 8.5 %all-to-all-done = bf16[8,64,256]{2,1,0:T(8,128)(2,1)S(1)} async-done(((bf16[8,64,256]{2,1,0:T(8,128)(2,1)}), bf16[8,64,256]{2,1,0:T(8,128)(2,1)S(1)}, u32[]{:S(2)}, u32[]{:S(2)}) %all-to-all-start) | async-done | bytes 262176 | tf_op jit(solution)/shard_map/all_to_all | solution.py:64
  37.2 2.1 collective-permute-start.20
  40.3 4.0 %collective-permute-start.11 = (bf16[1,16,16,512]{3,2,1,0:T(8,128)(2,1)S(1)}, bf16[1,16,16,512]{3,2,1,0:T(8,128)(2,1)}, u32[]{:S(2)}, u32[]{:S(2)}) collective-permute-start(bf16[1,16,16,512]{3,2,1,0:T(8,128)(2,1)S(1)} %copy-done.18), channel_id=1, source_target_pairs={{0,16},{4,20},{8,24},{12,28},{16,0},{20,4},{24,8},{28,12},{1,17},{... | collective-permute-start | bytes 786440 | tf_op jit(solution)/shard_map/ppermute | solution.py:15
  44.3 1.5 collective-permute-start.8
  45.8 2.0 collective-permute-start.6
  47.9 2.8 gather_fusion
  50.7 2.5 copy.37
  53.9 1.5 dynamic-slice_bitcast_fusion.4
  55.4 3.3 collective-permute-start.9
  58.7 6.0 %collective-permute-done.11 = bf16[1,16,16,512]{3,2,1,0:T(8,128)(2,1)} collective-permute-done((bf16[1,16,16,512]{3,2,1,0:T(8,128)(2,1)S(1)}, bf16[1,16,16,512]{3,2,1,0:T(8,128)(2,1)}, u32[]{:S(2)}, u32[]{:S(2)}) %collective-permute-start.11) | collective-permute-done | bytes 262176 | tf_op jit(solution)/shard_map/ppermute | solution.py:15
  64.7 2.6 collective-permute-start.17
  68.7 2.0 collective-permute-start.10
  70.7 2.4 pad_maximum_fusion.2
  73.9 8.1 %fusion.63 = (bf16[4,16,16,512]{3,2,1,0:T(8,128)(2,1)}, bf16[4,16,16,512]{3,2,1,0:T(8,128)(2,1)}, bf16[4,16,16,2304]{3,2,1,0:T(8,128)(2,1)S(1)}) fusion(s32[]{:T(128)S(6)} %select_n.706, s32[]{:T(128)S(6)} %select_n.709, s32[]{:T(128)S(6)} %select_n.711, bf16[4,18,18,512]{3,2,1,0:T(8,128)(2,1)S(1)} %pad.17, pred[512]{0:T(512)(128)(4,1)S(1)} %get-tuple-element.77, ...), kind=kLoop, calls=%fused_computation.157 | loop fusion | flops 9437183 | bytes 4473896 | tf_op jit(solution)/shard_map/jit(_where)/select_n | solution.py:36
  84.1 1.8 collective-permute-done.10
  85.8 1.8 select_maximum_fusion.6
  87.7 7.8 %fusion.53 = (bf16[4,16,16,512]{3,2,1,0:T(8,128)(2,1)}, bf16[4,16,16,512]{3,2,1,0:T(8,128)(2,1)}, bf16[4,16,16,2304]{3,2,1,0:T(8,128)(2,1)S(1)}) fusion(s32[]{:T(128)S(6)} %select_n.706, s32[]{:T(128)S(6)} %select_n.709, s32[]{:T(128)S(6)} %select_n.711, bf16[4,18,18,512]{3,2,1,0:T(8,128)(2,1)S(1)} %select_maximum_fusion.6, ...), kind=kLoop, calls=%fused_computation.147 | loop fusion | flops 9437183 | bytes 4473896 | tf_op jit(solution)/shard_map/jit(_where)/select_n | solution.py:36
  95.5 1.8 select_maximum_fusion
  97.3 7.8 %fusion.33 = (bf16[4,16,16,512]{3,2,1,0:T(8,128)(2,1)}, bf16[4,16,16,512]{3,2,1,0:T(8,128)(2,1)}, bf16[4,16,16,2304]{3,2,1,0:T(8,128)(2,1)S(1)}) fusion(s32[]{:T(128)S(6)} %select_n.706, s32[]{:T(128)S(6)} %select_n.709, s32[]{:T(128)S(6)} %select_n.711, bf16[4,18,18,512]{3,2,1,0:T(8,128)(2,1)S(1)} %select_maximum_fusion, ...), kind=kLoop, calls=%fused_computation.127 | loop fusion | flops 9437183 | bytes 4473896 | tf_op jit(solution)/shard_map/jit(_where)/select_n | solution.py:36
  105.0 2.3 select_maximum_fusion.3
  107.3 7.8 %fusion.43 = (bf16[4,16,16,512]{3,2,1,0:T(8,128)(2,1)}, bf16[4,16,16,512]{3,2,1,0:T(8,128)(2,1)}, bf16[4,16,16,2304]{3,2,1,0:T(8,128)(2,1)S(1)}) fusion(s32[]{:T(128)S(6)} %select_n.706, s32[]{:T(128)S(6)} %select_n.709, s32[]{:T(128)S(6)} %select_n.711, bf16[4,18,18,512]{3,2,1,0:T(8,128)(2,1)S(1)} %select_maximum_fusion.3, ...), kind=kLoop, calls=%fused_computation.137 | loop fusion | flops 9437183 | bytes 4473896 | tf_op jit(solution)/shard_map/jit(_where)/select_n | solution.py:36
  115.1 3.3 select_dynamic-update-slice_fusion.2
  118.4 10.6 %select_dynamic-update-slice_fusion.1 = (bf16[4,16,16,2304]{3,2,1,0:T(8,128)(2,1)S(1)}, bf16[4,16,16,2304]{3,2,1,0:T(8,128)(2,1)S(1)}, bf16[4,16,16,2304]{3,2,1,0:T(8,128)(2,1)S(1)}) fusion(bf16[4,16,16,2304]{3,2,1,0:T(8,128)(2,1)S(1)} %select_dynamic-update-slice_fusion.2, pred[512]{0:T(512)(128)(4,1)S(1)} %get-tuple-element.76, s32[]{:T(128)S(6)} %select_n.752, ...), kind=kLoop, calls=%fused_computation.170 | loop fusion | flops 14155776 | bytes 8454684
  129.0 7.5 %select_dynamic-update-slice_fusion = (bf16[4,16,16,2304]{3,2,1,0:T(8,128)(2,1)S(1)}, bf16[4,16,16,512]{3,2,1,0:T(8,128)(2,1)S(1)}, bf16[4,16,16,2304]{3,2,1,0:T(8,128)(2,1)S(1)}) fusion(bf16[4,16,16,2304]{3,2,1,0:T(8,128)(2,1)S(1)} %get-tuple-element.63, pred[512]{0:T(512)(128)(4,1)S(1)} %get-tuple-element.76, s32[]{:T(128)S(6)} %select_n.752, ...), kind=kLoop, calls=%fused_computation.169 | loop fusion | flops 9437184 | bytes 6685220
  136.5 3.3 select_dynamic-update-slice_fusion.10
  139.8 11.3 %select_dynamic-update-slice_fusion.9 = (bf16[4,16,16,2304]{3,2,1,0:T(8,128)(2,1)S(1)}, bf16[4,16,16,512]{3,2,1,0:T(8,128)(2,1)}, bf16[4,16,16,2304]{3,2,1,0:T(8,128)(2,1)S(1)}, bf16[4,16,16,2304]{3,2,1,0:T(8,128)(2,1)S(1)}) fusion(bf16[4,16,16,2304]{3,2,1,0:T(8,128)(2,1)S(1)} %select_dynamic-update-slice_fusion.10, ...), kind=kLoop, calls=%fused_computation.178 | loop fusion | flops 14155776 | bytes 9503260
  151.1 7.2 %select_dynamic-update-slice_fusion.6 = (bf16[4,16,16,2304]{3,2,1,0:T(8,128)(2,1)S(1)}, bf16[4,16,16,512]{3,2,1,0:T(8,128)(2,1)S(1)}, bf16[4,16,16,2304]{3,2,1,0:T(8,128)(2,1)S(1)}, bf16[4,16,16,512]{3,2,1,0:T(8,128)(2,1)S(1)}) fusion(bf16[4,16,16,2304]{3,2,1,0:T(8,128)(2,1)S(1)} %get-tuple-element.66, pred[512]{0:T(512)(128)(4,1)S(1)} %get-tuple-element.76, ...), kind=kLoop, calls=%fused_computation.175 | loop fusion | flops 9437184 | bytes 7733780
  159.5 3.1 fusion.74
  167.7 1.8 convolution_add_fusion
  169.5 2.3 reshape.127
  171.8 2.0 constant_dynamic-slice_fusion.1
  174.5 5.5 %slice_select_fusion = (bf16[4,16,16,64]{3,2,1,0:T(8,128)(2,1)}, bf16[4,16,16,64]{3,2,1,0:T(8,128)(2,1)S(1)}, bf16[4,16,16,64]{3,2,1,0:T(8,128)(2,1)S(1)}, bf16[4,16,16,64]{3,2,1,0:T(8,128)(2,1)S(1)}) fusion(bf16[4,16,16,512]{3,2,1,0:T(8,128)(2,1)} %get-tuple-element.7, s32[]{:T(128)S(6)} %select_n.721, s32[]{:T(128)S(6)} %select_n.724, s32[]{:T(128)S(6)} %select_n.711, ...), kind=kLoop, calls=%fused_computation.205 | loop fusion | flops 1310720 | bytes 6357068 | tf_op jit(solution)/shard_map/jit(_where)/select_n | solution.py:36
  180.1 3.1 fusion.15
  183.3 3.0 fusion.19
  186.4 3.0 fusion.11
  189.4 5.7 %bitcast_add_fusion = f32[576,2304]{1,0:T(8,128)} fusion(f32[576,2304,1,1]{1,0,3,2:T(8,128)S(1)} %fusion.19, f32[576,2304,1,1]{1,0,3,2:T(8,128)S(1)} %fusion.15, f32[576,2304,1,1]{1,0,3,2:T(8,128)S(1)} %fusion.11, bf16[4,16,16,2304]{3,2,1,0:T(8,128)(2,1)S(1)} %bitcast.177, bf16[4,16,16,64]{3,2,1,0:T(8,128)(2,1)S(1)} %copy-done.21, ...), kind=kOutput, calls=%fused_computation.77 | convolution fusion | flops 2724249600 | bytes 27131904 | tf_op jit(solution)/shard_map/dot_general | solution.py:8
  195.0 7.4 %reshape.119 = f32[576,2,1152]{2,1,0:T(2,128)} reshape(f32[576,2304]{1,0:T(8,128)} %bitcast_add_fusion) | data formatting | bytes 10616832 | tf_op jit(solution)/shard_map/reshape | solution.py:97
  202.4 1.8 constant_dynamic-update-slice_fusion.4
  204.3 2.2 collective-permute-start.22
  206.5 12.0 %constant_dynamic-slice_fusion.3 = (f32[576,1,1152]{2,1,0:T(1,128)}, f32[576,1,1152]{2,1,0:T(1,128)}) fusion(f32[576,2,1152]{2,1,0:T(2,128)} %reshape.119, s32[]{:T(128)S(6)} %select_n.792, s32[]{:T(128)S(6)} %select_n.793), kind=kLoop, calls=%fused_computation.274 | loop fusion | bytes 10616840 | tf_op jit(solution)/shard_map/jit(dynamic_index_in_dim)/dynamic_slice | solution.py:98
  218.5 1.8 copy.47
  220.6 1.5 copy-done.10
  222.0 1.7 copy.65
  223.7 1.9 fusion.7
  225.6 4.7 %collective-permute-done.23 = f32[64,1152]{1,0:T(8,128)S(1)} collective-permute-done((f32[64,1152]{1,0:T(8,128)}, f32[64,1152]{1,0:T(8,128)S(1)}, u32[]{:S(2)}, u32[]{:S(2)}) %collective-permute-start.23) | collective-permute-done | bytes 294944 | tf_op jit(solution)/shard_map/ppermute | solution.py:15
  230.3 2.1 pad_maximum_fusion
  232.4 2.0 collective-permute-start.25
  235.8 6.0 %fusion.29 = bf16[16,32,3,128]{3,1,2,0:T(8,128)(2,1)S(1)} fusion(bf16[3,3,512,128]{3,2,1,0:T(8,128)(2,1)} %bitcast.191, bf16[16,4,8,5,512]{4,0,3,2,1:T(8,128)(2,1)} %fusion.7, pred[32,3]{0,1:T(4,128)(4,1)S(1)} %copy-done.31), kind=kOutput, calls=%fused_computation.124 | convolution fusion | flops 1736835072 | bytes 4194400 | tf_op jit(solution)/shard_map/conv_general_dilated | solution.py:138
  244.8 1.5 collective-permute-done.4
  247.3 14.2 %collective-permute-done.25 = f32[256,1152]{1,0:T(8,128)} collective-permute-done((f32[256,1152]{1,0:T(8,128)}, f32[256,1152]{1,0:T(8,128)}, u32[]{:S(2)}, u32[]{:S(2)}) %collective-permute-start.25) | collective-permute-done | bytes 1179680 | tf_op jit(solution)/shard_map/ppermute | solution.py:15
  261.5 2.4 constant_dynamic-update-slice_fusion
  263.9 4.5 %convolution_bitcast_fusion = f32[512,576,1,1]{0,1,3,2:T(8,128)S(1)} fusion(f32[512,1152]{1,0:T(8,128)} %constant_dynamic-update-slice_fusion, f32[576,1152]{1,0:T(8,128)S(1)} %copy-done), kind=kOutput, calls=%fused_computation.106 | convolution fusion | flops 2038431744 | bytes 6193152 | tf_op jit(solution)/shard_map/dot_general | solution.py:115
  271.5 44.3 %all-reduce.6.cloned.1.call-done = f32[128,512]{1,0:T(8,128)} async-done(((f32[128,512]{1,0:T(8,128)}), f32[128,512]{1,0:T(8,128)}) %all-reduce.6.cloned.1.call-update) | async-done | bytes 262160 | tf_op jit(solution)/shard_map/psum | solution.py:174
  315.8 1.8 add_multiply_fusion
  319.0 1.5 collective-permute-start.27
  320.5 4.5 %fusion.6 = f32[1152,576]{0,1:T(8,128)} fusion(f32[576,1152]{1,0:T(8,128)} %collective-permute-done.19, f32[576,1,1152]{2,1,0:T(1,128)S(1)} %copy-done.9, f32[1152,576]{0,1:T(8,128)} %param.10), kind=kLoop, calls=%fused_computation.92 | loop fusion | flops 2654208 | bytes 10616832 | tf_op jit(solution)/shard_map/add | solution.py:107
  (159 shorter events, 24.6 us)
Async XLA Ops:
  8.0 255.9 %copy-start = (f32[576,1152]{1,0:T(8,128)S(1)}, f32[576,1152]{1,0:T(8,128)}, u32[]{:S(2)}) copy-start(f32[576,1152]{1,0:T(8,128)} %param.12) | copy-start | bytes 7962628
  8.0 227.8 %all-gather.2.cloned.1.call-start = ((), (), s32[]{:S(2)}) async-start(), calls=%async_computation.2 | async-start | bytes 1327104 | tf_op jit(solution)/shard_map/all_gather | solution.py:136
  11.6 25.6 %all-to-all-start = ((bf16[8,64,256]{2,1,0:T(8,128)(2,1)}), bf16[8,64,256]{2,1,0:T(8,128)(2,1)S(1)}, u32[]{:S(2)}, u32[]{:S(2)}) async-start(bf16[8,64,256]{2,1,0:T(8,128)(2,1)} %bitcast.35), calls=%async_computation.1 | async-start | bytes 524288 | tf_op jit(solution)/shard_map/all_to_all | solution.py:64
  18.9 20.5 %copy-start.18 = (bf16[1,16,16,512]{3,2,1,0:T(8,128)(2,1)S(1)}, bf16[1,16,16,512]{3,2,1,0:T(8,128)(2,1)}, u32[]{:S(2)}) copy-start(bf16[1,16,16,512]{3,2,1,0:T(8,128)(2,1)} %param.7) | copy-start | bytes 786436
  18.9 225.9 %reduce-scatter.2.cloned.1.call-start = ((), (), s32[]{:S(2)}) async-start(), calls=%async_computation.3 | async-start | bytes 1310720 | tf_op jit(solution)/shard_map/reduce_scatter | solution.py:171
  18.9 21.3 %collective-permute-start.7 = (bf16[1,16,16,512]{3,2,1,0:T(8,128)(2,1)}, bf16[1,16,16,512]{3,2,1,0:T(8,128)(2,1)}, u32[]{:S(2)}, u32[]{:S(2)}) collective-permute-start(bf16[1,16,16,512]{3,2,1,0:T(8,128)(2,1)} %param.7), channel_id=1, source_target_pairs={{0,8},{4,12},{8,16},{12,20},{16,24},{20,28},{24,0},{28,4},{1,9},{5... | collective-permute-start | bytes 786440 | tf_op jit(solution)/shard_map/ppermute | solution.py:15
  20.9 23.4 %collective-permute-start.5 = (bf16[1,16,16,512]{3,2,1,0:T(8,128)(2,1)}, bf16[1,16,16,512]{3,2,1,0:T(8,128)(2,1)}, u32[]{:S(2)}, u32[]{:S(2)}) collective-permute-start(bf16[1,16,16,512]{3,2,1,0:T(8,128)(2,1)} %param.7), channel_id=1, source_target_pairs={{0,4},{4,0},{8,12},{12,8},{16,20},{20,16},{24,28},{28,24},{1,5},{5... | collective-permute-start | bytes 786440 | tf_op jit(solution)/shard_map/ppermute | solution.py:15
  22.4 16.9 %collective-permute-start = (bf16[1,16,16,512]{3,2,1,0:T(8,128)(2,1)}, bf16[1,16,16,512]{3,2,1,0:T(8,128)(2,1)S(1)}, u32[]{:S(2)}, u32[]{:S(2)}) collective-permute-start(bf16[1,16,16,512]{3,2,1,0:T(8,128)(2,1)} %param.7), channel_id=1, source_target_pairs={{0,2},{1,3},{2,0},{3,1},{4,6},{5,7},{6,4},{7,5},{8,10},{9,11},{10,... | collective-permute-start | bytes 786440 | tf_op jit(solution)/shard_map/ppermute | solution.py:15
  23.9 31.5 %collective-permute-start.15 = (bf16[1,16,16,512]{3,2,1,0:T(8,128)(2,1)}, bf16[1,16,16,512]{3,2,1,0:T(8,128)(2,1)}, u32[]{:S(2)}, u32[]{:S(2)}) collective-permute-start(bf16[1,16,16,512]{3,2,1,0:T(8,128)(2,1)} %param.7), channel_id=1, source_target_pairs={{0,24},{4,28},{8,0},{12,4},{16,8},{20,12},{24,16},{28,20},{1,25},{... | collective-permute-start | bytes 786440 | tf_op jit(solution)/shard_map/ppermute | solution.py:15
  28.7 287.1 %all-reduce.6.cloned.1.call-start = ((), (), s32[]{:S(2)}) async-start(), calls=%async_computation.4 | async-start | bytes 524288 | tf_op jit(solution)/shard_map/psum | solution.py:174
  37.2 8.6 %collective-permute-start.20 = (bf16[8,64,256]{2,1,0:T(8,128)(2,1)S(1)}, bf16[8,64,256]{2,1,0:T(8,128)(2,1)}, u32[]{:S(2)}, u32[]{:S(2)}) collective-permute-start(bf16[8,64,256]{2,1,0:T(8,128)(2,1)S(1)} %all-to-all-done), channel_id=1, source_target_pairs={{0,2},{1,3},{2,0},{3,1},{4,6},{5,7},{6,4},{7,5},{8,10},{9,11},{10,... | collective-permute-start | bytes 786440 | tf_op jit(solution)/shard_map/ppermute | solution.py:15
  40.2 28.5 %collective-permute-start.1 = (bf16[2,16,16,512]{3,2,1,0:T(8,128)(2,1)}, bf16[2,16,16,512]{3,2,1,0:T(8,128)(2,1)}, u32[]{:S(2)}, u32[]{:S(2)}) collective-permute-start(bf16[2,16,16,512]{3,2,1,0:T(8,128)(2,1)} %pad_maximum_fusion.3), channel_id=1, source_target_pairs={{0,1},{1,0},{2,3},{3,2},{4,5},{5,4},{6,7},{7,6},{8,9},{9,8},{10,11... | collective-permute-start | bytes 1572872 | tf_op jit(solution)/shard_map/ppermute | solution.py:15
  40.3 24.4 %collective-permute-start.11 = (bf16[1,16,16,512]{3,2,1,0:T(8,128)(2,1)S(1)}, bf16[1,16,16,512]{3,2,1,0:T(8,128)(2,1)}, u32[]{:S(2)}, u32[]{:S(2)}) collective-permute-start(bf16[1,16,16,512]{3,2,1,0:T(8,128)(2,1)S(1)} %copy-done.18), channel_id=1, source_target_pairs={{0,16},{4,20},{8,24},{12,28},{16,0},{20,4},{24,8},{28,12},{1,17},{... | collective-permute-start | bytes 786440 | tf_op jit(solution)/shard_map/ppermute | solution.py:15
  44.3 22.9 %collective-permute-start.8 = (bf16[1,16,16,512]{3,2,1,0:T(8,128)(2,1)}, bf16[1,16,16,512]{3,2,1,0:T(8,128)(2,1)}, u32[]{:S(2)}, u32[]{:S(2)}) collective-permute-start(bf16[1,16,16,512]{3,2,1,0:T(8,128)(2,1)} %collective-permute-done.7), channel_id=1, source_target_pairs={{0,2},{1,3},{2,0},{3,1},{4,6},{5,7},{6,4},{7,5},{8,10},{9,11},{10,... | collective-permute-start | bytes 786440 | tf_op jit(solution)/shard_map/ppermute | solution.py:15
  45.8 22.9 %collective-permute-start.6 = (bf16[1,16,16,512]{3,2,1,0:T(8,128)(2,1)}, bf16[1,16,16,512]{3,2,1,0:T(8,128)(2,1)}, u32[]{:S(2)}, u32[]{:S(2)}) collective-permute-start(bf16[1,16,16,512]{3,2,1,0:T(8,128)(2,1)} %collective-permute-done.5), channel_id=1, source_target_pairs={{0,2},{1,3},{2,0},{3,1},{4,6},{5,7},{6,4},{7,5},{8,10},{9,11},{10,... | collective-permute-start | bytes 786440 | tf_op jit(solution)/shard_map/ppermute | solution.py:15
  55.4 26.6 %collective-permute-start.9 = (bf16[1,16,16,512]{3,2,1,0:T(8,128)(2,1)}, bf16[1,16,16,512]{3,2,1,0:T(8,128)(2,1)S(1)}, u32[]{:S(2)}, u32[]{:S(2)}) collective-permute-start(bf16[1,16,16,512]{3,2,1,0:T(8,128)(2,1)} %collective-permute-done.7), channel_id=1, source_target_pairs={{0,4},{4,0},{8,12},{12,8},{16,20},{20,16},{24,28},{28,24},{1,5},{5... | collective-permute-start | bytes 786440 | tf_op jit(solution)/shard_map/ppermute | solution.py:15
  64.7 30.8 %collective-permute-start.17 = (bf16[1,16,16,512]{3,2,1,0:T(8,128)(2,1)}, bf16[1,16,16,512]{3,2,1,0:T(8,128)(2,1)S(1)}, u32[]{:S(2)}, u32[]{:S(2)}) collective-permute-start(bf16[1,16,16,512]{3,2,1,0:T(8,128)(2,1)} %collective-permute-done.15), channel_id=1, source_target_pairs={{0,4},{4,0},{8,12},{12,8},{16,20},{20,16},{24,28},{28,24},{1,5},{5... | collective-permute-start | bytes 786440 | tf_op jit(solution)/shard_map/ppermute | solution.py:15
  67.3 15.3 %collective-permute-start.16 = (bf16[1,16,16,512]{3,2,1,0:T(8,128)(2,1)}, bf16[1,16,16,512]{3,2,1,0:T(8,128)(2,1)S(1)}, u32[]{:S(2)}, u32[]{:S(2)}) collective-permute-start(bf16[1,16,16,512]{3,2,1,0:T(8,128)(2,1)} %collective-permute-done.15), channel_id=1, source_target_pairs={{0,2},{1,3},{2,0},{3,1},{4,6},{5,7},{6,4},{7,5},{8,10},{9,11},{10,... | collective-permute-start | bytes 786440 | tf_op jit(solution)/shard_map/ppermute | solution.py:15
  68.7 13.9 %collective-permute-start.13 = (bf16[1,16,16,512]{3,2,1,0:T(8,128)(2,1)}, bf16[1,16,16,512]{3,2,1,0:T(8,128)(2,1)S(1)}, u32[]{:S(2)}, u32[]{:S(2)}) collective-permute-start(bf16[1,16,16,512]{3,2,1,0:T(8,128)(2,1)} %collective-permute-done.11), channel_id=1, source_target_pairs={{0,4},{4,0},{8,12},{12,8},{16,20},{20,16},{24,28},{28,24},{1,5},{5... | collective-permute-start | bytes 786440 | tf_op jit(solution)/shard_map/ppermute | solution.py:15
  68.7 17.1 %collective-permute-start.10 = (bf16[1,16,16,512]{3,2,1,0:T(8,128)(2,1)}, bf16[1,16,16,512]{3,2,1,0:T(8,128)(2,1)S(1)}, u32[]{:S(2)}, u32[]{:S(2)}) collective-permute-start(bf16[1,16,16,512]{3,2,1,0:T(8,128)(2,1)} %collective-permute-done.8), channel_id=1, source_target_pairs={{0,4},{4,0},{8,12},{12,8},{16,20},{20,16},{24,28},{28,24},{1,5},{5... | collective-permute-start | bytes 786440 | tf_op jit(solution)/shard_map/ppermute | solution.py:15
  73.9 84.5 %copy-start.1 = (bf16[4,18,18,512]{3,2,1,0:T(8,128)(2,1)}, bf16[4,18,18,512]{3,2,1,0:T(8,128)(2,1)S(1)}, u32[]{:S(2)}) copy-start(bf16[4,18,18,512]{3,2,1,0:T(8,128)(2,1)S(1)} %pad.17) | copy-start | bytes 3981316
  81.9 23.1 %collective-permute-start.12 = (bf16[1,16,16,512]{3,2,1,0:T(8,128)(2,1)}, bf16[1,16,16,512]{3,2,1,0:T(8,128)(2,1)S(1)}, u32[]{:S(2)}, u32[]{:S(2)}) collective-permute-start(bf16[1,16,16,512]{3,2,1,0:T(8,128)(2,1)} %collective-permute-done.11), channel_id=1, source_target_pairs={{0,2},{1,3},{2,0},{3,1},{4,6},{5,7},{6,4},{7,5},{8,10},{9,11},{10,... | collective-permute-start | bytes 786440 | tf_op jit(solution)/shard_map/ppermute | solution.py:15
  82.6 12.9 %collective-permute-start.18 = (bf16[1,16,16,512]{3,2,1,0:T(8,128)(2,1)S(1)}, bf16[1,16,16,512]{3,2,1,0:T(8,128)(2,1)S(1)}, u32[]{:S(2)}, u32[]{:S(2)}) collective-permute-start(bf16[1,16,16,512]{3,2,1,0:T(8,128)(2,1)S(1)} %collective-permute-done.16), channel_id=1, source_target_pairs={{0,4},{4,0},{8,12},{12,8},{16,20},{20,16},{24,28},{28,24},{1,5},{5... | collective-permute-start | bytes 786440 | tf_op jit(solution)/shard_map/ppermute | solution.py:15
  82.6 22.4 %collective-permute-start.14 = (bf16[1,16,16,512]{3,2,1,0:T(8,128)(2,1)S(1)}, bf16[1,16,16,512]{3,2,1,0:T(8,128)(2,1)S(1)}, u32[]{:S(2)}, u32[]{:S(2)}) collective-permute-start(bf16[1,16,16,512]{3,2,1,0:T(8,128)(2,1)S(1)} %collective-permute-done.13), channel_id=1, source_target_pairs={{0,2},{1,3},{2,0},{3,1},{4,6},{5,7},{6,4},{7,5},{8,10},{9,11},{10,... | collective-permute-start | bytes 786440 | tf_op jit(solution)/shard_map/ppermute | solution.py:15
  87.7 71.8 %copy-start.3 = (bf16[4,18,18,512]{3,2,1,0:T(8,128)(2,1)}, bf16[4,18,18,512]{3,2,1,0:T(8,128)(2,1)S(1)}, u32[]{:S(2)}) copy-start(bf16[4,18,18,512]{3,2,1,0:T(8,128)(2,1)S(1)} %select_maximum_fusion.6) | copy-start | bytes 3981316
  97.2 62.2 %copy-start.4 = (bf16[4,18,18,512]{3,2,1,0:T(8,128)(2,1)}, bf16[4,18,18,512]{3,2,1,0:T(8,128)(2,1)S(1)}, u32[]{:S(2)}) copy-start(bf16[4,18,18,512]{3,2,1,0:T(8,128)(2,1)S(1)} %select_maximum_fusion) | copy-start | bytes 3981316
  107.3 52.2 %copy-start.5 = (bf16[4,18,18,512]{3,2,1,0:T(8,128)(2,1)}, bf16[4,18,18,512]{3,2,1,0:T(8,128)(2,1)S(1)}, u32[]{:S(2)}) copy-start(bf16[4,18,18,512]{3,2,1,0:T(8,128)(2,1)S(1)} %select_maximum_fusion.3) | copy-start | bytes 3981316
  151.1 7.2 %copy-start.17 = (bf16[4,16,16,512]{3,2,1,0:T(8,128)(2,1)S(1)}, bf16[4,16,16,512]{3,2,1,0:T(8,128)(2,1)}, u32[]{:S(2)}) copy-start(bf16[4,16,16,512]{3,2,1,0:T(8,128)(2,1)} %get-tuple-element.13) | copy-start | bytes 3145732
  159.5 5.3 %copy-start.6 = (bf16[4,16,16,2304]{3,2,1,0:T(8,128)(2,1)}, bf16[4,16,16,2304]{3,2,1,0:T(8,128)(2,1)S(1)}, u32[]{:S(2)}) copy-start(bf16[4,16,16,2304]{3,2,1,0:T(8,128)(2,1)S(1)} %fusion.83) | copy-start | bytes 14155780
  159.5 3.2 copy-start.25
  159.5 3.2 copy-start.26
  159.5 3.2 copy-start.29
  159.5 3.2 copy-start.30
  162.7 3.6 %copy-start.8 = (bf16[4,16,16,2304]{3,2,1,0:T(8,128)(2,1)}, bf16[4,16,16,2304]{3,2,1,0:T(8,128)(2,1)S(1)}, u32[]{:S(2)}) copy-start(bf16[4,16,16,2304]{3,2,1,0:T(8,128)(2,1)S(1)} %get-tuple-element.61) | copy-start | bytes 14155780
  162.7 5.0 %copy-start.11 = (bf16[4,16,16,2304]{3,2,1,0:T(8,128)(2,1)}, bf16[4,16,16,2304]{3,2,1,0:T(8,128)(2,1)S(1)}, u32[]{:S(2)}) copy-start(bf16[4,16,16,2304]{3,2,1,0:T(8,128)(2,1)S(1)} %get-tuple-element.59) | copy-start | bytes 14155780
  169.5 13.7 %slice-start.4 = ((s8[4718592]{0:T(1024)(128)(4,1)}), s8[524288]{0:T(1024)(128)(4,1)S(1)}, s32[]{:S(2)}) async-start(s8[4718592]{0:T(1024)(128)(4,1)} %bitcast.171), calls=%async_computation.9 | async-start | bytes 1048576
  171.8 2.8 copy-start.2
  173.8 6.3 %slice-start.2 = ((s8[4718592]{0:T(1024)(128)(4,1)}), s8[4194304]{0:T(1024)(128)(4,1)S(1)}, s32[]{:S(2)}) async-start(s8[4718592]{0:T(1024)(128)(4,1)} %bitcast.168), calls=%async_computation.7 | async-start | bytes 8388608
  173.8 6.3 %copy-start.15 = (bf16[4,16,16,512]{3,2,1,0:T(8,128)(2,1)S(1)}, bf16[4,16,16,512]{3,2,1,0:T(8,128)(2,1)}, u32[]{:S(2)}) copy-start(bf16[4,16,16,512]{3,2,1,0:T(8,128)(2,1)} %get-tuple-element.14) | copy-start | bytes 3145732
  174.5 27.9 %collective-permute-start.21 = (f32[64,1152]{1,0:T(8,128)}, f32[64,1152]{1,0:T(8,128)}, u32[]{:S(2)}, u32[]{:S(2)}) collective-permute-start(f32[64,1152]{1,0:T(8,128)} %bitcast.161), channel_id=1, source_target_pairs={{0,1},{1,0},{2,3},{3,2},{4,5},{5,4},{6,7},{7,6},{8,9},{9,8},{10,11... | collective-permute-start | bytes 884744 | tf_op jit(solution)/shard_map/ppermute | solution.py:15
  174.5 5.6 %slice-start.3 = ((s8[4718592]{0:T(1024)(128)(4,1)}), s8[524288]{0:T(1024)(128)(4,1)S(1)}, s32[]{:S(2)}) async-start(s8[4718592]{0:T(1024)(128)(4,1)} %bitcast.168), calls=%async_computation.8 | async-start | bytes 1048576
  174.5 8.7 %slice-start.5 = ((s8[4718592]{0:T(1024)(128)(4,1)}), s8[4194304]{0:T(1024)(128)(4,1)S(1)}, s32[]{:S(2)}) async-start(s8[4718592]{0:T(1024)(128)(4,1)} %bitcast.171), calls=%async_computation.10 | async-start | bytes 8388608
  180.1 3.2 copy-start.16
  180.1 6.2 %slice-start = ((s8[4718592]{0:T(1024)(128)(4,1)}), s8[4194304]{0:T(1024)(128)(4,1)S(1)}, s32[]{:S(2)}) async-start(s8[4718592]{0:T(1024)(128)(4,1)} %bitcast.165), calls=%async_computation.5 | async-start | bytes 8388608
  183.3 3.0 slice-start.1
  183.3 3.0 copy-start.14
  183.3 6.0 %slice-start.6 = ((s8[4718592]{0:T(1024)(128)(4,1)}), s8[4194304]{0:T(1024)(128)(4,1)S(1)}, s32[]{:S(2)}) async-start(s8[4718592]{0:T(1024)(128)(4,1)} %bitcast.176), calls=%async_computation.11 | async-start | bytes 8388608
  186.3 3.0 slice-start.7
  186.3 3.0 copy-start.19
  186.4 3.0 copy-start.21
  204.3 21.3 %collective-permute-start.24 = (f32[64,1152]{1,0:T(8,128)}, f32[64,1152]{1,0:T(8,128)S(1)}, u32[]{:S(2)}, u32[]{:S(2)}) collective-permute-start(f32[64,1152]{1,0:T(8,128)} %get-tuple-element.5), channel_id=1, source_target_pairs={{0,24},{4,28},{8,0},{12,4},{16,8},{20,12},{24,16},{28,20},{1,25},{... | collective-permute-start | bytes 884744 | tf_op jit(solution)/shard_map/ppermute | solution.py:15
  204.3 26.0 %collective-permute-start.23 = (f32[64,1152]{1,0:T(8,128)}, f32[64,1152]{1,0:T(8,128)S(1)}, u32[]{:S(2)}, u32[]{:S(2)}) collective-permute-start(f32[64,1152]{1,0:T(8,128)} %get-tuple-element.5), channel_id=1, source_target_pairs={{0,16},{4,20},{8,24},{12,28},{16,0},{20,4},{24,8},{28,12},{1,17},{... | collective-permute-start | bytes 884744 | tf_op jit(solution)/shard_map/ppermute | solution.py:15
  204.3 26.0 %collective-permute-start.22 = (f32[64,1152]{1,0:T(8,128)}, f32[64,1152]{1,0:T(8,128)S(1)}, u32[]{:S(2)}, u32[]{:S(2)}) collective-permute-start(f32[64,1152]{1,0:T(8,128)} %get-tuple-element.5), channel_id=1, source_target_pairs={{0,8},{4,12},{8,16},{12,20},{16,24},{20,28},{24,0},{28,4},{1,9},{5... | collective-permute-start | bytes 884744 | tf_op jit(solution)/shard_map/ppermute | solution.py:15
  223.7 96.8 %collective-permute-start.19 = (f32[576,1152]{1,0:T(8,128)}, f32[576,1152]{1,0:T(8,128)}, u32[]{:S(2)}, u32[]{:S(2)}) collective-permute-start(f32[576,1152]{1,0:T(8,128)} %bitcast.160), channel_id=1, source_target_pairs={{0,1},{1,0},{2,3},{3,2},{4,5},{5,4},{6,7},{7,6},{8,9},{9,8},{10,11... | collective-permute-start | bytes 7962632 | tf_op jit(solution)/shard_map/ppermute | solution.py:15
  225.6 10.3 %copy-start.31 = (pred[32,3]{0,1:T(4,128)(4,1)S(1)}, pred[32,3]{0,1:T(4,128)(4,1)}, u32[]{:S(2)}) copy-start(pred[32,3]{0,1:T(4,128)(4,1)} %constant.1472) | copy-start | bytes 292
  232.4 29.1 %collective-permute-start.25 = (f32[256,1152]{1,0:T(8,128)}, f32[256,1152]{1,0:T(8,128)}, u32[]{:S(2)}, u32[]{:S(2)}) collective-permute-start(f32[256,1152]{1,0:T(8,128)} %pad_maximum_fusion), channel_id=1, source_target_pairs={{0,4},{4,0},{8,12},{12,8},{16,20},{20,16},{24,28},{28,24},{1,5},{5... | collective-permute-start | bytes 3538952 | tf_op jit(solution)/shard_map/ppermute | solution.py:15
  242.1 4.3 %collective-permute-start.4 = (bf16[1,16,16,128]{3,1,2,0:T(8,128)(2,1)S(1)}, bf16[1,16,16,128]{3,1,2,0:T(8,128)(2,1)S(1)}, u32[]{:S(2)}, u32[]{:S(2)}) collective-permute-start(bf16[1,16,16,128]{3,1,2,0:T(8,128)(2,1)S(1)} %slice_bitcast_fusion), channel_id=1, source_target_pairs={{0,3},{1,2},{2,1},{3,0},{4,7},{5,6},{6,5},{7,4},{8,11},{9,10},{10,... | collective-permute-start | bytes 196616 | tf_op jit(solution)/shard_map/ppermute | solution.py:15
  242.2 5.0 %collective-permute-start.3 = (bf16[1,16,16,128]{3,1,2,0:T(8,128)(2,1)S(1)}, bf16[1,16,16,128]{3,1,2,0:T(8,128)(2,1)S(1)}, u32[]{:S(2)}, u32[]{:S(2)}) collective-permute-start(bf16[1,16,16,128]{3,1,2,0:T(8,128)(2,1)S(1)} %get-tuple-element.53), channel_id=1, source_target_pairs={{0,2},{1,3},{2,0},{3,1},{4,6},{5,7},{6,4},{7,5},{8,10},{9,11},{10,... | collective-permute-start | bytes 196616 | tf_op jit(solution)/shard_map/ppermute | solution.py:15
  243.2 3.9 %collective-permute-start.2 = (bf16[1,16,16,128]{3,1,2,0:T(8,128)(2,1)S(1)}, bf16[1,16,16,128]{3,1,2,0:T(8,128)(2,1)S(1)}, u32[]{:S(2)}, u32[]{:S(2)}) collective-permute-start(bf16[1,16,16,128]{3,1,2,0:T(8,128)(2,1)S(1)} %get-tuple-element.54), channel_id=1, source_target_pairs={{0,1},{1,0},{2,3},{3,2},{4,5},{5,4},{6,7},{7,6},{8,9},{9,8},{10,11... | collective-permute-start | bytes 196616 | tf_op jit(solution)/shard_map/ppermute | solution.py:15
  263.9 4.5 %copy-start.13 = (f32[512,512]{0,1:T(8,128)S(1)}, f32[512,512]{0,1:T(8,128)}, u32[]{:S(2)}) copy-start(f32[512,512]{0,1:T(8,128)} %copy.37) | copy-start | bytes 3145732
  268.4 47.4 %copy-start.20 = (f32[128,512]{1,0:T(8,128)S(1)}, f32[128,512]{1,0:T(8,128)}, u32[]{:S(2)}) copy-start(f32[128,512]{1,0:T(8,128)} %param.11) | copy-start | bytes 786436
  270.6 47.0 %collective-permute-start.26 = (f32[576,2,128]{2,0,1:T(8,128)S(1)}, f32[576,2,128]{2,0,1:T(8,128)}, u32[]{:S(2)}, u32[]{:S(2)}) collective-permute-start(f32[576,2,128]{2,0,1:T(8,128)S(1)} %dynamic-slice_bitcast_fusion), channel_id=1, source_target_pairs={{0,1},{1,0},{2,3},{3,2},{4,5},{5,4},{6,7},{7,6},{8,9},{9,8},{10,11... | collective-permute-start | bytes 1769480 | tf_op jit(solution)/shard_map/ppermute | solution.py:15
  315.8 4.7 %copy-start.9 = (f32[576,1,1152]{2,1,0:T(1,128)S(1)}, f32[576,1,1152]{2,1,0:T(1,128)}, u32[]{:S(2)}) copy-start(f32[576,1,1152]{2,1,0:T(1,128)} %get-tuple-element.22) | copy-start | bytes 7962628
  319.0 7.0 %collective-permute-start.27 = (f32[576,128]{1,0:T(8,128)S(1)}, f32[576,128]{1,0:T(8,128)S(1)}, u32[]{:S(2)}, u32[]{:S(2)}) collective-permute-start(f32[576,128]{1,0:T(8,128)S(1)} %dynamic-slice_bitcast_fusion.1), channel_id=1, source_target_pairs={{0,2},{1,3},{2,0},{3,1},{4,6},{5,7},{6,4},{7,5},{8,10},{9,11},{10,... | collective-permute-start | bytes 884744 | tf_op jit(solution)/shard_map/ppermute | solution.py:15
  (8 other events, 14.5 us)
Sparse Core Ops, SparseCore 0:
  11.6 53.9 all-gather.1
  245.0 70.7 all-reduce.5
Sparse Core Ops, SparseCore 1:
  28.8 25.7 reduce-scatter.1

commit v2 on v1

--- a/solution.py
+++ b/solution.py
@@ -1,7 +1,11 @@
 import jax
 import jax.numpy as jnp
 from jax import lax
+from jax.experimental import pallas as pl
+from jax.experimental.pallas import tpu as pltpu
 from jax.sharding import PartitionSpec as P
+
+LANES = 128
 
 
 def by_rows(first_op, second_op):
@@ -36,6 +40,117 @@
         piece = jnp.where(lane < channels - offset, tap(first_tap + step), tap(first_tap + step + 1))
         pieces.append(piece[..., : min(channels, width - at)])
     return jnp.concatenate(pieces, axis=3).reshape(-1, width)
+
+
+def products_kernel(n_pair, first, *refs):
+    place = refs[0]
+    image_refs = refs[1 : 1 + 2 * n_pair]
+    strip_refs = refs[1 + 2 * n_pair : 1 + 3 * n_pair]
+    refs = refs[1 + 3 * n_pair :]
+    before, refs = (None, refs) if first else (refs[:4], refs[4:])
+    totals, (shifted, turned, left) = refs[:4], refs[4:]
+    n_images, side, channels = len(image_refs), image_refs[0].shape[1], image_refs[0].shape[3]
+    spots = side * side
+    cols, rows = totals[0].shape
+    strip = totals[1].shape[0]
+    fsdp_at = place[2]
+
+    spot = lax.broadcasted_iota(jnp.int32, (spots, LANES), 0) % side
+    empty = jnp.zeros((side, channels), jnp.bfloat16)
+    for at, ref in enumerate(image_refs):
+        for col_off in range(3):
+            shifted[col_off, at, 0] = empty
+            shifted[col_off, at, side + 1] = empty
+        shifted[1, at, 1 : side + 1] = ref[0]
+        for lane in range(0, channels, LANES):
+            part = ref[0, :, :, lane : lane + LANES].reshape(spots, LANES).astype(jnp.float32)
+            before_it = jnp.where(spot == 0, 0.0, pltpu.roll(part, 1, 0))
+            after_it = jnp.where(spot == side - 1, 0.0, pltpu.roll(part, spots - 1, 0))
+            for col_off, moved_part in ((0, before_it), (2, after_it)):
+                shifted[col_off, at, 1 : side + 1, :, lane : lane + LANES] = moved_part.astype(
+                    jnp.bfloat16
+                ).reshape(side, side, LANES)
+
+    def lanes_of_tap(tap, lane):
+        piece = shifted[tap % 3, :, pl.ds(tap // 3, side), :, pl.ds(pl.multiple_of(lane, LANES), LANES)]
+        return piece.reshape(n_images * spots, LANES)
+
+    first_tap = (fsdp_at * cols) // channels
+    for step in range(2):
+        tap = jnp.minimum(first_tap + step, 8)
+        for lane in range(0, channels, LANES):
+            turned[step, lane : lane + LANES, :] = lanes_of_tap(tap, lane).T
+    for at in range(cols // strip):
+        start = fsdp_at * cols + at * strip
+        left[at * strip : (at + 1) * strip, :] = turned[
+            start // channels - first_tap, pl.ds(pl.multiple_of(start % channels, strip), strip), :
+        ]
+    for far in range(2):
+        for pair in range(n_pair):
+            at = far * n_pair + pair
+            left[cols : cols + strip, at * spots : (at + 1) * spots] = strip_refs[pair][place[3 + far]]
+
+    tiles_per = rows // LANES
+
+    def lanes_at(index):
+        whose = jnp.where(index >= tiles_per, 1, 0)
+        start = (place[whose] * tiles_per + index - whose * tiles_per) * LANES
+        return lanes_of_tap(start // channels, start % channels)
+
+    def product(first_index, count):
+        right = jnp.concatenate([lanes_at(first_index + k) for k in range(count)], axis=1)
+        return jnp.dot(left[...], right, preferred_element_type=jnp.float32)
+
+    def keep(whose, lane, count, value):
+        at = pl.ds(pl.multiple_of(lane, LANES), count * LANES)
+        for kind, part in ((0, value[:cols]), (1, value[cols:])):
+            if not first:
+                part = part + before[2 * whose + kind][:, at]
+            totals[2 * whose + kind][:, at] = part
+
+    half = tiles_per // 2
+
+    @pl.loop(0, half)
+    def _(step):
+        keep(0, step * 2 * LANES, 2, product(2 * step, 2))
+
+    if tiles_per % 2:
+        both = product(2 * half, 2)
+        keep(0, 2 * half * LANES, 1, both[:, :LANES])
+        keep(1, 0, 1, both[:, LANES:])
+
+    odd = tiles_per % 2
+
+    @pl.loop(0, half)
+    def _(step):
+        keep(1, (odd + 2 * step) * LANES, 2, product(tiles_per + odd + 2 * step, 2))
+
+
+def add_products(place, images, strips, before, cols, rows):
+    n_images, channels, strip = len(images), images[0].shape[3], strips[0].shape[1]
+    spots = images[0].shape[1] * images[0].shape[2]
+    shapes = [jax.ShapeDtypeStruct((height, rows), jnp.float32) for height in (cols, strip)] * 2
+    whole = pl.BlockSpec(memory_space=pltpu.VMEM)
+    operands = [place, *images, *strips, *(before or [])]
+    n_front = 1 + n_images + len(strips)
+    return pl.pallas_call(
+        lambda *refs: products_kernel(len(strips), before is None, *refs),
+        out_shape=shapes,
+        in_specs=[pl.BlockSpec(memory_space=pltpu.SMEM)] + [whole] * (len(operands) - 1),
+        out_specs=[whole] * 4,
+        scratch_shapes=[
+            pltpu.VMEM((3, n_images, images[0].shape[1] + 2, images[0].shape[2], channels), jnp.bfloat16),
+            pltpu.VMEM((2, channels, n_images * spots), jnp.bfloat16),
+            pltpu.VMEM((cols + strip, n_images * spots), jnp.bfloat16),
+        ],
+        input_output_aliases={} if before is None else {n_front + k: k for k in range(4)},
+        compiler_params=pltpu.CompilerParams(vmem_limit_bytes=40 * 1024 * 1024),
+        cost_estimate=pl.CostEstimate(
+            flops=4 * (cols + strip) * rows * n_images * spots,
+            bytes_accessed=4 * 4 * (cols + strip) * rows,
+            transcendentals=0,
+        ),
+    )(*operands)
 
 
 def per_device(activations, cotangent, weight, a_factor_old, g_factor_old, a_inverse, g_inverse):
@@ -67,8 +182,8 @@
     strips_by_pair = [strips] + [over_pair(strips, step) for step in range(1, n_pair)]
 
     layers = [activations] + [over_layer(activations, step) for step in range(1, n_layer)]
-    cov_pair = jnp.zeros((cols, 2 * rows), jnp.float32)
-    grad_pair = jnp.zeros((strip, 2 * rows), jnp.float32)
+    aligned = rows % LANES == 0 and channels % LANES == 0 and activations.shape[0] == 1
+    totals = None
     group_images = []
     for step, layer in enumerate(layers):
         near = [layer] + [over_pair(layer, pair) for pair in range(1, n_pair)]
@@ -79,28 +194,30 @@
             far = [over_side(image) for image in near]
         if step == 0:
             group_images = near
+        owner = (fsdp_at - 2 * step) % n_fsdp
+        if aligned:
+            place = jnp.stack([factor_at ^ 1, factor_at, fsdp_at, owner, owner ^ 1])
+            totals = add_products(place, near + far, strips_by_pair, totals, cols, rows)
+            continue
         images = jnp.concatenate(near + far, axis=0)
-        row_tile = tile_of_patches(images, pair_at * (2 * rows), 2 * rows)
         col_tile = tile_of_patches(images, fsdp_at * cols, cols)
-        owner = (fsdp_at - 2 * step) % n_fsdp
-        cot_list = [
-            lax.dynamic_index_in_dim(strips_by_pair[pair], which, 0, keepdims=False)
-            for which in (owner, owner ^ 1)
-            for pair in range(n_pair)
-        ]
-        cov_pair = cov_pair + by_rows(col_tile, row_tile)
-        grad_pair = grad_pair + jnp.dot(
-            jnp.concatenate(cot_list, axis=1), row_tile, preferred_element_type=jnp.float32
+        cot_tile = jnp.concatenate(
+            [
+                lax.dynamic_index_in_dim(strips_by_pair[pair], which, 0, keepdims=False)
+                for which in (owner, owner ^ 1)
+                for pair in range(n_pair)
+            ],
+            axis=1,
         )
-
-    def own_half(array):
-        halves = array.reshape(array.shape[0], 2, rows)
-        mine = lax.dynamic_index_in_dim(halves, core_at, 1, keepdims=False)
-        theirs = lax.dynamic_index_in_dim(halves, 1 - core_at, 1, keepdims=False)
-        return mine + over_core(theirs)
-
-    grad_own = own_half(grad_pair)
-    cov_own = own_half(cov_pair)
+        more = []
+        for tile in (factor_at ^ 1, factor_at):
+            row_tile = tile_of_patches(images, tile * rows, rows)
+            more.append(by_rows(col_tile, row_tile))
+            more.append(jnp.dot(cot_tile, row_tile, preferred_element_type=jnp.float32))
+        totals = more if totals is None else [total + new for total, new in zip(totals, more)]
+
+    grad_own = totals[3] + over_core(totals[1])
+    cov_own = totals[2] + over_core(totals[0])
     pixel_total = float(
         activations.shape[0] * activations.shape[1] * activations.shape[2] * n_fsdp * n_factor
     )
@@ -111,7 +228,18 @@
     grad_cols = jnp.concatenate([near_grads, over_side(near_grads)], axis=0)
     came_from = (fsdp_at - 2 * jnp.arange(n_layer)) % n_fsdp
     came_from = jnp.concatenate([came_from, came_from ^ 1])
-    inverse_rows = g_inverse.reshape(n_fsdp, strip, channels)[came_from].reshape(channels, channels)
+    order = [
+        (2 * ((pair_at + step) % n_pair) + (core_at + other) % 2) * block
+        for other in (1, 0)
+        for step in range(n_pair)
+    ]
+    inverse = jnp.concatenate(
+        [lax.dynamic_slice_in_dim(g_inverse, at, block, 1) for at in order], axis=1
+    )
+    inverse = inverse.reshape(n_fsdp, strip, channels)
+    inverse = jnp.concatenate(
+        [lax.dynamic_index_in_dim(inverse, came_from[at], 0, keepdims=False) for at in range(n_fsdp)]
+    )
     partial = lax.dot_general(
         a_inverse,
         grad_cols,
@@ -120,16 +248,12 @@
         preferred_element_type=jnp.float32,
     )
     partial = jnp.dot(
-        partial, inverse_rows, precision=lax.Precision.HIGH, preferred_element_type=jnp.float32
-    )
-    by_block = partial.reshape(-1, n_pair, 2, block)
-    mine = lax.dynamic_index_in_dim(by_block, core_at, 2, keepdims=False)
-    theirs = lax.dynamic_index_in_dim(by_block, 1 - core_at, 2, keepdims=False)
-    by_pair = mine + over_core(theirs)
-    result = lax.dynamic_index_in_dim(by_pair, pair_at, 1, keepdims=False)
+        partial, inverse, precision=lax.Precision.HIGH, preferred_element_type=jnp.float32
+    )
+    by_pair = partial[:, channels // 2 :] + over_core(partial[:, : channels // 2])
+    result = by_pair[:, :block]
     for step in range(1, n_pair):
-        away = lax.dynamic_index_in_dim(by_pair, (pair_at + step) % n_pair, 1, keepdims=False)
-        result = result + over_pair(away, step)
+        result = result + over_pair(by_pair[:, step * block : (step + 1) * block], step)
     natural_grad = result.astype(jnp.bfloat16)
 
     weight_part = lax.dynamic_slice_in_dim(weight, factor_at * block, block, 1)
@@ -168,10 +292,18 @@
         axis=3,
     )
 
-    g_partial = lax.psum_scatter(
-        by_rows(own_cot, own_cot), "factor", scatter_dimension=0, tiled=True
-    )
-    g_factor = 0.5 * g_factor_old + 0.5 * lax.psum(g_partial, "fsdp")
+    g_partial = [
+        by_rows(lax.dynamic_slice_in_dim(own_cot, at, block, 1), own_cot) for at in order
+    ]
+    g_pairs = jnp.concatenate(g_partial[n_pair:]) + over_core(jnp.concatenate(g_partial[:n_pair]))
+    g_sum = g_pairs[:block]
+    for step in range(1, n_pair):
+        g_sum = g_sum + over_pair(g_pairs[step * block : (step + 1) * block], step)
+    distance = 1
+    while distance < n_fsdp:
+        g_sum = g_sum + moved(g_sum, "fsdp", lambda at, d=distance: at ^ d)
+        distance *= 2
+    g_factor = 0.5 * g_factor_old + 0.5 * g_sum
     return (conv_out, a_factor, g_factor, natural_grad)
 
 

time: 339 us -> 227 us (0.67)
  the two profiles are of different devices: /device:TPU:0 before, /device:TPU:10 now
where the time goes in v2:
time: 227 us; the launch traced here: 226 us
  waiting for transfers between devices  62.6 us (28%)
  Pallas kernels  32.2 us (14%)
  starting transfers between devices  31.5 us (14%)
  between operations  30.2 us (13%)
  local copies, waits for them, and re-layouts  29.6 us (13%)
  other arithmetic  20 us (9%)
  matrix products  19.8 us (9%)
    ppermute x33, waiting for transfers between devices, moved(): lax.ppermute(array, axis, [(at, target(at) % count) for at in range(count)])  62.6 us
    pallas_call x4, Pallas kernels, add_products(): pl.pallas_call(lambda *refs: products_kernel(len(strips), before is None,...  32.2 us
    ppermute x33, starting transfers between devices, moved(): lax.ppermute(array, axis, [(at, target(at) % count) for at in range(count)])  25.4 us
    unnamed x35, local copies, waits for them, and re-layouts  17.8 us
    all_to_all x1, starting transfers between devices, per_device(): lax.all_to_all(own_cot.T.reshape(n_fsdp, strip, own_cot.shape[0]), 'fsdp'...  6.06 us
    dot_general x4, matrix products, by_rows(): lax.dot_general(first_op, second_op, (((0,), (0,)), ((), ())), preferred_...  6.06 us
    conv_general_dilated x1, matrix products, per_device(): lax.conv_general_dilated(jnp.concatenate([near_images, over_core(near_ima...  6.05 us
    dot_general x1, matrix products, per_device(): lax.dot_general(a_inverse, grad_cols, (((1,), (1,)), ((), ())), precision...  4.96 us
  transfers between devices with their start and end apart: 35, of which 12 were waited for; matrix products, arithmetic and copies ran while one was open for 29% of the time, Pallas kernels for 14%

profile of v2, /device:TPU:10, one launch (start us, length us, event | category | flops | bytes accessed | tf_op | source)
XLA Modules:
  0.0 225.9 jit_solution(13794188570352659181)
XLA Ops:
  7.2 1.6 collective-permute-start
  9.3 1.6 collective-permute-start.14
  10.9 1.2 collective-permute-start.10
  12.1 1.8 copy.35
  13.9 6.1 %all-to-all-start = ((bf16[8,64,256]{2,1,0:T(8,128)(2,1)}), bf16[8,64,256]{2,1,0:T(8,128)(2,1)S(1)}, u32[]{:S(2)}, u32[]{:S(2)}) async-start(bf16[8,64,256]{2,1,0:T(8,128)(2,1)} %bitcast.99), calls=%async_computation | async-start | bytes 524288 | tf_op jit(solution)/shard_map/all_to_all | solution.py:179
  20.0 1.9 fusion.12
  21.9 1.2 fusion.14
  23.2 1.8 pad_maximum_fusion.3
  24.9 1.6 constant_dynamic-slice_fusion.8
  31.2 0.9 fusion.16
  32.1 2.3 constant_dynamic-slice_fusion.3
  35.1 2.3 %pad_maximum_fusion.1 = f32[512,512]{1,0:T(8,128)} fusion(f32[512,128]{1,0:T(8,128)} %get-tuple-element.40, f32[512,128]{1,0:T(8,128)} %get-tuple-element.41, f32[512,128]{1,0:T(8,128)} %get-tuple-element.39, f32[512,128]{1,0:T(8,128)} %get-tuple-element.38), kind=kLoop, calls=%fused_computation.11 | loop fusion | flops 786432 | bytes 2097152 | tf_op jit(solution)/shard_map/concatenate | solution.py:236
  37.4 1.6 bitcast_dynamic-update-slice_fusion.7
  39.6 1.6 bitcast_dynamic-update-slice_fusion.6
  41.8 1.6 bitcast_dynamic-update-slice_fusion.5
  48.2 1.6 bitcast_dynamic-update-slice_fusion.4
  49.7 1.6 bitcast_dynamic-update-slice_fusion.3
  53.2 2.0 fusion.18
  56.2 1.5 collective-permute-start.15
  58.3 1.6 bitcast_dynamic-update-slice_fusion.2
  62.2 1.3 maximum_add_fusion
  63.8 6.0 %collective-permute-done.5.refs_1_ = bf16[1,16,16,512]{3,2,1,0:T(8,128)(2,1)} collective-permute-done((bf16[1,16,16,512]{3,2,1,0:T(8,128)(2,1)S(1)}, bf16[1,16,16,512]{3,2,1,0:T(8,128)(2,1)}, u32[]{:S(2)}, u32[]{:S(2)}) %collective-permute-start.5) | collective-permute-done | bytes 262176 | tf_op jit(solution)/shard_map/ppermute | solution.py:19
  70.4 1.1 collective-permute-start.11
  71.5 0.9 collective-permute-start.6
  72.5 3.9 %collective-permute-done.9.refs_6_ = bf16[8,64,256]{2,1,0:T(8,128)(2,1)} collective-permute-done((bf16[8,64,256]{2,1,0:T(8,128)(2,1)S(1)}, bf16[8,64,256]{2,1,0:T(8,128)(2,1)}, u32[]{:S(2)}, u32[]{:S(2)}) %collective-permute-start.9) | collective-permute-done | bytes 262176 | tf_op jit(solution)/shard_map/ppermute | solution.py:19
  76.6 0.9 copy-done.5
  77.6 8.1 %shard_map.102 = (f32[576,1152]{1,0:T(8,128)S(1)}, f32[64,1152]{1,0:T(8,128)}, f32[576,1152]{1,0:T(8,128)S(1)}, f32[64,1152]{1,0:T(8,128)S(1)}) custom-call(s32[5]{0:T(128)S(1)} %stack.84.refs_0_, bf16[1,16,16,512]{3,2,1,0:T(8,128)(2,1)S(1)} %copy-done.3, bf16[1,16,16,512]{3,2,1,0:T(8,128)(2,1)S(1)} %collective-permute-done.refs_2_, ...), custom_call_target="tpu_custom_call" | custom-call | flops 3019898880 | bytes 11796480 | tf_op jit(solution)/shard_map/pallas_call | solution.py:136
  85.7 1.8 collective-permute-start.7
  88.0 1.5 collective-permute-start.13
  89.7 8.1 %shard_map.103 = (f32[576,1152]{1,0:T(8,128)S(1)}, f32[64,1152]{1,0:T(8,128)}, f32[576,1152]{1,0:T(8,128)S(1)}, f32[64,1152]{1,0:T(8,128)S(1)}) custom-call(s32[5]{0:T(128)S(1)} %stack.81.refs_0_, bf16[1,16,16,512]{3,2,1,0:T(8,128)(2,1)} %collective-permute-done.14.refs_1_, ...), custom_call_target="tpu_custom_call", output_to_operand_aliasing={{0}: (7, {}), {1}: (8, {}), {2}: (9, {}), {3}: (10, {})} | custom-call | flops 3019898880 | bytes 11796480 | tf_op jit(solution)/shard_map/pallas_call | solution.py:136
  97.8 1.5 collective-permute-done.13.refs_4_
  99.4 8.0 %shard_map.104 = (f32[576,1152]{1,0:T(8,128)S(1)}, f32[64,1152]{1,0:T(8,128)}, f32[576,1152]{1,0:T(8,128)S(1)}, f32[64,1152]{1,0:T(8,128)S(1)}) custom-call(s32[5]{0:T(128)S(1)} %stack.78.refs_0_, bf16[1,16,16,512]{3,2,1,0:T(8,128)(2,1)} %collective-permute-done.10.refs_1_, ...), custom_call_target="tpu_custom_call", output_to_operand_aliasing={{0}: (7, {}), {1}: (8, {}), {2}: (9, {}), {3}: (10, {})} | custom-call | flops 3019898880 | bytes 11796480 | tf_op jit(solution)/shard_map/pallas_call | solution.py:136
  107.4 8.0 %shard_map.105 = (f32[576,1152]{1,0:T(8,128)S(1)}, f32[64,1152]{1,0:T(8,128)}, f32[576,1152]{1,0:T(8,128)S(1)}, f32[64,1152]{1,0:T(8,128)S(1)}) custom-call(s32[5]{0:T(128)S(1)} %stack.75.refs_0_, bf16[1,16,16,512]{3,2,1,0:T(8,128)(2,1)} %collective-permute-done.5.refs_1_, ...), custom_call_target="tpu_custom_call", output_to_operand_aliasing={{0}: (7, {}), {1}: (8, {}), {2}: (9, {}), {3}: (10, {})} | custom-call | flops 3019898880 | bytes 11796480 | tf_op jit(solution)/shard_map/pallas_call | solution.py:136
  115.4 1.5 copy-done.1
  116.9 1.5 copy-done.7
  118.4 0.7 slice_add_fusion.2
  119.7 1.6 bitcast_dynamic-update-slice_fusion.1
  123.2 0.9 pad_maximum_fusion.2
  124.3 1.6 bitcast_dynamic-update-slice_fusion
  126.1 2.1 collective-permute-done.23
  128.2 1.1 add.222
  129.2 3.4 %collective-permute-start.24 = (f32[128,512]{1,0:T(8,128)S(1)}, f32[128,512]{1,0:T(8,128)S(1)}, u32[]{:S(2)}, u32[]{:S(2)}) collective-permute-start(f32[128,512]{1,0:T(8,128)S(1)} %add.222), channel_id=1, source_target_pairs={{0,8},{4,12},{8,0},{12,4},{16,24},{20,28},{24,16},{28,20},{1,9},{5... | collective-permute-start | bytes 786440 | tf_op jit(solution)/shard_map/ppermute | solution.py:19
  132.6 1.7 constant_dynamic-update-slice_fusion.4
  134.4 2.4 %collective-permute-start.28 = (f32[64,1152]{1,0:T(8,128)S(1)}, f32[64,1152]{1,0:T(8,128)S(1)}, u32[]{:S(2)}, u32[]{:S(2)}) collective-permute-start(f32[64,1152]{1,0:T(8,128)S(1)} %get-tuple-element.37), channel_id=1, source_target_pairs={{0,16},{4,20},{8,24},{12,28},{16,0},{20,4},{24,8},{28,12},{1,17},{... | collective-permute-start | bytes 884744 | tf_op jit(solution)/shard_map/ppermute | solution.py:19
  136.8 1.1 maximum_bitcast_fusion
  138.8 1.9 fusion.1
  140.6 5.8 %collective-permute-done.24 = f32[128,512]{1,0:T(8,128)S(1)} collective-permute-done((f32[128,512]{1,0:T(8,128)S(1)}, f32[128,512]{1,0:T(8,128)S(1)}, u32[]{:S(2)}, u32[]{:S(2)}) %collective-permute-start.24) | collective-permute-done | bytes 262176 | tf_op jit(solution)/shard_map/ppermute | solution.py:19
  146.6 19.9 %collective-permute-done.28 = f32[64,1152]{1,0:T(8,128)S(1)} collective-permute-done((f32[64,1152]{1,0:T(8,128)S(1)}, f32[64,1152]{1,0:T(8,128)S(1)}, u32[]{:S(2)}, u32[]{:S(2)}) %collective-permute-start.28) | collective-permute-done | bytes 294944 | tf_op jit(solution)/shard_map/ppermute | solution.py:19
  166.4 2.7 %collective-permute-done.29 = f32[64,1152]{1,0:T(8,128)S(1)} collective-permute-done((f32[64,1152]{1,0:T(8,128)S(1)}, f32[64,1152]{1,0:T(8,128)S(1)}, u32[]{:S(2)}, u32[]{:S(2)}) %collective-permute-start.29) | collective-permute-done | bytes 294944 | tf_op jit(solution)/shard_map/ppermute | solution.py:19
  169.2 1.1 pad_maximum_fusion
  170.8 0.8 constant_dynamic-update-slice_fusion.3
  172.3 0.7 constant_dynamic-update-slice_fusion.1
  173.1 6.0 %fusion.8 = bf16[16,32,3,128]{3,1,2,0:T(8,128)(2,1)S(1)} fusion(bf16[3,3,512,128]{3,2,1,0:T(8,128)(2,1)} %bitcast.103, bf16[16,4,8,5,512]{4,0,3,2,1:T(8,128)(2,1)} %fusion.1, pred[32,3]{0,1:T(4,128)(4,1)S(1)} %copy-done.11), kind=kOutput, calls=%fused_computation.8 | convolution fusion | flops 1736835072 | bytes 4194400 | tf_op jit(solution)/shard_map/conv_general_dilated | solution.py:262
  180.1 1.3 collective-permute-start.4
  181.4 0.8 add_multiply_fusion
  182.1 2.3 collective-permute-done.3
  184.9 12.0 %collective-permute-done.30 = f32[256,1152]{1,0:T(8,128)} collective-permute-done((f32[256,1152]{1,0:T(8,128)}, f32[256,1152]{1,0:T(8,128)}, u32[]{:S(2)}, u32[]{:S(2)}) %collective-permute-start.30) | collective-permute-done | bytes 1179680 | tf_op jit(solution)/shard_map/ppermute | solution.py:19
  196.9 2.4 %constant_dynamic-update-slice_fusion = f32[512,1152]{1,0:T(8,128)} fusion(f32[512,1152]{1,0:T(8,128)} %constant_dynamic-update-slice_fusion.1, f32[256,1152]{1,0:T(8,128)} %collective-permute-done.30), kind=kLoop, calls=%fused_computation.46 | loop fusion | bytes 2359296 | tf_op jit(solution)/shard_map/concatenate | solution.py:228
  199.3 5.0 %fusion.27 = f32[512,576]{1,0:T(8,128)S(1)} fusion(f32[512,1152]{1,0:T(8,128)} %constant_dynamic-update-slice_fusion, f32[576,1152]{1,0:T(8,128)S(1)} %copy-done), kind=kOutput, calls=%fused_computation.71 | convolution fusion | flops 2038431744 | bytes 6193152 | tf_op jit(solution)/shard_map/dot_general | solution.py:243
  204.3 2.7 %fusion.28 = f32[576,512]{1,0:T(8,128)S(1)} fusion(f32[512,576]{1,0:T(8,128)S(1)} %fusion.27, f32[512,512]{1,0:T(8,128)} %bitcast_dynamic-update-slice_fusion), kind=kOutput, calls=%fused_computation.72 | convolution fusion | flops 905969664 | bytes 3407872 | tf_op jit(solution)/shard_map/dot_general | solution.py:250
  207.2 0.7 pad_maximum_fusion.5
  208.0 1.1 collective-permute-done.31
  209.8 3.8 %bitcast_add_fusion = f32[1152,576]{0,1:T(8,128)} fusion(f32[576,1152]{1,0:T(8,128)S(1)} %copy-done.2, f32[576,1152]{1,0:T(8,128)} %collective-permute-done.20, f32[1152,576]{0,1:T(8,128)S(1)} %copy-done.9), kind=kLoop, calls=%fused_computation.2 | loop fusion | flops 2654208 | bytes 10616832 | tf_op jit(solution)/shard_map/add | solution.py:224
  213.7 4.7 %collective-permute-done.32 = f32[576,128]{1,0:T(8,128)S(1)} collective-permute-done((f32[576,128]{1,0:T(8,128)S(1)}, f32[576,128]{1,0:T(8,128)S(1)}, u32[]{:S(2)}, u32[]{:S(2)}) %collective-permute-start.32) | collective-permute-done | bytes 294944 | tf_op jit(solution)/shard_map/ppermute | solution.py:19
  (94 shorter events, 12.1 us)
Async XLA Ops:
  7.2 192.1 %copy-start = (f32[576,1152]{1,0:T(8,128)S(1)}, f32[576,1152]{1,0:T(8,128)}, u32[]{:S(2)}) copy-start(f32[576,1152]{1,0:T(8,128)} %param.12) | copy-start | bytes 7962628
  7.2 24.0 %copy-start.8 = (bf16[1,16,16,512]{3,2,1,0:T(8,128)(2,1)S(1)}, bf16[1,16,16,512]{3,2,1,0:T(8,128)(2,1)}, u32[]{:S(2)}) copy-start(bf16[1,16,16,512]{3,2,1,0:T(8,128)(2,1)} %param.8) | copy-start | bytes 786436
  7.2 48.0 %collective-permute-start = (bf16[1,16,16,512]{3,2,1,0:T(8,128)(2,1)}, bf16[1,16,16,512]{3,2,1,0:T(8,128)(2,1)S(1)}, u32[]{:S(2)}, u32[]{:S(2)}) collective-permute-start(bf16[1,16,16,512]{3,2,1,0:T(8,128)(2,1)} %refs_1_.1), channel_id=1, source_target_pairs={{0,2},{1,3},{2,0},{3,1},{4,6},{5,7},{6,4},{7,5},{8,10},{9,11},{10,... | collective-permute-start | bytes 786440 | tf_op jit(solution)/shard_map/ppermute | solution.py:19
  8.8 46.9 %collective-permute-start.18 = (bf16[1,16,16,512]{3,2,1,0:T(8,128)(2,1)}, bf16[1,16,16,512]{3,2,1,0:T(8,128)(2,1)}, u32[]{:S(2)}, u32[]{:S(2)}) collective-permute-start(bf16[1,16,16,512]{3,2,1,0:T(8,128)(2,1)} %refs_1_.1), channel_id=1, source_target_pairs={{0,4},{4,0},{8,12},{12,8},{16,20},{20,16},{24,28},{28,24},{1,5},{5... | collective-permute-start | bytes 786440 | tf_op jit(solution)/shard_map/ppermute | solution.py:19
  9.3 46.9 %collective-permute-start.14 = (bf16[1,16,16,512]{3,2,1,0:T(8,128)(2,1)}, bf16[1,16,16,512]{3,2,1,0:T(8,128)(2,1)}, u32[]{:S(2)}, u32[]{:S(2)}) collective-permute-start(bf16[1,16,16,512]{3,2,1,0:T(8,128)(2,1)} %refs_1_.1), channel_id=1, source_target_pairs={{0,8},{4,12},{8,16},{12,20},{16,24},{20,28},{24,0},{28,4},{1,9},{5... | collective-permute-start | bytes 786440 | tf_op jit(solution)/shard_map/ppermute | solution.py:19
  10.9 52.6 %collective-permute-start.10 = (bf16[1,16,16,512]{3,2,1,0:T(8,128)(2,1)}, bf16[1,16,16,512]{3,2,1,0:T(8,128)(2,1)}, u32[]{:S(2)}, u32[]{:S(2)}) collective-permute-start(bf16[1,16,16,512]{3,2,1,0:T(8,128)(2,1)} %refs_1_.1), channel_id=1, source_target_pairs={{0,16},{4,20},{8,24},{12,28},{16,0},{20,4},{24,8},{28,12},{1,17},{... | collective-permute-start | bytes 786440 | tf_op jit(solution)/shard_map/ppermute | solution.py:19
  13.9 43.8 %all-to-all-start = ((bf16[8,64,256]{2,1,0:T(8,128)(2,1)}), bf16[8,64,256]{2,1,0:T(8,128)(2,1)S(1)}, u32[]{:S(2)}, u32[]{:S(2)}) async-start(bf16[8,64,256]{2,1,0:T(8,128)(2,1)} %bitcast.99), calls=%async_computation | async-start | bytes 524288 | tf_op jit(solution)/shard_map/all_to_all | solution.py:179
  20.0 153.1 %all-gather.2.cloned.1.call-start = ((), (), s32[]{:S(2)}) async-start(), calls=%async_computation.1 | async-start | bytes 1327104 | tf_op jit(solution)/shard_map/all_gather | solution.py:260
  24.9 32.8 %collective-permute-start.21 = (f32[256,512]{1,0:T(8,128)}, f32[256,512]{1,0:T(8,128)}, u32[]{:S(2)}, u32[]{:S(2)}) collective-permute-start(f32[256,512]{1,0:T(8,128)} %pad_maximum_fusion.3), channel_id=1, source_target_pairs={{0,1},{1,0},{2,3},{3,2},{4,5},{5,4},{6,7},{7,6},{8,9},{9,8},{10,11... | collective-permute-start | bytes 1572872 | tf_op jit(solution)/shard_map/ppermute | solution.py:19
  34.4 20.8 %copy-start.3 = (bf16[1,16,16,512]{3,2,1,0:T(8,128)(2,1)S(1)}, bf16[1,16,16,512]{3,2,1,0:T(8,128)(2,1)}, u32[]{:S(2)}) copy-start(bf16[1,16,16,512]{3,2,1,0:T(8,128)(2,1)} %refs_1_.1) | copy-start | bytes 786436
  55.2 14.7 %collective-permute-start.5 = (bf16[1,16,16,512]{3,2,1,0:T(8,128)(2,1)S(1)}, bf16[1,16,16,512]{3,2,1,0:T(8,128)(2,1)}, u32[]{:S(2)}, u32[]{:S(2)}) collective-permute-start(bf16[1,16,16,512]{3,2,1,0:T(8,128)(2,1)S(1)} %copy-done.3), channel_id=1, source_target_pairs={{0,24},{4,28},{8,0},{12,4},{16,8},{20,12},{24,16},{28,20},{1,25},{... | collective-permute-start | bytes 786440 | tf_op jit(solution)/shard_map/ppermute | solution.py:19
  55.7 14.7 %collective-permute-start.19 = (bf16[1,16,16,512]{3,2,1,0:T(8,128)(2,1)}, bf16[1,16,16,512]{3,2,1,0:T(8,128)(2,1)}, u32[]{:S(2)}, u32[]{:S(2)}) collective-permute-start(bf16[1,16,16,512]{3,2,1,0:T(8,128)(2,1)} %collective-permute-done.18.refs_3_), channel_id=1, source_target_pairs={{0,2},{1,3},{2,0},{3,1},{4,6},{5,7},{6,4},{7,5},{8,10},{9,11},{10,... | collective-permute-start | bytes 786440 | tf_op jit(solution)/shard_map/ppermute | solution.py:19
  56.2 15.3 %collective-permute-start.15 = (bf16[1,16,16,512]{3,2,1,0:T(8,128)(2,1)}, bf16[1,16,16,512]{3,2,1,0:T(8,128)(2,1)}, u32[]{:S(2)}, u32[]{:S(2)}) collective-permute-start(bf16[1,16,16,512]{3,2,1,0:T(8,128)(2,1)} %collective-permute-done.14.refs_1_), channel_id=1, source_target_pairs={{0,2},{1,3},{2,0},{3,1},{4,6},{5,7},{6,4},{7,5},{8,10},{9,11},{10,... | collective-permute-start | bytes 786440 | tf_op jit(solution)/shard_map/ppermute | solution.py:19
  57.8 18.7 %copy-start.4 = (bf16[8,64,256]{2,1,0:T(8,128)(2,1)}, bf16[8,64,256]{2,1,0:T(8,128)(2,1)S(1)}, u32[]{:S(2)}) copy-start(bf16[8,64,256]{2,1,0:T(8,128)(2,1)S(1)} %all-to-all-done.refs_5_) | copy-start | bytes 786436
  57.8 18.7 %collective-permute-start.9 = (bf16[8,64,256]{2,1,0:T(8,128)(2,1)S(1)}, bf16[8,64,256]{2,1,0:T(8,128)(2,1)}, u32[]{:S(2)}, u32[]{:S(2)}) collective-permute-start(bf16[8,64,256]{2,1,0:T(8,128)(2,1)S(1)} %all-to-all-done.refs_5_), channel_id=1, source_target_pairs={{0,2},{1,3},{2,0},{3,1},{4,6},{5,7},{6,4},{7,5},{8,10},{9,11},{10,... | collective-permute-start | bytes 786440 | tf_op jit(solution)/shard_map/ppermute | solution.py:19
  63.5 22.2 %collective-permute-start.16 = (bf16[1,16,16,512]{3,2,1,0:T(8,128)(2,1)}, bf16[1,16,16,512]{3,2,1,0:T(8,128)(2,1)S(1)}, u32[]{:S(2)}, u32[]{:S(2)}) collective-permute-start(bf16[1,16,16,512]{3,2,1,0:T(8,128)(2,1)} %collective-permute-done.14.refs_1_), channel_id=1, source_target_pairs={{0,4},{4,0},{8,12},{12,8},{16,20},{20,16},{24,28},{28,24},{1,5},{5... | collective-permute-start | bytes 786440 | tf_op jit(solution)/shard_map/ppermute | solution.py:19
  69.9 17.6 %collective-permute-start.12 = (bf16[1,16,16,512]{3,2,1,0:T(8,128)(2,1)}, bf16[1,16,16,512]{3,2,1,0:T(8,128)(2,1)S(1)}, u32[]{:S(2)}, u32[]{:S(2)}) collective-permute-start(bf16[1,16,16,512]{3,2,1,0:T(8,128)(2,1)} %collective-permute-done.10.refs_1_), channel_id=1, source_target_pairs={{0,4},{4,0},{8,12},{12,8},{16,20},{20,16},{24,28},{28,24},{1,5},{5... | collective-permute-start | bytes 786440 | tf_op jit(solution)/shard_map/ppermute | solution.py:19
  70.4 27.4 %collective-permute-start.11 = (bf16[1,16,16,512]{3,2,1,0:T(8,128)(2,1)}, bf16[1,16,16,512]{3,2,1,0:T(8,128)(2,1)S(1)}, u32[]{:S(2)}, u32[]{:S(2)}) collective-permute-start(bf16[1,16,16,512]{3,2,1,0:T(8,128)(2,1)} %collective-permute-done.10.refs_1_), channel_id=1, source_target_pairs={{0,2},{1,3},{2,0},{3,1},{4,6},{5,7},{6,4},{7,5},{8,10},{9,11},{10,... | collective-permute-start | bytes 786440 | tf_op jit(solution)/shard_map/ppermute | solution.py:19
  71.5 16.4 %collective-permute-start.6 = (bf16[1,16,16,512]{3,2,1,0:T(8,128)(2,1)}, bf16[1,16,16,512]{3,2,1,0:T(8,128)(2,1)S(1)}, u32[]{:S(2)}, u32[]{:S(2)}) collective-permute-start(bf16[1,16,16,512]{3,2,1,0:T(8,128)(2,1)} %collective-permute-done.5.refs_1_), channel_id=1, source_target_pairs={{0,2},{1,3},{2,0},{3,1},{4,6},{5,7},{6,4},{7,5},{8,10},{9,11},{10,... | collective-permute-start | bytes 786440 | tf_op jit(solution)/shard_map/ppermute | solution.py:19
  76.4 13.1 %collective-permute-start.17 = (bf16[1,16,16,512]{3,2,1,0:T(8,128)(2,1)}, bf16[1,16,16,512]{3,2,1,0:T(8,128)(2,1)S(1)}, u32[]{:S(2)}, u32[]{:S(2)}) collective-permute-start(bf16[1,16,16,512]{3,2,1,0:T(8,128)(2,1)} %collective-permute-done.15.refs_2_), channel_id=1, source_target_pairs={{0,4},{4,0},{8,12},{12,8},{16,20},{20,16},{24,28},{28,24},{1,5},{5... | collective-permute-start | bytes 786440 | tf_op jit(solution)/shard_map/ppermute | solution.py:19
  76.6 0.9 copy-start.5
  77.6 12.2 %copy-start.6 = (bf16[8,64,256]{2,1,0:T(8,128)(2,1)S(1)}, bf16[8,64,256]{2,1,0:T(8,128)(2,1)}, u32[]{:S(2)}) copy-start(bf16[8,64,256]{2,1,0:T(8,128)(2,1)} %copy-done.4) | copy-start | bytes 786436
  85.7 21.7 %collective-permute-start.7 = (bf16[1,16,16,512]{3,2,1,0:T(8,128)(2,1)}, bf16[1,16,16,512]{3,2,1,0:T(8,128)(2,1)S(1)}, u32[]{:S(2)}, u32[]{:S(2)}) collective-permute-start(bf16[1,16,16,512]{3,2,1,0:T(8,128)(2,1)} %collective-permute-done.5.refs_1_), channel_id=1, source_target_pairs={{0,4},{4,0},{8,12},{12,8},{16,20},{20,16},{24,28},{28,24},{1,5},{5... | collective-permute-start | bytes 786440 | tf_op jit(solution)/shard_map/ppermute | solution.py:19
  87.5 30.9 %collective-permute-start.22 = (f32[128,512]{1,0:T(8,128)S(1)}, f32[128,512]{1,0:T(8,128)S(1)}, u32[]{:S(2)}, u32[]{:S(2)}) collective-permute-start(f32[128,512]{1,0:T(8,128)S(1)} %slice.81), channel_id=1, source_target_pairs={{0,2},{1,3},{2,0},{3,1},{4,6},{5,7},{6,4},{7,5},{8,10},{9,11},{10,... | collective-permute-start | bytes 786440 | tf_op jit(solution)/shard_map/ppermute | solution.py:19
  88.0 11.4 %collective-permute-start.13 = (bf16[1,16,16,512]{3,2,1,0:T(8,128)(2,1)S(1)}, bf16[1,16,16,512]{3,2,1,0:T(8,128)(2,1)S(1)}, u32[]{:S(2)}, u32[]{:S(2)}) collective-permute-start(bf16[1,16,16,512]{3,2,1,0:T(8,128)(2,1)S(1)} %collective-permute-done.12.refs_3_), channel_id=1, source_target_pairs={{0,2},{1,3},{2,0},{3,1},{4,6},{5,7},{6,4},{7,5},{8,10},{9,11},{10,... | collective-permute-start | bytes 786440 | tf_op jit(solution)/shard_map/ppermute | solution.py:19
  89.5 17.9 %collective-permute-start.8 = (bf16[1,16,16,512]{3,2,1,0:T(8,128)(2,1)S(1)}, bf16[1,16,16,512]{3,2,1,0:T(8,128)(2,1)S(1)}, u32[]{:S(2)}, u32[]{:S(2)}) collective-permute-start(bf16[1,16,16,512]{3,2,1,0:T(8,128)(2,1)S(1)} %collective-permute-done.6.refs_2_), channel_id=1, source_target_pairs={{0,4},{4,0},{8,12},{12,8},{16,20},{20,16},{24,28},{28,24},{1,5},{5... | collective-permute-start | bytes 786440 | tf_op jit(solution)/shard_map/ppermute | solution.py:19
  115.4 1.5 copy-start.1
  116.9 1.5 copy-start.7
  118.4 14.2 %collective-permute-start.26 = (f32[64,1152]{1,0:T(8,128)}, f32[64,1152]{1,0:T(8,128)}, u32[]{:S(2)}, u32[]{:S(2)}) collective-permute-start(f32[64,1152]{1,0:T(8,128)} %get-tuple-element.35), channel_id=1, source_target_pairs={{0,1},{1,0},{2,3},{3,2},{4,5},{5,4},{6,7},{7,6},{8,9},{9,8},{10,11... | collective-permute-start | bytes 884744 | tf_op jit(solution)/shard_map/ppermute | solution.py:19
  119.1 9.0 %collective-permute-start.23 = (f32[128,512]{1,0:T(8,128)}, f32[128,512]{1,0:T(8,128)}, u32[]{:S(2)}, u32[]{:S(2)}) collective-permute-start(f32[128,512]{1,0:T(8,128)} %slice_add_fusion.2), channel_id=1, source_target_pairs={{0,4},{4,0},{8,12},{12,8},{16,20},{20,16},{24,28},{28,24},{1,5},{5... | collective-permute-start | bytes 786440 | tf_op jit(solution)/shard_map/ppermute | solution.py:19
  124.0 12.7 %collective-permute-start.1 = (bf16[2,16,16,512]{3,2,1,0:T(8,128)(2,1)}, bf16[2,16,16,512]{3,2,1,0:T(8,128)(2,1)}, u32[]{:S(2)}, u32[]{:S(2)}) collective-permute-start(bf16[2,16,16,512]{3,2,1,0:T(8,128)(2,1)} %pad_maximum_fusion.2), channel_id=1, source_target_pairs={{0,1},{1,0},{2,3},{3,2},{4,5},{5,4},{6,7},{7,6},{8,9},{9,8},{10,11... | collective-permute-start | bytes 1572872 | tf_op jit(solution)/shard_map/ppermute | solution.py:19
  125.8 84.0 %collective-permute-start.20 = (f32[576,1152]{1,0:T(8,128)}, f32[576,1152]{1,0:T(8,128)}, u32[]{:S(2)}, u32[]{:S(2)}) collective-permute-start(f32[576,1152]{1,0:T(8,128)} %copy-done.7), channel_id=1, source_target_pairs={{0,1},{1,0},{2,3},{3,2},{4,5},{5,4},{6,7},{7,6},{8,9},{9,8},{10,11... | collective-permute-start | bytes 7962632 | tf_op jit(solution)/shard_map/ppermute | solution.py:19
  129.2 17.2 %collective-permute-start.24 = (f32[128,512]{1,0:T(8,128)S(1)}, f32[128,512]{1,0:T(8,128)S(1)}, u32[]{:S(2)}, u32[]{:S(2)}) collective-permute-start(f32[128,512]{1,0:T(8,128)S(1)} %add.222), channel_id=1, source_target_pairs={{0,8},{4,12},{8,0},{12,4},{16,24},{20,28},{24,16},{28,20},{1,9},{5... | collective-permute-start | bytes 786440 | tf_op jit(solution)/shard_map/ppermute | solution.py:19
  134.4 12.2 %collective-permute-start.27 = (f32[64,1152]{1,0:T(8,128)S(1)}, f32[64,1152]{1,0:T(8,128)S(1)}, u32[]{:S(2)}, u32[]{:S(2)}) collective-permute-start(f32[64,1152]{1,0:T(8,128)S(1)} %get-tuple-element.37), channel_id=1, source_target_pairs={{0,8},{4,12},{8,16},{12,20},{16,24},{20,28},{24,0},{28,4},{1,9},{5... | collective-permute-start | bytes 884744 | tf_op jit(solution)/shard_map/ppermute | solution.py:19
  134.4 32.1 %collective-permute-start.28 = (f32[64,1152]{1,0:T(8,128)S(1)}, f32[64,1152]{1,0:T(8,128)S(1)}, u32[]{:S(2)}, u32[]{:S(2)}) collective-permute-start(f32[64,1152]{1,0:T(8,128)S(1)} %get-tuple-element.37), channel_id=1, source_target_pairs={{0,16},{4,20},{8,24},{12,28},{16,0},{20,4},{24,8},{28,12},{1,17},{... | collective-permute-start | bytes 884744 | tf_op jit(solution)/shard_map/ppermute | solution.py:19
  136.8 32.4 %collective-permute-start.29 = (f32[64,1152]{1,0:T(8,128)S(1)}, f32[64,1152]{1,0:T(8,128)S(1)}, u32[]{:S(2)}, u32[]{:S(2)}) collective-permute-start(f32[64,1152]{1,0:T(8,128)S(1)} %get-tuple-element.37), channel_id=1, source_target_pairs={{0,24},{4,28},{8,0},{12,4},{16,8},{20,12},{24,16},{28,20},{1,25},{... | collective-permute-start | bytes 884744 | tf_op jit(solution)/shard_map/ppermute | solution.py:19
  140.6 32.4 %copy-start.11 = (pred[32,3]{0,1:T(4,128)(4,1)S(1)}, pred[32,3]{0,1:T(4,128)(4,1)}, u32[]{:S(2)}) copy-start(pred[32,3]{0,1:T(4,128)(4,1)} %constant.169) | copy-start | bytes 292
  146.5 33.6 %collective-permute-start.25 = (f32[128,512]{1,0:T(8,128)S(1)}, f32[128,512]{1,0:T(8,128)S(1)}, u32[]{:S(2)}, u32[]{:S(2)}) collective-permute-start(f32[128,512]{1,0:T(8,128)S(1)} %add.223), channel_id=1, source_target_pairs={{0,16},{4,20},{8,24},{12,28},{16,0},{20,4},{24,8},{28,12},{1,17},{... | collective-permute-start | bytes 786440 | tf_op jit(solution)/shard_map/ppermute | solution.py:19
  170.3 26.6 %collective-permute-start.30 = (f32[256,1152]{1,0:T(8,128)}, f32[256,1152]{1,0:T(8,128)}, u32[]{:S(2)}, u32[]{:S(2)}) collective-permute-start(f32[256,1152]{1,0:T(8,128)} %pad_maximum_fusion), channel_id=1, source_target_pairs={{0,4},{4,0},{8,12},{12,8},{16,20},{20,16},{24,28},{28,24},{1,5},{5... | collective-permute-start | bytes 3538952 | tf_op jit(solution)/shard_map/ppermute | solution.py:19
  173.1 8.3 %copy-start.10 = (f32[128,512]{1,0:T(8,128)S(1)}, f32[128,512]{1,0:T(8,128)}, u32[]{:S(2)}) copy-start(f32[128,512]{1,0:T(8,128)} %param.11) | copy-start | bytes 786436
  179.4 2.8 %collective-permute-start.2 = (bf16[1,16,16,128]{3,1,2,0:T(8,128)(2,1)S(1)}, bf16[1,16,16,128]{3,1,2,0:T(8,128)(2,1)S(1)}, u32[]{:S(2)}, u32[]{:S(2)}) collective-permute-start(bf16[1,16,16,128]{3,1,2,0:T(8,128)(2,1)S(1)} %get-tuple-element.48), channel_id=1, source_target_pairs={{0,1},{1,0},{2,3},{3,2},{4,5},{5,4},{6,7},{7,6},{8,9},{9,8},{10,11... | collective-permute-start | bytes 196616 | tf_op jit(solution)/shard_map/ppermute | solution.py:19
  179.4 5.0 %collective-permute-start.3 = (bf16[1,16,16,128]{3,1,2,0:T(8,128)(2,1)S(1)}, bf16[1,16,16,128]{3,1,2,0:T(8,128)(2,1)S(1)}, u32[]{:S(2)}, u32[]{:S(2)}) collective-permute-start(bf16[1,16,16,128]{3,1,2,0:T(8,128)(2,1)S(1)} %get-tuple-element.47), channel_id=1, source_target_pairs={{0,2},{1,3},{2,0},{3,1},{4,6},{5,7},{6,4},{7,5},{8,10},{9,11},{10,... | collective-permute-start | bytes 196616 | tf_op jit(solution)/shard_map/ppermute | solution.py:19
  180.1 4.8 %collective-permute-start.4 = (bf16[1,16,16,128]{3,1,2,0:T(8,128)(2,1)S(1)}, bf16[1,16,16,128]{3,1,2,0:T(8,128)(2,1)S(1)}, u32[]{:S(2)}, u32[]{:S(2)}) collective-permute-start(bf16[1,16,16,128]{3,1,2,0:T(8,128)(2,1)S(1)} %slice_bitcast_fusion), channel_id=1, source_target_pairs={{0,3},{1,2},{2,1},{3,0},{4,7},{5,6},{6,5},{7,4},{8,11},{9,10},{10,... | collective-permute-start | bytes 196616 | tf_op jit(solution)/shard_map/ppermute | solution.py:19
  204.2 5.6 %copy-start.9 = (f32[1152,576]{0,1:T(8,128)S(1)}, f32[1152,576]{0,1:T(8,128)}, u32[]{:S(2)}) copy-start(f32[1152,576]{0,1:T(8,128)} %param.10) | copy-start | bytes 7962628
  207.0 2.9 %copy-start.2 = (f32[576,1152]{1,0:T(8,128)S(1)}, f32[576,1152]{1,0:T(8,128)}, u32[]{:S(2)}) copy-start(f32[576,1152]{1,0:T(8,128)} %copy-done.1) | copy-start | bytes 7962628
  207.0 2.1 collective-permute-start.31
  209.2 9.1 %collective-permute-start.32 = (f32[576,128]{1,0:T(8,128)S(1)}, f32[576,128]{1,0:T(8,128)S(1)}, u32[]{:S(2)}, u32[]{:S(2)}) collective-permute-start(f32[576,128]{1,0:T(8,128)S(1)} %slice.85), channel_id=1, source_target_pairs={{0,2},{1,3},{2,0},{3,1},{4,6},{5,7},{6,4},{7,5},{8,10},{9,11},{10,... | collective-permute-start | bytes 884744 | tf_op jit(solution)/shard_map/ppermute | solution.py:19
Sparse Core Ops, SparseCore 0:
  26.7 42.9 all-gather.1

commit v3 on v2

--- a/solution.py
+++ b/solution.py
@@ -75,16 +75,13 @@
         piece = shifted[tap % 3, :, pl.ds(tap // 3, side), :, pl.ds(pl.multiple_of(lane, LANES), LANES)]
         return piece.reshape(n_images * spots, LANES)
 
-    first_tap = (fsdp_at * cols) // channels
-    for step in range(2):
-        tap = jnp.minimum(first_tap + step, 8)
-        for lane in range(0, channels, LANES):
-            turned[step, lane : lane + LANES, :] = lanes_of_tap(tap, lane).T
-    for at in range(cols // strip):
-        start = fsdp_at * cols + at * strip
-        left[at * strip : (at + 1) * strip, :] = turned[
-            start // channels - first_tap, pl.ds(pl.multiple_of(start % channels, strip), strip), :
-        ]
+    start = fsdp_at * cols
+    inside = start % LANES
+    for at in range(0, turned.shape[0], LANES):
+        lane = start - inside + at
+        tap = jnp.minimum(lane // channels, 8)
+        turned[at : at + LANES, :] = lanes_of_tap(tap, lane % channels).T
+    left[:cols, :] = turned[pl.ds(pl.multiple_of(inside, strip), cols), :]
     for far in range(2):
         for pair in range(n_pair):
             at = far * n_pair + pair
@@ -140,7 +137,7 @@
         out_specs=[whole] * 4,
         scratch_shapes=[
             pltpu.VMEM((3, n_images, images[0].shape[1] + 2, images[0].shape[2], channels), jnp.bfloat16),
-            pltpu.VMEM((2, channels, n_images * spots), jnp.bfloat16),
+            pltpu.VMEM(((cols + strip + LANES - 1) // LANES * LANES, n_images * spots), jnp.bfloat16),
             pltpu.VMEM((cols + strip, n_images * spots), jnp.bfloat16),
         ],
         input_output_aliases={} if before is None else {n_front + k: k for k in range(4)},
@@ -153,6 +150,53 @@
     )(*operands)
 
 
+def tail_kernel(strip, block, *refs):
+    order, a_ref, g_ref = refs[:3]
+    away_ref, kept_ref, columns, inverse = refs[-4:]
+    strip_refs = refs[3:-4]
+    channels = g_ref.shape[0]
+    for at, ref in enumerate(strip_refs):
+        columns[at * strip : (at + 1) * strip, :] = ref[...]
+        rows = pl.ds(pl.multiple_of(order[at] * strip, strip), strip)
+        for to in range(channels // block):
+            lanes = pl.ds(pl.multiple_of(order[len(strip_refs) + to] * block, block), block)
+            inverse[at * strip : (at + 1) * strip, to * block : (to + 1) * block] = g_ref[rows, lanes]
+    first = lax.dot_general(
+        a_ref[...],
+        columns[...],
+        (((1,), (1,)), ((), ())),
+        precision=lax.Precision.HIGH,
+        preferred_element_type=jnp.float32,
+    )
+    both = jnp.dot(
+        first, inverse[...], precision=lax.Precision.HIGH, preferred_element_type=jnp.float32
+    )
+    away_ref[...] = both[:, : channels // 2]
+    kept_ref[...] = both[:, channels // 2 :]
+
+
+def tail_products(order, a_inverse, g_inverse, strips, block):
+    channels, strip = g_inverse.shape[0], strips[0].shape[0]
+    rows, depth = a_inverse.shape
+    whole = pl.BlockSpec(memory_space=pltpu.VMEM)
+    return pl.pallas_call(
+        lambda *refs: tail_kernel(strip, block, *refs),
+        out_shape=[jax.ShapeDtypeStruct((rows, channels // 2), jnp.float32)] * 2,
+        in_specs=[pl.BlockSpec(memory_space=pltpu.SMEM)] + [whole] * (2 + len(strips)),
+        out_specs=[whole] * 2,
+        scratch_shapes=[
+            pltpu.VMEM((channels, depth), jnp.float32),
+            pltpu.VMEM((channels, channels), jnp.float32),
+        ],
+        compiler_params=pltpu.CompilerParams(vmem_limit_bytes=32 * 1024 * 1024),
+        cost_estimate=pl.CostEstimate(
+            flops=6 * rows * channels * (depth + channels),
+            bytes_accessed=4 * rows * (depth + channels),
+            transcendentals=0,
+        ),
+    )(order, a_inverse, g_inverse, *strips)
+
+
 def per_device(activations, cotangent, weight, a_factor_old, g_factor_old, a_inverse, g_inverse):
     channels = activations.shape[3]
     n_fsdp, n_factor = lax.axis_size("fsdp"), lax.axis_size("factor")
@@ -181,7 +225,12 @@
     )
     strips_by_pair = [strips] + [over_pair(strips, step) for step in range(1, n_pair)]
 
-    layers = [activations] + [over_layer(activations, step) for step in range(1, n_layer)]
+    layers = [activations]
+    source = activations
+    for step in range(1, n_layer):
+        layers.append(over_layer(source, step))
+        source, _ = lax.optimization_barrier((source, layers[-1]))
+    weight, _ = lax.optimization_barrier((weight, layers[-1]))
     aligned = rows % LANES == 0 and channels % LANES == 0 and activations.shape[0] == 1
     totals = None
     group_images = []
@@ -216,6 +265,9 @@
             more.append(jnp.dot(cot_tile, row_tile, preferred_element_type=jnp.float32))
         totals = more if totals is None else [total + new for total, new in zip(totals, more)]
 
+    late_cot, late_g, late_images, _ = lax.optimization_barrier(
+        (own_cot, g_factor_old, group_images, far[-1])
+    )
     grad_own = totals[3] + over_core(totals[1])
     cov_own = totals[2] + over_core(totals[0])
     pixel_total = float(
@@ -223,42 +275,66 @@
     )
     a_factor = 0.5 * a_factor_old + (0.5 / pixel_total) * cov_own.T
 
-    grad_layers = [grad_own] + [over_layer(grad_own, step) for step in range(1, n_layer)]
-    near_grads = jnp.concatenate(grad_layers, axis=0)
-    grad_cols = jnp.concatenate([near_grads, over_side(near_grads)], axis=0)
-    came_from = (fsdp_at - 2 * jnp.arange(n_layer)) % n_fsdp
-    came_from = jnp.concatenate([came_from, came_from ^ 1])
+    exponent = jnp.floor(jnp.log2(jnp.maximum(jnp.max(jnp.abs(grad_own)), 1e-30))) - 14.0
+    packed = (grad_own * jnp.exp2(-exponent)).astype(jnp.float16)
+    exponent = jnp.full((strip, LANES), exponent, jnp.float16)
+    packed = jnp.concatenate([packed, exponent], axis=1)
+    near_packed = [packed] + [over_layer(packed, step) for step in range(1, n_layer)]
+    far_packed = [over_side(array) for array in near_packed]
+    strips_of_grad = [
+        array[:, :rows].astype(jnp.float32) * jnp.exp2(array[:, rows : rows + 1].astype(jnp.float32))
+        for array in near_packed + far_packed
+    ]
+    came_from = [(fsdp_at - 2 * step) % n_fsdp for step in range(n_layer)]
+    came_from = came_from + [at ^ 1 for at in came_from]
     order = [
-        (2 * ((pair_at + step) % n_pair) + (core_at + other) % 2) * block
+        2 * ((pair_at + step) % n_pair) + (core_at + other) % 2
         for other in (1, 0)
         for step in range(n_pair)
     ]
-    inverse = jnp.concatenate(
-        [lax.dynamic_slice_in_dim(g_inverse, at, block, 1) for at in order], axis=1
-    )
-    inverse = inverse.reshape(n_fsdp, strip, channels)
-    inverse = jnp.concatenate(
-        [lax.dynamic_index_in_dim(inverse, came_from[at], 0, keepdims=False) for at in range(n_fsdp)]
-    )
-    partial = lax.dot_general(
-        a_inverse,
-        grad_cols,
-        (((1,), (1,)), ((), ())),
-        precision=lax.Precision.HIGH,
-        preferred_element_type=jnp.float32,
-    )
-    partial = jnp.dot(
-        partial, inverse, precision=lax.Precision.HIGH, preferred_element_type=jnp.float32
-    )
-    by_pair = partial[:, channels // 2 :] + over_core(partial[:, : channels // 2])
+    if aligned and block % LANES == 0:
+        away, kept = tail_products(
+            jnp.stack(came_from + order), a_inverse, g_inverse, strips_of_grad, block
+        )
+    else:
+        inverse = jnp.concatenate(
+            [lax.dynamic_slice_in_dim(g_inverse, at * block, block, 1) for at in order], axis=1
+        )
+        inverse = jnp.concatenate(
+            [lax.dynamic_slice_in_dim(inverse, at * strip, strip, 0) for at in came_from]
+        )
+        partial = lax.dot_general(
+            a_inverse,
+            jnp.concatenate(strips_of_grad),
+            (((1,), (1,)), ((), ())),
+            precision=lax.Precision.HIGH,
+            preferred_element_type=jnp.float32,
+        )
+        partial = jnp.dot(
+            partial, inverse, precision=lax.Precision.HIGH, preferred_element_type=jnp.float32
+        )
+        away, kept = partial[:, : channels // 2], partial[:, channels // 2 :]
+    by_pair = kept + over_core(away)
     result = by_pair[:, :block]
     for step in range(1, n_pair):
         result = result + over_pair(by_pair[:, step * block : (step + 1) * block], step)
     natural_grad = result.astype(jnp.bfloat16)
 
     weight_part = lax.dynamic_slice_in_dim(weight, factor_at * block, block, 1)
-    kernel = lax.all_gather(weight_part, "fsdp", axis=0, tiled=True).reshape(3, 3, channels, block)
-    near_images = jnp.concatenate(group_images, axis=0)
+    near_parts = [weight_part] + [over_layer(weight_part, step) for step in range(1, n_layer)]
+    near_parts = jnp.stack(near_parts)
+    parts = jnp.stack([near_parts, over_side(near_parts)])
+    kernel = jnp.concatenate(
+        [
+            lax.dynamic_slice(
+                parts,
+                ((fsdp_at + at) % 2, (fsdp_at // 2 - at // 2) % n_layer, 0, 0),
+                (1, 1) + weight_part.shape,
+            )[0, 0]
+            for at in range(n_fsdp)
+        ]
+    ).reshape(3, 3, channels, block)
+    near_images = jnp.concatenate(late_images, axis=0)
     maps = lax.conv_general_dilated(
         jnp.concatenate([near_images, over_core(near_images)], axis=0),
         kernel,
@@ -292,18 +368,19 @@
         axis=3,
     )
 
-    g_partial = [
-        by_rows(lax.dynamic_slice_in_dim(own_cot, at, block, 1), own_cot) for at in order
-    ]
-    g_pairs = jnp.concatenate(g_partial[n_pair:]) + over_core(jnp.concatenate(g_partial[:n_pair]))
-    g_sum = g_pairs[:block]
+    g_partial = by_rows(late_cot, late_cot).reshape(n_pair, 2, block, channels)
+    g_pairs = lax.dynamic_index_in_dim(g_partial, core_at, 1, keepdims=False) + over_core(
+        lax.dynamic_index_in_dim(g_partial, 1 - core_at, 1, keepdims=False)
+    )
+    g_sum = lax.dynamic_index_in_dim(g_pairs, pair_at, 0, keepdims=False)
     for step in range(1, n_pair):
-        g_sum = g_sum + over_pair(g_pairs[step * block : (step + 1) * block], step)
+        away = lax.dynamic_index_in_dim(g_pairs, (pair_at + step) % n_pair, 0, keepdims=False)
+        g_sum = g_sum + over_pair(away, step)
     distance = 1
     while distance < n_fsdp:
         g_sum = g_sum + moved(g_sum, "fsdp", lambda at, d=distance: at ^ d)
         distance *= 2
-    g_factor = 0.5 * g_factor_old + 0.5 * g_sum
+    g_factor = 0.5 * late_g + 0.5 * g_sum
     return (conv_out, a_factor, g_factor, natural_grad)
 
 

time: 227 us -> 206 us (0.907)
  the two profiles are of different devices: /device:TPU:10 before, /device:TPU:0 now
where the time goes in v3:
time: 206 us; the launch traced here: 205 us
  waiting for transfers between devices  77.8 us (38%)
  starting transfers between devices  46 us (22%)
  Pallas kernels  40.5 us (20%)
  other arithmetic  18.8 us (9%)
  local copies, waits for them, and re-layouts  14.7 us (7%)
  matrix products  5.61 us (3%)
    ppermute x40, waiting for transfers between devices, moved(): lax.ppermute(array, axis, [(at, target(at) % count) for at in range(count)])  77.8 us
    ppermute x40, starting transfers between devices, moved(): lax.ppermute(array, axis, [(at, target(at) % count) for at in range(count)])  41.2 us
    pallas_call x4, Pallas kernels, add_products(): pl.pallas_call(lambda *refs: products_kernel(len(strips), before is None,...  35.5 us
    unnamed x69, local copies, waits for them, and re-layouts  9.56 us
    conv_general_dilated x1, matrix products, per_device(): lax.conv_general_dilated(jnp.concatenate([near_images, over_core(near_ima...  5.29 us
    pallas_call x1, Pallas kernels, tail_products(): pl.pallas_call(lambda *refs: tail_kernel(strip, block, *refs), out_shape=...  4.91 us
    all_to_all x1, starting transfers between devices, per_device(): lax.all_to_all(own_cot.T.reshape(n_fsdp, strip, own_cot.shape[0]), 'fsdp'...  4.79 us
  transfers between devices with their start and end apart: 41, of which 15 were waited for; matrix products, arithmetic and copies ran while one was open for 13% of the time, Pallas kernels for 20%

profile of v3, /device:TPU:0, one launch (start us, length us, event | category | flops | bytes accessed | tf_op | source)
XLA Modules:
  0.0 205.3 jit_solution(6270687153637411432)
XLA Ops:
  0.7 3.1 %collective-permute-start.1 = (bf16[1,16,16,512]{3,2,1,0:T(8,128)(2,1)}, bf16[1,16,16,512]{3,2,1,0:T(8,128)(2,1)}, u32[]{:S(2)}, u32[]{:S(2)}) collective-permute-start(bf16[1,16,16,512]{3,2,1,0:T(8,128)(2,1)} %refs_1_.2), channel_id=1, source_target_pairs={{0,8},{4,12},{8,16},{12,20},{16,24},{20,28},{24,0},{28,4},{1,9},{5... | collective-permute-start | bytes 786440 | tf_op jit(solution)/shard_map/ppermute | solution.py:19
  3.7 1.8 copy.35
  5.5 4.8 %all-to-all-start = ((bf16[8,64,256]{2,1,0:T(8,128)(2,1)}), bf16[8,64,256]{2,1,0:T(8,128)(2,1)S(1)}, u32[]{:S(2)}, u32[]{:S(2)}) async-start(bf16[8,64,256]{2,1,0:T(8,128)(2,1)} %bitcast.43), calls=%async_computation | async-start | bytes 524288 | tf_op jit(solution)/shard_map/all_to_all | solution.py:223
  10.3 2.1 %collective-permute-done.1.refs_1_ = bf16[1,16,16,512]{3,2,1,0:T(8,128)(2,1)} collective-permute-done((bf16[1,16,16,512]{3,2,1,0:T(8,128)(2,1)}, bf16[1,16,16,512]{3,2,1,0:T(8,128)(2,1)}, u32[]{:S(2)}, u32[]{:S(2)}) %collective-permute-start.1) | collective-permute-done | bytes 262176 | tf_op jit(solution)/shard_map/ppermute | solution.py:19
  12.4 0.9 collective-permute-start.2
  13.2 1.5 collective-permute-start.22
  14.7 15.5 %collective-permute-done.2.refs_1_ = bf16[1,16,16,512]{3,2,1,0:T(8,128)(2,1)} collective-permute-done((bf16[1,16,16,512]{3,2,1,0:T(8,128)(2,1)}, bf16[1,16,16,512]{3,2,1,0:T(8,128)(2,1)}, u32[]{:S(2)}, u32[]{:S(2)}) %collective-permute-start.2) | collective-permute-done | bytes 262176 | tf_op jit(solution)/shard_map/ppermute | solution.py:19
  30.2 1.2 collective-permute-start.3
  31.4 1.5 collective-permute-start
  33.5 1.5 collective-permute-start.19
  35.9 1.6 collective-permute-done.3.refs_1_
  37.6 1.4 collective-permute-start.20
  39.0 1.9 collective-permute-done.refs_2_
  41.6 1.8 collective-permute-start.17
  43.3 3.2 %collective-permute-done.23.refs_4_ = bf16[1,16,16,512]{3,2,1,0:T(8,128)(2,1)S(1)} collective-permute-done((bf16[1,16,16,512]{3,2,1,0:T(8,128)(2,1)S(1)}, bf16[1,16,16,512]{3,2,1,0:T(8,128)(2,1)S(1)}, u32[]{:S(2)}, u32[]{:S(2)}) %collective-permute-start.23) | collective-permute-done | bytes 262176 | tf_op jit(solution)/shard_map/ppermute | solution.py:19
  47.2 1.5 collective-permute-start.16
  48.7 3.5 %collective-permute-done.19.refs_2_ = bf16[1,16,16,512]{3,2,1,0:T(8,128)(2,1)} collective-permute-done((bf16[1,16,16,512]{3,2,1,0:T(8,128)(2,1)}, bf16[1,16,16,512]{3,2,1,0:T(8,128)(2,1)}, u32[]{:S(2)}, u32[]{:S(2)}) %collective-permute-start.19) | collective-permute-done | bytes 262176 | tf_op jit(solution)/shard_map/ppermute | solution.py:19
  52.2 1.8 collective-permute-start.21
  54.0 3.8 %collective-permute-done.15.refs_6_ = bf16[8,64,256]{2,1,0:T(8,128)(2,1)S(1)} collective-permute-done((bf16[8,64,256]{2,1,0:T(8,128)(2,1)S(1)}, bf16[8,64,256]{2,1,0:T(8,128)(2,1)S(1)}, u32[]{:S(2)}, u32[]{:S(2)}) %collective-permute-start.15) | collective-permute-done | bytes 262176 | tf_op jit(solution)/shard_map/ppermute | solution.py:19
  57.8 0.7 copy-done.15
  58.5 0.8 collective-permute-start.7
  59.3 0.9 copy-done.3
  60.3 0.9 copy-done.9
  61.2 0.9 copy-done.16
  62.2 0.9 copy-done.19
  63.1 0.9 copy-done.21
  64.1 7.9 %shard_map.102 = (f32[576,1152]{1,0:T(8,128)}, f32[64,1152]{1,0:T(8,128)S(1)}, f32[576,1152]{1,0:T(8,128)S(1)}, f32[64,1152]{1,0:T(8,128)S(1)}) custom-call(s32[5]{0:T(128)S(1)} %stack.139.refs_0_, bf16[1,16,16,512]{3,2,1,0:T(8,128)(2,1)S(1)} %copy-done.1, bf16[1,16,16,512]{3,2,1,0:T(8,128)(2,1)S(1)} %copy-done.3, bf16[1,16,16,512]{3,2,1,0:T(8,128)(2,1)S(1)} %copy-done.19, ...), custom_call_target="tpu_custom_call" | custom-call | flops 3019898880 | bytes 11796480 | tf_op jit(solution)/shard_map/pallas_call | solution.py:133
  72.0 3.2 %collective-permute-start.9 = (bf16[576,128]{1,0:T(8,128)(2,1)S(1)}, bf16[576,128]{1,0:T(8,128)(2,1)S(1)}, u32[]{:S(2)}, u32[]{:S(2)}) collective-permute-start(bf16[576,128]{1,0:T(8,128)(2,1)S(1)} %constant_dynamic-slice_fusion.4), channel_id=1, source_target_pairs={{0,24},{4,28},{8,0},{12,4},{16,8},{20,12},{24,16},{28,20},{1,25},{... | collective-permute-start | bytes 442376 | tf_op jit(solution)/shard_map/ppermute | solution.py:19
  75.2 1.5 collective-permute-start.4
  77.2 9.3 %shard_map.103 = (f32[576,1152]{1,0:T(8,128)}, f32[64,1152]{1,0:T(8,128)S(1)}, f32[576,1152]{1,0:T(8,128)S(1)}, f32[64,1152]{1,0:T(8,128)S(1)}) custom-call(s32[5]{0:T(128)S(1)} %stack.136.refs_0_, bf16[1,16,16,512]{3,2,1,0:T(8,128)(2,1)} %collective-permute-done.1.refs_1_, ...), custom_call_target="tpu_custom_call", output_to_operand_aliasing={{0}: (7, {}), {1}: (8, {}), {2}: (9, {}), {3}: (10, {})} | custom-call | flops 3019898880 | bytes 11796480 | tf_op jit(solution)/shard_map/pallas_call | solution.py:133
  86.6 1.8 collective-permute-start.14
  88.8 1.7 collective-permute-start.5
  90.6 9.2 %shard_map.104 = (f32[576,1152]{1,0:T(8,128)}, f32[64,1152]{1,0:T(8,128)S(1)}, f32[576,1152]{1,0:T(8,128)S(1)}, f32[64,1152]{1,0:T(8,128)S(1)}) custom-call(s32[5]{0:T(128)S(1)} %stack.133.refs_0_, bf16[1,16,16,512]{3,2,1,0:T(8,128)(2,1)} %collective-permute-done.2.refs_1_, ...), custom_call_target="tpu_custom_call", output_to_operand_aliasing={{0}: (7, {}), {1}: (8, {}), {2}: (9, {}), {3}: (10, {})} | custom-call | flops 3019898880 | bytes 11796480 | tf_op jit(solution)/shard_map/pallas_call | solution.py:133
  99.8 8.4 %collective-permute-done.5.refs_4_ = bf16[1,16,16,512]{3,2,1,0:T(8,128)(2,1)S(1)} collective-permute-done((bf16[1,16,16,512]{3,2,1,0:T(8,128)(2,1)S(1)}, bf16[1,16,16,512]{3,2,1,0:T(8,128)(2,1)S(1)}, u32[]{:S(2)}, u32[]{:S(2)}) %collective-permute-start.5) | collective-permute-done | bytes 262176 | tf_op jit(solution)/shard_map/ppermute | solution.py:19
  108.3 9.2 %shard_map.105 = (f32[576,1152]{1,0:T(8,128)}, f32[64,1152]{1,0:T(8,128)S(1)}, f32[576,1152]{1,0:T(8,128)S(1)}, f32[64,1152]{1,0:T(8,128)S(1)}) custom-call(s32[5]{0:T(128)S(1)} %stack.130.refs_0_, bf16[1,16,16,512]{3,2,1,0:T(8,128)(2,1)S(1)} %copy-done.14, ...), custom_call_target="tpu_custom_call", output_to_operand_aliasing={{0}: (7, {}), {1}: (8, {}), {2}: (9, {}), {3}: (10, {})} | custom-call | flops 3019898880 | bytes 11796480 | tf_op jit(solution)/shard_map/pallas_call | solution.py:133
  117.8 1.0 dynamic-slice_bitcast_fusion
  119.2 0.9 pad_maximum_fusion.1
  121.4 1.4 abs_reduce_fusion
  123.6 1.1 convert_multiply_fusion.7
  124.8 1.8 collective-permute-start.34
  128.4 2.5 %collective-permute-done.34 = f16[64,1280]{1,0:T(8,128)(2,1)S(1)} collective-permute-done((f16[64,1280]{1,0:T(8,128)(2,1)S(1)}, f16[64,1280]{1,0:T(8,128)(2,1)S(1)}, u32[]{:S(2)}, u32[]{:S(2)}) %collective-permute-start.34) | collective-permute-done | bytes 163872 | tf_op jit(solution)/shard_map/ppermute | solution.py:19
  130.9 1.5 collective-permute-start.32
  132.7 1.2 collective-permute-done.33
  134.8 9.5 %collective-permute-done.32 = f16[64,1280]{1,0:T(8,128)(2,1)S(1)} collective-permute-done((f16[64,1280]{1,0:T(8,128)(2,1)S(1)}, f16[64,1280]{1,0:T(8,128)(2,1)S(1)}, u32[]{:S(2)}, u32[]{:S(2)}) %collective-permute-start.32) | collective-permute-done | bytes 163872 | tf_op jit(solution)/shard_map/ppermute | solution.py:19
  144.2 1.6 collective-permute-start.37
  146.8 1.7 collective-permute-start.35
  148.4 1.1 bitcast_add_fusion.1
  149.6 1.6 collective-permute-start.26
  151.2 1.1 maximum_bitcast_fusion
  153.6 0.9 copy-done.32
  154.5 5.3 %fusion.8 = bf16[16,32,3,128]{3,1,2,0:T(8,128)(2,1)S(1)} fusion(bf16[3,3,512,128]{3,2,1,0:T(8,128)(2,1)S(1)} %bitcast.115, bf16[16,4,8,5,512]{4,0,3,2,1:T(8,128)(2,1)S(1)} %fusion.1, pred[32,3]{0,1:T(4,128)(4,1)S(1)} %copy-done.33), kind=kOutput, calls=%fused_computation.24 | convolution fusion | flops 1736835072 | bytes 4194400 | tf_op jit(solution)/shard_map/conv_general_dilated | solution.py:338
  162.2 1.4 collective-permute-start.13
  164.0 4.9 %shard_map.106 = (f32[576,256]{1,0:T(8,128)}, f32[576,256]{1,0:T(8,128)S(1)}) custom-call(s32[12]{0:T(128)S(1)} %stack.144.refs_0_, f32[576,1152]{1,0:T(8,128)S(1)} %copy-done.11, f32[512,512]{1,0:T(8,128)S(1)} %copy-done.12, f32[64,1152]{1,0:T(8,128)S(1)} %get-tuple-element.54.refs_3_, f32[64,1152]{1,0:T(8,128)S(1)} %convert_multiply_fusion.6.refs_4_, ...), custom_call_target="tpu_custom_call" | custom-call | flops 2944401408 | bytes 3833856 | tf_op jit(solution)/shard_map/pallas_call | solution.py:182
  168.9 0.8 copy-done.6
  170.6 1.0 pad_maximum_fusion.2
  171.7 7.0 %collective-permute-done.27 = f32[128,512]{1,0:T(8,128)} collective-permute-done((f32[128,512]{1,0:T(8,128)S(1)}, f32[128,512]{1,0:T(8,128)}, u32[]{:S(2)}, u32[]{:S(2)}) %collective-permute-start.27) | collective-permute-done | bytes 262176 | tf_op jit(solution)/shard_map/ppermute | solution.py:19
  178.7 1.0 add.331
  179.8 1.1 add.341
  181.6 5.8 %collective-permute-done.28 = f32[128,512]{1,0:T(8,128)S(1)} collective-permute-done((f32[128,512]{1,0:T(8,128)S(1)}, f32[128,512]{1,0:T(8,128)S(1)}, u32[]{:S(2)}, u32[]{:S(2)}) %collective-permute-start.28) | collective-permute-done | bytes 262176 | tf_op jit(solution)/shard_map/ppermute | solution.py:19
  187.5 0.8 pad_maximum_fusion.3
  188.2 1.2 collective-permute-done.39
  190.1 10.6 %collective-permute-done.29 = f32[128,512]{1,0:T(8,128)S(1)} collective-permute-done((f32[128,512]{1,0:T(8,128)S(1)}, f32[128,512]{1,0:T(8,128)S(1)}, u32[]{:S(2)}, u32[]{:S(2)}) %collective-permute-start.29) | collective-permute-done | bytes 262176 | tf_op jit(solution)/shard_map/ppermute | solution.py:19
  200.7 0.8 add_multiply_fusion
  201.5 3.8 %bitcast_add_fusion = f32[1152,576]{0,1:T(8,128)} fusion(f32[576,1152]{1,0:T(8,128)S(1)} %get-tuple-element.46, f32[576,1152]{1,0:T(8,128)} %collective-permute-done.24, f32[1152,576]{0,1:T(8,128)S(1)} %copy-done.28), kind=kLoop, calls=%fused_computation.2 | loop fusion | flops 2654208 | bytes 10616832 | tf_op jit(solution)/shard_map/add | solution.py:276
  (153 shorter events, 16.2 us)
Async XLA Ops:
  0.6 38.3 %copy-start = (bf16[576,512]{1,0:T(8,128)(2,1)S(1)}, bf16[576,512]{1,0:T(8,128)(2,1)}, u32[]{:S(2)}) copy-start(bf16[576,512]{1,0:T(8,128)(2,1)} %param.9) | copy-start | bytes 1769476
  0.6 58.7 %copy-start.1 = (bf16[1,16,16,512]{3,2,1,0:T(8,128)(2,1)S(1)}, bf16[1,16,16,512]{3,2,1,0:T(8,128)(2,1)}, u32[]{:S(2)}) copy-start(bf16[1,16,16,512]{3,2,1,0:T(8,128)(2,1)} %refs_1_.2) | copy-start | bytes 786436
  0.7 11.7 %collective-permute-start.1 = (bf16[1,16,16,512]{3,2,1,0:T(8,128)(2,1)}, bf16[1,16,16,512]{3,2,1,0:T(8,128)(2,1)}, u32[]{:S(2)}, u32[]{:S(2)}) collective-permute-start(bf16[1,16,16,512]{3,2,1,0:T(8,128)(2,1)} %refs_1_.2), channel_id=1, source_target_pairs={{0,8},{4,12},{8,16},{12,20},{16,24},{20,28},{24,0},{28,4},{1,9},{5... | collective-permute-start | bytes 786440 | tf_op jit(solution)/shard_map/ppermute | solution.py:19
  5.5 29.5 %all-to-all-start = ((bf16[8,64,256]{2,1,0:T(8,128)(2,1)}), bf16[8,64,256]{2,1,0:T(8,128)(2,1)S(1)}, u32[]{:S(2)}, u32[]{:S(2)}) async-start(bf16[8,64,256]{2,1,0:T(8,128)(2,1)} %bitcast.43), calls=%async_computation | async-start | bytes 524288 | tf_op jit(solution)/shard_map/all_to_all | solution.py:223
  12.4 17.9 %collective-permute-start.2 = (bf16[1,16,16,512]{3,2,1,0:T(8,128)(2,1)}, bf16[1,16,16,512]{3,2,1,0:T(8,128)(2,1)}, u32[]{:S(2)}, u32[]{:S(2)}) collective-permute-start(bf16[1,16,16,512]{3,2,1,0:T(8,128)(2,1)} %refs_1_.2), channel_id=1, source_target_pairs={{0,16},{4,20},{8,24},{12,28},{16,0},{20,4},{24,8},{28,12},{1,17},{... | collective-permute-start | bytes 786440 | tf_op jit(solution)/shard_map/ppermute | solution.py:19
  13.2 19.7 %collective-permute-start.22 = (bf16[1,16,16,512]{3,2,1,0:T(8,128)(2,1)}, bf16[1,16,16,512]{3,2,1,0:T(8,128)(2,1)S(1)}, u32[]{:S(2)}, u32[]{:S(2)}) collective-permute-start(bf16[1,16,16,512]{3,2,1,0:T(8,128)(2,1)} %refs_1_.2), channel_id=1, source_target_pairs={{0,4},{4,0},{8,12},{12,8},{16,20},{20,16},{24,28},{28,24},{1,5},{5... | collective-permute-start | bytes 786440 | tf_op jit(solution)/shard_map/ppermute | solution.py:19
  30.2 7.3 %collective-permute-start.3 = (bf16[1,16,16,512]{3,2,1,0:T(8,128)(2,1)}, bf16[1,16,16,512]{3,2,1,0:T(8,128)(2,1)S(1)}, u32[]{:S(2)}, u32[]{:S(2)}) collective-permute-start(bf16[1,16,16,512]{3,2,1,0:T(8,128)(2,1)} %refs_1_.2), channel_id=1, source_target_pairs={{0,24},{4,28},{8,0},{12,4},{16,8},{20,12},{24,16},{28,20},{1,25},{... | collective-permute-start | bytes 786440 | tf_op jit(solution)/shard_map/ppermute | solution.py:19
  31.4 9.5 %collective-permute-start = (bf16[1,16,16,512]{3,2,1,0:T(8,128)(2,1)}, bf16[1,16,16,512]{3,2,1,0:T(8,128)(2,1)S(1)}, u32[]{:S(2)}, u32[]{:S(2)}) collective-permute-start(bf16[1,16,16,512]{3,2,1,0:T(8,128)(2,1)} %refs_1_.2), channel_id=1, source_target_pairs={{0,2},{1,3},{2,0},{3,1},{4,6},{5,7},{6,4},{7,5},{8,10},{9,11},{10,... | collective-permute-start | bytes 786440 | tf_op jit(solution)/shard_map/ppermute | solution.py:19
  33.0 24.8 %copy-start.18 = (bf16[1,16,16,512]{3,2,1,0:T(8,128)(2,1)}, bf16[1,16,16,512]{3,2,1,0:T(8,128)(2,1)S(1)}, u32[]{:S(2)}) copy-start(bf16[1,16,16,512]{3,2,1,0:T(8,128)(2,1)S(1)} %collective-permute-done.22.refs_3_) | copy-start | bytes 786436
  33.0 13.5 %collective-permute-start.23 = (bf16[1,16,16,512]{3,2,1,0:T(8,128)(2,1)S(1)}, bf16[1,16,16,512]{3,2,1,0:T(8,128)(2,1)S(1)}, u32[]{:S(2)}, u32[]{:S(2)}) collective-permute-start(bf16[1,16,16,512]{3,2,1,0:T(8,128)(2,1)S(1)} %collective-permute-done.22.refs_3_), channel_id=1, source_target_pairs={{0,2},{1,3},{2,0},{3,1},{4,6},{5,7},{6,4},{7,5},{8,10},{9,11},{10,... | collective-permute-start | bytes 786440 | tf_op jit(solution)/shard_map/ppermute | solution.py:19
  33.5 18.8 %collective-permute-start.19 = (bf16[1,16,16,512]{3,2,1,0:T(8,128)(2,1)}, bf16[1,16,16,512]{3,2,1,0:T(8,128)(2,1)}, u32[]{:S(2)}, u32[]{:S(2)}) collective-permute-start(bf16[1,16,16,512]{3,2,1,0:T(8,128)(2,1)} %collective-permute-done.1.refs_1_), channel_id=1, source_target_pairs={{0,2},{1,3},{2,0},{3,1},{4,6},{5,7},{6,4},{7,5},{8,10},{9,11},{10,... | collective-permute-start | bytes 786440 | tf_op jit(solution)/shard_map/ppermute | solution.py:19
  35.0 22.8 %copy-start.8 = (bf16[8,64,256]{2,1,0:T(8,128)(2,1)}, bf16[8,64,256]{2,1,0:T(8,128)(2,1)S(1)}, u32[]{:S(2)}) copy-start(bf16[8,64,256]{2,1,0:T(8,128)(2,1)S(1)} %all-to-all-done.refs_5_) | copy-start | bytes 786436
  35.0 22.7 %collective-permute-start.15 = (bf16[8,64,256]{2,1,0:T(8,128)(2,1)S(1)}, bf16[8,64,256]{2,1,0:T(8,128)(2,1)S(1)}, u32[]{:S(2)}, u32[]{:S(2)}) collective-permute-start(bf16[8,64,256]{2,1,0:T(8,128)(2,1)S(1)} %all-to-all-done.refs_5_), channel_id=1, source_target_pairs={{0,2},{1,3},{2,0},{3,1},{4,6},{5,7},{6,4},{7,5},{8,10},{9,11},{10,... | collective-permute-start | bytes 786440 | tf_op jit(solution)/shard_map/ppermute | solution.py:19
  37.6 20.2 %copy-start.13 = (bf16[1,16,16,512]{3,2,1,0:T(8,128)(2,1)}, bf16[1,16,16,512]{3,2,1,0:T(8,128)(2,1)S(1)}, u32[]{:S(2)}) copy-start(bf16[1,16,16,512]{3,2,1,0:T(8,128)(2,1)S(1)} %collective-permute-done.3.refs_1_) | copy-start | bytes 786436
  37.6 34.4 %collective-permute-start.20 = (bf16[1,16,16,512]{3,2,1,0:T(8,128)(2,1)}, bf16[1,16,16,512]{3,2,1,0:T(8,128)(2,1)S(1)}, u32[]{:S(2)}, u32[]{:S(2)}) collective-permute-start(bf16[1,16,16,512]{3,2,1,0:T(8,128)(2,1)} %collective-permute-done.1.refs_1_), channel_id=1, source_target_pairs={{0,4},{4,0},{8,12},{12,8},{16,20},{20,16},{24,28},{28,24},{1,5},{5... | collective-permute-start | bytes 786440 | tf_op jit(solution)/shard_map/ppermute | solution.py:19
  41.6 33.6 %collective-permute-start.17 = (bf16[1,16,16,512]{3,2,1,0:T(8,128)(2,1)}, bf16[1,16,16,512]{3,2,1,0:T(8,128)(2,1)S(1)}, u32[]{:S(2)}, u32[]{:S(2)}) collective-permute-start(bf16[1,16,16,512]{3,2,1,0:T(8,128)(2,1)} %collective-permute-done.2.refs_1_), channel_id=1, source_target_pairs={{0,4},{4,0},{8,12},{12,8},{16,20},{20,16},{24,28},{28,24},{1,5},{5... | collective-permute-start | bytes 786440 | tf_op jit(solution)/shard_map/ppermute | solution.py:19
  47.2 43.4 %collective-permute-start.16 = (bf16[1,16,16,512]{3,2,1,0:T(8,128)(2,1)}, bf16[1,16,16,512]{3,2,1,0:T(8,128)(2,1)S(1)}, u32[]{:S(2)}, u32[]{:S(2)}) collective-permute-start(bf16[1,16,16,512]{3,2,1,0:T(8,128)(2,1)} %collective-permute-done.2.refs_1_), channel_id=1, source_target_pairs={{0,2},{1,3},{2,0},{3,1},{4,6},{5,7},{6,4},{7,5},{8,10},{9,11},{10,... | collective-permute-start | bytes 786440 | tf_op jit(solution)/shard_map/ppermute | solution.py:19
  52.2 19.7 %collective-permute-start.21 = (bf16[1,16,16,512]{3,2,1,0:T(8,128)(2,1)}, bf16[1,16,16,512]{3,2,1,0:T(8,128)(2,1)S(1)}, u32[]{:S(2)}, u32[]{:S(2)}) collective-permute-start(bf16[1,16,16,512]{3,2,1,0:T(8,128)(2,1)} %collective-permute-done.19.refs_2_), channel_id=1, source_target_pairs={{0,4},{4,0},{8,12},{12,8},{16,20},{20,16},{24,28},{28,24},{1,5},{5... | collective-permute-start | bytes 786440 | tf_op jit(solution)/shard_map/ppermute | solution.py:19
  58.5 18.2 %collective-permute-start.7 = (bf16[576,128]{1,0:T(8,128)(2,1)S(1)}, bf16[576,128]{1,0:T(8,128)(2,1)S(1)}, u32[]{:S(2)}, u32[]{:S(2)}) collective-permute-start(bf16[576,128]{1,0:T(8,128)(2,1)S(1)} %constant_dynamic-slice_fusion.4), channel_id=1, source_target_pairs={{0,8},{4,12},{8,16},{12,20},{16,24},{20,28},{24,0},{28,4},{1,9},{5... | collective-permute-start | bytes 442376 | tf_op jit(solution)/shard_map/ppermute | solution.py:19
  64.1 11.1 %copy-start.14 = (bf16[1,16,16,512]{3,2,1,0:T(8,128)(2,1)S(1)}, bf16[1,16,16,512]{3,2,1,0:T(8,128)(2,1)}, u32[]{:S(2)}) copy-start(bf16[1,16,16,512]{3,2,1,0:T(8,128)(2,1)} %copy-done.13) | copy-start | bytes 786436
  64.1 13.1 %copy-start.10 = (bf16[8,64,256]{2,1,0:T(8,128)(2,1)S(1)}, bf16[8,64,256]{2,1,0:T(8,128)(2,1)}, u32[]{:S(2)}) copy-start(bf16[8,64,256]{2,1,0:T(8,128)(2,1)} %copy-done.8) | copy-start | bytes 786436
  64.1 13.1 %copy-start.17 = (bf16[8,64,256]{2,1,0:T(8,128)(2,1)S(1)}, bf16[8,64,256]{2,1,0:T(8,128)(2,1)}, u32[]{:S(2)}) copy-start(bf16[8,64,256]{2,1,0:T(8,128)(2,1)} %copy-done.15) | copy-start | bytes 786436
  72.0 14.6 %collective-permute-start.8 = (bf16[576,128]{1,0:T(8,128)(2,1)S(1)}, bf16[576,128]{1,0:T(8,128)(2,1)S(1)}, u32[]{:S(2)}, u32[]{:S(2)}) collective-permute-start(bf16[576,128]{1,0:T(8,128)(2,1)S(1)} %constant_dynamic-slice_fusion.4), channel_id=1, source_target_pairs={{0,16},{4,20},{8,24},{12,28},{16,0},{20,4},{24,8},{28,12},{1,17},{... | collective-permute-start | bytes 442376 | tf_op jit(solution)/shard_map/ppermute | solution.py:19
  72.0 16.4 %collective-permute-start.9 = (bf16[576,128]{1,0:T(8,128)(2,1)S(1)}, bf16[576,128]{1,0:T(8,128)(2,1)S(1)}, u32[]{:S(2)}, u32[]{:S(2)}) collective-permute-start(bf16[576,128]{1,0:T(8,128)(2,1)S(1)} %constant_dynamic-slice_fusion.4), channel_id=1, source_target_pairs={{0,24},{4,28},{8,0},{12,4},{16,8},{20,12},{24,16},{28,20},{1,25},{... | collective-permute-start | bytes 442376 | tf_op jit(solution)/shard_map/ppermute | solution.py:19
  75.2 13.6 %collective-permute-start.4 = (bf16[1,16,16,512]{3,2,1,0:T(8,128)(2,1)S(1)}, bf16[1,16,16,512]{3,2,1,0:T(8,128)(2,1)S(1)}, u32[]{:S(2)}, u32[]{:S(2)}) collective-permute-start(bf16[1,16,16,512]{3,2,1,0:T(8,128)(2,1)S(1)} %copy-done.14), channel_id=1, source_target_pairs={{0,2},{1,3},{2,0},{3,1},{4,6},{5,7},{6,4},{7,5},{8,10},{9,11},{10,... | collective-permute-start | bytes 786440 | tf_op jit(solution)/shard_map/ppermute | solution.py:19
  76.7 13.9 %collective-permute-start.18 = (bf16[1,16,16,512]{3,2,1,0:T(8,128)(2,1)S(1)}, bf16[1,16,16,512]{3,2,1,0:T(8,128)(2,1)S(1)}, u32[]{:S(2)}, u32[]{:S(2)}) collective-permute-start(bf16[1,16,16,512]{3,2,1,0:T(8,128)(2,1)S(1)} %collective-permute-done.17.refs_3_), channel_id=1, source_target_pairs={{0,2},{1,3},{2,0},{3,1},{4,6},{5,7},{6,4},{7,5},{8,10},{9,11},{10,... | collective-permute-start | bytes 786440 | tf_op jit(solution)/shard_map/ppermute | solution.py:19
  86.6 13.2 %collective-permute-start.14 = (bf16[1,16,16,512]{3,2,1,0:T(8,128)(2,1)S(1)}, bf16[1,16,16,512]{3,2,1,0:T(8,128)(2,1)S(1)}, u32[]{:S(2)}, u32[]{:S(2)}) collective-permute-start(bf16[1,16,16,512]{3,2,1,0:T(8,128)(2,1)S(1)} %copy-done.14), channel_id=1, source_target_pairs={{0,4},{4,0},{8,12},{12,8},{16,20},{20,16},{24,28},{28,24},{1,5},{5... | collective-permute-start | bytes 786440 | tf_op jit(solution)/shard_map/ppermute | solution.py:19
  88.5 32.6 %copy-start.22 = (bf16[1,4,576,128]{3,2,1,0:T(8,128)(2,1)}, bf16[1,4,576,128]{3,2,1,0:T(8,128)(2,1)S(1)}, u32[]{:S(2)}) copy-start(bf16[1,4,576,128]{3,2,1,0:T(8,128)(2,1)S(1)} %get-tuple-element.58) | copy-start | bytes 1769476
  88.5 32.1 %collective-permute-start.10 = (bf16[4,576,128]{2,1,0:T(8,128)(2,1)S(1)}, bf16[4,576,128]{2,1,0:T(8,128)(2,1)S(1)}, u32[]{:S(2)}, u32[]{:S(2)}) collective-permute-start(bf16[4,576,128]{2,1,0:T(8,128)(2,1)S(1)} %get-tuple-element.59), channel_id=1, source_target_pairs={{0,4},{4,0},{8,12},{12,8},{16,20},{20,16},{24,28},{28,24},{1,5},{5... | collective-permute-start | bytes 1769480 | tf_op jit(solution)/shard_map/ppermute | solution.py:19
  88.8 19.4 %collective-permute-start.5 = (bf16[1,16,16,512]{3,2,1,0:T(8,128)(2,1)S(1)}, bf16[1,16,16,512]{3,2,1,0:T(8,128)(2,1)S(1)}, u32[]{:S(2)}, u32[]{:S(2)}) collective-permute-start(bf16[1,16,16,512]{3,2,1,0:T(8,128)(2,1)S(1)} %collective-permute-done.4.refs_2_), channel_id=1, source_target_pairs={{0,4},{4,0},{8,12},{12,8},{16,20},{20,16},{24,28},{28,24},{1,5},{5... | collective-permute-start | bytes 786440 | tf_op jit(solution)/shard_map/ppermute | solution.py:19
  108.3 9.2 %copy-start.29 = (bf16[1,16,16,512]{3,2,1,0:T(8,128)(2,1)S(1)}, bf16[1,16,16,512]{3,2,1,0:T(8,128)(2,1)}, u32[]{:S(2)}) copy-start(bf16[1,16,16,512]{3,2,1,0:T(8,128)(2,1)} %param.8) | copy-start | bytes 786436
  117.4 1.8 copy-start.4
  117.4 4.0 %collective-permute-start.30 = (f32[64,1152]{1,0:T(8,128)S(1)}, f32[64,1152]{1,0:T(8,128)S(1)}, u32[]{:S(2)}, u32[]{:S(2)}) collective-permute-start(f32[64,1152]{1,0:T(8,128)S(1)} %get-tuple-element.51), channel_id=1, source_target_pairs={{0,1},{1,0},{2,3},{3,2},{4,5},{5,4},{6,7},{7,6},{8,9},{9,8},{10,11... | collective-permute-start | bytes 884744 | tf_op jit(solution)/shard_map/ppermute | solution.py:19
  117.8 2.9 %copy-start.26 = (f32[512,512]{1,0:T(8,128)}, f32[512,512]{1,0:T(8,128)S(1)}, u32[]{:S(2)}) copy-start(f32[512,512]{1,0:T(8,128)S(1)} %fusion.21) | copy-start | bytes 3145732
  118.7 28.1 %collective-permute-start.25 = (f32[2,128,512]{2,1,0:T(8,128)}, f32[2,128,512]{2,1,0:T(8,128)}, u32[]{:S(2)}, u32[]{:S(2)}) collective-permute-start(f32[2,128,512]{2,1,0:T(8,128)} %dynamic-slice_bitcast_fusion), channel_id=1, source_target_pairs={{0,1},{1,0},{2,3},{3,2},{4,5},{5,4},{6,7},{7,6},{8,9},{9,8},{10,11... | collective-permute-start | bytes 1572872 | tf_op jit(solution)/shard_map/ppermute | solution.py:19
  119.2 82.2 %collective-permute-start.24 = (f32[576,1152]{1,0:T(8,128)}, f32[576,1152]{1,0:T(8,128)}, u32[]{:S(2)}, u32[]{:S(2)}) collective-permute-start(f32[576,1152]{1,0:T(8,128)} %get-tuple-element.47), channel_id=1, source_target_pairs={{0,1},{1,0},{2,3},{3,2},{4,5},{5,4},{6,7},{7,6},{8,9},{9,8},{10,11... | collective-permute-start | bytes 7962632 | tf_op jit(solution)/shard_map/ppermute | solution.py:19
  120.1 29.5 %collective-permute-start.6 = (bf16[2,16,16,512]{3,2,1,0:T(8,128)(2,1)}, bf16[2,16,16,512]{3,2,1,0:T(8,128)(2,1)}, u32[]{:S(2)}, u32[]{:S(2)}) collective-permute-start(bf16[2,16,16,512]{3,2,1,0:T(8,128)(2,1)} %pad_maximum_fusion.1), channel_id=1, source_target_pairs={{0,1},{1,0},{2,3},{3,2},{4,5},{5,4},{6,7},{7,6},{8,9},{9,8},{10,11... | collective-permute-start | bytes 1572872 | tf_op jit(solution)/shard_map/ppermute | solution.py:19
  121.4 1.4 copy-start.31
  123.6 3.0 %copy-start.23 = (bf16[1,4,576,128]{3,2,1,0:T(8,128)(2,1)S(1)}, bf16[1,4,576,128]{3,2,1,0:T(8,128)(2,1)}, u32[]{:S(2)}) copy-start(bf16[1,4,576,128]{3,2,1,0:T(8,128)(2,1)} %copy-done.22) | copy-start | bytes 1769476
  123.6 3.7 %copy-start.25 = (bf16[4,576,128]{2,1,0:T(8,128)(2,1)S(1)}, bf16[4,576,128]{2,1,0:T(8,128)(2,1)}, u32[]{:S(2)}) copy-start(bf16[4,576,128]{2,1,0:T(8,128)(2,1)} %copy-done.24) | copy-start | bytes 1769476
  124.8 6.2 %collective-permute-start.34 = (f16[64,1280]{1,0:T(8,128)(2,1)S(1)}, f16[64,1280]{1,0:T(8,128)(2,1)S(1)}, u32[]{:S(2)}, u32[]{:S(2)}) collective-permute-start(f16[64,1280]{1,0:T(8,128)(2,1)S(1)} %concatenate.20), channel_id=1, source_target_pairs={{0,4},{4,0},{8,12},{12,8},{16,20},{20,16},{24,28},{28,24},{1,5},{5... | collective-permute-start | bytes 491528 | tf_op jit(solution)/shard_map/ppermute | solution.py:19
  128.0 20.4 %copy-start.27 = (f32[512,512]{1,0:T(8,128)S(1)}, f32[512,512]{1,0:T(8,128)}, u32[]{:S(2)}) copy-start(f32[512,512]{1,0:T(8,128)} %copy-done.26) | copy-start | bytes 3145732
  128.0 5.9 %collective-permute-start.33 = (f16[64,1280]{1,0:T(8,128)(2,1)S(1)}, f16[64,1280]{1,0:T(8,128)(2,1)S(1)}, u32[]{:S(2)}, u32[]{:S(2)}) collective-permute-start(f16[64,1280]{1,0:T(8,128)(2,1)S(1)} %concatenate.20), channel_id=1, source_target_pairs={{0,24},{4,28},{8,0},{12,4},{16,8},{20,12},{24,16},{28,20},{1,25},{... | collective-permute-start | bytes 491528 | tf_op jit(solution)/shard_map/ppermute | solution.py:19
  130.9 13.3 %collective-permute-start.32 = (f16[64,1280]{1,0:T(8,128)(2,1)S(1)}, f16[64,1280]{1,0:T(8,128)(2,1)S(1)}, u32[]{:S(2)}, u32[]{:S(2)}) collective-permute-start(f16[64,1280]{1,0:T(8,128)(2,1)S(1)} %concatenate.20), channel_id=1, source_target_pairs={{0,16},{4,20},{8,24},{12,28},{16,0},{20,4},{24,8},{28,12},{1,17},{... | collective-permute-start | bytes 491528 | tf_op jit(solution)/shard_map/ppermute | solution.py:19
  133.9 12.1 %collective-permute-start.31 = (f16[64,1280]{1,0:T(8,128)(2,1)S(1)}, f16[64,1280]{1,0:T(8,128)(2,1)S(1)}, u32[]{:S(2)}, u32[]{:S(2)}) collective-permute-start(f16[64,1280]{1,0:T(8,128)(2,1)S(1)} %concatenate.20), channel_id=1, source_target_pairs={{0,8},{4,12},{8,16},{12,20},{16,24},{20,28},{24,0},{28,4},{1,9},{5... | collective-permute-start | bytes 491528 | tf_op jit(solution)/shard_map/ppermute | solution.py:19
  144.2 17.1 %collective-permute-start.37 = (f16[64,1280]{1,0:T(8,128)(2,1)S(1)}, f16[64,1280]{1,0:T(8,128)(2,1)S(1)}, u32[]{:S(2)}, u32[]{:S(2)}) collective-permute-start(f16[64,1280]{1,0:T(8,128)(2,1)S(1)} %collective-permute-done.33), channel_id=1, source_target_pairs={{0,4},{4,0},{8,12},{12,8},{16,20},{20,16},{24,28},{28,24},{1,5},{5... | collective-permute-start | bytes 491528 | tf_op jit(solution)/shard_map/ppermute | solution.py:19
  146.0 15.5 %collective-permute-start.36 = (f16[64,1280]{1,0:T(8,128)(2,1)S(1)}, f16[64,1280]{1,0:T(8,128)(2,1)S(1)}, u32[]{:S(2)}, u32[]{:S(2)}) collective-permute-start(f16[64,1280]{1,0:T(8,128)(2,1)S(1)} %collective-permute-done.32), channel_id=1, source_target_pairs={{0,4},{4,0},{8,12},{12,8},{16,20},{20,16},{24,28},{28,24},{1,5},{5... | collective-permute-start | bytes 491528 | tf_op jit(solution)/shard_map/ppermute | solution.py:19
  146.7 4.5 %copy-start.5 = (bf16[1,16,16,512]{3,2,1,0:T(8,128)(2,1)S(1)}, bf16[1,16,16,512]{3,2,1,0:T(8,128)(2,1)}, u32[]{:S(2)}) copy-start(bf16[1,16,16,512]{3,2,1,0:T(8,128)(2,1)} %copy-done.2) | copy-start | bytes 786436
  146.8 15.4 %collective-permute-start.35 = (f16[64,1280]{1,0:T(8,128)(2,1)S(1)}, f16[64,1280]{1,0:T(8,128)(2,1)S(1)}, u32[]{:S(2)}, u32[]{:S(2)}) collective-permute-start(f16[64,1280]{1,0:T(8,128)(2,1)S(1)} %collective-permute-done.31), channel_id=1, source_target_pairs={{0,4},{4,0},{8,12},{12,8},{16,20},{20,16},{24,28},{28,24},{1,5},{5... | collective-permute-start | bytes 491528 | tf_op jit(solution)/shard_map/ppermute | solution.py:19
  149.6 20.1 %collective-permute-start.26 = (f32[128,512]{1,0:T(8,128)S(1)}, f32[128,512]{1,0:T(8,128)S(1)}, u32[]{:S(2)}, u32[]{:S(2)}) collective-permute-start(f32[128,512]{1,0:T(8,128)S(1)} %dynamic-slice_bitcast_fusion.1), channel_id=1, source_target_pairs={{0,2},{1,3},{2,0},{3,1},{4,6},{5,7},{6,4},{7,5},{8,10},{9,11},{10,... | collective-permute-start | bytes 786440 | tf_op jit(solution)/shard_map/ppermute | solution.py:19
  153.2 1.3 copy-start.32
  154.5 9.5 %copy-start.12 = (f32[512,512]{1,0:T(8,128)S(1)}, f32[512,512]{1,0:T(8,128)}, u32[]{:S(2)}) copy-start(f32[512,512]{1,0:T(8,128)} %refs_2_.1) | copy-start | bytes 3145732
  159.8 4.2 %copy-start.11 = (f32[576,1152]{1,0:T(8,128)S(1)}, f32[576,1152]{1,0:T(8,128)}, u32[]{:S(2)}) copy-start(f32[576,1152]{1,0:T(8,128)} %refs_1_.3) | copy-start | bytes 7962628
  161.3 8.7 %collective-permute-start.11 = (bf16[1,16,16,128]{3,1,2,0:T(8,128)(2,1)S(1)}, bf16[1,16,16,128]{3,1,2,0:T(8,128)(2,1)}, u32[]{:S(2)}, u32[]{:S(2)}) collective-permute-start(bf16[1,16,16,128]{3,1,2,0:T(8,128)(2,1)S(1)} %get-tuple-element.66), channel_id=1, source_target_pairs={{0,1},{1,0},{2,3},{3,2},{4,5},{5,4},{6,7},{7,6},{8,9},{9,8},{10,11... | collective-permute-start | bytes 196616 | tf_op jit(solution)/shard_map/ppermute | solution.py:19
  161.6 9.0 %collective-permute-start.12 = (bf16[1,16,16,128]{3,1,2,0:T(8,128)(2,1)}, bf16[1,16,16,128]{3,1,2,0:T(8,128)(2,1)}, u32[]{:S(2)}, u32[]{:S(2)}) collective-permute-start(bf16[1,16,16,128]{3,1,2,0:T(8,128)(2,1)} %get-tuple-element.65), channel_id=1, source_target_pairs={{0,2},{1,3},{2,0},{3,1},{4,6},{5,7},{6,4},{7,5},{8,10},{9,11},{10,... | collective-permute-start | bytes 196616 | tf_op jit(solution)/shard_map/ppermute | solution.py:19
  162.2 8.3 %collective-permute-start.13 = (bf16[1,16,16,128]{3,1,2,0:T(8,128)(2,1)}, bf16[1,16,16,128]{3,1,2,0:T(8,128)(2,1)}, u32[]{:S(2)}, u32[]{:S(2)}) collective-permute-start(bf16[1,16,16,128]{3,1,2,0:T(8,128)(2,1)} %slice_bitcast_fusion), channel_id=1, source_target_pairs={{0,3},{1,2},{2,1},{3,0},{4,7},{5,6},{6,5},{7,4},{8,11},{9,10},{10,... | collective-permute-start | bytes 196616 | tf_op jit(solution)/shard_map/ppermute | solution.py:19
  169.7 10.1 %collective-permute-start.38 = (f32[576,256]{1,0:T(8,128)}, f32[576,256]{1,0:T(8,128)}, u32[]{:S(2)}, u32[]{:S(2)}) collective-permute-start(f32[576,256]{1,0:T(8,128)} %get-tuple-element.53), channel_id=1, source_target_pairs={{0,1},{1,0},{2,3},{3,2},{4,5},{5,4},{6,7},{7,6},{8,9},{9,8},{10,11... | collective-permute-start | bytes 1769480 | tf_op jit(solution)/shard_map/ppermute | solution.py:19
  170.1 8.6 %collective-permute-start.27 = (f32[128,512]{1,0:T(8,128)S(1)}, f32[128,512]{1,0:T(8,128)}, u32[]{:S(2)}, u32[]{:S(2)}) collective-permute-start(f32[128,512]{1,0:T(8,128)S(1)} %bitcast_add_fusion.2), channel_id=1, source_target_pairs={{0,4},{4,0},{8,12},{12,8},{16,20},{20,16},{24,28},{28,24},{1,5},{5... | collective-permute-start | bytes 786440 | tf_op jit(solution)/shard_map/ppermute | solution.py:19
  170.6 9.2 %copy-start.7 = (f32[576,256]{1,0:T(8,128)S(1)}, f32[576,256]{1,0:T(8,128)}, u32[]{:S(2)}) copy-start(f32[576,256]{1,0:T(8,128)} %copy-done.6) | copy-start | bytes 1769476
  179.7 7.7 %collective-permute-start.28 = (f32[128,512]{1,0:T(8,128)S(1)}, f32[128,512]{1,0:T(8,128)S(1)}, u32[]{:S(2)}, u32[]{:S(2)}) collective-permute-start(f32[128,512]{1,0:T(8,128)S(1)} %add.331), channel_id=1, source_target_pairs={{0,8},{4,12},{8,0},{12,4},{16,24},{20,28},{24,16},{28,20},{1,9},{5... | collective-permute-start | bytes 786440 | tf_op jit(solution)/shard_map/ppermute | solution.py:19
  181.0 19.7 %copy-start.30 = (f32[128,512]{1,0:T(8,128)S(1)}, f32[128,512]{1,0:T(8,128)}, u32[]{:S(2)}) copy-start(f32[128,512]{1,0:T(8,128)} %param.11) | copy-start | bytes 786436
  181.0 8.4 %collective-permute-start.39 = (f32[576,128]{1,0:T(8,128)S(1)}, f32[576,128]{1,0:T(8,128)S(1)}, u32[]{:S(2)}, u32[]{:S(2)}) collective-permute-start(f32[576,128]{1,0:T(8,128)S(1)} %slice.104), channel_id=1, source_target_pairs={{0,2},{1,3},{2,0},{3,1},{4,6},{5,7},{6,4},{7,5},{8,10},{9,11},{10,... | collective-permute-start | bytes 884744 | tf_op jit(solution)/shard_map/ppermute | solution.py:19
  187.4 14.1 %copy-start.28 = (f32[1152,576]{0,1:T(8,128)S(1)}, f32[1152,576]{0,1:T(8,128)}, u32[]{:S(2)}) copy-start(f32[1152,576]{0,1:T(8,128)} %param.10) | copy-start | bytes 7962628
  187.4 13.3 %collective-permute-start.29 = (f32[128,512]{1,0:T(8,128)S(1)}, f32[128,512]{1,0:T(8,128)S(1)}, u32[]{:S(2)}, u32[]{:S(2)}) collective-permute-start(f32[128,512]{1,0:T(8,128)S(1)} %add.332), channel_id=1, source_target_pairs={{0,16},{4,20},{8,24},{12,28},{16,0},{20,4},{24,8},{28,12},{1,17},{... | collective-permute-start | bytes 786440 | tf_op jit(solution)/shard_map/ppermute | solution.py:19
  (11 other events, 9.8 us)

commit v4 on v3

--- a/solution.py
+++ b/solution.py
@@ -42,11 +42,11 @@
     return jnp.concatenate(pieces, axis=3).reshape(-1, width)
 
 
-def products_kernel(n_pair, first, *refs):
+def products_kernel(pairs, n_pair, first, *refs):
     place = refs[0]
-    image_refs = refs[1 : 1 + 2 * n_pair]
-    strip_refs = refs[1 + 2 * n_pair : 1 + 3 * n_pair]
-    refs = refs[1 + 3 * n_pair :]
+    image_refs = refs[1 : 1 + len(pairs)]
+    strip_refs = refs[1 + len(pairs) : 1 + len(pairs) + n_pair]
+    refs = refs[1 + len(pairs) + n_pair :]
     before, refs = (None, refs) if first else (refs[:4], refs[4:])
     totals, (shifted, turned, left) = refs[:4], refs[4:]
     n_images, side, channels = len(image_refs), image_refs[0].shape[1], image_refs[0].shape[3]
@@ -82,10 +82,8 @@
         tap = jnp.minimum(lane // channels, 8)
         turned[at : at + LANES, :] = lanes_of_tap(tap, lane % channels).T
     left[:cols, :] = turned[pl.ds(pl.multiple_of(inside, strip), cols), :]
-    for far in range(2):
-        for pair in range(n_pair):
-            at = far * n_pair + pair
-            left[cols : cols + strip, at * spots : (at + 1) * spots] = strip_refs[pair][place[3 + far]]
+    for at, pair in enumerate(pairs):
+        left[cols : cols + strip, at * spots : (at + 1) * spots] = strip_refs[pair][place[3 + at]]
 
     tiles_per = rows // LANES
 
@@ -123,7 +121,7 @@
         keep(1, (odd + 2 * step) * LANES, 2, product(tiles_per + odd + 2 * step, 2))
 
 
-def add_products(place, images, strips, before, cols, rows):
+def add_products(place, images, pairs, strips, before, cols, rows):
     n_images, channels, strip = len(images), images[0].shape[3], strips[0].shape[1]
     spots = images[0].shape[1] * images[0].shape[2]
     shapes = [jax.ShapeDtypeStruct((height, rows), jnp.float32) for height in (cols, strip)] * 2
@@ -131,7 +129,7 @@
     operands = [place, *images, *strips, *(before or [])]
     n_front = 1 + n_images + len(strips)
     return pl.pallas_call(
-        lambda *refs: products_kernel(len(strips), before is None, *refs),
+        lambda *refs: products_kernel(pairs, len(strips), before is None, *refs),
         out_shape=shapes,
         in_specs=[pl.BlockSpec(memory_space=pltpu.SMEM)] + [whole] * (len(operands) - 1),
         out_specs=[whole] * 4,
@@ -144,7 +142,7 @@
         compiler_params=pltpu.CompilerParams(vmem_limit_bytes=40 * 1024 * 1024),
         cost_estimate=pl.CostEstimate(
             flops=4 * (cols + strip) * rows * n_images * spots,
-            bytes_accessed=4 * 4 * (cols + strip) * rows,
+            bytes_accessed=16 * (cols + strip) * rows,
             transcendentals=0,
         ),
     )(*operands)
@@ -197,6 +195,39 @@
     )(order, a_inverse, g_inverse, *strips)
 
 
+def gather_plan(n_layer, n_pair):
+    far_layers = sorted(range(1, n_layer), key=lambda step: min(step, n_layer - step))
+    by_side, by_pair = [], []
+    for turn, layer in enumerate([0] + far_layers):
+        by_side.append((("side", layer, 0), ("layer", layer, 0)))
+        for pair in range(1, n_pair):
+            by_pair.append((("pair", layer, pair), ("layer", layer, 0)))
+            if turn % 2 == 0:
+                by_pair.append((("both", layer, pair), ("side", layer, 0)))
+            else:
+                by_side.append((("both", layer, pair), ("pair", layer, pair)))
+    by_layer = [(("layer", layer, 0), None) for layer in far_layers]
+    for link in (by_side, by_pair):
+        link.sort(key=lambda item: item[0][0] == "both")
+    here, due, rounds = {None, ("layer", 0, 0)}, {}, []
+    while by_layer or by_side or by_pair:
+        here |= {item for item, when in due.items() if when <= len(rounds)}
+        due = {item: when for item, when in due.items() if when > len(rounds)}
+        now = []
+        for link in (by_layer, by_side, by_pair):
+            if link is by_layer and any(item[0] == "layer" for item in due):
+                continue
+            free = [item for item in link if item[1] in here]
+            if free:
+                link.remove(free[0])
+                item, source = free[0]
+                hops = min(item[1], n_layer - item[1]) if item[0] == "layer" else 1
+                due[item] = len(rounds) + hops
+                now.append((item, source, "pair" if link is by_pair else item[0], hops))
+        rounds.append(now)
+    return rounds
+
+
 def per_device(activations, cotangent, weight, a_factor_old, g_factor_old, a_inverse, g_inverse):
     channels = activations.shape[3]
     n_fsdp, n_factor = lax.axis_size("fsdp"), lax.axis_size("factor")
@@ -219,55 +250,74 @@
     def over_core(array):
         return moved(array, "factor", lambda at: at ^ 1)
 
+    def after(arrays, events):
+        return lax.optimization_barrier((arrays, events))[0]
+
+    def transfer(array, item, how):
+        if how == "layer":
+            return over_layer(array, item[1])
+        if how == "pair":
+            return over_pair(array, item[2])
+        return over_side(array)
+
     own_cot = cotangent.reshape(-1, channels)
-    strips = lax.all_to_all(
-        own_cot.T.reshape(n_fsdp, strip, own_cot.shape[0]), "fsdp", split_axis=0, concat_axis=0
-    )
-    strips_by_pair = [strips] + [over_pair(strips, step) for step in range(1, n_pair)]
-
-    layers = [activations]
-    source = activations
-    for step in range(1, n_layer):
-        layers.append(over_layer(source, step))
-        source, _ = lax.optimization_barrier((source, layers[-1]))
-    weight, _ = lax.optimization_barrier((weight, layers[-1]))
+    maps = {("layer", 0, 0): activations}
+    plan = gather_plan(n_layer, n_pair)
+    events, due = [[]], []
+    for at, now in enumerate(plan):
+        sources = [activations if source is None else maps[source] for _, source, _, _ in now]
+        sources = after(sources, events[at])
+        for array, (item, _, how, hops) in zip(sources, now):
+            maps[item] = transfer(array, item, how)
+            due.append((at + hops, maps[item]))
+        events.append([array for when, array in due if when == at + 1])
+    last = len(plan) - 1
+
+    strips = after(own_cot, events[1]).T.reshape(n_fsdp, strip, own_cot.shape[0])
+    strips = lax.all_to_all(strips, "fsdp", split_axis=0, concat_axis=0)
+    strips_by_pair = [strips] + [
+        over_pair(after(strips, events[3]), step) for step in range(1, n_pair)
+    ]
+
     aligned = rows % LANES == 0 and channels % LANES == 0 and activations.shape[0] == 1
+    arrived = {("layer", 0, 0): 0}
+    for at, now in enumerate(plan):
+        arrived.update({item: at + hops for item, _, _, hops in now})
+    images = sorted(maps, key=lambda item: arrived[item])
+    images.sort(
+        key=lambda item: max(when for other, when in arrived.items() if other[1] == item[1])
+    )
+    half = len(images) // 2
     totals = None
-    group_images = []
-    for step, layer in enumerate(layers):
-        near = [layer] + [over_pair(layer, pair) for pair in range(1, n_pair)]
-        if step % 2 == 0:
-            aside = over_side(layer)
-            far = [aside] + [over_pair(aside, pair) for pair in range(1, n_pair)]
-        else:
-            far = [over_side(image) for image in near]
-        if step == 0:
-            group_images = near
-        owner = (fsdp_at - 2 * step) % n_fsdp
+    for batch in (images[:half], images[half:]):
+        owners, pairs = [], []
+        for kind, layer, pair in batch:
+            owner = (fsdp_at - 2 * layer) % n_fsdp
+            owners.append(owner ^ 1 if kind in ("side", "both") else owner)
+            pairs.append(pair)
         if aligned:
-            place = jnp.stack([factor_at ^ 1, factor_at, fsdp_at, owner, owner ^ 1])
-            totals = add_products(place, near + far, strips_by_pair, totals, cols, rows)
+            place = jnp.stack([factor_at ^ 1, factor_at, fsdp_at] + owners)
+            totals = add_products(
+                place, [maps[item] for item in batch], pairs, strips_by_pair, totals, cols, rows
+            )
             continue
-        images = jnp.concatenate(near + far, axis=0)
-        col_tile = tile_of_patches(images, fsdp_at * cols, cols)
-        cot_tile = jnp.concatenate(
-            [
-                lax.dynamic_index_in_dim(strips_by_pair[pair], which, 0, keepdims=False)
-                for which in (owner, owner ^ 1)
-                for pair in range(n_pair)
-            ],
-            axis=1,
-        )
-        more = []
-        for tile in (factor_at ^ 1, factor_at):
-            row_tile = tile_of_patches(images, tile * rows, rows)
-            more.append(by_rows(col_tile, row_tile))
-            more.append(jnp.dot(cot_tile, row_tile, preferred_element_type=jnp.float32))
-        totals = more if totals is None else [total + new for total, new in zip(totals, more)]
-
-    late_cot, late_g, late_images, _ = lax.optimization_barrier(
-        (own_cot, g_factor_old, group_images, far[-1])
-    )
+        for at in range(0, len(batch), 2 * n_pair):
+            part = jnp.concatenate([maps[item] for item in batch[at : at + 2 * n_pair]], axis=0)
+            col_tile = tile_of_patches(part, fsdp_at * cols, cols)
+            cot_tile = jnp.concatenate(
+                [
+                    lax.dynamic_index_in_dim(strips_by_pair[pair], owner, 0, keepdims=False)
+                    for pair, owner in list(zip(pairs, owners))[at : at + 2 * n_pair]
+                ],
+                axis=1,
+            )
+            more = []
+            for tile in (factor_at ^ 1, factor_at):
+                row_tile = tile_of_patches(part, tile * rows, rows)
+                more.append(by_rows(col_tile, row_tile))
+                more.append(jnp.dot(cot_tile, row_tile, preferred_element_type=jnp.float32))
+            totals = more if totals is None else [old + new for old, new in zip(totals, more)]
+
     grad_own = totals[3] + over_core(totals[1])
     cov_own = totals[2] + over_core(totals[0])
     pixel_total = float(
@@ -320,9 +370,11 @@
         result = result + over_pair(by_pair[:, step * block : (step + 1) * block], step)
     natural_grad = result.astype(jnp.bfloat16)
 
-    weight_part = lax.dynamic_slice_in_dim(weight, factor_at * block, block, 1)
+    weight_part = lax.dynamic_slice_in_dim(
+        after(weight, events[last - 1]), factor_at * block, block, 1
+    )
     near_parts = [weight_part] + [over_layer(weight_part, step) for step in range(1, n_layer)]
-    near_parts = jnp.stack(near_parts)
+    near_parts = after(jnp.stack(near_parts), events[last + 1])
     parts = jnp.stack([near_parts, over_side(near_parts)])
     kernel = jnp.concatenate(
         [
@@ -334,8 +386,9 @@
             for at in range(n_fsdp)
         ]
     ).reshape(3, 3, channels, block)
-    near_images = jnp.concatenate(late_images, axis=0)
-    maps = lax.conv_general_dilated(
+    near_images = [activations] + [maps["pair", 0, step] for step in range(1, n_pair)]
+    near_images = after(jnp.concatenate(near_images, axis=0), events[last - 1])
+    outputs = lax.conv_general_dilated(
         jnp.concatenate([near_images, over_core(near_images)], axis=0),
         kernel,
         (1, 1),
@@ -343,15 +396,15 @@
         dimension_numbers=("NHWC", "HWIO", "NHWC"),
         preferred_element_type=jnp.float32,
     ).astype(jnp.bfloat16)
-    maps = maps.reshape((2, n_pair) + activations.shape[:3] + (block,))
+    outputs = outputs.reshape((2, n_pair) + activations.shape[:3] + (block,))
     own_maps = []
     for pair in range(n_pair):
         for other in range(2):
             own_maps.append(
-                maps[other, pair]
+                outputs[other, pair]
                 if pair + other == 0
                 else moved(
-                    maps[other, pair], "factor", lambda at, o=other, p=pair: (at ^ o) - 2 * p
+                    outputs[other, pair], "factor", lambda at, o=other, p=pair: (at ^ o) - 2 * p
                 )
             )
     own_maps = jnp.stack(own_maps)
@@ -368,10 +421,12 @@
         axis=3,
     )
 
+    late_cot = after(own_cot, events[2])
     g_partial = by_rows(late_cot, late_cot).reshape(n_pair, 2, block, channels)
     g_pairs = lax.dynamic_index_in_dim(g_partial, core_at, 1, keepdims=False) + over_core(
         lax.dynamic_index_in_dim(g_partial, 1 - core_at, 1, keepdims=False)
     )
+    g_pairs = after(g_pairs, events[last + 1])
     g_sum = lax.dynamic_index_in_dim(g_pairs, pair_at, 0, keepdims=False)
     for step in range(1, n_pair):
         away = lax.dynamic_index_in_dim(g_pairs, (pair_at + step) % n_pair, 0, keepdims=False)
@@ -380,7 +435,7 @@
     while distance < n_fsdp:
         g_sum = g_sum + moved(g_sum, "fsdp", lambda at, d=distance: at ^ d)
         distance *= 2
-    g_factor = 0.5 * late_g + 0.5 * g_sum
+    g_factor = 0.5 * g_factor_old + 0.5 * g_sum
     return (conv_out, a_factor, g_factor, natural_grad)
 
 

time: 206 us -> 178 us (0.86)
  waiting for transfers between devices: 77.8 us -> 58.6 us
  Pallas kernels: 40.5 us -> 29.6 us
  local copies, waits for them, and re-layouts: 14.7 us -> 7.76 us
  other arithmetic: 18.8 us -> 24 us
  starting transfers between devices: 46 us -> 49.8 us
    ppermute x40, waiting for transfers between devices: 77.8 us -> 56.8 us  [moved(): lax.ppermute(array, axis, [(at, target(at) % count) for at in range(count)])]
    pallas_call x4 -> x2, Pallas kernels: 35.5 us -> 25.5 us  [add_products(): pl.pallas_call(lambda *refs: products_kernel(pairs, len(strips), before i...]
    unnamed x7, other arithmetic: 1.3 us -> 7.21 us
    unnamed x69 -> x57, local copies, waits for them, and re-layouts: 9.56 us -> 4.29 us
    ppermute x40, starting transfers between devices: 41.2 us -> 46.3 us  [moved(): lax.ppermute(array, axis, [(at, target(at) % count) for at in range(count)])]
  transfers between devices with their start and end apart: 41 -> 41, of which waited for: 15 -> 16; matrix products, arithmetic and copies ran while one was open for 13% -> 17% of each run, Pallas kernels for 20% -> 9%
where the time goes in v4:
time: 178 us
  waiting for transfers between devices  58.6 us (33%)
  starting transfers between devices  49.8 us (28%)
  Pallas kernels  29.6 us (17%)
  other arithmetic  24 us (13%)
  local copies, waits for them, and re-layouts  7.76 us (4%)
  matrix products  5.65 us (3%)
  between operations  2.04 us (1%)
    ppermute x40, waiting for transfers between devices, moved(): lax.ppermute(array, axis, [(at, target(at) % count) for at in range(count)])  56.8 us
    ppermute x40, starting transfers between devices, moved(): lax.ppermute(array, axis, [(at, target(at) % count) for at in range(count)])  46.3 us
    pallas_call x2, Pallas kernels, add_products(): pl.pallas_call(lambda *refs: products_kernel(pairs, len(strips), before i...  25.5 us
    unnamed x7, other arithmetic  7.21 us
    conv_general_dilated x1, matrix products, per_device(): lax.conv_general_dilated(jnp.concatenate([near_images, over_core(near_ima...  5.34 us
    unnamed x57, local copies, waits for them, and re-layouts  4.29 us
    pallas_call x1, Pallas kernels, tail_products(): pl.pallas_call(lambda *refs: tail_kernel(strip, block, *refs), out_shape=...  4.09 us
    add x1, other arithmetic, per_device(): a_factor = 0.5 * a_factor_old + 0.5 / pixel_total * cov_own.T  3.84 us
  transfers between devices with their start and end apart: 41, of which 16 were waited for; matrix products, arithmetic and copies ran while one was open for 17% of the time, Pallas kernels for 9%

profile of v4, /device:TPU:0, one launch (start us, length us, event | category | flops | bytes accessed | tf_op | source)
XLA Modules:
  0.0 177.5 jit_solution(10096616736435002269)
XLA Ops:
  0.7 3.0 %collective-permute-start = (bf16[1,16,16,512]{3,2,1,0:T(8,128)(2,1)}, bf16[1,16,16,512]{3,2,1,0:T(8,128)(2,1)S(1)}, u32[]{:S(2)}, u32[]{:S(2)}) collective-permute-start(bf16[1,16,16,512]{3,2,1,0:T(8,128)(2,1)} %refs_1_.2), channel_id=1, source_target_pairs={{0,2},{1,3},{2,0},{3,1},{4,6},{5,7},{6,4},{7,5},{8,10},{9,11},{10,... | collective-permute-start | bytes 786440 | tf_op jit(solution)/shard_map/ppermute | solution.py:19
  3.7 1.6 collective-permute-start.1
  5.3 1.5 collective-permute-start.2
  6.8 3.4 %collective-permute-done.refs_4_ = bf16[1,16,16,512]{3,2,1,0:T(8,128)(2,1)S(1)} collective-permute-done((bf16[1,16,16,512]{3,2,1,0:T(8,128)(2,1)}, bf16[1,16,16,512]{3,2,1,0:T(8,128)(2,1)S(1)}, u32[]{:S(2)}, u32[]{:S(2)}) %collective-permute-start) | collective-permute-done | bytes 262176 | tf_op jit(solution)/shard_map/ppermute | solution.py:19
  10.2 3.3 %collective-permute-done.1.refs_2_ = bf16[1,16,16,512]{3,2,1,0:T(8,128)(2,1)S(1)} collective-permute-done((bf16[1,16,16,512]{3,2,1,0:T(8,128)(2,1)}, bf16[1,16,16,512]{3,2,1,0:T(8,128)(2,1)S(1)}, u32[]{:S(2)}, u32[]{:S(2)}) %collective-permute-start.1) | collective-permute-done | bytes 262176 | tf_op jit(solution)/shard_map/ppermute | solution.py:19
  13.6 1.8 collective-permute-start.3
  15.3 1.5 collective-permute-start.4
  17.3 1.8 %copy.27 = bf16[256,512]{0,1:T(8,128)(2,1)} copy(bf16[256,512]{1,0:T(8,128)(2,1)} %bitcast.98) | data formatting | bytes 524288 | tf_op jit(solution)/shard_map/optimization_barrier | solution.py:254
  19.1 3.5 %all-to-all-start = ((bf16[8,64,256]{2,1,0:T(8,128)(2,1)}), bf16[8,64,256]{2,1,0:T(8,128)(2,1)S(1)}, u32[]{:S(2)}, u32[]{:S(2)}) async-start(bf16[8,64,256]{2,1,0:T(8,128)(2,1)} %bitcast.45), calls=%async_computation | async-start | bytes 524288 | tf_op jit(solution)/shard_map/all_to_all | solution.py:277
  22.7 0.7 copy-done.17
  23.5 1.9 %collective-permute-start.7 = (bf16[1,16,16,512]{3,2,1,0:T(8,128)(2,1)S(1)}, bf16[1,16,16,512]{3,2,1,0:T(8,128)(2,1)S(1)}, u32[]{:S(2)}, u32[]{:S(2)}) collective-permute-start(bf16[1,16,16,512]{3,2,1,0:T(8,128)(2,1)S(1)} %collective-permute-done.3.refs_1_), channel_id=1, source_target_pairs={{0,4},{4,0},{8,12},{12,8},{16,20},{20,16},{24,28},{28,24},{1,5},{5... | collective-permute-start | bytes 786440 | tf_op jit(solution)/shard_map/ppermute | solution.py:19
  25.4 1.5 collective-permute-start.8
  27.2 0.9 pad_maximum_fusion.1
  28.0 2.4 %collective-permute-start.6 = (bf16[1,16,16,512]{3,2,1,0:T(8,128)(2,1)S(1)}, bf16[1,16,16,512]{3,2,1,0:T(8,128)(2,1)}, u32[]{:S(2)}, u32[]{:S(2)}) collective-permute-start(bf16[1,16,16,512]{3,2,1,0:T(8,128)(2,1)S(1)} %copy-done.1), channel_id=1, source_target_pairs={{0,16},{4,20},{8,24},{12,28},{16,0},{20,4},{24,8},{28,12},{1,17},{... | collective-permute-start | bytes 786440 | tf_op jit(solution)/shard_map/ppermute | solution.py:19
  30.4 1.8 %all-to-all-done.refs_9_ = bf16[8,64,256]{2,1,0:T(8,128)(2,1)S(1)} async-done(((bf16[8,64,256]{2,1,0:T(8,128)(2,1)}), bf16[8,64,256]{2,1,0:T(8,128)(2,1)S(1)}, u32[]{:S(2)}, u32[]{:S(2)}) %all-to-all-start) | async-done | bytes 262176 | tf_op jit(solution)/shard_map/all_to_all | solution.py:277
  32.3 6.2 %collective-permute-start.9 = (bf16[1,16,16,512]{3,2,1,0:T(8,128)(2,1)S(1)}, bf16[1,16,16,512]{3,2,1,0:T(8,128)(2,1)S(1)}, u32[]{:S(2)}, u32[]{:S(2)}) collective-permute-start(bf16[1,16,16,512]{3,2,1,0:T(8,128)(2,1)S(1)} %collective-permute-done.5.refs_6_), channel_id=1, source_target_pairs={{0,4},{4,0},{8,12},{12,8},{16,20},{20,16},{24,28},{28,24},{1,5},{5... | collective-permute-start | bytes 786440 | tf_op jit(solution)/shard_map/ppermute | solution.py:19
  38.5 1.7 collective-permute-start.10
  41.4 1.4 collective-permute-done.9.refs_7_
  42.8 2.0 %collective-permute-done.10.refs_8_ = bf16[1,16,16,512]{3,2,1,0:T(8,128)(2,1)S(1)} collective-permute-done((bf16[1,16,16,512]{3,2,1,0:T(8,128)(2,1)S(1)}, bf16[1,16,16,512]{3,2,1,0:T(8,128)(2,1)S(1)}, u32[]{:S(2)}, u32[]{:S(2)}) %collective-permute-start.10) | collective-permute-done | bytes 262176 | tf_op jit(solution)/shard_map/ppermute | solution.py:19
  44.9 1.2 collective-permute-start.12
  46.2 2.0 %collective-permute-start.15 = (bf16[1,16,16,512]{3,2,1,0:T(8,128)(2,1)}, bf16[1,16,16,512]{3,2,1,0:T(8,128)(2,1)S(1)}, u32[]{:S(2)}, u32[]{:S(2)}) collective-permute-start(bf16[1,16,16,512]{3,2,1,0:T(8,128)(2,1)} %collective-permute-done.6.refs_4_), channel_id=1, source_target_pairs={{0,2},{1,3},{2,0},{3,1},{4,6},{5,7},{6,4},{7,5},{8,10},{9,11},{10,... | collective-permute-start | bytes 786440 | tf_op jit(solution)/shard_map/ppermute | solution.py:19
  48.2 1.6 collective-permute-done.23.refs_10_
  49.9 0.9 copy-done.2
  50.8 0.9 copy-done.14
  51.8 0.9 copy-done.18
  52.7 12.3 %shard_map.102 = (f32[576,1152]{1,0:T(8,128)}, f32[64,1152]{1,0:T(8,128)S(1)}, f32[576,1152]{1,0:T(8,128)S(1)}, f32[64,1152]{1,0:T(8,128)S(1)}) custom-call(s32[11]{0:T(128)S(1)} %stack.133.refs_0_, bf16[1,16,16,512]{3,2,1,0:T(8,128)(2,1)S(1)} %copy-done.2, bf16[1,16,16,512]{3,2,1,0:T(8,128)(2,1)S(1)} %copy-done.14, bf16[1,16,16,512]{3,2,1,0:T(8,128)(2,1)S(1)} %copy-done.16, ...), custom_call_target="tpu_custom_call" | custom-call | flops 6039797760 | bytes 11796480 | tf_op jit(solution)/shard_map/pallas_call | solution.py:131
  65.7 0.8 collective-permute-start.16
  66.7 7.7 %collective-permute-done.16.refs_5_ = bf16[1,16,16,512]{3,2,1,0:T(8,128)(2,1)S(1)} collective-permute-done((bf16[1,16,16,512]{3,2,1,0:T(8,128)(2,1)}, bf16[1,16,16,512]{3,2,1,0:T(8,128)(2,1)S(1)}, u32[]{:S(2)}, u32[]{:S(2)}) %collective-permute-start.16) | collective-permute-done | bytes 262176 | tf_op jit(solution)/shard_map/ppermute | solution.py:19
  74.3 0.8 collective-permute-start.17
  75.2 0.8 collective-permute-start.18
  76.0 0.9 pad_maximum_fusion
  76.9 1.1 maximum_bitcast_fusion
  78.9 3.1 %collective-permute-done.17.refs_7_ = bf16[1,16,16,512]{3,2,1,0:T(8,128)(2,1)S(1)} collective-permute-done((bf16[1,16,16,512]{3,2,1,0:T(8,128)(2,1)S(1)}, bf16[1,16,16,512]{3,2,1,0:T(8,128)(2,1)S(1)}, u32[]{:S(2)}, u32[]{:S(2)}) %collective-permute-start.17) | collective-permute-done | bytes 262176 | tf_op jit(solution)/shard_map/ppermute | solution.py:19
  82.5 13.2 %shard_map.103 = (f32[576,1152]{1,0:T(8,128)}, f32[64,1152]{1,0:T(8,128)S(1)}, f32[576,1152]{1,0:T(8,128)S(1)}, f32[64,1152]{1,0:T(8,128)S(1)}) custom-call(s32[11]{0:T(128)S(1)} %stack.128.refs_0_, bf16[1,16,16,512]{3,2,1,0:T(8,128)(2,1)S(1)} %copy-done.8, ...), custom_call_target="tpu_custom_call", output_to_operand_aliasing={{0}: (11, {}), {1}: (12, {}), {2}: (13, {}), {3}: (14, {})} | custom-call | flops 6039797760 | bytes 11796480 | tf_op jit(solution)/shard_map/pallas_call | solution.py:131
  95.7 1.8 fusion.1
  97.5 1.2 collective-permute-start.19
  99.4 1.7 collective-permute-start.26
  101.1 1.3 abs_reduce_fusion
  103.2 1.1 convert_multiply_fusion.7
  104.9 3.3 %collective-permute-done.26 = f32[128,512]{1,0:T(8,128)} collective-permute-done((f32[128,512]{1,0:T(8,128)}, f32[128,512]{1,0:T(8,128)}, u32[]{:S(2)}, u32[]{:S(2)}) %collective-permute-start.26) | collective-permute-done | bytes 262176 | tf_op jit(solution)/shard_map/ppermute | solution.py:19
  108.2 1.0 bitcast_add_fusion.2
  109.7 2.3 %collective-permute-start.32 = (f16[64,1280]{1,0:T(8,128)(2,1)S(1)}, f16[64,1280]{1,0:T(8,128)(2,1)S(1)}, u32[]{:S(2)}, u32[]{:S(2)}) collective-permute-start(f16[64,1280]{1,0:T(8,128)(2,1)S(1)} %concatenate.19), channel_id=1, source_target_pairs={{0,16},{4,20},{8,24},{12,28},{16,0},{20,4},{24,8},{28,12},{1,17},{... | collective-permute-start | bytes 491528 | tf_op jit(solution)/shard_map/ppermute | solution.py:19
  112.0 4.9 %collective-permute-done.34 = f16[64,1280]{1,0:T(8,128)(2,1)S(1)} collective-permute-done((f16[64,1280]{1,0:T(8,128)(2,1)S(1)}, f16[64,1280]{1,0:T(8,128)(2,1)S(1)}, u32[]{:S(2)}, u32[]{:S(2)}) %collective-permute-start.34) | collective-permute-done | bytes 163872 | tf_op jit(solution)/shard_map/ppermute | solution.py:19
  117.0 1.1 collective-permute-start.31
  118.3 7.7 %collective-permute-done.32 = f16[64,1280]{1,0:T(8,128)(2,1)S(1)} collective-permute-done((f16[64,1280]{1,0:T(8,128)(2,1)S(1)}, f16[64,1280]{1,0:T(8,128)(2,1)S(1)}, u32[]{:S(2)}, u32[]{:S(2)}) %collective-permute-start.32) | collective-permute-done | bytes 163872 | tf_op jit(solution)/shard_map/ppermute | solution.py:19
  126.8 1.5 collective-permute-start.36
  129.4 5.1 %collective-permute-done.27 = f32[128,512]{1,0:T(8,128)S(1)} collective-permute-done((f32[128,512]{1,0:T(8,128)S(1)}, f32[128,512]{1,0:T(8,128)S(1)}, u32[]{:S(2)}, u32[]{:S(2)}) %collective-permute-start.27) | collective-permute-done | bytes 262176 | tf_op jit(solution)/shard_map/ppermute | solution.py:19
  135.2 1.0 bitcast_dynamic-update-slice_fusion.7
  136.2 1.0 bitcast_dynamic-update-slice_fusion.6
  137.2 1.0 bitcast_dynamic-update-slice_fusion.5
  138.3 1.0 bitcast_dynamic-update-slice_fusion.4
  139.3 1.0 bitcast_dynamic-update-slice_fusion.3
  140.3 1.0 bitcast_dynamic-update-slice_fusion.2
  141.3 1.2 bitcast_dynamic-update-slice_fusion.1
  142.5 1.0 bitcast_dynamic-update-slice_fusion
  143.5 5.3 %fusion.8 = bf16[16,32,3,128]{3,1,2,0:T(8,128)(2,1)S(1)} fusion(bf16[3,3,512,128]{3,2,1,0:T(8,128)(2,1)S(1)} %bitcast.109, bf16[16,4,8,5,512]{4,0,3,2,1:T(8,128)(2,1)S(1)} %copy-done.22, pred[32,3]{0,1:T(4,128)(4,1)S(1)} %copy-done.27), kind=kOutput, calls=%fused_computation.24 | convolution fusion | flops 1736835072 | bytes 4194400 | tf_op jit(solution)/shard_map/conv_general_dilated | solution.py:391
  149.4 2.5 %collective-permute-start.21 = (bf16[1,16,16,128]{3,1,2,0:T(8,128)(2,1)S(1)}, bf16[1,16,16,128]{3,1,2,0:T(8,128)(2,1)S(1)}, u32[]{:S(2)}, u32[]{:S(2)}) collective-permute-start(bf16[1,16,16,128]{3,1,2,0:T(8,128)(2,1)S(1)} %get-tuple-element.77), channel_id=1, source_target_pairs={{0,2},{1,3},{2,0},{3,1},{4,6},{5,7},{6,4},{7,5},{8,10},{9,11},{10,... | collective-permute-start | bytes 196616 | tf_op jit(solution)/shard_map/ppermute | solution.py:19
  152.5 4.1 %shard_map.104 = (f32[576,256]{1,0:T(8,128)S(1)}, f32[576,256]{1,0:T(8,128)S(1)}) custom-call(s32[12]{0:T(128)S(1)} %stack.138.refs_0_, f32[576,1152]{1,0:T(8,128)S(1)} %copy-done.5, f32[512,512]{1,0:T(8,128)S(1)} %copy-done.6, f32[64,1152]{1,0:T(8,128)S(1)} %get-tuple-element.68.refs_3_, f32[64,1152]{1,0:T(8,128)S(1)} %convert_multiply_fusion.6.refs_4_, ...), custom_call_target="tpu_custom_call" | custom-call | flops 2944401408 | bytes 3833856 | tf_op jit(solution)/shard_map/pallas_call | solution.py:180
  157.4 1.3 collective-permute-done.38
  158.9 1.8 %collective-permute-start.39 = (f32[576,128]{1,0:T(8,128)S(1)}, f32[576,128]{1,0:T(8,128)S(1)}, u32[]{:S(2)}, u32[]{:S(2)}) collective-permute-start(f32[576,128]{1,0:T(8,128)S(1)} %slice.104), channel_id=1, source_target_pairs={{0,2},{1,3},{2,0},{3,1},{4,6},{5,7},{6,4},{7,5},{8,10},{9,11},{10,... | collective-permute-start | bytes 884744 | tf_op jit(solution)/shard_map/ppermute | solution.py:19
  160.7 0.7 pad_maximum_fusion.3
  161.4 10.8 %collective-permute-done.29 = f32[128,512]{1,0:T(8,128)S(1)} collective-permute-done((f32[128,512]{1,0:T(8,128)S(1)}, f32[128,512]{1,0:T(8,128)S(1)}, u32[]{:S(2)}, u32[]{:S(2)}) %collective-permute-start.29) | collective-permute-done | bytes 262176 | tf_op jit(solution)/shard_map/ppermute | solution.py:19
  172.2 0.8 add_multiply_fusion
  173.7 3.8 %bitcast_add_fusion = f32[1152,576]{0,1:T(8,128)} fusion(f32[576,1152]{1,0:T(8,128)S(1)} %get-tuple-element.60, f32[576,1152]{1,0:T(8,128)} %collective-permute-done.24, f32[1152,576]{0,1:T(8,128)S(1)} %copy-done.21), kind=kLoop, calls=%fused_computation.2 | loop fusion | flops 2654208 | bytes 10616832 | tf_op jit(solution)/shard_map/add | solution.py:326
  (137 shorter events, 11.6 us)
Async XLA Ops:
  0.6 44.2 %copy-start = (bf16[576,512]{1,0:T(8,128)(2,1)S(1)}, bf16[576,512]{1,0:T(8,128)(2,1)}, u32[]{:S(2)}) copy-start(bf16[576,512]{1,0:T(8,128)(2,1)} %param.9) | copy-start | bytes 1769476
  0.6 26.5 %copy-start.1 = (bf16[1,16,16,512]{3,2,1,0:T(8,128)(2,1)S(1)}, bf16[1,16,16,512]{3,2,1,0:T(8,128)(2,1)}, u32[]{:S(2)}) copy-start(bf16[1,16,16,512]{3,2,1,0:T(8,128)(2,1)} %refs_1_.2) | copy-start | bytes 786436
  0.7 9.5 %collective-permute-start = (bf16[1,16,16,512]{3,2,1,0:T(8,128)(2,1)}, bf16[1,16,16,512]{3,2,1,0:T(8,128)(2,1)S(1)}, u32[]{:S(2)}, u32[]{:S(2)}) collective-permute-start(bf16[1,16,16,512]{3,2,1,0:T(8,128)(2,1)} %refs_1_.2), channel_id=1, source_target_pairs={{0,2},{1,3},{2,0},{3,1},{4,6},{5,7},{6,4},{7,5},{8,10},{9,11},{10,... | collective-permute-start | bytes 786440 | tf_op jit(solution)/shard_map/ppermute | solution.py:19
  3.7 9.9 %collective-permute-start.1 = (bf16[1,16,16,512]{3,2,1,0:T(8,128)(2,1)}, bf16[1,16,16,512]{3,2,1,0:T(8,128)(2,1)S(1)}, u32[]{:S(2)}, u32[]{:S(2)}) collective-permute-start(bf16[1,16,16,512]{3,2,1,0:T(8,128)(2,1)} %refs_1_.2), channel_id=1, source_target_pairs={{0,8},{4,12},{8,16},{12,20},{16,24},{20,28},{24,0},{28,4},{1,9},{5... | collective-permute-start | bytes 786440 | tf_op jit(solution)/shard_map/ppermute | solution.py:19
  5.3 8.3 %collective-permute-start.2 = (bf16[1,16,16,512]{3,2,1,0:T(8,128)(2,1)}, bf16[1,16,16,512]{3,2,1,0:T(8,128)(2,1)S(1)}, u32[]{:S(2)}, u32[]{:S(2)}) collective-permute-start(bf16[1,16,16,512]{3,2,1,0:T(8,128)(2,1)} %refs_1_.2), channel_id=1, source_target_pairs={{0,4},{4,0},{8,12},{12,8},{16,20},{20,16},{24,28},{28,24},{1,5},{5... | collective-permute-start | bytes 786440 | tf_op jit(solution)/shard_map/ppermute | solution.py:19
  10.2 17.8 %copy-start.3 = (bf16[1,16,16,512]{3,2,1,0:T(8,128)(2,1)}, bf16[1,16,16,512]{3,2,1,0:T(8,128)(2,1)S(1)}, u32[]{:S(2)}) copy-start(bf16[1,16,16,512]{3,2,1,0:T(8,128)(2,1)S(1)} %collective-permute-done.refs_4_) | copy-start | bytes 786436
  13.6 9.1 %copy-start.13 = (bf16[1,16,16,512]{3,2,1,0:T(8,128)(2,1)}, bf16[1,16,16,512]{3,2,1,0:T(8,128)(2,1)S(1)}, u32[]{:S(2)}) copy-start(bf16[1,16,16,512]{3,2,1,0:T(8,128)(2,1)S(1)} %collective-permute-done.1.refs_2_) | copy-start | bytes 786436
  13.6 24.9 %copy-start.15 = (bf16[1,16,16,512]{3,2,1,0:T(8,128)(2,1)}, bf16[1,16,16,512]{3,2,1,0:T(8,128)(2,1)S(1)}, u32[]{:S(2)}) copy-start(bf16[1,16,16,512]{3,2,1,0:T(8,128)(2,1)S(1)} %collective-permute-done.2.refs_3_) | copy-start | bytes 786436
  13.6 9.1 %collective-permute-start.3 = (bf16[1,16,16,512]{3,2,1,0:T(8,128)(2,1)}, bf16[1,16,16,512]{3,2,1,0:T(8,128)(2,1)S(1)}, u32[]{:S(2)}, u32[]{:S(2)}) collective-permute-start(bf16[1,16,16,512]{3,2,1,0:T(8,128)(2,1)} %refs_1_.2), channel_id=1, source_target_pairs={{0,24},{4,28},{8,0},{12,4},{16,8},{20,12},{24,16},{28,20},{1,25},{... | collective-permute-start | bytes 786440 | tf_op jit(solution)/shard_map/ppermute | solution.py:19
  15.3 7.4 %collective-permute-start.4 = (bf16[1,16,16,512]{3,2,1,0:T(8,128)(2,1)S(1)}, bf16[1,16,16,512]{3,2,1,0:T(8,128)(2,1)S(1)}, u32[]{:S(2)}, u32[]{:S(2)}) collective-permute-start(bf16[1,16,16,512]{3,2,1,0:T(8,128)(2,1)S(1)} %collective-permute-done.1.refs_2_), channel_id=1, source_target_pairs={{0,4},{4,0},{8,12},{12,8},{16,20},{20,16},{24,28},{28,24},{1,5},{5... | collective-permute-start | bytes 786440 | tf_op jit(solution)/shard_map/ppermute | solution.py:19
  16.8 6.7 %collective-permute-start.5 = (bf16[1,16,16,512]{3,2,1,0:T(8,128)(2,1)S(1)}, bf16[1,16,16,512]{3,2,1,0:T(8,128)(2,1)S(1)}, u32[]{:S(2)}, u32[]{:S(2)}) collective-permute-start(bf16[1,16,16,512]{3,2,1,0:T(8,128)(2,1)S(1)} %collective-permute-done.1.refs_2_), channel_id=1, source_target_pairs={{0,2},{1,3},{2,0},{3,1},{4,6},{5,7},{6,4},{7,5},{8,10},{9,11},{10,... | collective-permute-start | bytes 786440 | tf_op jit(solution)/shard_map/ppermute | solution.py:19
  19.1 21.4 %copy-start.23 = (bf16[1,16,16,512]{3,2,1,0:T(8,128)(2,1)S(1)}, bf16[1,16,16,512]{3,2,1,0:T(8,128)(2,1)}, u32[]{:S(2)}) copy-start(bf16[1,16,16,512]{3,2,1,0:T(8,128)(2,1)} %param.8) | copy-start | bytes 786436
  19.1 13.1 %all-to-all-start = ((bf16[8,64,256]{2,1,0:T(8,128)(2,1)}), bf16[8,64,256]{2,1,0:T(8,128)(2,1)S(1)}, u32[]{:S(2)}, u32[]{:S(2)}) async-start(bf16[8,64,256]{2,1,0:T(8,128)(2,1)} %bitcast.45), calls=%async_computation | async-start | bytes 524288 | tf_op jit(solution)/shard_map/all_to_all | solution.py:277
  22.7 18.1 %copy-start.7 = (bf16[1,16,16,512]{3,2,1,0:T(8,128)(2,1)}, bf16[1,16,16,512]{3,2,1,0:T(8,128)(2,1)S(1)}, u32[]{:S(2)}) copy-start(bf16[1,16,16,512]{3,2,1,0:T(8,128)(2,1)S(1)} %collective-permute-done.3.refs_1_) | copy-start | bytes 786436
  23.5 17.4 %copy-start.19 = (bf16[1,16,16,512]{3,2,1,0:T(8,128)(2,1)}, bf16[1,16,16,512]{3,2,1,0:T(8,128)(2,1)S(1)}, u32[]{:S(2)}) copy-start(bf16[1,16,16,512]{3,2,1,0:T(8,128)(2,1)S(1)} %collective-permute-done.5.refs_6_) | copy-start | bytes 786436
  23.5 8.8 %collective-permute-start.7 = (bf16[1,16,16,512]{3,2,1,0:T(8,128)(2,1)S(1)}, bf16[1,16,16,512]{3,2,1,0:T(8,128)(2,1)S(1)}, u32[]{:S(2)}, u32[]{:S(2)}) collective-permute-start(bf16[1,16,16,512]{3,2,1,0:T(8,128)(2,1)S(1)} %collective-permute-done.3.refs_1_), channel_id=1, source_target_pairs={{0,4},{4,0},{8,12},{12,8},{16,20},{20,16},{24,28},{28,24},{1,5},{5... | collective-permute-start | bytes 786440 | tf_op jit(solution)/shard_map/ppermute | solution.py:19
  25.4 6.9 %collective-permute-start.8 = (bf16[1,16,16,512]{3,2,1,0:T(8,128)(2,1)S(1)}, bf16[1,16,16,512]{3,2,1,0:T(8,128)(2,1)S(1)}, u32[]{:S(2)}, u32[]{:S(2)}) collective-permute-start(bf16[1,16,16,512]{3,2,1,0:T(8,128)(2,1)S(1)} %collective-permute-done.3.refs_1_), channel_id=1, source_target_pairs={{0,2},{1,3},{2,0},{3,1},{4,6},{5,7},{6,4},{7,5},{8,10},{9,11},{10,... | collective-permute-start | bytes 786440 | tf_op jit(solution)/shard_map/ppermute | solution.py:19
  28.0 13.4 %collective-permute-start.6 = (bf16[1,16,16,512]{3,2,1,0:T(8,128)(2,1)S(1)}, bf16[1,16,16,512]{3,2,1,0:T(8,128)(2,1)}, u32[]{:S(2)}, u32[]{:S(2)}) collective-permute-start(bf16[1,16,16,512]{3,2,1,0:T(8,128)(2,1)S(1)} %copy-done.1), channel_id=1, source_target_pairs={{0,16},{4,20},{8,24},{12,28},{16,0},{20,4},{24,8},{28,12},{1,17},{... | collective-permute-start | bytes 786440 | tf_op jit(solution)/shard_map/ppermute | solution.py:19
  32.3 17.6 %copy-start.4 = (bf16[1,16,16,512]{3,2,1,0:T(8,128)(2,1)S(1)}, bf16[1,16,16,512]{3,2,1,0:T(8,128)(2,1)}, u32[]{:S(2)}) copy-start(bf16[1,16,16,512]{3,2,1,0:T(8,128)(2,1)} %copy-done.3) | copy-start | bytes 786436
  32.3 8.6 %copy-start.9 = (bf16[1,16,16,512]{3,2,1,0:T(8,128)(2,1)}, bf16[1,16,16,512]{3,2,1,0:T(8,128)(2,1)S(1)}, u32[]{:S(2)}) copy-start(bf16[1,16,16,512]{3,2,1,0:T(8,128)(2,1)S(1)} %collective-permute-done.7.refs_2_) | copy-start | bytes 786436
  32.3 8.6 %copy-start.11 = (bf16[1,16,16,512]{3,2,1,0:T(8,128)(2,1)}, bf16[1,16,16,512]{3,2,1,0:T(8,128)(2,1)S(1)}, u32[]{:S(2)}) copy-start(bf16[1,16,16,512]{3,2,1,0:T(8,128)(2,1)S(1)} %collective-permute-done.8.refs_3_) | copy-start | bytes 786436
  32.3 10.5 %collective-permute-start.9 = (bf16[1,16,16,512]{3,2,1,0:T(8,128)(2,1)S(1)}, bf16[1,16,16,512]{3,2,1,0:T(8,128)(2,1)S(1)}, u32[]{:S(2)}, u32[]{:S(2)}) collective-permute-start(bf16[1,16,16,512]{3,2,1,0:T(8,128)(2,1)S(1)} %collective-permute-done.5.refs_6_), channel_id=1, source_target_pairs={{0,4},{4,0},{8,12},{12,8},{16,20},{20,16},{24,28},{28,24},{1,5},{5... | collective-permute-start | bytes 786440 | tf_op jit(solution)/shard_map/ppermute | solution.py:19
  38.5 6.4 %collective-permute-start.10 = (bf16[1,16,16,512]{3,2,1,0:T(8,128)(2,1)S(1)}, bf16[1,16,16,512]{3,2,1,0:T(8,128)(2,1)S(1)}, u32[]{:S(2)}, u32[]{:S(2)}) collective-permute-start(bf16[1,16,16,512]{3,2,1,0:T(8,128)(2,1)S(1)} %collective-permute-done.2.refs_3_), channel_id=1, source_target_pairs={{0,2},{1,3},{2,0},{3,1},{4,6},{5,7},{6,4},{7,5},{8,10},{9,11},{10,... | collective-permute-start | bytes 786440 | tf_op jit(solution)/shard_map/ppermute | solution.py:19
  40.2 9.7 %copy-start.16 = (bf16[1,16,16,512]{3,2,1,0:T(8,128)(2,1)S(1)}, bf16[1,16,16,512]{3,2,1,0:T(8,128)(2,1)}, u32[]{:S(2)}) copy-start(bf16[1,16,16,512]{3,2,1,0:T(8,128)(2,1)} %copy-done.15) | copy-start | bytes 786436
  40.2 9.7 %collective-permute-start.23 = (bf16[8,64,256]{2,1,0:T(8,128)(2,1)S(1)}, bf16[8,64,256]{2,1,0:T(8,128)(2,1)S(1)}, u32[]{:S(2)}, u32[]{:S(2)}) collective-permute-start(bf16[8,64,256]{2,1,0:T(8,128)(2,1)S(1)} %all-to-all-done.refs_9_), channel_id=1, source_target_pairs={{0,2},{1,3},{2,0},{3,1},{4,6},{5,7},{6,4},{7,5},{8,10},{9,11},{10,... | collective-permute-start | bytes 786440 | tf_op jit(solution)/shard_map/ppermute | solution.py:19
  40.8 9.0 %copy-start.20 = (bf16[1,16,16,512]{3,2,1,0:T(8,128)(2,1)S(1)}, bf16[1,16,16,512]{3,2,1,0:T(8,128)(2,1)}, u32[]{:S(2)}) copy-start(bf16[1,16,16,512]{3,2,1,0:T(8,128)(2,1)} %copy-done.19) | copy-start | bytes 786436
  40.9 24.1 %collective-permute-start.25 = (f32[2,128,512]{2,1,0:T(8,128)S(1)}, f32[2,128,512]{2,1,0:T(8,128)S(1)}, u32[]{:S(2)}, u32[]{:S(2)}) collective-permute-start(f32[2,128,512]{2,1,0:T(8,128)S(1)} %dynamic-slice_bitcast_fusion), channel_id=1, source_target_pairs={{0,1},{1,0},{2,3},{3,2},{4,5},{5,4},{6,7},{7,6},{8,9},{9,8},{10,11... | collective-permute-start | bytes 1572872 | tf_op jit(solution)/shard_map/ppermute | solution.py:19
  44.9 30.3 %collective-permute-start.13 = (bf16[576,128]{1,0:T(8,128)(2,1)S(1)}, bf16[576,128]{1,0:T(8,128)(2,1)S(1)}, u32[]{:S(2)}, u32[]{:S(2)}) collective-permute-start(bf16[576,128]{1,0:T(8,128)(2,1)S(1)} %constant_dynamic-slice_fusion.4), channel_id=1, source_target_pairs={{0,16},{4,20},{8,24},{12,28},{16,0},{20,4},{24,8},{28,12},{1,17},{... | collective-permute-start | bytes 442376 | tf_op jit(solution)/shard_map/ppermute | solution.py:19
  44.9 31.0 %collective-permute-start.12 = (bf16[576,128]{1,0:T(8,128)(2,1)S(1)}, bf16[576,128]{1,0:T(8,128)(2,1)S(1)}, u32[]{:S(2)}, u32[]{:S(2)}) collective-permute-start(bf16[576,128]{1,0:T(8,128)(2,1)S(1)} %constant_dynamic-slice_fusion.4), channel_id=1, source_target_pairs={{0,8},{4,12},{8,16},{12,20},{16,24},{20,28},{24,0},{28,4},{1,9},{5... | collective-permute-start | bytes 442376 | tf_op jit(solution)/shard_map/ppermute | solution.py:19
  46.2 19.5 %collective-permute-start.15 = (bf16[1,16,16,512]{3,2,1,0:T(8,128)(2,1)}, bf16[1,16,16,512]{3,2,1,0:T(8,128)(2,1)S(1)}, u32[]{:S(2)}, u32[]{:S(2)}) collective-permute-start(bf16[1,16,16,512]{3,2,1,0:T(8,128)(2,1)} %collective-permute-done.6.refs_4_), channel_id=1, source_target_pairs={{0,2},{1,3},{2,0},{3,1},{4,6},{5,7},{6,4},{7,5},{8,10},{9,11},{10,... | collective-permute-start | bytes 786440 | tf_op jit(solution)/shard_map/ppermute | solution.py:19
  49.8 27.0 %collective-permute-start.11 = (bf16[2,16,16,512]{3,2,1,0:T(8,128)(2,1)}, bf16[2,16,16,512]{3,2,1,0:T(8,128)(2,1)S(1)}, u32[]{:S(2)}, u32[]{:S(2)}) collective-permute-start(bf16[2,16,16,512]{3,2,1,0:T(8,128)(2,1)} %pad_maximum_fusion.1), channel_id=1, source_target_pairs={{0,1},{1,0},{2,3},{3,2},{4,5},{5,4},{6,7},{7,6},{8,9},{9,8},{10,11... | collective-permute-start | bytes 1572872 | tf_op jit(solution)/shard_map/ppermute | solution.py:19
  65.0 10.2 %copy-start.10 = (bf16[1,16,16,512]{3,2,1,0:T(8,128)(2,1)S(1)}, bf16[1,16,16,512]{3,2,1,0:T(8,128)(2,1)}, u32[]{:S(2)}) copy-start(bf16[1,16,16,512]{3,2,1,0:T(8,128)(2,1)} %copy-done.9) | copy-start | bytes 786436
  65.0 11.0 %collective-permute-start.14 = (bf16[576,128]{1,0:T(8,128)(2,1)S(1)}, bf16[576,128]{1,0:T(8,128)(2,1)S(1)}, u32[]{:S(2)}, u32[]{:S(2)}) collective-permute-start(bf16[576,128]{1,0:T(8,128)(2,1)S(1)} %constant_dynamic-slice_fusion.4), channel_id=1, source_target_pairs={{0,24},{4,28},{8,0},{12,4},{16,8},{20,12},{24,16},{28,20},{1,25},{... | collective-permute-start | bytes 442376 | tf_op jit(solution)/shard_map/ppermute | solution.py:19
  65.7 8.6 %collective-permute-start.16 = (bf16[1,16,16,512]{3,2,1,0:T(8,128)(2,1)}, bf16[1,16,16,512]{3,2,1,0:T(8,128)(2,1)S(1)}, u32[]{:S(2)}, u32[]{:S(2)}) collective-permute-start(bf16[1,16,16,512]{3,2,1,0:T(8,128)(2,1)} %collective-permute-done.6.refs_4_), channel_id=1, source_target_pairs={{0,4},{4,0},{8,12},{12,8},{16,20},{20,16},{24,28},{28,24},{1,5},{5... | collective-permute-start | bytes 786440 | tf_op jit(solution)/shard_map/ppermute | solution.py:19
  66.6 32.1 %copy-start.24 = (f32[2,128,512]{2,1,0:T(8,128)}, f32[2,128,512]{2,1,0:T(8,128)S(1)}, u32[]{:S(2)}) copy-start(f32[2,128,512]{2,1,0:T(8,128)S(1)} %bitcast_add_fusion.1) | copy-start | bytes 1572868
  74.3 7.6 %collective-permute-start.17 = (bf16[1,16,16,512]{3,2,1,0:T(8,128)(2,1)S(1)}, bf16[1,16,16,512]{3,2,1,0:T(8,128)(2,1)S(1)}, u32[]{:S(2)}, u32[]{:S(2)}) collective-permute-start(bf16[1,16,16,512]{3,2,1,0:T(8,128)(2,1)S(1)} %collective-permute-done.15.refs_6_), channel_id=1, source_target_pairs={{0,4},{4,0},{8,12},{12,8},{16,20},{20,16},{24,28},{28,24},{1,5},{5... | collective-permute-start | bytes 786440 | tf_op jit(solution)/shard_map/ppermute | solution.py:19
  75.2 7.3 %collective-permute-start.18 = (bf16[1,16,16,512]{3,2,1,0:T(8,128)(2,1)S(1)}, bf16[1,16,16,512]{3,2,1,0:T(8,128)(2,1)S(1)}, u32[]{:S(2)}, u32[]{:S(2)}) collective-permute-start(bf16[1,16,16,512]{3,2,1,0:T(8,128)(2,1)S(1)} %copy-done.10), channel_id=1, source_target_pairs={{0,2},{1,3},{2,0},{3,1},{4,6},{5,7},{6,4},{7,5},{8,10},{9,11},{10,... | collective-permute-start | bytes 786440 | tf_op jit(solution)/shard_map/ppermute | solution.py:19
  78.8 3.7 %copy-start.8 = (bf16[1,16,16,512]{3,2,1,0:T(8,128)(2,1)S(1)}, bf16[1,16,16,512]{3,2,1,0:T(8,128)(2,1)}, u32[]{:S(2)}) copy-start(bf16[1,16,16,512]{3,2,1,0:T(8,128)(2,1)} %copy-done.7) | copy-start | bytes 786436
  78.8 3.7 %copy-start.12 = (bf16[1,16,16,512]{3,2,1,0:T(8,128)(2,1)S(1)}, bf16[1,16,16,512]{3,2,1,0:T(8,128)(2,1)}, u32[]{:S(2)}) copy-start(bf16[1,16,16,512]{3,2,1,0:T(8,128)(2,1)} %copy-done.11) | copy-start | bytes 786436
  95.7 5.4 %collective-permute-start.30 = (f32[64,1152]{1,0:T(8,128)S(1)}, f32[64,1152]{1,0:T(8,128)S(1)}, u32[]{:S(2)}, u32[]{:S(2)}) collective-permute-start(f32[64,1152]{1,0:T(8,128)S(1)} %get-tuple-element.65), channel_id=1, source_target_pairs={{0,1},{1,0},{2,3},{3,2},{4,5},{5,4},{6,7},{7,6},{8,9},{9,8},{10,11... | collective-permute-start | bytes 884744 | tf_op jit(solution)/shard_map/ppermute | solution.py:19
  97.5 37.7 %collective-permute-start.19 = (bf16[4,576,128]{2,1,0:T(8,128)(2,1)}, bf16[4,576,128]{2,1,0:T(8,128)(2,1)}, u32[]{:S(2)}, u32[]{:S(2)}) collective-permute-start(bf16[4,576,128]{2,1,0:T(8,128)(2,1)} %pad_maximum_fusion), channel_id=1, source_target_pairs={{0,4},{4,0},{8,12},{12,8},{16,20},{20,16},{24,28},{28,24},{1,5},{5... | collective-permute-start | bytes 1769480 | tf_op jit(solution)/shard_map/ppermute | solution.py:19
  99.4 8.8 %collective-permute-start.26 = (f32[128,512]{1,0:T(8,128)}, f32[128,512]{1,0:T(8,128)}, u32[]{:S(2)}, u32[]{:S(2)}) collective-permute-start(f32[128,512]{1,0:T(8,128)} %dynamic-slice_bitcast_fusion.1), channel_id=1, source_target_pairs={{0,2},{1,3},{2,0},{3,1},{4,6},{5,7},{6,4},{7,5},{8,10},{9,11},{10,... | collective-permute-start | bytes 786440 | tf_op jit(solution)/shard_map/ppermute | solution.py:19
  101.1 72.6 %collective-permute-start.24 = (f32[576,1152]{1,0:T(8,128)}, f32[576,1152]{1,0:T(8,128)}, u32[]{:S(2)}, u32[]{:S(2)}) collective-permute-start(f32[576,1152]{1,0:T(8,128)} %get-tuple-element.61), channel_id=1, source_target_pairs={{0,1},{1,0},{2,3},{3,2},{4,5},{5,4},{6,7},{7,6},{8,9},{9,8},{10,11... | collective-permute-start | bytes 7962632 | tf_op jit(solution)/shard_map/ppermute | solution.py:19
  103.2 5.0 %copy-start.25 = (f32[2,128,512]{2,1,0:T(8,128)S(1)}, f32[2,128,512]{2,1,0:T(8,128)}, u32[]{:S(2)}) copy-start(f32[2,128,512]{2,1,0:T(8,128)} %copy-done.24) | copy-start | bytes 1572868
  104.3 12.6 %collective-permute-start.34 = (f16[64,1280]{1,0:T(8,128)(2,1)S(1)}, f16[64,1280]{1,0:T(8,128)(2,1)S(1)}, u32[]{:S(2)}, u32[]{:S(2)}) collective-permute-start(f16[64,1280]{1,0:T(8,128)(2,1)S(1)} %concatenate.19), channel_id=1, source_target_pairs={{0,4},{4,0},{8,12},{12,8},{16,20},{20,16},{24,28},{28,24},{1,5},{5... | collective-permute-start | bytes 491528 | tf_op jit(solution)/shard_map/ppermute | solution.py:19
  109.2 17.6 %collective-permute-start.33 = (f16[64,1280]{1,0:T(8,128)(2,1)S(1)}, f16[64,1280]{1,0:T(8,128)(2,1)S(1)}, u32[]{:S(2)}, u32[]{:S(2)}) collective-permute-start(f16[64,1280]{1,0:T(8,128)(2,1)S(1)} %concatenate.19), channel_id=1, source_target_pairs={{0,24},{4,28},{8,0},{12,4},{16,8},{20,12},{24,16},{28,20},{1,25},{... | collective-permute-start | bytes 491528 | tf_op jit(solution)/shard_map/ppermute | solution.py:19
  109.7 16.3 %collective-permute-start.32 = (f16[64,1280]{1,0:T(8,128)(2,1)S(1)}, f16[64,1280]{1,0:T(8,128)(2,1)S(1)}, u32[]{:S(2)}, u32[]{:S(2)}) collective-permute-start(f16[64,1280]{1,0:T(8,128)(2,1)S(1)} %concatenate.19), channel_id=1, source_target_pairs={{0,16},{4,20},{8,24},{12,28},{16,0},{20,4},{24,8},{28,12},{1,17},{... | collective-permute-start | bytes 491528 | tf_op jit(solution)/shard_map/ppermute | solution.py:19
  117.0 11.3 %collective-permute-start.31 = (f16[64,1280]{1,0:T(8,128)(2,1)S(1)}, f16[64,1280]{1,0:T(8,128)(2,1)S(1)}, u32[]{:S(2)}, u32[]{:S(2)}) collective-permute-start(f16[64,1280]{1,0:T(8,128)(2,1)S(1)} %concatenate.19), channel_id=1, source_target_pairs={{0,8},{4,12},{8,16},{12,20},{16,24},{20,28},{24,0},{28,4},{1,9},{5... | collective-permute-start | bytes 491528 | tf_op jit(solution)/shard_map/ppermute | solution.py:19
  126.0 8.5 %collective-permute-start.27 = (f32[128,512]{1,0:T(8,128)S(1)}, f32[128,512]{1,0:T(8,128)S(1)}, u32[]{:S(2)}, u32[]{:S(2)}) collective-permute-start(f32[128,512]{1,0:T(8,128)S(1)} %bitcast_add_fusion.2), channel_id=1, source_target_pairs={{0,4},{4,0},{8,12},{12,8},{16,20},{20,16},{24,28},{28,24},{1,5},{5... | collective-permute-start | bytes 786440 | tf_op jit(solution)/shard_map/ppermute | solution.py:19
  126.8 22.6 %collective-permute-start.36 = (f16[64,1280]{1,0:T(8,128)(2,1)S(1)}, f16[64,1280]{1,0:T(8,128)(2,1)S(1)}, u32[]{:S(2)}, u32[]{:S(2)}) collective-permute-start(f16[64,1280]{1,0:T(8,128)(2,1)S(1)} %collective-permute-done.32), channel_id=1, source_target_pairs={{0,4},{4,0},{8,12},{12,8},{16,20},{20,16},{24,28},{28,24},{1,5},{5... | collective-permute-start | bytes 491528 | tf_op jit(solution)/shard_map/ppermute | solution.py:19
  128.3 20.8 %collective-permute-start.37 = (f16[64,1280]{1,0:T(8,128)(2,1)S(1)}, f16[64,1280]{1,0:T(8,128)(2,1)S(1)}, u32[]{:S(2)}, u32[]{:S(2)}) collective-permute-start(f16[64,1280]{1,0:T(8,128)(2,1)S(1)} %collective-permute-done.33), channel_id=1, source_target_pairs={{0,4},{4,0},{8,12},{12,8},{16,20},{20,16},{24,28},{28,24},{1,5},{5... | collective-permute-start | bytes 491528 | tf_op jit(solution)/shard_map/ppermute | solution.py:19
  134.5 17.5 %collective-permute-start.35 = (f16[64,1280]{1,0:T(8,128)(2,1)S(1)}, f16[64,1280]{1,0:T(8,128)(2,1)S(1)}, u32[]{:S(2)}, u32[]{:S(2)}) collective-permute-start(f16[64,1280]{1,0:T(8,128)(2,1)S(1)} %collective-permute-done.31), channel_id=1, source_target_pairs={{0,4},{4,0},{8,12},{12,8},{16,20},{20,16},{24,28},{28,24},{1,5},{5... | collective-permute-start | bytes 491528 | tf_op jit(solution)/shard_map/ppermute | solution.py:19
  135.2 22.1 %collective-permute-start.28 = (f32[128,512]{1,0:T(8,128)S(1)}, f32[128,512]{1,0:T(8,128)S(1)}, u32[]{:S(2)}, u32[]{:S(2)}) collective-permute-start(f32[128,512]{1,0:T(8,128)S(1)} %add.343), channel_id=1, source_target_pairs={{0,8},{4,12},{8,0},{12,4},{16,24},{20,28},{24,16},{28,20},{1,9},{5... | collective-permute-start | bytes 786440 | tf_op jit(solution)/shard_map/ppermute | solution.py:19
  141.3 2.2 %copy-start.27 = (pred[32,3]{0,1:T(4,128)(4,1)S(1)}, pred[32,3]{0,1:T(4,128)(4,1)}, u32[]{:S(2)}) copy-start(pred[32,3]{0,1:T(4,128)(4,1)} %constant.290) | copy-start | bytes 292
  143.5 9.0 %copy-start.6 = (f32[512,512]{1,0:T(8,128)S(1)}, f32[512,512]{1,0:T(8,128)}, u32[]{:S(2)}) copy-start(f32[512,512]{1,0:T(8,128)} %refs_2_.1) | copy-start | bytes 3145732
  148.9 3.7 %copy-start.5 = (f32[576,1152]{1,0:T(8,128)S(1)}, f32[576,1152]{1,0:T(8,128)}, u32[]{:S(2)}) copy-start(f32[576,1152]{1,0:T(8,128)} %refs_1_.3) | copy-start | bytes 7962628
  149.1 7.5 %collective-permute-start.22 = (bf16[1,16,16,128]{3,1,2,0:T(8,128)(2,1)S(1)}, bf16[1,16,16,128]{3,1,2,0:T(8,128)(2,1)S(1)}, u32[]{:S(2)}, u32[]{:S(2)}) collective-permute-start(bf16[1,16,16,128]{3,1,2,0:T(8,128)(2,1)S(1)} %slice_bitcast_fusion), channel_id=1, source_target_pairs={{0,3},{1,2},{2,1},{3,0},{4,7},{5,6},{6,5},{7,4},{8,11},{9,10},{10,... | collective-permute-start | bytes 196616 | tf_op jit(solution)/shard_map/ppermute | solution.py:19
  149.4 7.7 %collective-permute-start.21 = (bf16[1,16,16,128]{3,1,2,0:T(8,128)(2,1)S(1)}, bf16[1,16,16,128]{3,1,2,0:T(8,128)(2,1)S(1)}, u32[]{:S(2)}, u32[]{:S(2)}) collective-permute-start(bf16[1,16,16,128]{3,1,2,0:T(8,128)(2,1)S(1)} %get-tuple-element.77), channel_id=1, source_target_pairs={{0,2},{1,3},{2,0},{3,1},{4,6},{5,7},{6,4},{7,5},{8,10},{9,11},{10,... | collective-permute-start | bytes 196616 | tf_op jit(solution)/shard_map/ppermute | solution.py:19
  152.0 5.1 %collective-permute-start.20 = (bf16[1,16,16,128]{3,1,2,0:T(8,128)(2,1)S(1)}, bf16[1,16,16,128]{3,1,2,0:T(8,128)(2,1)S(1)}, u32[]{:S(2)}, u32[]{:S(2)}) collective-permute-start(bf16[1,16,16,128]{3,1,2,0:T(8,128)(2,1)S(1)} %get-tuple-element.78), channel_id=1, source_target_pairs={{0,1},{1,0},{2,3},{3,2},{4,5},{5,4},{6,7},{7,6},{8,9},{9,8},{10,11... | collective-permute-start | bytes 196616 | tf_op jit(solution)/shard_map/ppermute | solution.py:19
  156.7 2.1 %collective-permute-start.38 = (f32[576,256]{1,0:T(8,128)S(1)}, f32[576,256]{1,0:T(8,128)S(1)}, u32[]{:S(2)}, u32[]{:S(2)}) collective-permute-start(f32[576,256]{1,0:T(8,128)S(1)} %get-tuple-element.67), channel_id=1, source_target_pairs={{0,1},{1,0},{2,3},{3,2},{4,5},{5,4},{6,7},{7,6},{8,9},{9,8},{10,11... | collective-permute-start | bytes 1769480 | tf_op jit(solution)/shard_map/ppermute | solution.py:19
  157.3 14.9 %collective-permute-start.29 = (f32[128,512]{1,0:T(8,128)S(1)}, f32[128,512]{1,0:T(8,128)S(1)}, u32[]{:S(2)}, u32[]{:S(2)}) collective-permute-start(f32[128,512]{1,0:T(8,128)S(1)} %add.344), channel_id=1, source_target_pairs={{0,16},{4,20},{8,24},{12,28},{16,0},{20,4},{24,8},{28,12},{1,17},{... | collective-permute-start | bytes 786440 | tf_op jit(solution)/shard_map/ppermute | solution.py:19
  158.7 13.5 %copy-start.26 = (f32[128,512]{1,0:T(8,128)S(1)}, f32[128,512]{1,0:T(8,128)}, u32[]{:S(2)}) copy-start(f32[128,512]{1,0:T(8,128)} %param.11) | copy-start | bytes 786436
  158.8 14.9 %copy-start.21 = (f32[1152,576]{0,1:T(8,128)S(1)}, f32[1152,576]{0,1:T(8,128)}, u32[]{:S(2)}) copy-start(f32[1152,576]{0,1:T(8,128)} %param.10) | copy-start | bytes 7962628
  158.9 14.1 %collective-permute-start.39 = (f32[576,128]{1,0:T(8,128)S(1)}, f32[576,128]{1,0:T(8,128)S(1)}, u32[]{:S(2)}, u32[]{:S(2)}) collective-permute-start(f32[576,128]{1,0:T(8,128)S(1)} %slice.104), channel_id=1, source_target_pairs={{0,2},{1,3},{2,0},{3,1},{4,6},{5,7},{6,4},{7,5},{8,10},{9,11},{10,... | collective-permute-start | bytes 884744 | tf_op jit(solution)/shard_map/ppermute | solution.py:19
  (5 other events, 5.8 us)

commit v5 on v4

--- a/solution.py
+++ b/solution.py
@@ -42,19 +42,9 @@
     return jnp.concatenate(pieces, axis=3).reshape(-1, width)
 
 
-def products_kernel(pairs, n_pair, first, *refs):
-    place = refs[0]
-    image_refs = refs[1 : 1 + len(pairs)]
-    strip_refs = refs[1 + len(pairs) : 1 + len(pairs) + n_pair]
-    refs = refs[1 + len(pairs) + n_pair :]
-    before, refs = (None, refs) if first else (refs[:4], refs[4:])
-    totals, (shifted, turned, left) = refs[:4], refs[4:]
-    n_images, side, channels = len(image_refs), image_refs[0].shape[1], image_refs[0].shape[3]
+def fill_shifted(image_refs, shifted):
+    side, channels = image_refs[0].shape[1], image_refs[0].shape[3]
     spots = side * side
-    cols, rows = totals[0].shape
-    strip = totals[1].shape[0]
-    fsdp_at = place[2]
-
     spot = lax.broadcasted_iota(jnp.int32, (spots, LANES), 0) % side
     empty = jnp.zeros((side, channels), jnp.bfloat16)
     for at, ref in enumerate(image_refs):
@@ -70,6 +60,22 @@
                 shifted[col_off, at, 1 : side + 1, :, lane : lane + LANES] = moved_part.astype(
                     jnp.bfloat16
                 ).reshape(side, side, LANES)
+
+
+def products_kernel(pairs, n_pair, first, *refs):
+    place = refs[0]
+    image_refs = refs[1 : 1 + len(pairs)]
+    strip_refs = refs[1 + len(pairs) : 1 + len(pairs) + n_pair]
+    refs = refs[1 + len(pairs) + n_pair :]
+    before, refs = (None, refs) if first else (refs[:4], refs[4:])
+    totals, (shifted, turned, left) = refs[:4], refs[4:]
+    n_images, side, channels = len(image_refs), image_refs[0].shape[1], image_refs[0].shape[3]
+    spots = side * side
+    cols, rows = totals[0].shape
+    strip = totals[1].shape[0]
+    fsdp_at = place[2]
+
+    fill_shifted(image_refs, shifted)
 
     def lanes_of_tap(tap, lane):
         piece = shifted[tap % 3, :, pl.ds(tap // 3, side), :, pl.ds(pl.multiple_of(lane, LANES), LANES)]
@@ -193,6 +199,68 @@
             transcendentals=0,
         ),
     )(order, a_inverse, g_inverse, *strips)
+
+
+def conv_kernel(order, *refs):
+    order_ref, refs = refs[0], refs[1:]
+    n_images, n_parts = order
+    image_refs, part_refs = refs[:n_images], refs[n_images : n_images + n_parts]
+    out_refs = refs[n_images + n_parts : -2]
+    shifted, weight = refs[-2:]
+    side, channels = image_refs[0].shape[1], image_refs[0].shape[3]
+    depth = part_refs[0].shape[0]
+    fill_shifted(image_refs, shifted)
+    for at, ref in enumerate(part_refs):
+        weight[pl.ds(pl.multiple_of(order_ref[at] * depth, 64), depth), :] = ref[...]
+    for at, ref in enumerate(out_refs):
+        total = jnp.zeros((side * side, weight.shape[1]), jnp.float32)
+        for tap in range(9):
+            left = shifted[tap % 3, at, tap // 3 : tap // 3 + side].reshape(side * side, channels)
+            total += jnp.dot(
+                left,
+                weight[tap * channels : (tap + 1) * channels, :],
+                preferred_element_type=jnp.float32,
+            )
+        ref[0] = total.astype(jnp.bfloat16).reshape(side, side, weight.shape[1])
+
+
+def convolve(order, images, parts):
+    n_images, (_, side, _, channels) = len(images), images[0].shape
+    depth, block = parts[0].shape
+    whole = pl.BlockSpec(memory_space=pltpu.VMEM)
+    return pl.pallas_call(
+        lambda *refs: conv_kernel((n_images, len(parts)), *refs),
+        out_shape=[jax.ShapeDtypeStruct((1, side, side, block), jnp.bfloat16)] * n_images,
+        in_specs=[pl.BlockSpec(memory_space=pltpu.SMEM)] + [whole] * (n_images + len(parts)),
+        out_specs=[whole] * n_images,
+        scratch_shapes=[
+            pltpu.VMEM((3, n_images, side + 2, side, channels), jnp.bfloat16),
+            pltpu.VMEM((9 * channels, block), jnp.bfloat16),
+        ],
+        compiler_params=pltpu.CompilerParams(vmem_limit_bytes=24 * 1024 * 1024),
+        cost_estimate=pl.CostEstimate(
+            flops=36 * n_images * side * side * channels * block,
+            bytes_accessed=2 * (9 * channels * block + n_images * side * side * channels),
+            transcendentals=0,
+        ),
+    )(order, *images, *parts)
+
+
+def side_by_side_kernel(order_ref, *refs):
+    block = refs[0].shape[3]
+    for at, ref in enumerate(refs[:-1]):
+        refs[-1][:, :, :, pl.ds(pl.multiple_of(order_ref[at] * block, LANES), block)] = ref[...]
+
+
+def side_by_side(order, blocks):
+    whole = pl.BlockSpec(memory_space=pltpu.VMEM)
+    shape = blocks[0].shape[:3] + (len(blocks) * blocks[0].shape[3],)
+    return pl.pallas_call(
+        side_by_side_kernel,
+        out_shape=jax.ShapeDtypeStruct(shape, blocks[0].dtype),
+        in_specs=[pl.BlockSpec(memory_space=pltpu.SMEM)] + [whole] * len(blocks),
+        out_specs=whole,
+    )(order, *blocks)
 
 
 def gather_plan(n_layer, n_pair):
@@ -264,7 +332,15 @@
     maps = {("layer", 0, 0): activations}
     plan = gather_plan(n_layer, n_pair)
     events, due = [[]], []
+    strips_by_pair = []
     for at, now in enumerate(plan):
+        if at == 1:
+            strips = after(own_cot, events[1]).T.reshape(n_fsdp, strip, own_cot.shape[0])
+            strips_by_pair.append(lax.all_to_all(strips, "fsdp", split_axis=0, concat_axis=0))
+        if at == 3:
+            strips = after(strips_by_pair[0], events[3])
+            strips_by_pair += [over_pair(strips, step) for step in range(1, n_pair)]
+            due += [(4, strips) for strips in strips_by_pair]
         sources = [activations if source is None else maps[source] for _, source, _, _ in now]
         sources = after(sources, events[at])
         for array, (item, _, how, hops) in zip(sources, now):
@@ -273,12 +349,6 @@
         events.append([array for when, array in due if when == at + 1])
     last = len(plan) - 1
 
-    strips = after(own_cot, events[1]).T.reshape(n_fsdp, strip, own_cot.shape[0])
-    strips = lax.all_to_all(strips, "fsdp", split_axis=0, concat_axis=0)
-    strips_by_pair = [strips] + [
-        over_pair(after(strips, events[3]), step) for step in range(1, n_pair)
-    ]
-
     aligned = rows % LANES == 0 and channels % LANES == 0 and activations.shape[0] == 1
     arrived = {("layer", 0, 0): 0}
     for at, now in enumerate(plan):
@@ -288,7 +358,7 @@
         key=lambda item: max(when for other, when in arrived.items() if other[1] == item[1])
     )
     half = len(images) // 2
-    totals = None
+    totals, early = None, []
     for batch in (images[:half], images[half:]):
         owners, pairs = [], []
         for kind, layer, pair in batch:
@@ -300,6 +370,7 @@
             totals = add_products(
                 place, [maps[item] for item in batch], pairs, strips_by_pair, totals, cols, rows
             )
+            early = early or [totals[3]]
             continue
         for at in range(0, len(batch), 2 * n_pair):
             part = jnp.concatenate([maps[item] for item in batch[at : at + 2 * n_pair]], axis=0)
@@ -318,12 +389,36 @@
                 more.append(jnp.dot(cot_tile, row_tile, preferred_element_type=jnp.float32))
             totals = more if totals is None else [old + new for old, new in zip(totals, more)]
 
-    grad_own = totals[3] + over_core(totals[1])
-    cov_own = totals[2] + over_core(totals[0])
+    g_partial = by_rows(after(own_cot, events[2]), own_cot).reshape(n_pair, 2, block, channels)
+    g_pairs = lax.dynamic_index_in_dim(g_partial, core_at, 1, keepdims=False) + over_core(
+        lax.dynamic_index_in_dim(g_partial, 1 - core_at, 1, keepdims=False)
+    )
+    g_pairs = after(g_pairs, events[last])
+    g_sum = lax.dynamic_index_in_dim(g_pairs, pair_at, 0, keepdims=False)
+    for step in range(1, n_pair):
+        away = lax.dynamic_index_in_dim(g_pairs, (pair_at + step) % n_pair, 0, keepdims=False)
+        g_sum = g_sum + over_pair(away, step)
+    weight_part = after(weight, events[1])
+    near_parts = [lax.dynamic_slice_in_dim(weight_part, factor_at * block, block, 1)]
+    g_steps, distance, at = [g_sum], 2, 2
+    while distance < n_fsdp:
+        both = after(jnp.stack(near_parts), events[min(at, last)])
+        both = moved(both, "fsdp", lambda to, d=distance: to ^ d)
+        near_parts = near_parts + [both[k] for k in range(len(near_parts))]
+        g_sum = after(g_sum, events[last] if distance == 2 else events[last + 1] + early)
+        g_sum = g_sum + moved(g_sum, "fsdp", lambda to, d=distance: to ^ d)
+        g_steps.append(g_sum)
+        distance, at = 2 * distance, at + 2
+    far_parts = over_side(after(jnp.stack(near_parts), events[last + 1] + early))
+    parts = [
+        part for k in range(len(near_parts)) for part in (near_parts[k], far_parts[k])
+    ]
+
+    theirs = after(totals[1], [far_parts, g_steps[-1]])
+    grad_own = totals[3] + over_core(theirs)
     pixel_total = float(
         activations.shape[0] * activations.shape[1] * activations.shape[2] * n_fsdp * n_factor
     )
-    a_factor = 0.5 * a_factor_old + (0.5 / pixel_total) * cov_own.T
 
     exponent = jnp.floor(jnp.log2(jnp.maximum(jnp.max(jnp.abs(grad_own)), 1e-30))) - 14.0
     packed = (grad_own * jnp.exp2(-exponent)).astype(jnp.float16)
@@ -335,6 +430,8 @@
         array[:, :rows].astype(jnp.float32) * jnp.exp2(array[:, rows : rows + 1].astype(jnp.float32))
         for array in near_packed + far_packed
     ]
+    cov_own = totals[2] + over_core(after(totals[0], near_packed[1:2]))
+    a_factor = 0.5 * a_factor_old + (0.5 / pixel_total) * cov_own.T
     came_from = [(fsdp_at - 2 * step) % n_fsdp for step in range(n_layer)]
     came_from = came_from + [at ^ 1 for at in came_from]
     order = [
@@ -342,9 +439,30 @@
         for other in (1, 0)
         for step in range(n_pair)
     ]
+    near_images = [activations] + [maps["pair", 0, step] for step in range(1, n_pair)]
+    other_images = after(near_images, events[last] + [near_parts[0]])
+    group = near_images + [over_core(image) for image in other_images]
+    part_order = [fsdp_at ^ at for at in range(n_fsdp)]
+    if aligned and block % LANES == 0:
+        group_out = convolve(jnp.stack(part_order), group, parts)
+    else:
+        kernel = jnp.stack(parts)
+        kernel = jnp.concatenate(
+            [lax.dynamic_index_in_dim(kernel, at, 0, keepdims=False) for at in part_order]
+        ).reshape(3, 3, channels, block)
+        group_out = lax.conv_general_dilated(
+            jnp.concatenate(group),
+            kernel,
+            (1, 1),
+            "SAME",
+            dimension_numbers=("NHWC", "HWIO", "NHWC"),
+            preferred_element_type=jnp.float32,
+        ).astype(jnp.bfloat16)
+        group_out = jnp.split(group_out, n_factor)
+
     if aligned and block % LANES == 0:
         away, kept = tail_products(
-            jnp.stack(came_from + order), a_inverse, g_inverse, strips_of_grad, block
+            jnp.stack(came_from + order), after(a_inverse, group_out), g_inverse, strips_of_grad, block
         )
     else:
         inverse = jnp.concatenate(
@@ -367,75 +485,31 @@
     by_pair = kept + over_core(away)
     result = by_pair[:, :block]
     for step in range(1, n_pair):
-        result = result + over_pair(by_pair[:, step * block : (step + 1) * block], step)
+        back = over_pair(by_pair[:, step * block : (step + 1) * block], step)
+        result = result + after(back, a_factor)
     natural_grad = result.astype(jnp.bfloat16)
 
-    weight_part = lax.dynamic_slice_in_dim(
-        after(weight, events[last - 1]), factor_at * block, block, 1
-    )
-    near_parts = [weight_part] + [over_layer(weight_part, step) for step in range(1, n_layer)]
-    near_parts = after(jnp.stack(near_parts), events[last + 1])
-    parts = jnp.stack([near_parts, over_side(near_parts)])
-    kernel = jnp.concatenate(
-        [
-            lax.dynamic_slice(
-                parts,
-                ((fsdp_at + at) % 2, (fsdp_at // 2 - at // 2) % n_layer, 0, 0),
-                (1, 1) + weight_part.shape,
-            )[0, 0]
-            for at in range(n_fsdp)
-        ]
-    ).reshape(3, 3, channels, block)
-    near_images = [activations] + [maps["pair", 0, step] for step in range(1, n_pair)]
-    near_images = after(jnp.concatenate(near_images, axis=0), events[last - 1])
-    outputs = lax.conv_general_dilated(
-        jnp.concatenate([near_images, over_core(near_images)], axis=0),
-        kernel,
-        (1, 1),
-        "SAME",
-        dimension_numbers=("NHWC", "HWIO", "NHWC"),
-        preferred_element_type=jnp.float32,
-    ).astype(jnp.bfloat16)
-    outputs = outputs.reshape((2, n_pair) + activations.shape[:3] + (block,))
-    own_maps = []
-    for pair in range(n_pair):
-        for other in range(2):
-            own_maps.append(
-                outputs[other, pair]
-                if pair + other == 0
-                else moved(
-                    outputs[other, pair], "factor", lambda at, o=other, p=pair: (at ^ o) - 2 * p
-                )
-            )
-    own_maps = jnp.stack(own_maps)
-    conv_out = jnp.concatenate(
-        [
-            lax.dynamic_index_in_dim(
-                own_maps,
-                2 * ((at // 2 - pair_at) % n_pair) + (at + core_at) % 2,
-                0,
-                keepdims=False,
-            )
-            for at in range(n_factor)
-        ],
-        axis=3,
-    )
-
-    late_cot = after(own_cot, events[2])
-    g_partial = by_rows(late_cot, late_cot).reshape(n_pair, 2, block, channels)
-    g_pairs = lax.dynamic_index_in_dim(g_partial, core_at, 1, keepdims=False) + over_core(
-        lax.dynamic_index_in_dim(g_partial, 1 - core_at, 1, keepdims=False)
-    )
-    g_pairs = after(g_pairs, events[last + 1])
-    g_sum = lax.dynamic_index_in_dim(g_pairs, pair_at, 0, keepdims=False)
-    for step in range(1, n_pair):
-        away = lax.dynamic_index_in_dim(g_pairs, (pair_at + step) % n_pair, 0, keepdims=False)
-        g_sum = g_sum + over_pair(away, step)
-    distance = 1
-    while distance < n_fsdp:
-        g_sum = g_sum + moved(g_sum, "fsdp", lambda at, d=distance: at ^ d)
-        distance *= 2
-    g_factor = 0.5 * g_factor_old + 0.5 * g_sum
+
+    own_maps, block_order = [], []
+    for other in range(2):
+        for pair in range(n_pair):
+            out = group_out[other * n_pair + pair]
+            if pair + other:
+                out = moved(out, "factor", lambda at, o=other, p=pair: (at ^ o) - 2 * p)
+            own_maps.append(out)
+            block_order.append(2 * ((pair_at + pair) % n_pair) + (core_at + other) % 2)
+    own_maps = after(own_maps, by_pair)
+    if aligned and block % LANES == 0:
+        conv_out = side_by_side(jnp.stack(block_order), own_maps)
+    else:
+        stacked = jnp.zeros((n_factor,) + own_maps[0].shape, jnp.bfloat16)
+        for at, out in zip(block_order, own_maps):
+            stacked = lax.dynamic_update_index_in_dim(stacked, out, at, 0)
+        conv_out = jnp.concatenate(jnp.split(stacked, n_factor), axis=4)[0]
+
+    g_back = over_side(after(g_steps[-1], strips_of_grad[1:2]))
+    g_factor_sum = g_steps[-1] + after(g_back, by_pair)
+    g_factor = 0.5 * g_factor_old + 0.5 * g_factor_sum
     return (conv_out, a_factor, g_factor, natural_grad)
 
 

time: 178 us -> 169 us (0.949)
  waiting for transfers between devices: 58.6 us -> 41.2 us
  local copies, waits for them, and re-layouts: 7.76 us -> 24.3 us
  Pallas kernels: 29.6 us -> 36.2 us
  other arithmetic: 24 us -> 18.3 us
  starting transfers between devices: 49.8 us -> 44.3 us
  matrix products: 5.65 us -> 1.24 us
    ppermute x40, waiting for transfers between devices: 56.8 us -> 41.2 us  [moved(): lax.ppermute(array, axis, [(at, target(at) % count) for at in range(count)])]
    unnamed x57 -> x88, local copies, waits for them, and re-layouts: 4.29 us -> 15.5 us
    unnamed x7 -> x0, other arithmetic: 7.21 us -> none
    pallas_call x0 -> x2, Pallas kernels: none -> 5.77 us  [the longest x1 4.08 us: convolve(): pl.pallas_call(lambda *refs: conv_kernel((n_images, len(parts)), *refs),...]
    ppermute x40, starting transfers between devices: 46.3 us -> 40.9 us  [moved(): lax.ppermute(array, axis, [(at, target(at) % count) for at in range(count)])]
    conv_general_dilated x1 -> x0, matrix products: 5.34 us -> none  [per_device(): lax.conv_general_dilated(jnp.concatenate([near_images, over_core(near_ima...]
    concatenate x4 -> x0, other arithmetic: 3.74 us -> none  [the longest x1 1.13 us: per_device(): jnp.concatenate([near_images, over_core(near_images)], axis=0)]
    add x1, other arithmetic: 0.08 us -> 2.08 us  [per_device(): lax.dynamic_index_in_dim(g_partial, core_at, 1, keepdims=False)]
  transfers between devices with their start and end apart: 41 -> 41, of which waited for: 16 -> 18; matrix products, arithmetic and copies ran while one was open for 17% -> 16% of each run, Pallas kernels for 9% -> 22%
where the time goes in v5:
time: 169 us; the launch traced here: 168 us
  starting transfers between devices  44.3 us (26%)
  waiting for transfers between devices  41.2 us (24%)
  Pallas kernels  36.2 us (21%)
  local copies, waits for them, and re-layouts  24.3 us (14%)
  other arithmetic  18.3 us (11%)
  between operations  2.07 us (1%)
    ppermute x40, waiting for transfers between devices, moved(): lax.ppermute(array, axis, [(at, target(at) % count) for at in range(count)])  41.2 us
    ppermute x40, starting transfers between devices, moved(): lax.ppermute(array, axis, [(at, target(at) % count) for at in range(count)])  40.9 us
    pallas_call x2, Pallas kernels, add_products(): pl.pallas_call(lambda *refs: products_kernel(pairs, len(strips), before i...  26.3 us
    unnamed x88, local copies, waits for them, and re-layouts  15.5 us
    add x1, other arithmetic, per_device(): a_factor = 0.5 * a_factor_old + 0.5 / pixel_total * cov_own.T  4.5 us
    pallas_call x1, Pallas kernels, tail_products(): pl.pallas_call(lambda *refs: tail_kernel(strip, block, *refs), out_shape=...  4.09 us
    pallas_call x1, Pallas kernels, convolve(): pl.pallas_call(lambda *refs: conv_kernel((n_images, len(parts)), *refs),...  4.08 us
    all_to_all x1, starting transfers between devices, per_device(): lax.all_to_all(strips, 'fsdp', split_axis=0, concat_axis=0)  3.41 us
  transfers between devices with their start and end apart: 41, of which 18 were waited for; matrix products, arithmetic and copies ran while one was open for 16% of the time, Pallas kernels for 22%

profile of v5, /device:TPU:0, one launch (start us, length us, event | category | flops | bytes accessed | tf_op | source)
XLA Modules:
  0.0 167.6 jit_solution(18106785607167094354)
XLA Ops:
  0.6 3.0 %collective-permute-start = (bf16[1,16,16,512]{3,2,1,0:T(8,128)(2,1)}, bf16[1,16,16,512]{3,2,1,0:T(8,128)(2,1)}, u32[]{:S(2)}, u32[]{:S(2)}) collective-permute-start(bf16[1,16,16,512]{3,2,1,0:T(8,128)(2,1)} %refs_1_.3), channel_id=1, source_target_pairs={{0,2},{1,3},{2,0},{3,1},{4,6},{5,7},{6,4},{7,5},{8,10},{9,11},{10,... | collective-permute-start | bytes 786440 | tf_op jit(solution)/shard_map/ppermute | solution.py:19
  3.7 1.6 collective-permute-start.1
  5.3 1.5 collective-permute-start.2
  6.7 3.6 %collective-permute-done.refs_4_.refs_2_ = bf16[1,16,16,512]{3,2,1,0:T(8,128)(2,1)} collective-permute-done((bf16[1,16,16,512]{3,2,1,0:T(8,128)(2,1)}, bf16[1,16,16,512]{3,2,1,0:T(8,128)(2,1)}, u32[]{:S(2)}, u32[]{:S(2)}) %collective-permute-start) | collective-permute-done | bytes 262176 | tf_op jit(solution)/shard_map/ppermute | solution.py:19
  10.3 3.2 %collective-permute-done.1.refs_2_ = bf16[1,16,16,512]{3,2,1,0:T(8,128)(2,1)S(1)} collective-permute-done((bf16[1,16,16,512]{3,2,1,0:T(8,128)(2,1)}, bf16[1,16,16,512]{3,2,1,0:T(8,128)(2,1)S(1)}, u32[]{:S(2)}, u32[]{:S(2)}) %collective-permute-start.1) | collective-permute-done | bytes 262176 | tf_op jit(solution)/shard_map/ppermute | solution.py:19
  13.6 1.8 %collective-permute-start.3 = (bf16[1,16,16,512]{3,2,1,0:T(8,128)(2,1)}, bf16[1,16,16,512]{3,2,1,0:T(8,128)(2,1)S(1)}, u32[]{:S(2)}, u32[]{:S(2)}) collective-permute-start(bf16[1,16,16,512]{3,2,1,0:T(8,128)(2,1)} %refs_1_.3), channel_id=1, source_target_pairs={{0,24},{4,28},{8,0},{12,4},{16,8},{20,12},{24,16},{28,20},{1,25},{... | collective-permute-start | bytes 786440 | tf_op jit(solution)/shard_map/ppermute | solution.py:19
  15.3 1.5 collective-permute-start.4
  17.3 1.8 %copy.17 = bf16[512,256]{1,0:T(8,128)(2,1)} copy(bf16[512,256]{0,1:T(8,128)(2,1)} %bitcast.59) | data formatting | bytes 524288 | tf_op jit(solution)/shard_map/transpose | solution.py:338
  19.1 3.4 %all-to-all-start = ((bf16[8,64,256]{2,1,0:T(8,128)(2,1)}), bf16[8,64,256]{2,1,0:T(8,128)(2,1)S(1)}, u32[]{:S(2)}, u32[]{:S(2)}) async-start(bf16[8,64,256]{2,1,0:T(8,128)(2,1)} %bitcast.14), calls=%async_computation | async-start | bytes 524288 | tf_op jit(solution)/shard_map/all_to_all | solution.py:339
  23.2 1.3 collective-permute-start.7
  24.6 1.5 collective-permute-start.8
  26.1 1.1 copy.18
  27.2 1.2 fusion.1
  28.4 0.9 dynamic-slice_bitcast_fusion
  29.5 2.4 %collective-permute-start.6 = (bf16[1,16,16,512]{3,2,1,0:T(8,128)(2,1)}, bf16[1,16,16,512]{3,2,1,0:T(8,128)(2,1)S(1)}, u32[]{:S(2)}, u32[]{:S(2)}) collective-permute-start(bf16[1,16,16,512]{3,2,1,0:T(8,128)(2,1)} %refs_1_.3), channel_id=1, source_target_pairs={{0,16},{4,20},{8,24},{12,28},{16,0},{20,4},{24,8},{28,12},{1,17},{... | collective-permute-start | bytes 786440 | tf_op jit(solution)/shard_map/ppermute | solution.py:19
  32.0 1.2 collective-permute-start.9
  33.2 1.1 collective-permute-start.10
  34.9 9.9 %collective-permute-done.6.refs_4_ = bf16[1,16,16,512]{3,2,1,0:T(8,128)(2,1)S(1)} collective-permute-done((bf16[1,16,16,512]{3,2,1,0:T(8,128)(2,1)}, bf16[1,16,16,512]{3,2,1,0:T(8,128)(2,1)S(1)}, u32[]{:S(2)}, u32[]{:S(2)}) %collective-permute-start.6) | collective-permute-done | bytes 262176 | tf_op jit(solution)/shard_map/ppermute | solution.py:19
  44.8 1.1 collective-permute-done.11.refs_8_
  48.4 1.5 collective-permute-start.16
  49.8 2.1 %bitcast_add_fusion.1 = f32[2,128,512]{2,1,0:T(8,128)} fusion(f32[2,128,512]{2,1,0:T(8,128)} %collective-permute-done.24, f32[2,2,128,512]{3,2,1,0:T(8,128)} %copy-done.36, s32[]{:T(128)S(6)} %select_n.129), kind=kLoop, calls=%fused_computation.2 | loop fusion | flops 131072 | bytes 1572868 | tf_op jit(solution)/shard_map/add | solution.py:393
  51.9 2.1 %collective-permute-done.12.refs_5_ = bf16[1,16,16,512]{3,2,1,0:T(8,128)(2,1)S(1)} collective-permute-done((bf16[1,16,16,512]{3,2,1,0:T(8,128)(2,1)S(1)}, bf16[1,16,16,512]{3,2,1,0:T(8,128)(2,1)S(1)}, u32[]{:S(2)}, u32[]{:S(2)}) %collective-permute-start.12) | collective-permute-done | bytes 262176 | tf_op jit(solution)/shard_map/ppermute | solution.py:19
  54.7 1.0 dynamic-slice_bitcast_fusion.1
  56.3 0.9 pad_maximum_fusion.1
  58.1 1.3 collective-permute-start.18
  59.4 1.0 collective-permute-start.19
  60.4 3.6 %collective-permute-done.25 = f32[128,512]{1,0:T(8,128)S(1)} collective-permute-done((f32[128,512]{1,0:T(8,128)S(1)}, f32[128,512]{1,0:T(8,128)S(1)}, u32[]{:S(2)}, u32[]{:S(2)}) %collective-permute-start.25) | collective-permute-done | bytes 262176 | tf_op jit(solution)/shard_map/ppermute | solution.py:19
  64.0 1.0 bitcast_add_fusion.2
  65.3 0.9 copy-done.2
  66.2 0.9 copy-done.16
  67.2 0.9 copy-done.18
  68.1 0.9 copy-done.20
  69.1 0.9 copy-done.22
  70.0 0.9 copy-done.28
  71.0 0.9 copy-done.31
  71.9 0.9 copy-done.33
  72.9 12.9 %shard_map.102 = (f32[576,1152]{1,0:T(8,128)}, f32[64,1152]{1,0:T(8,128)S(1)}, f32[576,1152]{1,0:T(8,128)S(1)}, f32[64,1152]{1,0:T(8,128)S(1)}) custom-call(s32[11]{0:T(128)S(1)} %stack.140.refs_0_, bf16[1,16,16,512]{3,2,1,0:T(8,128)(2,1)} %refs_1_.3, bf16[1,16,16,512]{3,2,1,0:T(8,128)(2,1)S(1)} %copy-done.16, bf16[1,16,16,512]{3,2,1,0:T(8,128)(2,1)S(1)} %copy-done.18, ...), custom_call_target="tpu_custom_call" | custom-call | flops 6039797760 | bytes 11796480 | tf_op jit(solution)/shard_map/pallas_call | solution.py:137
  85.8 1.0 pad_maximum_fusion
  86.8 1.4 collective-permute-start.20
  89.4 4.5 %collective-permute-start.27 = (f32[128,512]{1,0:T(8,128)S(1)}, f32[128,512]{1,0:T(8,128)S(1)}, u32[]{:S(2)}, u32[]{:S(2)}) collective-permute-start(f32[128,512]{1,0:T(8,128)S(1)} %add.167), channel_id=1, source_target_pairs={{0,16},{4,20},{8,24},{12,28},{16,0},{20,4},{24,8},{28,12},{1,17},{... | collective-permute-start | bytes 786440 | tf_op jit(solution)/shard_map/ppermute | solution.py:19
  93.9 13.4 %shard_map.104 = (f32[576,1152]{1,0:T(8,128)}, f32[64,1152]{1,0:T(8,128)S(1)}, f32[576,1152]{1,0:T(8,128)S(1)}, f32[64,1152]{1,0:T(8,128)S(1)}) custom-call(s32[11]{0:T(128)S(1)} %stack.146.refs_0_, bf16[1,16,16,512]{3,2,1,0:T(8,128)(2,1)S(1)} %copy-done.14, ...), custom_call_target="tpu_custom_call", output_to_operand_aliasing={{0}: (11, {}), {1}: (12, {}), {2}: (13, {}), {3}: (14, {})} | custom-call | flops 6039797760 | bytes 11796480 | tf_op jit(solution)/shard_map/pallas_call | solution.py:137
  109.7 1.4 abs_reduce_fusion
  111.9 1.0 convert_multiply_fusion.7
  113.0 1.3 collective-permute-start.30
  116.1 0.9 copy-done.6
  117.0 0.9 copy-done.7
  117.9 0.9 copy-done.8
  119.8 4.1 %shard_map.103 = (bf16[1,16,16,128]{3,2,1,0:T(8,128)(2,1)S(1)}, bf16[1,16,16,128]{3,2,1,0:T(8,128)(2,1)S(1)}, bf16[1,16,16,128]{3,2,1,0:T(8,128)(2,1)S(1)}, bf16[1,16,16,128]{3,2,1,0:T(8,128)(2,1)S(1)}) custom-call(s32[8]{0:T(128)S(1)} %stack.130.refs_0_, bf16[1,16,16,512]{3,2,1,0:T(8,128)(2,1)} %refs_1_.3, ...), custom_call_target="tpu_custom_call" | custom-call | flops 2415919104 | bytes 2228224 | tf_op jit(solution)/shard_map/pallas_call | solution.py:231
  123.9 2.6 %collective-permute-start.31 = (f16[64,1280]{1,0:T(8,128)(2,1)S(1)}, f16[64,1280]{1,0:T(8,128)(2,1)S(1)}, u32[]{:S(2)}, u32[]{:S(2)}) collective-permute-start(f16[64,1280]{1,0:T(8,128)(2,1)S(1)} %concatenate.3), channel_id=1, source_target_pairs={{0,24},{4,28},{8,0},{12,4},{16,8},{20,12},{24,16},{28,20},{1,25},{... | collective-permute-start | bytes 491528 | tf_op jit(solution)/shard_map/ppermute | solution.py:19
  127.5 1.2 collective-permute-start.33
  129.7 1.6 collective-permute-done.31
  131.4 0.9 collective-permute-start.35
  132.6 0.9 collective-permute-done.32
  133.8 3.3 %collective-permute-done.33 = f16[64,1280]{1,0:T(8,128)(2,1)S(1)} collective-permute-done((f16[64,1280]{1,0:T(8,128)(2,1)S(1)}, f16[64,1280]{1,0:T(8,128)(2,1)S(1)}, u32[]{:S(2)}, u32[]{:S(2)}) %collective-permute-start.33) | collective-permute-done | bytes 163872 | tf_op jit(solution)/shard_map/ppermute | solution.py:19
  137.2 3.4 %collective-permute-done.34 = f16[64,1280]{1,0:T(8,128)(2,1)S(1)} collective-permute-done((f16[64,1280]{1,0:T(8,128)(2,1)S(1)}, f16[64,1280]{1,0:T(8,128)(2,1)S(1)}, u32[]{:S(2)}, u32[]{:S(2)}) %collective-permute-start.34) | collective-permute-done | bytes 163872 | tf_op jit(solution)/shard_map/ppermute | solution.py:19
  140.7 2.3 %collective-permute-done.35 = f16[64,1280]{1,0:T(8,128)(2,1)S(1)} collective-permute-done((f16[64,1280]{1,0:T(8,128)(2,1)S(1)}, f16[64,1280]{1,0:T(8,128)(2,1)S(1)}, u32[]{:S(2)}, u32[]{:S(2)}) %collective-permute-start.35) | collective-permute-done | bytes 163872 | tf_op jit(solution)/shard_map/ppermute | solution.py:19
  143.4 4.1 %shard_map.105 = (f32[576,256]{1,0:T(8,128)S(1)}, f32[576,256]{1,0:T(8,128)S(1)}) custom-call(s32[12]{0:T(128)S(1)} %stack.145.refs_0_, f32[576,1152]{1,0:T(8,128)S(1)} %copy-done.11, f32[512,512]{1,0:T(8,128)S(1)} %copy-done.12, f32[64,1152]{1,0:T(8,128)S(1)} %get-tuple-element.106.refs_3_, f32[64,1152]{1,0:T(8,128)S(1)} %convert_multiply_fusion.6.refs_4_, ...), custom_call_target="tpu_custom_call" | custom-call | flops 2944401408 | bytes 3833856 | tf_op jit(solution)/shard_map/pallas_call | solution.py:186
  147.6 0.9 collective-permute-start.38
  149.6 1.1 collective-permute-start.23
  153.9 2.4 %collective-permute-done.38 = f32[128,512]{1,0:T(8,128)S(1)} collective-permute-done((f32[128,512]{1,0:T(8,128)S(1)}, f32[128,512]{1,0:T(8,128)S(1)}, u32[]{:S(2)}, u32[]{:S(2)}) %collective-permute-start.38) | collective-permute-done | bytes 262176 | tf_op jit(solution)/shard_map/ppermute | solution.py:19
  157.1 1.7 %shard_map.106 = bf16[1,16,16,512]{3,2,1,0:T(8,128)(2,1)} custom-call(s32[4]{0:T(128)} %pad_add_fusion.order_ref, bf16[1,16,16,128]{3,2,1,0:T(8,128)(2,1)} %copy-done.10, bf16[1,16,16,128]{3,2,1,0:T(8,128)(2,1)} %copy-done.41, bf16[1,16,16,128]{3,2,1,0:T(8,128)(2,1)} %copy-done.42, bf16[1,16,16,128]{3,2,1,0:T(8,128)(2,1)} %copy-done.43), custom_call_target="tpu_custom_call" | custom-call | tf_op jit(solution)/shard_map/pallas_call | solution.py:258
  158.8 1.8 %add_multiply_fusion = f32[128,512]{1,0:T(8,128)} fusion(f32[128,512]{1,0:T(8,128)} %param.11, f32[128,512]{1,0:T(8,128)S(1)} %copy-done.39, f32[128,512]{1,0:T(8,128)} %copy-done.40), kind=kLoop, calls=%fused_computation.18 | loop fusion | flops 196608 | bytes 1048576 | tf_op jit(solution)/shard_map/add | solution.py:512
  160.6 4.5 %bitcast_add_fusion = f32[1152,576]{0,1:T(8,128)} fusion(f32[576,1152]{1,0:T(8,128)S(1)} %get-tuple-element.100, f32[576,1152]{1,0:T(8,128)} %collective-permute-done.37, f32[1152,576]{0,1:T(8,128)} %param.10), kind=kLoop, calls=%fused_computation | loop fusion | flops 2654208 | bytes 10616832 | tf_op jit(solution)/shard_map/add | solution.py:434
  165.9 1.7 fusion
  (153 shorter events, 22.3 us)
Async XLA Ops:
  0.6 47.0 %copy-start = (bf16[576,512]{1,0:T(8,128)(2,1)S(1)}, bf16[576,512]{1,0:T(8,128)(2,1)}, u32[]{:S(2)}) copy-start(bf16[576,512]{1,0:T(8,128)(2,1)} %param.9) | copy-start | bytes 1769476
  0.6 9.7 %collective-permute-start = (bf16[1,16,16,512]{3,2,1,0:T(8,128)(2,1)}, bf16[1,16,16,512]{3,2,1,0:T(8,128)(2,1)}, u32[]{:S(2)}, u32[]{:S(2)}) collective-permute-start(bf16[1,16,16,512]{3,2,1,0:T(8,128)(2,1)} %refs_1_.3), channel_id=1, source_target_pairs={{0,2},{1,3},{2,0},{3,1},{4,6},{5,7},{6,4},{7,5},{8,10},{9,11},{10,... | collective-permute-start | bytes 786440 | tf_op jit(solution)/shard_map/ppermute | solution.py:19
  3.7 9.9 %collective-permute-start.1 = (bf16[1,16,16,512]{3,2,1,0:T(8,128)(2,1)}, bf16[1,16,16,512]{3,2,1,0:T(8,128)(2,1)S(1)}, u32[]{:S(2)}, u32[]{:S(2)}) collective-permute-start(bf16[1,16,16,512]{3,2,1,0:T(8,128)(2,1)} %refs_1_.3), channel_id=1, source_target_pairs={{0,8},{4,12},{8,16},{12,20},{16,24},{20,28},{24,0},{28,4},{1,9},{5... | collective-permute-start | bytes 786440 | tf_op jit(solution)/shard_map/ppermute | solution.py:19
  5.3 8.3 %collective-permute-start.2 = (bf16[1,16,16,512]{3,2,1,0:T(8,128)(2,1)}, bf16[1,16,16,512]{3,2,1,0:T(8,128)(2,1)S(1)}, u32[]{:S(2)}, u32[]{:S(2)}) collective-permute-start(bf16[1,16,16,512]{3,2,1,0:T(8,128)(2,1)} %refs_1_.3), channel_id=1, source_target_pairs={{0,4},{4,0},{8,12},{12,8},{16,20},{20,16},{24,28},{28,24},{1,5},{5... | collective-permute-start | bytes 786440 | tf_op jit(solution)/shard_map/ppermute | solution.py:19
  13.5 38.4 %copy-start.15 = (bf16[1,16,16,512]{3,2,1,0:T(8,128)(2,1)}, bf16[1,16,16,512]{3,2,1,0:T(8,128)(2,1)S(1)}, u32[]{:S(2)}) copy-start(bf16[1,16,16,512]{3,2,1,0:T(8,128)(2,1)S(1)} %collective-permute-done.1.refs_2_) | copy-start | bytes 786436
  13.6 38.4 %copy-start.17 = (bf16[1,16,16,512]{3,2,1,0:T(8,128)(2,1)}, bf16[1,16,16,512]{3,2,1,0:T(8,128)(2,1)S(1)}, u32[]{:S(2)}) copy-start(bf16[1,16,16,512]{3,2,1,0:T(8,128)(2,1)S(1)} %collective-permute-done.2.refs_3_) | copy-start | bytes 786436
  13.6 9.0 %collective-permute-start.3 = (bf16[1,16,16,512]{3,2,1,0:T(8,128)(2,1)}, bf16[1,16,16,512]{3,2,1,0:T(8,128)(2,1)S(1)}, u32[]{:S(2)}, u32[]{:S(2)}) collective-permute-start(bf16[1,16,16,512]{3,2,1,0:T(8,128)(2,1)} %refs_1_.3), channel_id=1, source_target_pairs={{0,24},{4,28},{8,0},{12,4},{16,8},{20,12},{24,16},{28,20},{1,25},{... | collective-permute-start | bytes 786440 | tf_op jit(solution)/shard_map/ppermute | solution.py:19
  15.3 7.2 %collective-permute-start.4 = (bf16[1,16,16,512]{3,2,1,0:T(8,128)(2,1)S(1)}, bf16[1,16,16,512]{3,2,1,0:T(8,128)(2,1)S(1)}, u32[]{:S(2)}, u32[]{:S(2)}) collective-permute-start(bf16[1,16,16,512]{3,2,1,0:T(8,128)(2,1)S(1)} %collective-permute-done.1.refs_2_), channel_id=1, source_target_pairs={{0,4},{4,0},{8,12},{12,8},{16,20},{20,16},{24,28},{28,24},{1,5},{5... | collective-permute-start | bytes 786440 | tf_op jit(solution)/shard_map/ppermute | solution.py:19
  16.8 6.4 %collective-permute-start.5 = (bf16[1,16,16,512]{3,2,1,0:T(8,128)(2,1)S(1)}, bf16[1,16,16,512]{3,2,1,0:T(8,128)(2,1)S(1)}, u32[]{:S(2)}, u32[]{:S(2)}) collective-permute-start(bf16[1,16,16,512]{3,2,1,0:T(8,128)(2,1)S(1)} %collective-permute-done.1.refs_2_), channel_id=1, source_target_pairs={{0,2},{1,3},{2,0},{3,1},{4,6},{5,7},{6,4},{7,5},{8,10},{9,11},{10,... | collective-permute-start | bytes 786440 | tf_op jit(solution)/shard_map/ppermute | solution.py:19
  19.1 12.8 %all-to-all-start = ((bf16[8,64,256]{2,1,0:T(8,128)(2,1)}), bf16[8,64,256]{2,1,0:T(8,128)(2,1)S(1)}, u32[]{:S(2)}, u32[]{:S(2)}) async-start(bf16[8,64,256]{2,1,0:T(8,128)(2,1)} %bitcast.14), calls=%async_computation | async-start | bytes 524288 | tf_op jit(solution)/shard_map/all_to_all | solution.py:339
  22.5 33.1 %copy-start.13 = (bf16[1,16,16,512]{3,2,1,0:T(8,128)(2,1)}, bf16[1,16,16,512]{3,2,1,0:T(8,128)(2,1)S(1)}, u32[]{:S(2)}) copy-start(bf16[1,16,16,512]{3,2,1,0:T(8,128)(2,1)S(1)} %collective-permute-done.3.refs_1_) | copy-start | bytes 786436
  22.6 33.1 %copy-start.19 = (bf16[1,16,16,512]{3,2,1,0:T(8,128)(2,1)}, bf16[1,16,16,512]{3,2,1,0:T(8,128)(2,1)S(1)}, u32[]{:S(2)}) copy-start(bf16[1,16,16,512]{3,2,1,0:T(8,128)(2,1)S(1)} %collective-permute-done.4.refs_5_) | copy-start | bytes 786436
  23.2 32.5 %copy-start.21 = (bf16[1,16,16,512]{3,2,1,0:T(8,128)(2,1)}, bf16[1,16,16,512]{3,2,1,0:T(8,128)(2,1)S(1)}, u32[]{:S(2)}) copy-start(bf16[1,16,16,512]{3,2,1,0:T(8,128)(2,1)S(1)} %collective-permute-done.5.refs_6_) | copy-start | bytes 786436
  23.2 8.7 %collective-permute-start.7 = (bf16[1,16,16,512]{3,2,1,0:T(8,128)(2,1)S(1)}, bf16[1,16,16,512]{3,2,1,0:T(8,128)(2,1)}, u32[]{:S(2)}, u32[]{:S(2)}) collective-permute-start(bf16[1,16,16,512]{3,2,1,0:T(8,128)(2,1)S(1)} %collective-permute-done.3.refs_1_), channel_id=1, source_target_pairs={{0,4},{4,0},{8,12},{12,8},{16,20},{20,16},{24,28},{28,24},{1,5},{5... | collective-permute-start | bytes 786440 | tf_op jit(solution)/shard_map/ppermute | solution.py:19
  24.6 7.4 %collective-permute-start.8 = (bf16[1,16,16,512]{3,2,1,0:T(8,128)(2,1)S(1)}, bf16[1,16,16,512]{3,2,1,0:T(8,128)(2,1)S(1)}, u32[]{:S(2)}, u32[]{:S(2)}) collective-permute-start(bf16[1,16,16,512]{3,2,1,0:T(8,128)(2,1)S(1)} %collective-permute-done.3.refs_1_), channel_id=1, source_target_pairs={{0,2},{1,3},{2,0},{3,1},{4,6},{5,7},{6,4},{7,5},{8,10},{9,11},{10,... | collective-permute-start | bytes 786440 | tf_op jit(solution)/shard_map/ppermute | solution.py:19
  29.3 20.5 %collective-permute-start.24 = (f32[2,128,512]{2,1,0:T(8,128)}, f32[2,128,512]{2,1,0:T(8,128)}, u32[]{:S(2)}, u32[]{:S(2)}) collective-permute-start(f32[2,128,512]{2,1,0:T(8,128)} %dynamic-slice_bitcast_fusion), channel_id=1, source_target_pairs={{0,1},{1,0},{2,3},{3,2},{4,5},{5,4},{6,7},{7,6},{8,9},{9,8},{10,11... | collective-permute-start | bytes 1572872 | tf_op jit(solution)/shard_map/ppermute | solution.py:19
  29.5 15.2 %collective-permute-start.6 = (bf16[1,16,16,512]{3,2,1,0:T(8,128)(2,1)}, bf16[1,16,16,512]{3,2,1,0:T(8,128)(2,1)S(1)}, u32[]{:S(2)}, u32[]{:S(2)}) collective-permute-start(bf16[1,16,16,512]{3,2,1,0:T(8,128)(2,1)} %refs_1_.3), channel_id=1, source_target_pairs={{0,16},{4,20},{8,24},{12,28},{16,0},{20,4},{24,8},{28,12},{1,17},{... | collective-permute-start | bytes 786440 | tf_op jit(solution)/shard_map/ppermute | solution.py:19
  31.9 33.1 %copy-start.1 = (bf16[8,64,256]{2,1,0:T(8,128)(2,1)}, bf16[8,64,256]{2,1,0:T(8,128)(2,1)S(1)}, u32[]{:S(2)}) copy-start(bf16[8,64,256]{2,1,0:T(8,128)(2,1)S(1)} %all-to-all-done.refs_9_) | copy-start | bytes 786436
  32.0 33.1 %copy-start.23 = (bf16[1,16,16,512]{3,2,1,0:T(8,128)(2,1)}, bf16[1,16,16,512]{3,2,1,0:T(8,128)(2,1)S(1)}, u32[]{:S(2)}) copy-start(bf16[1,16,16,512]{3,2,1,0:T(8,128)(2,1)S(1)} %collective-permute-done.8.refs_3_) | copy-start | bytes 786436
  32.0 12.8 %collective-permute-start.9 = (bf16[8,64,256]{2,1,0:T(8,128)(2,1)S(1)}, bf16[8,64,256]{2,1,0:T(8,128)(2,1)S(1)}, u32[]{:S(2)}, u32[]{:S(2)}) collective-permute-start(bf16[8,64,256]{2,1,0:T(8,128)(2,1)S(1)} %all-to-all-done.refs_9_), channel_id=1, source_target_pairs={{0,2},{1,3},{2,0},{3,1},{4,6},{5,7},{6,4},{7,5},{8,10},{9,11},{10,... | collective-permute-start | bytes 786440 | tf_op jit(solution)/shard_map/ppermute | solution.py:19
  33.2 11.6 %collective-permute-start.10 = (bf16[1,16,16,512]{3,2,1,0:T(8,128)(2,1)S(1)}, bf16[1,16,16,512]{3,2,1,0:T(8,128)(2,1)S(1)}, u32[]{:S(2)}, u32[]{:S(2)}) collective-permute-start(bf16[1,16,16,512]{3,2,1,0:T(8,128)(2,1)S(1)} %collective-permute-done.5.refs_6_), channel_id=1, source_target_pairs={{0,4},{4,0},{8,12},{12,8},{16,20},{20,16},{24,28},{28,24},{1,5},{5... | collective-permute-start | bytes 786440 | tf_op jit(solution)/shard_map/ppermute | solution.py:19
  34.3 11.6 %collective-permute-start.11 = (bf16[1,16,16,512]{3,2,1,0:T(8,128)(2,1)S(1)}, bf16[1,16,16,512]{3,2,1,0:T(8,128)(2,1)S(1)}, u32[]{:S(2)}, u32[]{:S(2)}) collective-permute-start(bf16[1,16,16,512]{3,2,1,0:T(8,128)(2,1)S(1)} %collective-permute-done.2.refs_3_), channel_id=1, source_target_pairs={{0,2},{1,3},{2,0},{3,1},{4,6},{5,7},{6,4},{7,5},{8,10},{9,11},{10,... | collective-permute-start | bytes 786440 | tf_op jit(solution)/shard_map/ppermute | solution.py:19
  44.8 20.2 %copy-start.25 = (bf16[1,16,16,512]{3,2,1,0:T(8,128)(2,1)}, bf16[1,16,16,512]{3,2,1,0:T(8,128)(2,1)S(1)}, u32[]{:S(2)}) copy-start(bf16[1,16,16,512]{3,2,1,0:T(8,128)(2,1)S(1)} %collective-permute-done.6.refs_4_) | copy-start | bytes 786436
  44.8 20.2 %copy-start.27 = (bf16[8,64,256]{2,1,0:T(8,128)(2,1)}, bf16[8,64,256]{2,1,0:T(8,128)(2,1)S(1)}, u32[]{:S(2)}) copy-start(bf16[8,64,256]{2,1,0:T(8,128)(2,1)S(1)} %collective-permute-done.9.refs_10_) | copy-start | bytes 786436
  44.8 20.2 %copy-start.30 = (bf16[1,16,16,512]{3,2,1,0:T(8,128)(2,1)}, bf16[1,16,16,512]{3,2,1,0:T(8,128)(2,1)S(1)}, u32[]{:S(2)}) copy-start(bf16[1,16,16,512]{3,2,1,0:T(8,128)(2,1)S(1)} %collective-permute-done.10.refs_7_) | copy-start | bytes 786436
  46.6 7.4 %collective-permute-start.12 = (bf16[1,16,16,512]{3,2,1,0:T(8,128)(2,1)S(1)}, bf16[1,16,16,512]{3,2,1,0:T(8,128)(2,1)S(1)}, u32[]{:S(2)}, u32[]{:S(2)}) collective-permute-start(bf16[1,16,16,512]{3,2,1,0:T(8,128)(2,1)S(1)} %collective-permute-done.6.refs_4_), channel_id=1, source_target_pairs={{0,4},{4,0},{8,12},{12,8},{16,20},{20,16},{24,28},{28,24},{1,5},{5... | collective-permute-start | bytes 786440 | tf_op jit(solution)/shard_map/ppermute | solution.py:19
  47.2 7.5 %collective-permute-start.13 = (bf16[1,16,16,512]{3,2,1,0:T(8,128)(2,1)S(1)}, bf16[1,16,16,512]{3,2,1,0:T(8,128)(2,1)}, u32[]{:S(2)}, u32[]{:S(2)}) collective-permute-start(bf16[1,16,16,512]{3,2,1,0:T(8,128)(2,1)S(1)} %collective-permute-done.6.refs_4_), channel_id=1, source_target_pairs={{0,2},{1,3},{2,0},{3,1},{4,6},{5,7},{6,4},{7,5},{8,10},{9,11},{10,... | collective-permute-start | bytes 786440 | tf_op jit(solution)/shard_map/ppermute | solution.py:19
  48.4 7.9 %collective-permute-start.16 = (bf16[1,576,128]{2,1,0:T(8,128)(2,1)}, bf16[1,576,128]{2,1,0:T(8,128)(2,1)S(1)}, u32[]{:S(2)}, u32[]{:S(2)}) collective-permute-start(bf16[1,576,128]{2,1,0:T(8,128)(2,1)} %fusion.4), channel_id=1, source_target_pairs={{0,8},{4,12},{8,0},{12,4},{16,24},{20,28},{24,16},{28,20},{1,9},{5... | collective-permute-start | bytes 442376 | tf_op jit(solution)/shard_map/ppermute | solution.py:19
  55.7 8.3 %collective-permute-start.25 = (f32[128,512]{1,0:T(8,128)S(1)}, f32[128,512]{1,0:T(8,128)S(1)}, u32[]{:S(2)}, u32[]{:S(2)}) collective-permute-start(f32[128,512]{1,0:T(8,128)S(1)} %dynamic-slice_bitcast_fusion.1), channel_id=1, source_target_pairs={{0,2},{1,3},{2,0},{3,1},{4,6},{5,7},{6,4},{7,5},{8,10},{9,11},{10,... | collective-permute-start | bytes 786440 | tf_op jit(solution)/shard_map/ppermute | solution.py:19
  57.2 28.6 %collective-permute-start.17 = (bf16[2,576,128]{2,1,0:T(8,128)(2,1)S(1)}, bf16[2,576,128]{2,1,0:T(8,128)(2,1)S(1)}, u32[]{:S(2)}, u32[]{:S(2)}) collective-permute-start(bf16[2,576,128]{2,1,0:T(8,128)(2,1)S(1)} %pad_maximum_fusion.1), channel_id=1, source_target_pairs={{0,16},{4,20},{8,24},{12,28},{16,0},{20,4},{24,8},{28,12},{1,17},{... | collective-permute-start | bytes 884744 | tf_op jit(solution)/shard_map/ppermute | solution.py:19
  58.1 28.7 %collective-permute-start.18 = (bf16[1,16,16,512]{3,2,1,0:T(8,128)(2,1)}, bf16[1,16,16,512]{3,2,1,0:T(8,128)(2,1)S(1)}, u32[]{:S(2)}, u32[]{:S(2)}) collective-permute-start(bf16[1,16,16,512]{3,2,1,0:T(8,128)(2,1)} %collective-permute-done.13.refs_6_), channel_id=1, source_target_pairs={{0,4},{4,0},{8,12},{12,8},{16,20},{20,16},{24,28},{28,24},{1,5},{5... | collective-permute-start | bytes 786440 | tf_op jit(solution)/shard_map/ppermute | solution.py:19
  59.4 27.4 %collective-permute-start.19 = (bf16[1,16,16,512]{3,2,1,0:T(8,128)(2,1)}, bf16[1,16,16,512]{3,2,1,0:T(8,128)(2,1)S(1)}, u32[]{:S(2)}, u32[]{:S(2)}) collective-permute-start(bf16[1,16,16,512]{3,2,1,0:T(8,128)(2,1)} %collective-permute-done.7.refs_2_), channel_id=1, source_target_pairs={{0,2},{1,3},{2,0},{3,1},{4,6},{5,7},{6,4},{7,5},{8,10},{9,11},{10,... | collective-permute-start | bytes 786440 | tf_op jit(solution)/shard_map/ppermute | solution.py:19
  65.1 24.3 %collective-permute-start.26 = (f32[128,512]{1,0:T(8,128)S(1)}, f32[128,512]{1,0:T(8,128)S(1)}, u32[]{:S(2)}, u32[]{:S(2)}) collective-permute-start(f32[128,512]{1,0:T(8,128)S(1)} %bitcast_add_fusion.2), channel_id=1, source_target_pairs={{0,8},{4,12},{8,0},{12,4},{16,24},{20,28},{24,16},{28,20},{1,9},{5... | collective-permute-start | bytes 786440 | tf_op jit(solution)/shard_map/ppermute | solution.py:19
  72.9 21.0 %copy-start.3 = (bf16[8,64,256]{2,1,0:T(8,128)(2,1)S(1)}, bf16[8,64,256]{2,1,0:T(8,128)(2,1)}, u32[]{:S(2)}) copy-start(bf16[8,64,256]{2,1,0:T(8,128)(2,1)} %copy-done.1) | copy-start | bytes 786436
  72.9 21.0 %copy-start.14 = (bf16[1,16,16,512]{3,2,1,0:T(8,128)(2,1)S(1)}, bf16[1,16,16,512]{3,2,1,0:T(8,128)(2,1)}, u32[]{:S(2)}) copy-start(bf16[1,16,16,512]{3,2,1,0:T(8,128)(2,1)} %copy-done.13) | copy-start | bytes 786436
  72.9 21.0 %copy-start.24 = (bf16[1,16,16,512]{3,2,1,0:T(8,128)(2,1)S(1)}, bf16[1,16,16,512]{3,2,1,0:T(8,128)(2,1)}, u32[]{:S(2)}) copy-start(bf16[1,16,16,512]{3,2,1,0:T(8,128)(2,1)} %copy-done.23) | copy-start | bytes 786436
  72.9 21.0 %copy-start.26 = (bf16[1,16,16,512]{3,2,1,0:T(8,128)(2,1)S(1)}, bf16[1,16,16,512]{3,2,1,0:T(8,128)(2,1)}, u32[]{:S(2)}) copy-start(bf16[1,16,16,512]{3,2,1,0:T(8,128)(2,1)} %copy-done.25) | copy-start | bytes 786436
  72.9 21.0 %copy-start.29 = (bf16[8,64,256]{2,1,0:T(8,128)(2,1)S(1)}, bf16[8,64,256]{2,1,0:T(8,128)(2,1)}, u32[]{:S(2)}) copy-start(bf16[8,64,256]{2,1,0:T(8,128)(2,1)} %copy-done.27) | copy-start | bytes 786436
  72.9 21.0 %copy-start.35 = (bf16[1,16,16,512]{3,2,1,0:T(8,128)(2,1)S(1)}, bf16[1,16,16,512]{3,2,1,0:T(8,128)(2,1)}, u32[]{:S(2)}) copy-start(bf16[1,16,16,512]{3,2,1,0:T(8,128)(2,1)} %copy-done.34) | copy-start | bytes 786436
  86.8 21.3 %collective-permute-start.20 = (bf16[4,576,128]{2,1,0:T(8,128)(2,1)S(1)}, bf16[4,576,128]{2,1,0:T(8,128)(2,1)S(1)}, u32[]{:S(2)}, u32[]{:S(2)}) collective-permute-start(bf16[4,576,128]{2,1,0:T(8,128)(2,1)S(1)} %pad_maximum_fusion), channel_id=1, source_target_pairs={{0,4},{4,0},{8,12},{12,8},{16,20},{20,16},{24,28},{28,24},{1,5},{5... | collective-permute-start | bytes 1769480 | tf_op jit(solution)/shard_map/ppermute | solution.py:19
  88.9 25.4 %collective-permute-start.14 = (bf16[1,16,16,512]{3,2,1,0:T(8,128)(2,1)}, bf16[1,16,16,512]{3,2,1,0:T(8,128)(2,1)}, u32[]{:S(2)}, u32[]{:S(2)}) collective-permute-start(bf16[1,16,16,512]{3,2,1,0:T(8,128)(2,1)} %refs_1_.3), channel_id=1, source_target_pairs={{0,1},{1,0},{2,3},{3,2},{4,5},{5,4},{6,7},{7,6},{8,9},{9,8},{10,11... | collective-permute-start | bytes 786440 | tf_op jit(solution)/shard_map/ppermute | solution.py:19
  88.9 25.4 %collective-permute-start.15 = (bf16[1,16,16,512]{3,2,1,0:T(8,128)(2,1)}, bf16[1,16,16,512]{3,2,1,0:T(8,128)(2,1)}, u32[]{:S(2)}, u32[]{:S(2)}) collective-permute-start(bf16[1,16,16,512]{3,2,1,0:T(8,128)(2,1)} %collective-permute-done.refs_4_.refs_2_), channel_id=1, source_target_pairs={{0,1},{1,0},{2,3},{3,2},{4,5},{5,4},{6,7},{7,6},{8,9},{9,8},{10,11... | collective-permute-start | bytes 786440 | tf_op jit(solution)/shard_map/ppermute | solution.py:19
  89.4 17.9 %collective-permute-start.27 = (f32[128,512]{1,0:T(8,128)S(1)}, f32[128,512]{1,0:T(8,128)S(1)}, u32[]{:S(2)}, u32[]{:S(2)}) collective-permute-start(f32[128,512]{1,0:T(8,128)S(1)} %add.167), channel_id=1, source_target_pairs={{0,16},{4,20},{8,24},{12,28},{16,0},{20,4},{24,8},{28,12},{1,17},{... | collective-permute-start | bytes 786440 | tf_op jit(solution)/shard_map/ppermute | solution.py:19
  108.1 1.6 collective-permute-start.28
  112.9 14.4 %collective-permute-start.29 = (f16[64,1280]{1,0:T(8,128)(2,1)S(1)}, f16[64,1280]{1,0:T(8,128)(2,1)S(1)}, u32[]{:S(2)}, u32[]{:S(2)}) collective-permute-start(f16[64,1280]{1,0:T(8,128)(2,1)S(1)} %concatenate.3), channel_id=1, source_target_pairs={{0,8},{4,12},{8,16},{12,20},{16,24},{20,28},{24,0},{28,4},{1,9},{5... | collective-permute-start | bytes 491528 | tf_op jit(solution)/shard_map/ppermute | solution.py:19
  113.0 15.7 %collective-permute-start.30 = (f16[64,1280]{1,0:T(8,128)(2,1)S(1)}, f16[64,1280]{1,0:T(8,128)(2,1)S(1)}, u32[]{:S(2)}, u32[]{:S(2)}) collective-permute-start(f16[64,1280]{1,0:T(8,128)(2,1)S(1)} %concatenate.3), channel_id=1, source_target_pairs={{0,16},{4,20},{8,24},{12,28},{16,0},{20,4},{24,8},{28,12},{1,17},{... | collective-permute-start | bytes 491528 | tf_op jit(solution)/shard_map/ppermute | solution.py:19
  119.8 23.6 %copy-start.12 = (f32[512,512]{1,0:T(8,128)S(1)}, f32[512,512]{1,0:T(8,128)}, u32[]{:S(2)}) copy-start(f32[512,512]{1,0:T(8,128)} %refs_2_.1) | copy-start | bytes 3145732
  123.8 19.6 %copy-start.10 = (bf16[1,16,16,128]{3,2,1,0:T(8,128)(2,1)}, bf16[1,16,16,128]{3,2,1,0:T(8,128)(2,1)S(1)}, u32[]{:S(2)}) copy-start(bf16[1,16,16,128]{3,2,1,0:T(8,128)(2,1)S(1)} %get-tuple-element.96.refs_0_) | copy-start | bytes 196612
  123.9 19.6 %copy-start.11 = (f32[576,1152]{1,0:T(8,128)S(1)}, f32[576,1152]{1,0:T(8,128)}, u32[]{:S(2)}) copy-start(f32[576,1152]{1,0:T(8,128)} %refs_1_.4) | copy-start | bytes 7962628
  123.9 7.4 %collective-permute-start.31 = (f16[64,1280]{1,0:T(8,128)(2,1)S(1)}, f16[64,1280]{1,0:T(8,128)(2,1)S(1)}, u32[]{:S(2)}, u32[]{:S(2)}) collective-permute-start(f16[64,1280]{1,0:T(8,128)(2,1)S(1)} %concatenate.3), channel_id=1, source_target_pairs={{0,24},{4,28},{8,0},{12,4},{16,8},{20,12},{24,16},{28,20},{1,25},{... | collective-permute-start | bytes 491528 | tf_op jit(solution)/shard_map/ppermute | solution.py:19
  126.5 7.1 %collective-permute-start.32 = (f16[64,1280]{1,0:T(8,128)(2,1)S(1)}, f16[64,1280]{1,0:T(8,128)(2,1)S(1)}, u32[]{:S(2)}, u32[]{:S(2)}) collective-permute-start(f16[64,1280]{1,0:T(8,128)(2,1)S(1)} %concatenate.3), channel_id=1, source_target_pairs={{0,4},{4,0},{8,12},{12,8},{16,20},{20,16},{24,28},{28,24},{1,5},{5... | collective-permute-start | bytes 491528 | tf_op jit(solution)/shard_map/ppermute | solution.py:19
  127.3 33.2 %collective-permute-start.37 = (f32[576,1152]{1,0:T(8,128)}, f32[576,1152]{1,0:T(8,128)}, u32[]{:S(2)}, u32[]{:S(2)}) collective-permute-start(f32[576,1152]{1,0:T(8,128)} %get-tuple-element.102), channel_id=1, source_target_pairs={{0,1},{1,0},{2,3},{3,2},{4,5},{5,4},{6,7},{7,6},{8,9},{9,8},{10,11... | collective-permute-start | bytes 7962632 | tf_op jit(solution)/shard_map/ppermute | solution.py:19
  127.5 9.6 %collective-permute-start.33 = (f16[64,1280]{1,0:T(8,128)(2,1)S(1)}, f16[64,1280]{1,0:T(8,128)(2,1)S(1)}, u32[]{:S(2)}, u32[]{:S(2)}) collective-permute-start(f16[64,1280]{1,0:T(8,128)(2,1)S(1)} %collective-permute-done.29), channel_id=1, source_target_pairs={{0,4},{4,0},{8,12},{12,8},{16,20},{20,16},{24,28},{28,24},{1,5},{5... | collective-permute-start | bytes 491528 | tf_op jit(solution)/shard_map/ppermute | solution.py:19
  128.7 11.9 %collective-permute-start.34 = (f16[64,1280]{1,0:T(8,128)(2,1)S(1)}, f16[64,1280]{1,0:T(8,128)(2,1)S(1)}, u32[]{:S(2)}, u32[]{:S(2)}) collective-permute-start(f16[64,1280]{1,0:T(8,128)(2,1)S(1)} %collective-permute-done.30), channel_id=1, source_target_pairs={{0,4},{4,0},{8,12},{12,8},{16,20},{20,16},{24,28},{28,24},{1,5},{5... | collective-permute-start | bytes 491528 | tf_op jit(solution)/shard_map/ppermute | solution.py:19
  131.4 11.6 %collective-permute-start.35 = (f16[64,1280]{1,0:T(8,128)(2,1)S(1)}, f16[64,1280]{1,0:T(8,128)(2,1)S(1)}, u32[]{:S(2)}, u32[]{:S(2)}) collective-permute-start(f16[64,1280]{1,0:T(8,128)(2,1)S(1)} %collective-permute-done.31), channel_id=1, source_target_pairs={{0,4},{4,0},{8,12},{12,8},{16,20},{20,16},{24,28},{28,24},{1,5},{5... | collective-permute-start | bytes 491528 | tf_op jit(solution)/shard_map/ppermute | solution.py:19
  143.4 4.2 %copy-start.39 = (f32[128,512]{1,0:T(8,128)S(1)}, f32[128,512]{1,0:T(8,128)}, u32[]{:S(2)}) copy-start(f32[128,512]{1,0:T(8,128)} %add.168) | copy-start | bytes 786436
  147.5 2.1 %collective-permute-start.36 = (f32[576,256]{1,0:T(8,128)S(1)}, f32[576,256]{1,0:T(8,128)S(1)}, u32[]{:S(2)}, u32[]{:S(2)}) collective-permute-start(f32[576,256]{1,0:T(8,128)S(1)} %get-tuple-element.95), channel_id=1, source_target_pairs={{0,1},{1,0},{2,3},{3,2},{4,5},{5,4},{6,7},{7,6},{8,9},{9,8},{10,11... | collective-permute-start | bytes 1769480 | tf_op jit(solution)/shard_map/ppermute | solution.py:19
  147.6 8.7 %collective-permute-start.38 = (f32[128,512]{1,0:T(8,128)S(1)}, f32[128,512]{1,0:T(8,128)S(1)}, u32[]{:S(2)}, u32[]{:S(2)}) collective-permute-start(f32[128,512]{1,0:T(8,128)S(1)} %copy-done.39), channel_id=1, source_target_pairs={{0,4},{4,0},{8,12},{12,8},{16,20},{20,16},{24,28},{28,24},{1,5},{5... | collective-permute-start | bytes 786440 | tf_op jit(solution)/shard_map/ppermute | solution.py:19
  148.5 4.6 %collective-permute-start.21 = (bf16[1,16,16,128]{3,2,1,0:T(8,128)(2,1)S(1)}, bf16[1,16,16,128]{3,2,1,0:T(8,128)(2,1)S(1)}, u32[]{:S(2)}, u32[]{:S(2)}) collective-permute-start(bf16[1,16,16,128]{3,2,1,0:T(8,128)(2,1)S(1)} %get-tuple-element.80), channel_id=1, source_target_pairs={{0,2},{1,3},{2,0},{3,1},{4,6},{5,7},{6,4},{7,5},{8,10},{9,11},{10,... | collective-permute-start | bytes 196616 | tf_op jit(solution)/shard_map/ppermute | solution.py:19
  149.1 4.0 %collective-permute-start.22 = (bf16[1,16,16,128]{3,2,1,0:T(8,128)(2,1)S(1)}, bf16[1,16,16,128]{3,2,1,0:T(8,128)(2,1)S(1)}, u32[]{:S(2)}, u32[]{:S(2)}) collective-permute-start(bf16[1,16,16,128]{3,2,1,0:T(8,128)(2,1)S(1)} %get-tuple-element.81), channel_id=1, source_target_pairs={{0,1},{1,0},{2,3},{3,2},{4,5},{5,4},{6,7},{7,6},{8,9},{9,8},{10,11... | collective-permute-start | bytes 196616 | tf_op jit(solution)/shard_map/ppermute | solution.py:19
  149.6 4.3 %collective-permute-start.23 = (bf16[1,16,16,128]{3,2,1,0:T(8,128)(2,1)S(1)}, bf16[1,16,16,128]{3,2,1,0:T(8,128)(2,1)S(1)}, u32[]{:S(2)}, u32[]{:S(2)}) collective-permute-start(bf16[1,16,16,128]{3,2,1,0:T(8,128)(2,1)S(1)} %get-tuple-element.82), channel_id=1, source_target_pairs={{0,3},{1,2},{2,1},{3,0},{4,7},{5,6},{6,5},{7,4},{8,11},{9,10},{10,... | collective-permute-start | bytes 196616 | tf_op jit(solution)/shard_map/ppermute | solution.py:19
  153.1 3.2 %copy-start.41 = (bf16[1,16,16,128]{3,2,1,0:T(8,128)(2,1)}, bf16[1,16,16,128]{3,2,1,0:T(8,128)(2,1)S(1)}, u32[]{:S(2)}) copy-start(bf16[1,16,16,128]{3,2,1,0:T(8,128)(2,1)S(1)} %collective-permute-done.21.refs_1_) | copy-start | bytes 196612
  157.0 8.9 %collective-permute-start.39 = (f32[576,128]{1,0:T(8,128)}, f32[576,128]{1,0:T(8,128)}, u32[]{:S(2)}, u32[]{:S(2)}) collective-permute-start(f32[576,128]{1,0:T(8,128)} %slice.111), channel_id=1, source_target_pairs={{0,2},{1,3},{2,0},{3,1},{4,6},{5,7},{6,4},{7,5},{8,10},{9,11},{10,... | collective-permute-start | bytes 884744 | tf_op jit(solution)/shard_map/ppermute | solution.py:19
  160.6 5.4 %copy-start.38 = (f32[576,256]{1,0:T(8,128)S(1)}, f32[576,256]{1,0:T(8,128)}, u32[]{:S(2)}) copy-start(f32[576,256]{1,0:T(8,128)} %copy-done.37) | copy-start | bytes 1769476
  (21 other events, 24.4 us)

commit v6 on v5

--- a/solution.py
+++ b/solution.py
@@ -42,18 +42,20 @@
     return jnp.concatenate(pieces, axis=3).reshape(-1, width)
 
 
-def fill_shifted(image_refs, shifted):
-    side, channels = image_refs[0].shape[1], image_refs[0].shape[3]
+def fill_shifted(shifted, arrivals):
+    n_images, tall, side, channels = shifted.shape[1:]
     spots = side * side
     spot = lax.broadcasted_iota(jnp.int32, (spots, LANES), 0) % side
     empty = jnp.zeros((side, channels), jnp.bfloat16)
-    for at, ref in enumerate(image_refs):
+    for at in range(n_images):
         for col_off in range(3):
             shifted[col_off, at, 0] = empty
-            shifted[col_off, at, side + 1] = empty
-        shifted[1, at, 1 : side + 1] = ref[0]
+            shifted[col_off, at, tall - 1] = empty
+    for at, arrival in enumerate(arrivals):
+        arrival.wait()
         for lane in range(0, channels, LANES):
-            part = ref[0, :, :, lane : lane + LANES].reshape(spots, LANES).astype(jnp.float32)
+            part = shifted[1, at, 1 : side + 1, :, lane : lane + LANES]
+            part = part.reshape(spots, LANES).astype(jnp.float32)
             before_it = jnp.where(spot == 0, 0.0, pltpu.roll(part, 1, 0))
             after_it = jnp.where(spot == side - 1, 0.0, pltpu.roll(part, spots - 1, 0))
             for col_off, moved_part in ((0, before_it), (2, after_it)):
@@ -62,20 +64,37 @@
                 ).reshape(side, side, LANES)
 
 
-def products_kernel(pairs, n_pair, first, *refs):
-    place = refs[0]
-    image_refs = refs[1 : 1 + len(pairs)]
-    strip_refs = refs[1 + len(pairs) : 1 + len(pairs) + n_pair]
-    refs = refs[1 + len(pairs) + n_pair :]
+def fetch(sources, targets, sems):
+    copies = [
+        pltpu.make_async_copy(source, target, sems.at[at])
+        for at, (source, target) in enumerate(zip(sources, targets))
+    ]
+    for copy in copies:
+        copy.start()
+    return copies
+
+
+def products_kernel(owners, pairs, n_pair, first, *refs):
+    image_refs, strip_refs = refs[: len(pairs)], refs[len(pairs) : len(pairs) + n_pair]
+    refs = refs[len(pairs) + n_pair :]
     before, refs = (None, refs) if first else (refs[:4], refs[4:])
-    totals, (shifted, turned, left) = refs[:4], refs[4:]
+    out_refs, totals, (shifted, turned, left, strips, sems) = refs[:4], refs[4:8], refs[8:]
     n_images, side, channels = len(image_refs), image_refs[0].shape[1], image_refs[0].shape[3]
     spots = side * side
     cols, rows = totals[0].shape
     strip = totals[1].shape[0]
-    fsdp_at = place[2]
-
-    fill_shifted(image_refs, shifted)
+    n_fsdp = strip_refs[0].shape[0]
+    fsdp_at, factor_at = lax.axis_index("fsdp"), lax.axis_index("factor")
+
+    arrivals = fetch(
+        [ref.at[0] for ref in image_refs],
+        [shifted.at[1, at, pl.ds(1, side)] for at in range(n_images)],
+        sems.at[0],
+    )
+    strip_copies = fetch(strip_refs, [strips.at[at] for at in range(n_pair)], sems.at[1])
+    if not first:
+        total_copies = fetch(before, totals, sems.at[2])
+    fill_shifted(shifted, arrivals)
 
     def lanes_of_tap(tap, lane):
         piece = shifted[tap % 3, :, pl.ds(tap // 3, side), :, pl.ds(pl.multiple_of(lane, LANES), LANES)]
@@ -88,14 +107,24 @@
         tap = jnp.minimum(lane // channels, 8)
         turned[at : at + LANES, :] = lanes_of_tap(tap, lane % channels).T
     left[:cols, :] = turned[pl.ds(pl.multiple_of(inside, strip), cols), :]
+    for copy in strip_copies:
+        copy.wait()
     for at, pair in enumerate(pairs):
-        left[cols : cols + strip, at * spots : (at + 1) * spots] = strip_refs[pair][place[3 + at]]
+        layer, other = owners[at]
+        owner = (fsdp_at + n_fsdp - 2 * layer) % n_fsdp
+        owner = owner + other * (1 - 2 * (owner % 2))
+        left[cols : cols + strip, at * spots : (at + 1) * spots] = strips[pair, owner]
+    if not first:
+        for copy in total_copies:
+            copy.wait()
 
     tiles_per = rows // LANES
+    other_tile = factor_at + 1 - 2 * (factor_at % 2)
 
     def lanes_at(index):
         whose = jnp.where(index >= tiles_per, 1, 0)
-        start = (place[whose] * tiles_per + index - whose * tiles_per) * LANES
+        tile = jnp.where(index >= tiles_per, factor_at, other_tile)
+        start = (tile * tiles_per + index - whose * tiles_per) * LANES
         return lanes_of_tap(start // channels, start % channels)
 
     def product(first_index, count):
@@ -106,46 +135,52 @@
         at = pl.ds(pl.multiple_of(lane, LANES), count * LANES)
         for kind, part in ((0, value[:cols]), (1, value[cols:])):
             if not first:
-                part = part + before[2 * whose + kind][:, at]
+                part = part + totals[2 * whose + kind][:, at]
             totals[2 * whose + kind][:, at] = part
 
     half = tiles_per // 2
+    odd = tiles_per % 2
 
     @pl.loop(0, half)
     def _(step):
         keep(0, step * 2 * LANES, 2, product(2 * step, 2))
 
-    if tiles_per % 2:
+    if odd:
         both = product(2 * half, 2)
         keep(0, 2 * half * LANES, 1, both[:, :LANES])
         keep(1, 0, 1, both[:, LANES:])
-
-    odd = tiles_per % 2
+    theirs_out = fetch(totals[:2], out_refs[:2], sems.at[3])
 
     @pl.loop(0, half)
     def _(step):
         keep(1, (odd + 2 * step) * LANES, 2, product(tiles_per + odd + 2 * step, 2))
 
-
-def add_products(place, images, pairs, strips, before, cols, rows):
-    n_images, channels, strip = len(images), images[0].shape[3], strips[0].shape[1]
-    spots = images[0].shape[1] * images[0].shape[2]
-    shapes = [jax.ShapeDtypeStruct((height, rows), jnp.float32) for height in (cols, strip)] * 2
-    whole = pl.BlockSpec(memory_space=pltpu.VMEM)
-    operands = [place, *images, *strips, *(before or [])]
-    n_front = 1 + n_images + len(strips)
+    mine_out = fetch(totals[2:], out_refs[2:], sems.at[4])
+    for copy in theirs_out + mine_out:
+        copy.wait()
+
+
+def add_products(owners, images, pairs, strips, before, cols, rows):
+    n_images, side, channels, strip = len(images), images[0].shape[1], images[0].shape[3], strips[0].shape[1]
+    spots = side * side
+    shapes = [(height, rows) for height in (cols, strip)] * 2
+    operands = [*images, *strips, *(before or [])]
+    n_front = n_images + len(strips)
     return pl.pallas_call(
-        lambda *refs: products_kernel(pairs, len(strips), before is None, *refs),
-        out_shape=shapes,
-        in_specs=[pl.BlockSpec(memory_space=pltpu.SMEM)] + [whole] * (len(operands) - 1),
-        out_specs=[whole] * 4,
-        scratch_shapes=[
-            pltpu.VMEM((3, n_images, images[0].shape[1] + 2, images[0].shape[2], channels), jnp.bfloat16),
+        lambda *refs: products_kernel(owners, pairs, len(strips), before is None, *refs),
+        out_shape=[jax.ShapeDtypeStruct(shape, jnp.float32) for shape in shapes],
+        in_specs=[pl.BlockSpec(memory_space=pl.ANY)] * len(operands),
+        out_specs=[pl.BlockSpec(memory_space=pl.ANY)] * 4,
+        scratch_shapes=[pltpu.VMEM(shape, jnp.float32) for shape in shapes]
+        + [
+            pltpu.VMEM((3, n_images, side + 2, side, channels), jnp.bfloat16),
             pltpu.VMEM(((cols + strip + LANES - 1) // LANES * LANES, n_images * spots), jnp.bfloat16),
             pltpu.VMEM((cols + strip, n_images * spots), jnp.bfloat16),
+            pltpu.VMEM((len(strips),) + strips[0].shape, jnp.bfloat16),
+            pltpu.SemaphoreType.DMA((5, max(4, n_images))),
         ],
         input_output_aliases={} if before is None else {n_front + k: k for k in range(4)},
-        compiler_params=pltpu.CompilerParams(vmem_limit_bytes=40 * 1024 * 1024),
+        compiler_params=pltpu.CompilerParams(vmem_limit_bytes=26 * 1024 * 1024),
         cost_estimate=pl.CostEstimate(
             flops=4 * (cols + strip) * rows * n_images * spots,
             bytes_accessed=16 * (cols + strip) * rows,
@@ -154,66 +189,103 @@
     )(*operands)
 
 
-def tail_kernel(strip, block, *refs):
-    order, a_ref, g_ref = refs[:3]
-    away_ref, kept_ref, columns, inverse = refs[-4:]
-    strip_refs = refs[3:-4]
-    channels = g_ref.shape[0]
-    for at, ref in enumerate(strip_refs):
-        columns[at * strip : (at + 1) * strip, :] = ref[...]
-        rows = pl.ds(pl.multiple_of(order[at] * strip, strip), strip)
-        for to in range(channels // block):
-            lanes = pl.ds(pl.multiple_of(order[len(strip_refs) + to] * block, block), block)
-            inverse[at * strip : (at + 1) * strip, to * block : (to + 1) * block] = g_ref[rows, lanes]
+def tail_kernel(strip, block, layers, *refs):
+    a_any, g_any = refs[:2]
+    strip_refs, (away_ref, kept_ref) = refs[2:-8], refs[-8:-6]
+    a_tile, g_whole, columns, inverse, away_vmem, sems = refs[-6:]
+    channels = g_any.shape[0]
+    n_fsdp, n_factor = lax.axis_size("fsdp"), lax.axis_size("factor")
+    fsdp_at, factor_at = lax.axis_index("fsdp"), lax.axis_index("factor")
+    core_at, pair_at = factor_at % 2, factor_at // 2
+    copies = fetch([a_any, g_any], [a_tile, g_whole], sems.at[0])
+    strip_copies = fetch(
+        strip_refs,
+        [columns.at[pl.ds(at * strip, strip)] for at in range(len(strip_refs))],
+        sems.at[1],
+    )
+    copies[1].wait()
+    for at, (layer, other) in enumerate(layers):
+        owner = (fsdp_at + n_fsdp - 2 * layer) % n_fsdp
+        owner = owner + other * (1 - 2 * (owner % 2))
+        rows = pl.ds(pl.multiple_of(owner * strip, strip), strip)
+        for to in range(n_factor):
+            away, step = 1 - to // (n_factor // 2), to % (n_factor // 2)
+            place = 2 * ((pair_at + step) % (n_factor // 2)) + (core_at + away) % 2
+            lanes = pl.ds(pl.multiple_of(place * block, block), block)
+            inverse[at * strip : (at + 1) * strip, to * block : (to + 1) * block] = g_whole[rows, lanes]
+    copies[0].wait()
+    for copy in strip_copies:
+        copy.wait()
     first = lax.dot_general(
-        a_ref[...],
+        a_tile[...],
         columns[...],
         (((1,), (1,)), ((), ())),
         precision=lax.Precision.HIGH,
         preferred_element_type=jnp.float32,
     )
-    both = jnp.dot(
-        first, inverse[...], precision=lax.Precision.HIGH, preferred_element_type=jnp.float32
-    )
-    away_ref[...] = both[:, : channels // 2]
-    kept_ref[...] = both[:, channels // 2 :]
-
-
-def tail_products(order, a_inverse, g_inverse, strips, block):
+    away_vmem[...] = jnp.dot(
+        first,
+        inverse[:, : channels // 2],
+        precision=lax.Precision.HIGH,
+        preferred_element_type=jnp.float32,
+    )
+    away_out = fetch([away_vmem], [away_ref], sems.at[2])
+    kept_ref[...] = jnp.dot(
+        first,
+        inverse[:, channels // 2 :],
+        precision=lax.Precision.HIGH,
+        preferred_element_type=jnp.float32,
+    )
+    away_out[0].wait()
+
+
+def tail_products(a_inverse, g_inverse, strips, layers, block):
     channels, strip = g_inverse.shape[0], strips[0].shape[0]
     rows, depth = a_inverse.shape
-    whole = pl.BlockSpec(memory_space=pltpu.VMEM)
+    half = (rows, channels // 2)
     return pl.pallas_call(
-        lambda *refs: tail_kernel(strip, block, *refs),
-        out_shape=[jax.ShapeDtypeStruct((rows, channels // 2), jnp.float32)] * 2,
-        in_specs=[pl.BlockSpec(memory_space=pltpu.SMEM)] + [whole] * (2 + len(strips)),
-        out_specs=[whole] * 2,
+        lambda *refs: tail_kernel(strip, block, layers, *refs),
+        out_shape=[jax.ShapeDtypeStruct(half, jnp.float32)] * 2,
+        in_specs=[pl.BlockSpec(memory_space=pl.ANY)] * (2 + len(strips)),
+        out_specs=[pl.BlockSpec(memory_space=pl.ANY), pl.BlockSpec(memory_space=pltpu.VMEM)],
         scratch_shapes=[
+            pltpu.VMEM((rows, depth), jnp.float32),
+            pltpu.VMEM((channels, channels), jnp.float32),
             pltpu.VMEM((channels, depth), jnp.float32),
             pltpu.VMEM((channels, channels), jnp.float32),
+            pltpu.VMEM(half, jnp.float32),
+            pltpu.SemaphoreType.DMA((3, max(2, len(strips)))),
         ],
-        compiler_params=pltpu.CompilerParams(vmem_limit_bytes=32 * 1024 * 1024),
+        compiler_params=pltpu.CompilerParams(vmem_limit_bytes=26 * 1024 * 1024),
         cost_estimate=pl.CostEstimate(
             flops=6 * rows * channels * (depth + channels),
             bytes_accessed=4 * rows * (depth + channels),
             transcendentals=0,
         ),
-    )(order, a_inverse, g_inverse, *strips)
-
-
-def conv_kernel(order, *refs):
-    order_ref, refs = refs[0], refs[1:]
-    n_images, n_parts = order
-    image_refs, part_refs = refs[:n_images], refs[n_images : n_images + n_parts]
-    out_refs = refs[n_images + n_parts : -2]
-    shifted, weight = refs[-2:]
+    )(a_inverse, g_inverse, *strips)
+
+
+def conv_kernel(n_images, *refs):
+    image_refs, part_refs = refs[:n_images], refs[n_images : n_images + 2]
+    out_refs, (shifted, parts, weight, sems) = refs[n_images + 2 : -4], refs[-4:]
     side, channels = image_refs[0].shape[1], image_refs[0].shape[3]
-    depth = part_refs[0].shape[0]
-    fill_shifted(image_refs, shifted)
-    for at, ref in enumerate(part_refs):
-        weight[pl.ds(pl.multiple_of(order_ref[at] * depth, 64), depth), :] = ref[...]
+    n_near, depth, block = part_refs[0].shape
+    fsdp_at = lax.axis_index("fsdp")
+    arrivals = fetch(
+        [ref.at[0] for ref in image_refs],
+        [shifted.at[1, at, pl.ds(1, side)] for at in range(n_images)],
+        sems.at[0],
+    )
+    part_copies = fetch(part_refs, [parts.at[at] for at in range(2)], sems.at[1])
+    fill_shifted(shifted, arrivals)
+    for copy in part_copies:
+        copy.wait()
+    for near in range(n_near):
+        for far in range(2):
+            owner = (fsdp_at ^ (2 * near + far)) * depth
+            weight[pl.ds(pl.multiple_of(owner, 64), depth), :] = parts[far, near]
     for at, ref in enumerate(out_refs):
-        total = jnp.zeros((side * side, weight.shape[1]), jnp.float32)
+        total = jnp.zeros((side * side, block), jnp.float32)
         for tap in range(9):
             left = shifted[tap % 3, at, tap // 3 : tap // 3 + side].reshape(side * side, channels)
             total += jnp.dot(
@@ -221,46 +293,50 @@
                 weight[tap * channels : (tap + 1) * channels, :],
                 preferred_element_type=jnp.float32,
             )
-        ref[0] = total.astype(jnp.bfloat16).reshape(side, side, weight.shape[1])
-
-
-def convolve(order, images, parts):
+        ref[0] = total.astype(jnp.bfloat16).reshape(side, side, block)
+
+
+def convolve(images, near_parts, far_parts):
     n_images, (_, side, _, channels) = len(images), images[0].shape
-    depth, block = parts[0].shape
-    whole = pl.BlockSpec(memory_space=pltpu.VMEM)
+    block = near_parts.shape[2]
     return pl.pallas_call(
-        lambda *refs: conv_kernel((n_images, len(parts)), *refs),
+        lambda *refs: conv_kernel(n_images, *refs),
         out_shape=[jax.ShapeDtypeStruct((1, side, side, block), jnp.bfloat16)] * n_images,
-        in_specs=[pl.BlockSpec(memory_space=pltpu.SMEM)] + [whole] * (n_images + len(parts)),
-        out_specs=[whole] * n_images,
+        in_specs=[pl.BlockSpec(memory_space=pl.ANY)] * (n_images + 2),
+        out_specs=[pl.BlockSpec(memory_space=pltpu.VMEM)] * n_images,
         scratch_shapes=[
             pltpu.VMEM((3, n_images, side + 2, side, channels), jnp.bfloat16),
+            pltpu.VMEM((2,) + near_parts.shape, jnp.bfloat16),
             pltpu.VMEM((9 * channels, block), jnp.bfloat16),
+            pltpu.SemaphoreType.DMA((2, n_images)),
         ],
-        compiler_params=pltpu.CompilerParams(vmem_limit_bytes=24 * 1024 * 1024),
+        compiler_params=pltpu.CompilerParams(vmem_limit_bytes=16 * 1024 * 1024),
         cost_estimate=pl.CostEstimate(
             flops=36 * n_images * side * side * channels * block,
             bytes_accessed=2 * (9 * channels * block + n_images * side * side * channels),
             transcendentals=0,
         ),
-    )(order, *images, *parts)
-
-
-def side_by_side_kernel(order_ref, *refs):
-    block = refs[0].shape[3]
+    )(*images, near_parts, far_parts)
+
+
+def side_by_side_kernel(*refs):
+    block, n_factor = refs[0].shape[3], lax.axis_size("factor")
+    factor_at, n_pair = lax.axis_index("factor"), n_factor // 2
     for at, ref in enumerate(refs[:-1]):
-        refs[-1][:, :, :, pl.ds(pl.multiple_of(order_ref[at] * block, LANES), block)] = ref[...]
-
-
-def side_by_side(order, blocks):
+        place = 2 * ((factor_at // 2 + at % n_pair) % n_pair) + (factor_at + at // n_pair) % 2
+        refs[-1][:, :, :, pl.ds(pl.multiple_of(place * block, LANES), block)] = ref[...]
+
+
+def side_by_side(blocks):
     whole = pl.BlockSpec(memory_space=pltpu.VMEM)
     shape = blocks[0].shape[:3] + (len(blocks) * blocks[0].shape[3],)
     return pl.pallas_call(
         side_by_side_kernel,
         out_shape=jax.ShapeDtypeStruct(shape, blocks[0].dtype),
-        in_specs=[pl.BlockSpec(memory_space=pltpu.SMEM)] + [whole] * len(blocks),
+        in_specs=[whole] * len(blocks),
         out_specs=whole,
-    )(order, *blocks)
+        compiler_params=pltpu.CompilerParams(vmem_limit_bytes=4 * 1024 * 1024),
+    )(*blocks)
 
 
 def gather_plan(n_layer, n_pair):
@@ -283,12 +359,10 @@
         due = {item: when for item, when in due.items() if when > len(rounds)}
         now = []
         for link in (by_layer, by_side, by_pair):
-            if link is by_layer and any(item[0] == "layer" for item in due):
-                continue
             free = [item for item in link if item[1] in here]
-            if free:
-                link.remove(free[0])
-                item, source = free[0]
+            for chosen in free[: 2 if link is by_layer and rounds else 1]:
+                link.remove(chosen)
+                item, source = chosen
                 hops = min(item[1], n_layer - item[1]) if item[0] == "layer" else 1
                 due[item] = len(rounds) + hops
                 now.append((item, source, "pair" if link is by_pair else item[0], hops))
@@ -366,9 +440,9 @@
             owners.append(owner ^ 1 if kind in ("side", "both") else owner)
             pairs.append(pair)
         if aligned:
-            place = jnp.stack([factor_at ^ 1, factor_at, fsdp_at] + owners)
             totals = add_products(
-                place, [maps[item] for item in batch], pairs, strips_by_pair, totals, cols, rows
+                [(layer, int(kind in ("side", "both"))) for kind, layer, _ in batch],
+                [maps[item] for item in batch], pairs, strips_by_pair, totals, cols, rows
             )
             early = early or [totals[3]]
             continue
@@ -389,7 +463,7 @@
                 more.append(jnp.dot(cot_tile, row_tile, preferred_element_type=jnp.float32))
             totals = more if totals is None else [old + new for old, new in zip(totals, more)]
 
-    g_partial = by_rows(after(own_cot, events[2]), own_cot).reshape(n_pair, 2, block, channels)
+    g_partial = by_rows(own_cot, own_cot).reshape(n_pair, 2, block, channels)
     g_pairs = lax.dynamic_index_in_dim(g_partial, core_at, 1, keepdims=False) + over_core(
         lax.dynamic_index_in_dim(g_partial, 1 - core_at, 1, keepdims=False)
     )
@@ -400,21 +474,20 @@
         g_sum = g_sum + over_pair(away, step)
     weight_part = after(weight, events[1])
     near_parts = [lax.dynamic_slice_in_dim(weight_part, factor_at * block, block, 1)]
-    g_steps, distance, at = [g_sum], 2, 2
+    distance, at = 2, 2
     while distance < n_fsdp:
         both = after(jnp.stack(near_parts), events[min(at, last)])
         both = moved(both, "fsdp", lambda to, d=distance: to ^ d)
         near_parts = near_parts + [both[k] for k in range(len(near_parts))]
-        g_sum = after(g_sum, events[last] if distance == 2 else events[last + 1] + early)
-        g_sum = g_sum + moved(g_sum, "fsdp", lambda to, d=distance: to ^ d)
-        g_steps.append(g_sum)
         distance, at = 2 * distance, at + 2
-    far_parts = over_side(after(jnp.stack(near_parts), events[last + 1] + early))
-    parts = [
-        part for k in range(len(near_parts)) for part in (near_parts[k], far_parts[k])
-    ]
-
-    theirs = after(totals[1], [far_parts, g_steps[-1]])
+    near_stack = jnp.stack(near_parts)
+    far_parts = over_side(after(near_stack, events[last + 1] + early))
+
+    g_sum = after(g_sum, events[last + 1] + early)
+    g_sum = g_sum + moved(g_sum, "fsdp", lambda to: to ^ 2)
+    near_images = [activations] + [maps["pair", 0, step] for step in range(1, n_pair)]
+    group = near_images + [over_core(image) for image in after(near_images, events[last])]
+    theirs = after(totals[1], [far_parts, g_sum] + group)
     grad_own = totals[3] + over_core(theirs)
     pixel_total = float(
         activations.shape[0] * activations.shape[1] * activations.shape[2] * n_fsdp * n_factor
@@ -430,7 +503,7 @@
         array[:, :rows].astype(jnp.float32) * jnp.exp2(array[:, rows : rows + 1].astype(jnp.float32))
         for array in near_packed + far_packed
     ]
-    cov_own = totals[2] + over_core(after(totals[0], near_packed[1:2]))
+    cov_own = totals[2] + over_core(after(totals[0], [packed]))
     a_factor = 0.5 * a_factor_old + (0.5 / pixel_total) * cov_own.T
     came_from = [(fsdp_at - 2 * step) % n_fsdp for step in range(n_layer)]
     came_from = came_from + [at ^ 1 for at in came_from]
@@ -439,14 +512,14 @@
         for other in (1, 0)
         for step in range(n_pair)
     ]
-    near_images = [activations] + [maps["pair", 0, step] for step in range(1, n_pair)]
-    other_images = after(near_images, events[last] + [near_parts[0]])
-    group = near_images + [over_core(image) for image in other_images]
+    g_sum = after(g_sum, near_packed[1:2])
+    g_sum = g_sum + over_side(g_sum)
+    group = after(group, near_packed[1:2])
     part_order = [fsdp_at ^ at for at in range(n_fsdp)]
     if aligned and block % LANES == 0:
-        group_out = convolve(jnp.stack(part_order), group, parts)
+        group_out = convolve(group, near_stack, far_parts)
     else:
-        kernel = jnp.stack(parts)
+        kernel = jnp.stack([part for pair in zip(near_stack, far_parts) for part in pair])
         kernel = jnp.concatenate(
             [lax.dynamic_index_in_dim(kernel, at, 0, keepdims=False) for at in part_order]
         ).reshape(3, 3, channels, block)
@@ -462,7 +535,11 @@
 
     if aligned and block % LANES == 0:
         away, kept = tail_products(
-            jnp.stack(came_from + order), after(a_inverse, group_out), g_inverse, strips_of_grad, block
+            after(a_inverse, [*group_out, a_factor, g_sum]),
+            g_inverse,
+            strips_of_grad,
+            [(step, other) for other in range(2) for step in range(n_layer)],
+            block,
         )
     else:
         inverse = jnp.concatenate(
@@ -486,7 +563,7 @@
     result = by_pair[:, :block]
     for step in range(1, n_pair):
         back = over_pair(by_pair[:, step * block : (step + 1) * block], step)
-        result = result + after(back, a_factor)
+        result = result + back
     natural_grad = result.astype(jnp.bfloat16)
 
 
@@ -500,15 +577,19 @@
             block_order.append(2 * ((pair_at + pair) % n_pair) + (core_at + other) % 2)
     own_maps = after(own_maps, by_pair)
     if aligned and block % LANES == 0:
-        conv_out = side_by_side(jnp.stack(block_order), own_maps)
+        conv_out = side_by_side(own_maps)
     else:
         stacked = jnp.zeros((n_factor,) + own_maps[0].shape, jnp.bfloat16)
         for at, out in zip(block_order, own_maps):
             stacked = lax.dynamic_update_index_in_dim(stacked, out, at, 0)
         conv_out = jnp.concatenate(jnp.split(stacked, n_factor), axis=4)[0]
 
-    g_back = over_side(after(g_steps[-1], strips_of_grad[1:2]))
-    g_factor_sum = g_steps[-1] + after(g_back, by_pair)
+    distance = 4
+    while distance < n_fsdp:
+        g_sum = after(g_sum, strips_of_grad[:n_layer])
+        g_sum = g_sum + moved(g_sum, "fsdp", lambda to, d=distance: to ^ d)
+        distance *= 2
+    g_factor_sum = g_sum
     g_factor = 0.5 * g_factor_old + 0.5 * g_factor_sum
     return (conv_out, a_factor, g_factor, natural_grad)
 

time: 169 us -> 166 us (0.982)
  local copies, waits for them, and re-layouts: 24.3 us -> 13.8 us
  starting transfers between devices: 44.3 us -> 53.8 us
  other arithmetic: 18.3 us -> 9.59 us
  waiting for transfers between devices: 41.2 us -> 49.6 us
    ppermute x40, starting transfers between devices: 40.9 us -> 49.6 us  [moved(): lax.ppermute(array, axis, [(at, target(at) % count) for at in range(count)])]
    ppermute x40, waiting for transfers between devices: 41.2 us -> 49.6 us  [moved(): lax.ppermute(array, axis, [(at, target(at) % count) for at in range(count)])]
    unnamed x88 -> x74, local copies, waits for them, and re-layouts: 15.5 us -> 9.79 us
    add x1, other arithmetic: 4.5 us -> 1.96 us  [per_device(): a_factor = 0.5 * a_factor_old + 0.5 / pixel_total * cov_own.T]
  transfers between devices with their start and end apart: 41 -> 41, of which waited for: 18 -> 14; matrix products, arithmetic and copies ran while one was open for 16% -> 5% of each run, Pallas kernels for 22% -> 18%
where the time goes in v6:
time: 166 us; the launch traced here: 165 us
  starting transfers between devices  53.8 us (32%)
  waiting for transfers between devices  49.6 us (30%)
  Pallas kernels  35.2 us (21%)
  local copies, waits for them, and re-layouts  13.8 us (8%)
  other arithmetic  9.59 us (6%)
  between operations  2.03 us (1%)
    ppermute x40, starting transfers between devices, moved(): lax.ppermute(array, axis, [(at, target(at) % count) for at in range(count)])  49.6 us
    ppermute x40, waiting for transfers between devices, moved(): lax.ppermute(array, axis, [(at, target(at) % count) for at in range(count)])  49.6 us
    pallas_call x2, Pallas kernels, add_products(): pl.pallas_call(lambda *refs: products_kernel(owners, pairs, len(strips),...  24.2 us
    unnamed x74, local copies, waits for them, and re-layouts  9.79 us
    pallas_call x1, Pallas kernels, tail_products(): pl.pallas_call(lambda *refs: tail_kernel(strip, block, layers, *refs), ou...  5.72 us
    pallas_call x1, Pallas kernels, convolve(): pl.pallas_call(lambda *refs: conv_kernel(n_images, *refs), out_shape=[jax...  4.53 us
    all_to_all x1, starting transfers between devices, per_device(): lax.all_to_all(strips, 'fsdp', split_axis=0, concat_axis=0)  4.12 us
  transfers between devices with their start and end apart: 41, of which 14 were waited for; matrix products, arithmetic and copies ran while one was open for 5% of the time, Pallas kernels for 18%

profile of v6, /device:TPU:0, one launch (start us, length us, event | category | flops | bytes accessed | tf_op | source)
XLA Modules:
  0.0 165.2 jit_solution(10196566043714994825)
XLA Ops:
  0.6 3.0 %collective-permute-start = (bf16[1,16,16,512]{3,2,1,0:T(8,128)(2,1)}, bf16[1,16,16,512]{3,2,1,0:T(8,128)(2,1)S(1)}, u32[]{:S(2)}, u32[]{:S(2)}) collective-permute-start(bf16[1,16,16,512]{3,2,1,0:T(8,128)(2,1)} %refs_0_.2), channel_id=1, source_target_pairs={{0,2},{1,3},{2,0},{3,1},{4,6},{5,7},{6,4},{7,5},{8,10},{9,11},{10,... | collective-permute-start | bytes 786440 | tf_op jit(solution)/shard_map/ppermute | solution.py:19
  3.7 1.6 collective-permute-start.1
  5.3 1.5 collective-permute-start.2
  6.7 1.1 copy.18
  7.8 2.4 %collective-permute-done.refs_3_.refs_1_ = bf16[1,16,16,512]{3,2,1,0:T(8,128)(2,1)S(1)} collective-permute-done((bf16[1,16,16,512]{3,2,1,0:T(8,128)(2,1)}, bf16[1,16,16,512]{3,2,1,0:T(8,128)(2,1)S(1)}, u32[]{:S(2)}, u32[]{:S(2)}) %collective-permute-start) | collective-permute-done | bytes 262176 | tf_op jit(solution)/shard_map/ppermute | solution.py:19
  10.2 3.3 %collective-permute-done.1.refs_1_ = bf16[1,16,16,512]{3,2,1,0:T(8,128)(2,1)S(1)} collective-permute-done((bf16[1,16,16,512]{3,2,1,0:T(8,128)(2,1)}, bf16[1,16,16,512]{3,2,1,0:T(8,128)(2,1)S(1)}, u32[]{:S(2)}, u32[]{:S(2)}) %collective-permute-start.1) | collective-permute-done | bytes 262176 | tf_op jit(solution)/shard_map/ppermute | solution.py:19
  13.6 2.0 %copy.17 = bf16[512,256]{1,0:T(8,128)(2,1)} copy(bf16[512,256]{0,1:T(8,128)(2,1)} %bitcast.25) | data formatting | bytes 524288 | tf_op jit(solution)/shard_map/transpose | solution.py:412
  15.5 4.1 %all-to-all-start = ((bf16[8,64,256]{2,1,0:T(8,128)(2,1)}), bf16[8,64,256]{2,1,0:T(8,128)(2,1)S(1)}, u32[]{:S(2)}, u32[]{:S(2)}) async-start(bf16[8,64,256]{2,1,0:T(8,128)(2,1)} %bitcast.2), calls=%async_computation | async-start | bytes 524288 | tf_op jit(solution)/shard_map/all_to_all | solution.py:413
  20.1 3.8 %collective-permute-start.5 = (bf16[1,16,16,512]{3,2,1,0:T(8,128)(2,1)}, bf16[1,16,16,512]{3,2,1,0:T(8,128)(2,1)S(1)}, u32[]{:S(2)}, u32[]{:S(2)}) collective-permute-start(bf16[1,16,16,512]{3,2,1,0:T(8,128)(2,1)} %refs_0_.2), channel_id=1, source_target_pairs={{0,24},{4,28},{8,0},{12,4},{16,8},{20,12},{24,16},{28,20},{1,25},{... | collective-permute-start | bytes 786440 | tf_op jit(solution)/shard_map/ppermute | solution.py:19
  24.0 1.5 collective-permute-start.6
  25.4 1.2 fusion.1
  26.8 4.2 %collective-permute-done.5.refs_0_ = bf16[1,16,16,512]{3,2,1,0:T(8,128)(2,1)S(1)} collective-permute-done((bf16[1,16,16,512]{3,2,1,0:T(8,128)(2,1)}, bf16[1,16,16,512]{3,2,1,0:T(8,128)(2,1)S(1)}, u32[]{:S(2)}, u32[]{:S(2)}) %collective-permute-start.5) | collective-permute-done | bytes 262176 | tf_op jit(solution)/shard_map/ppermute | solution.py:19
  31.1 1.5 collective-permute-start.7
  32.5 1.5 collective-permute-start.8
  34.0 0.8 dynamic-slice_bitcast_fusion
  34.9 9.1 %collective-permute-done.4.refs_1_ = bf16[1,16,16,512]{3,2,1,0:T(8,128)(2,1)S(1)} collective-permute-done((bf16[1,16,16,512]{3,2,1,0:T(8,128)(2,1)}, bf16[1,16,16,512]{3,2,1,0:T(8,128)(2,1)S(1)}, u32[]{:S(2)}, u32[]{:S(2)}) %collective-permute-start.4) | collective-permute-done | bytes 262176 | tf_op jit(solution)/shard_map/ppermute | solution.py:19
  44.0 0.7 copy-done.23
  45.4 1.4 collective-permute-start.10
  46.9 1.4 collective-permute-start.11
  48.3 4.6 %collective-permute-start.18 = (bf16[1,576,128]{2,1,0:T(8,128)(2,1)S(1)}, bf16[1,576,128]{2,1,0:T(8,128)(2,1)S(1)}, u32[]{:S(2)}, u32[]{:S(2)}) collective-permute-start(bf16[1,576,128]{2,1,0:T(8,128)(2,1)S(1)} %dynamic-slice_bitcast_fusion.2), channel_id=1, source_target_pairs={{0,8},{4,12},{8,0},{12,4},{16,24},{20,28},{24,16},{28,20},{1,9},{5... | collective-permute-start | bytes 442376 | tf_op jit(solution)/shard_map/ppermute | solution.py:19
  52.8 1.2 collective-permute-done.9.refs_9_
  54.0 3.1 %collective-permute-done.11.refs_5_ = bf16[1,16,16,512]{3,2,1,0:T(8,128)(2,1)} collective-permute-done((bf16[1,16,16,512]{3,2,1,0:T(8,128)(2,1)S(1)}, bf16[1,16,16,512]{3,2,1,0:T(8,128)(2,1)}, u32[]{:S(2)}, u32[]{:S(2)}) %collective-permute-start.11) | collective-permute-done | bytes 262176 | tf_op jit(solution)/shard_map/ppermute | solution.py:19
  57.2 1.4 collective-permute-start.12
  58.5 0.7 collective-permute-start.13
  59.2 1.3 bitcast_add_fusion.1
  60.6 2.0 %collective-permute-start.19 = (bf16[2,576,128]{2,1,0:T(8,128)(2,1)S(1)}, bf16[2,576,128]{2,1,0:T(8,128)(2,1)S(1)}, u32[]{:S(2)}, u32[]{:S(2)}) collective-permute-start(bf16[2,576,128]{2,1,0:T(8,128)(2,1)S(1)} %pad_maximum_fusion.1), channel_id=1, source_target_pairs={{0,16},{4,20},{8,24},{12,28},{16,0},{20,4},{24,8},{28,12},{1,17},{... | collective-permute-start | bytes 884744 | tf_op jit(solution)/shard_map/ppermute | solution.py:19
  62.5 1.0 collective-permute-done.12.refs_6_
  63.5 1.4 collective-permute-done.13.refs_7_
  64.9 0.7 collective-permute-start.16
  65.6 1.1 collective-permute-start.17
  66.7 1.0 collective-permute-start.22
  67.7 0.9 copy-done.9
  68.7 0.9 copy-done.14
  69.6 0.9 copy-done.16
  70.6 0.9 copy-done.18
  71.5 0.9 copy-done.22
  72.5 0.9 copy-done.28
  73.5 12.2 %shard_map.102 = (f32[576,1152]{1,0:T(8,128)S(1)}, f32[64,1152]{1,0:T(8,128)S(1)}, f32[576,1152]{1,0:T(8,128)S(1)}, f32[64,1152]{1,0:T(8,128)S(1)}) custom-call(bf16[1,16,16,512]{3,2,1,0:T(8,128)(2,1)} %refs_0_.2, bf16[1,16,16,512]{3,2,1,0:T(8,128)(2,1)S(1)} %copy-done.14, bf16[1,16,16,512]{3,2,1,0:T(8,128)(2,1)S(1)} %copy-done.16, ...), custom_call_target="tpu_custom_call" | custom-call | flops 6039797760 | bytes 11796480 | tf_op jit(solution)/shard_map/pallas_call | solution.py:169
  85.8 1.4 collective-permute-start.20
  87.3 3.7 %collective-permute-start.23 = (f32[128,512]{1,0:T(8,128)S(1)}, f32[128,512]{1,0:T(8,128)S(1)}, u32[]{:S(2)}, u32[]{:S(2)}) collective-permute-start(f32[128,512]{1,0:T(8,128)S(1)} %bitcast_add_fusion.2), channel_id=1, source_target_pairs={{0,8},{4,12},{8,0},{12,4},{16,24},{20,28},{24,16},{28,20},{1,9},{5... | collective-permute-start | bytes 786440 | tf_op jit(solution)/shard_map/ppermute | solution.py:19
  91.0 12.0 %shard_map.103 = (f32[576,1152]{1,0:T(8,128)S(1)}, f32[64,1152]{1,0:T(8,128)S(1)}, f32[576,1152]{1,0:T(8,128)S(1)}, f32[64,1152]{1,0:T(8,128)S(1)}) custom-call(bf16[1,16,16,512]{3,2,1,0:T(8,128)(2,1)S(1)} %copy-done.12, bf16[1,16,16,512]{3,2,1,0:T(8,128)(2,1)S(1)} %copy-done.20, ...), custom_call_target="tpu_custom_call", output_to_operand_aliasing={{0}: (10, {}), {1}: (11, {}), {2}: (12, {}), {3}: (13, {})} | custom-call | flops 6039797760 | bytes 11796480 | tf_op jit(solution)/shard_map/pallas_call | solution.py:169
  103.0 1.5 copy-done.4
  104.5 0.7 add.76
  105.3 0.7 copy-done.31
  106.2 1.4 collective-permute-done.24
  107.6 1.3 abs_reduce_fusion
  109.8 1.1 convert_multiply_fusion.7
  112.0 2.0 %collective-permute-start.33 = (f16[64,1280]{1,0:T(8,128)(2,1)S(1)}, f16[64,1280]{1,0:T(8,128)(2,1)S(1)}, u32[]{:S(2)}, u32[]{:S(2)}) collective-permute-start(f16[64,1280]{1,0:T(8,128)(2,1)S(1)} %concatenate.3), channel_id=1, source_target_pairs={{0,4},{4,0},{8,12},{12,8},{16,20},{20,16},{24,28},{28,24},{1,5},{5... | collective-permute-start | bytes 491528 | tf_op jit(solution)/shard_map/ppermute | solution.py:19
  114.0 2.8 %collective-permute-start.32 = (f16[64,1280]{1,0:T(8,128)(2,1)S(1)}, f16[64,1280]{1,0:T(8,128)(2,1)S(1)}, u32[]{:S(2)}, u32[]{:S(2)}) collective-permute-start(f16[64,1280]{1,0:T(8,128)(2,1)S(1)} %concatenate.3), channel_id=1, source_target_pairs={{0,24},{4,28},{8,0},{12,4},{16,8},{20,12},{24,16},{28,20},{1,25},{... | collective-permute-start | bytes 491528 | tf_op jit(solution)/shard_map/ppermute | solution.py:19
  116.8 3.1 %collective-permute-done.25 = f16[64,1280]{1,0:T(8,128)(2,1)S(1)} collective-permute-done((f16[64,1280]{1,0:T(8,128)(2,1)S(1)}, f16[64,1280]{1,0:T(8,128)(2,1)S(1)}, u32[]{:S(2)}, u32[]{:S(2)}) %collective-permute-start.25) | collective-permute-done | bytes 163872 | tf_op jit(solution)/shard_map/ppermute | solution.py:19
  119.9 2.0 %collective-permute-start.30 = (f32[128,512]{1,0:T(8,128)}, f32[128,512]{1,0:T(8,128)S(1)}, u32[]{:S(2)}, u32[]{:S(2)}) collective-permute-start(f32[128,512]{1,0:T(8,128)} %add.76), channel_id=1, source_target_pairs={{0,4},{4,0},{8,12},{12,8},{16,20},{20,16},{24,28},{28,24},{1,5},{5... | collective-permute-start | bytes 786440 | tf_op jit(solution)/shard_map/ppermute | solution.py:19
  121.9 4.3 %collective-permute-done.31 = f16[64,1280]{1,0:T(8,128)(2,1)S(1)} collective-permute-done((f16[64,1280]{1,0:T(8,128)(2,1)S(1)}, f16[64,1280]{1,0:T(8,128)(2,1)S(1)}, u32[]{:S(2)}, u32[]{:S(2)}) %collective-permute-start.31) | collective-permute-done | bytes 163872 | tf_op jit(solution)/shard_map/ppermute | solution.py:19
  126.3 1.9 %collective-permute-start.35 = (f16[64,1280]{1,0:T(8,128)(2,1)S(1)}, f16[64,1280]{1,0:T(8,128)(2,1)S(1)}, u32[]{:S(2)}, u32[]{:S(2)}) collective-permute-start(f16[64,1280]{1,0:T(8,128)(2,1)S(1)} %collective-permute-done.31), channel_id=1, source_target_pairs={{0,4},{4,0},{8,12},{12,8},{16,20},{20,16},{24,28},{28,24},{1,5},{5... | collective-permute-start | bytes 491528 | tf_op jit(solution)/shard_map/ppermute | solution.py:19
  129.0 1.9 %collective-permute-start.36 = (f16[64,1280]{1,0:T(8,128)(2,1)S(1)}, f16[64,1280]{1,0:T(8,128)(2,1)S(1)}, u32[]{:S(2)}, u32[]{:S(2)}) collective-permute-start(f16[64,1280]{1,0:T(8,128)(2,1)S(1)} %collective-permute-done.32), channel_id=1, source_target_pairs={{0,4},{4,0},{8,12},{12,8},{16,20},{20,16},{24,28},{28,24},{1,5},{5... | collective-permute-start | bytes 491528 | tf_op jit(solution)/shard_map/ppermute | solution.py:19
  131.2 4.5 %shard_map.104 = (bf16[1,16,16,128]{3,2,1,0:T(8,128)(2,1)S(1)}, bf16[1,16,16,128]{3,2,1,0:T(8,128)(2,1)S(1)}, bf16[1,16,16,128]{3,2,1,0:T(8,128)(2,1)S(1)}, bf16[1,16,16,128]{3,2,1,0:T(8,128)(2,1)S(1)}) custom-call(bf16[1,16,16,512]{3,2,1,0:T(8,128)(2,1)} %refs_0_.2, bf16[1,16,16,512]{3,2,1,0:T(8,128)(2,1)S(1)} %copy-done.10, ...), custom_call_target="tpu_custom_call" | custom-call | flops 2415919104 | bytes 2228224 | tf_op jit(solution)/shard_map/pallas_call | solution.py:302
  135.7 2.4 %collective-permute-done.36 = f16[64,1280]{1,0:T(8,128)(2,1)S(1)} collective-permute-done((f16[64,1280]{1,0:T(8,128)(2,1)S(1)}, f16[64,1280]{1,0:T(8,128)(2,1)S(1)}, u32[]{:S(2)}, u32[]{:S(2)}) %collective-permute-start.36) | collective-permute-done | bytes 163872 | tf_op jit(solution)/shard_map/ppermute | solution.py:19
  138.9 2.0 %bitcast_add_fusion = f32[1152,576]{0,1:T(8,128)} fusion(f32[576,1152]{1,0:T(8,128)S(1)} %get-tuple-element.96, f32[576,1152]{1,0:T(8,128)S(1)} %collective-permute-done.29, f32[1152,576]{0,1:T(8,128)S(1)} %copy-done.34), kind=kLoop, calls=%fused_computation | loop fusion | flops 2654208 | bytes 10616832 | tf_op jit(solution)/shard_map/add | solution.py:507
  141.9 5.7 %shard_map.105 = (f32[576,256]{1,0:T(8,128)S(1)}, f32[576,256]{1,0:T(8,128)S(1)}) custom-call(f32[576,1152]{1,0:T(8,128)S(1)} %copy-done.3, f32[512,512]{1,0:T(8,128)S(1)} %copy-done.5, f32[64,1152]{1,0:T(8,128)S(1)} %get-tuple-element.108.refs_2_, f32[64,1152]{1,0:T(8,128)S(1)} %convert_multiply_fusion.6.refs_3_, ...), custom_call_target="tpu_custom_call" | custom-call | flops 2944401408 | bytes 3833856 | tf_op jit(solution)/shard_map/pallas_call | solution.py:246
  147.9 1.8 %collective-permute-done.37 = f32[576,256]{1,0:T(8,128)S(1)} collective-permute-done((f32[576,256]{1,0:T(8,128)S(1)}, f32[576,256]{1,0:T(8,128)S(1)}, u32[]{:S(2)}, u32[]{:S(2)}) %collective-permute-start.37) | collective-permute-done | bytes 589856 | tf_op jit(solution)/shard_map/ppermute | solution.py:19
  149.9 2.0 %collective-permute-start.26 = (bf16[1,16,16,128]{3,2,1,0:T(8,128)(2,1)S(1)}, bf16[1,16,16,128]{3,2,1,0:T(8,128)(2,1)S(1)}, u32[]{:S(2)}, u32[]{:S(2)}) collective-permute-start(bf16[1,16,16,128]{3,2,1,0:T(8,128)(2,1)S(1)} %get-tuple-element.93), channel_id=1, source_target_pairs={{0,2},{1,3},{2,0},{3,1},{4,6},{5,7},{6,4},{7,5},{8,10},{9,11},{10,... | collective-permute-start | bytes 196616 | tf_op jit(solution)/shard_map/ppermute | solution.py:19
  152.1 10.9 %collective-permute-done.38 = f32[128,512]{1,0:T(8,128)S(1)} collective-permute-done((f32[128,512]{1,0:T(8,128)S(1)}, f32[128,512]{1,0:T(8,128)S(1)}, u32[]{:S(2)}, u32[]{:S(2)}) %collective-permute-start.38) | collective-permute-done | bytes 262176 | tf_op jit(solution)/shard_map/ppermute | solution.py:19
  162.9 0.8 add_multiply_fusion
  163.7 0.8 shard_map.106
  164.5 0.7 fusion
  (131 shorter events, 6.4 us)
Async XLA Ops:
  0.6 47.6 %copy-start = (bf16[576,512]{1,0:T(8,128)(2,1)S(1)}, bf16[576,512]{1,0:T(8,128)(2,1)}, u32[]{:S(2)}) copy-start(bf16[576,512]{1,0:T(8,128)(2,1)} %param.9) | copy-start | bytes 1769476
  0.6 9.6 %collective-permute-start = (bf16[1,16,16,512]{3,2,1,0:T(8,128)(2,1)}, bf16[1,16,16,512]{3,2,1,0:T(8,128)(2,1)S(1)}, u32[]{:S(2)}, u32[]{:S(2)}) collective-permute-start(bf16[1,16,16,512]{3,2,1,0:T(8,128)(2,1)} %refs_0_.2), channel_id=1, source_target_pairs={{0,2},{1,3},{2,0},{3,1},{4,6},{5,7},{6,4},{7,5},{8,10},{9,11},{10,... | collective-permute-start | bytes 786440 | tf_op jit(solution)/shard_map/ppermute | solution.py:19
  3.7 9.9 %collective-permute-start.1 = (bf16[1,16,16,512]{3,2,1,0:T(8,128)(2,1)}, bf16[1,16,16,512]{3,2,1,0:T(8,128)(2,1)S(1)}, u32[]{:S(2)}, u32[]{:S(2)}) collective-permute-start(bf16[1,16,16,512]{3,2,1,0:T(8,128)(2,1)} %refs_0_.2), channel_id=1, source_target_pairs={{0,8},{4,12},{8,16},{12,20},{16,24},{20,28},{24,0},{28,4},{1,9},{5... | collective-permute-start | bytes 786440 | tf_op jit(solution)/shard_map/ppermute | solution.py:19
  5.3 8.3 %collective-permute-start.2 = (bf16[1,16,16,512]{3,2,1,0:T(8,128)(2,1)}, bf16[1,16,16,512]{3,2,1,0:T(8,128)(2,1)S(1)}, u32[]{:S(2)}, u32[]{:S(2)}) collective-permute-start(bf16[1,16,16,512]{3,2,1,0:T(8,128)(2,1)} %refs_0_.2), channel_id=1, source_target_pairs={{0,4},{4,0},{8,12},{12,8},{16,20},{20,16},{24,28},{28,24},{1,5},{5... | collective-permute-start | bytes 786440 | tf_op jit(solution)/shard_map/ppermute | solution.py:19
  13.5 46.9 %copy-start.13 = (bf16[1,16,16,512]{3,2,1,0:T(8,128)(2,1)}, bf16[1,16,16,512]{3,2,1,0:T(8,128)(2,1)S(1)}, u32[]{:S(2)}) copy-start(bf16[1,16,16,512]{3,2,1,0:T(8,128)(2,1)S(1)} %collective-permute-done.1.refs_1_) | copy-start | bytes 786436
  13.6 47.0 %copy-start.15 = (bf16[1,16,16,512]{3,2,1,0:T(8,128)(2,1)}, bf16[1,16,16,512]{3,2,1,0:T(8,128)(2,1)S(1)}, u32[]{:S(2)}) copy-start(bf16[1,16,16,512]{3,2,1,0:T(8,128)(2,1)S(1)} %collective-permute-done.2.refs_2_) | copy-start | bytes 786436
  15.5 29.3 %all-to-all-start = ((bf16[8,64,256]{2,1,0:T(8,128)(2,1)}), bf16[8,64,256]{2,1,0:T(8,128)(2,1)S(1)}, u32[]{:S(2)}, u32[]{:S(2)}) async-start(bf16[8,64,256]{2,1,0:T(8,128)(2,1)} %bitcast.2), calls=%async_computation | async-start | bytes 524288 | tf_op jit(solution)/shard_map/all_to_all | solution.py:413
  19.6 7.2 %collective-permute-start.3 = (bf16[1,16,16,512]{3,2,1,0:T(8,128)(2,1)S(1)}, bf16[1,16,16,512]{3,2,1,0:T(8,128)(2,1)S(1)}, u32[]{:S(2)}, u32[]{:S(2)}) collective-permute-start(bf16[1,16,16,512]{3,2,1,0:T(8,128)(2,1)S(1)} %collective-permute-done.1.refs_1_), channel_id=1, source_target_pairs={{0,2},{1,3},{2,0},{3,1},{4,6},{5,7},{6,4},{7,5},{8,10},{9,11},{10,... | collective-permute-start | bytes 786440 | tf_op jit(solution)/shard_map/ppermute | solution.py:19
  20.1 10.9 %collective-permute-start.5 = (bf16[1,16,16,512]{3,2,1,0:T(8,128)(2,1)}, bf16[1,16,16,512]{3,2,1,0:T(8,128)(2,1)S(1)}, u32[]{:S(2)}, u32[]{:S(2)}) collective-permute-start(bf16[1,16,16,512]{3,2,1,0:T(8,128)(2,1)} %refs_0_.2), channel_id=1, source_target_pairs={{0,24},{4,28},{8,0},{12,4},{16,8},{20,12},{24,16},{28,20},{1,25},{... | collective-permute-start | bytes 786440 | tf_op jit(solution)/shard_map/ppermute | solution.py:19
  24.0 7.1 %collective-permute-start.6 = (bf16[1,16,16,512]{3,2,1,0:T(8,128)(2,1)S(1)}, bf16[1,16,16,512]{3,2,1,0:T(8,128)(2,1)S(1)}, u32[]{:S(2)}, u32[]{:S(2)}) collective-permute-start(bf16[1,16,16,512]{3,2,1,0:T(8,128)(2,1)S(1)} %collective-permute-done.1.refs_1_), channel_id=1, source_target_pairs={{0,4},{4,0},{8,12},{12,8},{16,20},{20,16},{24,28},{28,24},{1,5},{5... | collective-permute-start | bytes 786440 | tf_op jit(solution)/shard_map/ppermute | solution.py:19
  26.7 17.4 %copy-start.33 = (f32[2,2,128,512]{3,2,1,0:T(8,128)}, f32[2,2,128,512]{3,2,1,0:T(8,128)S(1)}, u32[]{:S(2)}) copy-start(f32[2,2,128,512]{3,2,1,0:T(8,128)S(1)} %fusion.1) | copy-start | bytes 3145732
  26.7 17.3 %collective-permute-start.4 = (bf16[1,16,16,512]{3,2,1,0:T(8,128)(2,1)}, bf16[1,16,16,512]{3,2,1,0:T(8,128)(2,1)S(1)}, u32[]{:S(2)}, u32[]{:S(2)}) collective-permute-start(bf16[1,16,16,512]{3,2,1,0:T(8,128)(2,1)} %refs_0_.2), channel_id=1, source_target_pairs={{0,16},{4,20},{8,24},{12,28},{16,0},{20,4},{24,8},{28,12},{1,17},{... | collective-permute-start | bytes 786440 | tf_op jit(solution)/shard_map/ppermute | solution.py:19
  26.8 39.9 %copy-start.17 = (bf16[1,16,16,512]{3,2,1,0:T(8,128)(2,1)}, bf16[1,16,16,512]{3,2,1,0:T(8,128)(2,1)S(1)}, u32[]{:S(2)}) copy-start(bf16[1,16,16,512]{3,2,1,0:T(8,128)(2,1)S(1)} %collective-permute-done.3.refs_5_) | copy-start | bytes 786436
  31.0 35.6 %copy-start.11 = (bf16[1,16,16,512]{3,2,1,0:T(8,128)(2,1)}, bf16[1,16,16,512]{3,2,1,0:T(8,128)(2,1)S(1)}, u32[]{:S(2)}) copy-start(bf16[1,16,16,512]{3,2,1,0:T(8,128)(2,1)S(1)} %collective-permute-done.5.refs_0_) | copy-start | bytes 786436
  31.1 35.6 %copy-start.21 = (bf16[1,16,16,512]{3,2,1,0:T(8,128)(2,1)}, bf16[1,16,16,512]{3,2,1,0:T(8,128)(2,1)S(1)}, u32[]{:S(2)}) copy-start(bf16[1,16,16,512]{3,2,1,0:T(8,128)(2,1)S(1)} %collective-permute-done.6.refs_4_) | copy-start | bytes 786436
  31.1 13.0 %collective-permute-start.7 = (bf16[1,16,16,512]{3,2,1,0:T(8,128)(2,1)S(1)}, bf16[1,16,16,512]{3,2,1,0:T(8,128)(2,1)}, u32[]{:S(2)}, u32[]{:S(2)}) collective-permute-start(bf16[1,16,16,512]{3,2,1,0:T(8,128)(2,1)S(1)} %collective-permute-done.5.refs_0_), channel_id=1, source_target_pairs={{0,4},{4,0},{8,12},{12,8},{16,20},{20,16},{24,28},{28,24},{1,5},{5... | collective-permute-start | bytes 786440 | tf_op jit(solution)/shard_map/ppermute | solution.py:19
  32.5 11.5 %collective-permute-start.8 = (bf16[1,16,16,512]{3,2,1,0:T(8,128)(2,1)S(1)}, bf16[1,16,16,512]{3,2,1,0:T(8,128)(2,1)S(1)}, u32[]{:S(2)}, u32[]{:S(2)}) collective-permute-start(bf16[1,16,16,512]{3,2,1,0:T(8,128)(2,1)S(1)} %collective-permute-done.5.refs_0_), channel_id=1, source_target_pairs={{0,2},{1,3},{2,0},{3,1},{4,6},{5,7},{6,4},{7,5},{8,10},{9,11},{10,... | collective-permute-start | bytes 786440 | tf_op jit(solution)/shard_map/ppermute | solution.py:19
  34.9 24.3 %collective-permute-start.21 = (f32[2,128,512]{2,1,0:T(8,128)}, f32[2,128,512]{2,1,0:T(8,128)}, u32[]{:S(2)}, u32[]{:S(2)}) collective-permute-start(f32[2,128,512]{2,1,0:T(8,128)} %dynamic-slice_bitcast_fusion), channel_id=1, source_target_pairs={{0,1},{1,0},{2,3},{3,2},{4,5},{5,4},{6,7},{7,6},{8,9},{9,8},{10,11... | collective-permute-start | bytes 1572872 | tf_op jit(solution)/shard_map/ppermute | solution.py:19
  44.0 22.7 %copy-start.19 = (bf16[1,16,16,512]{3,2,1,0:T(8,128)(2,1)}, bf16[1,16,16,512]{3,2,1,0:T(8,128)(2,1)S(1)}, u32[]{:S(2)}) copy-start(bf16[1,16,16,512]{3,2,1,0:T(8,128)(2,1)S(1)} %collective-permute-done.4.refs_1_) | copy-start | bytes 786436
  44.8 9.2 %collective-permute-start.9 = (bf16[8,64,256]{2,1,0:T(8,128)(2,1)S(1)}, bf16[8,64,256]{2,1,0:T(8,128)(2,1)S(1)}, u32[]{:S(2)}, u32[]{:S(2)}) collective-permute-start(bf16[8,64,256]{2,1,0:T(8,128)(2,1)S(1)} %all-to-all-done.refs_8_), channel_id=1, source_target_pairs={{0,2},{1,3},{2,0},{3,1},{4,6},{5,7},{6,4},{7,5},{8,10},{9,11},{10,... | collective-permute-start | bytes 786440 | tf_op jit(solution)/shard_map/ppermute | solution.py:19
  45.4 8.6 %collective-permute-start.10 = (bf16[1,16,16,512]{3,2,1,0:T(8,128)(2,1)S(1)}, bf16[1,16,16,512]{3,2,1,0:T(8,128)(2,1)S(1)}, u32[]{:S(2)}, u32[]{:S(2)}) collective-permute-start(bf16[1,16,16,512]{3,2,1,0:T(8,128)(2,1)S(1)} %collective-permute-done.4.refs_1_), channel_id=1, source_target_pairs={{0,4},{4,0},{8,12},{12,8},{16,20},{20,16},{24,28},{28,24},{1,5},{5... | collective-permute-start | bytes 786440 | tf_op jit(solution)/shard_map/ppermute | solution.py:19
  46.9 10.3 %collective-permute-start.11 = (bf16[1,16,16,512]{3,2,1,0:T(8,128)(2,1)S(1)}, bf16[1,16,16,512]{3,2,1,0:T(8,128)(2,1)}, u32[]{:S(2)}, u32[]{:S(2)}) collective-permute-start(bf16[1,16,16,512]{3,2,1,0:T(8,128)(2,1)S(1)} %collective-permute-done.4.refs_1_), channel_id=1, source_target_pairs={{0,2},{1,3},{2,0},{3,1},{4,6},{5,7},{6,4},{7,5},{8,10},{9,11},{10,... | collective-permute-start | bytes 786440 | tf_op jit(solution)/shard_map/ppermute | solution.py:19
  48.3 12.3 %collective-permute-start.18 = (bf16[1,576,128]{2,1,0:T(8,128)(2,1)S(1)}, bf16[1,576,128]{2,1,0:T(8,128)(2,1)S(1)}, u32[]{:S(2)}, u32[]{:S(2)}) collective-permute-start(bf16[1,576,128]{2,1,0:T(8,128)(2,1)S(1)} %dynamic-slice_bitcast_fusion.2), channel_id=1, source_target_pairs={{0,8},{4,12},{8,0},{12,4},{16,24},{20,28},{24,16},{28,20},{1,9},{5... | collective-permute-start | bytes 442376 | tf_op jit(solution)/shard_map/ppermute | solution.py:19
  54.0 12.7 %copy-start.27 = (bf16[8,64,256]{2,1,0:T(8,128)(2,1)}, bf16[8,64,256]{2,1,0:T(8,128)(2,1)S(1)}, u32[]{:S(2)}) copy-start(bf16[8,64,256]{2,1,0:T(8,128)(2,1)S(1)} %collective-permute-done.9.refs_9_) | copy-start | bytes 786436
  54.0 12.7 %copy-start.29 = (bf16[1,16,16,512]{3,2,1,0:T(8,128)(2,1)}, bf16[1,16,16,512]{3,2,1,0:T(8,128)(2,1)S(1)}, u32[]{:S(2)}) copy-start(bf16[1,16,16,512]{3,2,1,0:T(8,128)(2,1)S(1)} %collective-permute-done.10.refs_4_) | copy-start | bytes 786436
  57.2 6.4 %collective-permute-start.12 = (bf16[1,16,16,512]{3,2,1,0:T(8,128)(2,1)S(1)}, bf16[1,16,16,512]{3,2,1,0:T(8,128)(2,1)S(1)}, u32[]{:S(2)}, u32[]{:S(2)}) collective-permute-start(bf16[1,16,16,512]{3,2,1,0:T(8,128)(2,1)S(1)} %collective-permute-done.3.refs_5_), channel_id=1, source_target_pairs={{0,4},{4,0},{8,12},{12,8},{16,20},{20,16},{24,28},{28,24},{1,5},{5... | collective-permute-start | bytes 786440 | tf_op jit(solution)/shard_map/ppermute | solution.py:19
  58.5 6.4 %collective-permute-start.13 = (bf16[1,16,16,512]{3,2,1,0:T(8,128)(2,1)S(1)}, bf16[1,16,16,512]{3,2,1,0:T(8,128)(2,1)S(1)}, u32[]{:S(2)}, u32[]{:S(2)}) collective-permute-start(bf16[1,16,16,512]{3,2,1,0:T(8,128)(2,1)S(1)} %collective-permute-done.2.refs_2_), channel_id=1, source_target_pairs={{0,2},{1,3},{2,0},{3,1},{4,6},{5,7},{6,4},{7,5},{8,10},{9,11},{10,... | collective-permute-start | bytes 786440 | tf_op jit(solution)/shard_map/ppermute | solution.py:19
  60.6 25.1 %collective-permute-start.19 = (bf16[2,576,128]{2,1,0:T(8,128)(2,1)S(1)}, bf16[2,576,128]{2,1,0:T(8,128)(2,1)S(1)}, u32[]{:S(2)}, u32[]{:S(2)}) collective-permute-start(bf16[2,576,128]{2,1,0:T(8,128)(2,1)S(1)} %pad_maximum_fusion.1), channel_id=1, source_target_pairs={{0,16},{4,20},{8,24},{12,28},{16,0},{20,4},{24,8},{28,12},{1,17},{... | collective-permute-start | bytes 884744 | tf_op jit(solution)/shard_map/ppermute | solution.py:19
  64.9 40.3 %collective-permute-start.14 = (bf16[1,16,16,512]{3,2,1,0:T(8,128)(2,1)}, bf16[1,16,16,512]{3,2,1,0:T(8,128)(2,1)S(1)}, u32[]{:S(2)}, u32[]{:S(2)}) collective-permute-start(bf16[1,16,16,512]{3,2,1,0:T(8,128)(2,1)} %refs_0_.2), channel_id=1, source_target_pairs={{0,1},{1,0},{2,3},{3,2},{4,5},{5,4},{6,7},{7,6},{8,9},{9,8},{10,11... | collective-permute-start | bytes 786440 | tf_op jit(solution)/shard_map/ppermute | solution.py:19
  64.9 20.9 %collective-permute-start.16 = (bf16[1,16,16,512]{3,2,1,0:T(8,128)(2,1)}, bf16[1,16,16,512]{3,2,1,0:T(8,128)(2,1)S(1)}, u32[]{:S(2)}, u32[]{:S(2)}) collective-permute-start(bf16[1,16,16,512]{3,2,1,0:T(8,128)(2,1)} %collective-permute-done.11.refs_5_), channel_id=1, source_target_pairs={{0,4},{4,0},{8,12},{12,8},{16,20},{20,16},{24,28},{28,24},{1,5},{5... | collective-permute-start | bytes 786440 | tf_op jit(solution)/shard_map/ppermute | solution.py:19
  65.6 20.3 %collective-permute-start.17 = (bf16[1,16,16,512]{3,2,1,0:T(8,128)(2,1)}, bf16[1,16,16,512]{3,2,1,0:T(8,128)(2,1)S(1)}, u32[]{:S(2)}, u32[]{:S(2)}) collective-permute-start(bf16[1,16,16,512]{3,2,1,0:T(8,128)(2,1)} %collective-permute-done.7.refs_2_), channel_id=1, source_target_pairs={{0,2},{1,3},{2,0},{3,1},{4,6},{5,7},{6,4},{7,5},{8,10},{9,11},{10,... | collective-permute-start | bytes 786440 | tf_op jit(solution)/shard_map/ppermute | solution.py:19
  66.7 20.5 %collective-permute-start.22 = (f32[128,512]{1,0:T(8,128)S(1)}, f32[128,512]{1,0:T(8,128)S(1)}, u32[]{:S(2)}, u32[]{:S(2)}) collective-permute-start(f32[128,512]{1,0:T(8,128)S(1)} %dynamic-slice_bitcast_fusion.1), channel_id=1, source_target_pairs={{0,2},{1,3},{2,0},{3,1},{4,6},{5,7},{6,4},{7,5},{8,10},{9,11},{10,... | collective-permute-start | bytes 786440 | tf_op jit(solution)/shard_map/ppermute | solution.py:19
  73.4 17.5 %copy-start.12 = (bf16[1,16,16,512]{3,2,1,0:T(8,128)(2,1)S(1)}, bf16[1,16,16,512]{3,2,1,0:T(8,128)(2,1)}, u32[]{:S(2)}) copy-start(bf16[1,16,16,512]{3,2,1,0:T(8,128)(2,1)} %copy-done.11) | copy-start | bytes 786436
  73.4 17.5 %copy-start.20 = (bf16[1,16,16,512]{3,2,1,0:T(8,128)(2,1)S(1)}, bf16[1,16,16,512]{3,2,1,0:T(8,128)(2,1)}, u32[]{:S(2)}) copy-start(bf16[1,16,16,512]{3,2,1,0:T(8,128)(2,1)} %copy-done.19) | copy-start | bytes 786436
  73.4 17.5 %copy-start.24 = (bf16[1,16,16,512]{3,2,1,0:T(8,128)(2,1)S(1)}, bf16[1,16,16,512]{3,2,1,0:T(8,128)(2,1)}, u32[]{:S(2)}) copy-start(bf16[1,16,16,512]{3,2,1,0:T(8,128)(2,1)} %copy-done.23) | copy-start | bytes 786436
  73.5 17.5 %copy-start.30 = (bf16[1,16,16,512]{3,2,1,0:T(8,128)(2,1)S(1)}, bf16[1,16,16,512]{3,2,1,0:T(8,128)(2,1)}, u32[]{:S(2)}) copy-start(bf16[1,16,16,512]{3,2,1,0:T(8,128)(2,1)} %copy-done.29) | copy-start | bytes 786436
  85.7 19.6 %collective-permute-start.15 = (bf16[1,16,16,512]{3,2,1,0:T(8,128)(2,1)S(1)}, bf16[1,16,16,512]{3,2,1,0:T(8,128)(2,1)S(1)}, u32[]{:S(2)}, u32[]{:S(2)}) collective-permute-start(bf16[1,16,16,512]{3,2,1,0:T(8,128)(2,1)S(1)} %copy-done.9), channel_id=1, source_target_pairs={{0,1},{1,0},{2,3},{3,2},{4,5},{5,4},{6,7},{7,6},{8,9},{9,8},{10,11... | collective-permute-start | bytes 786440 | tf_op jit(solution)/shard_map/ppermute | solution.py:19
  85.8 17.2 %copy-start.1 = (bf16[4,576,128]{2,1,0:T(8,128)(2,1)}, bf16[4,576,128]{2,1,0:T(8,128)(2,1)S(1)}, u32[]{:S(2)}) copy-start(bf16[4,576,128]{2,1,0:T(8,128)(2,1)S(1)} %pad_maximum_fusion.refs_4_) | copy-start | bytes 1769476
  85.8 20.2 %collective-permute-start.20 = (bf16[4,576,128]{2,1,0:T(8,128)(2,1)S(1)}, bf16[4,576,128]{2,1,0:T(8,128)(2,1)S(1)}, u32[]{:S(2)}, u32[]{:S(2)}) collective-permute-start(bf16[4,576,128]{2,1,0:T(8,128)(2,1)S(1)} %pad_maximum_fusion.refs_4_), channel_id=1, source_target_pairs={{0,4},{4,0},{8,12},{12,8},{16,20},{20,16},{24,28},{28,24},{1,5},{5... | collective-permute-start | bytes 1769480 | tf_op jit(solution)/shard_map/ppermute | solution.py:19
  87.3 17.2 %collective-permute-start.23 = (f32[128,512]{1,0:T(8,128)S(1)}, f32[128,512]{1,0:T(8,128)S(1)}, u32[]{:S(2)}, u32[]{:S(2)}) collective-permute-start(f32[128,512]{1,0:T(8,128)S(1)} %bitcast_add_fusion.2), channel_id=1, source_target_pairs={{0,8},{4,12},{8,0},{12,4},{16,24},{20,28},{24,16},{28,20},{1,9},{5... | collective-permute-start | bytes 786440 | tf_op jit(solution)/shard_map/ppermute | solution.py:19
  104.5 26.6 %copy-start.10 = (bf16[1,16,16,512]{3,2,1,0:T(8,128)(2,1)S(1)}, bf16[1,16,16,512]{3,2,1,0:T(8,128)(2,1)}, u32[]{:S(2)}) copy-start(bf16[1,16,16,512]{3,2,1,0:T(8,128)(2,1)} %copy-done.8) | copy-start | bytes 786436
  106.0 1.6 collective-permute-start.24
  109.7 21.4 %copy-start.2 = (bf16[4,576,128]{2,1,0:T(8,128)(2,1)S(1)}, bf16[4,576,128]{2,1,0:T(8,128)(2,1)}, u32[]{:S(2)}) copy-start(bf16[4,576,128]{2,1,0:T(8,128)(2,1)} %copy-done.1) | copy-start | bytes 1769476
  109.7 21.4 %copy-start.7 = (bf16[4,576,128]{2,1,0:T(8,128)(2,1)S(1)}, bf16[4,576,128]{2,1,0:T(8,128)(2,1)}, u32[]{:S(2)}) copy-start(bf16[4,576,128]{2,1,0:T(8,128)(2,1)} %copy-done.6) | copy-start | bytes 1769476
  109.7 21.4 %copy-start.26 = (bf16[1,16,16,512]{3,2,1,0:T(8,128)(2,1)S(1)}, bf16[1,16,16,512]{3,2,1,0:T(8,128)(2,1)}, u32[]{:S(2)}) copy-start(bf16[1,16,16,512]{3,2,1,0:T(8,128)(2,1)} %copy-done.25) | copy-start | bytes 786436
  109.7 21.4 %copy-start.32 = (bf16[1,16,16,512]{3,2,1,0:T(8,128)(2,1)S(1)}, bf16[1,16,16,512]{3,2,1,0:T(8,128)(2,1)}, u32[]{:S(2)}) copy-start(bf16[1,16,16,512]{3,2,1,0:T(8,128)(2,1)} %copy-done.31) | copy-start | bytes 786436
  110.9 9.0 %collective-permute-start.25 = (f16[64,1280]{1,0:T(8,128)(2,1)S(1)}, f16[64,1280]{1,0:T(8,128)(2,1)S(1)}, u32[]{:S(2)}, u32[]{:S(2)}) collective-permute-start(f16[64,1280]{1,0:T(8,128)(2,1)S(1)} %concatenate.3), channel_id=1, source_target_pairs={{0,8},{4,12},{8,16},{12,20},{16,24},{20,28},{24,0},{28,4},{1,9},{5... | collective-permute-start | bytes 491528 | tf_op jit(solution)/shard_map/ppermute | solution.py:19
  111.5 14.7 %collective-permute-start.31 = (f16[64,1280]{1,0:T(8,128)(2,1)S(1)}, f16[64,1280]{1,0:T(8,128)(2,1)S(1)}, u32[]{:S(2)}, u32[]{:S(2)}) collective-permute-start(f16[64,1280]{1,0:T(8,128)(2,1)S(1)} %concatenate.3), channel_id=1, source_target_pairs={{0,16},{4,20},{8,24},{12,28},{16,0},{20,4},{24,8},{28,12},{1,17},{... | collective-permute-start | bytes 491528 | tf_op jit(solution)/shard_map/ppermute | solution.py:19
  112.0 16.3 %collective-permute-start.33 = (f16[64,1280]{1,0:T(8,128)(2,1)S(1)}, f16[64,1280]{1,0:T(8,128)(2,1)S(1)}, u32[]{:S(2)}, u32[]{:S(2)}) collective-permute-start(f16[64,1280]{1,0:T(8,128)(2,1)S(1)} %concatenate.3), channel_id=1, source_target_pairs={{0,4},{4,0},{8,12},{12,8},{16,20},{20,16},{24,28},{28,24},{1,5},{5... | collective-permute-start | bytes 491528 | tf_op jit(solution)/shard_map/ppermute | solution.py:19
  114.0 15.0 %collective-permute-start.32 = (f16[64,1280]{1,0:T(8,128)(2,1)S(1)}, f16[64,1280]{1,0:T(8,128)(2,1)S(1)}, u32[]{:S(2)}, u32[]{:S(2)}) collective-permute-start(f16[64,1280]{1,0:T(8,128)(2,1)S(1)} %concatenate.3), channel_id=1, source_target_pairs={{0,24},{4,28},{8,0},{12,4},{16,8},{20,12},{24,16},{28,20},{1,25},{... | collective-permute-start | bytes 491528 | tf_op jit(solution)/shard_map/ppermute | solution.py:19
  116.8 22.1 %collective-permute-start.29 = (f32[576,1152]{1,0:T(8,128)}, f32[576,1152]{1,0:T(8,128)S(1)}, u32[]{:S(2)}, u32[]{:S(2)}) collective-permute-start(f32[576,1152]{1,0:T(8,128)} %copy-done.4), channel_id=1, source_target_pairs={{0,1},{1,0},{2,3},{3,2},{4,5},{5,4},{6,7},{7,6},{8,9},{9,8},{10,11... | collective-permute-start | bytes 7962632 | tf_op jit(solution)/shard_map/ppermute | solution.py:19
  119.9 18.9 %collective-permute-start.30 = (f32[128,512]{1,0:T(8,128)}, f32[128,512]{1,0:T(8,128)S(1)}, u32[]{:S(2)}, u32[]{:S(2)}) collective-permute-start(f32[128,512]{1,0:T(8,128)} %add.76), channel_id=1, source_target_pairs={{0,4},{4,0},{8,12},{12,8},{16,20},{20,16},{24,28},{28,24},{1,5},{5... | collective-permute-start | bytes 786440 | tf_op jit(solution)/shard_map/ppermute | solution.py:19
  126.3 11.9 %collective-permute-start.35 = (f16[64,1280]{1,0:T(8,128)(2,1)S(1)}, f16[64,1280]{1,0:T(8,128)(2,1)S(1)}, u32[]{:S(2)}, u32[]{:S(2)}) collective-permute-start(f16[64,1280]{1,0:T(8,128)(2,1)S(1)} %collective-permute-done.31), channel_id=1, source_target_pairs={{0,4},{4,0},{8,12},{12,8},{16,20},{20,16},{24,28},{28,24},{1,5},{5... | collective-permute-start | bytes 491528 | tf_op jit(solution)/shard_map/ppermute | solution.py:19
  128.3 10.0 %collective-permute-start.34 = (f16[64,1280]{1,0:T(8,128)(2,1)S(1)}, f16[64,1280]{1,0:T(8,128)(2,1)S(1)}, u32[]{:S(2)}, u32[]{:S(2)}) collective-permute-start(f16[64,1280]{1,0:T(8,128)(2,1)S(1)} %collective-permute-done.25), channel_id=1, source_target_pairs={{0,4},{4,0},{8,12},{12,8},{16,20},{20,16},{24,28},{28,24},{1,5},{5... | collective-permute-start | bytes 491528 | tf_op jit(solution)/shard_map/ppermute | solution.py:19
  129.0 9.1 %collective-permute-start.36 = (f16[64,1280]{1,0:T(8,128)(2,1)S(1)}, f16[64,1280]{1,0:T(8,128)(2,1)S(1)}, u32[]{:S(2)}, u32[]{:S(2)}) collective-permute-start(f16[64,1280]{1,0:T(8,128)(2,1)S(1)} %collective-permute-done.32), channel_id=1, source_target_pairs={{0,4},{4,0},{8,12},{12,8},{16,20},{20,16},{24,28},{28,24},{1,5},{5... | collective-permute-start | bytes 491528 | tf_op jit(solution)/shard_map/ppermute | solution.py:19
  131.2 7.6 %copy-start.35 = (f32[128,512]{1,0:T(8,128)S(1)}, f32[128,512]{1,0:T(8,128)}, u32[]{:S(2)}) copy-start(f32[128,512]{1,0:T(8,128)} %add.76) | copy-start | bytes 786436
  131.2 7.7 %copy-start.34 = (f32[1152,576]{0,1:T(8,128)S(1)}, f32[1152,576]{0,1:T(8,128)}, u32[]{:S(2)}) copy-start(f32[1152,576]{0,1:T(8,128)} %param.10) | copy-start | bytes 7962628
  141.9 21.0 %copy-start.36 = (f32[128,512]{1,0:T(8,128)S(1)}, f32[128,512]{1,0:T(8,128)}, u32[]{:S(2)}) copy-start(f32[128,512]{1,0:T(8,128)} %param.11) | copy-start | bytes 786436
  147.6 2.1 %collective-permute-start.37 = (f32[576,256]{1,0:T(8,128)S(1)}, f32[576,256]{1,0:T(8,128)S(1)}, u32[]{:S(2)}, u32[]{:S(2)}) collective-permute-start(f32[576,256]{1,0:T(8,128)S(1)} %get-tuple-element.102), channel_id=1, source_target_pairs={{0,1},{1,0},{2,3},{3,2},{4,5},{5,4},{6,7},{7,6},{8,9},{9,8},{10,11... | collective-permute-start | bytes 1769480 | tf_op jit(solution)/shard_map/ppermute | solution.py:19
  147.7 15.2 %collective-permute-start.38 = (f32[128,512]{1,0:T(8,128)S(1)}, f32[128,512]{1,0:T(8,128)S(1)}, u32[]{:S(2)}, u32[]{:S(2)}) collective-permute-start(f32[128,512]{1,0:T(8,128)S(1)} %add.80), channel_id=1, source_target_pairs={{0,16},{4,20},{8,24},{12,28},{16,0},{20,4},{24,8},{28,12},{1,17},{... | collective-permute-start | bytes 786440 | tf_op jit(solution)/shard_map/ppermute | solution.py:19
  149.8 14.7 %collective-permute-start.39 = (f32[576,128]{1,0:T(8,128)S(1)}, f32[576,128]{1,0:T(8,128)S(1)}, u32[]{:S(2)}, u32[]{:S(2)}) collective-permute-start(f32[576,128]{1,0:T(8,128)S(1)} %slice.83), channel_id=1, source_target_pairs={{0,2},{1,3},{2,0},{3,1},{4,6},{5,7},{6,4},{7,5},{8,10},{9,11},{10,... | collective-permute-start | bytes 884744 | tf_op jit(solution)/shard_map/ppermute | solution.py:19
  149.9 13.8 %collective-permute-start.26 = (bf16[1,16,16,128]{3,2,1,0:T(8,128)(2,1)S(1)}, bf16[1,16,16,128]{3,2,1,0:T(8,128)(2,1)S(1)}, u32[]{:S(2)}, u32[]{:S(2)}) collective-permute-start(bf16[1,16,16,128]{3,2,1,0:T(8,128)(2,1)S(1)} %get-tuple-element.93), channel_id=1, source_target_pairs={{0,2},{1,3},{2,0},{3,1},{4,6},{5,7},{6,4},{7,5},{8,10},{9,11},{10,... | collective-permute-start | bytes 196616 | tf_op jit(solution)/shard_map/ppermute | solution.py:19
  151.9 11.8 %collective-permute-start.27 = (bf16[1,16,16,128]{3,2,1,0:T(8,128)(2,1)S(1)}, bf16[1,16,16,128]{3,2,1,0:T(8,128)(2,1)S(1)}, u32[]{:S(2)}, u32[]{:S(2)}) collective-permute-start(bf16[1,16,16,128]{3,2,1,0:T(8,128)(2,1)S(1)} %get-tuple-element.94), channel_id=1, source_target_pairs={{0,1},{1,0},{2,3},{3,2},{4,5},{5,4},{6,7},{7,6},{8,9},{9,8},{10,11... | collective-permute-start | bytes 196616 | tf_op jit(solution)/shard_map/ppermute | solution.py:19
  151.9 11.8 %collective-permute-start.28 = (bf16[1,16,16,128]{3,2,1,0:T(8,128)(2,1)S(1)}, bf16[1,16,16,128]{3,2,1,0:T(8,128)(2,1)S(1)}, u32[]{:S(2)}, u32[]{:S(2)}) collective-permute-start(bf16[1,16,16,128]{3,2,1,0:T(8,128)(2,1)S(1)} %get-tuple-element.95), channel_id=1, source_target_pairs={{0,3},{1,2},{2,1},{3,0},{4,7},{5,6},{6,5},{7,4},{8,11},{9,10},{10,... | collective-permute-start | bytes 196616 | tf_op jit(solution)/shard_map/ppermute | solution.py:19
  (14 other events, 26.1 us)

commit v7 on v6

--- a/solution.py
+++ b/solution.py
@@ -132,29 +132,15 @@
         return jnp.dot(left[...], right, preferred_element_type=jnp.float32)
 
     def keep(whose, lane, count, value):
-        at = pl.ds(pl.multiple_of(lane, LANES), count * LANES)
+        at = slice(lane, lane + count * LANES)
         for kind, part in ((0, value[:cols]), (1, value[cols:])):
             if not first:
                 part = part + totals[2 * whose + kind][:, at]
             totals[2 * whose + kind][:, at] = part
 
-    half = tiles_per // 2
-    odd = tiles_per % 2
-
-    @pl.loop(0, half)
-    def _(step):
-        keep(0, step * 2 * LANES, 2, product(2 * step, 2))
-
-    if odd:
-        both = product(2 * half, 2)
-        keep(0, 2 * half * LANES, 1, both[:, :LANES])
-        keep(1, 0, 1, both[:, LANES:])
+    keep(0, 0, tiles_per, product(0, tiles_per))
     theirs_out = fetch(totals[:2], out_refs[:2], sems.at[3])
-
-    @pl.loop(0, half)
-    def _(step):
-        keep(1, (odd + 2 * step) * LANES, 2, product(tiles_per + odd + 2 * step, 2))
-
+    keep(1, 0, tiles_per, product(tiles_per, tiles_per))
     mine_out = fetch(totals[2:], out_refs[2:], sems.at[4])
     for copy in theirs_out + mine_out:
         copy.wait()
@@ -180,7 +166,7 @@
             pltpu.SemaphoreType.DMA((5, max(4, n_images))),
         ],
         input_output_aliases={} if before is None else {n_front + k: k for k in range(4)},
-        compiler_params=pltpu.CompilerParams(vmem_limit_bytes=26 * 1024 * 1024),
+        compiler_params=pltpu.CompilerParams(vmem_limit_bytes=58 * 1024 * 1024),
         cost_estimate=pl.CostEstimate(
             flops=4 * (cols + strip) * rows * n_images * spots,
             bytes_accessed=16 * (cols + strip) * rows,
@@ -310,7 +296,7 @@
             pltpu.VMEM((9 * channels, block), jnp.bfloat16),
             pltpu.SemaphoreType.DMA((2, n_images)),
         ],
-        compiler_params=pltpu.CompilerParams(vmem_limit_bytes=16 * 1024 * 1024),
+        compiler_params=pltpu.CompilerParams(vmem_limit_bytes=58 * 1024 * 1024),
         cost_estimate=pl.CostEstimate(
             flops=36 * n_images * side * side * channels * block,
             bytes_accessed=2 * (9 * channels * block + n_images * side * side * channels),
@@ -409,14 +395,14 @@
     strips_by_pair = []
     for at, now in enumerate(plan):
         if at == 1:
-            strips = after(own_cot, events[1]).T.reshape(n_fsdp, strip, own_cot.shape[0])
+            strips = after(own_cot, [maps["side", 0, 0]]).T.reshape(n_fsdp, strip, own_cot.shape[0])
             strips_by_pair.append(lax.all_to_all(strips, "fsdp", split_axis=0, concat_axis=0))
         if at == 3:
             strips = after(strips_by_pair[0], events[3])
             strips_by_pair += [over_pair(strips, step) for step in range(1, n_pair)]
             due += [(4, strips) for strips in strips_by_pair]
         sources = [activations if source is None else maps[source] for _, source, _, _ in now]
-        sources = after(sources, events[at])
+        sources = after(sources, events[max(at - 1, 0)])
         for array, (item, _, how, hops) in zip(sources, now):
             maps[item] = transfer(array, item, how)
             due.append((at + hops, maps[item]))
@@ -463,11 +449,11 @@
                 more.append(jnp.dot(cot_tile, row_tile, preferred_element_type=jnp.float32))
             totals = more if totals is None else [old + new for old, new in zip(totals, more)]
 
-    g_partial = by_rows(own_cot, own_cot).reshape(n_pair, 2, block, channels)
+    g_partial = by_rows(after(own_cot, events[2]), own_cot).reshape(n_pair, 2, block, channels)
     g_pairs = lax.dynamic_index_in_dim(g_partial, core_at, 1, keepdims=False) + over_core(
         lax.dynamic_index_in_dim(g_partial, 1 - core_at, 1, keepdims=False)
     )
-    g_pairs = after(g_pairs, events[last])
+    g_pairs = after(g_pairs, events[last - 1])
     g_sum = lax.dynamic_index_in_dim(g_pairs, pair_at, 0, keepdims=False)
     for step in range(1, n_pair):
         away = lax.dynamic_index_in_dim(g_pairs, (pair_at + step) % n_pair, 0, keepdims=False)
@@ -483,8 +469,11 @@
     near_stack = jnp.stack(near_parts)
     far_parts = over_side(after(near_stack, events[last + 1] + early))
 
-    g_sum = after(g_sum, events[last + 1] + early)
-    g_sum = g_sum + moved(g_sum, "fsdp", lambda to: to ^ 2)
+    distance = 2
+    while distance < n_fsdp:
+        g_sum = after(g_sum, events[last] if distance == 2 else events[last + 1] + early)
+        g_sum = g_sum + moved(g_sum, "fsdp", lambda to, d=distance: to ^ d)
+        distance *= 2
     near_images = [activations] + [maps["pair", 0, step] for step in range(1, n_pair)]
     group = near_images + [over_core(image) for image in after(near_images, events[last])]
     theirs = after(totals[1], [far_parts, g_sum] + group)
@@ -498,7 +487,11 @@
     exponent = jnp.full((strip, LANES), exponent, jnp.float16)
     packed = jnp.concatenate([packed, exponent], axis=1)
     near_packed = [packed] + [over_layer(packed, step) for step in range(1, n_layer)]
-    far_packed = [over_side(array) for array in near_packed]
+    far_packed, came = {0: over_side(packed)}, []
+    for step in sorted(range(1, n_layer), key=lambda step: min(step, n_layer - step)):
+        far_packed[step] = over_side(after(near_packed[step], came))
+        came = came + [near_packed[step]]
+    far_packed = [far_packed[step] for step in range(n_layer)]
     strips_of_grad = [
         array[:, :rows].astype(jnp.float32) * jnp.exp2(array[:, rows : rows + 1].astype(jnp.float32))
         for array in near_packed + far_packed
@@ -584,11 +577,6 @@
             stacked = lax.dynamic_update_index_in_dim(stacked, out, at, 0)
         conv_out = jnp.concatenate(jnp.split(stacked, n_factor), axis=4)[0]
 
-    distance = 4
-    while distance < n_fsdp:
-        g_sum = after(g_sum, strips_of_grad[:n_layer])
-        g_sum = g_sum + moved(g_sum, "fsdp", lambda to, d=distance: to ^ d)
-        distance *= 2
     g_factor_sum = g_sum
     g_factor = 0.5 * g_factor_old + 0.5 * g_factor_sum
     return (conv_out, a_factor, g_factor, natural_grad)

time: 166 us -> 163 us (0.982)
  waiting for transfers between devices: 49.6 us -> 59.3 us
  local copies, waits for them, and re-layouts: 13.8 us -> 4.77 us
  starting transfers between devices: 53.8 us -> 45.4 us
  other arithmetic: 9.59 us -> 12.7 us
    ppermute x40, waiting for transfers between devices: 49.6 us -> 59.3 us  [moved(): lax.ppermute(array, axis, [(at, target(at) % count) for at in range(count)])]
    unnamed x74 -> x56, local copies, waits for them, and re-layouts: 9.79 us -> 1.47 us
    ppermute x40, starting transfers between devices: 49.6 us -> 42 us  [moved(): lax.ppermute(array, axis, [(at, target(at) % count) for at in range(count)])]
    add x1, other arithmetic: 1.96 us -> 4.59 us  [per_device(): a_factor = 0.5 * a_factor_old + 0.5 / pixel_total * cov_own.T]
  transfers between devices with their start and end apart: 41 -> 41, of which waited for: 14 -> 14; matrix products, arithmetic and copies ran while one was open for 5% -> 6% of each run, Pallas kernels for 18% -> 19%
where the time goes in v7:
time: 163 us; the launch traced here: 162 us
  waiting for transfers between devices  59.3 us (36%)
  starting transfers between devices  45.4 us (28%)
  Pallas kernels  36.8 us (23%)
  other arithmetic  12.7 us (8%)
  local copies, waits for them, and re-layouts  4.77 us (3%)
  between operations  2.04 us (1%)
    ppermute x40, waiting for transfers between devices, moved(): lax.ppermute(array, axis, [(at, target(at) % count) for at in range(count)])  59.3 us
    ppermute x40, starting transfers between devices, moved(): lax.ppermute(array, axis, [(at, target(at) % count) for at in range(count)])  42 us
    pallas_call x2, Pallas kernels, add_products(): pl.pallas_call(lambda *refs: products_kernel(owners, pairs, len(strips),...  24.9 us
    pallas_call x1, Pallas kernels, tail_products(): pl.pallas_call(lambda *refs: tail_kernel(strip, block, layers, *refs), ou...  5.96 us
    pallas_call x1, Pallas kernels, convolve(): pl.pallas_call(lambda *refs: conv_kernel(n_images, *refs), out_shape=[jax...  5.17 us
    add x1, other arithmetic, per_device(): a_factor = 0.5 * a_factor_old + 0.5 / pixel_total * cov_own.T  4.59 us
    all_to_all x1, starting transfers between devices, per_device(): lax.all_to_all(strips, 'fsdp', split_axis=0, concat_axis=0)  3.41 us
  transfers between devices with their start and end apart: 41, of which 14 were waited for; matrix products, arithmetic and copies ran while one was open for 6% of the time, Pallas kernels for 19%

profile of v7, /device:TPU:0, one launch (start us, length us, event | category | flops | bytes accessed | tf_op | source)
XLA Modules:
  0.0 162.3 jit_solution(3909490071188285246)
XLA Ops:
  0.7 3.1 %collective-permute-start.1 = (bf16[1,16,16,512]{3,2,1,0:T(8,128)(2,1)}, bf16[1,16,16,512]{3,2,1,0:T(8,128)(2,1)S(1)}, u32[]{:S(2)}, u32[]{:S(2)}) collective-permute-start(bf16[1,16,16,512]{3,2,1,0:T(8,128)(2,1)} %refs_0_.2), channel_id=1, source_target_pairs={{0,8},{4,12},{8,16},{12,20},{16,24},{20,28},{24,0},{28,4},{1,9},{5... | collective-permute-start | bytes 786440 | tf_op jit(solution)/shard_map/ppermute | solution.py:19
  3.7 1.5 collective-permute-start.3
  5.2 7.1 %collective-permute-done.1.refs_1_ = bf16[1,16,16,512]{3,2,1,0:T(8,128)(2,1)S(1)} collective-permute-done((bf16[1,16,16,512]{3,2,1,0:T(8,128)(2,1)}, bf16[1,16,16,512]{3,2,1,0:T(8,128)(2,1)S(1)}, u32[]{:S(2)}, u32[]{:S(2)}) %collective-permute-start.1) | collective-permute-done | bytes 262176 | tf_op jit(solution)/shard_map/ppermute | solution.py:19
  12.3 1.5 collective-permute-start.2
  13.8 1.7 %collective-permute-start.5 = (bf16[1,16,16,512]{3,2,1,0:T(8,128)(2,1)}, bf16[1,16,16,512]{3,2,1,0:T(8,128)(2,1)S(1)}, u32[]{:S(2)}, u32[]{:S(2)}) collective-permute-start(bf16[1,16,16,512]{3,2,1,0:T(8,128)(2,1)} %refs_0_.2), channel_id=1, source_target_pairs={{0,24},{4,28},{8,0},{12,4},{16,8},{20,12},{24,16},{28,20},{1,25},{... | collective-permute-start | bytes 786440 | tf_op jit(solution)/shard_map/ppermute | solution.py:19
  15.5 1.5 collective-permute-start.12
  17.0 0.5 collective-permute-start
  17.5 1.9 %copy.17 = bf16[512,256]{1,0:T(8,128)(2,1)} copy(bf16[512,256]{0,1:T(8,128)(2,1)} %bitcast.23) | data formatting | bytes 524288 | tf_op jit(solution)/shard_map/transpose | solution.py:398
  19.4 3.4 %all-to-all-start = ((bf16[8,64,256]{2,1,0:T(8,128)(2,1)}), bf16[8,64,256]{2,1,0:T(8,128)(2,1)S(1)}, u32[]{:S(2)}, u32[]{:S(2)}) async-start(bf16[8,64,256]{2,1,0:T(8,128)(2,1)} %bitcast.2), calls=%async_computation | async-start | bytes 524288 | tf_op jit(solution)/shard_map/all_to_all | solution.py:399
  22.9 1.3 copy.18
  24.2 1.2 fusion.1
  25.6 2.9 %collective-permute-start.4 = (bf16[1,16,16,512]{3,2,1,0:T(8,128)(2,1)S(1)}, bf16[1,16,16,512]{3,2,1,0:T(8,128)(2,1)}, u32[]{:S(2)}, u32[]{:S(2)}) collective-permute-start(bf16[1,16,16,512]{3,2,1,0:T(8,128)(2,1)S(1)} %copy-done.9), channel_id=1, source_target_pairs={{0,16},{4,20},{8,24},{12,28},{16,0},{20,4},{24,8},{28,12},{1,17},{... | collective-permute-start | bytes 786440 | tf_op jit(solution)/shard_map/ppermute | solution.py:19
  28.5 1.5 collective-permute-start.6
  30.0 1.5 collective-permute-start.7
  31.5 10.3 %collective-permute-done.4.refs_1_ = bf16[1,16,16,512]{3,2,1,0:T(8,128)(2,1)} collective-permute-done((bf16[1,16,16,512]{3,2,1,0:T(8,128)(2,1)S(1)}, bf16[1,16,16,512]{3,2,1,0:T(8,128)(2,1)}, u32[]{:S(2)}, u32[]{:S(2)}) %collective-permute-start.4) | collective-permute-done | bytes 262176 | tf_op jit(solution)/shard_map/ppermute | solution.py:19
  41.8 1.5 collective-permute-start.13
  43.3 1.5 collective-permute-start.14
  44.8 0.6 collective-permute-start.15
  45.6 4.8 %collective-permute-done.13.refs_4_ = bf16[1,16,16,512]{3,2,1,0:T(8,128)(2,1)} collective-permute-done((bf16[1,16,16,512]{3,2,1,0:T(8,128)(2,1)}, bf16[1,16,16,512]{3,2,1,0:T(8,128)(2,1)}, u32[]{:S(2)}, u32[]{:S(2)}) %collective-permute-start.13) | collective-permute-done | bytes 262176 | tf_op jit(solution)/shard_map/ppermute | solution.py:19
  50.4 2.4 %collective-permute-done.14.refs_5_ = bf16[1,16,16,512]{3,2,1,0:T(8,128)(2,1)} collective-permute-done((bf16[1,16,16,512]{3,2,1,0:T(8,128)(2,1)}, bf16[1,16,16,512]{3,2,1,0:T(8,128)(2,1)}, u32[]{:S(2)}, u32[]{:S(2)}) %collective-permute-start.14) | collective-permute-done | bytes 262176 | tf_op jit(solution)/shard_map/ppermute | solution.py:19
  52.8 4.2 %collective-permute-done.15.refs_9_ = bf16[8,64,256]{2,1,0:T(8,128)(2,1)S(1)} collective-permute-done((bf16[8,64,256]{2,1,0:T(8,128)(2,1)S(1)}, bf16[8,64,256]{2,1,0:T(8,128)(2,1)S(1)}, u32[]{:S(2)}, u32[]{:S(2)}) %collective-permute-start.15) | collective-permute-done | bytes 262176 | tf_op jit(solution)/shard_map/ppermute | solution.py:19
  57.0 0.7 copy-done.20
  57.7 1.6 collective-permute-start.22
  59.3 0.7 collective-permute-start.8
  60.0 0.5 collective-permute-start.9
  60.6 1.4 collective-permute-start.16
  62.0 1.5 collective-permute-start.17
  63.5 3.6 %collective-permute-done.22 = f32[128,512]{1,0:T(8,128)S(1)} collective-permute-done((f32[128,512]{1,0:T(8,128)S(1)}, f32[128,512]{1,0:T(8,128)S(1)}, u32[]{:S(2)}, u32[]{:S(2)}) %collective-permute-start.22) | collective-permute-done | bytes 262176 | tf_op jit(solution)/shard_map/ppermute | solution.py:19
  67.1 1.7 %collective-permute-done.8.refs_6_ = bf16[1,16,16,512]{3,2,1,0:T(8,128)(2,1)S(1)} collective-permute-done((bf16[1,16,16,512]{3,2,1,0:T(8,128)(2,1)}, bf16[1,16,16,512]{3,2,1,0:T(8,128)(2,1)S(1)}, u32[]{:S(2)}, u32[]{:S(2)}) %collective-permute-start.8) | collective-permute-done | bytes 262176 | tf_op jit(solution)/shard_map/ppermute | solution.py:19
  68.8 3.9 %collective-permute-done.9.refs_7_ = bf16[1,16,16,512]{3,2,1,0:T(8,128)(2,1)S(1)} collective-permute-done((bf16[1,16,16,512]{3,2,1,0:T(8,128)(2,1)}, bf16[1,16,16,512]{3,2,1,0:T(8,128)(2,1)S(1)}, u32[]{:S(2)}, u32[]{:S(2)}) %collective-permute-start.9) | collective-permute-done | bytes 262176 | tf_op jit(solution)/shard_map/ppermute | solution.py:19
  72.7 0.6 copy-done.24
  73.4 12.5 %shard_map.102 = (f32[576,1152]{1,0:T(8,128)}, f32[64,1152]{1,0:T(8,128)}, f32[576,1152]{1,0:T(8,128)}, f32[64,1152]{1,0:T(8,128)}) custom-call(bf16[1,16,16,512]{3,2,1,0:T(8,128)(2,1)} %refs_0_.2, bf16[1,16,16,512]{3,2,1,0:T(8,128)(2,1)} %copy-done.14, bf16[1,16,16,512]{3,2,1,0:T(8,128)(2,1)} %copy-done.15, bf16[1,16,16,512]{3,2,1,0:T(8,128)(2,1)} %copy-done.11, ...), custom_call_target="tpu_custom_call" | custom-call | flops 6039797760 | bytes 11796480 | tf_op jit(solution)/shard_map/pallas_call | solution.py:155
  86.0 0.8 collective-permute-start.20
  86.8 0.5 collective-permute-start.11
  87.4 2.8 %collective-permute-start.24 = (f32[128,512]{1,0:T(8,128)S(1)}, f32[128,512]{1,0:T(8,128)S(1)}, u32[]{:S(2)}, u32[]{:S(2)}) collective-permute-start(f32[128,512]{1,0:T(8,128)S(1)} %add.76), channel_id=1, source_target_pairs={{0,16},{4,20},{8,24},{12,28},{16,0},{20,4},{24,8},{28,12},{1,17},{... | collective-permute-start | bytes 786440 | tf_op jit(solution)/shard_map/ppermute | solution.py:19
  90.2 12.4 %shard_map.103 = (f32[576,1152]{1,0:T(8,128)}, f32[64,1152]{1,0:T(8,128)}, f32[576,1152]{1,0:T(8,128)}, f32[64,1152]{1,0:T(8,128)}) custom-call(bf16[1,16,16,512]{3,2,1,0:T(8,128)(2,1)} %copy-done.13, bf16[1,16,16,512]{3,2,1,0:T(8,128)(2,1)} %collective-permute-done.4.refs_1_, ...), custom_call_target="tpu_custom_call", output_to_operand_aliasing={{0}: (10, {}), {1}: (11, {}), {2}: (12, {}), {3}: (13, {})} | custom-call | flops 6039797760 | bytes 11796480 | tf_op jit(solution)/shard_map/pallas_call | solution.py:155
  102.8 1.8 %collective-permute-done.25 = f32[64,1152]{1,0:T(8,128)S(1)} collective-permute-done((f32[64,1152]{1,0:T(8,128)}, f32[64,1152]{1,0:T(8,128)S(1)}, u32[]{:S(2)}, u32[]{:S(2)}) %collective-permute-start.25) | collective-permute-done | bytes 294944 | tf_op jit(solution)/shard_map/ppermute | solution.py:19
  104.5 1.6 abs_reduce_fusion
  107.0 2.6 %collective-permute-start.33 = (f16[64,1280]{1,0:T(8,128)(2,1)S(1)}, f16[64,1280]{1,0:T(8,128)(2,1)S(1)}, u32[]{:S(2)}, u32[]{:S(2)}) collective-permute-start(f16[64,1280]{1,0:T(8,128)(2,1)S(1)} %concatenate.3), channel_id=1, source_target_pairs={{0,24},{4,28},{8,0},{12,4},{16,8},{20,12},{24,16},{28,20},{1,25},{... | collective-permute-start | bytes 491528 | tf_op jit(solution)/shard_map/ppermute | solution.py:19
  109.6 0.6 collective-permute-start.32
  110.2 1.5 collective-permute-start.34
  111.7 2.5 %collective-permute-done.33 = f16[64,1280]{1,0:T(8,128)(2,1)S(1)} collective-permute-done((f16[64,1280]{1,0:T(8,128)(2,1)S(1)}, f16[64,1280]{1,0:T(8,128)(2,1)S(1)}, u32[]{:S(2)}, u32[]{:S(2)}) %collective-permute-start.33) | collective-permute-done | bytes 163872 | tf_op jit(solution)/shard_map/ppermute | solution.py:19
  114.2 4.4 %collective-permute-done.26 = f16[64,1280]{1,0:T(8,128)(2,1)S(1)} collective-permute-done((f16[64,1280]{1,0:T(8,128)(2,1)S(1)}, f16[64,1280]{1,0:T(8,128)(2,1)S(1)}, u32[]{:S(2)}, u32[]{:S(2)}) %collective-permute-start.26) | collective-permute-done | bytes 163872 | tf_op jit(solution)/shard_map/ppermute | solution.py:19
  118.6 1.5 collective-permute-start.37
  120.0 0.6 collective-permute-start.35
  120.7 3.3 %collective-permute-done.32 = f16[64,1280]{1,0:T(8,128)(2,1)S(1)} collective-permute-done((f16[64,1280]{1,0:T(8,128)(2,1)S(1)}, f16[64,1280]{1,0:T(8,128)(2,1)S(1)}, u32[]{:S(2)}, u32[]{:S(2)}) %collective-permute-start.32) | collective-permute-done | bytes 163872 | tf_op jit(solution)/shard_map/ppermute | solution.py:19
  124.1 1.5 collective-permute-start.36
  125.7 0.6 collective-permute-start.31
  126.9 5.2 %shard_map.104 = (bf16[1,16,16,128]{3,2,1,0:T(8,128)(2,1)}, bf16[1,16,16,128]{3,2,1,0:T(8,128)(2,1)}, bf16[1,16,16,128]{3,2,1,0:T(8,128)(2,1)}, bf16[1,16,16,128]{3,2,1,0:T(8,128)(2,1)}) custom-call(bf16[1,16,16,512]{3,2,1,0:T(8,128)(2,1)} %refs_0_.2, bf16[1,16,16,512]{3,2,1,0:T(8,128)(2,1)} %copy-done.11, bf16[1,16,16,512]{3,2,1,0:T(8,128)(2,1)} %copy-done.18, ...), custom_call_target="tpu_custom_call" | custom-call | flops 2415919104 | bytes 2228224 | tf_op jit(solution)/shard_map/pallas_call | solution.py:288
  132.1 0.8 exponential_reduce_fusion.1
  132.9 0.1 exponential_reduce_fusion
  133.1 0.8 exponential_reduce_fusion.2
  133.9 1.0 convert_multiply_fusion.1.refs_8_
  135.0 1.0 convert_multiply_fusion.2.refs_7_
  136.0 0.8 add_multiply_fusion
  136.8 4.6 %bitcast_add_fusion = f32[1152,576]{0,1:T(8,128)} fusion(f32[576,1152]{1,0:T(8,128)} %get-tuple-element.101, f32[576,1152]{1,0:T(8,128)} %collective-permute-done.30, f32[1152,576]{0,1:T(8,128)S(1)} %copy-done.4), kind=kLoop, calls=%fused_computation | loop fusion | flops 2654208 | bytes 10616832 | tf_op jit(solution)/shard_map/add | solution.py:500
  141.4 6.0 %shard_map.105 = (f32[576,256]{1,0:T(8,128)S(1)}, f32[576,256]{1,0:T(8,128)S(1)}) custom-call(f32[576,1152]{1,0:T(8,128)S(1)} %copy-done.2, f32[512,512]{1,0:T(8,128)S(1)} %copy-done.3, f32[64,1152]{1,0:T(8,128)S(1)} %get-tuple-element.116.refs_2_, f32[64,1152]{1,0:T(8,128)S(1)} %convert_multiply_fusion.6.refs_3_, ...), custom_call_target="tpu_custom_call" | custom-call | flops 2944401408 | bytes 3833856 | tf_op jit(solution)/shard_map/pallas_call | solution.py:232
  147.5 2.0 %collective-permute-done.38 = f32[576,256]{1,0:T(8,128)S(1)} collective-permute-done((f32[576,256]{1,0:T(8,128)S(1)}, f32[576,256]{1,0:T(8,128)S(1)}, u32[]{:S(2)}, u32[]{:S(2)}) %collective-permute-start.38) | collective-permute-done | bytes 589856 | tf_op jit(solution)/shard_map/ppermute | solution.py:19
  149.6 1.6 %collective-permute-start.39 = (f32[576,128]{1,0:T(8,128)S(1)}, f32[576,128]{1,0:T(8,128)S(1)}, u32[]{:S(2)}, u32[]{:S(2)}) collective-permute-start(f32[576,128]{1,0:T(8,128)S(1)} %slice.83), channel_id=1, source_target_pairs={{0,2},{1,3},{2,0},{3,1},{4,6},{5,7},{6,4},{7,5},{8,10},{9,11},{10,... | collective-permute-start | bytes 884744 | tf_op jit(solution)/shard_map/ppermute | solution.py:19
  151.2 0.5 collective-permute-start.27
  151.7 1.7 %collective-permute-start.29 = (bf16[1,16,16,128]{3,2,1,0:T(8,128)(2,1)S(1)}, bf16[1,16,16,128]{3,2,1,0:T(8,128)(2,1)S(1)}, u32[]{:S(2)}, u32[]{:S(2)}) collective-permute-start(bf16[1,16,16,128]{3,2,1,0:T(8,128)(2,1)S(1)} %copy-done.25), channel_id=1, source_target_pairs={{0,3},{1,2},{2,1},{3,0},{4,7},{5,6},{6,5},{7,4},{8,11},{9,10},{10,... | collective-permute-start | bytes 196616 | tf_op jit(solution)/shard_map/ppermute | solution.py:19
  153.4 7.4 %collective-permute-done.27.refs_1_ = bf16[1,16,16,128]{3,2,1,0:T(8,128)(2,1)S(1)} collective-permute-done((bf16[1,16,16,128]{3,2,1,0:T(8,128)(2,1)S(1)}, bf16[1,16,16,128]{3,2,1,0:T(8,128)(2,1)S(1)}, u32[]{:S(2)}, u32[]{:S(2)}) %collective-permute-start.27) | collective-permute-done | bytes 65568 | tf_op jit(solution)/shard_map/ppermute | solution.py:19
  160.8 0.8 shard_map.106
  161.6 0.7 fusion
  (113 shorter events, 2.0 us)
Async XLA Ops:
  0.6 44.8 %copy-start = (bf16[576,512]{1,0:T(8,128)(2,1)S(1)}, bf16[576,512]{1,0:T(8,128)(2,1)}, u32[]{:S(2)}) copy-start(bf16[576,512]{1,0:T(8,128)(2,1)} %param.9) | copy-start | bytes 1769476
  0.6 25.0 %copy-start.9 = (bf16[1,16,16,512]{3,2,1,0:T(8,128)(2,1)S(1)}, bf16[1,16,16,512]{3,2,1,0:T(8,128)(2,1)}, u32[]{:S(2)}) copy-start(bf16[1,16,16,512]{3,2,1,0:T(8,128)(2,1)} %refs_0_.2) | copy-start | bytes 786436
  0.7 11.6 %collective-permute-start.1 = (bf16[1,16,16,512]{3,2,1,0:T(8,128)(2,1)}, bf16[1,16,16,512]{3,2,1,0:T(8,128)(2,1)S(1)}, u32[]{:S(2)}, u32[]{:S(2)}) collective-permute-start(bf16[1,16,16,512]{3,2,1,0:T(8,128)(2,1)} %refs_0_.2), channel_id=1, source_target_pairs={{0,8},{4,12},{8,16},{12,20},{16,24},{20,28},{24,0},{28,4},{1,9},{5... | collective-permute-start | bytes 786440 | tf_op jit(solution)/shard_map/ppermute | solution.py:19
  3.7 13.8 %collective-permute-start.3 = (bf16[1,16,16,512]{3,2,1,0:T(8,128)(2,1)}, bf16[1,16,16,512]{3,2,1,0:T(8,128)(2,1)S(1)}, u32[]{:S(2)}, u32[]{:S(2)}) collective-permute-start(bf16[1,16,16,512]{3,2,1,0:T(8,128)(2,1)} %refs_0_.2), channel_id=1, source_target_pairs={{0,4},{4,0},{8,12},{12,8},{16,20},{20,16},{24,28},{28,24},{1,5},{5... | collective-permute-start | bytes 786440 | tf_op jit(solution)/shard_map/ppermute | solution.py:19
  12.3 11.9 %copy-start.14 = (bf16[1,16,16,512]{3,2,1,0:T(8,128)(2,1)}, bf16[1,16,16,512]{3,2,1,0:T(8,128)(2,1)S(1)}, u32[]{:S(2)}) copy-start(bf16[1,16,16,512]{3,2,1,0:T(8,128)(2,1)S(1)} %collective-permute-done.1.refs_1_) | copy-start | bytes 786436
  12.3 10.6 %collective-permute-start.2 = (bf16[1,16,16,512]{3,2,1,0:T(8,128)(2,1)S(1)}, bf16[1,16,16,512]{3,2,1,0:T(8,128)(2,1)S(1)}, u32[]{:S(2)}, u32[]{:S(2)}) collective-permute-start(bf16[1,16,16,512]{3,2,1,0:T(8,128)(2,1)S(1)} %collective-permute-done.1.refs_1_), channel_id=1, source_target_pairs={{0,2},{1,3},{2,0},{3,1},{4,6},{5,7},{6,4},{7,5},{8,10},{9,11},{10,... | collective-permute-start | bytes 786440 | tf_op jit(solution)/shard_map/ppermute | solution.py:19
  13.8 9.1 %collective-permute-start.5 = (bf16[1,16,16,512]{3,2,1,0:T(8,128)(2,1)}, bf16[1,16,16,512]{3,2,1,0:T(8,128)(2,1)S(1)}, u32[]{:S(2)}, u32[]{:S(2)}) collective-permute-start(bf16[1,16,16,512]{3,2,1,0:T(8,128)(2,1)} %refs_0_.2), channel_id=1, source_target_pairs={{0,24},{4,28},{8,0},{12,4},{16,8},{20,12},{24,16},{28,20},{1,25},{... | collective-permute-start | bytes 786440 | tf_op jit(solution)/shard_map/ppermute | solution.py:19
  15.5 7.4 %collective-permute-start.12 = (bf16[1,16,16,512]{3,2,1,0:T(8,128)(2,1)S(1)}, bf16[1,16,16,512]{3,2,1,0:T(8,128)(2,1)S(1)}, u32[]{:S(2)}, u32[]{:S(2)}) collective-permute-start(bf16[1,16,16,512]{3,2,1,0:T(8,128)(2,1)S(1)} %collective-permute-done.1.refs_1_), channel_id=1, source_target_pairs={{0,4},{4,0},{8,12},{12,8},{16,20},{20,16},{24,28},{28,24},{1,5},{5... | collective-permute-start | bytes 786440 | tf_op jit(solution)/shard_map/ppermute | solution.py:19
  17.0 11.5 %collective-permute-start = (bf16[1,16,16,512]{3,2,1,0:T(8,128)(2,1)}, bf16[1,16,16,512]{3,2,1,0:T(8,128)(2,1)S(1)}, u32[]{:S(2)}, u32[]{:S(2)}) collective-permute-start(bf16[1,16,16,512]{3,2,1,0:T(8,128)(2,1)} %refs_0_.2), channel_id=1, source_target_pairs={{0,2},{1,3},{2,0},{3,1},{4,6},{5,7},{6,4},{7,5},{8,10},{9,11},{10,... | collective-permute-start | bytes 786440 | tf_op jit(solution)/shard_map/ppermute | solution.py:19
  17.5 1.9 %copy-start.15 = (bf16[1,16,16,512]{3,2,1,0:T(8,128)(2,1)}, bf16[1,16,16,512]{3,2,1,0:T(8,128)(2,1)S(1)}, u32[]{:S(2)}) copy-start(bf16[1,16,16,512]{3,2,1,0:T(8,128)(2,1)S(1)} %collective-permute-done.3.refs_2_) | copy-start | bytes 786436
  19.4 25.4 %all-to-all-start = ((bf16[8,64,256]{2,1,0:T(8,128)(2,1)}), bf16[8,64,256]{2,1,0:T(8,128)(2,1)S(1)}, u32[]{:S(2)}, u32[]{:S(2)}) async-start(bf16[8,64,256]{2,1,0:T(8,128)(2,1)} %bitcast.2), calls=%async_computation | async-start | bytes 524288 | tf_op jit(solution)/shard_map/all_to_all | solution.py:399
  25.5 19.9 %collective-permute-start.21 = (f32[2,128,512]{2,1,0:T(8,128)S(1)}, f32[2,128,512]{2,1,0:T(8,128)S(1)}, u32[]{:S(2)}, u32[]{:S(2)}) collective-permute-start(f32[2,128,512]{2,1,0:T(8,128)S(1)} %dynamic-slice_bitcast_fusion), channel_id=1, source_target_pairs={{0,1},{1,0},{2,3},{3,2},{4,5},{5,4},{6,7},{7,6},{8,9},{9,8},{10,11... | collective-permute-start | bytes 1572872 | tf_op jit(solution)/shard_map/ppermute | solution.py:19
  25.6 16.2 %collective-permute-start.4 = (bf16[1,16,16,512]{3,2,1,0:T(8,128)(2,1)S(1)}, bf16[1,16,16,512]{3,2,1,0:T(8,128)(2,1)}, u32[]{:S(2)}, u32[]{:S(2)}) collective-permute-start(bf16[1,16,16,512]{3,2,1,0:T(8,128)(2,1)S(1)} %copy-done.9), channel_id=1, source_target_pairs={{0,16},{4,20},{8,24},{12,28},{16,0},{20,4},{24,8},{28,12},{1,17},{... | collective-permute-start | bytes 786440 | tf_op jit(solution)/shard_map/ppermute | solution.py:19
  28.5 16.3 %copy-start.11 = (bf16[1,16,16,512]{3,2,1,0:T(8,128)(2,1)}, bf16[1,16,16,512]{3,2,1,0:T(8,128)(2,1)S(1)}, u32[]{:S(2)}) copy-start(bf16[1,16,16,512]{3,2,1,0:T(8,128)(2,1)S(1)} %collective-permute-done.refs_3_.refs_1_) | copy-start | bytes 786436
  28.5 16.3 %collective-permute-start.6 = (bf16[1,16,16,512]{3,2,1,0:T(8,128)(2,1)}, bf16[1,16,16,512]{3,2,1,0:T(8,128)(2,1)}, u32[]{:S(2)}, u32[]{:S(2)}) collective-permute-start(bf16[1,16,16,512]{3,2,1,0:T(8,128)(2,1)} %copy-done.13), channel_id=1, source_target_pairs={{0,4},{4,0},{8,12},{12,8},{16,20},{20,16},{24,28},{28,24},{1,5},{5... | collective-permute-start | bytes 786440 | tf_op jit(solution)/shard_map/ppermute | solution.py:19
  30.0 14.8 %collective-permute-start.7 = (bf16[1,16,16,512]{3,2,1,0:T(8,128)(2,1)}, bf16[1,16,16,512]{3,2,1,0:T(8,128)(2,1)}, u32[]{:S(2)}, u32[]{:S(2)}) collective-permute-start(bf16[1,16,16,512]{3,2,1,0:T(8,128)(2,1)} %copy-done.13), channel_id=1, source_target_pairs={{0,2},{1,3},{2,0},{3,1},{4,6},{5,7},{6,4},{7,5},{8,10},{9,11},{10,... | collective-permute-start | bytes 786440 | tf_op jit(solution)/shard_map/ppermute | solution.py:19
  41.8 8.6 %collective-permute-start.13 = (bf16[1,16,16,512]{3,2,1,0:T(8,128)(2,1)}, bf16[1,16,16,512]{3,2,1,0:T(8,128)(2,1)}, u32[]{:S(2)}, u32[]{:S(2)}) collective-permute-start(bf16[1,16,16,512]{3,2,1,0:T(8,128)(2,1)} %collective-permute-done.4.refs_1_), channel_id=1, source_target_pairs={{0,4},{4,0},{8,12},{12,8},{16,20},{20,16},{24,28},{28,24},{1,5},{5... | collective-permute-start | bytes 786440 | tf_op jit(solution)/shard_map/ppermute | solution.py:19
  43.3 9.5 %collective-permute-start.14 = (bf16[1,16,16,512]{3,2,1,0:T(8,128)(2,1)}, bf16[1,16,16,512]{3,2,1,0:T(8,128)(2,1)}, u32[]{:S(2)}, u32[]{:S(2)}) collective-permute-start(bf16[1,16,16,512]{3,2,1,0:T(8,128)(2,1)} %collective-permute-done.4.refs_1_), channel_id=1, source_target_pairs={{0,2},{1,3},{2,0},{3,1},{4,6},{5,7},{6,4},{7,5},{8,10},{9,11},{10,... | collective-permute-start | bytes 786440 | tf_op jit(solution)/shard_map/ppermute | solution.py:19
  44.8 27.9 %copy-start.6 = (bf16[8,64,256]{2,1,0:T(8,128)(2,1)}, bf16[8,64,256]{2,1,0:T(8,128)(2,1)S(1)}, u32[]{:S(2)}) copy-start(bf16[8,64,256]{2,1,0:T(8,128)(2,1)S(1)} %all-to-all-done.refs_8_) | copy-start | bytes 786436
  44.8 12.2 %collective-permute-start.15 = (bf16[8,64,256]{2,1,0:T(8,128)(2,1)S(1)}, bf16[8,64,256]{2,1,0:T(8,128)(2,1)S(1)}, u32[]{:S(2)}, u32[]{:S(2)}) collective-permute-start(bf16[8,64,256]{2,1,0:T(8,128)(2,1)S(1)} %all-to-all-done.refs_8_), channel_id=1, source_target_pairs={{0,2},{1,3},{2,0},{3,1},{4,6},{5,7},{6,4},{7,5},{8,10},{9,11},{10,... | collective-permute-start | bytes 786440 | tf_op jit(solution)/shard_map/ppermute | solution.py:19
  45.4 15.1 %collective-permute-start.18 = (bf16[1,576,128]{2,1,0:T(8,128)(2,1)S(1)}, bf16[1,576,128]{2,1,0:T(8,128)(2,1)S(1)}, u32[]{:S(2)}, u32[]{:S(2)}) collective-permute-start(bf16[1,576,128]{2,1,0:T(8,128)(2,1)S(1)} %dynamic-slice_bitcast_fusion.2), channel_id=1, source_target_pairs={{0,8},{4,12},{8,0},{12,4},{16,24},{20,28},{24,16},{28,20},{1,9},{5... | collective-permute-start | bytes 442376 | tf_op jit(solution)/shard_map/ppermute | solution.py:19
  57.7 9.3 %collective-permute-start.22 = (f32[128,512]{1,0:T(8,128)S(1)}, f32[128,512]{1,0:T(8,128)S(1)}, u32[]{:S(2)}, u32[]{:S(2)}) collective-permute-start(f32[128,512]{1,0:T(8,128)S(1)} %dynamic-slice_bitcast_fusion.1), channel_id=1, source_target_pairs={{0,2},{1,3},{2,0},{3,1},{4,6},{5,7},{6,4},{7,5},{8,10},{9,11},{10,... | collective-permute-start | bytes 786440 | tf_op jit(solution)/shard_map/ppermute | solution.py:19
  59.3 9.5 %collective-permute-start.8 = (bf16[1,16,16,512]{3,2,1,0:T(8,128)(2,1)}, bf16[1,16,16,512]{3,2,1,0:T(8,128)(2,1)S(1)}, u32[]{:S(2)}, u32[]{:S(2)}) collective-permute-start(bf16[1,16,16,512]{3,2,1,0:T(8,128)(2,1)} %copy-done.16), channel_id=1, source_target_pairs={{0,4},{4,0},{8,12},{12,8},{16,20},{20,16},{24,28},{28,24},{1,5},{5... | collective-permute-start | bytes 786440 | tf_op jit(solution)/shard_map/ppermute | solution.py:19
  60.0 12.6 %collective-permute-start.9 = (bf16[1,16,16,512]{3,2,1,0:T(8,128)(2,1)}, bf16[1,16,16,512]{3,2,1,0:T(8,128)(2,1)S(1)}, u32[]{:S(2)}, u32[]{:S(2)}) collective-permute-start(bf16[1,16,16,512]{3,2,1,0:T(8,128)(2,1)} %copy-done.15), channel_id=1, source_target_pairs={{0,2},{1,3},{2,0},{3,1},{4,6},{5,7},{6,4},{7,5},{8,10},{9,11},{10,... | collective-permute-start | bytes 786440 | tf_op jit(solution)/shard_map/ppermute | solution.py:19
  60.6 25.5 %collective-permute-start.16 = (bf16[1,16,16,512]{3,2,1,0:T(8,128)(2,1)}, bf16[1,16,16,512]{3,2,1,0:T(8,128)(2,1)S(1)}, u32[]{:S(2)}, u32[]{:S(2)}) collective-permute-start(bf16[1,16,16,512]{3,2,1,0:T(8,128)(2,1)} %collective-permute-done.14.refs_5_), channel_id=1, source_target_pairs={{0,4},{4,0},{8,12},{12,8},{16,20},{20,16},{24,28},{28,24},{1,5},{5... | collective-permute-start | bytes 786440 | tf_op jit(solution)/shard_map/ppermute | solution.py:19
  62.0 24.1 %collective-permute-start.17 = (bf16[1,16,16,512]{3,2,1,0:T(8,128)(2,1)}, bf16[1,16,16,512]{3,2,1,0:T(8,128)(2,1)S(1)}, u32[]{:S(2)}, u32[]{:S(2)}) collective-permute-start(bf16[1,16,16,512]{3,2,1,0:T(8,128)(2,1)} %collective-permute-done.6.refs_2_), channel_id=1, source_target_pairs={{0,2},{1,3},{2,0},{3,1},{4,6},{5,7},{6,4},{7,5},{8,10},{9,11},{10,... | collective-permute-start | bytes 786440 | tf_op jit(solution)/shard_map/ppermute | solution.py:19
  67.0 18.9 %collective-permute-start.19 = (bf16[2,576,128]{2,1,0:T(8,128)(2,1)S(1)}, bf16[2,576,128]{2,1,0:T(8,128)(2,1)S(1)}, u32[]{:S(2)}, u32[]{:S(2)}) collective-permute-start(bf16[2,576,128]{2,1,0:T(8,128)(2,1)S(1)} %pad_maximum_fusion.1), channel_id=1, source_target_pairs={{0,16},{4,20},{8,24},{12,28},{16,0},{20,4},{24,8},{28,12},{1,17},{... | collective-permute-start | bytes 884744 | tf_op jit(solution)/shard_map/ppermute | solution.py:19
  67.1 19.7 %copy-start.10 = (bf16[1,16,16,512]{3,2,1,0:T(8,128)(2,1)S(1)}, bf16[1,16,16,512]{3,2,1,0:T(8,128)(2,1)}, u32[]{:S(2)}) copy-start(bf16[1,16,16,512]{3,2,1,0:T(8,128)(2,1)} %refs_0_.2) | copy-start | bytes 786436
  67.1 19.7 %copy-start.12 = (bf16[1,16,16,512]{3,2,1,0:T(8,128)(2,1)S(1)}, bf16[1,16,16,512]{3,2,1,0:T(8,128)(2,1)}, u32[]{:S(2)}) copy-start(bf16[1,16,16,512]{3,2,1,0:T(8,128)(2,1)} %copy-done.11) | copy-start | bytes 786436
  68.8 4.0 %copy-start.23 = (bf16[1,16,16,512]{3,2,1,0:T(8,128)(2,1)}, bf16[1,16,16,512]{3,2,1,0:T(8,128)(2,1)S(1)}, u32[]{:S(2)}) copy-start(bf16[1,16,16,512]{3,2,1,0:T(8,128)(2,1)S(1)} %collective-permute-done.8.refs_6_) | copy-start | bytes 786436
  72.7 14.7 %collective-permute-start.23 = (f32[128,512]{1,0:T(8,128)S(1)}, f32[128,512]{1,0:T(8,128)S(1)}, u32[]{:S(2)}, u32[]{:S(2)}) collective-permute-start(f32[128,512]{1,0:T(8,128)S(1)} %bitcast_add_fusion.2), channel_id=1, source_target_pairs={{0,8},{4,12},{8,0},{12,4},{16,24},{20,28},{24,16},{28,20},{1,9},{5... | collective-permute-start | bytes 786440 | tf_op jit(solution)/shard_map/ppermute | solution.py:19
  86.0 16.6 %copy-start.5 = (bf16[4,576,128]{2,1,0:T(8,128)(2,1)}, bf16[4,576,128]{2,1,0:T(8,128)(2,1)S(1)}, u32[]{:S(2)}) copy-start(bf16[4,576,128]{2,1,0:T(8,128)(2,1)S(1)} %pad_maximum_fusion.refs_4_) | copy-start | bytes 1769476
  86.0 4.1 %copy-start.21 = (bf16[1,16,16,512]{3,2,1,0:T(8,128)(2,1)}, bf16[1,16,16,512]{3,2,1,0:T(8,128)(2,1)S(1)}, u32[]{:S(2)}) copy-start(bf16[1,16,16,512]{3,2,1,0:T(8,128)(2,1)S(1)} %collective-permute-done.16.refs_6_) | copy-start | bytes 786436
  86.0 4.1 %copy-start.22 = (bf16[1,16,16,512]{3,2,1,0:T(8,128)(2,1)}, bf16[1,16,16,512]{3,2,1,0:T(8,128)(2,1)S(1)}, u32[]{:S(2)}) copy-start(bf16[1,16,16,512]{3,2,1,0:T(8,128)(2,1)S(1)} %collective-permute-done.17.refs_7_) | copy-start | bytes 786436
  86.0 16.6 %collective-permute-start.20 = (bf16[4,576,128]{2,1,0:T(8,128)(2,1)S(1)}, bf16[4,576,128]{2,1,0:T(8,128)(2,1)S(1)}, u32[]{:S(2)}, u32[]{:S(2)}) collective-permute-start(bf16[4,576,128]{2,1,0:T(8,128)(2,1)S(1)} %pad_maximum_fusion.refs_4_), channel_id=1, source_target_pairs={{0,4},{4,0},{8,12},{12,8},{16,20},{20,16},{24,28},{28,24},{1,5},{5... | collective-permute-start | bytes 1769480 | tf_op jit(solution)/shard_map/ppermute | solution.py:19
  86.8 15.8 %collective-permute-start.10 = (bf16[1,16,16,512]{3,2,1,0:T(8,128)(2,1)S(1)}, bf16[1,16,16,512]{3,2,1,0:T(8,128)(2,1)S(1)}, u32[]{:S(2)}, u32[]{:S(2)}) collective-permute-start(bf16[1,16,16,512]{3,2,1,0:T(8,128)(2,1)S(1)} %copy-done.10), channel_id=1, source_target_pairs={{0,1},{1,0},{2,3},{3,2},{4,5},{5,4},{6,7},{7,6},{8,9},{9,8},{10,11... | collective-permute-start | bytes 786440 | tf_op jit(solution)/shard_map/ppermute | solution.py:19
  86.8 15.8 %collective-permute-start.11 = (bf16[1,16,16,512]{3,2,1,0:T(8,128)(2,1)S(1)}, bf16[1,16,16,512]{3,2,1,0:T(8,128)(2,1)S(1)}, u32[]{:S(2)}, u32[]{:S(2)}) collective-permute-start(bf16[1,16,16,512]{3,2,1,0:T(8,128)(2,1)S(1)} %copy-done.12), channel_id=1, source_target_pairs={{0,1},{1,0},{2,3},{3,2},{4,5},{5,4},{6,7},{7,6},{8,9},{9,8},{10,11... | collective-permute-start | bytes 786440 | tf_op jit(solution)/shard_map/ppermute | solution.py:19
  87.4 15.2 %collective-permute-start.24 = (f32[128,512]{1,0:T(8,128)S(1)}, f32[128,512]{1,0:T(8,128)S(1)}, u32[]{:S(2)}, u32[]{:S(2)}) collective-permute-start(f32[128,512]{1,0:T(8,128)S(1)} %add.76), channel_id=1, source_target_pairs={{0,16},{4,20},{8,24},{12,28},{16,0},{20,4},{24,8},{28,12},{1,17},{... | collective-permute-start | bytes 786440 | tf_op jit(solution)/shard_map/ppermute | solution.py:19
  102.6 1.9 %copy-start.18 = (bf16[1,16,16,512]{3,2,1,0:T(8,128)(2,1)}, bf16[1,16,16,512]{3,2,1,0:T(8,128)(2,1)S(1)}, u32[]{:S(2)}) copy-start(bf16[1,16,16,512]{3,2,1,0:T(8,128)(2,1)S(1)} %collective-permute-done.10.refs_2_) | copy-start | bytes 786436
  102.7 1.9 %copy-start.19 = (bf16[1,16,16,512]{3,2,1,0:T(8,128)(2,1)}, bf16[1,16,16,512]{3,2,1,0:T(8,128)(2,1)S(1)}, u32[]{:S(2)}) copy-start(bf16[1,16,16,512]{3,2,1,0:T(8,128)(2,1)S(1)} %collective-permute-done.11.refs_3_) | copy-start | bytes 786436
  102.7 3.5 %copy-start.8 = (bf16[4,576,128]{2,1,0:T(8,128)(2,1)}, bf16[4,576,128]{2,1,0:T(8,128)(2,1)S(1)}, u32[]{:S(2)}) copy-start(bf16[4,576,128]{2,1,0:T(8,128)(2,1)S(1)} %collective-permute-done.20.refs_5_) | copy-start | bytes 1769476
  102.7 1.9 %collective-permute-start.25 = (f32[64,1152]{1,0:T(8,128)}, f32[64,1152]{1,0:T(8,128)S(1)}, u32[]{:S(2)}, u32[]{:S(2)}) collective-permute-start(f32[64,1152]{1,0:T(8,128)} %get-tuple-element.92), channel_id=1, source_target_pairs={{0,1},{1,0},{2,3},{3,2},{4,5},{5,4},{6,7},{7,6},{8,9},{9,8},{10,11... | collective-permute-start | bytes 884744 | tf_op jit(solution)/shard_map/ppermute | solution.py:19
  107.0 7.2 %collective-permute-start.33 = (f16[64,1280]{1,0:T(8,128)(2,1)S(1)}, f16[64,1280]{1,0:T(8,128)(2,1)S(1)}, u32[]{:S(2)}, u32[]{:S(2)}) collective-permute-start(f16[64,1280]{1,0:T(8,128)(2,1)S(1)} %concatenate.3), channel_id=1, source_target_pairs={{0,24},{4,28},{8,0},{12,4},{16,8},{20,12},{24,16},{28,20},{1,25},{... | collective-permute-start | bytes 491528 | tf_op jit(solution)/shard_map/ppermute | solution.py:19
  109.6 9.0 %collective-permute-start.26 = (f16[64,1280]{1,0:T(8,128)(2,1)S(1)}, f16[64,1280]{1,0:T(8,128)(2,1)S(1)}, u32[]{:S(2)}, u32[]{:S(2)}) collective-permute-start(f16[64,1280]{1,0:T(8,128)(2,1)S(1)} %concatenate.3), channel_id=1, source_target_pairs={{0,8},{4,12},{8,16},{12,20},{16,24},{20,28},{24,0},{28,4},{1,9},{5... | collective-permute-start | bytes 491528 | tf_op jit(solution)/shard_map/ppermute | solution.py:19
  109.6 14.4 %collective-permute-start.32 = (f16[64,1280]{1,0:T(8,128)(2,1)S(1)}, f16[64,1280]{1,0:T(8,128)(2,1)S(1)}, u32[]{:S(2)}, u32[]{:S(2)}) collective-permute-start(f16[64,1280]{1,0:T(8,128)(2,1)S(1)} %concatenate.3), channel_id=1, source_target_pairs={{0,16},{4,20},{8,24},{12,28},{16,0},{20,4},{24,8},{28,12},{1,17},{... | collective-permute-start | bytes 491528 | tf_op jit(solution)/shard_map/ppermute | solution.py:19
  110.2 15.5 %collective-permute-start.34 = (f16[64,1280]{1,0:T(8,128)(2,1)S(1)}, f16[64,1280]{1,0:T(8,128)(2,1)S(1)}, u32[]{:S(2)}, u32[]{:S(2)}) collective-permute-start(f16[64,1280]{1,0:T(8,128)(2,1)S(1)} %concatenate.3), channel_id=1, source_target_pairs={{0,4},{4,0},{8,12},{12,8},{16,20},{20,16},{24,28},{28,24},{1,5},{5... | collective-permute-start | bytes 491528 | tf_op jit(solution)/shard_map/ppermute | solution.py:19
  111.7 25.1 %collective-permute-start.30 = (f32[576,1152]{1,0:T(8,128)}, f32[576,1152]{1,0:T(8,128)}, u32[]{:S(2)}, u32[]{:S(2)}) collective-permute-start(f32[576,1152]{1,0:T(8,128)} %get-tuple-element.103), channel_id=1, source_target_pairs={{0,1},{1,0},{2,3},{3,2},{4,5},{5,4},{6,7},{7,6},{8,9},{9,8},{10,11... | collective-permute-start | bytes 7962632 | tf_op jit(solution)/shard_map/ppermute | solution.py:19
  118.6 14.4 %collective-permute-start.37 = (f16[64,1280]{1,0:T(8,128)(2,1)S(1)}, f16[64,1280]{1,0:T(8,128)(2,1)S(1)}, u32[]{:S(2)}, u32[]{:S(2)}) collective-permute-start(f16[64,1280]{1,0:T(8,128)(2,1)S(1)} %collective-permute-done.33), channel_id=1, source_target_pairs={{0,4},{4,0},{8,12},{12,8},{16,20},{20,16},{24,28},{28,24},{1,5},{5... | collective-permute-start | bytes 491528 | tf_op jit(solution)/shard_map/ppermute | solution.py:19
  120.0 13.0 %collective-permute-start.35 = (f16[64,1280]{1,0:T(8,128)(2,1)S(1)}, f16[64,1280]{1,0:T(8,128)(2,1)}, u32[]{:S(2)}, u32[]{:S(2)}) collective-permute-start(f16[64,1280]{1,0:T(8,128)(2,1)S(1)} %collective-permute-done.26), channel_id=1, source_target_pairs={{0,4},{4,0},{8,12},{12,8},{16,20},{20,16},{24,28},{28,24},{1,5},{5... | collective-permute-start | bytes 491528 | tf_op jit(solution)/shard_map/ppermute | solution.py:19
  124.1 8.0 %collective-permute-start.36 = (f16[64,1280]{1,0:T(8,128)(2,1)S(1)}, f16[64,1280]{1,0:T(8,128)(2,1)}, u32[]{:S(2)}, u32[]{:S(2)}) collective-permute-start(f16[64,1280]{1,0:T(8,128)(2,1)S(1)} %collective-permute-done.32), channel_id=1, source_target_pairs={{0,4},{4,0},{8,12},{12,8},{16,20},{20,16},{24,28},{28,24},{1,5},{5... | collective-permute-start | bytes 491528 | tf_op jit(solution)/shard_map/ppermute | solution.py:19
  125.7 10.3 %collective-permute-start.31 = (f32[128,512]{1,0:T(8,128)S(1)}, f32[128,512]{1,0:T(8,128)S(1)}, u32[]{:S(2)}, u32[]{:S(2)}) collective-permute-start(f32[128,512]{1,0:T(8,128)S(1)} %add.77), channel_id=1, source_target_pairs={{0,4},{4,0},{8,12},{12,8},{16,20},{20,16},{24,28},{28,24},{1,5},{5... | collective-permute-start | bytes 786440 | tf_op jit(solution)/shard_map/ppermute | solution.py:19
  126.9 9.1 %copy-start.7 = (f32[128,512]{1,0:T(8,128)S(1)}, f32[128,512]{1,0:T(8,128)}, u32[]{:S(2)}) copy-start(f32[128,512]{1,0:T(8,128)} %param.11) | copy-start | bytes 786436
  126.9 9.9 %copy-start.4 = (f32[1152,576]{0,1:T(8,128)S(1)}, f32[1152,576]{0,1:T(8,128)}, u32[]{:S(2)}) copy-start(f32[1152,576]{0,1:T(8,128)} %param.10) | copy-start | bytes 7962628
  136.8 4.6 %copy-start.2 = (f32[576,1152]{1,0:T(8,128)S(1)}, f32[576,1152]{1,0:T(8,128)}, u32[]{:S(2)}) copy-start(f32[576,1152]{1,0:T(8,128)} %refs_0_.3) | copy-start | bytes 7962628
  136.8 4.6 %copy-start.3 = (f32[512,512]{1,0:T(8,128)S(1)}, f32[512,512]{1,0:T(8,128)}, u32[]{:S(2)}) copy-start(f32[512,512]{1,0:T(8,128)} %refs_1_.1) | copy-start | bytes 3145732
  141.4 9.8 %copy-start.27 = (bf16[1,16,16,128]{3,2,1,0:T(8,128)(2,1)S(1)}, bf16[1,16,16,128]{3,2,1,0:T(8,128)(2,1)}, u32[]{:S(2)}) copy-start(bf16[1,16,16,128]{3,2,1,0:T(8,128)(2,1)} %get-tuple-element.98) | copy-start | bytes 196612
  141.4 10.3 %copy-start.26 = (bf16[1,16,16,128]{3,2,1,0:T(8,128)(2,1)S(1)}, bf16[1,16,16,128]{3,2,1,0:T(8,128)(2,1)}, u32[]{:S(2)}) copy-start(bf16[1,16,16,128]{3,2,1,0:T(8,128)(2,1)} %get-tuple-element.99) | copy-start | bytes 196612
  141.4 10.3 %copy-start.25 = (bf16[1,16,16,128]{3,2,1,0:T(8,128)(2,1)S(1)}, bf16[1,16,16,128]{3,2,1,0:T(8,128)(2,1)}, u32[]{:S(2)}) copy-start(bf16[1,16,16,128]{3,2,1,0:T(8,128)(2,1)} %get-tuple-element.100) | copy-start | bytes 196612
  141.4 19.4 %copy-start.1 = (bf16[1,16,16,128]{3,2,1,0:T(8,128)(2,1)S(1)}, bf16[1,16,16,128]{3,2,1,0:T(8,128)(2,1)}, u32[]{:S(2)}) copy-start(bf16[1,16,16,128]{3,2,1,0:T(8,128)(2,1)} %get-tuple-element.110.refs_0_) | copy-start | bytes 196612
  147.4 2.1 %collective-permute-start.38 = (f32[576,256]{1,0:T(8,128)S(1)}, f32[576,256]{1,0:T(8,128)S(1)}, u32[]{:S(2)}, u32[]{:S(2)}) collective-permute-start(f32[576,256]{1,0:T(8,128)S(1)} %get-tuple-element.109), channel_id=1, source_target_pairs={{0,1},{1,0},{2,3},{3,2},{4,5},{5,4},{6,7},{7,6},{8,9},{9,8},{10,11... | collective-permute-start | bytes 1769480 | tf_op jit(solution)/shard_map/ppermute | solution.py:19
  149.6 12.0 %collective-permute-start.39 = (f32[576,128]{1,0:T(8,128)S(1)}, f32[576,128]{1,0:T(8,128)S(1)}, u32[]{:S(2)}, u32[]{:S(2)}) collective-permute-start(f32[576,128]{1,0:T(8,128)S(1)} %slice.83), channel_id=1, source_target_pairs={{0,2},{1,3},{2,0},{3,1},{4,6},{5,7},{6,4},{7,5},{8,10},{9,11},{10,... | collective-permute-start | bytes 884744 | tf_op jit(solution)/shard_map/ppermute | solution.py:19
  151.2 9.6 %collective-permute-start.27 = (bf16[1,16,16,128]{3,2,1,0:T(8,128)(2,1)S(1)}, bf16[1,16,16,128]{3,2,1,0:T(8,128)(2,1)S(1)}, u32[]{:S(2)}, u32[]{:S(2)}) collective-permute-start(bf16[1,16,16,128]{3,2,1,0:T(8,128)(2,1)S(1)} %copy-done.27), channel_id=1, source_target_pairs={{0,2},{1,3},{2,0},{3,1},{4,6},{5,7},{6,4},{7,5},{8,10},{9,11},{10,... | collective-permute-start | bytes 196616 | tf_op jit(solution)/shard_map/ppermute | solution.py:19
  151.7 9.1 %collective-permute-start.28 = (bf16[1,16,16,128]{3,2,1,0:T(8,128)(2,1)S(1)}, bf16[1,16,16,128]{3,2,1,0:T(8,128)(2,1)S(1)}, u32[]{:S(2)}, u32[]{:S(2)}) collective-permute-start(bf16[1,16,16,128]{3,2,1,0:T(8,128)(2,1)S(1)} %copy-done.26), channel_id=1, source_target_pairs={{0,1},{1,0},{2,3},{3,2},{4,5},{5,4},{6,7},{7,6},{8,9},{9,8},{10,11... | collective-permute-start | bytes 196616 | tf_op jit(solution)/shard_map/ppermute | solution.py:19
  151.7 9.1 %collective-permute-start.29 = (bf16[1,16,16,128]{3,2,1,0:T(8,128)(2,1)S(1)}, bf16[1,16,16,128]{3,2,1,0:T(8,128)(2,1)S(1)}, u32[]{:S(2)}, u32[]{:S(2)}) collective-permute-start(bf16[1,16,16,128]{3,2,1,0:T(8,128)(2,1)S(1)} %copy-done.25), channel_id=1, source_target_pairs={{0,3},{1,2},{2,1},{3,0},{4,7},{5,6},{6,5},{7,4},{8,11},{9,10},{10,... | collective-permute-start | bytes 196616 | tf_op jit(solution)/shard_map/ppermute | solution.py:19
  (5 other events, 5.5 us)

commit v8 on v7

--- a/solution.py
+++ b/solution.py
@@ -137,6 +137,8 @@
             if not first:
                 part = part + totals[2 * whose + kind][:, at]
             totals[2 * whose + kind][:, at] = part
+        grads = totals[2 * whose + 1]
+        grads[:, rows:] = jnp.full((strip, LANES), jnp.max(jnp.abs(grads[:, :rows])))
 
     keep(0, 0, tiles_per, product(0, tiles_per))
     theirs_out = fetch(totals[:2], out_refs[:2], sems.at[3])
@@ -149,7 +151,7 @@
 def add_products(owners, images, pairs, strips, before, cols, rows):
     n_images, side, channels, strip = len(images), images[0].shape[1], images[0].shape[3], strips[0].shape[1]
     spots = side * side
-    shapes = [(height, rows) for height in (cols, strip)] * 2
+    shapes = [(cols, rows), (strip, rows + LANES)] * 2
     operands = [*images, *strips, *(before or [])]
     n_front = n_images + len(strips)
     return pl.pallas_call(
@@ -327,33 +329,34 @@
 
 def gather_plan(n_layer, n_pair):
     far_layers = sorted(range(1, n_layer), key=lambda step: min(step, n_layer - step))
-    by_side, by_pair = [], []
+    waiting = {"layer": [(("layer", layer, 0), None) for layer in far_layers], "side": [], "pair": []}
     for turn, layer in enumerate([0] + far_layers):
-        by_side.append((("side", layer, 0), ("layer", layer, 0)))
+        waiting["side"].append((("side", layer, 0), ("layer", layer, 0)))
         for pair in range(1, n_pair):
-            by_pair.append((("pair", layer, pair), ("layer", layer, 0)))
+            waiting["pair"].append((("pair", layer, pair), ("layer", layer, 0)))
             if turn % 2 == 0:
-                by_pair.append((("both", layer, pair), ("side", layer, 0)))
+                waiting["pair"].append((("both", layer, pair), ("side", layer, 0)))
             else:
-                by_side.append((("both", layer, pair), ("pair", layer, pair)))
-    by_layer = [(("layer", layer, 0), None) for layer in far_layers]
-    for link in (by_side, by_pair):
-        link.sort(key=lambda item: item[0][0] == "both")
-    here, due, rounds = {None, ("layer", 0, 0)}, {}, []
-    while by_layer or by_side or by_pair:
-        here |= {item for item, when in due.items() if when <= len(rounds)}
-        due = {item: when for item, when in due.items() if when > len(rounds)}
-        now = []
-        for link in (by_layer, by_side, by_pair):
-            free = [item for item in link if item[1] in here]
-            for chosen in free[: 2 if link is by_layer and rounds else 1]:
-                link.remove(chosen)
-                item, source = chosen
-                hops = min(item[1], n_layer - item[1]) if item[0] == "layer" else 1
-                due[item] = len(rounds) + hops
-                now.append((item, source, "pair" if link is by_pair else item[0], hops))
-        rounds.append(now)
-    return rounds
+                waiting["side"].append((("both", layer, pair), ("pair", layer, pair)))
+    for link in waiting.values():
+        link.sort(key=lambda entry: entry[0][0] == "both")
+    ready, busy, turns = {None: 0, ("layer", 0, 0): 0}, {link: 0 for link in waiting}, {}
+    order, step = [], 0
+    while any(waiting.values()):
+        for link, entries in waiting.items():
+            free = [entry for entry in entries if ready.get(entry[1], step + 1) <= step]
+            if busy[link] > step or not free:
+                continue
+            count = 2 if link == "layer" and step == 0 else 1
+            for item, source in free[:count]:
+                entries.remove((item, source))
+                hops = min(item[1], n_layer - item[1]) if link == "layer" else 1
+                busy[link] = step + hops * count
+                ready[item] = busy[link]
+                turns[link] = turns.get(link, -1) + 1
+                order.append((item, source, link, turns[link]))
+        step += 1
+    return order, ready
 
 
 def per_device(activations, cotangent, weight, a_factor_old, g_factor_old, a_inverse, g_inverse):
@@ -390,33 +393,28 @@
 
     own_cot = cotangent.reshape(-1, channels)
     maps = {("layer", 0, 0): activations}
-    plan = gather_plan(n_layer, n_pair)
-    events, due = [[]], []
+    plan, ready = gather_plan(n_layer, n_pair)
+    sent = {"layer": [], "side": [], "pair": []}
     strips_by_pair = []
-    for at, now in enumerate(plan):
-        if at == 1:
-            strips = after(own_cot, [maps["side", 0, 0]]).T.reshape(n_fsdp, strip, own_cot.shape[0])
-            strips_by_pair.append(lax.all_to_all(strips, "fsdp", split_axis=0, concat_axis=0))
-        if at == 3:
-            strips = after(strips_by_pair[0], events[3])
-            strips_by_pair += [over_pair(strips, step) for step in range(1, n_pair)]
-            due += [(4, strips) for strips in strips_by_pair]
-        sources = [activations if source is None else maps[source] for _, source, _, _ in now]
-        sources = after(sources, events[max(at - 1, 0)])
-        for array, (item, _, how, hops) in zip(sources, now):
-            maps[item] = transfer(array, item, how)
-            due.append((at + hops, maps[item]))
-        events.append([array for when, array in due if when == at + 1])
-    last = len(plan) - 1
+    for item, source, link, turn in plan:
+        array = activations if source is None else maps[source]
+        events = sent[link][max(turn - 2, 0) : turn - 1]
+        if link == "pair" and item == [entry[0] for entry in plan if entry[2] == "pair"][-1]:
+            events = events + strips_by_pair
+        maps[item] = transfer(after(array, events), item, link)
+        sent[link].append(maps[item])
+        if link == "side" and turn == 0:
+            strips = after(own_cot, [maps[item]]).T.reshape(n_fsdp, strip, own_cot.shape[0])
+            strips = lax.all_to_all(strips, "fsdp", split_axis=0, concat_axis=0)
+        if link == "pair" and turn == 2:
+            strips_by_pair = [strips] + [
+                over_pair(after(strips, [maps[item]]), step) for step in range(1, n_pair)
+            ]
+    first_event, last_layer = sent["side"][:1], sent["layer"][-1:]
+    near_end, at_end = sent["pair"][-2:-1], sent["pair"][-1:] + sent["side"][-1:]
 
     aligned = rows % LANES == 0 and channels % LANES == 0 and activations.shape[0] == 1
-    arrived = {("layer", 0, 0): 0}
-    for at, now in enumerate(plan):
-        arrived.update({item: at + hops for item, _, _, hops in now})
-    images = sorted(maps, key=lambda item: arrived[item])
-    images.sort(
-        key=lambda item: max(when for other, when in arrived.items() if other[1] == item[1])
-    )
+    images = sorted(maps, key=lambda item: ready[item])
     half = len(images) // 2
     totals, early = None, []
     for batch in (images[:half], images[half:]):
@@ -448,73 +446,60 @@
                 more.append(by_rows(col_tile, row_tile))
                 more.append(jnp.dot(cot_tile, row_tile, preferred_element_type=jnp.float32))
             totals = more if totals is None else [old + new for old, new in zip(totals, more)]
-
-    g_partial = by_rows(after(own_cot, events[2]), own_cot).reshape(n_pair, 2, block, channels)
+    if not aligned:
+        for at in (1, 3):
+            largest = jnp.full((strip, LANES), jnp.max(jnp.abs(totals[at])))
+            totals[at] = jnp.concatenate([totals[at], largest], axis=1)
+
+    g_partial = by_rows(after(own_cot, first_event), own_cot).reshape(n_pair, 2, block, channels)
     g_pairs = lax.dynamic_index_in_dim(g_partial, core_at, 1, keepdims=False) + over_core(
         lax.dynamic_index_in_dim(g_partial, 1 - core_at, 1, keepdims=False)
     )
-    g_pairs = after(g_pairs, events[last - 1])
+    g_pairs = after(g_pairs, near_end)
     g_sum = lax.dynamic_index_in_dim(g_pairs, pair_at, 0, keepdims=False)
     for step in range(1, n_pair):
         away = lax.dynamic_index_in_dim(g_pairs, (pair_at + step) % n_pair, 0, keepdims=False)
         g_sum = g_sum + over_pair(away, step)
-    weight_part = after(weight, events[1])
+    weight_part = after(weight, last_layer)
     near_parts = [lax.dynamic_slice_in_dim(weight_part, factor_at * block, block, 1)]
-    distance, at = 2, 2
-    while distance < n_fsdp:
-        both = after(jnp.stack(near_parts), events[min(at, last)])
-        both = moved(both, "fsdp", lambda to, d=distance: to ^ d)
-        near_parts = near_parts + [both[k] for k in range(len(near_parts))]
-        distance, at = 2 * distance, at + 2
-    near_stack = jnp.stack(near_parts)
-    far_parts = over_side(after(near_stack, events[last + 1] + early))
-
     distance = 2
     while distance < n_fsdp:
-        g_sum = after(g_sum, events[last] if distance == 2 else events[last + 1] + early)
+        both = moved(jnp.stack(near_parts), "fsdp", lambda to, d=distance: to ^ d)
+        near_parts = near_parts + [both[k] for k in range(len(near_parts))]
+        distance *= 2
+    near_stack = jnp.stack(near_parts)
+    far_parts = over_side(after(near_stack, at_end + early))
+    distance = n_fsdp // 2
+    g_sum = after(g_sum, at_end + early)
+    while distance > 2:
         g_sum = g_sum + moved(g_sum, "fsdp", lambda to, d=distance: to ^ d)
-        distance *= 2
+        distance //= 2
     near_images = [activations] + [maps["pair", 0, step] for step in range(1, n_pair)]
-    group = near_images + [over_core(image) for image in after(near_images, events[last])]
+    group = near_images + [over_core(image) for image in after(near_images, near_end)]
     theirs = after(totals[1], [far_parts, g_sum] + group)
-    grad_own = totals[3] + over_core(theirs)
+    theirs = over_core(theirs)
     pixel_total = float(
         activations.shape[0] * activations.shape[1] * activations.shape[2] * n_fsdp * n_factor
     )
 
-    exponent = jnp.floor(jnp.log2(jnp.maximum(jnp.max(jnp.abs(grad_own)), 1e-30))) - 14.0
-    packed = (grad_own * jnp.exp2(-exponent)).astype(jnp.float16)
-    exponent = jnp.full((strip, LANES), exponent, jnp.float16)
+    largest = totals[3][:, rows : rows + 1] + theirs[:, rows : rows + 1]
+    exponent = jnp.floor(jnp.log2(jnp.maximum(largest, 1e-30))) - 14.0
+    packed = ((totals[3] + theirs)[:, :rows] * jnp.exp2(-exponent)).astype(jnp.float16)
+    exponent = jnp.broadcast_to(exponent.astype(jnp.float16), (strip, LANES))
     packed = jnp.concatenate([packed, exponent], axis=1)
     near_packed = [packed] + [over_layer(packed, step) for step in range(1, n_layer)]
-    far_packed, came = {0: over_side(packed)}, []
-    for step in sorted(range(1, n_layer), key=lambda step: min(step, n_layer - step)):
-        far_packed[step] = over_side(after(near_packed[step], came))
-        came = came + [near_packed[step]]
-    far_packed = [far_packed[step] for step in range(n_layer)]
-    strips_of_grad = [
-        array[:, :rows].astype(jnp.float32) * jnp.exp2(array[:, rows : rows + 1].astype(jnp.float32))
-        for array in near_packed + far_packed
-    ]
-    cov_own = totals[2] + over_core(after(totals[0], [packed]))
-    a_factor = 0.5 * a_factor_old + (0.5 / pixel_total) * cov_own.T
-    came_from = [(fsdp_at - 2 * step) % n_fsdp for step in range(n_layer)]
-    came_from = came_from + [at ^ 1 for at in came_from]
-    order = [
-        2 * ((pair_at + step) % n_pair) + (core_at + other) % 2
-        for other in (1, 0)
-        for step in range(n_pair)
-    ]
-    g_sum = after(g_sum, near_packed[1:2])
+
     g_sum = g_sum + over_side(g_sum)
-    group = after(group, near_packed[1:2])
-    part_order = [fsdp_at ^ at for at in range(n_fsdp)]
+    group = after(group, near_packed[n_layer - 1 :] + [g_sum])
     if aligned and block % LANES == 0:
         group_out = convolve(group, near_stack, far_parts)
     else:
         kernel = jnp.stack([part for pair in zip(near_stack, far_parts) for part in pair])
         kernel = jnp.concatenate(
-            [lax.dynamic_index_in_dim(kernel, at, 0, keepdims=False) for at in part_order]
+            [
+                lax.dynamic_index_in_dim(kernel, fsdp_at ^ at, 0, keepdims=False)
+                for at in range(n_fsdp)
+            ]
         ).reshape(3, 3, channels, block)
         group_out = lax.conv_general_dilated(
             jnp.concatenate(group),
@@ -525,10 +510,38 @@
             preferred_element_type=jnp.float32,
         ).astype(jnp.bfloat16)
         group_out = jnp.split(group_out, n_factor)
-
+    own_maps, block_order = [], []
+    for other in range(2):
+        for pair in range(n_pair):
+            out = group_out[other * n_pair + pair]
+            if pair + other:
+                out = moved(out, "factor", lambda at, o=other, p=pair: (at ^ o) - 2 * p)
+            own_maps.append(out)
+            block_order.append(2 * ((pair_at + pair) % n_pair) + (core_at + other) % 2)
+
+    far_packed, came = {0: over_side(packed)}, []
+    for step in sorted(range(1, n_layer), key=lambda step: min(step, n_layer - step)):
+        if step == n_layer // 2:
+            came = came + list(group_out)
+        far_packed[step] = over_side(after(near_packed[step], came))
+        came = came + [near_packed[step]]
+    far_packed = [far_packed[step] for step in range(n_layer)]
+    g_sum = after(g_sum, near_packed)
+    g_sum = g_sum + moved(g_sum, "fsdp", lambda to: to ^ 2)
+    strips_of_grad = [
+        array[:, :rows].astype(jnp.float32) * jnp.exp2(array[:, rows : rows + 1].astype(jnp.float32))
+        for array in near_packed + far_packed
+    ]
+    came_from = [(fsdp_at - 2 * step) % n_fsdp for step in range(n_layer)]
+    came_from = came_from + [at ^ 1 for at in came_from]
+    order = [
+        2 * ((pair_at + step) % n_pair) + (core_at + other) % 2
+        for other in (1, 0)
+        for step in range(n_pair)
+    ]
     if aligned and block % LANES == 0:
         away, kept = tail_products(
-            after(a_inverse, [*group_out, a_factor, g_sum]),
+            after(a_inverse, own_maps[1:n_pair] + own_maps[n_pair + 1 :]),
             g_inverse,
             strips_of_grad,
             [(step, other) for other in range(2) for step in range(n_layer)],
@@ -553,21 +566,15 @@
         )
         away, kept = partial[:, : channels // 2], partial[:, channels // 2 :]
     by_pair = kept + over_core(away)
+    cov_own = totals[2] + after(over_core(after(totals[0], [packed])), by_pair)
+    a_factor = 0.5 * a_factor_old + (0.5 / pixel_total) * cov_own.T
     result = by_pair[:, :block]
     for step in range(1, n_pair):
         back = over_pair(by_pair[:, step * block : (step + 1) * block], step)
-        result = result + back
+        result = result + after(back, a_factor)
     natural_grad = result.astype(jnp.bfloat16)
 
 
-    own_maps, block_order = [], []
-    for other in range(2):
-        for pair in range(n_pair):
-            out = group_out[other * n_pair + pair]
-            if pair + other:
-                out = moved(out, "factor", lambda at, o=other, p=pair: (at ^ o) - 2 * p)
-            own_maps.append(out)
-            block_order.append(2 * ((pair_at + pair) % n_pair) + (core_at + other) % 2)
     own_maps = after(own_maps, by_pair)
     if aligned and block % LANES == 0:
         conv_out = side_by_side(own_maps)
@@ -577,8 +584,7 @@
             stacked = lax.dynamic_update_index_in_dim(stacked, out, at, 0)
         conv_out = jnp.concatenate(jnp.split(stacked, n_factor), axis=4)[0]
 
-    g_factor_sum = g_sum
-    g_factor = 0.5 * g_factor_old + 0.5 * g_factor_sum
+    g_factor = 0.5 * g_factor_old + 0.5 * g_sum
     return (conv_out, a_factor, g_factor, natural_grad)
 
 

time: 163 us -> 161 us (0.988)
  starting transfers between devices: 45.4 us -> 56.6 us
  waiting for transfers between devices: 59.3 us -> 51.7 us
  other arithmetic: 12.7 us -> 8.99 us
  local copies, waits for them, and re-layouts: 4.77 us -> 2.84 us
    ppermute x40, starting transfers between devices: 42 us -> 53.2 us  [moved(): lax.ppermute(array, axis, [(at, target(at) % count) for at in range(count)])]
    ppermute x40, waiting for transfers between devices: 59.3 us -> 51.7 us  [moved(): lax.ppermute(array, axis, [(at, target(at) % count) for at in range(count)])]
    add x1, other arithmetic: 4.59 us -> 1.88 us  [per_device(): a_factor = 0.5 * a_factor_old + 0.5 / pixel_total * cov_own.T]
  transfers between devices with their start and end apart: 41 -> 41, of which waited for: 14 -> 17; matrix products, arithmetic and copies ran while one was open for 6% -> 7% of each run, Pallas kernels for 19% -> 23%
where the time goes in v8:
time: 161 us; the launch traced here: 160 us
  starting transfers between devices  56.6 us (35%)
  waiting for transfers between devices  51.7 us (32%)
  Pallas kernels  37.5 us (23%)
  other arithmetic  8.99 us (6%)
  local copies, waits for them, and re-layouts  2.84 us (2%)
    ppermute x40, starting transfers between devices, moved(): lax.ppermute(array, axis, [(at, target(at) % count) for at in range(count)])  53.2 us
    ppermute x40, waiting for transfers between devices, moved(): lax.ppermute(array, axis, [(at, target(at) % count) for at in range(count)])  51.7 us
    pallas_call x2, Pallas kernels, add_products(): pl.pallas_call(lambda *refs: products_kernel(owners, pairs, len(strips),...  25.7 us
    pallas_call x1, Pallas kernels, tail_products(): pl.pallas_call(lambda *refs: tail_kernel(strip, block, layers, *refs), ou...  5.96 us
    pallas_call x1, Pallas kernels, convolve(): pl.pallas_call(lambda *refs: conv_kernel(n_images, *refs), out_shape=[jax...  5.09 us
    all_to_all x1, starting transfers between devices, per_device(): strips = lax.all_to_all(strips, 'fsdp', split_axis=0, concat_axis=0)  3.42 us
  transfers between devices with their start and end apart: 41, of which 17 were waited for; matrix products, arithmetic and copies ran while one was open for 7% of the time, Pallas kernels for 23%

profile of v8, /device:TPU:0, one launch (start us, length us, event | category | flops | bytes accessed | tf_op | source)
XLA Modules:
  0.0 160.1 jit_solution(10311971835559386232)
XLA Ops:
  0.6 3.0 %collective-permute-start.8 = (bf16[1,16,16,512]{3,2,1,0:T(8,128)(2,1)}, bf16[1,16,16,512]{3,2,1,0:T(8,128)(2,1)S(1)}, u32[]{:S(2)}, u32[]{:S(2)}) collective-permute-start(bf16[1,16,16,512]{3,2,1,0:T(8,128)(2,1)} %refs_0_.2), channel_id=1, source_target_pairs={{0,4},{4,0},{8,12},{12,8},{16,20},{20,16},{24,28},{28,24},{1,5},{5... | collective-permute-start | bytes 786440 | tf_op jit(solution)/shard_map/ppermute | solution.py:19
  3.6 1.5 collective-permute-start
  5.2 1.6 collective-permute-start.1
  6.7 2.2 %collective-permute-start.7 = (bf16[1,16,16,512]{3,2,1,0:T(8,128)(2,1)}, bf16[1,16,16,512]{3,2,1,0:T(8,128)(2,1)}, u32[]{:S(2)}, u32[]{:S(2)}) collective-permute-start(bf16[1,16,16,512]{3,2,1,0:T(8,128)(2,1)} %refs_0_.2), channel_id=1, source_target_pairs={{0,24},{4,28},{8,0},{12,4},{16,8},{20,12},{24,16},{28,20},{1,25},{... | collective-permute-start | bytes 786440 | tf_op jit(solution)/shard_map/ppermute | solution.py:19
  9.0 1.2 collective-permute-done.8.refs_1_
  10.2 1.9 %copy.19 = bf16[512,256]{1,0:T(8,128)(2,1)} copy(bf16[512,256]{0,1:T(8,128)(2,1)} %bitcast.22) | data formatting | bytes 524288 | tf_op jit(solution)/shard_map/transpose | solution.py:407
  12.1 4.5 %collective-permute-done.1.refs_3_ = bf16[1,16,16,512]{3,2,1,0:T(8,128)(2,1)} collective-permute-done((bf16[1,16,16,512]{3,2,1,0:T(8,128)(2,1)}, bf16[1,16,16,512]{3,2,1,0:T(8,128)(2,1)}, u32[]{:S(2)}, u32[]{:S(2)}) %collective-permute-start.1) | collective-permute-done | bytes 262176 | tf_op jit(solution)/shard_map/ppermute | solution.py:19
  16.6 0.5 collective-permute-start.3
  17.1 7.4 %collective-permute-start.2 = (bf16[1,16,16,512]{3,2,1,0:T(8,128)(2,1)}, bf16[1,16,16,512]{3,2,1,0:T(8,128)(2,1)}, u32[]{:S(2)}, u32[]{:S(2)}) collective-permute-start(bf16[1,16,16,512]{3,2,1,0:T(8,128)(2,1)} %refs_0_.2), channel_id=1, source_target_pairs={{0,16},{4,20},{8,24},{12,28},{16,0},{20,4},{24,8},{28,12},{1,17},{... | collective-permute-start | bytes 786440 | tf_op jit(solution)/shard_map/ppermute | solution.py:19
  24.5 1.3 fusion.9
  26.0 3.4 %all-to-all-start = ((bf16[8,64,256]{2,1,0:T(8,128)(2,1)}), bf16[8,64,256]{2,1,0:T(8,128)(2,1)S(1)}, u32[]{:S(2)}, u32[]{:S(2)}) async-start(bf16[8,64,256]{2,1,0:T(8,128)(2,1)} %bitcast.2), calls=%async_computation | async-start | bytes 524288 | tf_op jit(solution)/shard_map/all_to_all | solution.py:408
  29.4 1.6 collective-permute-start.10
  31.0 1.9 %collective-permute-start.12 = (bf16[1,16,16,512]{3,2,1,0:T(8,128)(2,1)}, bf16[1,16,16,512]{3,2,1,0:T(8,128)(2,1)}, u32[]{:S(2)}, u32[]{:S(2)}) collective-permute-start(bf16[1,16,16,512]{3,2,1,0:T(8,128)(2,1)} %collective-permute-done.1.refs_3_), channel_id=1, source_target_pairs={{0,4},{4,0},{8,12},{12,8},{16,20},{20,16},{24,28},{28,24},{1,5},{5... | collective-permute-start | bytes 786440 | tf_op jit(solution)/shard_map/ppermute | solution.py:19
  33.0 1.9 %collective-permute-start.18 = (bf16[1,576,128]{2,1,0:T(8,128)(2,1)S(1)}, bf16[1,576,128]{2,1,0:T(8,128)(2,1)S(1)}, u32[]{:S(2)}, u32[]{:S(2)}) collective-permute-start(bf16[1,576,128]{2,1,0:T(8,128)(2,1)S(1)} %dynamic-slice_bitcast_fusion.2), channel_id=1, source_target_pairs={{0,8},{4,12},{8,0},{12,4},{16,24},{20,28},{24,16},{28,20},{1,9},{5... | collective-permute-start | bytes 442376 | tf_op jit(solution)/shard_map/ppermute | solution.py:19
  35.0 3.3 %collective-permute-done.10.refs_5_ = bf16[1,16,16,512]{3,2,1,0:T(8,128)(2,1)} collective-permute-done((bf16[1,16,16,512]{3,2,1,0:T(8,128)(2,1)S(1)}, bf16[1,16,16,512]{3,2,1,0:T(8,128)(2,1)}, u32[]{:S(2)}, u32[]{:S(2)}) %collective-permute-start.10) | collective-permute-done | bytes 262176 | tf_op jit(solution)/shard_map/ppermute | solution.py:19
  38.3 1.5 collective-permute-start.4
  39.8 2.2 %collective-permute-done.12.refs_6_ = bf16[1,16,16,512]{3,2,1,0:T(8,128)(2,1)} collective-permute-done((bf16[1,16,16,512]{3,2,1,0:T(8,128)(2,1)}, bf16[1,16,16,512]{3,2,1,0:T(8,128)(2,1)}, u32[]{:S(2)}, u32[]{:S(2)}) %collective-permute-start.12) | collective-permute-done | bytes 262176 | tf_op jit(solution)/shard_map/ppermute | solution.py:19
  42.0 1.1 collective-permute-start.11
  43.1 4.2 %collective-permute-done.9.refs_1_ = bf16[1,16,16,512]{3,2,1,0:T(8,128)(2,1)} collective-permute-done((bf16[1,16,16,512]{3,2,1,0:T(8,128)(2,1)}, bf16[1,16,16,512]{3,2,1,0:T(8,128)(2,1)}, u32[]{:S(2)}, u32[]{:S(2)}) %collective-permute-start.9) | collective-permute-done | bytes 262176 | tf_op jit(solution)/shard_map/ppermute | solution.py:19
  47.3 1.0 collective-permute-start.13
  48.3 1.7 %collective-permute-start.19 = (bf16[2,576,128]{2,1,0:T(8,128)(2,1)S(1)}, bf16[2,576,128]{2,1,0:T(8,128)(2,1)}, u32[]{:S(2)}, u32[]{:S(2)}) collective-permute-start(bf16[2,576,128]{2,1,0:T(8,128)(2,1)S(1)} %pad_maximum_fusion.1), channel_id=1, source_target_pairs={{0,16},{4,20},{8,24},{12,28},{16,0},{20,4},{24,8},{28,12},{1,17},{... | collective-permute-start | bytes 884744 | tf_op jit(solution)/shard_map/ppermute | solution.py:19
  50.1 1.3 collective-permute-start.15
  51.5 1.5 collective-permute-start.14
  53.0 3.8 %collective-permute-done.13.refs_3_ = bf16[1,16,16,512]{3,2,1,0:T(8,128)(2,1)} collective-permute-done((bf16[1,16,16,512]{3,2,1,0:T(8,128)(2,1)}, bf16[1,16,16,512]{3,2,1,0:T(8,128)(2,1)}, u32[]{:S(2)}, u32[]{:S(2)}) %collective-permute-start.13) | collective-permute-done | bytes 262176 | tf_op jit(solution)/shard_map/ppermute | solution.py:19
  56.8 1.0 collective-permute-start.22
  57.8 6.0 %collective-permute-done.19 = bf16[2,576,128]{2,1,0:T(8,128)(2,1)} collective-permute-done((bf16[2,576,128]{2,1,0:T(8,128)(2,1)S(1)}, bf16[2,576,128]{2,1,0:T(8,128)(2,1)}, u32[]{:S(2)}, u32[]{:S(2)}) %collective-permute-start.19) | collective-permute-done | bytes 294944 | tf_op jit(solution)/shard_map/ppermute | solution.py:19
  63.8 1.3 collective-permute-start.17
  65.2 1.0 pad_maximum_fusion.refs_4_
  66.3 1.0 collective-permute-start.16
  67.3 12.9 %shard_map.102 = (f32[576,1152]{1,0:T(8,128)}, f32[64,1280]{1,0:T(8,128)}, f32[576,1152]{1,0:T(8,128)}, f32[64,1280]{1,0:T(8,128)}) custom-call(bf16[1,16,16,512]{3,2,1,0:T(8,128)(2,1)} %refs_0_.2, bf16[1,16,16,512]{3,2,1,0:T(8,128)(2,1)} %copy-done.13, bf16[1,16,16,512]{3,2,1,0:T(8,128)(2,1)} %copy-done.11, ...), custom_call_target="tpu_custom_call" | custom-call | flops 6039797760 | bytes 11796480 | tf_op jit(solution)/shard_map/pallas_call | solution.py:157
  80.3 0.3 collective-permute-start.6
  80.6 0.8 collective-permute-start.20
  81.5 0.7 copy-done.17
  82.2 12.7 %shard_map.103 = (f32[576,1152]{1,0:T(8,128)}, f32[64,1280]{1,0:T(8,128)}, f32[576,1152]{1,0:T(8,128)}, f32[64,1280]{1,0:T(8,128)}) custom-call(bf16[1,16,16,512]{3,2,1,0:T(8,128)(2,1)} %collective-permute-done.2.refs_0_, ...), custom_call_target="tpu_custom_call", output_to_operand_aliasing={{0}: (10, {}), {1}: (11, {}), {2}: (12, {}), {3}: (13, {})} | custom-call | flops 6039797760 | bytes 11796480 | tf_op jit(solution)/shard_map/pallas_call | solution.py:157
  94.9 1.1 collective-permute-done.23
  96.2 1.5 collective-permute-start.26
  97.8 0.3 collective-permute-done.24
  98.0 0.9 exponential_reduce_fusion.7
  98.9 0.9 convert_reduce_fusion
  99.8 1.1 convert_multiply_fusion.7
  101.0 3.3 %collective-permute-start.25 = (f16[64,1280]{1,0:T(8,128)(2,1)S(1)}, f16[64,1280]{1,0:T(8,128)(2,1)S(1)}, u32[]{:S(2)}, u32[]{:S(2)}) collective-permute-start(f16[64,1280]{1,0:T(8,128)(2,1)S(1)} %pad_maximum_fusion.2), channel_id=1, source_target_pairs={{0,24},{4,28},{8,0},{12,4},{16,8},{20,12},{24,16},{28,20},{1,25},{... | collective-permute-start | bytes 491528 | tf_op jit(solution)/shard_map/ppermute | solution.py:19
  104.4 0.6 collective-permute-done.26
  105.0 1.9 %collective-permute-start.31 = (f16[64,1280]{1,0:T(8,128)(2,1)S(1)}, f16[64,1280]{1,0:T(8,128)(2,1)S(1)}, u32[]{:S(2)}, u32[]{:S(2)}) collective-permute-start(f16[64,1280]{1,0:T(8,128)(2,1)S(1)} %pad_maximum_fusion.2), channel_id=1, source_target_pairs={{0,16},{4,20},{8,24},{12,28},{16,0},{20,4},{24,8},{28,12},{1,17},{... | collective-permute-start | bytes 491528 | tf_op jit(solution)/shard_map/ppermute | solution.py:19
  106.9 1.3 collective-permute-start.32
  108.2 0.8 collective-permute-done.25
  109.0 4.4 %collective-permute-done.30 = f16[64,1280]{1,0:T(8,128)(2,1)S(1)} collective-permute-done((f16[64,1280]{1,0:T(8,128)(2,1)S(1)}, f16[64,1280]{1,0:T(8,128)(2,1)S(1)}, u32[]{:S(2)}, u32[]{:S(2)}) %collective-permute-start.30) | collective-permute-done | bytes 163872 | tf_op jit(solution)/shard_map/ppermute | solution.py:19
  113.4 1.0 collective-permute-start.35
  114.3 5.1 %shard_map.104 = (bf16[1,16,16,128]{3,2,1,0:T(8,128)(2,1)}, bf16[1,16,16,128]{3,2,1,0:T(8,128)(2,1)}, bf16[1,16,16,128]{3,2,1,0:T(8,128)(2,1)}, bf16[1,16,16,128]{3,2,1,0:T(8,128)(2,1)}) custom-call(bf16[1,16,16,512]{3,2,1,0:T(8,128)(2,1)} %refs_0_.2, bf16[1,16,16,512]{3,2,1,0:T(8,128)(2,1)} %copy-done.11, bf16[1,16,16,512]{3,2,1,0:T(8,128)(2,1)} %copy-done.14, ...), custom_call_target="tpu_custom_call" | custom-call | flops 2415919104 | bytes 2228224 | tf_op jit(solution)/shard_map/pallas_call | solution.py:290
  119.4 1.1 collective-permute-start.27
  121.0 0.7 collective-permute-start.34
  122.2 1.8 %collective-permute-done.27.refs_1_ = bf16[1,16,16,128]{3,2,1,0:T(8,128)(2,1)S(1)} collective-permute-done((bf16[1,16,16,128]{3,2,1,0:T(8,128)(2,1)}, bf16[1,16,16,128]{3,2,1,0:T(8,128)(2,1)S(1)}, u32[]{:S(2)}, u32[]{:S(2)}) %collective-permute-start.27) | collective-permute-done | bytes 65568 | tf_op jit(solution)/shard_map/ppermute | solution.py:19
  124.0 1.5 collective-permute-start.33
  125.6 2.5 %collective-permute-done.34 = f16[64,1280]{1,0:T(8,128)(2,1)S(1)} collective-permute-done((f16[64,1280]{1,0:T(8,128)(2,1)S(1)}, f16[64,1280]{1,0:T(8,128)(2,1)S(1)}, u32[]{:S(2)}, u32[]{:S(2)}) %collective-permute-start.34) | collective-permute-done | bytes 163872 | tf_op jit(solution)/shard_map/ppermute | solution.py:19
  128.2 3.4 %collective-permute-done.33 = f16[64,1280]{1,0:T(8,128)(2,1)S(1)} collective-permute-done((f16[64,1280]{1,0:T(8,128)(2,1)S(1)}, f16[64,1280]{1,0:T(8,128)(2,1)S(1)}, u32[]{:S(2)}, u32[]{:S(2)}) %collective-permute-start.33) | collective-permute-done | bytes 163872 | tf_op jit(solution)/shard_map/ppermute | solution.py:19
  132.1 6.0 %shard_map.105 = (f32[576,256]{1,0:T(8,128)S(1)}, f32[576,256]{1,0:T(8,128)S(1)}) custom-call(f32[576,1152]{1,0:T(8,128)S(1)} %copy-done.2, f32[512,512]{1,0:T(8,128)S(1)} %copy-done.3, f32[64,1152]{1,0:T(8,128)S(1)} %get-tuple-element.100.refs_2_, f32[64,1152]{1,0:T(8,128)S(1)} %convert_multiply_fusion.6.refs_3_, ...), custom_call_target="tpu_custom_call" | custom-call | flops 2944401408 | bytes 3833856 | tf_op jit(solution)/shard_map/pallas_call | solution.py:234
  138.1 0.2 collective-permute-start.36
  138.2 4.6 %collective-permute-start.38 = (f32[128,512]{1,0:T(8,128)S(1)}, f32[128,512]{1,0:T(8,128)S(1)}, u32[]{:S(2)}, u32[]{:S(2)}) collective-permute-start(f32[128,512]{1,0:T(8,128)S(1)} %add.80), channel_id=1, source_target_pairs={{0,8},{4,12},{8,0},{12,4},{16,24},{20,28},{24,16},{28,20},{1,9},{5... | collective-permute-start | bytes 786440 | tf_op jit(solution)/shard_map/ppermute | solution.py:19
  143.0 6.7 %collective-permute-done.38 = f32[128,512]{1,0:T(8,128)S(1)} collective-permute-done((f32[128,512]{1,0:T(8,128)S(1)}, f32[128,512]{1,0:T(8,128)S(1)}, u32[]{:S(2)}, u32[]{:S(2)}) %collective-permute-start.38) | collective-permute-done | bytes 262176 | tf_op jit(solution)/shard_map/ppermute | solution.py:19
  149.7 0.8 add_multiply_fusion
  150.6 1.3 collective-permute-start.39
  151.9 0.8 shard_map.106
  152.7 1.9 %bitcast_add_fusion = f32[1152,576]{0,1:T(8,128)} fusion(f32[576,1152]{1,0:T(8,128)S(1)} %copy-done.5, f32[576,1152]{1,0:T(8,128)S(1)} %collective-permute-done.37, f32[1152,576]{0,1:T(8,128)S(1)} %copy-done.4), kind=kLoop, calls=%fused_computation | loop fusion | flops 2654208 | bytes 10616832 | tf_op jit(solution)/shard_map/add | solution.py:570
  154.6 4.8 %collective-permute-done.39 = f32[576,128]{1,0:T(8,128)S(1)} collective-permute-done((f32[576,128]{1,0:T(8,128)S(1)}, f32[576,128]{1,0:T(8,128)S(1)}, u32[]{:S(2)}, u32[]{:S(2)}) %collective-permute-start.39) | collective-permute-done | bytes 294944 | tf_op jit(solution)/shard_map/ppermute | solution.py:19
  159.4 0.7 fusion
  (100 shorter events, 2.8 us)
Async XLA Ops:
  0.6 32.4 %copy-start = (bf16[576,512]{1,0:T(8,128)(2,1)S(1)}, bf16[576,512]{1,0:T(8,128)(2,1)}, u32[]{:S(2)}) copy-start(bf16[576,512]{1,0:T(8,128)(2,1)} %param.9) | copy-start | bytes 1769476
  0.6 9.5 %collective-permute-start.8 = (bf16[1,16,16,512]{3,2,1,0:T(8,128)(2,1)}, bf16[1,16,16,512]{3,2,1,0:T(8,128)(2,1)S(1)}, u32[]{:S(2)}, u32[]{:S(2)}) collective-permute-start(bf16[1,16,16,512]{3,2,1,0:T(8,128)(2,1)} %refs_0_.2), channel_id=1, source_target_pairs={{0,4},{4,0},{8,12},{12,8},{16,20},{20,16},{24,28},{28,24},{1,5},{5... | collective-permute-start | bytes 786440 | tf_op jit(solution)/shard_map/ppermute | solution.py:19
  3.6 8.4 %collective-permute-start = (bf16[1,16,16,512]{3,2,1,0:T(8,128)(2,1)}, bf16[1,16,16,512]{3,2,1,0:T(8,128)(2,1)S(1)}, u32[]{:S(2)}, u32[]{:S(2)}) collective-permute-start(bf16[1,16,16,512]{3,2,1,0:T(8,128)(2,1)} %refs_0_.2), channel_id=1, source_target_pairs={{0,2},{1,3},{2,0},{3,1},{4,6},{5,7},{6,4},{7,5},{8,10},{9,11},{10,... | collective-permute-start | bytes 786440 | tf_op jit(solution)/shard_map/ppermute | solution.py:19
  5.2 11.4 %collective-permute-start.1 = (bf16[1,16,16,512]{3,2,1,0:T(8,128)(2,1)}, bf16[1,16,16,512]{3,2,1,0:T(8,128)(2,1)}, u32[]{:S(2)}, u32[]{:S(2)}) collective-permute-start(bf16[1,16,16,512]{3,2,1,0:T(8,128)(2,1)} %refs_0_.2), channel_id=1, source_target_pairs={{0,8},{4,12},{8,16},{12,20},{16,24},{20,28},{24,0},{28,4},{1,9},{5... | collective-permute-start | bytes 786440 | tf_op jit(solution)/shard_map/ppermute | solution.py:19
  6.7 24.2 %collective-permute-start.7 = (bf16[1,16,16,512]{3,2,1,0:T(8,128)(2,1)}, bf16[1,16,16,512]{3,2,1,0:T(8,128)(2,1)}, u32[]{:S(2)}, u32[]{:S(2)}) collective-permute-start(bf16[1,16,16,512]{3,2,1,0:T(8,128)(2,1)} %refs_0_.2), channel_id=1, source_target_pairs={{0,24},{4,28},{8,0},{12,4},{16,8},{20,12},{24,16},{28,20},{1,25},{... | collective-permute-start | bytes 786440 | tf_op jit(solution)/shard_map/ppermute | solution.py:19
  10.2 38.1 %copy-start.13 = (bf16[1,16,16,512]{3,2,1,0:T(8,128)(2,1)}, bf16[1,16,16,512]{3,2,1,0:T(8,128)(2,1)S(1)}, u32[]{:S(2)}) copy-start(bf16[1,16,16,512]{3,2,1,0:T(8,128)(2,1)S(1)} %collective-permute-done.8.refs_1_) | copy-start | bytes 786436
  12.1 12.4 %copy-start.11 = (bf16[1,16,16,512]{3,2,1,0:T(8,128)(2,1)}, bf16[1,16,16,512]{3,2,1,0:T(8,128)(2,1)S(1)}, u32[]{:S(2)}) copy-start(bf16[1,16,16,512]{3,2,1,0:T(8,128)(2,1)S(1)} %collective-permute-done.refs_2_.refs_1_) | copy-start | bytes 786436
  16.6 16.5 %collective-permute-start.3 = (bf16[1,16,16,512]{3,2,1,0:T(8,128)(2,1)}, bf16[1,16,16,512]{3,2,1,0:T(8,128)(2,1)}, u32[]{:S(2)}, u32[]{:S(2)}) collective-permute-start(bf16[1,16,16,512]{3,2,1,0:T(8,128)(2,1)} %collective-permute-done.1.refs_3_), channel_id=1, source_target_pairs={{0,2},{1,3},{2,0},{3,1},{4,6},{5,7},{6,4},{7,5},{8,10},{9,11},{10,... | collective-permute-start | bytes 786440 | tf_op jit(solution)/shard_map/ppermute | solution.py:19
  17.1 15.8 %collective-permute-start.2 = (bf16[1,16,16,512]{3,2,1,0:T(8,128)(2,1)}, bf16[1,16,16,512]{3,2,1,0:T(8,128)(2,1)}, u32[]{:S(2)}, u32[]{:S(2)}) collective-permute-start(bf16[1,16,16,512]{3,2,1,0:T(8,128)(2,1)} %refs_0_.2), channel_id=1, source_target_pairs={{0,16},{4,20},{8,24},{12,28},{16,0},{20,4},{24,8},{28,12},{1,17},{... | collective-permute-start | bytes 786440 | tf_op jit(solution)/shard_map/ppermute | solution.py:19
  25.9 24.2 %collective-permute-start.21 = (f32[2,128,512]{2,1,0:T(8,128)S(1)}, f32[2,128,512]{2,1,0:T(8,128)S(1)}, u32[]{:S(2)}, u32[]{:S(2)}) collective-permute-start(f32[2,128,512]{2,1,0:T(8,128)S(1)} %dynamic-slice_bitcast_fusion), channel_id=1, source_target_pairs={{0,1},{1,0},{2,3},{3,2},{4,5},{5,4},{6,7},{7,6},{8,9},{9,8},{10,11... | collective-permute-start | bytes 1572872 | tf_op jit(solution)/shard_map/ppermute | solution.py:19
  26.0 24.1 %all-to-all-start = ((bf16[8,64,256]{2,1,0:T(8,128)(2,1)}), bf16[8,64,256]{2,1,0:T(8,128)(2,1)S(1)}, u32[]{:S(2)}, u32[]{:S(2)}) async-start(bf16[8,64,256]{2,1,0:T(8,128)(2,1)} %bitcast.2), calls=%async_computation | async-start | bytes 524288 | tf_op jit(solution)/shard_map/all_to_all | solution.py:408
  29.4 8.9 %collective-permute-start.10 = (bf16[1,16,16,512]{3,2,1,0:T(8,128)(2,1)S(1)}, bf16[1,16,16,512]{3,2,1,0:T(8,128)(2,1)}, u32[]{:S(2)}, u32[]{:S(2)}) collective-permute-start(bf16[1,16,16,512]{3,2,1,0:T(8,128)(2,1)S(1)} %collective-permute-done.8.refs_1_), channel_id=1, source_target_pairs={{0,2},{1,3},{2,0},{3,1},{4,6},{5,7},{6,4},{7,5},{8,10},{9,11},{10,... | collective-permute-start | bytes 786440 | tf_op jit(solution)/shard_map/ppermute | solution.py:19
  31.0 11.0 %collective-permute-start.12 = (bf16[1,16,16,512]{3,2,1,0:T(8,128)(2,1)}, bf16[1,16,16,512]{3,2,1,0:T(8,128)(2,1)}, u32[]{:S(2)}, u32[]{:S(2)}) collective-permute-start(bf16[1,16,16,512]{3,2,1,0:T(8,128)(2,1)} %collective-permute-done.1.refs_3_), channel_id=1, source_target_pairs={{0,4},{4,0},{8,12},{12,8},{16,20},{20,16},{24,28},{28,24},{1,5},{5... | collective-permute-start | bytes 786440 | tf_op jit(solution)/shard_map/ppermute | solution.py:19
  32.8 14.5 %collective-permute-start.9 = (bf16[1,16,16,512]{3,2,1,0:T(8,128)(2,1)}, bf16[1,16,16,512]{3,2,1,0:T(8,128)(2,1)}, u32[]{:S(2)}, u32[]{:S(2)}) collective-permute-start(bf16[1,16,16,512]{3,2,1,0:T(8,128)(2,1)} %collective-permute-done.7.refs_4_), channel_id=1, source_target_pairs={{0,4},{4,0},{8,12},{12,8},{16,20},{20,16},{24,28},{28,24},{1,5},{5... | collective-permute-start | bytes 786440 | tf_op jit(solution)/shard_map/ppermute | solution.py:19
  33.0 15.3 %collective-permute-start.18 = (bf16[1,576,128]{2,1,0:T(8,128)(2,1)S(1)}, bf16[1,576,128]{2,1,0:T(8,128)(2,1)S(1)}, u32[]{:S(2)}, u32[]{:S(2)}) collective-permute-start(bf16[1,576,128]{2,1,0:T(8,128)(2,1)S(1)} %dynamic-slice_bitcast_fusion.2), channel_id=1, source_target_pairs={{0,8},{4,12},{8,0},{12,4},{16,24},{20,28},{24,16},{28,20},{1,9},{5... | collective-permute-start | bytes 442376 | tf_op jit(solution)/shard_map/ppermute | solution.py:19
  38.3 13.2 %collective-permute-start.4 = (bf16[1,16,16,512]{3,2,1,0:T(8,128)(2,1)}, bf16[1,16,16,512]{3,2,1,0:T(8,128)(2,1)}, u32[]{:S(2)}, u32[]{:S(2)}) collective-permute-start(bf16[1,16,16,512]{3,2,1,0:T(8,128)(2,1)} %collective-permute-done.2.refs_0_), channel_id=1, source_target_pairs={{0,2},{1,3},{2,0},{3,1},{4,6},{5,7},{6,4},{7,5},{8,10},{9,11},{10,... | collective-permute-start | bytes 786440 | tf_op jit(solution)/shard_map/ppermute | solution.py:19
  42.0 24.2 %collective-permute-start.11 = (bf16[1,16,16,512]{3,2,1,0:T(8,128)(2,1)}, bf16[1,16,16,512]{3,2,1,0:T(8,128)(2,1)}, u32[]{:S(2)}, u32[]{:S(2)}) collective-permute-start(bf16[1,16,16,512]{3,2,1,0:T(8,128)(2,1)} %collective-permute-done.7.refs_4_), channel_id=1, source_target_pairs={{0,2},{1,3},{2,0},{3,1},{4,6},{5,7},{6,4},{7,5},{8,10},{9,11},{10,... | collective-permute-start | bytes 786440 | tf_op jit(solution)/shard_map/ppermute | solution.py:19
  47.3 9.5 %collective-permute-start.13 = (bf16[1,16,16,512]{3,2,1,0:T(8,128)(2,1)}, bf16[1,16,16,512]{3,2,1,0:T(8,128)(2,1)}, u32[]{:S(2)}, u32[]{:S(2)}) collective-permute-start(bf16[1,16,16,512]{3,2,1,0:T(8,128)(2,1)} %collective-permute-done.2.refs_0_), channel_id=1, source_target_pairs={{0,4},{4,0},{8,12},{12,8},{16,20},{20,16},{24,28},{28,24},{1,5},{5... | collective-permute-start | bytes 786440 | tf_op jit(solution)/shard_map/ppermute | solution.py:19
  48.3 15.5 %collective-permute-start.19 = (bf16[2,576,128]{2,1,0:T(8,128)(2,1)S(1)}, bf16[2,576,128]{2,1,0:T(8,128)(2,1)}, u32[]{:S(2)}, u32[]{:S(2)}) collective-permute-start(bf16[2,576,128]{2,1,0:T(8,128)(2,1)S(1)} %pad_maximum_fusion.1), channel_id=1, source_target_pairs={{0,16},{4,20},{8,24},{12,28},{16,0},{20,4},{24,8},{28,12},{1,17},{... | collective-permute-start | bytes 884744 | tf_op jit(solution)/shard_map/ppermute | solution.py:19
  50.1 17.2 %copy-start.7 = (bf16[8,64,256]{2,1,0:T(8,128)(2,1)}, bf16[8,64,256]{2,1,0:T(8,128)(2,1)S(1)}, u32[]{:S(2)}) copy-start(bf16[8,64,256]{2,1,0:T(8,128)(2,1)S(1)} %all-to-all-done.refs_8_) | copy-start | bytes 786436
  50.1 16.2 %copy-start.10 = (bf16[1,16,16,512]{3,2,1,0:T(8,128)(2,1)S(1)}, bf16[1,16,16,512]{3,2,1,0:T(8,128)(2,1)}, u32[]{:S(2)}) copy-start(bf16[1,16,16,512]{3,2,1,0:T(8,128)(2,1)} %refs_0_.2) | copy-start | bytes 786436
  50.1 16.2 %collective-permute-start.15 = (bf16[8,64,256]{2,1,0:T(8,128)(2,1)S(1)}, bf16[8,64,256]{2,1,0:T(8,128)(2,1)S(1)}, u32[]{:S(2)}, u32[]{:S(2)}) collective-permute-start(bf16[8,64,256]{2,1,0:T(8,128)(2,1)S(1)} %all-to-all-done.refs_8_), channel_id=1, source_target_pairs={{0,2},{1,3},{2,0},{3,1},{4,6},{5,7},{6,4},{7,5},{8,10},{9,11},{10,... | collective-permute-start | bytes 786440 | tf_op jit(solution)/shard_map/ppermute | solution.py:19
  51.5 30.0 %collective-permute-start.14 = (bf16[1,16,16,512]{3,2,1,0:T(8,128)(2,1)}, bf16[1,16,16,512]{3,2,1,0:T(8,128)(2,1)S(1)}, u32[]{:S(2)}, u32[]{:S(2)}) collective-permute-start(bf16[1,16,16,512]{3,2,1,0:T(8,128)(2,1)} %collective-permute-done.3.refs_7_), channel_id=1, source_target_pairs={{0,4},{4,0},{8,12},{12,8},{16,20},{20,16},{24,28},{28,24},{1,5},{5... | collective-permute-start | bytes 786440 | tf_op jit(solution)/shard_map/ppermute | solution.py:19
  56.8 24.5 %collective-permute-start.22 = (f32[128,512]{1,0:T(8,128)S(1)}, f32[128,512]{1,0:T(8,128)S(1)}, u32[]{:S(2)}, u32[]{:S(2)}) collective-permute-start(f32[128,512]{1,0:T(8,128)S(1)} %dynamic-slice_bitcast_fusion.1), channel_id=1, source_target_pairs={{0,2},{1,3},{2,0},{3,1},{4,6},{5,7},{6,4},{7,5},{8,10},{9,11},{10,... | collective-permute-start | bytes 786440 | tf_op jit(solution)/shard_map/ppermute | solution.py:19
  63.8 16.4 %collective-permute-start.17 = (bf16[1,16,16,512]{3,2,1,0:T(8,128)(2,1)}, bf16[1,16,16,512]{3,2,1,0:T(8,128)(2,1)S(1)}, u32[]{:S(2)}, u32[]{:S(2)}) collective-permute-start(bf16[1,16,16,512]{3,2,1,0:T(8,128)(2,1)} %collective-permute-done.4.refs_4_), channel_id=1, source_target_pairs={{0,4},{4,0},{8,12},{12,8},{16,20},{20,16},{24,28},{28,24},{1,5},{5... | collective-permute-start | bytes 786440 | tf_op jit(solution)/shard_map/ppermute | solution.py:19
  66.2 14.4 %copy-start.6 = (bf16[4,576,128]{2,1,0:T(8,128)(2,1)}, bf16[4,576,128]{2,1,0:T(8,128)(2,1)S(1)}, u32[]{:S(2)}) copy-start(bf16[4,576,128]{2,1,0:T(8,128)(2,1)S(1)} %pad_maximum_fusion.refs_4_) | copy-start | bytes 1769476
  66.2 14.1 %copy-start.12 = (bf16[1,16,16,512]{3,2,1,0:T(8,128)(2,1)S(1)}, bf16[1,16,16,512]{3,2,1,0:T(8,128)(2,1)}, u32[]{:S(2)}) copy-start(bf16[1,16,16,512]{3,2,1,0:T(8,128)(2,1)} %copy-done.11) | copy-start | bytes 786436
  66.2 29.9 %collective-permute-start.5 = (bf16[1,16,16,512]{3,2,1,0:T(8,128)(2,1)S(1)}, bf16[1,16,16,512]{3,2,1,0:T(8,128)(2,1)S(1)}, u32[]{:S(2)}, u32[]{:S(2)}) collective-permute-start(bf16[1,16,16,512]{3,2,1,0:T(8,128)(2,1)S(1)} %copy-done.10), channel_id=1, source_target_pairs={{0,1},{1,0},{2,3},{3,2},{4,5},{5,4},{6,7},{7,6},{8,9},{9,8},{10,11... | collective-permute-start | bytes 786440 | tf_op jit(solution)/shard_map/ppermute | solution.py:19
  66.3 1.0 copy-start.16
  66.3 14.2 %collective-permute-start.16 = (bf16[1,16,16,512]{3,2,1,0:T(8,128)(2,1)}, bf16[1,16,16,512]{3,2,1,0:T(8,128)(2,1)S(1)}, u32[]{:S(2)}, u32[]{:S(2)}) collective-permute-start(bf16[1,16,16,512]{3,2,1,0:T(8,128)(2,1)} %collective-permute-done.9.refs_1_), channel_id=1, source_target_pairs={{0,2},{1,3},{2,0},{3,1},{4,6},{5,7},{6,4},{7,5},{8,10},{9,11},{10,... | collective-permute-start | bytes 786440 | tf_op jit(solution)/shard_map/ppermute | solution.py:19
  80.3 1.2 copy-start.18
  80.3 15.8 %collective-permute-start.6 = (bf16[1,16,16,512]{3,2,1,0:T(8,128)(2,1)S(1)}, bf16[1,16,16,512]{3,2,1,0:T(8,128)(2,1)S(1)}, u32[]{:S(2)}, u32[]{:S(2)}) collective-permute-start(bf16[1,16,16,512]{3,2,1,0:T(8,128)(2,1)S(1)} %copy-done.12), channel_id=1, source_target_pairs={{0,1},{1,0},{2,3},{3,2},{4,5},{5,4},{6,7},{7,6},{8,9},{9,8},{10,11... | collective-permute-start | bytes 786440 | tf_op jit(solution)/shard_map/ppermute | solution.py:19
  80.6 0.9 copy-start.19
  80.6 15.6 %collective-permute-start.20 = (bf16[4,576,128]{2,1,0:T(8,128)(2,1)S(1)}, bf16[4,576,128]{2,1,0:T(8,128)(2,1)S(1)}, u32[]{:S(2)}, u32[]{:S(2)}) collective-permute-start(bf16[4,576,128]{2,1,0:T(8,128)(2,1)S(1)} %pad_maximum_fusion.refs_4_), channel_id=1, source_target_pairs={{0,4},{4,0},{8,12},{12,8},{16,20},{20,16},{24,28},{28,24},{1,5},{5... | collective-permute-start | bytes 1769480 | tf_op jit(solution)/shard_map/ppermute | solution.py:19
  81.4 14.6 %collective-permute-start.23 = (f32[128,512]{1,0:T(8,128)S(1)}, f32[128,512]{1,0:T(8,128)S(1)}, u32[]{:S(2)}, u32[]{:S(2)}) collective-permute-start(f32[128,512]{1,0:T(8,128)S(1)} %bitcast_add_fusion.2), channel_id=1, source_target_pairs={{0,16},{4,20},{8,24},{12,28},{16,0},{20,4},{24,8},{28,12},{1,17},{... | collective-permute-start | bytes 786440 | tf_op jit(solution)/shard_map/ppermute | solution.py:19
  81.5 0.7 copy-start.17
  96.1 12.1 %copy-start.14 = (bf16[1,16,16,512]{3,2,1,0:T(8,128)(2,1)}, bf16[1,16,16,512]{3,2,1,0:T(8,128)(2,1)S(1)}, u32[]{:S(2)}) copy-start(bf16[1,16,16,512]{3,2,1,0:T(8,128)(2,1)S(1)} %collective-permute-done.5.refs_2_) | copy-start | bytes 786436
  96.1 18.2 %copy-start.15 = (bf16[1,16,16,512]{3,2,1,0:T(8,128)(2,1)}, bf16[1,16,16,512]{3,2,1,0:T(8,128)(2,1)S(1)}, u32[]{:S(2)}) copy-start(bf16[1,16,16,512]{3,2,1,0:T(8,128)(2,1)S(1)} %collective-permute-done.6.refs_3_) | copy-start | bytes 786436
  96.2 12.0 %copy-start.9 = (bf16[4,576,128]{2,1,0:T(8,128)(2,1)}, bf16[4,576,128]{2,1,0:T(8,128)(2,1)S(1)}, u32[]{:S(2)}) copy-start(bf16[4,576,128]{2,1,0:T(8,128)(2,1)S(1)} %collective-permute-done.20.refs_5_) | copy-start | bytes 1769476
  96.2 1.9 %collective-permute-start.24 = (f32[64,1280]{1,0:T(8,128)}, f32[64,1280]{1,0:T(8,128)S(1)}, u32[]{:S(2)}, u32[]{:S(2)}) collective-permute-start(f32[64,1280]{1,0:T(8,128)} %get-tuple-element.74), channel_id=1, source_target_pairs={{0,1},{1,0},{2,3},{3,2},{4,5},{5,4},{6,7},{7,6},{8,9},{9,8},{10,11... | collective-permute-start | bytes 983048 | tf_op jit(solution)/shard_map/ppermute | solution.py:19
  96.2 8.7 %collective-permute-start.26 = (f32[128,512]{1,0:T(8,128)S(1)}, f32[128,512]{1,0:T(8,128)S(1)}, u32[]{:S(2)}, u32[]{:S(2)}) collective-permute-start(f32[128,512]{1,0:T(8,128)S(1)} %add.77), channel_id=1, source_target_pairs={{0,4},{4,0},{8,12},{12,8},{16,20},{20,16},{24,28},{28,24},{1,5},{5... | collective-permute-start | bytes 786440 | tf_op jit(solution)/shard_map/ppermute | solution.py:19
  101.0 7.9 %collective-permute-start.25 = (f16[64,1280]{1,0:T(8,128)(2,1)S(1)}, f16[64,1280]{1,0:T(8,128)(2,1)S(1)}, u32[]{:S(2)}, u32[]{:S(2)}) collective-permute-start(f16[64,1280]{1,0:T(8,128)(2,1)S(1)} %pad_maximum_fusion.2), channel_id=1, source_target_pairs={{0,24},{4,28},{8,0},{12,4},{16,8},{20,12},{24,16},{28,20},{1,25},{... | collective-permute-start | bytes 491528 | tf_op jit(solution)/shard_map/ppermute | solution.py:19
  104.4 9.0 %collective-permute-start.30 = (f16[64,1280]{1,0:T(8,128)(2,1)S(1)}, f16[64,1280]{1,0:T(8,128)(2,1)S(1)}, u32[]{:S(2)}, u32[]{:S(2)}) collective-permute-start(f16[64,1280]{1,0:T(8,128)(2,1)S(1)} %pad_maximum_fusion.2), channel_id=1, source_target_pairs={{0,8},{4,12},{8,16},{12,20},{16,24},{20,28},{24,0},{28,4},{1,9},{5... | collective-permute-start | bytes 491528 | tf_op jit(solution)/shard_map/ppermute | solution.py:19
  105.0 15.7 %collective-permute-start.31 = (f16[64,1280]{1,0:T(8,128)(2,1)S(1)}, f16[64,1280]{1,0:T(8,128)(2,1)S(1)}, u32[]{:S(2)}, u32[]{:S(2)}) collective-permute-start(f16[64,1280]{1,0:T(8,128)(2,1)S(1)} %pad_maximum_fusion.2), channel_id=1, source_target_pairs={{0,16},{4,20},{8,24},{12,28},{16,0},{20,4},{24,8},{28,12},{1,17},{... | collective-permute-start | bytes 491528 | tf_op jit(solution)/shard_map/ppermute | solution.py:19
  106.9 14.2 %collective-permute-start.32 = (f16[64,1280]{1,0:T(8,128)(2,1)S(1)}, f16[64,1280]{1,0:T(8,128)(2,1)S(1)}, u32[]{:S(2)}, u32[]{:S(2)}) collective-permute-start(f16[64,1280]{1,0:T(8,128)(2,1)S(1)} %pad_maximum_fusion.2), channel_id=1, source_target_pairs={{0,4},{4,0},{8,12},{12,8},{16,20},{20,16},{24,28},{28,24},{1,5},{5... | collective-permute-start | bytes 491528 | tf_op jit(solution)/shard_map/ppermute | solution.py:19
  108.2 44.5 %collective-permute-start.37 = (f32[576,1152]{1,0:T(8,128)}, f32[576,1152]{1,0:T(8,128)S(1)}, u32[]{:S(2)}, u32[]{:S(2)}) collective-permute-start(f32[576,1152]{1,0:T(8,128)} %get-tuple-element.94), channel_id=1, source_target_pairs={{0,1},{1,0},{2,3},{3,2},{4,5},{5,4},{6,7},{7,6},{8,9},{9,8},{10,11... | collective-permute-start | bytes 7962632 | tf_op jit(solution)/shard_map/ppermute | solution.py:19
  113.4 12.1 %collective-permute-start.35 = (f16[64,1280]{1,0:T(8,128)(2,1)S(1)}, f16[64,1280]{1,0:T(8,128)(2,1)S(1)}, u32[]{:S(2)}, u32[]{:S(2)}) collective-permute-start(f16[64,1280]{1,0:T(8,128)(2,1)S(1)} %collective-permute-done.25), channel_id=1, source_target_pairs={{0,4},{4,0},{8,12},{12,8},{16,20},{20,16},{24,28},{28,24},{1,5},{5... | collective-permute-start | bytes 491528 | tf_op jit(solution)/shard_map/ppermute | solution.py:19
  114.3 17.7 %copy-start.3 = (f32[512,512]{1,0:T(8,128)S(1)}, f32[512,512]{1,0:T(8,128)}, u32[]{:S(2)}) copy-start(f32[512,512]{1,0:T(8,128)} %refs_1_.1) | copy-start | bytes 3145732
  119.4 12.6 %copy-start.2 = (f32[576,1152]{1,0:T(8,128)S(1)}, f32[576,1152]{1,0:T(8,128)}, u32[]{:S(2)}) copy-start(f32[576,1152]{1,0:T(8,128)} %refs_0_.3) | copy-start | bytes 7962628
  119.4 4.5 %collective-permute-start.27 = (bf16[1,16,16,128]{3,2,1,0:T(8,128)(2,1)}, bf16[1,16,16,128]{3,2,1,0:T(8,128)(2,1)S(1)}, u32[]{:S(2)}, u32[]{:S(2)}) collective-permute-start(bf16[1,16,16,128]{3,2,1,0:T(8,128)(2,1)} %get-tuple-element.80), channel_id=1, source_target_pairs={{0,2},{1,3},{2,0},{3,1},{4,6},{5,7},{6,4},{7,5},{8,10},{9,11},{10,... | collective-permute-start | bytes 196616 | tf_op jit(solution)/shard_map/ppermute | solution.py:19
  120.7 4.8 %collective-permute-start.29 = (bf16[1,16,16,128]{3,2,1,0:T(8,128)(2,1)}, bf16[1,16,16,128]{3,2,1,0:T(8,128)(2,1)S(1)}, u32[]{:S(2)}, u32[]{:S(2)}) collective-permute-start(bf16[1,16,16,128]{3,2,1,0:T(8,128)(2,1)} %get-tuple-element.82), channel_id=1, source_target_pairs={{0,3},{1,2},{2,1},{3,0},{4,7},{5,6},{6,5},{7,4},{8,11},{9,10},{10,... | collective-permute-start | bytes 196616 | tf_op jit(solution)/shard_map/ppermute | solution.py:19
  121.0 7.1 %collective-permute-start.34 = (f16[64,1280]{1,0:T(8,128)(2,1)S(1)}, f16[64,1280]{1,0:T(8,128)(2,1)S(1)}, u32[]{:S(2)}, u32[]{:S(2)}) collective-permute-start(f16[64,1280]{1,0:T(8,128)(2,1)S(1)} %collective-permute-done.31), channel_id=1, source_target_pairs={{0,4},{4,0},{8,12},{12,8},{16,20},{20,16},{24,28},{28,24},{1,5},{5... | collective-permute-start | bytes 491528 | tf_op jit(solution)/shard_map/ppermute | solution.py:19
  124.0 7.6 %collective-permute-start.33 = (f16[64,1280]{1,0:T(8,128)(2,1)S(1)}, f16[64,1280]{1,0:T(8,128)(2,1)S(1)}, u32[]{:S(2)}, u32[]{:S(2)}) collective-permute-start(f16[64,1280]{1,0:T(8,128)(2,1)S(1)} %collective-permute-done.30), channel_id=1, source_target_pairs={{0,4},{4,0},{8,12},{12,8},{16,20},{20,16},{24,28},{28,24},{1,5},{5... | collective-permute-start | bytes 491528 | tf_op jit(solution)/shard_map/ppermute | solution.py:19
  132.0 10.8 %copy-start.20 = (bf16[1,16,16,128]{3,2,1,0:T(8,128)(2,1)S(1)}, bf16[1,16,16,128]{3,2,1,0:T(8,128)(2,1)}, u32[]{:S(2)}) copy-start(bf16[1,16,16,128]{3,2,1,0:T(8,128)(2,1)} %get-tuple-element.81) | copy-start | bytes 196612
  132.0 17.7 %copy-start.8 = (f32[128,512]{1,0:T(8,128)S(1)}, f32[128,512]{1,0:T(8,128)}, u32[]{:S(2)}) copy-start(f32[128,512]{1,0:T(8,128)} %param.11) | copy-start | bytes 786436
  132.1 20.6 %copy-start.5 = (f32[576,1152]{1,0:T(8,128)S(1)}, f32[576,1152]{1,0:T(8,128)}, u32[]{:S(2)}) copy-start(f32[576,1152]{1,0:T(8,128)} %get-tuple-element.92) | copy-start | bytes 7962628
  138.0 13.9 %copy-start.1 = (bf16[1,16,16,128]{3,2,1,0:T(8,128)(2,1)S(1)}, bf16[1,16,16,128]{3,2,1,0:T(8,128)(2,1)}, u32[]{:S(2)}) copy-start(bf16[1,16,16,128]{3,2,1,0:T(8,128)(2,1)} %get-tuple-element.88.refs_0_) | copy-start | bytes 196612
  138.0 14.6 %copy-start.4 = (f32[1152,576]{0,1:T(8,128)S(1)}, f32[1152,576]{0,1:T(8,128)}, u32[]{:S(2)}) copy-start(f32[1152,576]{0,1:T(8,128)} %param.10) | copy-start | bytes 7962628
  138.1 12.4 %collective-permute-start.36 = (f32[576,256]{1,0:T(8,128)S(1)}, f32[576,256]{1,0:T(8,128)S(1)}, u32[]{:S(2)}, u32[]{:S(2)}) collective-permute-start(f32[576,256]{1,0:T(8,128)S(1)} %get-tuple-element.87), channel_id=1, source_target_pairs={{0,1},{1,0},{2,3},{3,2},{4,5},{5,4},{6,7},{7,6},{8,9},{9,8},{10,11... | collective-permute-start | bytes 1769480 | tf_op jit(solution)/shard_map/ppermute | solution.py:19
  138.2 11.5 %collective-permute-start.38 = (f32[128,512]{1,0:T(8,128)S(1)}, f32[128,512]{1,0:T(8,128)S(1)}, u32[]{:S(2)}, u32[]{:S(2)}) collective-permute-start(f32[128,512]{1,0:T(8,128)S(1)} %add.80), channel_id=1, source_target_pairs={{0,8},{4,12},{8,0},{12,4},{16,24},{20,28},{24,16},{28,20},{1,9},{5... | collective-permute-start | bytes 786440 | tf_op jit(solution)/shard_map/ppermute | solution.py:19
  142.8 9.1 %collective-permute-start.28 = (bf16[1,16,16,128]{3,2,1,0:T(8,128)(2,1)S(1)}, bf16[1,16,16,128]{3,2,1,0:T(8,128)(2,1)S(1)}, u32[]{:S(2)}, u32[]{:S(2)}) collective-permute-start(bf16[1,16,16,128]{3,2,1,0:T(8,128)(2,1)S(1)} %copy-done.20), channel_id=1, source_target_pairs={{0,1},{1,0},{2,3},{3,2},{4,5},{5,4},{6,7},{7,6},{8,9},{9,8},{10,11... | collective-permute-start | bytes 196616 | tf_op jit(solution)/shard_map/ppermute | solution.py:19
  150.6 8.8 %collective-permute-start.39 = (f32[576,128]{1,0:T(8,128)S(1)}, f32[576,128]{1,0:T(8,128)S(1)}, u32[]{:S(2)}, u32[]{:S(2)}) collective-permute-start(f32[576,128]{1,0:T(8,128)S(1)} %slice.98), channel_id=1, source_target_pairs={{0,2},{1,3},{2,0},{3,1},{4,6},{5,7},{6,4},{7,5},{8,10},{9,11},{10,... | collective-permute-start | bytes 884744 | tf_op jit(solution)/shard_map/ppermute | solution.py:19

commit v9 on v8

--- a/solution.py
+++ b/solution.py
@@ -74,16 +74,16 @@
     return copies
 
 
-def products_kernel(owners, pairs, n_pair, first, *refs):
-    image_refs, strip_refs = refs[: len(pairs)], refs[len(pairs) : len(pairs) + n_pair]
-    refs = refs[len(pairs) + n_pair :]
+def products_kernel(owners, first, *refs):
+    image_refs, strips_ref = refs[: len(owners)], refs[len(owners)]
+    refs = refs[len(owners) + 1 :]
     before, refs = (None, refs) if first else (refs[:4], refs[4:])
     out_refs, totals, (shifted, turned, left, strips, sems) = refs[:4], refs[4:8], refs[8:]
     n_images, side, channels = len(image_refs), image_refs[0].shape[1], image_refs[0].shape[3]
     spots = side * side
     cols, rows = totals[0].shape
     strip = totals[1].shape[0]
-    n_fsdp = strip_refs[0].shape[0]
+    n_fsdp, n_pair = lax.axis_size("fsdp"), lax.axis_size("factor") // 2
     fsdp_at, factor_at = lax.axis_index("fsdp"), lax.axis_index("factor")
 
     arrivals = fetch(
@@ -91,7 +91,7 @@
         [shifted.at[1, at, pl.ds(1, side)] for at in range(n_images)],
         sems.at[0],
     )
-    strip_copies = fetch(strip_refs, [strips.at[at] for at in range(n_pair)], sems.at[1])
+    strip_copies = fetch([strips_ref], [strips], sems.at[1])
     if not first:
         total_copies = fetch(before, totals, sems.at[2])
     fill_shifted(shifted, arrivals)
@@ -109,11 +109,11 @@
     left[:cols, :] = turned[pl.ds(pl.multiple_of(inside, strip), cols), :]
     for copy in strip_copies:
         copy.wait()
-    for at, pair in enumerate(pairs):
-        layer, other = owners[at]
+    for at, (layer, other, pair) in enumerate(owners):
         owner = (fsdp_at + n_fsdp - 2 * layer) % n_fsdp
         owner = owner + other * (1 - 2 * (owner % 2))
-        left[cols : cols + strip, at * spots : (at + 1) * spots] = strips[pair, owner]
+        owner = owner * n_pair + (factor_at // 2 + n_pair - pair) % n_pair
+        left[cols : cols + strip, at * spots : (at + 1) * spots] = strips[owner]
     if not first:
         for copy in total_copies:
             copy.wait()
@@ -148,14 +148,14 @@
         copy.wait()
 
 
-def add_products(owners, images, pairs, strips, before, cols, rows):
-    n_images, side, channels, strip = len(images), images[0].shape[1], images[0].shape[3], strips[0].shape[1]
+def add_products(owners, images, strips, before, cols, rows):
+    n_images, side, channels, strip = len(images), images[0].shape[1], images[0].shape[3], strips.shape[1]
     spots = side * side
     shapes = [(cols, rows), (strip, rows + LANES)] * 2
-    operands = [*images, *strips, *(before or [])]
-    n_front = n_images + len(strips)
+    operands = [*images, strips, *(before or [])]
+    n_front = n_images + 1
     return pl.pallas_call(
-        lambda *refs: products_kernel(owners, pairs, len(strips), before is None, *refs),
+        lambda *refs: products_kernel(owners, before is None, *refs),
         out_shape=[jax.ShapeDtypeStruct(shape, jnp.float32) for shape in shapes],
         in_specs=[pl.BlockSpec(memory_space=pl.ANY)] * len(operands),
         out_specs=[pl.BlockSpec(memory_space=pl.ANY)] * 4,
@@ -164,7 +164,7 @@
             pltpu.VMEM((3, n_images, side + 2, side, channels), jnp.bfloat16),
             pltpu.VMEM(((cols + strip + LANES - 1) // LANES * LANES, n_images * spots), jnp.bfloat16),
             pltpu.VMEM((cols + strip, n_images * spots), jnp.bfloat16),
-            pltpu.VMEM((len(strips),) + strips[0].shape, jnp.bfloat16),
+            pltpu.VMEM(strips.shape, jnp.bfloat16),
             pltpu.SemaphoreType.DMA((5, max(4, n_images))),
         ],
         input_output_aliases={} if before is None else {n_front + k: k for k in range(4)},
@@ -175,6 +175,27 @@
             transcendentals=0,
         ),
     )(*operands)
+
+
+def scale_kernel(mine_ref, theirs_ref, out_ref):
+    rows = out_ref.shape[1] - LANES
+    largest = mine_ref[:, rows:] + theirs_ref[:, rows:]
+    exponent = jnp.floor(jnp.log2(jnp.maximum(largest, 1e-30))) - 14.0
+    scale = jnp.exp2(-exponent)
+    for at in range(0, rows, LANES):
+        lanes = slice(at, at + LANES)
+        out_ref[:, lanes] = (mine_ref[:, lanes] + theirs_ref[:, lanes]) * scale
+    out_ref[:, rows:] = exponent
+
+
+def scale_strips(mine, theirs):
+    return pl.pallas_call(
+        scale_kernel,
+        out_shape=jax.ShapeDtypeStruct(mine.shape, jnp.float32),
+        in_specs=[pl.BlockSpec(memory_space=pltpu.VMEM)] * 2,
+        out_specs=pl.BlockSpec(memory_space=pltpu.VMEM),
+        compiler_params=pltpu.CompilerParams(vmem_limit_bytes=4 * 1024 * 1024),
+    )(mine, theirs)
 
 
 def tail_kernel(strip, block, layers, *refs):
@@ -394,58 +415,63 @@
     own_cot = cotangent.reshape(-1, channels)
     maps = {("layer", 0, 0): activations}
     plan, ready = gather_plan(n_layer, n_pair)
-    sent = {"layer": [], "side": [], "pair": []}
-    strips_by_pair = []
-    for item, source, link, turn in plan:
-        array = activations if source is None else maps[source]
-        events = sent[link][max(turn - 2, 0) : turn - 1]
-        if link == "pair" and item == [entry[0] for entry in plan if entry[2] == "pair"][-1]:
-            events = events + strips_by_pair
-        maps[item] = transfer(after(array, events), item, link)
-        sent[link].append(maps[item])
-        if link == "side" and turn == 0:
-            strips = after(own_cot, [maps[item]]).T.reshape(n_fsdp, strip, own_cot.shape[0])
-            strips = lax.all_to_all(strips, "fsdp", split_axis=0, concat_axis=0)
-        if link == "pair" and turn == 2:
-            strips_by_pair = [strips] + [
-                over_pair(after(strips, [maps[item]]), step) for step in range(1, n_pair)
-            ]
-    first_event, last_layer = sent["side"][:1], sent["layer"][-1:]
-    near_end, at_end = sent["pair"][-2:-1], sent["pair"][-1:] + sent["side"][-1:]
-
+    images = sorted((item for item in ready if item), key=lambda item: ready[item])
+    half = len(images) // 2
     aligned = rows % LANES == 0 and channels % LANES == 0 and activations.shape[0] == 1
-    images = sorted(maps, key=lambda item: ready[item])
-    half = len(images) // 2
-    totals, early = None, []
-    for batch in (images[:half], images[half:]):
-        owners, pairs = [], []
-        for kind, layer, pair in batch:
-            owner = (fsdp_at - 2 * layer) % n_fsdp
-            owners.append(owner ^ 1 if kind in ("side", "both") else owner)
-            pairs.append(pair)
+
+    def products(batch, totals):
+        owners = [(layer, int(kind in ("side", "both")), pair) for kind, layer, pair in batch]
         if aligned:
-            totals = add_products(
-                [(layer, int(kind in ("side", "both"))) for kind, layer, _ in batch],
-                [maps[item] for item in batch], pairs, strips_by_pair, totals, cols, rows
-            )
-            early = early or [totals[3]]
-            continue
+            arrays = [maps[item] for item in batch]
+            return add_products(owners, arrays, strips, totals, cols, rows)
         for at in range(0, len(batch), 2 * n_pair):
             part = jnp.concatenate([maps[item] for item in batch[at : at + 2 * n_pair]], axis=0)
             col_tile = tile_of_patches(part, fsdp_at * cols, cols)
-            cot_tile = jnp.concatenate(
-                [
-                    lax.dynamic_index_in_dim(strips_by_pair[pair], owner, 0, keepdims=False)
-                    for pair, owner in list(zip(pairs, owners))[at : at + 2 * n_pair]
-                ],
-                axis=1,
-            )
+            cot_list = []
+            for layer, other, pair in owners[at : at + 2 * n_pair]:
+                owner = ((fsdp_at - 2 * layer) % n_fsdp ^ other) * n_pair + (pair_at - pair) % n_pair
+                cot_list.append(lax.dynamic_index_in_dim(strips, owner, 0, keepdims=False))
             more = []
             for tile in (factor_at ^ 1, factor_at):
                 row_tile = tile_of_patches(part, tile * rows, rows)
                 more.append(by_rows(col_tile, row_tile))
-                more.append(jnp.dot(cot_tile, row_tile, preferred_element_type=jnp.float32))
+                more.append(
+                    jnp.dot(
+                        jnp.concatenate(cot_list, axis=1),
+                        row_tile,
+                        preferred_element_type=jnp.float32,
+                    )
+                )
             totals = more if totals is None else [old + new for old, new in zip(totals, more)]
+        return totals
+
+    sent = {"layer": [], "side": [], "pair": []}
+    for item, source, link, turn in plan:
+        if item == plan[-1][0]:
+            totals = products(images[:half], None)
+            early = [totals[3]]
+        array = activations if source is None else maps[source]
+        events = [] if link == "layer" else sent[link][max(turn - 2, 0) : turn - 1]
+        maps[item] = transfer(after(array, events + (early if item == plan[-1][0] else [])), item, link)
+        sent[link].append(maps[item])
+        if link == "side" and turn == 0:
+            strips = after(own_cot, [maps[item]]).T.reshape(n_fsdp, 1, strip, own_cot.shape[0])
+            strips = jnp.broadcast_to(strips, (n_fsdp, n_pair) + strips.shape[2:])
+            groups = [
+                [at * n_factor + 2 * pair + core for at in range(n_fsdp) for pair in range(n_pair)]
+                for core in range(2)
+            ]
+            strips = lax.all_to_all(
+                strips.reshape((n_fsdp * n_pair,) + strips.shape[2:]),
+                ("fsdp", "factor"),
+                split_axis=0,
+                concat_axis=0,
+                axis_index_groups=groups,
+            )
+    first_event, last_layer = sent["side"][:1], sent["layer"][-1:]
+    near_end = sent["pair"][-2:-1]
+    at_end = [maps[plan[-1][0]]] + sent["pair"][-1:]
+    totals = list(products(images[half:], totals))
     if not aligned:
         for at in (1, 3):
             largest = jnp.full((strip, LANES), jnp.max(jnp.abs(totals[at])))
@@ -455,7 +481,7 @@
     g_pairs = lax.dynamic_index_in_dim(g_partial, core_at, 1, keepdims=False) + over_core(
         lax.dynamic_index_in_dim(g_partial, 1 - core_at, 1, keepdims=False)
     )
-    g_pairs = after(g_pairs, near_end)
+    g_pairs = after(g_pairs, early)
     g_sum = lax.dynamic_index_in_dim(g_pairs, pair_at, 0, keepdims=False)
     for step in range(1, n_pair):
         away = lax.dynamic_index_in_dim(g_pairs, (pair_at + step) % n_pair, 0, keepdims=False)
@@ -464,13 +490,15 @@
     near_parts = [lax.dynamic_slice_in_dim(weight_part, factor_at * block, block, 1)]
     distance = 2
     while distance < n_fsdp:
-        both = moved(jnp.stack(near_parts), "fsdp", lambda to, d=distance: to ^ d)
+        both = after(jnp.stack(near_parts), near_end if distance > 2 else [])
+        both = moved(both, "fsdp", lambda to, d=distance: to ^ d)
+        both = after(both, early) if distance > 2 else both
         near_parts = near_parts + [both[k] for k in range(len(near_parts))]
         distance *= 2
     near_stack = jnp.stack(near_parts)
-    far_parts = over_side(after(near_stack, at_end + early))
+    far_parts = over_side(after(near_stack, at_end))
     distance = n_fsdp // 2
-    g_sum = after(g_sum, at_end + early)
+    g_sum = after(g_sum, at_end)
     while distance > 2:
         g_sum = g_sum + moved(g_sum, "fsdp", lambda to, d=distance: to ^ d)
         distance //= 2
@@ -482,11 +510,14 @@
         activations.shape[0] * activations.shape[1] * activations.shape[2] * n_fsdp * n_factor
     )
 
-    largest = totals[3][:, rows : rows + 1] + theirs[:, rows : rows + 1]
-    exponent = jnp.floor(jnp.log2(jnp.maximum(largest, 1e-30))) - 14.0
-    packed = ((totals[3] + theirs)[:, :rows] * jnp.exp2(-exponent)).astype(jnp.float16)
-    exponent = jnp.broadcast_to(exponent.astype(jnp.float16), (strip, LANES))
-    packed = jnp.concatenate([packed, exponent], axis=1)
+    if aligned:
+        packed = scale_strips(totals[3], theirs).astype(jnp.float16)
+    else:
+        largest = totals[3][:, rows : rows + 1] + theirs[:, rows : rows + 1]
+        exponent = jnp.floor(jnp.log2(jnp.maximum(largest, 1e-30))) - 14.0
+        packed = (totals[3] + theirs)[:, :rows] * jnp.exp2(-exponent)
+        exponent = jnp.broadcast_to(exponent, (strip, LANES))
+        packed = jnp.concatenate([packed, exponent], axis=1).astype(jnp.float16)
     near_packed = [packed] + [over_layer(packed, step) for step in range(1, n_layer)]
 
     g_sum = g_sum + over_side(g_sum)
@@ -541,7 +572,7 @@
     ]
     if aligned and block % LANES == 0:
         away, kept = tail_products(
-            after(a_inverse, own_maps[1:n_pair] + own_maps[n_pair + 1 :]),
+            after(a_inverse, [*group_out, g_sum]),
             g_inverse,
             strips_of_grad,
             [(step, other) for other in range(2) for step in range(n_layer)],
@@ -566,7 +597,7 @@
         )
         away, kept = partial[:, : channels // 2], partial[:, channels // 2 :]
     by_pair = kept + over_core(away)
-    cov_own = totals[2] + after(over_core(after(totals[0], [packed])), by_pair)
+    cov_own = totals[2] + after(over_core(after(totals[0], far_packed)), by_pair)
     a_factor = 0.5 * a_factor_old + (0.5 / pixel_total) * cov_own.T
     result = by_pair[:, :block]
     for step in range(1, n_pair):

time: 161 us -> 167 us (1.037)
  waiting for transfers between devices: 51.7 us -> 59.3 us
  other arithmetic: 8.99 us -> 7.04 us
  local copies, waits for them, and re-layouts: 2.84 us -> 4.61 us
    ppermute x40 -> x39, waiting for transfers between devices: 51.7 us -> 59.3 us  [moved(): lax.ppermute(array, axis, [(at, target(at) % count) for at in range(count)])]
    ppermute x40 -> x39, starting transfers between devices: 53.2 us -> 48.3 us  [moved(): lax.ppermute(array, axis, [(at, target(at) % count) for at in range(count)])]
    all_to_all x1, starting transfers between devices: 3.42 us -> 8.29 us  [per_device(): lax.all_to_all(strips.reshape((n_fsdp * n_pair,) + strips.shape[2:]), ('f...]
    unnamed x42, local copies, waits for them, and re-layouts: 0.78 us -> 2.57 us
    pallas_call x2 -> x3, Pallas kernels: 25.7 us -> 25.1 us  [the longest x2 25.1 us: add_products(): pl.pallas_call(lambda *refs: products_kernel(owners, before is None, *ref...]
  transfers between devices with their start and end apart: 41 -> 40, of which waited for: 17 -> 15; matrix products, arithmetic and copies ran while one was open for 7% -> 6% of each run, Pallas kernels for 23% -> 22%
where the time goes in v9:
time: 167 us
  waiting for transfers between devices  59.3 us (36%)
  starting transfers between devices  56.6 us (34%)
  Pallas kernels  36.9 us (22%)
  other arithmetic  7.04 us (4%)
  local copies, waits for them, and re-layouts  4.61 us (3%)
    ppermute x39, waiting for transfers between devices, moved(): lax.ppermute(array, axis, [(at, target(at) % count) for at in range(count)])  59.3 us
    ppermute x39, starting transfers between devices, moved(): lax.ppermute(array, axis, [(at, target(at) % count) for at in range(count)])  48.3 us
    pallas_call x2, Pallas kernels, add_products(): pl.pallas_call(lambda *refs: products_kernel(owners, before is None, *ref...  25.1 us
    all_to_all x1, starting transfers between devices, per_device(): lax.all_to_all(strips.reshape((n_fsdp * n_pair,) + strips.shape[2:]), ('f...  8.29 us
    pallas_call x1, Pallas kernels, tail_products(): pl.pallas_call(lambda *refs: tail_kernel(strip, block, layers, *refs), ou...  5.96 us
    pallas_call x1, Pallas kernels, convolve(): pl.pallas_call(lambda *refs: conv_kernel(n_images, *refs), out_shape=[jax...  5.05 us
  transfers between devices with their start and end apart: 40, of which 15 were waited for; matrix products, arithmetic and copies ran while one was open for 6% of the time, Pallas kernels for 22%

profile of v9, /device:TPU:0, one launch (start us, length us, event | category | flops | bytes accessed | tf_op | source)
XLA Modules:
  0.0 166.9 jit_solution(5339766420522825796)
XLA Ops:
  0.6 3.0 %collective-permute-start.8 = (bf16[1,16,16,512]{3,2,1,0:T(8,128)(2,1)}, bf16[1,16,16,512]{3,2,1,0:T(8,128)(2,1)}, u32[]{:S(2)}, u32[]{:S(2)}) collective-permute-start(bf16[1,16,16,512]{3,2,1,0:T(8,128)(2,1)} %refs_0_.2), channel_id=1, source_target_pairs={{0,4},{4,0},{8,12},{12,8},{16,20},{20,16},{24,28},{28,24},{1,5},{5... | collective-permute-start | bytes 786440 | tf_op jit(solution)/shard_map/ppermute | solution.py:19
  3.6 2.6 %collective-permute-start.1 = (bf16[1,16,16,512]{3,2,1,0:T(8,128)(2,1)}, bf16[1,16,16,512]{3,2,1,0:T(8,128)(2,1)}, u32[]{:S(2)}, u32[]{:S(2)}) collective-permute-start(bf16[1,16,16,512]{3,2,1,0:T(8,128)(2,1)} %refs_0_.2), channel_id=1, source_target_pairs={{0,16},{4,20},{8,24},{12,28},{16,0},{20,4},{24,8},{28,12},{1,17},{... | collective-permute-start | bytes 786440 | tf_op jit(solution)/shard_map/ppermute | solution.py:19
  6.2 1.6 collective-permute-start.2
  7.8 1.5 collective-permute-start
  9.3 2.2 %collective-permute-start.7 = (bf16[1,16,16,512]{3,2,1,0:T(8,128)(2,1)}, bf16[1,16,16,512]{3,2,1,0:T(8,128)(2,1)}, u32[]{:S(2)}, u32[]{:S(2)}) collective-permute-start(bf16[1,16,16,512]{3,2,1,0:T(8,128)(2,1)} %refs_0_.2), channel_id=1, source_target_pairs={{0,24},{4,28},{8,0},{12,4},{16,8},{20,12},{24,16},{28,20},{1,25},{... | collective-permute-start | bytes 786440 | tf_op jit(solution)/shard_map/ppermute | solution.py:19
  11.6 1.1 copy.19
  12.7 0.6 collective-permute-start.10
  13.2 11.8 %collective-permute-done.1.refs_0_ = bf16[1,16,16,512]{3,2,1,0:T(8,128)(2,1)} collective-permute-done((bf16[1,16,16,512]{3,2,1,0:T(8,128)(2,1)}, bf16[1,16,16,512]{3,2,1,0:T(8,128)(2,1)}, u32[]{:S(2)}, u32[]{:S(2)}) %collective-permute-start.1) | collective-permute-done | bytes 262176 | tf_op jit(solution)/shard_map/ppermute | solution.py:19
  25.1 1.6 collective-permute-start.3
  26.7 0.8 broadcast_in_dim.8
  27.5 8.3 %all-to-all-start = ((bf16[16,64,256]{2,1,0:T(8,128)(2,1)}), bf16[16,64,256]{2,1,0:T(8,128)(2,1)S(1)}, u32[]{:S(2)}, u32[]{:S(2)}) async-start(bf16[16,64,256]{2,1,0:T(8,128)(2,1)} %bitcast.3), calls=%async_computation | async-start | bytes 1048576 | tf_op jit(solution)/shard_map/all_to_all | solution.py:464
  35.8 1.2 fusion.1
  37.3 2.0 %collective-permute-start.17 = (bf16[1,576,128]{2,1,0:T(8,128)(2,1)S(1)}, bf16[1,576,128]{2,1,0:T(8,128)(2,1)S(1)}, u32[]{:S(2)}, u32[]{:S(2)}) collective-permute-start(bf16[1,576,128]{2,1,0:T(8,128)(2,1)S(1)} %dynamic-slice_bitcast_fusion.2), channel_id=1, source_target_pairs={{0,8},{4,12},{8,0},{12,4},{16,24},{20,28},{24,16},{28,20},{1,9},{5... | collective-permute-start | bytes 442376 | tf_op jit(solution)/shard_map/ppermute | solution.py:19
  39.3 1.5 collective-permute-start.12
  40.7 0.6 collective-permute-start.9
  41.3 1.5 collective-permute-start.11
  42.8 6.8 %collective-permute-done.17 = bf16[1,576,128]{2,1,0:T(8,128)(2,1)S(1)} collective-permute-done((bf16[1,576,128]{2,1,0:T(8,128)(2,1)S(1)}, bf16[1,576,128]{2,1,0:T(8,128)(2,1)S(1)}, u32[]{:S(2)}, u32[]{:S(2)}) %collective-permute-start.17) | collective-permute-done | bytes 147488 | tf_op jit(solution)/shard_map/ppermute | solution.py:19
  49.6 1.5 collective-permute-start.4
  51.0 0.7 pad_maximum_fusion.1
  51.8 1.2 collective-permute-start.13
  53.0 3.7 %collective-permute-done.9.refs_1_ = bf16[1,16,16,512]{3,2,1,0:T(8,128)(2,1)} collective-permute-done((bf16[1,16,16,512]{3,2,1,0:T(8,128)(2,1)}, bf16[1,16,16,512]{3,2,1,0:T(8,128)(2,1)}, u32[]{:S(2)}, u32[]{:S(2)}) %collective-permute-start.9) | collective-permute-done | bytes 262176 | tf_op jit(solution)/shard_map/ppermute | solution.py:19
  56.7 1.5 collective-permute-start.15
  58.4 2.5 %collective-permute-start.18 = (bf16[2,576,128]{2,1,0:T(8,128)(2,1)}, bf16[2,576,128]{2,1,0:T(8,128)(2,1)}, u32[]{:S(2)}, u32[]{:S(2)}) collective-permute-start(bf16[2,576,128]{2,1,0:T(8,128)(2,1)} %pad_maximum_fusion.1), channel_id=1, source_target_pairs={{0,16},{4,20},{8,24},{12,28},{16,0},{20,4},{24,8},{28,12},{1,17},{... | collective-permute-start | bytes 884744 | tf_op jit(solution)/shard_map/ppermute | solution.py:19
  61.0 0.8 copy-done.8
  61.8 12.3 %shard_map.102 = (f32[576,1152]{1,0:T(8,128)}, f32[64,1280]{1,0:T(8,128)}, f32[576,1152]{1,0:T(8,128)}, f32[64,1280]{1,0:T(8,128)}) custom-call(bf16[1,16,16,512]{3,2,1,0:T(8,128)(2,1)} %refs_0_.2, bf16[1,16,16,512]{3,2,1,0:T(8,128)(2,1)} %collective-permute-done.8.refs_1_, bf16[1,16,16,512]{3,2,1,0:T(8,128)(2,1)} %copy-done.13, ...), custom_call_target="tpu_custom_call" | custom-call | flops 6039797760 | bytes 11796480 | tf_op jit(solution)/shard_map/pallas_call | solution.py:157
  74.1 1.6 collective-permute-start.16
  75.8 1.4 collective-permute-start.21
  77.2 0.3 collective-permute-start.14
  77.4 1.0 pad_maximum_fusion.refs_4_
  78.5 0.6 collective-permute-start.6
  79.1 4.7 %collective-permute-done.16.refs_7_ = bf16[1,16,16,512]{3,2,1,0:T(8,128)(2,1)} collective-permute-done((bf16[1,16,16,512]{3,2,1,0:T(8,128)(2,1)}, bf16[1,16,16,512]{3,2,1,0:T(8,128)(2,1)}, u32[]{:S(2)}, u32[]{:S(2)}) %collective-permute-start.16) | collective-permute-done | bytes 262176 | tf_op jit(solution)/shard_map/ppermute | solution.py:19
  83.8 1.5 collective-permute-start.19
  85.3 0.5 collective-permute-start.22
  85.8 3.5 %collective-permute-done.14.refs_5_ = bf16[1,16,16,512]{3,2,1,0:T(8,128)(2,1)S(1)} collective-permute-done((bf16[1,16,16,512]{3,2,1,0:T(8,128)(2,1)}, bf16[1,16,16,512]{3,2,1,0:T(8,128)(2,1)S(1)}, u32[]{:S(2)}, u32[]{:S(2)}) %collective-permute-start.14) | collective-permute-done | bytes 262176 | tf_op jit(solution)/shard_map/ppermute | solution.py:19
  89.3 0.7 copy-done.17
  90.0 12.8 %shard_map.103 = (f32[576,1152]{1,0:T(8,128)}, f32[64,1280]{1,0:T(8,128)}, f32[576,1152]{1,0:T(8,128)}, f32[64,1280]{1,0:T(8,128)}) custom-call(bf16[1,16,16,512]{3,2,1,0:T(8,128)(2,1)} %collective-permute-done.1.refs_0_, ...), custom_call_target="tpu_custom_call", output_to_operand_aliasing={{0}: (9, {}), {1}: (10, {}), {2}: (11, {}), {3}: (12, {})} | custom-call | flops 6039797760 | bytes 11796480 | tf_op jit(solution)/shard_map/pallas_call | solution.py:157
  103.0 1.6 collective-permute-start.25
  104.6 7.1 %collective-permute-done.25 = f32[128,512]{1,0:T(8,128)S(1)} collective-permute-done((f32[128,512]{1,0:T(8,128)S(1)}, f32[128,512]{1,0:T(8,128)S(1)}, u32[]{:S(2)}, u32[]{:S(2)}) %collective-permute-start.25) | collective-permute-done | bytes 262176 | tf_op jit(solution)/shard_map/ppermute | solution.py:19
  111.7 1.0 copy-done.1
  112.9 1.6 collective-permute-start.32
  114.5 0.4 collective-permute-start.30
  114.9 0.7 collective-permute-start.29
  115.6 3.1 %collective-permute-start.24 = (f16[64,1280]{1,0:T(8,128)(2,1)S(1)}, f16[64,1280]{1,0:T(8,128)(2,1)S(1)}, u32[]{:S(2)}, u32[]{:S(2)}) collective-permute-start(f16[64,1280]{1,0:T(8,128)(2,1)S(1)} %convert_element_type.54), channel_id=1, source_target_pairs={{0,24},{4,28},{8,0},{12,4},{16,8},{20,12},{24,16},{28,20},{1,25},{... | collective-permute-start | bytes 491528 | tf_op jit(solution)/shard_map/ppermute | solution.py:19
  118.8 6.6 %collective-permute-done.29 = f16[64,1280]{1,0:T(8,128)(2,1)S(1)} collective-permute-done((f16[64,1280]{1,0:T(8,128)(2,1)S(1)}, f16[64,1280]{1,0:T(8,128)(2,1)S(1)}, u32[]{:S(2)}, u32[]{:S(2)}) %collective-permute-start.29) | collective-permute-done | bytes 163872 | tf_op jit(solution)/shard_map/ppermute | solution.py:19
  125.5 0.8 collective-permute-start.33
  126.3 1.9 %collective-permute-done.24 = f16[64,1280]{1,0:T(8,128)(2,1)S(1)} collective-permute-done((f16[64,1280]{1,0:T(8,128)(2,1)S(1)}, f16[64,1280]{1,0:T(8,128)(2,1)S(1)}, u32[]{:S(2)}, u32[]{:S(2)}) %collective-permute-start.24) | collective-permute-done | bytes 163872 | tf_op jit(solution)/shard_map/ppermute | solution.py:19
  128.2 5.1 %shard_map.105 = (bf16[1,16,16,128]{3,2,1,0:T(8,128)(2,1)}, bf16[1,16,16,128]{3,2,1,0:T(8,128)(2,1)}, bf16[1,16,16,128]{3,2,1,0:T(8,128)(2,1)}, bf16[1,16,16,128]{3,2,1,0:T(8,128)(2,1)}) custom-call(bf16[1,16,16,512]{3,2,1,0:T(8,128)(2,1)} %refs_0_.2, bf16[1,16,16,512]{3,2,1,0:T(8,128)(2,1)} %copy-done.13, bf16[1,16,16,512]{3,2,1,0:T(8,128)(2,1)} %copy-done.15, ...), custom_call_target="tpu_custom_call" | custom-call | flops 2415919104 | bytes 2228224 | tf_op jit(solution)/shard_map/pallas_call | solution.py:311
  133.3 0.6 collective-permute-start.34
  133.9 1.5 collective-permute-start.35
  135.4 3.2 %collective-permute-start.31 = (f32[128,512]{1,0:T(8,128)S(1)}, f32[128,512]{1,0:T(8,128)S(1)}, u32[]{:S(2)}, u32[]{:S(2)}) collective-permute-start(f32[128,512]{1,0:T(8,128)S(1)} %add.71), channel_id=1, source_target_pairs={{0,8},{4,12},{8,0},{12,4},{16,24},{20,28},{24,16},{28,20},{1,9},{5... | collective-permute-start | bytes 786440 | tf_op jit(solution)/shard_map/ppermute | solution.py:19
  139.5 0.9 collective-permute-done.34
  140.3 1.8 %collective-permute-done.35 = f16[64,1280]{1,0:T(8,128)(2,1)S(1)} collective-permute-done((f16[64,1280]{1,0:T(8,128)(2,1)S(1)}, f16[64,1280]{1,0:T(8,128)(2,1)S(1)}, u32[]{:S(2)}, u32[]{:S(2)}) %collective-permute-start.35) | collective-permute-done | bytes 163872 | tf_op jit(solution)/shard_map/ppermute | solution.py:19
  142.7 1.7 %collective-permute-done.31 = f32[128,512]{1,0:T(8,128)S(1)} collective-permute-done((f32[128,512]{1,0:T(8,128)S(1)}, f32[128,512]{1,0:T(8,128)S(1)}, u32[]{:S(2)}, u32[]{:S(2)}) %collective-permute-start.31) | collective-permute-done | bytes 262176 | tf_op jit(solution)/shard_map/ppermute | solution.py:19
  144.5 0.8 add_multiply_fusion
  145.3 6.0 %shard_map.106 = (f32[576,256]{1,0:T(8,128)S(1)}, f32[576,256]{1,0:T(8,128)S(1)}) custom-call(f32[576,1152]{1,0:T(8,128)S(1)} %copy-done.3, f32[512,512]{1,0:T(8,128)S(1)} %copy-done.4, f32[64,1152]{1,0:T(8,128)S(1)} %convert_multiply_fusion.7.refs_2_, f32[64,1152]{1,0:T(8,128)S(1)} %convert_multiply_fusion.6.refs_3_, ...), custom_call_target="tpu_custom_call" | custom-call | flops 2944401408 | bytes 3833856 | tf_op jit(solution)/shard_map/pallas_call | solution.py:255
  151.4 1.5 collective-permute-start.26
  153.0 0.5 collective-permute-start.28
  153.7 2.2 %collective-permute-done.26.refs_1_ = bf16[1,16,16,128]{3,2,1,0:T(8,128)(2,1)S(1)} collective-permute-done((bf16[1,16,16,128]{3,2,1,0:T(8,128)(2,1)S(1)}, bf16[1,16,16,128]{3,2,1,0:T(8,128)(2,1)S(1)}, u32[]{:S(2)}, u32[]{:S(2)}) %collective-permute-start.26) | collective-permute-done | bytes 65568 | tf_op jit(solution)/shard_map/ppermute | solution.py:19
  155.9 1.1 collective-permute-done.28.refs_3_
  157.0 1.3 collective-permute-start.38
  158.2 0.8 shard_map.107
  159.0 1.9 %bitcast_add_fusion = f32[1152,576]{0,1:T(8,128)} fusion(f32[576,1152]{1,0:T(8,128)S(1)} %copy-done.6, f32[576,1152]{1,0:T(8,128)S(1)} %collective-permute-done.37, f32[1152,576]{0,1:T(8,128)S(1)} %copy-done.5), kind=kLoop, calls=%fused_computation | loop fusion | flops 2654208 | bytes 10616832 | tf_op jit(solution)/shard_map/add | solution.py:601
  160.9 5.3 %collective-permute-done.38 = f32[576,128]{1,0:T(8,128)S(1)} collective-permute-done((f32[576,128]{1,0:T(8,128)S(1)}, f32[576,128]{1,0:T(8,128)S(1)}, u32[]{:S(2)}, u32[]{:S(2)}) %collective-permute-start.38) | collective-permute-done | bytes 294944 | tf_op jit(solution)/shard_map/ppermute | solution.py:19
  166.2 0.7 fusion
  (98 shorter events, 2.9 us)
Async XLA Ops:
  0.6 36.6 %copy-start = (bf16[576,512]{1,0:T(8,128)(2,1)S(1)}, bf16[576,512]{1,0:T(8,128)(2,1)}, u32[]{:S(2)}) copy-start(bf16[576,512]{1,0:T(8,128)(2,1)} %param.9) | copy-start | bytes 1769476
  0.6 10.9 %collective-permute-start.8 = (bf16[1,16,16,512]{3,2,1,0:T(8,128)(2,1)}, bf16[1,16,16,512]{3,2,1,0:T(8,128)(2,1)}, u32[]{:S(2)}, u32[]{:S(2)}) collective-permute-start(bf16[1,16,16,512]{3,2,1,0:T(8,128)(2,1)} %refs_0_.2), channel_id=1, source_target_pairs={{0,4},{4,0},{8,12},{12,8},{16,20},{20,16},{24,28},{28,24},{1,5},{5... | collective-permute-start | bytes 786440 | tf_op jit(solution)/shard_map/ppermute | solution.py:19
  3.6 21.4 %collective-permute-start.1 = (bf16[1,16,16,512]{3,2,1,0:T(8,128)(2,1)}, bf16[1,16,16,512]{3,2,1,0:T(8,128)(2,1)}, u32[]{:S(2)}, u32[]{:S(2)}) collective-permute-start(bf16[1,16,16,512]{3,2,1,0:T(8,128)(2,1)} %refs_0_.2), channel_id=1, source_target_pairs={{0,16},{4,20},{8,24},{12,28},{16,0},{20,4},{24,8},{28,12},{1,17},{... | collective-permute-start | bytes 786440 | tf_op jit(solution)/shard_map/ppermute | solution.py:19
  6.2 18.9 %collective-permute-start.2 = (bf16[1,16,16,512]{3,2,1,0:T(8,128)(2,1)}, bf16[1,16,16,512]{3,2,1,0:T(8,128)(2,1)}, u32[]{:S(2)}, u32[]{:S(2)}) collective-permute-start(bf16[1,16,16,512]{3,2,1,0:T(8,128)(2,1)} %refs_0_.2), channel_id=1, source_target_pairs={{0,8},{4,12},{8,16},{12,20},{16,24},{20,28},{24,0},{28,4},{1,9},{5... | collective-permute-start | bytes 786440 | tf_op jit(solution)/shard_map/ppermute | solution.py:19
  7.8 17.3 %collective-permute-start = (bf16[1,16,16,512]{3,2,1,0:T(8,128)(2,1)}, bf16[1,16,16,512]{3,2,1,0:T(8,128)(2,1)S(1)}, u32[]{:S(2)}, u32[]{:S(2)}) collective-permute-start(bf16[1,16,16,512]{3,2,1,0:T(8,128)(2,1)} %refs_0_.2), channel_id=1, source_target_pairs={{0,2},{1,3},{2,0},{3,1},{4,6},{5,7},{6,4},{7,5},{8,10},{9,11},{10,... | collective-permute-start | bytes 786440 | tf_op jit(solution)/shard_map/ppermute | solution.py:19
  9.3 29.9 %collective-permute-start.7 = (bf16[1,16,16,512]{3,2,1,0:T(8,128)(2,1)}, bf16[1,16,16,512]{3,2,1,0:T(8,128)(2,1)}, u32[]{:S(2)}, u32[]{:S(2)}) collective-permute-start(bf16[1,16,16,512]{3,2,1,0:T(8,128)(2,1)} %refs_0_.2), channel_id=1, source_target_pairs={{0,24},{4,28},{8,0},{12,4},{16,8},{20,12},{24,16},{28,20},{1,25},{... | collective-permute-start | bytes 786440 | tf_op jit(solution)/shard_map/ppermute | solution.py:19
  12.7 28.1 %collective-permute-start.10 = (bf16[1,16,16,512]{3,2,1,0:T(8,128)(2,1)}, bf16[1,16,16,512]{3,2,1,0:T(8,128)(2,1)}, u32[]{:S(2)}, u32[]{:S(2)}) collective-permute-start(bf16[1,16,16,512]{3,2,1,0:T(8,128)(2,1)} %collective-permute-done.8.refs_1_), channel_id=1, source_target_pairs={{0,2},{1,3},{2,0},{3,1},{4,6},{5,7},{6,4},{7,5},{8,10},{9,11},{10,... | collective-permute-start | bytes 786440 | tf_op jit(solution)/shard_map/ppermute | solution.py:19
  25.1 10.7 %copy-start.13 = (bf16[1,16,16,512]{3,2,1,0:T(8,128)(2,1)}, bf16[1,16,16,512]{3,2,1,0:T(8,128)(2,1)S(1)}, u32[]{:S(2)}) copy-start(bf16[1,16,16,512]{3,2,1,0:T(8,128)(2,1)S(1)} %collective-permute-done.refs_2_.refs_1_) | copy-start | bytes 786436
  25.1 16.2 %collective-permute-start.3 = (bf16[1,16,16,512]{3,2,1,0:T(8,128)(2,1)}, bf16[1,16,16,512]{3,2,1,0:T(8,128)(2,1)}, u32[]{:S(2)}, u32[]{:S(2)}) collective-permute-start(bf16[1,16,16,512]{3,2,1,0:T(8,128)(2,1)} %collective-permute-done.2.refs_3_), channel_id=1, source_target_pairs={{0,2},{1,3},{2,0},{3,1},{4,6},{5,7},{6,4},{7,5},{8,10},{9,11},{10,... | collective-permute-start | bytes 786440 | tf_op jit(solution)/shard_map/ppermute | solution.py:19
  27.5 33.5 %all-to-all-start = ((bf16[16,64,256]{2,1,0:T(8,128)(2,1)}), bf16[16,64,256]{2,1,0:T(8,128)(2,1)S(1)}, u32[]{:S(2)}, u32[]{:S(2)}) async-start(bf16[16,64,256]{2,1,0:T(8,128)(2,1)} %bitcast.3), calls=%async_computation | async-start | bytes 1048576 | tf_op jit(solution)/shard_map/all_to_all | solution.py:464
  37.1 23.7 %collective-permute-start.20 = (f32[2,128,512]{2,1,0:T(8,128)S(1)}, f32[2,128,512]{2,1,0:T(8,128)S(1)}, u32[]{:S(2)}, u32[]{:S(2)}) collective-permute-start(f32[2,128,512]{2,1,0:T(8,128)S(1)} %dynamic-slice_bitcast_fusion), channel_id=1, source_target_pairs={{0,1},{1,0},{2,3},{3,2},{4,5},{5,4},{6,7},{7,6},{8,9},{9,8},{10,11... | collective-permute-start | bytes 1572872 | tf_op jit(solution)/shard_map/ppermute | solution.py:19
  37.3 12.3 %collective-permute-start.17 = (bf16[1,576,128]{2,1,0:T(8,128)(2,1)S(1)}, bf16[1,576,128]{2,1,0:T(8,128)(2,1)S(1)}, u32[]{:S(2)}, u32[]{:S(2)}) collective-permute-start(bf16[1,576,128]{2,1,0:T(8,128)(2,1)S(1)} %dynamic-slice_bitcast_fusion.2), channel_id=1, source_target_pairs={{0,8},{4,12},{8,0},{12,4},{16,24},{20,28},{24,16},{28,20},{1,9},{5... | collective-permute-start | bytes 442376 | tf_op jit(solution)/shard_map/ppermute | solution.py:19
  39.3 12.5 %collective-permute-start.12 = (bf16[1,16,16,512]{3,2,1,0:T(8,128)(2,1)}, bf16[1,16,16,512]{3,2,1,0:T(8,128)(2,1)}, u32[]{:S(2)}, u32[]{:S(2)}) collective-permute-start(bf16[1,16,16,512]{3,2,1,0:T(8,128)(2,1)} %collective-permute-done.2.refs_3_), channel_id=1, source_target_pairs={{0,4},{4,0},{8,12},{12,8},{16,20},{20,16},{24,28},{28,24},{1,5},{5... | collective-permute-start | bytes 786440 | tf_op jit(solution)/shard_map/ppermute | solution.py:19
  40.7 16.0 %collective-permute-start.9 = (bf16[1,16,16,512]{3,2,1,0:T(8,128)(2,1)}, bf16[1,16,16,512]{3,2,1,0:T(8,128)(2,1)}, u32[]{:S(2)}, u32[]{:S(2)}) collective-permute-start(bf16[1,16,16,512]{3,2,1,0:T(8,128)(2,1)} %collective-permute-done.7.refs_4_), channel_id=1, source_target_pairs={{0,4},{4,0},{8,12},{12,8},{16,20},{20,16},{24,28},{28,24},{1,5},{5... | collective-permute-start | bytes 786440 | tf_op jit(solution)/shard_map/ppermute | solution.py:19
  41.3 15.4 %collective-permute-start.11 = (bf16[1,16,16,512]{3,2,1,0:T(8,128)(2,1)}, bf16[1,16,16,512]{3,2,1,0:T(8,128)(2,1)}, u32[]{:S(2)}, u32[]{:S(2)}) collective-permute-start(bf16[1,16,16,512]{3,2,1,0:T(8,128)(2,1)} %collective-permute-done.7.refs_4_), channel_id=1, source_target_pairs={{0,2},{1,3},{2,0},{3,1},{4,6},{5,7},{6,4},{7,5},{8,10},{9,11},{10,... | collective-permute-start | bytes 786440 | tf_op jit(solution)/shard_map/ppermute | solution.py:19
  49.6 8.8 %collective-permute-start.4 = (bf16[1,16,16,512]{3,2,1,0:T(8,128)(2,1)}, bf16[1,16,16,512]{3,2,1,0:T(8,128)(2,1)}, u32[]{:S(2)}, u32[]{:S(2)}) collective-permute-start(bf16[1,16,16,512]{3,2,1,0:T(8,128)(2,1)} %collective-permute-done.1.refs_0_), channel_id=1, source_target_pairs={{0,2},{1,3},{2,0},{3,1},{4,6},{5,7},{6,4},{7,5},{8,10},{9,11},{10,... | collective-permute-start | bytes 786440 | tf_op jit(solution)/shard_map/ppermute | solution.py:19
  51.8 22.3 %collective-permute-start.13 = (bf16[1,16,16,512]{3,2,1,0:T(8,128)(2,1)}, bf16[1,16,16,512]{3,2,1,0:T(8,128)(2,1)}, u32[]{:S(2)}, u32[]{:S(2)}) collective-permute-start(bf16[1,16,16,512]{3,2,1,0:T(8,128)(2,1)} %collective-permute-done.1.refs_0_), channel_id=1, source_target_pairs={{0,4},{4,0},{8,12},{12,8},{16,20},{20,16},{24,28},{28,24},{1,5},{5... | collective-permute-start | bytes 786440 | tf_op jit(solution)/shard_map/ppermute | solution.py:19
  56.7 21.8 %collective-permute-start.15 = (bf16[1,16,16,512]{3,2,1,0:T(8,128)(2,1)}, bf16[1,16,16,512]{3,2,1,0:T(8,128)(2,1)}, u32[]{:S(2)}, u32[]{:S(2)}) collective-permute-start(bf16[1,16,16,512]{3,2,1,0:T(8,128)(2,1)} %collective-permute-done.9.refs_1_), channel_id=1, source_target_pairs={{0,2},{1,3},{2,0},{3,1},{4,6},{5,7},{6,4},{7,5},{8,10},{9,11},{10,... | collective-permute-start | bytes 786440 | tf_op jit(solution)/shard_map/ppermute | solution.py:19
  58.4 19.0 %collective-permute-start.18 = (bf16[2,576,128]{2,1,0:T(8,128)(2,1)}, bf16[2,576,128]{2,1,0:T(8,128)(2,1)}, u32[]{:S(2)}, u32[]{:S(2)}) collective-permute-start(bf16[2,576,128]{2,1,0:T(8,128)(2,1)} %pad_maximum_fusion.1), channel_id=1, source_target_pairs={{0,16},{4,20},{8,24},{12,28},{16,0},{20,4},{24,8},{28,12},{1,17},{... | collective-permute-start | bytes 884744 | tf_op jit(solution)/shard_map/ppermute | solution.py:19
  61.0 16.5 %copy-start.12 = (bf16[1,16,16,512]{3,2,1,0:T(8,128)(2,1)S(1)}, bf16[1,16,16,512]{3,2,1,0:T(8,128)(2,1)}, u32[]{:S(2)}) copy-start(bf16[1,16,16,512]{3,2,1,0:T(8,128)(2,1)} %refs_0_.2) | copy-start | bytes 786436
  61.0 17.5 %copy-start.14 = (bf16[1,16,16,512]{3,2,1,0:T(8,128)(2,1)S(1)}, bf16[1,16,16,512]{3,2,1,0:T(8,128)(2,1)}, u32[]{:S(2)}) copy-start(bf16[1,16,16,512]{3,2,1,0:T(8,128)(2,1)} %copy-done.13) | copy-start | bytes 786436
  61.0 0.8 copy-start.8
  74.1 9.6 %collective-permute-start.16 = (bf16[1,16,16,512]{3,2,1,0:T(8,128)(2,1)}, bf16[1,16,16,512]{3,2,1,0:T(8,128)(2,1)}, u32[]{:S(2)}, u32[]{:S(2)}) collective-permute-start(bf16[1,16,16,512]{3,2,1,0:T(8,128)(2,1)} %collective-permute-done.4.refs_4_), channel_id=1, source_target_pairs={{0,4},{4,0},{8,12},{12,8},{16,20},{20,16},{24,28},{28,24},{1,5},{5... | collective-permute-start | bytes 786440 | tf_op jit(solution)/shard_map/ppermute | solution.py:19
  75.8 9.5 %collective-permute-start.21 = (f32[128,512]{1,0:T(8,128)S(1)}, f32[128,512]{1,0:T(8,128)S(1)}, u32[]{:S(2)}, u32[]{:S(2)}) collective-permute-start(f32[128,512]{1,0:T(8,128)S(1)} %dynamic-slice_bitcast_fusion.1), channel_id=1, source_target_pairs={{0,2},{1,3},{2,0},{3,1},{4,6},{5,7},{6,4},{7,5},{8,10},{9,11},{10,... | collective-permute-start | bytes 786440 | tf_op jit(solution)/shard_map/ppermute | solution.py:19
  77.2 12.1 %collective-permute-start.14 = (bf16[1,16,16,512]{3,2,1,0:T(8,128)(2,1)}, bf16[1,16,16,512]{3,2,1,0:T(8,128)(2,1)S(1)}, u32[]{:S(2)}, u32[]{:S(2)}) collective-permute-start(bf16[1,16,16,512]{3,2,1,0:T(8,128)(2,1)} %collective-permute-done.3.refs_7_), channel_id=1, source_target_pairs={{0,4},{4,0},{8,12},{12,8},{16,20},{20,16},{24,28},{28,24},{1,5},{5... | collective-permute-start | bytes 786440 | tf_op jit(solution)/shard_map/ppermute | solution.py:19
  77.4 25.4 %collective-permute-start.5 = (bf16[1,16,16,512]{3,2,1,0:T(8,128)(2,1)S(1)}, bf16[1,16,16,512]{3,2,1,0:T(8,128)(2,1)S(1)}, u32[]{:S(2)}, u32[]{:S(2)}) collective-permute-start(bf16[1,16,16,512]{3,2,1,0:T(8,128)(2,1)S(1)} %copy-done.12), channel_id=1, source_target_pairs={{0,1},{1,0},{2,3},{3,2},{4,5},{5,4},{6,7},{7,6},{8,9},{9,8},{10,11... | collective-permute-start | bytes 786440 | tf_op jit(solution)/shard_map/ppermute | solution.py:19
  78.5 24.3 %copy-start.7 = (bf16[4,576,128]{2,1,0:T(8,128)(2,1)}, bf16[4,576,128]{2,1,0:T(8,128)(2,1)S(1)}, u32[]{:S(2)}) copy-start(bf16[4,576,128]{2,1,0:T(8,128)(2,1)S(1)} %pad_maximum_fusion.refs_4_) | copy-start | bytes 1769476
  78.5 24.3 %collective-permute-start.6 = (bf16[1,16,16,512]{3,2,1,0:T(8,128)(2,1)S(1)}, bf16[1,16,16,512]{3,2,1,0:T(8,128)(2,1)S(1)}, u32[]{:S(2)}, u32[]{:S(2)}) collective-permute-start(bf16[1,16,16,512]{3,2,1,0:T(8,128)(2,1)S(1)} %copy-done.14), channel_id=1, source_target_pairs={{0,1},{1,0},{2,3},{3,2},{4,5},{5,4},{6,7},{7,6},{8,9},{9,8},{10,11... | collective-permute-start | bytes 786440 | tf_op jit(solution)/shard_map/ppermute | solution.py:19
  83.8 19.1 %collective-permute-start.19 = (bf16[4,576,128]{2,1,0:T(8,128)(2,1)S(1)}, bf16[4,576,128]{2,1,0:T(8,128)(2,1)S(1)}, u32[]{:S(2)}, u32[]{:S(2)}) collective-permute-start(bf16[4,576,128]{2,1,0:T(8,128)(2,1)S(1)} %pad_maximum_fusion.refs_4_), channel_id=1, source_target_pairs={{0,4},{4,0},{8,12},{12,8},{16,20},{20,16},{24,28},{28,24},{1,5},{5... | collective-permute-start | bytes 1769480 | tf_op jit(solution)/shard_map/ppermute | solution.py:19
  85.3 17.4 %collective-permute-start.22 = (f32[128,512]{1,0:T(8,128)S(1)}, f32[128,512]{1,0:T(8,128)S(1)}, u32[]{:S(2)}, u32[]{:S(2)}) collective-permute-start(f32[128,512]{1,0:T(8,128)S(1)} %bitcast_add_fusion.2), channel_id=1, source_target_pairs={{0,16},{4,20},{8,24},{12,28},{16,0},{20,4},{24,8},{28,12},{1,17},{... | collective-permute-start | bytes 786440 | tf_op jit(solution)/shard_map/ppermute | solution.py:19
  89.3 0.7 copy-start.17
  102.8 25.4 %copy-start.15 = (bf16[1,16,16,512]{3,2,1,0:T(8,128)(2,1)}, bf16[1,16,16,512]{3,2,1,0:T(8,128)(2,1)S(1)}, u32[]{:S(2)}) copy-start(bf16[1,16,16,512]{3,2,1,0:T(8,128)(2,1)S(1)} %collective-permute-done.5.refs_2_) | copy-start | bytes 786436
  102.8 15.9 %copy-start.16 = (bf16[1,16,16,512]{3,2,1,0:T(8,128)(2,1)}, bf16[1,16,16,512]{3,2,1,0:T(8,128)(2,1)S(1)}, u32[]{:S(2)}) copy-start(bf16[1,16,16,512]{3,2,1,0:T(8,128)(2,1)S(1)} %collective-permute-done.6.refs_3_) | copy-start | bytes 786436
  102.9 25.3 %copy-start.11 = (bf16[4,576,128]{2,1,0:T(8,128)(2,1)}, bf16[4,576,128]{2,1,0:T(8,128)(2,1)S(1)}, u32[]{:S(2)}) copy-start(bf16[4,576,128]{2,1,0:T(8,128)(2,1)S(1)} %collective-permute-done.19.refs_5_) | copy-start | bytes 1769476
  102.9 8.8 %collective-permute-start.23 = (f32[64,1280]{1,0:T(8,128)}, f32[64,1280]{1,0:T(8,128)S(1)}, u32[]{:S(2)}, u32[]{:S(2)}) collective-permute-start(f32[64,1280]{1,0:T(8,128)} %get-tuple-element.74), channel_id=1, source_target_pairs={{0,1},{1,0},{2,3},{3,2},{4,5},{5,4},{6,7},{7,6},{8,9},{9,8},{10,11... | collective-permute-start | bytes 983048 | tf_op jit(solution)/shard_map/ppermute | solution.py:19
  103.0 8.7 %collective-permute-start.25 = (f32[128,512]{1,0:T(8,128)S(1)}, f32[128,512]{1,0:T(8,128)S(1)}, u32[]{:S(2)}, u32[]{:S(2)}) collective-permute-start(f32[128,512]{1,0:T(8,128)S(1)} %add.70), channel_id=1, source_target_pairs={{0,4},{4,0},{8,12},{12,8},{16,20},{20,16},{24,28},{28,24},{1,5},{5... | collective-permute-start | bytes 786440 | tf_op jit(solution)/shard_map/ppermute | solution.py:19
  111.7 1.0 copy-start.1
  112.9 26.0 %collective-permute-start.32 = (f16[64,1280]{1,0:T(8,128)(2,1)S(1)}, f16[64,1280]{1,0:T(8,128)(2,1)S(1)}, u32[]{:S(2)}, u32[]{:S(2)}) collective-permute-start(f16[64,1280]{1,0:T(8,128)(2,1)S(1)} %convert_element_type.54), channel_id=1, source_target_pairs={{0,4},{4,0},{8,12},{12,8},{16,20},{20,16},{24,28},{28,24},{1,5},{5... | collective-permute-start | bytes 491528 | tf_op jit(solution)/shard_map/ppermute | solution.py:19
  114.5 13.7 %collective-permute-start.30 = (f16[64,1280]{1,0:T(8,128)(2,1)S(1)}, f16[64,1280]{1,0:T(8,128)(2,1)S(1)}, u32[]{:S(2)}, u32[]{:S(2)}) collective-permute-start(f16[64,1280]{1,0:T(8,128)(2,1)S(1)} %convert_element_type.54), channel_id=1, source_target_pairs={{0,16},{4,20},{8,24},{12,28},{16,0},{20,4},{24,8},{28,12},{1,17},{... | collective-permute-start | bytes 491528 | tf_op jit(solution)/shard_map/ppermute | solution.py:19
  114.9 10.6 %collective-permute-start.29 = (f16[64,1280]{1,0:T(8,128)(2,1)S(1)}, f16[64,1280]{1,0:T(8,128)(2,1)S(1)}, u32[]{:S(2)}, u32[]{:S(2)}) collective-permute-start(f16[64,1280]{1,0:T(8,128)(2,1)S(1)} %convert_element_type.54), channel_id=1, source_target_pairs={{0,8},{4,12},{8,16},{12,20},{16,24},{20,28},{24,0},{28,4},{1,9},{5... | collective-permute-start | bytes 491528 | tf_op jit(solution)/shard_map/ppermute | solution.py:19
  115.6 12.5 %collective-permute-start.24 = (f16[64,1280]{1,0:T(8,128)(2,1)S(1)}, f16[64,1280]{1,0:T(8,128)(2,1)S(1)}, u32[]{:S(2)}, u32[]{:S(2)}) collective-permute-start(f16[64,1280]{1,0:T(8,128)(2,1)S(1)} %convert_element_type.54), channel_id=1, source_target_pairs={{0,24},{4,28},{8,0},{12,4},{16,8},{20,12},{24,16},{28,20},{1,25},{... | collective-permute-start | bytes 491528 | tf_op jit(solution)/shard_map/ppermute | solution.py:19
  118.8 23.3 %copy-start.10 = (f32[576,1152]{1,0:T(8,128)S(1)}, f32[576,1152]{1,0:T(8,128)}, u32[]{:S(2)}) copy-start(f32[576,1152]{1,0:T(8,128)} %get-tuple-element.95) | copy-start | bytes 7962628
  125.5 14.0 %collective-permute-start.33 = (f16[64,1280]{1,0:T(8,128)(2,1)S(1)}, f16[64,1280]{1,0:T(8,128)(2,1)S(1)}, u32[]{:S(2)}, u32[]{:S(2)}) collective-permute-start(f16[64,1280]{1,0:T(8,128)(2,1)S(1)} %collective-permute-done.29), channel_id=1, source_target_pairs={{0,4},{4,0},{8,12},{12,8},{16,20},{20,16},{24,28},{28,24},{1,5},{5... | collective-permute-start | bytes 491528 | tf_op jit(solution)/shard_map/ppermute | solution.py:19
  128.2 16.3 %copy-start.9 = (f32[128,512]{1,0:T(8,128)S(1)}, f32[128,512]{1,0:T(8,128)}, u32[]{:S(2)}) copy-start(f32[128,512]{1,0:T(8,128)} %param.11) | copy-start | bytes 786436
  133.3 12.0 %copy-start.3 = (f32[576,1152]{1,0:T(8,128)S(1)}, f32[576,1152]{1,0:T(8,128)}, u32[]{:S(2)}) copy-start(f32[576,1152]{1,0:T(8,128)} %refs_0_.3) | copy-start | bytes 7962628
  133.3 12.0 %copy-start.4 = (f32[512,512]{1,0:T(8,128)S(1)}, f32[512,512]{1,0:T(8,128)}, u32[]{:S(2)}) copy-start(f32[512,512]{1,0:T(8,128)} %refs_1_.1) | copy-start | bytes 3145732
  133.3 7.0 %collective-permute-start.34 = (f16[64,1280]{1,0:T(8,128)(2,1)S(1)}, f16[64,1280]{1,0:T(8,128)(2,1)S(1)}, u32[]{:S(2)}, u32[]{:S(2)}) collective-permute-start(f16[64,1280]{1,0:T(8,128)(2,1)S(1)} %collective-permute-done.30), channel_id=1, source_target_pairs={{0,4},{4,0},{8,12},{12,8},{16,20},{20,16},{24,28},{28,24},{1,5},{5... | collective-permute-start | bytes 491528 | tf_op jit(solution)/shard_map/ppermute | solution.py:19
  133.9 8.2 %collective-permute-start.35 = (f16[64,1280]{1,0:T(8,128)(2,1)S(1)}, f16[64,1280]{1,0:T(8,128)(2,1)S(1)}, u32[]{:S(2)}, u32[]{:S(2)}) collective-permute-start(f16[64,1280]{1,0:T(8,128)(2,1)S(1)} %collective-permute-done.24), channel_id=1, source_target_pairs={{0,4},{4,0},{8,12},{12,8},{16,20},{20,16},{24,28},{28,24},{1,5},{5... | collective-permute-start | bytes 491528 | tf_op jit(solution)/shard_map/ppermute | solution.py:19
  135.4 9.1 %collective-permute-start.31 = (f32[128,512]{1,0:T(8,128)S(1)}, f32[128,512]{1,0:T(8,128)S(1)}, u32[]{:S(2)}, u32[]{:S(2)}) collective-permute-start(f32[128,512]{1,0:T(8,128)S(1)} %add.71), channel_id=1, source_target_pairs={{0,8},{4,12},{8,0},{12,4},{16,24},{20,28},{24,16},{28,20},{1,9},{5... | collective-permute-start | bytes 786440 | tf_op jit(solution)/shard_map/ppermute | solution.py:19
  142.1 16.9 %collective-permute-start.37 = (f32[576,1152]{1,0:T(8,128)S(1)}, f32[576,1152]{1,0:T(8,128)S(1)}, u32[]{:S(2)}, u32[]{:S(2)}) collective-permute-start(f32[576,1152]{1,0:T(8,128)S(1)} %copy-done.10), channel_id=1, source_target_pairs={{0,1},{1,0},{2,3},{3,2},{4,5},{5,4},{6,7},{7,6},{8,9},{9,8},{10,11... | collective-permute-start | bytes 7962632 | tf_op jit(solution)/shard_map/ppermute | solution.py:19
  145.3 6.1 %copy-start.20 = (bf16[1,16,16,128]{3,2,1,0:T(8,128)(2,1)S(1)}, bf16[1,16,16,128]{3,2,1,0:T(8,128)(2,1)}, u32[]{:S(2)}) copy-start(bf16[1,16,16,128]{3,2,1,0:T(8,128)(2,1)} %get-tuple-element.80) | copy-start | bytes 196612
  145.3 7.6 %copy-start.19 = (bf16[1,16,16,128]{3,2,1,0:T(8,128)(2,1)S(1)}, bf16[1,16,16,128]{3,2,1,0:T(8,128)(2,1)}, u32[]{:S(2)}) copy-start(bf16[1,16,16,128]{3,2,1,0:T(8,128)(2,1)} %get-tuple-element.81) | copy-start | bytes 196612
  145.3 7.8 %copy-start.18 = (bf16[1,16,16,128]{3,2,1,0:T(8,128)(2,1)S(1)}, bf16[1,16,16,128]{3,2,1,0:T(8,128)(2,1)}, u32[]{:S(2)}) copy-start(bf16[1,16,16,128]{3,2,1,0:T(8,128)(2,1)} %get-tuple-element.82) | copy-start | bytes 196612
  145.3 13.0 %copy-start.2 = (bf16[1,16,16,128]{3,2,1,0:T(8,128)(2,1)S(1)}, bf16[1,16,16,128]{3,2,1,0:T(8,128)(2,1)}, u32[]{:S(2)}) copy-start(bf16[1,16,16,128]{3,2,1,0:T(8,128)(2,1)} %get-tuple-element.89.refs_0_) | copy-start | bytes 196612
  145.3 13.7 %copy-start.6 = (f32[576,1152]{1,0:T(8,128)S(1)}, f32[576,1152]{1,0:T(8,128)}, u32[]{:S(2)}) copy-start(f32[576,1152]{1,0:T(8,128)} %get-tuple-element.93) | copy-start | bytes 7962628
  151.3 7.7 %copy-start.5 = (f32[1152,576]{0,1:T(8,128)S(1)}, f32[1152,576]{0,1:T(8,128)}, u32[]{:S(2)}) copy-start(f32[1152,576]{0,1:T(8,128)} %param.10) | copy-start | bytes 7962628
  151.3 2.3 %collective-permute-start.36 = (f32[576,256]{1,0:T(8,128)S(1)}, f32[576,256]{1,0:T(8,128)S(1)}, u32[]{:S(2)}, u32[]{:S(2)}) collective-permute-start(f32[576,256]{1,0:T(8,128)S(1)} %get-tuple-element.88), channel_id=1, source_target_pairs={{0,1},{1,0},{2,3},{3,2},{4,5},{5,4},{6,7},{7,6},{8,9},{9,8},{10,11... | collective-permute-start | bytes 1769480 | tf_op jit(solution)/shard_map/ppermute | solution.py:19
  151.4 4.5 %collective-permute-start.26 = (bf16[1,16,16,128]{3,2,1,0:T(8,128)(2,1)S(1)}, bf16[1,16,16,128]{3,2,1,0:T(8,128)(2,1)S(1)}, u32[]{:S(2)}, u32[]{:S(2)}) collective-permute-start(bf16[1,16,16,128]{3,2,1,0:T(8,128)(2,1)S(1)} %copy-done.20), channel_id=1, source_target_pairs={{0,2},{1,3},{2,0},{3,1},{4,6},{5,7},{6,4},{7,5},{8,10},{9,11},{10,... | collective-permute-start | bytes 196616 | tf_op jit(solution)/shard_map/ppermute | solution.py:19
  152.9 3.0 %collective-permute-start.27 = (bf16[1,16,16,128]{3,2,1,0:T(8,128)(2,1)S(1)}, bf16[1,16,16,128]{3,2,1,0:T(8,128)(2,1)S(1)}, u32[]{:S(2)}, u32[]{:S(2)}) collective-permute-start(bf16[1,16,16,128]{3,2,1,0:T(8,128)(2,1)S(1)} %copy-done.19), channel_id=1, source_target_pairs={{0,1},{1,0},{2,3},{3,2},{4,5},{5,4},{6,7},{7,6},{8,9},{9,8},{10,11... | collective-permute-start | bytes 196616 | tf_op jit(solution)/shard_map/ppermute | solution.py:19
  153.0 3.9 %collective-permute-start.28 = (bf16[1,16,16,128]{3,2,1,0:T(8,128)(2,1)S(1)}, bf16[1,16,16,128]{3,2,1,0:T(8,128)(2,1)S(1)}, u32[]{:S(2)}, u32[]{:S(2)}) collective-permute-start(bf16[1,16,16,128]{3,2,1,0:T(8,128)(2,1)S(1)} %copy-done.18), channel_id=1, source_target_pairs={{0,3},{1,2},{2,1},{3,0},{4,7},{5,6},{6,5},{7,4},{8,11},{9,10},{10,... | collective-permute-start | bytes 196616 | tf_op jit(solution)/shard_map/ppermute | solution.py:19
  157.0 9.2 %collective-permute-start.38 = (f32[576,128]{1,0:T(8,128)S(1)}, f32[576,128]{1,0:T(8,128)S(1)}, u32[]{:S(2)}, u32[]{:S(2)}) collective-permute-start(f32[576,128]{1,0:T(8,128)S(1)} %slice.92), channel_id=1, source_target_pairs={{0,2},{1,3},{2,0},{3,1},{4,6},{5,7},{6,4},{7,5},{8,10},{9,11},{10,... | collective-permute-start | bytes 884744 | tf_op jit(solution)/shard_map/ppermute | solution.py:19

commit v10 on v9

--- a/solution.py
+++ b/solution.py
@@ -75,11 +75,12 @@
 
 
 def products_kernel(owners, first, *refs):
-    image_refs, strips_ref = refs[: len(owners)], refs[len(owners)]
-    refs = refs[len(owners) + 1 :]
+    n_arrays = 1 + max(array for _, (array, _) in owners)
+    image_refs = [refs[array].at[index] for _, (array, index) in owners]
+    strips_ref, refs = refs[n_arrays], refs[n_arrays + 1 :]
     before, refs = (None, refs) if first else (refs[:4], refs[4:])
     out_refs, totals, (shifted, turned, left, strips, sems) = refs[:4], refs[4:8], refs[8:]
-    n_images, side, channels = len(image_refs), image_refs[0].shape[1], image_refs[0].shape[3]
+    n_images, side, channels = len(image_refs), image_refs[0].shape[0], image_refs[0].shape[2]
     spots = side * side
     cols, rows = totals[0].shape
     strip = totals[1].shape[0]
@@ -87,9 +88,7 @@
     fsdp_at, factor_at = lax.axis_index("fsdp"), lax.axis_index("factor")
 
     arrivals = fetch(
-        [ref.at[0] for ref in image_refs],
-        [shifted.at[1, at, pl.ds(1, side)] for at in range(n_images)],
-        sems.at[0],
+        image_refs, [shifted.at[1, at, pl.ds(1, side)] for at in range(n_images)], sems.at[0]
     )
     strip_copies = fetch([strips_ref], [strips], sems.at[1])
     if not first:
@@ -109,7 +108,7 @@
     left[:cols, :] = turned[pl.ds(pl.multiple_of(inside, strip), cols), :]
     for copy in strip_copies:
         copy.wait()
-    for at, (layer, other, pair) in enumerate(owners):
+    for at, ((layer, other, pair), _) in enumerate(owners):
         owner = (fsdp_at + n_fsdp - 2 * layer) % n_fsdp
         owner = owner + other * (1 - 2 * (owner % 2))
         owner = owner * n_pair + (factor_at // 2 + n_pair - pair) % n_pair
@@ -148,12 +147,13 @@
         copy.wait()
 
 
-def add_products(owners, images, strips, before, cols, rows):
-    n_images, side, channels, strip = len(images), images[0].shape[1], images[0].shape[3], strips.shape[1]
+def add_products(owners, arrays, strips, before, cols, rows):
+    n_images, strip = len(owners), strips.shape[1]
+    side, channels = arrays[0].shape[1], arrays[0].shape[3]
     spots = side * side
     shapes = [(cols, rows), (strip, rows + LANES)] * 2
-    operands = [*images, strips, *(before or [])]
-    n_front = n_images + 1
+    operands = [*arrays, strips, *(before or [])]
+    n_front = len(arrays) + 1
     return pl.pallas_call(
         lambda *refs: products_kernel(owners, before is None, *refs),
         out_shape=[jax.ShapeDtypeStruct(shape, jnp.float32) for shape in shapes],
@@ -293,7 +293,7 @@
         for far in range(2):
             owner = (fsdp_at ^ (2 * near + far)) * depth
             weight[pl.ds(pl.multiple_of(owner, 64), depth), :] = parts[far, near]
-    for at, ref in enumerate(out_refs):
+    for at in range(n_images):
         total = jnp.zeros((side * side, block), jnp.float32)
         for tap in range(9):
             left = shifted[tap % 3, at, tap // 3 : tap // 3 + side].reshape(side * side, channels)
@@ -302,7 +302,8 @@
                 weight[tap * channels : (tap + 1) * channels, :],
                 preferred_element_type=jnp.float32,
             )
-        ref[0] = total.astype(jnp.bfloat16).reshape(side, side, block)
+        half = n_images // 2
+        out_refs[at // half][at % half] = total.astype(jnp.bfloat16).reshape(side, side, block)
 
 
 def convolve(images, near_parts, far_parts):
@@ -310,9 +311,9 @@
     block = near_parts.shape[2]
     return pl.pallas_call(
         lambda *refs: conv_kernel(n_images, *refs),
-        out_shape=[jax.ShapeDtypeStruct((1, side, side, block), jnp.bfloat16)] * n_images,
+        out_shape=[jax.ShapeDtypeStruct((n_images // 2, side, side, block), jnp.bfloat16)] * 2,
         in_specs=[pl.BlockSpec(memory_space=pl.ANY)] * (n_images + 2),
-        out_specs=[pl.BlockSpec(memory_space=pltpu.VMEM)] * n_images,
+        out_specs=[pl.BlockSpec(memory_space=pltpu.VMEM)] * 2,
         scratch_shapes=[
             pltpu.VMEM((3, n_images, side + 2, side, channels), jnp.bfloat16),
             pltpu.VMEM((2,) + near_parts.shape, jnp.bfloat16),
@@ -331,14 +332,16 @@
 def side_by_side_kernel(*refs):
     block, n_factor = refs[0].shape[3], lax.axis_size("factor")
     factor_at, n_pair = lax.axis_index("factor"), n_factor // 2
-    for at, ref in enumerate(refs[:-1]):
-        place = 2 * ((factor_at // 2 + at % n_pair) % n_pair) + (factor_at + at // n_pair) % 2
-        refs[-1][:, :, :, pl.ds(pl.multiple_of(place * block, LANES), block)] = ref[...]
+    for step, ref in enumerate(refs[:-1]):
+        for other in range(2):
+            place = 2 * ((factor_at // 2 + step) % n_pair) + (factor_at + other) % 2
+            lanes = pl.ds(pl.multiple_of(place * block, LANES), block)
+            refs[-1][0, :, :, lanes] = ref[other]
 
 
 def side_by_side(blocks):
     whole = pl.BlockSpec(memory_space=pltpu.VMEM)
-    shape = blocks[0].shape[:3] + (len(blocks) * blocks[0].shape[3],)
+    shape = (1,) + blocks[0].shape[1:3] + (2 * len(blocks) * blocks[0].shape[3],)
     return pl.pallas_call(
         side_by_side_kernel,
         out_shape=jax.ShapeDtypeStruct(shape, blocks[0].dtype),
@@ -346,38 +349,6 @@
         out_specs=whole,
         compiler_params=pltpu.CompilerParams(vmem_limit_bytes=4 * 1024 * 1024),
     )(*blocks)
-
-
-def gather_plan(n_layer, n_pair):
-    far_layers = sorted(range(1, n_layer), key=lambda step: min(step, n_layer - step))
-    waiting = {"layer": [(("layer", layer, 0), None) for layer in far_layers], "side": [], "pair": []}
-    for turn, layer in enumerate([0] + far_layers):
-        waiting["side"].append((("side", layer, 0), ("layer", layer, 0)))
-        for pair in range(1, n_pair):
-            waiting["pair"].append((("pair", layer, pair), ("layer", layer, 0)))
-            if turn % 2 == 0:
-                waiting["pair"].append((("both", layer, pair), ("side", layer, 0)))
-            else:
-                waiting["side"].append((("both", layer, pair), ("pair", layer, pair)))
-    for link in waiting.values():
-        link.sort(key=lambda entry: entry[0][0] == "both")
-    ready, busy, turns = {None: 0, ("layer", 0, 0): 0}, {link: 0 for link in waiting}, {}
-    order, step = [], 0
-    while any(waiting.values()):
-        for link, entries in waiting.items():
-            free = [entry for entry in entries if ready.get(entry[1], step + 1) <= step]
-            if busy[link] > step or not free:
-                continue
-            count = 2 if link == "layer" and step == 0 else 1
-            for item, source in free[:count]:
-                entries.remove((item, source))
-                hops = min(item[1], n_layer - item[1]) if link == "layer" else 1
-                busy[link] = step + hops * count
-                ready[item] = busy[link]
-                turns[link] = turns.get(link, -1) + 1
-                order.append((item, source, link, turns[link]))
-        step += 1
-    return order, ready
 
 
 def per_device(activations, cotangent, weight, a_factor_old, g_factor_old, a_inverse, g_inverse):
@@ -405,32 +376,74 @@
     def after(arrays, events):
         return lax.optimization_barrier((arrays, events))[0]
 
-    def transfer(array, item, how):
-        if how == "layer":
-            return over_layer(array, item[1])
-        if how == "pair":
-            return over_pair(array, item[2])
-        return over_side(array)
-
     own_cot = cotangent.reshape(-1, channels)
-    maps = {("layer", 0, 0): activations}
-    plan, ready = gather_plan(n_layer, n_pair)
-    images = sorted((item for item in ready if item), key=lambda item: ready[item])
-    half = len(images) // 2
     aligned = rows % LANES == 0 and channels % LANES == 0 and activations.shape[0] == 1
-
-    def products(batch, totals):
-        owners = [(layer, int(kind in ("side", "both")), pair) for kind, layer, pair in batch]
+    far_layers = sorted(range(1, n_layer), key=lambda step: min(step, n_layer - step))
+    pair_steps = range(1, n_pair)
+    arrays, what = {"own": activations}, {"own": [(0, 0, 0)]}
+
+    def add(name, array, whose):
+        arrays[name], what[name] = array, whose
+
+    add("side", over_side(activations), [(0, 1, 0)])
+    for step in pair_steps:
+        add(f"pair{step}", over_pair(activations, step), [(0, 0, step)])
+    for layer in far_layers[:2]:
+        add(f"layer{layer}", over_layer(activations, layer), [(layer, 0, 0)])
+    for step in pair_steps:
+        add(f"both{step}", over_pair(arrays["side"], step), [(0, 1, step)])
+    for layer in far_layers[2:]:
+        source = after(activations, [arrays[f"both{step}"] for step in pair_steps])
+        add(f"layer{layer}", over_layer(source, layer), [(layer, 0, 0)])
+
+    strips = after(own_cot, [arrays["side"]]).T.reshape(n_fsdp, 1, strip, own_cot.shape[0])
+    strips = jnp.broadcast_to(strips, (n_fsdp, n_pair) + strips.shape[2:])
+    groups = [
+        [at * n_factor + 2 * pair + core for at in range(n_fsdp) for pair in range(n_pair)]
+        for core in range(2)
+    ]
+    strips = lax.all_to_all(
+        strips.reshape((n_fsdp * n_pair,) + strips.shape[2:]),
+        ("fsdp", "factor"),
+        split_axis=0,
+        concat_axis=0,
+        axis_index_groups=groups,
+    )
+    first_names = list(arrays)
+
+    stacked = jnp.concatenate([arrays[f"layer{layer}"] for layer in far_layers])
+    stacked = after(stacked, strips)
+    add("far_side", over_side(stacked), [(layer, 1, 0) for layer in far_layers])
+    for step in pair_steps:
+        add(f"far_pair{step}", over_pair(stacked, step), [(layer, 0, step) for layer in far_layers])
+    second_names = [name for name in arrays if name not in first_names]
+    cut = (2 * len(far_layers) + 1) // 3
+    for step in pair_steps:
+        by_side = over_side(arrays[f"far_pair{step}"][:cut])
+        by_pair = over_pair(arrays["far_side"][cut:], step)
+        add(f"far_both_side{step}", by_side, [(layer, 1, step) for layer in far_layers[:cut]])
+        add(f"far_both_pair{step}", by_pair, [(layer, 1, step) for layer in far_layers[cut:]])
+    third_names = [name for name in arrays if name not in first_names + second_names]
+
+    def products(names, totals, events):
+        own_strips = after(strips, events)
+        owners = [
+            (whose, (at, index))
+            for at, name in enumerate(names)
+            for index, whose in enumerate(what[name])
+        ]
+        batch = [arrays[name] for name in names]
         if aligned:
-            arrays = [maps[item] for item in batch]
-            return add_products(owners, arrays, strips, totals, cols, rows)
+            return add_products(owners, batch, own_strips, totals, cols, rows)
+        batch = [array[index : index + 1] for array in batch for index in range(array.shape[0])]
+        owners = [whose for whose, _ in owners]
         for at in range(0, len(batch), 2 * n_pair):
-            part = jnp.concatenate([maps[item] for item in batch[at : at + 2 * n_pair]], axis=0)
+            part = jnp.concatenate(batch[at : at + 2 * n_pair], axis=0)
             col_tile = tile_of_patches(part, fsdp_at * cols, cols)
             cot_list = []
             for layer, other, pair in owners[at : at + 2 * n_pair]:
                 owner = ((fsdp_at - 2 * layer) % n_fsdp ^ other) * n_pair + (pair_at - pair) % n_pair
-                cot_list.append(lax.dynamic_index_in_dim(strips, owner, 0, keepdims=False))
+                cot_list.append(lax.dynamic_index_in_dim(own_strips, owner, 0, keepdims=False))
             more = []
             for tile in (factor_at ^ 1, factor_at):
                 row_tile = tile_of_patches(part, tile * rows, rows)
@@ -445,67 +458,45 @@
             totals = more if totals is None else [old + new for old, new in zip(totals, more)]
         return totals
 
-    sent = {"layer": [], "side": [], "pair": []}
-    for item, source, link, turn in plan:
-        if item == plan[-1][0]:
-            totals = products(images[:half], None)
-            early = [totals[3]]
-        array = activations if source is None else maps[source]
-        events = [] if link == "layer" else sent[link][max(turn - 2, 0) : turn - 1]
-        maps[item] = transfer(after(array, events + (early if item == plan[-1][0] else [])), item, link)
-        sent[link].append(maps[item])
-        if link == "side" and turn == 0:
-            strips = after(own_cot, [maps[item]]).T.reshape(n_fsdp, 1, strip, own_cot.shape[0])
-            strips = jnp.broadcast_to(strips, (n_fsdp, n_pair) + strips.shape[2:])
-            groups = [
-                [at * n_factor + 2 * pair + core for at in range(n_fsdp) for pair in range(n_pair)]
-                for core in range(2)
-            ]
-            strips = lax.all_to_all(
-                strips.reshape((n_fsdp * n_pair,) + strips.shape[2:]),
-                ("fsdp", "factor"),
-                split_axis=0,
-                concat_axis=0,
-                axis_index_groups=groups,
-            )
-    first_event, last_layer = sent["side"][:1], sent["layer"][-1:]
-    near_end = sent["pair"][-2:-1]
-    at_end = [maps[plan[-1][0]]] + sent["pair"][-1:]
-    totals = list(products(images[half:], totals))
+    layer_end = [arrays[f"layer{layer}"] for layer in far_layers]
+    weight_part = after(weight, layer_end)
+    near_parts = [lax.dynamic_slice_in_dim(weight_part, factor_at * block, block, 1)]
+    distance = 2
+    while distance < n_fsdp:
+        both = moved(jnp.stack(near_parts), "fsdp", lambda to, d=distance: to ^ d)
+        near_parts = near_parts + [both[k] for k in range(len(near_parts))]
+        distance *= 2
+
+    g_partial = by_rows(after(own_cot, layer_end), own_cot).reshape(n_pair, 2, block, channels)
+    g_pairs = lax.dynamic_index_in_dim(g_partial, core_at, 1, keepdims=False) + over_core(
+        lax.dynamic_index_in_dim(g_partial, 1 - core_at, 1, keepdims=False)
+    )
+    totals = products(first_names, None, [])
+    early = [totals[3]]
+    g_pairs = after(g_pairs, early)
+    g_sum = lax.dynamic_index_in_dim(g_pairs, pair_at, 0, keepdims=False)
+    for step in pair_steps:
+        away = lax.dynamic_index_in_dim(g_pairs, (pair_at + step) % n_pair, 0, keepdims=False)
+        g_sum = g_sum + over_pair(away, step)
+    totals = products(second_names, totals, [g_sum, near_parts[-1]])
+    middle = [totals[3]]
+    distance = n_fsdp // 2
+    while distance > 2:
+        g_sum = g_sum + moved(g_sum, "fsdp", lambda to, d=distance: to ^ d)
+        distance //= 2
+    totals = list(products(third_names, totals, [g_sum]))
     if not aligned:
         for at in (1, 3):
             largest = jnp.full((strip, LANES), jnp.max(jnp.abs(totals[at])))
             totals[at] = jnp.concatenate([totals[at], largest], axis=1)
 
-    g_partial = by_rows(after(own_cot, first_event), own_cot).reshape(n_pair, 2, block, channels)
-    g_pairs = lax.dynamic_index_in_dim(g_partial, core_at, 1, keepdims=False) + over_core(
-        lax.dynamic_index_in_dim(g_partial, 1 - core_at, 1, keepdims=False)
-    )
-    g_pairs = after(g_pairs, early)
-    g_sum = lax.dynamic_index_in_dim(g_pairs, pair_at, 0, keepdims=False)
-    for step in range(1, n_pair):
-        away = lax.dynamic_index_in_dim(g_pairs, (pair_at + step) % n_pair, 0, keepdims=False)
-        g_sum = g_sum + over_pair(away, step)
-    weight_part = after(weight, last_layer)
-    near_parts = [lax.dynamic_slice_in_dim(weight_part, factor_at * block, block, 1)]
-    distance = 2
-    while distance < n_fsdp:
-        both = after(jnp.stack(near_parts), near_end if distance > 2 else [])
-        both = moved(both, "fsdp", lambda to, d=distance: to ^ d)
-        both = after(both, early) if distance > 2 else both
-        near_parts = near_parts + [both[k] for k in range(len(near_parts))]
-        distance *= 2
     near_stack = jnp.stack(near_parts)
-    far_parts = over_side(after(near_stack, at_end))
-    distance = n_fsdp // 2
-    g_sum = after(g_sum, at_end)
-    while distance > 2:
-        g_sum = g_sum + moved(g_sum, "fsdp", lambda to, d=distance: to ^ d)
-        distance //= 2
-    near_images = [activations] + [maps["pair", 0, step] for step in range(1, n_pair)]
-    group = near_images + [over_core(image) for image in after(near_images, near_end)]
-    theirs = after(totals[1], [far_parts, g_sum] + group)
+    far_parts = over_side(after(near_stack, [arrays[name] for name in third_names] + middle))
+    near_images = [activations] + [arrays[f"pair{step}"] for step in pair_steps]
+    group = near_images + [over_core(image) for image in after(near_images, early)]
+    theirs = after(totals[1], group)
     theirs = over_core(theirs)
+    g_sum = g_sum + moved(g_sum, "fsdp", lambda to: to ^ 2)
     pixel_total = float(
         activations.shape[0] * activations.shape[1] * activations.shape[2] * n_fsdp * n_factor
     )
@@ -518,10 +509,15 @@
         packed = (totals[3] + theirs)[:, :rows] * jnp.exp2(-exponent)
         exponent = jnp.broadcast_to(exponent, (strip, LANES))
         packed = jnp.concatenate([packed, exponent], axis=1).astype(jnp.float16)
+    packed = after(packed, far_parts)
     near_packed = [packed] + [over_layer(packed, step) for step in range(1, n_layer)]
 
-    g_sum = g_sum + over_side(g_sum)
-    group = after(group, near_packed[n_layer - 1 :] + [g_sum])
+    far_packed, came = {0: over_side(packed)}, []
+    for step in far_layers:
+        far_packed[step] = over_side(after(near_packed[step], came))
+        came = came + [near_packed[step]]
+    far_packed = [far_packed[step] for step in range(n_layer)]
+    group = after(group, [far_packed[far_layers[0]], g_sum])
     if aligned and block % LANES == 0:
         group_out = convolve(group, near_stack, far_parts)
     else:
@@ -540,25 +536,17 @@
             dimension_numbers=("NHWC", "HWIO", "NHWC"),
             preferred_element_type=jnp.float32,
         ).astype(jnp.bfloat16)
-        group_out = jnp.split(group_out, n_factor)
+        group_out = jnp.split(group_out, 2)
+    swapped = over_core(group_out[1])
     own_maps, block_order = [], []
-    for other in range(2):
-        for pair in range(n_pair):
-            out = group_out[other * n_pair + pair]
-            if pair + other:
-                out = moved(out, "factor", lambda at, o=other, p=pair: (at ^ o) - 2 * p)
-            own_maps.append(out)
-            block_order.append(2 * ((pair_at + pair) % n_pair) + (core_at + other) % 2)
-
-    far_packed, came = {0: over_side(packed)}, []
-    for step in sorted(range(1, n_layer), key=lambda step: min(step, n_layer - step)):
-        if step == n_layer // 2:
-            came = came + list(group_out)
-        far_packed[step] = over_side(after(near_packed[step], came))
-        came = came + [near_packed[step]]
-    far_packed = [far_packed[step] for step in range(n_layer)]
-    g_sum = after(g_sum, near_packed)
-    g_sum = g_sum + moved(g_sum, "fsdp", lambda to: to ^ 2)
+    images_each = activations.shape[0]
+    for step in range(n_pair):
+        places = slice(step * images_each, (step + 1) * images_each)
+        both = jnp.concatenate([group_out[0][places], swapped[places]])
+        own_maps.append(over_pair(both, n_pair - step) if step else both)
+        block_order += [2 * ((pair_at + step) % n_pair) + (core_at + other) % 2 for other in range(2)]
+    g_back = over_side(after(g_sum, far_packed))
+    far_packed[far_layers[-1]] = after(far_packed[far_layers[-1]], group_out)
     strips_of_grad = [
         array[:, :rows].astype(jnp.float32) * jnp.exp2(array[:, rows : rows + 1].astype(jnp.float32))
         for array in near_packed + far_packed
@@ -572,7 +560,7 @@
     ]
     if aligned and block % LANES == 0:
         away, kept = tail_products(
-            after(a_inverse, [*group_out, g_sum]),
+            after(a_inverse, own_maps),
             g_inverse,
             strips_of_grad,
             [(step, other) for other in range(2) for step in range(n_layer)],
@@ -610,11 +598,12 @@
     if aligned and block % LANES == 0:
         conv_out = side_by_side(own_maps)
     else:
-        stacked = jnp.zeros((n_factor,) + own_maps[0].shape, jnp.bfloat16)
-        for at, out in zip(block_order, own_maps):
+        stacked = jnp.zeros((n_factor,) + activations.shape[:3] + (block,), jnp.bfloat16)
+        out_list = [out for both in own_maps for out in jnp.split(both, 2)]
+        for at, out in zip(block_order, out_list):
             stacked = lax.dynamic_update_index_in_dim(stacked, out, at, 0)
         conv_out = jnp.concatenate(jnp.split(stacked, n_factor), axis=4)[0]
-
+    g_sum = g_sum + after(g_back, by_pair)
     g_factor = 0.5 * g_factor_old + 0.5 * g_sum
     return (conv_out, a_factor, g_factor, natural_grad)
 

time: 167 us -> 170 us (1.018)
  starting transfers between devices: 56.6 us -> 38.8 us
  waiting for transfers between devices: 59.3 us -> 70.8 us
  local copies, waits for them, and re-layouts: 4.61 us -> 10 us
  Pallas kernels: 36.9 us -> 41.2 us
    ppermute x39 -> x33, starting transfers between devices: 48.3 us -> 33.9 us  [moved(): lax.ppermute(array, axis, [(at, target(at) % count) for at in range(count)])]
    ppermute x39 -> x33, waiting for transfers between devices: 59.3 us -> 70.8 us  [moved(): lax.ppermute(array, axis, [(at, target(at) % count) for at in range(count)])]
    pallas_call x2 -> x3, Pallas kernels: 25.1 us -> 29.6 us  [add_products(): pl.pallas_call(lambda *refs: products_kernel(owners, before is None, *ref...]
    all_to_all x1, starting transfers between devices: 8.29 us -> 4.89 us  [per_device(): lax.all_to_all(strips.reshape((n_fsdp * n_pair,) + strips.shape[2:]), ('f...]
    slice x0 -> x4, local copies, waits for them, and re-layouts: none -> 2.94 us  [the longest x1 1.08 us: per_device(): by_side = over_side(arrays[f'far_pair{step}'][:cut])]
    unnamed x42 -> x40, local copies, waits for them, and re-layouts: 2.57 us -> 3.87 us
  transfers between devices with their start and end apart: 40 -> 34, of which waited for: 15 -> 14; matrix products, arithmetic and copies ran while one was open for 6% -> 8% of each run, Pallas kernels for 22% -> 24%
where the time goes in v10:
time: 170 us
  waiting for transfers between devices  70.8 us (42%)
  Pallas kernels  41.2 us (24%)
  starting transfers between devices  38.8 us (23%)
  local copies, waits for them, and re-layouts  10 us (6%)
  other arithmetic  7.48 us (4%)
    ppermute x33, waiting for transfers between devices, moved(): lax.ppermute(array, axis, [(at, target(at) % count) for at in range(count)])  70.8 us
    ppermute x33, starting transfers between devices, moved(): lax.ppermute(array, axis, [(at, target(at) % count) for at in range(count)])  33.9 us
    pallas_call x3, Pallas kernels, add_products(): pl.pallas_call(lambda *refs: products_kernel(owners, before is None, *ref...  29.6 us
    pallas_call x1, Pallas kernels, tail_products(): pl.pallas_call(lambda *refs: tail_kernel(strip, block, layers, *refs), ou...  5.71 us
    pallas_call x1, Pallas kernels, convolve(): pl.pallas_call(lambda *refs: conv_kernel(n_images, *refs), out_shape=[jax...  5.02 us
    all_to_all x1, starting transfers between devices, per_device(): lax.all_to_all(strips.reshape((n_fsdp * n_pair,) + strips.shape[2:]), ('f...  4.89 us
    unnamed x40, local copies, waits for them, and re-layouts  3.87 us
  transfers between devices with their start and end apart: 34, of which 14 were waited for; matrix products, arithmetic and copies ran while one was open for 8% of the time, Pallas kernels for 24%

profile of v10, /device:TPU:0, one launch (start us, length us, event | category | flops | bytes accessed | tf_op | source)
XLA Modules:
  0.0 169.8 jit_solution(11987892867837791301)
XLA Ops:
  0.7 3.0 %collective-permute-start.1 = (bf16[1,16,16,512]{3,2,1,0:T(8,128)(2,1)}, bf16[1,16,16,512]{3,2,1,0:T(8,128)(2,1)S(1)}, u32[]{:S(2)}, u32[]{:S(2)}) collective-permute-start(bf16[1,16,16,512]{3,2,1,0:T(8,128)(2,1)} %refs_0_.2), channel_id=1, source_target_pairs={{0,4},{4,0},{8,12},{12,8},{16,20},{20,16},{24,28},{28,24},{1,5},{5... | collective-permute-start | bytes 786440 | tf_op jit(solution)/shard_map/ppermute | solution.py:19
  3.7 6.5 %collective-permute-done.1.refs_1_ = bf16[1,16,16,512]{3,2,1,0:T(8,128)(2,1)S(1)} collective-permute-done((bf16[1,16,16,512]{3,2,1,0:T(8,128)(2,1)}, bf16[1,16,16,512]{3,2,1,0:T(8,128)(2,1)S(1)}, u32[]{:S(2)}, u32[]{:S(2)}) %collective-permute-start.1) | collective-permute-done | bytes 262176 | tf_op jit(solution)/shard_map/ppermute | solution.py:19
  10.2 1.8 %collective-permute-start.4 = (bf16[1,16,16,512]{3,2,1,0:T(8,128)(2,1)S(1)}, bf16[1,16,16,512]{3,2,1,0:T(8,128)(2,1)}, u32[]{:S(2)}, u32[]{:S(2)}) collective-permute-start(bf16[1,16,16,512]{3,2,1,0:T(8,128)(2,1)S(1)} %collective-permute-done.1.refs_1_), channel_id=1, source_target_pairs={{0,2},{1,3},{2,0},{3,1},{4,6},{5,7},{6,4},{7,5},{8,10},{9,11},{10,... | collective-permute-start | bytes 786440 | tf_op jit(solution)/shard_map/ppermute | solution.py:19
  11.9 1.6 collective-permute-start.2
  13.5 2.2 %collective-permute-start.3 = (bf16[1,16,16,512]{3,2,1,0:T(8,128)(2,1)}, bf16[1,16,16,512]{3,2,1,0:T(8,128)(2,1)S(1)}, u32[]{:S(2)}, u32[]{:S(2)}) collective-permute-start(bf16[1,16,16,512]{3,2,1,0:T(8,128)(2,1)} %refs_0_.2), channel_id=1, source_target_pairs={{0,24},{4,28},{8,0},{12,4},{16,8},{20,12},{24,16},{28,20},{1,25},{... | collective-permute-start | bytes 786440 | tf_op jit(solution)/shard_map/ppermute | solution.py:19
  15.8 2.0 %collective-permute-done.4.refs_5_ = bf16[1,16,16,512]{3,2,1,0:T(8,128)(2,1)} collective-permute-done((bf16[1,16,16,512]{3,2,1,0:T(8,128)(2,1)S(1)}, bf16[1,16,16,512]{3,2,1,0:T(8,128)(2,1)}, u32[]{:S(2)}, u32[]{:S(2)}) %collective-permute-start.4) | collective-permute-done | bytes 262176 | tf_op jit(solution)/shard_map/ppermute | solution.py:19
  17.8 2.5 %collective-permute-start.5 = (bf16[1,16,16,512]{3,2,1,0:T(8,128)(2,1)}, bf16[1,16,16,512]{3,2,1,0:T(8,128)(2,1)S(1)}, u32[]{:S(2)}, u32[]{:S(2)}) collective-permute-start(bf16[1,16,16,512]{3,2,1,0:T(8,128)(2,1)} %refs_0_.2), channel_id=1, source_target_pairs={{0,16},{4,20},{8,24},{12,28},{16,0},{20,4},{24,8},{28,12},{1,17},{... | collective-permute-start | bytes 786440 | tf_op jit(solution)/shard_map/ppermute | solution.py:19
  20.3 1.1 copy.23
  21.4 0.9 broadcast_in_dim.8
  22.2 4.9 %all-to-all-start = ((bf16[16,64,256]{2,1,0:T(8,128)(2,1)}), bf16[16,64,256]{2,1,0:T(8,128)(2,1)}, u32[]{:S(2)}, u32[]{:S(2)}) async-start(bf16[16,64,256]{2,1,0:T(8,128)(2,1)} %bitcast.3), calls=%async_computation | async-start | bytes 1048576 | tf_op jit(solution)/shard_map/all_to_all | solution.py:405
  27.1 1.9 %collective-permute-start = (bf16[1,16,16,512]{3,2,1,0:T(8,128)(2,1)}, bf16[1,16,16,512]{3,2,1,0:T(8,128)(2,1)}, u32[]{:S(2)}, u32[]{:S(2)}) collective-permute-start(bf16[1,16,16,512]{3,2,1,0:T(8,128)(2,1)} %refs_0_.2), channel_id=1, source_target_pairs={{0,2},{1,3},{2,0},{3,1},{4,6},{5,7},{6,4},{7,5},{8,10},{9,11},{10,... | collective-permute-start | bytes 786440 | tf_op jit(solution)/shard_map/ppermute | solution.py:19
  29.0 14.4 %collective-permute-done.5.refs_6_ = bf16[1,16,16,512]{3,2,1,0:T(8,128)(2,1)S(1)} collective-permute-done((bf16[1,16,16,512]{3,2,1,0:T(8,128)(2,1)}, bf16[1,16,16,512]{3,2,1,0:T(8,128)(2,1)S(1)}, u32[]{:S(2)}, u32[]{:S(2)}) %collective-permute-start.5) | collective-permute-done | bytes 262176 | tf_op jit(solution)/shard_map/ppermute | solution.py:19
  43.5 1.2 copy.26
  44.8 0.3 fusion.3
  45.3 0.5 copy-done.11
  46.0 4.8 %collective-permute-done.16 = bf16[1,576,128]{2,1,0:T(8,128)(2,1)S(1)} collective-permute-done((bf16[1,576,128]{2,1,0:T(8,128)(2,1)S(1)}, bf16[1,576,128]{2,1,0:T(8,128)(2,1)S(1)}, u32[]{:S(2)}, u32[]{:S(2)}) %collective-permute-start.16) | collective-permute-done | bytes 147488 | tf_op jit(solution)/shard_map/ppermute | solution.py:19
  50.8 0.4 collective-permute-start.17
  51.2 1.3 collective-permute-start.10
  52.5 0.6 collective-permute-start.8
  53.1 11.1 %shard_map.102 = (f32[576,1152]{1,0:T(8,128)}, f32[64,1280]{1,0:T(8,128)}, f32[576,1152]{1,0:T(8,128)}, f32[64,1280]{1,0:T(8,128)}) custom-call(bf16[1,16,16,512]{3,2,1,0:T(8,128)(2,1)} %refs_0_.2, bf16[1,16,16,512]{3,2,1,0:T(8,128)(2,1)} %copy-done.16, bf16[1,16,16,512]{3,2,1,0:T(8,128)(2,1)} %collective-permute-done.refs_2_.refs_1_, ...), custom_call_target="tpu_custom_call" | custom-call | flops 5284823040 | bytes 11796480 | tf_op jit(solution)/shard_map/pallas_call | solution.py:157
  64.2 1.1 bitcast_add_fusion.1
  65.4 1.5 collective-permute-start.13
  66.9 1.0 pad_maximum_fusion.1.refs_4_
  68.0 0.5 collective-permute-start.7
  68.5 4.6 %collective-permute-done.8.refs_1_ = bf16[3,16,16,512]{3,2,1,0:T(8,128)(2,1)} collective-permute-done((bf16[3,16,16,512]{3,2,1,0:T(8,128)(2,1)S(1)}, bf16[3,16,16,512]{3,2,1,0:T(8,128)(2,1)}, u32[]{:S(2)}, u32[]{:S(2)}) %collective-permute-start.8) | collective-permute-done | bytes 786464 | tf_op jit(solution)/shard_map/ppermute | solution.py:19
  73.1 1.1 slice.99
  74.2 0.8 collective-permute-start.9
  74.9 1.7 collective-permute-done.13
  76.6 2.6 %collective-permute-start.14 = (f32[128,512]{1,0:T(8,128)S(1)}, f32[128,512]{1,0:T(8,128)S(1)}, u32[]{:S(2)}, u32[]{:S(2)}) collective-permute-start(f32[128,512]{1,0:T(8,128)S(1)} %bitcast_add_fusion.2), channel_id=1, source_target_pairs={{0,16},{4,20},{8,24},{12,28},{16,0},{20,4},{24,8},{28,12},{1,17},{... | collective-permute-start | bytes 786440 | tf_op jit(solution)/shard_map/ppermute | solution.py:19
  79.3 1.0 slice.100
  80.2 0.6 collective-permute-start.11
  80.8 10.8 %shard_map.103 = (f32[576,1152]{1,0:T(8,128)}, f32[64,1280]{1,0:T(8,128)}, f32[576,1152]{1,0:T(8,128)}, f32[64,1280]{1,0:T(8,128)}) custom-call(bf16[3,16,16,512]{3,2,1,0:T(8,128)(2,1)} %collective-permute-done.10.refs_0_, ...), custom_call_target="tpu_custom_call", output_to_operand_aliasing={{0}: (3, {}), {1}: (4, {}), {2}: (5, {}), {3}: (6, {})} | custom-call | flops 4529848320 | bytes 11796480 | tf_op jit(solution)/shard_map/pallas_call | solution.py:157
  91.6 0.6 collective-permute-start.18
  92.3 0.2 copy-done.15
  92.5 7.8 %shard_map.104 = (f32[576,1152]{1,0:T(8,128)}, f32[64,1280]{1,0:T(8,128)}, f32[576,1152]{1,0:T(8,128)}, f32[64,1280]{1,0:T(8,128)}) custom-call(bf16[2,16,16,512]{3,2,1,0:T(8,128)(2,1)} %copy-done.15, bf16[1,16,16,512]{3,2,1,0:T(8,128)(2,1)} %copy-done.19, ...), custom_call_target="tpu_custom_call", output_to_operand_aliasing={{0}: (3, {}), {1}: (4, {}), {2}: (5, {}), {3}: (6, {})} | custom-call | flops 2264924160 | bytes 11796480 | tf_op jit(solution)/shard_map/pallas_call | solution.py:157
  100.4 0.4 collective-permute-start.21
  100.8 8.3 %collective-permute-done.21 = f32[128,512]{1,0:T(8,128)S(1)} collective-permute-done((f32[128,512]{1,0:T(8,128)S(1)}, f32[128,512]{1,0:T(8,128)S(1)}, u32[]{:S(2)}, u32[]{:S(2)}) %collective-permute-start.21) | collective-permute-done | bytes 262176 | tf_op jit(solution)/shard_map/ppermute | solution.py:19
  109.2 1.0 copy-done.1
  110.2 0.8 copy-done.14
  111.1 0.4 collective-permute-start.19
  111.4 3.5 %collective-permute-start.25 = (f16[64,1280]{1,0:T(8,128)(2,1)S(1)}, f16[64,1280]{1,0:T(8,128)(2,1)S(1)}, u32[]{:S(2)}, u32[]{:S(2)}) collective-permute-start(f16[64,1280]{1,0:T(8,128)(2,1)S(1)} %convert_element_type.54), channel_id=1, source_target_pairs={{0,24},{4,28},{8,0},{12,4},{16,8},{20,12},{24,16},{28,20},{1,25},{... | collective-permute-start | bytes 491528 | tf_op jit(solution)/shard_map/ppermute | solution.py:19
  114.9 1.3 collective-permute-start.26
  116.4 3.5 %collective-permute-done.19 = f16[64,1280]{1,0:T(8,128)(2,1)S(1)} collective-permute-done((f16[64,1280]{1,0:T(8,128)(2,1)S(1)}, f16[64,1280]{1,0:T(8,128)(2,1)S(1)}, u32[]{:S(2)}, u32[]{:S(2)}) %collective-permute-start.19) | collective-permute-done | bytes 163872 | tf_op jit(solution)/shard_map/ppermute | solution.py:19
  120.0 0.4 collective-permute-done.25
  120.4 1.3 collective-permute-start.28
  121.7 6.7 %collective-permute-done.24 = f16[64,1280]{1,0:T(8,128)(2,1)S(1)} collective-permute-done((f16[64,1280]{1,0:T(8,128)(2,1)S(1)}, f16[64,1280]{1,0:T(8,128)(2,1)S(1)}, u32[]{:S(2)}, u32[]{:S(2)}) %collective-permute-start.24) | collective-permute-done | bytes 163872 | tf_op jit(solution)/shard_map/ppermute | solution.py:19
  128.4 1.3 collective-permute-start.27
  129.7 0.7 collective-permute-start.20
  131.3 5.9 %collective-permute-done.20 = f16[64,1280]{1,0:T(8,128)(2,1)S(1)} collective-permute-done((f16[64,1280]{1,0:T(8,128)(2,1)S(1)}, f16[64,1280]{1,0:T(8,128)(2,1)S(1)}, u32[]{:S(2)}, u32[]{:S(2)}) %collective-permute-start.20) | collective-permute-done | bytes 163872 | tf_op jit(solution)/shard_map/ppermute | solution.py:19
  137.3 5.0 %shard_map.106 = (bf16[2,16,16,128]{3,2,1,0:T(8,128)(2,1)}, bf16[2,16,16,128]{3,2,1,0:T(8,128)(2,1)}) custom-call(bf16[1,16,16,512]{3,2,1,0:T(8,128)(2,1)} %refs_0_.2, bf16[1,16,16,512]{3,2,1,0:T(8,128)(2,1)} %collective-permute-done.refs_2_.refs_1_, bf16[1,16,16,512]{3,2,1,0:T(8,128)(2,1)} %copy-done.17, bf16[1,16,16,512]{3,2,1,0:T(8,128)(2,1)} %copy-done.18, ...), custom_call_target="tpu_custom_call" | custom-call | flops 2415919104 | bytes 2228224 | tf_op jit(solution)/shard_map/pallas_call | solution.py:312
  142.5 0.6 collective-permute-start.30
  143.4 0.9 fusion.1
  144.4 0.4 collective-permute-start.23
  144.9 5.0 %collective-permute-done.23.refs_1_ = bf16[2,16,16,128]{3,2,1,0:T(8,128)(2,1)S(1)} collective-permute-done((bf16[2,16,16,128]{3,2,1,0:T(8,128)(2,1)S(1)}, bf16[2,16,16,128]{3,2,1,0:T(8,128)(2,1)S(1)}, u32[]{:S(2)}, u32[]{:S(2)}) %collective-permute-start.23) | collective-permute-done | bytes 131104 | tf_op jit(solution)/shard_map/ppermute | solution.py:19
  149.9 1.2 copy-done.3
  151.2 5.7 %shard_map.107 = (f32[576,256]{1,0:T(8,128)S(1)}, f32[576,256]{1,0:T(8,128)S(1)}) custom-call(f32[576,1152]{1,0:T(8,128)S(1)} %copy-done.2, f32[512,512]{1,0:T(8,128)S(1)} %copy-done.3, f32[64,1152]{1,0:T(8,128)S(1)} %convert_multiply_fusion.7.refs_2_, f32[64,1152]{1,0:T(8,128)S(1)} %convert_multiply_fusion.6.refs_3_, ...), custom_call_target="tpu_custom_call" | custom-call | flops 2944401408 | bytes 3833856 | tf_op jit(solution)/shard_map/pallas_call | solution.py:255
  157.0 1.4 collective-permute-start.31
  158.4 0.6 collective-permute-done.29
  159.1 0.4 collective-permute-start.32
  159.5 6.2 %collective-permute-done.31 = f32[128,512]{1,0:T(8,128)S(1)} collective-permute-done((f32[128,512]{1,0:T(8,128)S(1)}, f32[128,512]{1,0:T(8,128)S(1)}, u32[]{:S(2)}, u32[]{:S(2)}) %collective-permute-start.31) | collective-permute-done | bytes 262176 | tf_op jit(solution)/shard_map/ppermute | solution.py:19
  165.7 0.8 shard_map.108
  166.5 0.8 add_multiply_fusion
  167.2 1.9 %bitcast_add_fusion = f32[1152,576]{0,1:T(8,128)} fusion(f32[576,1152]{1,0:T(8,128)S(1)} %copy-done.5, f32[576,1152]{1,0:T(8,128)S(1)} %collective-permute-done.30, f32[1152,576]{0,1:T(8,128)S(1)} %copy-done.4), kind=kLoop, calls=%fused_computation | loop fusion | flops 2654208 | bytes 10616832 | tf_op jit(solution)/shard_map/add | solution.py:589
  169.1 0.7 fusion
  (93 shorter events, 2.8 us)
Async XLA Ops:
  0.6 44.0 %copy-start = (bf16[576,512]{1,0:T(8,128)(2,1)S(1)}, bf16[576,512]{1,0:T(8,128)(2,1)}, u32[]{:S(2)}) copy-start(bf16[576,512]{1,0:T(8,128)(2,1)} %param.9) | copy-start | bytes 1769476
  0.6 44.2 %copy-start.6 = (bf16[1,16,16,512]{3,2,1,0:T(8,128)(2,1)S(1)}, bf16[1,16,16,512]{3,2,1,0:T(8,128)(2,1)}, u32[]{:S(2)}) copy-start(bf16[1,16,16,512]{3,2,1,0:T(8,128)(2,1)} %param.8) | copy-start | bytes 786436
  0.7 9.5 %collective-permute-start.1 = (bf16[1,16,16,512]{3,2,1,0:T(8,128)(2,1)}, bf16[1,16,16,512]{3,2,1,0:T(8,128)(2,1)S(1)}, u32[]{:S(2)}, u32[]{:S(2)}) collective-permute-start(bf16[1,16,16,512]{3,2,1,0:T(8,128)(2,1)} %refs_0_.2), channel_id=1, source_target_pairs={{0,4},{4,0},{8,12},{12,8},{16,20},{20,16},{24,28},{28,24},{1,5},{5... | collective-permute-start | bytes 786440 | tf_op jit(solution)/shard_map/ppermute | solution.py:19
  10.2 10.1 %copy-start.16 = (bf16[1,16,16,512]{3,2,1,0:T(8,128)(2,1)}, bf16[1,16,16,512]{3,2,1,0:T(8,128)(2,1)S(1)}, u32[]{:S(2)}) copy-start(bf16[1,16,16,512]{3,2,1,0:T(8,128)(2,1)S(1)} %collective-permute-done.1.refs_1_) | copy-start | bytes 786436
  10.2 7.6 %collective-permute-start.4 = (bf16[1,16,16,512]{3,2,1,0:T(8,128)(2,1)S(1)}, bf16[1,16,16,512]{3,2,1,0:T(8,128)(2,1)}, u32[]{:S(2)}, u32[]{:S(2)}) collective-permute-start(bf16[1,16,16,512]{3,2,1,0:T(8,128)(2,1)S(1)} %collective-permute-done.1.refs_1_), channel_id=1, source_target_pairs={{0,2},{1,3},{2,0},{3,1},{4,6},{5,7},{6,4},{7,5},{8,10},{9,11},{10,... | collective-permute-start | bytes 786440 | tf_op jit(solution)/shard_map/ppermute | solution.py:19
  11.9 17.1 %collective-permute-start.2 = (bf16[1,16,16,512]{3,2,1,0:T(8,128)(2,1)}, bf16[1,16,16,512]{3,2,1,0:T(8,128)(2,1)S(1)}, u32[]{:S(2)}, u32[]{:S(2)}) collective-permute-start(bf16[1,16,16,512]{3,2,1,0:T(8,128)(2,1)} %refs_0_.2), channel_id=1, source_target_pairs={{0,8},{4,12},{8,16},{12,20},{16,24},{20,28},{24,0},{28,4},{1,9},{5... | collective-permute-start | bytes 786440 | tf_op jit(solution)/shard_map/ppermute | solution.py:19
  13.5 15.5 %collective-permute-start.3 = (bf16[1,16,16,512]{3,2,1,0:T(8,128)(2,1)}, bf16[1,16,16,512]{3,2,1,0:T(8,128)(2,1)S(1)}, u32[]{:S(2)}, u32[]{:S(2)}) collective-permute-start(bf16[1,16,16,512]{3,2,1,0:T(8,128)(2,1)} %refs_0_.2), channel_id=1, source_target_pairs={{0,24},{4,28},{8,0},{12,4},{16,8},{20,12},{24,16},{28,20},{1,25},{... | collective-permute-start | bytes 786440 | tf_op jit(solution)/shard_map/ppermute | solution.py:19
  17.8 25.7 %collective-permute-start.5 = (bf16[1,16,16,512]{3,2,1,0:T(8,128)(2,1)}, bf16[1,16,16,512]{3,2,1,0:T(8,128)(2,1)S(1)}, u32[]{:S(2)}, u32[]{:S(2)}) collective-permute-start(bf16[1,16,16,512]{3,2,1,0:T(8,128)(2,1)} %refs_0_.2), channel_id=1, source_target_pairs={{0,16},{4,20},{8,24},{12,28},{16,0},{20,4},{24,8},{28,12},{1,17},{... | collective-permute-start | bytes 786440 | tf_op jit(solution)/shard_map/ppermute | solution.py:19
  22.2 28.9 %all-to-all-start = ((bf16[16,64,256]{2,1,0:T(8,128)(2,1)}), bf16[16,64,256]{2,1,0:T(8,128)(2,1)}, u32[]{:S(2)}, u32[]{:S(2)}) async-start(bf16[16,64,256]{2,1,0:T(8,128)(2,1)} %bitcast.3), calls=%async_computation | async-start | bytes 1048576 | tf_op jit(solution)/shard_map/all_to_all | solution.py:405
  27.1 26.0 %collective-permute-start = (bf16[1,16,16,512]{3,2,1,0:T(8,128)(2,1)}, bf16[1,16,16,512]{3,2,1,0:T(8,128)(2,1)}, u32[]{:S(2)}, u32[]{:S(2)}) collective-permute-start(bf16[1,16,16,512]{3,2,1,0:T(8,128)(2,1)} %refs_0_.2), channel_id=1, source_target_pairs={{0,2},{1,3},{2,0},{3,1},{4,6},{5,7},{6,4},{7,5},{8,10},{9,11},{10,... | collective-permute-start | bytes 786440 | tf_op jit(solution)/shard_map/ppermute | solution.py:19
  29.0 16.9 %copy-start.9 = (bf16[1,16,16,512]{3,2,1,0:T(8,128)(2,1)}, bf16[1,16,16,512]{3,2,1,0:T(8,128)(2,1)S(1)}, u32[]{:S(2)}) copy-start(bf16[1,16,16,512]{3,2,1,0:T(8,128)(2,1)S(1)} %collective-permute-done.2.refs_3_) | copy-start | bytes 786436
  29.0 15.8 %copy-start.10 = (bf16[1,16,16,512]{3,2,1,0:T(8,128)(2,1)}, bf16[1,16,16,512]{3,2,1,0:T(8,128)(2,1)S(1)}, u32[]{:S(2)}) copy-start(bf16[1,16,16,512]{3,2,1,0:T(8,128)(2,1)S(1)} %collective-permute-done.3.refs_4_) | copy-start | bytes 786436
  43.5 1.3 copy-start.12
  44.7 6.0 %collective-permute-start.16 = (bf16[1,576,128]{2,1,0:T(8,128)(2,1)S(1)}, bf16[1,576,128]{2,1,0:T(8,128)(2,1)S(1)}, u32[]{:S(2)}, u32[]{:S(2)}) collective-permute-start(bf16[1,576,128]{2,1,0:T(8,128)(2,1)S(1)} %dynamic-slice_bitcast_fusion.2), channel_id=1, source_target_pairs={{0,8},{4,12},{8,0},{12,4},{16,24},{20,28},{24,16},{28,20},{1,9},{5... | collective-permute-start | bytes 442376 | tf_op jit(solution)/shard_map/ppermute | solution.py:19
  44.8 1.0 copy-start.11
  44.8 1.0 copy-start.13
  45.2 19.0 %collective-permute-start.12 = (f32[2,128,512]{2,1,0:T(8,128)S(1)}, f32[2,128,512]{2,1,0:T(8,128)}, u32[]{:S(2)}, u32[]{:S(2)}) collective-permute-start(f32[2,128,512]{2,1,0:T(8,128)S(1)} %dynamic-slice_bitcast_fusion), channel_id=1, source_target_pairs={{0,1},{1,0},{2,3},{3,2},{4,5},{5,4},{6,7},{7,6},{8,9},{9,8},{10,11... | collective-permute-start | bytes 1572872 | tf_op jit(solution)/shard_map/ppermute | solution.py:19
  50.8 16.1 %collective-permute-start.17 = (bf16[2,576,128]{2,1,0:T(8,128)(2,1)S(1)}, bf16[2,576,128]{2,1,0:T(8,128)(2,1)}, u32[]{:S(2)}, u32[]{:S(2)}) collective-permute-start(bf16[2,576,128]{2,1,0:T(8,128)(2,1)S(1)} %pad_maximum_fusion.2), channel_id=1, source_target_pairs={{0,16},{4,20},{8,24},{12,28},{16,0},{20,4},{24,8},{28,12},{1,17},{... | collective-permute-start | bytes 884744 | tf_op jit(solution)/shard_map/ppermute | solution.py:19
  51.2 28.1 %collective-permute-start.10 = (bf16[3,16,16,512]{3,2,1,0:T(8,128)(2,1)S(1)}, bf16[3,16,16,512]{3,2,1,0:T(8,128)(2,1)}, u32[]{:S(2)}, u32[]{:S(2)}) collective-permute-start(bf16[3,16,16,512]{3,2,1,0:T(8,128)(2,1)S(1)} %pad_maximum_fusion), channel_id=1, source_target_pairs={{0,4},{4,0},{8,12},{12,8},{16,20},{20,16},{24,28},{28,24},{1,5},{5... | collective-permute-start | bytes 2359304 | tf_op jit(solution)/shard_map/ppermute | solution.py:19
  52.5 20.6 %collective-permute-start.8 = (bf16[3,16,16,512]{3,2,1,0:T(8,128)(2,1)S(1)}, bf16[3,16,16,512]{3,2,1,0:T(8,128)(2,1)}, u32[]{:S(2)}, u32[]{:S(2)}) collective-permute-start(bf16[3,16,16,512]{3,2,1,0:T(8,128)(2,1)S(1)} %pad_maximum_fusion), channel_id=1, source_target_pairs={{0,2},{1,3},{2,0},{3,1},{4,6},{5,7},{6,4},{7,5},{8,10},{9,11},{10,... | collective-permute-start | bytes 2359304 | tf_op jit(solution)/shard_map/ppermute | solution.py:19
  65.4 11.2 %collective-permute-start.13 = (f32[128,512]{1,0:T(8,128)S(1)}, f32[128,512]{1,0:T(8,128)S(1)}, u32[]{:S(2)}, u32[]{:S(2)}) collective-permute-start(f32[128,512]{1,0:T(8,128)S(1)} %dynamic-slice_bitcast_fusion.1), channel_id=1, source_target_pairs={{0,2},{1,3},{2,0},{3,1},{4,6},{5,7},{6,4},{7,5},{8,10},{9,11},{10,... | collective-permute-start | bytes 786440 | tf_op jit(solution)/shard_map/ppermute | solution.py:19
  67.9 23.7 %copy-start.7 = (bf16[4,576,128]{2,1,0:T(8,128)(2,1)}, bf16[4,576,128]{2,1,0:T(8,128)(2,1)S(1)}, u32[]{:S(2)}) copy-start(bf16[4,576,128]{2,1,0:T(8,128)(2,1)S(1)} %pad_maximum_fusion.1.refs_4_) | copy-start | bytes 1769476
  67.9 32.3 %collective-permute-start.6 = (bf16[1,16,16,512]{3,2,1,0:T(8,128)(2,1)}, bf16[1,16,16,512]{3,2,1,0:T(8,128)(2,1)S(1)}, u32[]{:S(2)}, u32[]{:S(2)}) collective-permute-start(bf16[1,16,16,512]{3,2,1,0:T(8,128)(2,1)} %refs_0_.2), channel_id=1, source_target_pairs={{0,1},{1,0},{2,3},{3,2},{4,5},{5,4},{6,7},{7,6},{8,9},{9,8},{10,11... | collective-permute-start | bytes 786440 | tf_op jit(solution)/shard_map/ppermute | solution.py:19
  68.0 32.3 %collective-permute-start.7 = (bf16[1,16,16,512]{3,2,1,0:T(8,128)(2,1)}, bf16[1,16,16,512]{3,2,1,0:T(8,128)(2,1)S(1)}, u32[]{:S(2)}, u32[]{:S(2)}) collective-permute-start(bf16[1,16,16,512]{3,2,1,0:T(8,128)(2,1)} %collective-permute-done.refs_2_.refs_1_), channel_id=1, source_target_pairs={{0,1},{1,0},{2,3},{3,2},{4,5},{5,4},{6,7},{7,6},{8,9},{9,8},{10,11... | collective-permute-start | bytes 786440 | tf_op jit(solution)/shard_map/ppermute | solution.py:19
  74.2 17.5 %collective-permute-start.9 = (bf16[2,16,16,512]{3,2,1,0:T(8,128)(2,1)S(1)}, bf16[2,16,16,512]{3,2,1,0:T(8,128)(2,1)S(1)}, u32[]{:S(2)}, u32[]{:S(2)}) collective-permute-start(bf16[2,16,16,512]{3,2,1,0:T(8,128)(2,1)S(1)} %slice.99), channel_id=1, source_target_pairs={{0,4},{4,0},{8,12},{12,8},{16,20},{20,16},{24,28},{28,24},{1,5},{5... | collective-permute-start | bytes 1572872 | tf_op jit(solution)/shard_map/ppermute | solution.py:19
  76.6 15.6 %collective-permute-start.14 = (f32[128,512]{1,0:T(8,128)S(1)}, f32[128,512]{1,0:T(8,128)S(1)}, u32[]{:S(2)}, u32[]{:S(2)}) collective-permute-start(f32[128,512]{1,0:T(8,128)S(1)} %bitcast_add_fusion.2), channel_id=1, source_target_pairs={{0,16},{4,20},{8,24},{12,28},{16,0},{20,4},{24,8},{28,12},{1,17},{... | collective-permute-start | bytes 786440 | tf_op jit(solution)/shard_map/ppermute | solution.py:19
  80.2 11.4 %collective-permute-start.11 = (bf16[1,16,16,512]{3,2,1,0:T(8,128)(2,1)S(1)}, bf16[1,16,16,512]{3,2,1,0:T(8,128)(2,1)S(1)}, u32[]{:S(2)}, u32[]{:S(2)}) collective-permute-start(bf16[1,16,16,512]{3,2,1,0:T(8,128)(2,1)S(1)} %slice.100), channel_id=1, source_target_pairs={{0,2},{1,3},{2,0},{3,1},{4,6},{5,7},{6,4},{7,5},{8,10},{9,11},{10,... | collective-permute-start | bytes 786440 | tf_op jit(solution)/shard_map/ppermute | solution.py:19
  91.6 0.7 copy-start.19
  91.6 0.9 copy-start.15
  91.6 18.6 %collective-permute-start.18 = (bf16[4,576,128]{2,1,0:T(8,128)(2,1)S(1)}, bf16[4,576,128]{2,1,0:T(8,128)(2,1)S(1)}, u32[]{:S(2)}, u32[]{:S(2)}) collective-permute-start(bf16[4,576,128]{2,1,0:T(8,128)(2,1)S(1)} %pad_maximum_fusion.1.refs_4_), channel_id=1, source_target_pairs={{0,4},{4,0},{8,12},{12,8},{16,20},{20,16},{24,28},{28,24},{1,5},{5... | collective-permute-start | bytes 1769480 | tf_op jit(solution)/shard_map/ppermute | solution.py:19
  100.3 14.6 %copy-start.17 = (bf16[1,16,16,512]{3,2,1,0:T(8,128)(2,1)}, bf16[1,16,16,512]{3,2,1,0:T(8,128)(2,1)S(1)}, u32[]{:S(2)}) copy-start(bf16[1,16,16,512]{3,2,1,0:T(8,128)(2,1)S(1)} %collective-permute-done.6.refs_2_) | copy-start | bytes 786436
  100.3 30.7 %copy-start.18 = (bf16[1,16,16,512]{3,2,1,0:T(8,128)(2,1)}, bf16[1,16,16,512]{3,2,1,0:T(8,128)(2,1)S(1)}, u32[]{:S(2)}) copy-start(bf16[1,16,16,512]{3,2,1,0:T(8,128)(2,1)S(1)} %collective-permute-done.7.refs_3_) | copy-start | bytes 786436
  100.3 8.9 %collective-permute-start.15 = (f32[64,1280]{1,0:T(8,128)}, f32[64,1280]{1,0:T(8,128)S(1)}, u32[]{:S(2)}, u32[]{:S(2)}) collective-permute-start(f32[64,1280]{1,0:T(8,128)} %get-tuple-element.67), channel_id=1, source_target_pairs={{0,1},{1,0},{2,3},{3,2},{4,5},{5,4},{6,7},{7,6},{8,9},{9,8},{10,11... | collective-permute-start | bytes 983048 | tf_op jit(solution)/shard_map/ppermute | solution.py:19
  100.4 8.7 %collective-permute-start.21 = (f32[128,512]{1,0:T(8,128)S(1)}, f32[128,512]{1,0:T(8,128)S(1)}, u32[]{:S(2)}, u32[]{:S(2)}) collective-permute-start(f32[128,512]{1,0:T(8,128)S(1)} %add.69), channel_id=1, source_target_pairs={{0,8},{4,12},{8,0},{12,4},{16,24},{20,28},{24,16},{28,20},{1,9},{5... | collective-permute-start | bytes 786440 | tf_op jit(solution)/shard_map/ppermute | solution.py:19
  109.2 1.0 copy-start.1
  110.2 0.8 copy-start.14
  111.1 8.9 %collective-permute-start.19 = (f16[64,1280]{1,0:T(8,128)(2,1)S(1)}, f16[64,1280]{1,0:T(8,128)(2,1)S(1)}, u32[]{:S(2)}, u32[]{:S(2)}) collective-permute-start(f16[64,1280]{1,0:T(8,128)(2,1)S(1)} %convert_element_type.54), channel_id=1, source_target_pairs={{0,8},{4,12},{8,16},{12,20},{16,24},{20,28},{24,0},{28,4},{1,9},{5... | collective-permute-start | bytes 491528 | tf_op jit(solution)/shard_map/ppermute | solution.py:19
  111.4 9.0 %collective-permute-start.25 = (f16[64,1280]{1,0:T(8,128)(2,1)S(1)}, f16[64,1280]{1,0:T(8,128)(2,1)S(1)}, u32[]{:S(2)}, u32[]{:S(2)}) collective-permute-start(f16[64,1280]{1,0:T(8,128)(2,1)S(1)} %convert_element_type.54), channel_id=1, source_target_pairs={{0,24},{4,28},{8,0},{12,4},{16,8},{20,12},{24,16},{28,20},{1,25},{... | collective-permute-start | bytes 491528 | tf_op jit(solution)/shard_map/ppermute | solution.py:19
  114.9 13.5 %collective-permute-start.24 = (f16[64,1280]{1,0:T(8,128)(2,1)S(1)}, f16[64,1280]{1,0:T(8,128)(2,1)S(1)}, u32[]{:S(2)}, u32[]{:S(2)}) collective-permute-start(f16[64,1280]{1,0:T(8,128)(2,1)S(1)} %convert_element_type.54), channel_id=1, source_target_pairs={{0,16},{4,20},{8,24},{12,28},{16,0},{20,4},{24,8},{28,12},{1,17},{... | collective-permute-start | bytes 491528 | tf_op jit(solution)/shard_map/ppermute | solution.py:19
  114.9 15.9 %collective-permute-start.26 = (f16[64,1280]{1,0:T(8,128)(2,1)S(1)}, f16[64,1280]{1,0:T(8,128)(2,1)S(1)}, u32[]{:S(2)}, u32[]{:S(2)}) collective-permute-start(f16[64,1280]{1,0:T(8,128)(2,1)S(1)} %convert_element_type.54), channel_id=1, source_target_pairs={{0,4},{4,0},{8,12},{12,8},{16,20},{20,16},{24,28},{28,24},{1,5},{5... | collective-permute-start | bytes 491528 | tf_op jit(solution)/shard_map/ppermute | solution.py:19
  120.4 22.1 %collective-permute-start.28 = (f16[64,1280]{1,0:T(8,128)(2,1)S(1)}, f16[64,1280]{1,0:T(8,128)(2,1)S(1)}, u32[]{:S(2)}, u32[]{:S(2)}) collective-permute-start(f16[64,1280]{1,0:T(8,128)(2,1)S(1)} %collective-permute-done.25), channel_id=1, source_target_pairs={{0,4},{4,0},{8,12},{12,8},{16,20},{20,16},{24,28},{28,24},{1,5},{5... | collective-permute-start | bytes 491528 | tf_op jit(solution)/shard_map/ppermute | solution.py:19
  128.4 14.0 %collective-permute-start.27 = (f16[64,1280]{1,0:T(8,128)(2,1)S(1)}, f16[64,1280]{1,0:T(8,128)(2,1)S(1)}, u32[]{:S(2)}, u32[]{:S(2)}) collective-permute-start(f16[64,1280]{1,0:T(8,128)(2,1)S(1)} %collective-permute-done.24), channel_id=1, source_target_pairs={{0,4},{4,0},{8,12},{12,8},{16,20},{20,16},{24,28},{28,24},{1,5},{5... | collective-permute-start | bytes 491528 | tf_op jit(solution)/shard_map/ppermute | solution.py:19
  129.7 7.5 %collective-permute-start.20 = (f16[64,1280]{1,0:T(8,128)(2,1)S(1)}, f16[64,1280]{1,0:T(8,128)(2,1)S(1)}, u32[]{:S(2)}, u32[]{:S(2)}) collective-permute-start(f16[64,1280]{1,0:T(8,128)(2,1)S(1)} %collective-permute-done.19), channel_id=1, source_target_pairs={{0,4},{4,0},{8,12},{12,8},{16,20},{20,16},{24,28},{28,24},{1,5},{5... | collective-permute-start | bytes 491528 | tf_op jit(solution)/shard_map/ppermute | solution.py:19
  131.3 18.6 %copy-start.2 = (f32[576,1152]{1,0:T(8,128)S(1)}, f32[576,1152]{1,0:T(8,128)}, u32[]{:S(2)}) copy-start(f32[576,1152]{1,0:T(8,128)} %refs_0_.3) | copy-start | bytes 7962628
  142.3 2.1 %collective-permute-start.22 = (bf16[2,16,16,128]{3,2,1,0:T(8,128)(2,1)}, bf16[2,16,16,128]{3,2,1,0:T(8,128)(2,1)S(1)}, u32[]{:S(2)}, u32[]{:S(2)}) collective-permute-start(bf16[2,16,16,128]{3,2,1,0:T(8,128)(2,1)} %get-tuple-element.76), channel_id=1, source_target_pairs={{0,1},{1,0},{2,3},{3,2},{4,5},{5,4},{6,7},{7,6},{8,9},{9,8},{10,11... | collective-permute-start | bytes 393224 | tf_op jit(solution)/shard_map/ppermute | solution.py:19
  142.5 24.7 %collective-permute-start.30 = (f32[576,1152]{1,0:T(8,128)}, f32[576,1152]{1,0:T(8,128)S(1)}, u32[]{:S(2)}, u32[]{:S(2)}) collective-permute-start(f32[576,1152]{1,0:T(8,128)} %get-tuple-element.87), channel_id=1, source_target_pairs={{0,1},{1,0},{2,3},{3,2},{4,5},{5,4},{6,7},{7,6},{8,9},{9,8},{10,11... | collective-permute-start | bytes 7962632 | tf_op jit(solution)/shard_map/ppermute | solution.py:19
  144.4 5.5 %collective-permute-start.23 = (bf16[2,16,16,128]{3,2,1,0:T(8,128)(2,1)S(1)}, bf16[2,16,16,128]{3,2,1,0:T(8,128)(2,1)S(1)}, u32[]{:S(2)}, u32[]{:S(2)}) collective-permute-start(bf16[2,16,16,128]{3,2,1,0:T(8,128)(2,1)S(1)} %pad_maximum_fusion.4), channel_id=1, source_target_pairs={{0,2},{1,3},{2,0},{3,1},{4,6},{5,7},{6,4},{7,5},{8,10},{9,11},{10,... | collective-permute-start | bytes 393224 | tf_op jit(solution)/shard_map/ppermute | solution.py:19
  149.9 1.2 copy-start.3
  151.2 15.3 %copy-start.8 = (f32[128,512]{1,0:T(8,128)S(1)}, f32[128,512]{1,0:T(8,128)}, u32[]{:S(2)}) copy-start(f32[128,512]{1,0:T(8,128)} %param.11) | copy-start | bytes 786436
  151.2 16.1 %copy-start.5 = (f32[576,1152]{1,0:T(8,128)S(1)}, f32[576,1152]{1,0:T(8,128)}, u32[]{:S(2)}) copy-start(f32[576,1152]{1,0:T(8,128)} %get-tuple-element.85) | copy-start | bytes 7962628
  156.9 10.3 %copy-start.4 = (f32[1152,576]{0,1:T(8,128)S(1)}, f32[1152,576]{0,1:T(8,128)}, u32[]{:S(2)}) copy-start(f32[1152,576]{0,1:T(8,128)} %param.10) | copy-start | bytes 7962628
  156.9 2.1 %collective-permute-start.29 = (f32[576,256]{1,0:T(8,128)S(1)}, f32[576,256]{1,0:T(8,128)S(1)}, u32[]{:S(2)}, u32[]{:S(2)}) collective-permute-start(f32[576,256]{1,0:T(8,128)S(1)} %get-tuple-element.82), channel_id=1, source_target_pairs={{0,1},{1,0},{2,3},{3,2},{4,5},{5,4},{6,7},{7,6},{8,9},{9,8},{10,11... | collective-permute-start | bytes 1769480 | tf_op jit(solution)/shard_map/ppermute | solution.py:19
  157.0 8.7 %collective-permute-start.31 = (f32[128,512]{1,0:T(8,128)S(1)}, f32[128,512]{1,0:T(8,128)S(1)}, u32[]{:S(2)}, u32[]{:S(2)}) collective-permute-start(f32[128,512]{1,0:T(8,128)S(1)} %add.71), channel_id=1, source_target_pairs={{0,4},{4,0},{8,12},{12,8},{16,20},{20,16},{24,28},{28,24},{1,5},{5... | collective-permute-start | bytes 786440 | tf_op jit(solution)/shard_map/ppermute | solution.py:19
  159.1 10.0 %collective-permute-start.32 = (f32[576,128]{1,0:T(8,128)S(1)}, f32[576,128]{1,0:T(8,128)S(1)}, u32[]{:S(2)}, u32[]{:S(2)}) collective-permute-start(f32[576,128]{1,0:T(8,128)S(1)} %slice.116), channel_id=1, source_target_pairs={{0,2},{1,3},{2,0},{3,1},{4,6},{5,7},{6,4},{7,5},{8,10},{9,11},{10,... | collective-permute-start | bytes 884744 | tf_op jit(solution)/shard_map/ppermute | solution.py:19

commit v11 on v8

--- a/solution.py
+++ b/solution.py
@@ -132,17 +132,34 @@
         return jnp.dot(left[...], right, preferred_element_type=jnp.float32)
 
     def keep(whose, lane, count, value):
-        at = slice(lane, lane + count * LANES)
+        at = pl.ds(pl.multiple_of(lane, LANES), count * LANES)
         for kind, part in ((0, value[:cols]), (1, value[cols:])):
             if not first:
                 part = part + totals[2 * whose + kind][:, at]
             totals[2 * whose + kind][:, at] = part
+
+    def keep_largest(whose):
         grads = totals[2 * whose + 1]
         grads[:, rows:] = jnp.full((strip, LANES), jnp.max(jnp.abs(grads[:, :rows])))
 
-    keep(0, 0, tiles_per, product(0, tiles_per))
+    half, odd = tiles_per // 2, tiles_per % 2
+
+    @pl.loop(0, half)
+    def _(step):
+        keep(0, step * 2 * LANES, 2, product(2 * step, 2))
+
+    if odd:
+        both = product(2 * half, 2)
+        keep(0, 2 * half * LANES, 1, both[:, :LANES])
+        keep(1, 0, 1, both[:, LANES:])
+    keep_largest(0)
     theirs_out = fetch(totals[:2], out_refs[:2], sems.at[3])
-    keep(1, 0, tiles_per, product(tiles_per, tiles_per))
+
+    @pl.loop(0, half)
+    def _(step):
+        keep(1, (odd + 2 * step) * LANES, 2, product(tiles_per + odd + 2 * step, 2))
+
+    keep_largest(1)
     mine_out = fetch(totals[2:], out_refs[2:], sems.at[4])
     for copy in theirs_out + mine_out:
         copy.wait()
@@ -175,6 +192,27 @@
             transcendentals=0,
         ),
     )(*operands)
+
+
+def scale_kernel(mine_ref, theirs_ref, out_ref):
+    rows = out_ref.shape[1] - LANES
+    largest = mine_ref[:, rows:] + theirs_ref[:, rows:]
+    exponent = jnp.floor(jnp.log2(jnp.maximum(largest, 1e-30))) - 14.0
+    scale = jnp.exp2(-exponent)
+    for at in range(0, rows, LANES):
+        lanes = slice(at, at + LANES)
+        out_ref[:, lanes] = (mine_ref[:, lanes] + theirs_ref[:, lanes]) * scale
+    out_ref[:, rows:] = exponent
+
+
+def scale_strips(mine, theirs):
+    return pl.pallas_call(
+        scale_kernel,
+        out_shape=jax.ShapeDtypeStruct(mine.shape, jnp.float32),
+        in_specs=[pl.BlockSpec(memory_space=pltpu.VMEM)] * 2,
+        out_specs=pl.BlockSpec(memory_space=pltpu.VMEM),
+        compiler_params=pltpu.CompilerParams(vmem_limit_bytes=4 * 1024 * 1024),
+    )(mine, theirs)
 
 
 def tail_kernel(strip, block, layers, *refs):
@@ -415,9 +453,8 @@
 
     aligned = rows % LANES == 0 and channels % LANES == 0 and activations.shape[0] == 1
     images = sorted(maps, key=lambda item: ready[item])
-    half = len(images) // 2
-    totals, early = None, []
-    for batch in (images[:half], images[half:]):
+    totals = None
+    for batch in (images,):
         owners, pairs = [], []
         for kind, layer, pair in batch:
             owner = (fsdp_at - 2 * layer) % n_fsdp
@@ -428,7 +465,6 @@
                 [(layer, int(kind in ("side", "both"))) for kind, layer, _ in batch],
                 [maps[item] for item in batch], pairs, strips_by_pair, totals, cols, rows
             )
-            early = early or [totals[3]]
             continue
         for at in range(0, len(batch), 2 * n_pair):
             part = jnp.concatenate([maps[item] for item in batch[at : at + 2 * n_pair]], axis=0)
@@ -468,9 +504,9 @@
         near_parts = near_parts + [both[k] for k in range(len(near_parts))]
         distance *= 2
     near_stack = jnp.stack(near_parts)
-    far_parts = over_side(after(near_stack, at_end + early))
+    far_parts = over_side(after(near_stack, at_end))
     distance = n_fsdp // 2
-    g_sum = after(g_sum, at_end + early)
+    g_sum = after(g_sum, at_end)
     while distance > 2:
         g_sum = g_sum + moved(g_sum, "fsdp", lambda to, d=distance: to ^ d)
         distance //= 2
@@ -482,15 +518,18 @@
         activations.shape[0] * activations.shape[1] * activations.shape[2] * n_fsdp * n_factor
     )
 
-    largest = totals[3][:, rows : rows + 1] + theirs[:, rows : rows + 1]
-    exponent = jnp.floor(jnp.log2(jnp.maximum(largest, 1e-30))) - 14.0
-    packed = ((totals[3] + theirs)[:, :rows] * jnp.exp2(-exponent)).astype(jnp.float16)
-    exponent = jnp.broadcast_to(exponent.astype(jnp.float16), (strip, LANES))
-    packed = jnp.concatenate([packed, exponent], axis=1)
+    if aligned:
+        packed = scale_strips(totals[3], theirs).astype(jnp.float16)
+    else:
+        largest = totals[3][:, rows : rows + 1] + theirs[:, rows : rows + 1]
+        exponent = jnp.floor(jnp.log2(jnp.maximum(largest, 1e-30))) - 14.0
+        packed = (totals[3] + theirs)[:, :rows] * jnp.exp2(-exponent)
+        exponent = jnp.broadcast_to(exponent, (strip, LANES))
+        packed = jnp.concatenate([packed, exponent], axis=1).astype(jnp.float16)
     near_packed = [packed] + [over_layer(packed, step) for step in range(1, n_layer)]
 
-    g_sum = g_sum + over_side(g_sum)
-    group = after(group, near_packed[n_layer - 1 :] + [g_sum])
+    cov_back = over_core(after(totals[0], [packed]))
+    group = after(group, [packed])
     if aligned and block % LANES == 0:
         group_out = convolve(group, near_stack, far_parts)
     else:
@@ -510,24 +549,22 @@
             preferred_element_type=jnp.float32,
         ).astype(jnp.bfloat16)
         group_out = jnp.split(group_out, n_factor)
+    far_packed, came = {0: over_side(packed)}, list(group_out)
+    for step in sorted(range(1, n_layer), key=lambda step: min(step, n_layer - step)):
+        far_packed[step] = over_side(after(near_packed[step], came))
+        came = came + [near_packed[step]]
+    far_packed = [far_packed[step] for step in range(n_layer)]
+
     own_maps, block_order = [], []
+    outputs = after(list(group_out), far_packed)
     for other in range(2):
         for pair in range(n_pair):
-            out = group_out[other * n_pair + pair]
+            out = outputs[other * n_pair + pair]
             if pair + other:
                 out = moved(out, "factor", lambda at, o=other, p=pair: (at ^ o) - 2 * p)
             own_maps.append(out)
             block_order.append(2 * ((pair_at + pair) % n_pair) + (core_at + other) % 2)
-
-    far_packed, came = {0: over_side(packed)}, []
-    for step in sorted(range(1, n_layer), key=lambda step: min(step, n_layer - step)):
-        if step == n_layer // 2:
-            came = came + list(group_out)
-        far_packed[step] = over_side(after(near_packed[step], came))
-        came = came + [near_packed[step]]
-    far_packed = [far_packed[step] for step in range(n_layer)]
-    g_sum = after(g_sum, near_packed)
-    g_sum = g_sum + moved(g_sum, "fsdp", lambda to: to ^ 2)
+    g_side = over_side(after(g_sum, far_packed))
     strips_of_grad = [
         array[:, :rows].astype(jnp.float32) * jnp.exp2(array[:, rows : rows + 1].astype(jnp.float32))
         for array in near_packed + far_packed
@@ -541,7 +578,7 @@
     ]
     if aligned and block % LANES == 0:
         away, kept = tail_products(
-            after(a_inverse, own_maps[1:n_pair] + own_maps[n_pair + 1 :]),
+            after(a_inverse, [cov_back]),
             g_inverse,
             strips_of_grad,
             [(step, other) for other in range(2) for step in range(n_layer)],
@@ -566,12 +603,14 @@
         )
         away, kept = partial[:, : channels // 2], partial[:, channels // 2 :]
     by_pair = kept + over_core(away)
-    cov_own = totals[2] + after(over_core(after(totals[0], [packed])), by_pair)
+    cov_own = totals[2] + after(cov_back, by_pair)
     a_factor = 0.5 * a_factor_old + (0.5 / pixel_total) * cov_own.T
     result = by_pair[:, :block]
     for step in range(1, n_pair):
         back = over_pair(by_pair[:, step * block : (step + 1) * block], step)
         result = result + after(back, a_factor)
+    g_sum = g_sum + after(g_side, by_pair)
+    g_sum = g_sum + after(moved(g_sum, "fsdp", lambda to: to ^ 2), back)
     natural_grad = result.astype(jnp.bfloat16)
 
 

time: 161 us -> 151 us (0.938)
  waiting for transfers between devices: 51.7 us -> 45.2 us
  Pallas kernels: 37.5 us -> 33.5 us
  other arithmetic: 8.99 us -> 6.48 us
  starting transfers between devices: 56.6 us -> 59.1 us
    ppermute x40, waiting for transfers between devices: 51.7 us -> 45.2 us  [moved(): lax.ppermute(array, axis, [(at, target(at) % count) for at in range(count)])]
    pallas_call x2 -> x1, Pallas kernels: 25.7 us -> 21.9 us  [add_products(): pl.pallas_call(lambda *refs: products_kernel(owners, pairs, len(strips),...]
    ppermute x40, starting transfers between devices: 53.2 us -> 55.6 us  [moved(): lax.ppermute(array, axis, [(at, target(at) % count) for at in range(count)])]
  transfers between devices with their start and end apart: 41 -> 41, of which waited for: 17 -> 17; matrix products, arithmetic and copies ran while one was open for 7% -> 5% of each run, Pallas kernels for 23% -> 18%
where the time goes in v11:
time: 151 us; the launch traced here: 150 us
  starting transfers between devices  59.1 us (39%)
  waiting for transfers between devices  45.2 us (30%)
  Pallas kernels  33.5 us (22%)
  other arithmetic  6.48 us (4%)
  local copies, waits for them, and re-layouts  3.65 us (2%)
    ppermute x40, starting transfers between devices, moved(): lax.ppermute(array, axis, [(at, target(at) % count) for at in range(count)])  55.6 us
    ppermute x40, waiting for transfers between devices, moved(): lax.ppermute(array, axis, [(at, target(at) % count) for at in range(count)])  45.2 us
    pallas_call x1, Pallas kernels, add_products(): pl.pallas_call(lambda *refs: products_kernel(owners, pairs, len(strips),...  21.9 us
    pallas_call x1, Pallas kernels, tail_products(): pl.pallas_call(lambda *refs: tail_kernel(strip, block, layers, *refs), ou...  5.74 us
    pallas_call x1, Pallas kernels, convolve(): pl.pallas_call(lambda *refs: conv_kernel(n_images, *refs), out_shape=[jax...  5.09 us
    all_to_all x1, starting transfers between devices, per_device(): strips = lax.all_to_all(strips, 'fsdp', split_axis=0, concat_axis=0)  3.42 us
  transfers between devices with their start and end apart: 41, of which 17 were waited for; matrix products, arithmetic and copies ran while one was open for 5% of the time, Pallas kernels for 18%

profile of v11, /device:TPU:0, one launch (start us, length us, event | category | flops | bytes accessed | tf_op | source)
XLA Modules:
  0.0 150.3 jit_solution(1723477364996474355)
XLA Ops:
  0.6 3.1 %collective-permute-start.1 = (bf16[1,16,16,512]{3,2,1,0:T(8,128)(2,1)}, bf16[1,16,16,512]{3,2,1,0:T(8,128)(2,1)S(1)}, u32[]{:S(2)}, u32[]{:S(2)}) collective-permute-start(bf16[1,16,16,512]{3,2,1,0:T(8,128)(2,1)} %refs_0_.2), channel_id=1, source_target_pairs={{0,8},{4,12},{8,16},{12,20},{16,24},{20,28},{24,0},{28,4},{1,9},{5... | collective-permute-start | bytes 786440 | tf_op jit(solution)/shard_map/ppermute | solution.py:19
  3.7 1.5 %collective-permute-start = (bf16[1,16,16,512]{3,2,1,0:T(8,128)(2,1)}, bf16[1,16,16,512]{3,2,1,0:T(8,128)(2,1)S(1)}, u32[]{:S(2)}, u32[]{:S(2)}) collective-permute-start(bf16[1,16,16,512]{3,2,1,0:T(8,128)(2,1)} %refs_0_.2), channel_id=1, source_target_pairs={{0,2},{1,3},{2,0},{3,1},{4,6},{5,7},{6,4},{7,5},{8,10},{9,11},{10,... | collective-permute-start | bytes 786440 | tf_op jit(solution)/shard_map/ppermute | solution.py:19
  5.2 1.5 collective-permute-start.7
  6.7 2.2 %collective-permute-start.8 = (bf16[1,16,16,512]{3,2,1,0:T(8,128)(2,1)}, bf16[1,16,16,512]{3,2,1,0:T(8,128)(2,1)}, u32[]{:S(2)}, u32[]{:S(2)}) collective-permute-start(bf16[1,16,16,512]{3,2,1,0:T(8,128)(2,1)} %refs_0_.2), channel_id=1, source_target_pairs={{0,24},{4,28},{8,0},{12,4},{16,8},{20,12},{24,16},{28,20},{1,25},{... | collective-permute-start | bytes 786440 | tf_op jit(solution)/shard_map/ppermute | solution.py:19
  9.0 4.2 %collective-permute-done.1.refs_3_ = bf16[1,16,16,512]{3,2,1,0:T(8,128)(2,1)S(1)} collective-permute-done((bf16[1,16,16,512]{3,2,1,0:T(8,128)(2,1)}, bf16[1,16,16,512]{3,2,1,0:T(8,128)(2,1)S(1)}, u32[]{:S(2)}, u32[]{:S(2)}) %collective-permute-start.1) | collective-permute-done | bytes 262176 | tf_op jit(solution)/shard_map/ppermute | solution.py:19
  13.1 8.3 %collective-permute-start.2 = (bf16[1,16,16,512]{3,2,1,0:T(8,128)(2,1)}, bf16[1,16,16,512]{3,2,1,0:T(8,128)(2,1)}, u32[]{:S(2)}, u32[]{:S(2)}) collective-permute-start(bf16[1,16,16,512]{3,2,1,0:T(8,128)(2,1)} %refs_0_.2), channel_id=1, source_target_pairs={{0,16},{4,20},{8,24},{12,28},{16,0},{20,4},{24,8},{28,12},{1,17},{... | collective-permute-start | bytes 786440 | tf_op jit(solution)/shard_map/ppermute | solution.py:19
  21.4 1.5 %collective-permute-start.3 = (bf16[1,16,16,512]{3,2,1,0:T(8,128)(2,1)S(1)}, bf16[1,16,16,512]{3,2,1,0:T(8,128)(2,1)}, u32[]{:S(2)}, u32[]{:S(2)}) collective-permute-start(bf16[1,16,16,512]{3,2,1,0:T(8,128)(2,1)S(1)} %collective-permute-done.1.refs_3_), channel_id=1, source_target_pairs={{0,2},{1,3},{2,0},{3,1},{4,6},{5,7},{6,4},{7,5},{8,10},{9,11},{10,... | collective-permute-start | bytes 786440 | tf_op jit(solution)/shard_map/ppermute | solution.py:19
  22.9 1.8 %copy.13 = bf16[512,256]{1,0:T(8,128)(2,1)} copy(bf16[512,256]{0,1:T(8,128)(2,1)} %bitcast.22) | data formatting | bytes 524288 | tf_op jit(solution)/shard_map/transpose | solution.py:445
  24.7 1.3 fusion.1
  26.2 3.4 %all-to-all-start = ((bf16[8,64,256]{2,1,0:T(8,128)(2,1)}), bf16[8,64,256]{2,1,0:T(8,128)(2,1)S(1)}, u32[]{:S(2)}, u32[]{:S(2)}) async-start(bf16[8,64,256]{2,1,0:T(8,128)(2,1)} %bitcast.2), calls=%async_computation | async-start | bytes 524288 | tf_op jit(solution)/shard_map/all_to_all | solution.py:446
  29.6 0.6 collective-permute-start.9
  30.2 1.9 %collective-permute-start.10 = (bf16[1,16,16,512]{3,2,1,0:T(8,128)(2,1)S(1)}, bf16[1,16,16,512]{3,2,1,0:T(8,128)(2,1)}, u32[]{:S(2)}, u32[]{:S(2)}) collective-permute-start(bf16[1,16,16,512]{3,2,1,0:T(8,128)(2,1)S(1)} %collective-permute-done.1.refs_3_), channel_id=1, source_target_pairs={{0,4},{4,0},{8,12},{12,8},{16,20},{20,16},{24,28},{28,24},{1,5},{5... | collective-permute-start | bytes 786440 | tf_op jit(solution)/shard_map/ppermute | solution.py:19
  32.1 1.5 %collective-permute-start.18 = (bf16[1,576,128]{2,1,0:T(8,128)(2,1)S(1)}, bf16[1,576,128]{2,1,0:T(8,128)(2,1)S(1)}, u32[]{:S(2)}, u32[]{:S(2)}) collective-permute-start(bf16[1,576,128]{2,1,0:T(8,128)(2,1)S(1)} %dynamic-slice_bitcast_fusion.2), channel_id=1, source_target_pairs={{0,8},{4,12},{8,0},{12,4},{16,24},{20,28},{24,16},{28,20},{1,9},{5... | collective-permute-start | bytes 442376 | tf_op jit(solution)/shard_map/ppermute | solution.py:19
  33.6 1.5 %collective-permute-start.4 = (bf16[1,16,16,512]{3,2,1,0:T(8,128)(2,1)}, bf16[1,16,16,512]{3,2,1,0:T(8,128)(2,1)}, u32[]{:S(2)}, u32[]{:S(2)}) collective-permute-start(bf16[1,16,16,512]{3,2,1,0:T(8,128)(2,1)} %collective-permute-done.2.refs_8_), channel_id=1, source_target_pairs={{0,2},{1,3},{2,0},{3,1},{4,6},{5,7},{6,4},{7,5},{8,10},{9,11},{10,... | collective-permute-start | bytes 786440 | tf_op jit(solution)/shard_map/ppermute | solution.py:19
  35.2 4.0 %collective-permute-done.9.refs_5_ = bf16[1,16,16,512]{3,2,1,0:T(8,128)(2,1)} collective-permute-done((bf16[1,16,16,512]{3,2,1,0:T(8,128)(2,1)}, bf16[1,16,16,512]{3,2,1,0:T(8,128)(2,1)}, u32[]{:S(2)}, u32[]{:S(2)}) %collective-permute-start.9) | collective-permute-done | bytes 262176 | tf_op jit(solution)/shard_map/ppermute | solution.py:19
  39.1 1.9 %collective-permute-start.11 = (bf16[1,16,16,512]{3,2,1,0:T(8,128)(2,1)}, bf16[1,16,16,512]{3,2,1,0:T(8,128)(2,1)}, u32[]{:S(2)}, u32[]{:S(2)}) collective-permute-start(bf16[1,16,16,512]{3,2,1,0:T(8,128)(2,1)} %collective-permute-done.8.refs_4_), channel_id=1, source_target_pairs={{0,4},{4,0},{8,12},{12,8},{16,20},{20,16},{24,28},{28,24},{1,5},{5... | collective-permute-start | bytes 786440 | tf_op jit(solution)/shard_map/ppermute | solution.py:19
  41.0 0.3 collective-permute-done.10.refs_6_
  41.3 1.3 collective-permute-start.12
  42.7 0.6 collective-permute-start.13
  43.4 1.3 collective-permute-done.4.refs_12_
  44.6 2.4 %collective-permute-start.19 = (bf16[2,576,128]{2,1,0:T(8,128)(2,1)S(1)}, bf16[2,576,128]{2,1,0:T(8,128)(2,1)}, u32[]{:S(2)}, u32[]{:S(2)}) collective-permute-start(bf16[2,576,128]{2,1,0:T(8,128)(2,1)S(1)} %pad_maximum_fusion.1), channel_id=1, source_target_pairs={{0,16},{4,20},{8,24},{12,28},{16,0},{20,4},{24,8},{28,12},{1,17},{... | collective-permute-start | bytes 884744 | tf_op jit(solution)/shard_map/ppermute | solution.py:19
  47.0 0.7 collective-permute-start.15
  47.9 0.8 collective-permute-done.11.refs_9_
  48.7 0.6 collective-permute-start.22
  49.2 3.3 %collective-permute-done.13.refs_11_ = bf16[1,16,16,512]{3,2,1,0:T(8,128)(2,1)} collective-permute-done((bf16[1,16,16,512]{3,2,1,0:T(8,128)(2,1)}, bf16[1,16,16,512]{3,2,1,0:T(8,128)(2,1)}, u32[]{:S(2)}, u32[]{:S(2)}) %collective-permute-start.13) | collective-permute-done | bytes 262176 | tf_op jit(solution)/shard_map/ppermute | solution.py:19
  52.6 1.2 collective-permute-start.14
  53.8 2.7 %collective-permute-done.15.refs_17_ = bf16[8,64,256]{2,1,0:T(8,128)(2,1)} collective-permute-done((bf16[8,64,256]{2,1,0:T(8,128)(2,1)S(1)}, bf16[8,64,256]{2,1,0:T(8,128)(2,1)}, u32[]{:S(2)}, u32[]{:S(2)}) %collective-permute-start.15) | collective-permute-done | bytes 262176 | tf_op jit(solution)/shard_map/ppermute | solution.py:19
  56.5 1.9 %collective-permute-start.17 = (bf16[1,16,16,512]{3,2,1,0:T(8,128)(2,1)}, bf16[1,16,16,512]{3,2,1,0:T(8,128)(2,1)S(1)}, u32[]{:S(2)}, u32[]{:S(2)}) collective-permute-start(bf16[1,16,16,512]{3,2,1,0:T(8,128)(2,1)} %collective-permute-done.4.refs_12_), channel_id=1, source_target_pairs={{0,4},{4,0},{8,12},{12,8},{16,20},{20,16},{24,28},{28,24},{1,5},{5... | collective-permute-start | bytes 786440 | tf_op jit(solution)/shard_map/ppermute | solution.py:19
  58.4 1.9 %collective-permute-done.19 = bf16[2,576,128]{2,1,0:T(8,128)(2,1)} collective-permute-done((bf16[2,576,128]{2,1,0:T(8,128)(2,1)S(1)}, bf16[2,576,128]{2,1,0:T(8,128)(2,1)}, u32[]{:S(2)}, u32[]{:S(2)}) %collective-permute-start.19) | collective-permute-done | bytes 294944 | tf_op jit(solution)/shard_map/ppermute | solution.py:19
  60.3 0.5 collective-permute-start.16
  60.8 1.0 pad_maximum_fusion.refs_4_
  61.9 3.1 %collective-permute-done.17.refs_15_ = bf16[1,16,16,512]{3,2,1,0:T(8,128)(2,1)S(1)} collective-permute-done((bf16[1,16,16,512]{3,2,1,0:T(8,128)(2,1)}, bf16[1,16,16,512]{3,2,1,0:T(8,128)(2,1)S(1)}, u32[]{:S(2)}, u32[]{:S(2)}) %collective-permute-start.17) | collective-permute-done | bytes 262176 | tf_op jit(solution)/shard_map/ppermute | solution.py:19
  65.0 2.9 %collective-permute-done.16.refs_14_ = bf16[1,16,16,512]{3,2,1,0:T(8,128)(2,1)S(1)} collective-permute-done((bf16[1,16,16,512]{3,2,1,0:T(8,128)(2,1)}, bf16[1,16,16,512]{3,2,1,0:T(8,128)(2,1)S(1)}, u32[]{:S(2)}, u32[]{:S(2)}) %collective-permute-start.16) | collective-permute-done | bytes 262176 | tf_op jit(solution)/shard_map/ppermute | solution.py:19
  67.9 1.0 collective-permute-start.20
  69.0 1.7 %collective-permute-start.23 = (f32[128,512]{1,0:T(8,128)S(1)}, f32[128,512]{1,0:T(8,128)S(1)}, u32[]{:S(2)}, u32[]{:S(2)}) collective-permute-start(f32[128,512]{1,0:T(8,128)S(1)} %bitcast_add_fusion.2), channel_id=1, source_target_pairs={{0,16},{4,20},{8,24},{12,28},{16,0},{20,4},{24,8},{28,12},{1,17},{... | collective-permute-start | bytes 786440 | tf_op jit(solution)/shard_map/ppermute | solution.py:19
  70.7 0.7 copy-done.15
  71.4 21.9 %shard_map.102 = (f32[576,1152]{1,0:T(8,128)}, f32[64,1280]{1,0:T(8,128)}, f32[576,1152]{1,0:T(8,128)}, f32[64,1280]{1,0:T(8,128)}) custom-call(bf16[1,16,16,512]{3,2,1,0:T(8,128)(2,1)} %refs_0_.2, bf16[1,16,16,512]{3,2,1,0:T(8,128)(2,1)} %collective-permute-done.7.refs_1_, bf16[1,16,16,512]{3,2,1,0:T(8,128)(2,1)} %copy-done.11, ...), custom_call_target="tpu_custom_call" | custom-call | flops 12079595520 | bytes 11796480 | tf_op jit(solution)/shard_map/pallas_call | solution.py:174
  93.4 1.8 %collective-permute-done.24.theirs_ref = f32[64,1280]{1,0:T(8,128)S(1)} collective-permute-done((f32[64,1280]{1,0:T(8,128)}, f32[64,1280]{1,0:T(8,128)S(1)}, u32[]{:S(2)}, u32[]{:S(2)}) %collective-permute-start.24) | collective-permute-done | bytes 327712 | tf_op jit(solution)/shard_map/ppermute | solution.py:19
  95.3 1.0 copy-done.1
  96.3 0.6 collective-permute-start.25
  97.0 3.1 %collective-permute-start.26 = (f16[64,1280]{1,0:T(8,128)(2,1)S(1)}, f16[64,1280]{1,0:T(8,128)(2,1)S(1)}, u32[]{:S(2)}, u32[]{:S(2)}) collective-permute-start(f16[64,1280]{1,0:T(8,128)(2,1)S(1)} %convert_element_type.54), channel_id=1, source_target_pairs={{0,8},{4,12},{8,16},{12,20},{16,24},{20,28},{24,0},{28,4},{1,9},{5... | collective-permute-start | bytes 491528 | tf_op jit(solution)/shard_map/ppermute | solution.py:19
  100.1 0.1 collective-permute-start.28
  100.2 2.2 %collective-permute-start.29 = (f16[64,1280]{1,0:T(8,128)(2,1)S(1)}, f16[64,1280]{1,0:T(8,128)(2,1)S(1)}, u32[]{:S(2)}, u32[]{:S(2)}) collective-permute-start(f16[64,1280]{1,0:T(8,128)(2,1)S(1)} %convert_element_type.54), channel_id=1, source_target_pairs={{0,24},{4,28},{8,0},{12,4},{16,8},{20,12},{24,16},{28,20},{1,25},{... | collective-permute-start | bytes 491528 | tf_op jit(solution)/shard_map/ppermute | solution.py:19
  102.8 5.1 %shard_map.104 = (bf16[1,16,16,128]{3,2,1,0:T(8,128)(2,1)}, bf16[1,16,16,128]{3,2,1,0:T(8,128)(2,1)}, bf16[1,16,16,128]{3,2,1,0:T(8,128)(2,1)}, bf16[1,16,16,128]{3,2,1,0:T(8,128)(2,1)}) custom-call(bf16[1,16,16,512]{3,2,1,0:T(8,128)(2,1)} %refs_0_.2, bf16[1,16,16,512]{3,2,1,0:T(8,128)(2,1)} %copy-done.11, bf16[1,16,16,512]{3,2,1,0:T(8,128)(2,1)} %copy-done.13, ...), custom_call_target="tpu_custom_call" | custom-call | flops 2415919104 | bytes 2228224 | tf_op jit(solution)/shard_map/pallas_call | solution.py:328
  107.9 1.5 %collective-permute-start.27 = (f16[64,1280]{1,0:T(8,128)(2,1)S(1)}, f16[64,1280]{1,0:T(8,128)(2,1)S(1)}, u32[]{:S(2)}, u32[]{:S(2)}) collective-permute-start(f16[64,1280]{1,0:T(8,128)(2,1)S(1)} %collective-permute-done.26), channel_id=1, source_target_pairs={{0,4},{4,0},{8,12},{12,8},{16,20},{20,16},{24,28},{28,24},{1,5},{5... | collective-permute-start | bytes 491528 | tf_op jit(solution)/shard_map/ppermute | solution.py:19
  109.4 2.4 %collective-permute-done.28 = f16[64,1280]{1,0:T(8,128)(2,1)S(1)} collective-permute-done((f16[64,1280]{1,0:T(8,128)(2,1)S(1)}, f16[64,1280]{1,0:T(8,128)(2,1)S(1)}, u32[]{:S(2)}, u32[]{:S(2)}) %collective-permute-start.28) | collective-permute-done | bytes 163872 | tf_op jit(solution)/shard_map/ppermute | solution.py:19
  111.8 1.5 collective-permute-start.30
  113.3 0.6 collective-permute-start.31
  114.0 0.1 exponential_reduce_fusion.5
  114.9 4.0 %collective-permute-done.30 = f16[64,1280]{1,0:T(8,128)(2,1)S(1)} collective-permute-done((f16[64,1280]{1,0:T(8,128)(2,1)S(1)}, f16[64,1280]{1,0:T(8,128)(2,1)S(1)}, u32[]{:S(2)}, u32[]{:S(2)}) %collective-permute-start.30) | collective-permute-done | bytes 163872 | tf_op jit(solution)/shard_map/ppermute | solution.py:19
  119.0 2.6 %collective-permute-done.31 = f16[64,1280]{1,0:T(8,128)(2,1)S(1)} collective-permute-done((f16[64,1280]{1,0:T(8,128)(2,1)S(1)}, f16[64,1280]{1,0:T(8,128)(2,1)S(1)}, u32[]{:S(2)}, u32[]{:S(2)}) %collective-permute-start.31) | collective-permute-done | bytes 163872 | tf_op jit(solution)/shard_map/ppermute | solution.py:19
  122.1 5.7 %shard_map.105 = (f32[576,256]{1,0:T(8,128)S(1)}, f32[576,256]{1,0:T(8,128)S(1)}) custom-call(f32[576,1152]{1,0:T(8,128)S(1)} %copy-done.3, f32[512,512]{1,0:T(8,128)S(1)} %copy-done.4, f32[64,1152]{1,0:T(8,128)S(1)} %convert_multiply_fusion.7.refs_2_, f32[64,1152]{1,0:T(8,128)S(1)} %convert_multiply_fusion.6.refs_3_, ...), custom_call_target="tpu_custom_call" | custom-call | flops 2944401408 | bytes 3833856 | tf_op jit(solution)/shard_map/pallas_call | solution.py:272
  127.9 1.5 %collective-permute-start.37 = (f32[128,512]{1,0:T(8,128)S(1)}, f32[128,512]{1,0:T(8,128)S(1)}, u32[]{:S(2)}, u32[]{:S(2)}) collective-permute-start(f32[128,512]{1,0:T(8,128)S(1)} %add.70), channel_id=1, source_target_pairs={{0,4},{4,0},{8,12},{12,8},{16,20},{20,16},{24,28},{28,24},{1,5},{5... | collective-permute-start | bytes 786440 | tf_op jit(solution)/shard_map/ppermute | solution.py:19
  129.4 0.5 collective-permute-start.32
  130.0 1.6 %collective-permute-start.34 = (bf16[1,16,16,128]{3,2,1,0:T(8,128)(2,1)S(1)}, bf16[1,16,16,128]{3,2,1,0:T(8,128)(2,1)S(1)}, u32[]{:S(2)}, u32[]{:S(2)}) collective-permute-start(bf16[1,16,16,128]{3,2,1,0:T(8,128)(2,1)S(1)} %copy-done.18), channel_id=1, source_target_pairs={{0,3},{1,2},{2,1},{3,0},{4,7},{5,6},{6,5},{7,4},{8,11},{9,10},{10,... | collective-permute-start | bytes 196616 | tf_op jit(solution)/shard_map/ppermute | solution.py:19
  131.7 4.9 %collective-permute-done.37 = f32[128,512]{1,0:T(8,128)S(1)} collective-permute-done((f32[128,512]{1,0:T(8,128)S(1)}, f32[128,512]{1,0:T(8,128)S(1)}, u32[]{:S(2)}, u32[]{:S(2)}) %collective-permute-start.37) | collective-permute-done | bytes 262176 | tf_op jit(solution)/shard_map/ppermute | solution.py:19
  136.7 3.9 %collective-permute-start.38 = (f32[128,512]{1,0:T(8,128)S(1)}, f32[128,512]{1,0:T(8,128)S(1)}, u32[]{:S(2)}, u32[]{:S(2)}) collective-permute-start(f32[128,512]{1,0:T(8,128)S(1)} %add.74), channel_id=1, source_target_pairs={{0,8},{4,12},{8,0},{12,4},{16,24},{20,28},{24,16},{28,20},{1,9},{5... | collective-permute-start | bytes 786440 | tf_op jit(solution)/shard_map/ppermute | solution.py:19
  140.6 0.5 collective-permute-start.39
  141.1 2.0 %bitcast_add_fusion = f32[1152,576]{0,1:T(8,128)} fusion(f32[576,1152]{1,0:T(8,128)S(1)} %copy-done.6, f32[576,1152]{1,0:T(8,128)S(1)} %collective-permute-done.35, f32[1152,576]{0,1:T(8,128)S(1)} %copy-done.5), kind=kLoop, calls=%fused_computation | loop fusion | flops 2654208 | bytes 10616832 | tf_op jit(solution)/shard_map/add | solution.py:607
  143.2 0.8 shard_map.106
  144.0 2.8 %collective-permute-done.38 = f32[128,512]{1,0:T(8,128)S(1)} collective-permute-done((f32[128,512]{1,0:T(8,128)S(1)}, f32[128,512]{1,0:T(8,128)S(1)}, u32[]{:S(2)}, u32[]{:S(2)}) %collective-permute-start.38) | collective-permute-done | bytes 262176 | tf_op jit(solution)/shard_map/ppermute | solution.py:19
  146.7 2.2 %collective-permute-done.39 = f32[576,128]{1,0:T(8,128)S(1)} collective-permute-done((f32[576,128]{1,0:T(8,128)S(1)}, f32[576,128]{1,0:T(8,128)S(1)}, u32[]{:S(2)}, u32[]{:S(2)}) %collective-permute-start.39) | collective-permute-done | bytes 294944 | tf_op jit(solution)/shard_map/ppermute | solution.py:19
  148.9 0.7 fusion
  149.6 0.8 add_multiply_fusion
  (98 shorter events, 2.5 us)
Async XLA Ops:
  0.6 31.4 %copy-start = (bf16[576,512]{1,0:T(8,128)(2,1)S(1)}, bf16[576,512]{1,0:T(8,128)(2,1)}, u32[]{:S(2)}) copy-start(bf16[576,512]{1,0:T(8,128)(2,1)} %param.9) | copy-start | bytes 1769476
  0.6 12.5 %collective-permute-start.1 = (bf16[1,16,16,512]{3,2,1,0:T(8,128)(2,1)}, bf16[1,16,16,512]{3,2,1,0:T(8,128)(2,1)S(1)}, u32[]{:S(2)}, u32[]{:S(2)}) collective-permute-start(bf16[1,16,16,512]{3,2,1,0:T(8,128)(2,1)} %refs_0_.2), channel_id=1, source_target_pairs={{0,8},{4,12},{8,16},{12,20},{16,24},{20,28},{24,0},{28,4},{1,9},{5... | collective-permute-start | bytes 786440 | tf_op jit(solution)/shard_map/ppermute | solution.py:19
  3.7 17.7 %collective-permute-start = (bf16[1,16,16,512]{3,2,1,0:T(8,128)(2,1)}, bf16[1,16,16,512]{3,2,1,0:T(8,128)(2,1)S(1)}, u32[]{:S(2)}, u32[]{:S(2)}) collective-permute-start(bf16[1,16,16,512]{3,2,1,0:T(8,128)(2,1)} %refs_0_.2), channel_id=1, source_target_pairs={{0,2},{1,3},{2,0},{3,1},{4,6},{5,7},{6,4},{7,5},{8,10},{9,11},{10,... | collective-permute-start | bytes 786440 | tf_op jit(solution)/shard_map/ppermute | solution.py:19
  5.2 17.7 %collective-permute-start.7 = (bf16[1,16,16,512]{3,2,1,0:T(8,128)(2,1)}, bf16[1,16,16,512]{3,2,1,0:T(8,128)(2,1)}, u32[]{:S(2)}, u32[]{:S(2)}) collective-permute-start(bf16[1,16,16,512]{3,2,1,0:T(8,128)(2,1)} %refs_0_.2), channel_id=1, source_target_pairs={{0,4},{4,0},{8,12},{12,8},{16,20},{20,16},{24,28},{28,24},{1,5},{5... | collective-permute-start | bytes 786440 | tf_op jit(solution)/shard_map/ppermute | solution.py:19
  6.7 26.9 %collective-permute-start.8 = (bf16[1,16,16,512]{3,2,1,0:T(8,128)(2,1)}, bf16[1,16,16,512]{3,2,1,0:T(8,128)(2,1)}, u32[]{:S(2)}, u32[]{:S(2)}) collective-permute-start(bf16[1,16,16,512]{3,2,1,0:T(8,128)(2,1)} %refs_0_.2), channel_id=1, source_target_pairs={{0,24},{4,28},{8,0},{12,4},{16,8},{20,12},{24,16},{28,20},{1,25},{... | collective-permute-start | bytes 786440 | tf_op jit(solution)/shard_map/ppermute | solution.py:19
  13.1 29.5 %copy-start.12 = (bf16[1,16,16,512]{3,2,1,0:T(8,128)(2,1)}, bf16[1,16,16,512]{3,2,1,0:T(8,128)(2,1)S(1)}, u32[]{:S(2)}) copy-start(bf16[1,16,16,512]{3,2,1,0:T(8,128)(2,1)S(1)} %collective-permute-done.1.refs_3_) | copy-start | bytes 786436
  13.1 17.1 %collective-permute-start.2 = (bf16[1,16,16,512]{3,2,1,0:T(8,128)(2,1)}, bf16[1,16,16,512]{3,2,1,0:T(8,128)(2,1)}, u32[]{:S(2)}, u32[]{:S(2)}) collective-permute-start(bf16[1,16,16,512]{3,2,1,0:T(8,128)(2,1)} %refs_0_.2), channel_id=1, source_target_pairs={{0,16},{4,20},{8,24},{12,28},{16,0},{20,4},{24,8},{28,12},{1,17},{... | collective-permute-start | bytes 786440 | tf_op jit(solution)/shard_map/ppermute | solution.py:19
  21.4 4.8 %copy-start.11 = (bf16[1,16,16,512]{3,2,1,0:T(8,128)(2,1)}, bf16[1,16,16,512]{3,2,1,0:T(8,128)(2,1)S(1)}, u32[]{:S(2)}) copy-start(bf16[1,16,16,512]{3,2,1,0:T(8,128)(2,1)S(1)} %collective-permute-done.refs_2_.refs_1_) | copy-start | bytes 786436
  21.4 10.7 %collective-permute-start.3 = (bf16[1,16,16,512]{3,2,1,0:T(8,128)(2,1)S(1)}, bf16[1,16,16,512]{3,2,1,0:T(8,128)(2,1)}, u32[]{:S(2)}, u32[]{:S(2)}) collective-permute-start(bf16[1,16,16,512]{3,2,1,0:T(8,128)(2,1)S(1)} %collective-permute-done.1.refs_3_), channel_id=1, source_target_pairs={{0,2},{1,3},{2,0},{3,1},{4,6},{5,7},{6,4},{7,5},{8,10},{9,11},{10,... | collective-permute-start | bytes 786440 | tf_op jit(solution)/shard_map/ppermute | solution.py:19
  26.1 20.9 %collective-permute-start.21 = (f32[2,128,512]{2,1,0:T(8,128)S(1)}, f32[2,128,512]{2,1,0:T(8,128)S(1)}, u32[]{:S(2)}, u32[]{:S(2)}) collective-permute-start(f32[2,128,512]{2,1,0:T(8,128)S(1)} %dynamic-slice_bitcast_fusion), channel_id=1, source_target_pairs={{0,1},{1,0},{2,3},{3,2},{4,5},{5,4},{6,7},{7,6},{8,9},{9,8},{10,11... | collective-permute-start | bytes 1572872 | tf_op jit(solution)/shard_map/ppermute | solution.py:19
  26.2 17.2 %all-to-all-start = ((bf16[8,64,256]{2,1,0:T(8,128)(2,1)}), bf16[8,64,256]{2,1,0:T(8,128)(2,1)S(1)}, u32[]{:S(2)}, u32[]{:S(2)}) async-start(bf16[8,64,256]{2,1,0:T(8,128)(2,1)} %bitcast.2), calls=%async_computation | async-start | bytes 524288 | tf_op jit(solution)/shard_map/all_to_all | solution.py:446
  29.6 9.5 %collective-permute-start.9 = (bf16[1,16,16,512]{3,2,1,0:T(8,128)(2,1)}, bf16[1,16,16,512]{3,2,1,0:T(8,128)(2,1)}, u32[]{:S(2)}, u32[]{:S(2)}) collective-permute-start(bf16[1,16,16,512]{3,2,1,0:T(8,128)(2,1)} %collective-permute-done.7.refs_1_), channel_id=1, source_target_pairs={{0,2},{1,3},{2,0},{3,1},{4,6},{5,7},{6,4},{7,5},{8,10},{9,11},{10,... | collective-permute-start | bytes 786440 | tf_op jit(solution)/shard_map/ppermute | solution.py:19
  30.2 11.1 %collective-permute-start.10 = (bf16[1,16,16,512]{3,2,1,0:T(8,128)(2,1)S(1)}, bf16[1,16,16,512]{3,2,1,0:T(8,128)(2,1)}, u32[]{:S(2)}, u32[]{:S(2)}) collective-permute-start(bf16[1,16,16,512]{3,2,1,0:T(8,128)(2,1)S(1)} %collective-permute-done.1.refs_3_), channel_id=1, source_target_pairs={{0,4},{4,0},{8,12},{12,8},{16,20},{20,16},{24,28},{28,24},{1,5},{5... | collective-permute-start | bytes 786440 | tf_op jit(solution)/shard_map/ppermute | solution.py:19
  32.1 10.6 %collective-permute-start.18 = (bf16[1,576,128]{2,1,0:T(8,128)(2,1)S(1)}, bf16[1,576,128]{2,1,0:T(8,128)(2,1)S(1)}, u32[]{:S(2)}, u32[]{:S(2)}) collective-permute-start(bf16[1,576,128]{2,1,0:T(8,128)(2,1)S(1)} %dynamic-slice_bitcast_fusion.2), channel_id=1, source_target_pairs={{0,8},{4,12},{8,0},{12,4},{16,24},{20,28},{24,16},{28,20},{1,9},{5... | collective-permute-start | bytes 442376 | tf_op jit(solution)/shard_map/ppermute | solution.py:19
  33.6 11.0 %collective-permute-start.4 = (bf16[1,16,16,512]{3,2,1,0:T(8,128)(2,1)}, bf16[1,16,16,512]{3,2,1,0:T(8,128)(2,1)}, u32[]{:S(2)}, u32[]{:S(2)}) collective-permute-start(bf16[1,16,16,512]{3,2,1,0:T(8,128)(2,1)} %collective-permute-done.2.refs_8_), channel_id=1, source_target_pairs={{0,2},{1,3},{2,0},{3,1},{4,6},{5,7},{6,4},{7,5},{8,10},{9,11},{10,... | collective-permute-start | bytes 786440 | tf_op jit(solution)/shard_map/ppermute | solution.py:19
  39.1 9.6 %collective-permute-start.11 = (bf16[1,16,16,512]{3,2,1,0:T(8,128)(2,1)}, bf16[1,16,16,512]{3,2,1,0:T(8,128)(2,1)}, u32[]{:S(2)}, u32[]{:S(2)}) collective-permute-start(bf16[1,16,16,512]{3,2,1,0:T(8,128)(2,1)} %collective-permute-done.8.refs_4_), channel_id=1, source_target_pairs={{0,4},{4,0},{8,12},{12,8},{16,20},{20,16},{24,28},{28,24},{1,5},{5... | collective-permute-start | bytes 786440 | tf_op jit(solution)/shard_map/ppermute | solution.py:19
  41.3 12.5 %collective-permute-start.12 = (bf16[1,16,16,512]{3,2,1,0:T(8,128)(2,1)}, bf16[1,16,16,512]{3,2,1,0:T(8,128)(2,1)}, u32[]{:S(2)}, u32[]{:S(2)}) collective-permute-start(bf16[1,16,16,512]{3,2,1,0:T(8,128)(2,1)} %collective-permute-done.8.refs_4_), channel_id=1, source_target_pairs={{0,2},{1,3},{2,0},{3,1},{4,6},{5,7},{6,4},{7,5},{8,10},{9,11},{10,... | collective-permute-start | bytes 786440 | tf_op jit(solution)/shard_map/ppermute | solution.py:19
  42.7 9.9 %collective-permute-start.13 = (bf16[1,16,16,512]{3,2,1,0:T(8,128)(2,1)}, bf16[1,16,16,512]{3,2,1,0:T(8,128)(2,1)}, u32[]{:S(2)}, u32[]{:S(2)}) collective-permute-start(bf16[1,16,16,512]{3,2,1,0:T(8,128)(2,1)} %collective-permute-done.2.refs_8_), channel_id=1, source_target_pairs={{0,4},{4,0},{8,12},{12,8},{16,20},{20,16},{24,28},{28,24},{1,5},{5... | collective-permute-start | bytes 786440 | tf_op jit(solution)/shard_map/ppermute | solution.py:19
  43.4 27.3 %copy-start.8 = (bf16[8,64,256]{2,1,0:T(8,128)(2,1)}, bf16[8,64,256]{2,1,0:T(8,128)(2,1)S(1)}, u32[]{:S(2)}) copy-start(bf16[8,64,256]{2,1,0:T(8,128)(2,1)S(1)} %all-to-all-done.refs_16_) | copy-start | bytes 786436
  44.6 15.6 %collective-permute-start.19 = (bf16[2,576,128]{2,1,0:T(8,128)(2,1)S(1)}, bf16[2,576,128]{2,1,0:T(8,128)(2,1)}, u32[]{:S(2)}, u32[]{:S(2)}) collective-permute-start(bf16[2,576,128]{2,1,0:T(8,128)(2,1)S(1)} %pad_maximum_fusion.1), channel_id=1, source_target_pairs={{0,16},{4,20},{8,24},{12,28},{16,0},{20,4},{24,8},{28,12},{1,17},{... | collective-permute-start | bytes 884744 | tf_op jit(solution)/shard_map/ppermute | solution.py:19
  47.0 9.5 %collective-permute-start.15 = (bf16[8,64,256]{2,1,0:T(8,128)(2,1)S(1)}, bf16[8,64,256]{2,1,0:T(8,128)(2,1)}, u32[]{:S(2)}, u32[]{:S(2)}) collective-permute-start(bf16[8,64,256]{2,1,0:T(8,128)(2,1)S(1)} %all-to-all-done.refs_16_), channel_id=1, source_target_pairs={{0,2},{1,3},{2,0},{3,1},{4,6},{5,7},{6,4},{7,5},{8,10},{9,11},{10,... | collective-permute-start | bytes 786440 | tf_op jit(solution)/shard_map/ppermute | solution.py:19
  48.7 13.1 %collective-permute-start.22 = (f32[128,512]{1,0:T(8,128)S(1)}, f32[128,512]{1,0:T(8,128)S(1)}, u32[]{:S(2)}, u32[]{:S(2)}) collective-permute-start(f32[128,512]{1,0:T(8,128)S(1)} %dynamic-slice_bitcast_fusion.1), channel_id=1, source_target_pairs={{0,2},{1,3},{2,0},{3,1},{4,6},{5,7},{6,4},{7,5},{8,10},{9,11},{10,... | collective-permute-start | bytes 786440 | tf_op jit(solution)/shard_map/ppermute | solution.py:19
  52.6 18.1 %collective-permute-start.14 = (bf16[1,16,16,512]{3,2,1,0:T(8,128)(2,1)}, bf16[1,16,16,512]{3,2,1,0:T(8,128)(2,1)S(1)}, u32[]{:S(2)}, u32[]{:S(2)}) collective-permute-start(bf16[1,16,16,512]{3,2,1,0:T(8,128)(2,1)} %collective-permute-done.3.refs_7_), channel_id=1, source_target_pairs={{0,4},{4,0},{8,12},{12,8},{16,20},{20,16},{24,28},{28,24},{1,5},{5... | collective-permute-start | bytes 786440 | tf_op jit(solution)/shard_map/ppermute | solution.py:19
  53.8 39.5 %collective-permute-start.5 = (bf16[1,16,16,512]{3,2,1,0:T(8,128)(2,1)}, bf16[1,16,16,512]{3,2,1,0:T(8,128)(2,1)S(1)}, u32[]{:S(2)}, u32[]{:S(2)}) collective-permute-start(bf16[1,16,16,512]{3,2,1,0:T(8,128)(2,1)} %refs_0_.2), channel_id=1, source_target_pairs={{0,1},{1,0},{2,3},{3,2},{4,5},{5,4},{6,7},{7,6},{8,9},{9,8},{10,11... | collective-permute-start | bytes 786440 | tf_op jit(solution)/shard_map/ppermute | solution.py:19
  56.5 8.5 %collective-permute-start.17 = (bf16[1,16,16,512]{3,2,1,0:T(8,128)(2,1)}, bf16[1,16,16,512]{3,2,1,0:T(8,128)(2,1)S(1)}, u32[]{:S(2)}, u32[]{:S(2)}) collective-permute-start(bf16[1,16,16,512]{3,2,1,0:T(8,128)(2,1)} %collective-permute-done.4.refs_12_), channel_id=1, source_target_pairs={{0,4},{4,0},{8,12},{12,8},{16,20},{20,16},{24,28},{28,24},{1,5},{5... | collective-permute-start | bytes 786440 | tf_op jit(solution)/shard_map/ppermute | solution.py:19
  60.3 7.7 %collective-permute-start.16 = (bf16[1,16,16,512]{3,2,1,0:T(8,128)(2,1)}, bf16[1,16,16,512]{3,2,1,0:T(8,128)(2,1)S(1)}, u32[]{:S(2)}, u32[]{:S(2)}) collective-permute-start(bf16[1,16,16,512]{3,2,1,0:T(8,128)(2,1)} %collective-permute-done.11.refs_9_), channel_id=1, source_target_pairs={{0,2},{1,3},{2,0},{3,1},{4,6},{5,7},{6,4},{7,5},{8,10},{9,11},{10,... | collective-permute-start | bytes 786440 | tf_op jit(solution)/shard_map/ppermute | solution.py:19
  61.8 31.5 %copy-start.7 = (bf16[4,576,128]{2,1,0:T(8,128)(2,1)}, bf16[4,576,128]{2,1,0:T(8,128)(2,1)S(1)}, u32[]{:S(2)}) copy-start(bf16[4,576,128]{2,1,0:T(8,128)(2,1)S(1)} %pad_maximum_fusion.refs_4_) | copy-start | bytes 1769476
  61.8 31.5 %collective-permute-start.6 = (bf16[1,16,16,512]{3,2,1,0:T(8,128)(2,1)}, bf16[1,16,16,512]{3,2,1,0:T(8,128)(2,1)S(1)}, u32[]{:S(2)}, u32[]{:S(2)}) collective-permute-start(bf16[1,16,16,512]{3,2,1,0:T(8,128)(2,1)} %copy-done.11), channel_id=1, source_target_pairs={{0,1},{1,0},{2,3},{3,2},{4,5},{5,4},{6,7},{7,6},{8,9},{9,8},{10,11... | collective-permute-start | bytes 786440 | tf_op jit(solution)/shard_map/ppermute | solution.py:19
  65.0 5.7 %copy-start.16 = (bf16[1,16,16,512]{3,2,1,0:T(8,128)(2,1)}, bf16[1,16,16,512]{3,2,1,0:T(8,128)(2,1)S(1)}, u32[]{:S(2)}) copy-start(bf16[1,16,16,512]{3,2,1,0:T(8,128)(2,1)S(1)} %collective-permute-done.17.refs_15_) | copy-start | bytes 786436
  67.9 2.7 %copy-start.17 = (bf16[1,16,16,512]{3,2,1,0:T(8,128)(2,1)}, bf16[1,16,16,512]{3,2,1,0:T(8,128)(2,1)S(1)}, u32[]{:S(2)}) copy-start(bf16[1,16,16,512]{3,2,1,0:T(8,128)(2,1)S(1)} %collective-permute-done.16.refs_14_) | copy-start | bytes 786436
  67.9 25.4 %collective-permute-start.20 = (bf16[4,576,128]{2,1,0:T(8,128)(2,1)S(1)}, bf16[4,576,128]{2,1,0:T(8,128)(2,1)S(1)}, u32[]{:S(2)}, u32[]{:S(2)}) collective-permute-start(bf16[4,576,128]{2,1,0:T(8,128)(2,1)S(1)} %pad_maximum_fusion.refs_4_), channel_id=1, source_target_pairs={{0,4},{4,0},{8,12},{12,8},{16,20},{20,16},{24,28},{28,24},{1,5},{5... | collective-permute-start | bytes 1769480 | tf_op jit(solution)/shard_map/ppermute | solution.py:19
  69.0 24.3 %collective-permute-start.23 = (f32[128,512]{1,0:T(8,128)S(1)}, f32[128,512]{1,0:T(8,128)S(1)}, u32[]{:S(2)}, u32[]{:S(2)}) collective-permute-start(f32[128,512]{1,0:T(8,128)S(1)} %bitcast_add_fusion.2), channel_id=1, source_target_pairs={{0,16},{4,20},{8,24},{12,28},{16,0},{20,4},{24,8},{28,12},{1,17},{... | collective-permute-start | bytes 786440 | tf_op jit(solution)/shard_map/ppermute | solution.py:19
  70.7 0.7 copy-start.15
  93.3 9.3 %copy-start.13 = (bf16[1,16,16,512]{3,2,1,0:T(8,128)(2,1)}, bf16[1,16,16,512]{3,2,1,0:T(8,128)(2,1)S(1)}, u32[]{:S(2)}) copy-start(bf16[1,16,16,512]{3,2,1,0:T(8,128)(2,1)S(1)} %collective-permute-done.5.refs_2_) | copy-start | bytes 786436
  93.3 9.4 %copy-start.14 = (bf16[1,16,16,512]{3,2,1,0:T(8,128)(2,1)}, bf16[1,16,16,512]{3,2,1,0:T(8,128)(2,1)S(1)}, u32[]{:S(2)}) copy-start(bf16[1,16,16,512]{3,2,1,0:T(8,128)(2,1)S(1)} %collective-permute-done.6.refs_3_) | copy-start | bytes 786436
  93.4 1.9 %copy-start.10 = (bf16[4,576,128]{2,1,0:T(8,128)(2,1)}, bf16[4,576,128]{2,1,0:T(8,128)(2,1)S(1)}, u32[]{:S(2)}) copy-start(bf16[4,576,128]{2,1,0:T(8,128)(2,1)S(1)} %collective-permute-done.20.refs_5_) | copy-start | bytes 1769476
  93.4 1.9 %collective-permute-start.24 = (f32[64,1280]{1,0:T(8,128)}, f32[64,1280]{1,0:T(8,128)S(1)}, u32[]{:S(2)}, u32[]{:S(2)}) collective-permute-start(f32[64,1280]{1,0:T(8,128)} %get-tuple-element.73), channel_id=1, source_target_pairs={{0,1},{1,0},{2,3},{3,2},{4,5},{5,4},{6,7},{7,6},{8,9},{9,8},{10,11... | collective-permute-start | bytes 983048 | tf_op jit(solution)/shard_map/ppermute | solution.py:19
  95.3 1.0 copy-start.1
  96.3 18.1 %collective-permute-start.25 = (f16[64,1280]{1,0:T(8,128)(2,1)S(1)}, f16[64,1280]{1,0:T(8,128)(2,1)S(1)}, u32[]{:S(2)}, u32[]{:S(2)}) collective-permute-start(f16[64,1280]{1,0:T(8,128)(2,1)S(1)} %convert_element_type.54), channel_id=1, source_target_pairs={{0,4},{4,0},{8,12},{12,8},{16,20},{20,16},{24,28},{28,24},{1,5},{5... | collective-permute-start | bytes 491528 | tf_op jit(solution)/shard_map/ppermute | solution.py:19
  97.0 10.9 %collective-permute-start.26 = (f16[64,1280]{1,0:T(8,128)(2,1)S(1)}, f16[64,1280]{1,0:T(8,128)(2,1)S(1)}, u32[]{:S(2)}, u32[]{:S(2)}) collective-permute-start(f16[64,1280]{1,0:T(8,128)(2,1)S(1)} %convert_element_type.54), channel_id=1, source_target_pairs={{0,8},{4,12},{8,16},{12,20},{16,24},{20,28},{24,0},{28,4},{1,9},{5... | collective-permute-start | bytes 491528 | tf_op jit(solution)/shard_map/ppermute | solution.py:19
  100.1 11.7 %collective-permute-start.28 = (f16[64,1280]{1,0:T(8,128)(2,1)S(1)}, f16[64,1280]{1,0:T(8,128)(2,1)S(1)}, u32[]{:S(2)}, u32[]{:S(2)}) collective-permute-start(f16[64,1280]{1,0:T(8,128)(2,1)S(1)} %convert_element_type.54), channel_id=1, source_target_pairs={{0,16},{4,20},{8,24},{12,28},{16,0},{20,4},{24,8},{28,12},{1,17},{... | collective-permute-start | bytes 491528 | tf_op jit(solution)/shard_map/ppermute | solution.py:19
  100.2 11.6 %collective-permute-start.29 = (f16[64,1280]{1,0:T(8,128)(2,1)S(1)}, f16[64,1280]{1,0:T(8,128)(2,1)S(1)}, u32[]{:S(2)}, u32[]{:S(2)}) collective-permute-start(f16[64,1280]{1,0:T(8,128)(2,1)S(1)} %convert_element_type.54), channel_id=1, source_target_pairs={{0,24},{4,28},{8,0},{12,4},{16,8},{20,12},{24,16},{28,20},{1,25},{... | collective-permute-start | bytes 491528 | tf_op jit(solution)/shard_map/ppermute | solution.py:19
  102.6 19.4 %collective-permute-start.35 = (f32[576,1152]{1,0:T(8,128)}, f32[576,1152]{1,0:T(8,128)S(1)}, u32[]{:S(2)}, u32[]{:S(2)}) collective-permute-start(f32[576,1152]{1,0:T(8,128)} %get-tuple-element.90), channel_id=1, source_target_pairs={{0,1},{1,0},{2,3},{3,2},{4,5},{5,4},{6,7},{7,6},{8,9},{9,8},{10,11... | collective-permute-start | bytes 7962632 | tf_op jit(solution)/shard_map/ppermute | solution.py:19
  102.8 19.3 %copy-start.4 = (f32[512,512]{1,0:T(8,128)S(1)}, f32[512,512]{1,0:T(8,128)}, u32[]{:S(2)}) copy-start(f32[512,512]{1,0:T(8,128)} %refs_1_.1) | copy-start | bytes 3145732
  107.9 14.2 %copy-start.3 = (f32[576,1152]{1,0:T(8,128)S(1)}, f32[576,1152]{1,0:T(8,128)}, u32[]{:S(2)}) copy-start(f32[576,1152]{1,0:T(8,128)} %refs_0_.3) | copy-start | bytes 7962628
  107.9 6.8 %collective-permute-start.27 = (f16[64,1280]{1,0:T(8,128)(2,1)S(1)}, f16[64,1280]{1,0:T(8,128)(2,1)S(1)}, u32[]{:S(2)}, u32[]{:S(2)}) collective-permute-start(f16[64,1280]{1,0:T(8,128)(2,1)S(1)} %collective-permute-done.26), channel_id=1, source_target_pairs={{0,4},{4,0},{8,12},{12,8},{16,20},{20,16},{24,28},{28,24},{1,5},{5... | collective-permute-start | bytes 491528 | tf_op jit(solution)/shard_map/ppermute | solution.py:19
  111.8 7.1 %collective-permute-start.30 = (f16[64,1280]{1,0:T(8,128)(2,1)S(1)}, f16[64,1280]{1,0:T(8,128)(2,1)S(1)}, u32[]{:S(2)}, u32[]{:S(2)}) collective-permute-start(f16[64,1280]{1,0:T(8,128)(2,1)S(1)} %collective-permute-done.28), channel_id=1, source_target_pairs={{0,4},{4,0},{8,12},{12,8},{16,20},{20,16},{24,28},{28,24},{1,5},{5... | collective-permute-start | bytes 491528 | tf_op jit(solution)/shard_map/ppermute | solution.py:19
  113.3 8.3 %collective-permute-start.31 = (f16[64,1280]{1,0:T(8,128)(2,1)S(1)}, f16[64,1280]{1,0:T(8,128)(2,1)S(1)}, u32[]{:S(2)}, u32[]{:S(2)}) collective-permute-start(f16[64,1280]{1,0:T(8,128)(2,1)S(1)} %collective-permute-done.29), channel_id=1, source_target_pairs={{0,4},{4,0},{8,12},{12,8},{16,20},{20,16},{24,28},{28,24},{1,5},{5... | collective-permute-start | bytes 491528 | tf_op jit(solution)/shard_map/ppermute | solution.py:19
  122.0 7.5 %copy-start.20 = (bf16[1,16,16,128]{3,2,1,0:T(8,128)(2,1)S(1)}, bf16[1,16,16,128]{3,2,1,0:T(8,128)(2,1)}, u32[]{:S(2)}) copy-start(bf16[1,16,16,128]{3,2,1,0:T(8,128)(2,1)} %get-tuple-element.86) | copy-start | bytes 196612
  122.0 8.0 %copy-start.19 = (bf16[1,16,16,128]{3,2,1,0:T(8,128)(2,1)S(1)}, bf16[1,16,16,128]{3,2,1,0:T(8,128)(2,1)}, u32[]{:S(2)}) copy-start(bf16[1,16,16,128]{3,2,1,0:T(8,128)(2,1)} %get-tuple-element.87) | copy-start | bytes 196612
  122.0 8.0 %copy-start.18 = (bf16[1,16,16,128]{3,2,1,0:T(8,128)(2,1)S(1)}, bf16[1,16,16,128]{3,2,1,0:T(8,128)(2,1)}, u32[]{:S(2)}) copy-start(bf16[1,16,16,128]{3,2,1,0:T(8,128)(2,1)} %get-tuple-element.88) | copy-start | bytes 196612
  122.1 19.1 %copy-start.6 = (f32[576,1152]{1,0:T(8,128)S(1)}, f32[576,1152]{1,0:T(8,128)}, u32[]{:S(2)}) copy-start(f32[576,1152]{1,0:T(8,128)} %get-tuple-element.98) | copy-start | bytes 7962628
  127.8 13.3 %copy-start.5 = (f32[1152,576]{0,1:T(8,128)S(1)}, f32[1152,576]{0,1:T(8,128)}, u32[]{:S(2)}) copy-start(f32[1152,576]{0,1:T(8,128)} %param.10) | copy-start | bytes 7962628
  127.8 3.8 %collective-permute-start.36 = (f32[576,256]{1,0:T(8,128)S(1)}, f32[576,256]{1,0:T(8,128)S(1)}, u32[]{:S(2)}, u32[]{:S(2)}) collective-permute-start(f32[576,256]{1,0:T(8,128)S(1)} %get-tuple-element.93), channel_id=1, source_target_pairs={{0,1},{1,0},{2,3},{3,2},{4,5},{5,4},{6,7},{7,6},{8,9},{9,8},{10,11... | collective-permute-start | bytes 1769480 | tf_op jit(solution)/shard_map/ppermute | solution.py:19
  127.9 8.7 %collective-permute-start.37 = (f32[128,512]{1,0:T(8,128)S(1)}, f32[128,512]{1,0:T(8,128)S(1)}, u32[]{:S(2)}, u32[]{:S(2)}) collective-permute-start(f32[128,512]{1,0:T(8,128)S(1)} %add.70), channel_id=1, source_target_pairs={{0,4},{4,0},{8,12},{12,8},{16,20},{20,16},{24,28},{28,24},{1,5},{5... | collective-permute-start | bytes 786440 | tf_op jit(solution)/shard_map/ppermute | solution.py:19
  129.4 13.7 %collective-permute-start.32 = (bf16[1,16,16,128]{3,2,1,0:T(8,128)(2,1)S(1)}, bf16[1,16,16,128]{3,2,1,0:T(8,128)(2,1)S(1)}, u32[]{:S(2)}, u32[]{:S(2)}) collective-permute-start(bf16[1,16,16,128]{3,2,1,0:T(8,128)(2,1)S(1)} %copy-done.20), channel_id=1, source_target_pairs={{0,2},{1,3},{2,0},{3,1},{4,6},{5,7},{6,4},{7,5},{8,10},{9,11},{10,... | collective-permute-start | bytes 196616 | tf_op jit(solution)/shard_map/ppermute | solution.py:19
  130.0 13.2 %collective-permute-start.33 = (bf16[1,16,16,128]{3,2,1,0:T(8,128)(2,1)S(1)}, bf16[1,16,16,128]{3,2,1,0:T(8,128)(2,1)S(1)}, u32[]{:S(2)}, u32[]{:S(2)}) collective-permute-start(bf16[1,16,16,128]{3,2,1,0:T(8,128)(2,1)S(1)} %copy-done.19), channel_id=1, source_target_pairs={{0,1},{1,0},{2,3},{3,2},{4,5},{5,4},{6,7},{7,6},{8,9},{9,8},{10,11... | collective-permute-start | bytes 196616 | tf_op jit(solution)/shard_map/ppermute | solution.py:19
  130.0 13.2 %collective-permute-start.34 = (bf16[1,16,16,128]{3,2,1,0:T(8,128)(2,1)S(1)}, bf16[1,16,16,128]{3,2,1,0:T(8,128)(2,1)S(1)}, u32[]{:S(2)}, u32[]{:S(2)}) collective-permute-start(bf16[1,16,16,128]{3,2,1,0:T(8,128)(2,1)S(1)} %copy-done.18), channel_id=1, source_target_pairs={{0,3},{1,2},{2,1},{3,0},{4,7},{5,6},{6,5},{7,4},{8,11},{9,10},{10,... | collective-permute-start | bytes 196616 | tf_op jit(solution)/shard_map/ppermute | solution.py:19
  136.7 10.0 %collective-permute-start.38 = (f32[128,512]{1,0:T(8,128)S(1)}, f32[128,512]{1,0:T(8,128)S(1)}, u32[]{:S(2)}, u32[]{:S(2)}) collective-permute-start(f32[128,512]{1,0:T(8,128)S(1)} %add.74), channel_id=1, source_target_pairs={{0,8},{4,12},{8,0},{12,4},{16,24},{20,28},{24,16},{28,20},{1,9},{5... | collective-permute-start | bytes 786440 | tf_op jit(solution)/shard_map/ppermute | solution.py:19
  140.6 8.3 %collective-permute-start.39 = (f32[576,128]{1,0:T(8,128)S(1)}, f32[576,128]{1,0:T(8,128)S(1)}, u32[]{:S(2)}, u32[]{:S(2)}) collective-permute-start(f32[576,128]{1,0:T(8,128)S(1)} %slice.91), channel_id=1, source_target_pairs={{0,2},{1,3},{2,0},{3,1},{4,6},{5,7},{6,4},{7,5},{8,10},{9,11},{10,... | collective-permute-start | bytes 884744 | tf_op jit(solution)/shard_map/ppermute | solution.py:19
  141.1 2.1 %copy-start.2 = (bf16[1,16,16,128]{3,2,1,0:T(8,128)(2,1)S(1)}, bf16[1,16,16,128]{3,2,1,0:T(8,128)(2,1)}, u32[]{:S(2)}) copy-start(bf16[1,16,16,128]{3,2,1,0:T(8,128)(2,1)} %get-tuple-element.94.refs_0_) | copy-start | bytes 196612
  141.1 8.5 %copy-start.9 = (f32[128,512]{1,0:T(8,128)S(1)}, f32[128,512]{1,0:T(8,128)}, u32[]{:S(2)}) copy-start(f32[128,512]{1,0:T(8,128)} %param.11) | copy-start | bytes 786436

commit v12 on v11

--- a/solution.py
+++ b/solution.py
@@ -506,6 +506,7 @@
     near_stack = jnp.stack(near_parts)
     far_parts = over_side(after(near_stack, at_end))
     distance = n_fsdp // 2
+    g_sum = g_sum + moved(g_sum, "fsdp", lambda to: to ^ 2)
     g_sum = after(g_sum, at_end)
     while distance > 2:
         g_sum = g_sum + moved(g_sum, "fsdp", lambda to, d=distance: to ^ d)
@@ -609,8 +610,7 @@
     for step in range(1, n_pair):
         back = over_pair(by_pair[:, step * block : (step + 1) * block], step)
         result = result + after(back, a_factor)
-    g_sum = g_sum + after(g_side, by_pair)
-    g_sum = g_sum + after(moved(g_sum, "fsdp", lambda to: to ^ 2), back)
+    g_sum = g_sum + after(g_side, back)
     natural_grad = result.astype(jnp.bfloat16)
 
 

time: 151 us -> 150 us (level)
  starting transfers between devices: 59.1 us -> 47.2 us
  waiting for transfers between devices: 45.2 us -> 56.2 us
    ppermute x40, starting transfers between devices: 55.6 us -> 41.1 us  [moved(): lax.ppermute(array, axis, [(at, target(at) % count) for at in range(count)])]
    ppermute x40, waiting for transfers between devices: 45.2 us -> 56.2 us  [moved(): lax.ppermute(array, axis, [(at, target(at) % count) for at in range(count)])]
    all_to_all x1, starting transfers between devices: 3.42 us -> 6.08 us  [per_device(): strips = lax.all_to_all(strips, 'fsdp', split_axis=0, concat_axis=0)]
  transfers between devices with their start and end apart: 41 -> 41, of which waited for: 17 -> 16; matrix products, arithmetic and copies ran while one was open for 5% -> 5% of each run, Pallas kernels for 18% -> 19%
where the time goes in v12:
time: 150 us; the launch traced here: 149 us
  waiting for transfers between devices  56.2 us (37%)
  starting transfers between devices  47.2 us (31%)
  Pallas kernels  33.5 us (22%)
  other arithmetic  5.36 us (4%)
  local copies, waits for them, and re-layouts  3.76 us (3%)
    ppermute x40, waiting for transfers between devices, moved(): lax.ppermute(array, axis, [(at, target(at) % count) for at in range(count)])  56.2 us
    ppermute x40, starting transfers between devices, moved(): lax.ppermute(array, axis, [(at, target(at) % count) for at in range(count)])  41.1 us
    pallas_call x1, Pallas kernels, add_products(): pl.pallas_call(lambda *refs: products_kernel(owners, pairs, len(strips),...  21.9 us
    all_to_all x1, starting transfers between devices, per_device(): strips = lax.all_to_all(strips, 'fsdp', split_axis=0, concat_axis=0)  6.08 us
    pallas_call x1, Pallas kernels, tail_products(): pl.pallas_call(lambda *refs: tail_kernel(strip, block, layers, *refs), ou...  5.74 us
    pallas_call x1, Pallas kernels, convolve(): pl.pallas_call(lambda *refs: conv_kernel(n_images, *refs), out_shape=[jax...  5.08 us
  transfers between devices with their start and end apart: 41, of which 16 were waited for; matrix products, arithmetic and copies ran while one was open for 5% of the time, Pallas kernels for 19%

profile of v12, /device:TPU:0, one launch (start us, length us, event | category | flops | bytes accessed | tf_op | source)
XLA Modules:
  0.0 148.6 jit_solution(13765716085641514222)
XLA Ops:
  0.7 3.0 %collective-permute-start.7 = (bf16[1,16,16,512]{3,2,1,0:T(8,128)(2,1)}, bf16[1,16,16,512]{3,2,1,0:T(8,128)(2,1)S(1)}, u32[]{:S(2)}, u32[]{:S(2)}) collective-permute-start(bf16[1,16,16,512]{3,2,1,0:T(8,128)(2,1)} %refs_0_.2), channel_id=1, source_target_pairs={{0,4},{4,0},{8,12},{12,8},{16,20},{20,16},{24,28},{28,24},{1,5},{5... | collective-permute-start | bytes 786440 | tf_op jit(solution)/shard_map/ppermute | solution.py:19
  3.7 1.5 %collective-permute-start = (bf16[1,16,16,512]{3,2,1,0:T(8,128)(2,1)}, bf16[1,16,16,512]{3,2,1,0:T(8,128)(2,1)S(1)}, u32[]{:S(2)}, u32[]{:S(2)}) collective-permute-start(bf16[1,16,16,512]{3,2,1,0:T(8,128)(2,1)} %refs_0_.2), channel_id=1, source_target_pairs={{0,2},{1,3},{2,0},{3,1},{4,6},{5,7},{6,4},{7,5},{8,10},{9,11},{10,... | collective-permute-start | bytes 786440 | tf_op jit(solution)/shard_map/ppermute | solution.py:19
  5.2 1.6 %collective-permute-start.1 = (bf16[1,16,16,512]{3,2,1,0:T(8,128)(2,1)}, bf16[1,16,16,512]{3,2,1,0:T(8,128)(2,1)}, u32[]{:S(2)}, u32[]{:S(2)}) collective-permute-start(bf16[1,16,16,512]{3,2,1,0:T(8,128)(2,1)} %refs_0_.2), channel_id=1, source_target_pairs={{0,8},{4,12},{8,16},{12,20},{16,24},{20,28},{24,0},{28,4},{1,9},{5... | collective-permute-start | bytes 786440 | tf_op jit(solution)/shard_map/ppermute | solution.py:19
  6.8 2.2 %collective-permute-start.8 = (bf16[1,16,16,512]{3,2,1,0:T(8,128)(2,1)}, bf16[1,16,16,512]{3,2,1,0:T(8,128)(2,1)}, u32[]{:S(2)}, u32[]{:S(2)}) collective-permute-start(bf16[1,16,16,512]{3,2,1,0:T(8,128)(2,1)} %refs_0_.2), channel_id=1, source_target_pairs={{0,24},{4,28},{8,0},{12,4},{16,8},{20,12},{24,16},{28,20},{1,25},{... | collective-permute-start | bytes 786440 | tf_op jit(solution)/shard_map/ppermute | solution.py:19
  9.0 1.2 collective-permute-done.7.refs_1_
  10.2 1.9 %copy.13 = bf16[512,256]{1,0:T(8,128)(2,1)} copy(bf16[512,256]{0,1:T(8,128)(2,1)} %bitcast.22) | data formatting | bytes 524288 | tf_op jit(solution)/shard_map/transpose | solution.py:445
  12.1 1.3 fusion.1
  13.5 6.1 %all-to-all-start = ((bf16[8,64,256]{2,1,0:T(8,128)(2,1)}), bf16[8,64,256]{2,1,0:T(8,128)(2,1)S(1)}, u32[]{:S(2)}, u32[]{:S(2)}) async-start(bf16[8,64,256]{2,1,0:T(8,128)(2,1)} %bitcast.2), calls=%async_computation | async-start | bytes 524288 | tf_op jit(solution)/shard_map/all_to_all | solution.py:446
  19.6 3.0 %collective-permute-start.2 = (bf16[1,16,16,512]{3,2,1,0:T(8,128)(2,1)S(1)}, bf16[1,16,16,512]{3,2,1,0:T(8,128)(2,1)}, u32[]{:S(2)}, u32[]{:S(2)}) collective-permute-start(bf16[1,16,16,512]{3,2,1,0:T(8,128)(2,1)S(1)} %copy-done.11), channel_id=1, source_target_pairs={{0,16},{4,20},{8,24},{12,28},{16,0},{20,4},{24,8},{28,12},{1,17},{... | collective-permute-start | bytes 786440 | tf_op jit(solution)/shard_map/ppermute | solution.py:19
  22.6 1.5 %collective-permute-start.3 = (bf16[1,16,16,512]{3,2,1,0:T(8,128)(2,1)}, bf16[1,16,16,512]{3,2,1,0:T(8,128)(2,1)}, u32[]{:S(2)}, u32[]{:S(2)}) collective-permute-start(bf16[1,16,16,512]{3,2,1,0:T(8,128)(2,1)} %collective-permute-done.1.refs_3_), channel_id=1, source_target_pairs={{0,2},{1,3},{2,0},{3,1},{4,6},{5,7},{6,4},{7,5},{8,10},{9,11},{10,... | collective-permute-start | bytes 786440 | tf_op jit(solution)/shard_map/ppermute | solution.py:19
  24.1 0.5 collective-permute-start.9
  24.6 1.5 collective-permute-start.10
  26.1 14.4 %collective-permute-done.2.refs_8_ = bf16[1,16,16,512]{3,2,1,0:T(8,128)(2,1)} collective-permute-done((bf16[1,16,16,512]{3,2,1,0:T(8,128)(2,1)S(1)}, bf16[1,16,16,512]{3,2,1,0:T(8,128)(2,1)}, u32[]{:S(2)}, u32[]{:S(2)}) %collective-permute-start.2) | collective-permute-done | bytes 262176 | tf_op jit(solution)/shard_map/ppermute | solution.py:19
  40.5 1.5 collective-permute-start.11
  41.9 1.5 %collective-permute-start.4 = (bf16[1,16,16,512]{3,2,1,0:T(8,128)(2,1)}, bf16[1,16,16,512]{3,2,1,0:T(8,128)(2,1)}, u32[]{:S(2)}, u32[]{:S(2)}) collective-permute-start(bf16[1,16,16,512]{3,2,1,0:T(8,128)(2,1)} %collective-permute-done.2.refs_8_), channel_id=1, source_target_pairs={{0,2},{1,3},{2,0},{3,1},{4,6},{5,7},{6,4},{7,5},{8,10},{9,11},{10,... | collective-permute-start | bytes 786440 | tf_op jit(solution)/shard_map/ppermute | solution.py:19
  43.5 0.5 collective-permute-start.12
  44.0 0.6 collective-permute-start.13
  44.8 6.7 %collective-permute-done.4.refs_12_ = bf16[1,16,16,512]{3,2,1,0:T(8,128)(2,1)} collective-permute-done((bf16[1,16,16,512]{3,2,1,0:T(8,128)(2,1)}, bf16[1,16,16,512]{3,2,1,0:T(8,128)(2,1)}, u32[]{:S(2)}, u32[]{:S(2)}) %collective-permute-start.4) | collective-permute-done | bytes 262176 | tf_op jit(solution)/shard_map/ppermute | solution.py:19
  51.5 1.5 %collective-permute-start.15 = (bf16[8,64,256]{2,1,0:T(8,128)(2,1)S(1)}, bf16[8,64,256]{2,1,0:T(8,128)(2,1)S(1)}, u32[]{:S(2)}, u32[]{:S(2)}) collective-permute-start(bf16[8,64,256]{2,1,0:T(8,128)(2,1)S(1)} %all-to-all-done.refs_16_), channel_id=1, source_target_pairs={{0,2},{1,3},{2,0},{3,1},{4,6},{5,7},{6,4},{7,5},{8,10},{9,11},{10,... | collective-permute-start | bytes 786440 | tf_op jit(solution)/shard_map/ppermute | solution.py:19
  53.0 0.6 collective-permute-start.22
  53.6 0.3 collective-permute-done.13.refs_11_
  54.0 1.5 collective-permute-start.17
  55.5 1.6 %collective-permute-done.12.refs_10_ = bf16[1,16,16,512]{3,2,1,0:T(8,128)(2,1)} collective-permute-done((bf16[1,16,16,512]{3,2,1,0:T(8,128)(2,1)}, bf16[1,16,16,512]{3,2,1,0:T(8,128)(2,1)}, u32[]{:S(2)}, u32[]{:S(2)}) %collective-permute-start.12) | collective-permute-done | bytes 262176 | tf_op jit(solution)/shard_map/ppermute | solution.py:19
  57.1 5.5 %collective-permute-done.15.refs_17_ = bf16[8,64,256]{2,1,0:T(8,128)(2,1)S(1)} collective-permute-done((bf16[8,64,256]{2,1,0:T(8,128)(2,1)S(1)}, bf16[8,64,256]{2,1,0:T(8,128)(2,1)S(1)}, u32[]{:S(2)}, u32[]{:S(2)}) %collective-permute-start.15) | collective-permute-done | bytes 262176 | tf_op jit(solution)/shard_map/ppermute | solution.py:19
  62.6 1.5 %collective-permute-start.16 = (bf16[1,16,16,512]{3,2,1,0:T(8,128)(2,1)}, bf16[1,16,16,512]{3,2,1,0:T(8,128)(2,1)S(1)}, u32[]{:S(2)}, u32[]{:S(2)}) collective-permute-start(bf16[1,16,16,512]{3,2,1,0:T(8,128)(2,1)} %collective-permute-done.11.refs_9_), channel_id=1, source_target_pairs={{0,2},{1,3},{2,0},{3,1},{4,6},{5,7},{6,4},{7,5},{8,10},{9,11},{10,... | collective-permute-start | bytes 786440 | tf_op jit(solution)/shard_map/ppermute | solution.py:19
  64.1 4.1 %collective-permute-done.22 = f32[128,512]{1,0:T(8,128)S(1)} collective-permute-done((f32[128,512]{1,0:T(8,128)S(1)}, f32[128,512]{1,0:T(8,128)S(1)}, u32[]{:S(2)}, u32[]{:S(2)}) %collective-permute-start.22) | collective-permute-done | bytes 262176 | tf_op jit(solution)/shard_map/ppermute | solution.py:19
  68.4 0.6 collective-permute-start.14
  69.1 0.6 collective-permute-start.6
  69.7 2.3 %collective-permute-done.16.refs_14_ = bf16[1,16,16,512]{3,2,1,0:T(8,128)(2,1)S(1)} collective-permute-done((bf16[1,16,16,512]{3,2,1,0:T(8,128)(2,1)}, bf16[1,16,16,512]{3,2,1,0:T(8,128)(2,1)S(1)}, u32[]{:S(2)}, u32[]{:S(2)}) %collective-permute-start.16) | collective-permute-done | bytes 262176 | tf_op jit(solution)/shard_map/ppermute | solution.py:19
  71.9 0.6 collective-permute-start.20
  72.5 2.2 %collective-permute-done.23 = f32[128,512]{1,0:T(8,128)S(1)} collective-permute-done((f32[128,512]{1,0:T(8,128)S(1)}, f32[128,512]{1,0:T(8,128)S(1)}, u32[]{:S(2)}, u32[]{:S(2)}) %collective-permute-start.23) | collective-permute-done | bytes 262176 | tf_op jit(solution)/shard_map/ppermute | solution.py:19
  74.8 2.5 %collective-permute-done.14.refs_13_ = bf16[1,16,16,512]{3,2,1,0:T(8,128)(2,1)S(1)} collective-permute-done((bf16[1,16,16,512]{3,2,1,0:T(8,128)(2,1)}, bf16[1,16,16,512]{3,2,1,0:T(8,128)(2,1)S(1)}, u32[]{:S(2)}, u32[]{:S(2)}) %collective-permute-start.14) | collective-permute-done | bytes 262176 | tf_op jit(solution)/shard_map/ppermute | solution.py:19
  77.4 0.7 copy-done.20
  78.1 21.9 %shard_map.102 = (f32[576,1152]{1,0:T(8,128)}, f32[64,1280]{1,0:T(8,128)}, f32[576,1152]{1,0:T(8,128)}, f32[64,1280]{1,0:T(8,128)}) custom-call(bf16[1,16,16,512]{3,2,1,0:T(8,128)(2,1)} %refs_0_.2, bf16[1,16,16,512]{3,2,1,0:T(8,128)(2,1)} %copy-done.14, bf16[1,16,16,512]{3,2,1,0:T(8,128)(2,1)} %copy-done.12, ...), custom_call_target="tpu_custom_call" | custom-call | flops 12079595520 | bytes 11796480 | tf_op jit(solution)/shard_map/pallas_call | solution.py:174
  100.2 1.8 %collective-permute-done.25.theirs_ref = f32[64,1280]{1,0:T(8,128)S(1)} collective-permute-done((f32[64,1280]{1,0:T(8,128)}, f32[64,1280]{1,0:T(8,128)S(1)}, u32[]{:S(2)}, u32[]{:S(2)}) %collective-permute-start.25) | collective-permute-done | bytes 327712 | tf_op jit(solution)/shard_map/ppermute | solution.py:19
  102.1 1.0 copy-done.1
  103.2 2.3 %collective-permute-start.27 = (f16[64,1280]{1,0:T(8,128)(2,1)S(1)}, f16[64,1280]{1,0:T(8,128)(2,1)S(1)}, u32[]{:S(2)}, u32[]{:S(2)}) collective-permute-start(f16[64,1280]{1,0:T(8,128)(2,1)S(1)} %convert_element_type.54), channel_id=1, source_target_pairs={{0,8},{4,12},{8,16},{12,20},{16,24},{20,28},{24,0},{28,4},{1,9},{5... | collective-permute-start | bytes 491528 | tf_op jit(solution)/shard_map/ppermute | solution.py:19
  105.4 0.2 collective-permute-start.29
  105.6 2.8 %collective-permute-start.30 = (f16[64,1280]{1,0:T(8,128)(2,1)S(1)}, f16[64,1280]{1,0:T(8,128)(2,1)S(1)}, u32[]{:S(2)}, u32[]{:S(2)}) collective-permute-start(f16[64,1280]{1,0:T(8,128)(2,1)S(1)} %convert_element_type.54), channel_id=1, source_target_pairs={{0,24},{4,28},{8,0},{12,4},{16,8},{20,12},{24,16},{28,20},{1,25},{... | collective-permute-start | bytes 491528 | tf_op jit(solution)/shard_map/ppermute | solution.py:19
  108.5 0.1 exponential_reduce_fusion.7
  108.8 5.1 %shard_map.104 = (bf16[1,16,16,128]{3,2,1,0:T(8,128)(2,1)}, bf16[1,16,16,128]{3,2,1,0:T(8,128)(2,1)}, bf16[1,16,16,128]{3,2,1,0:T(8,128)(2,1)}, bf16[1,16,16,128]{3,2,1,0:T(8,128)(2,1)}) custom-call(bf16[1,16,16,512]{3,2,1,0:T(8,128)(2,1)} %refs_0_.2, bf16[1,16,16,512]{3,2,1,0:T(8,128)(2,1)} %copy-done.12, bf16[1,16,16,512]{3,2,1,0:T(8,128)(2,1)} %copy-done.16, ...), custom_call_target="tpu_custom_call" | custom-call | flops 2415919104 | bytes 2228224 | tf_op jit(solution)/shard_map/pallas_call | solution.py:328
  113.9 2.0 %collective-permute-start.28 = (f16[64,1280]{1,0:T(8,128)(2,1)S(1)}, f16[64,1280]{1,0:T(8,128)(2,1)S(1)}, u32[]{:S(2)}, u32[]{:S(2)}) collective-permute-start(f16[64,1280]{1,0:T(8,128)(2,1)S(1)} %collective-permute-done.27), channel_id=1, source_target_pairs={{0,4},{4,0},{8,12},{12,8},{16,20},{20,16},{24,28},{28,24},{1,5},{5... | collective-permute-start | bytes 491528 | tf_op jit(solution)/shard_map/ppermute | solution.py:19
  116.0 2.5 %collective-permute-done.29 = f16[64,1280]{1,0:T(8,128)(2,1)S(1)} collective-permute-done((f16[64,1280]{1,0:T(8,128)(2,1)S(1)}, f16[64,1280]{1,0:T(8,128)(2,1)S(1)}, u32[]{:S(2)}, u32[]{:S(2)}) %collective-permute-start.29) | collective-permute-done | bytes 163872 | tf_op jit(solution)/shard_map/ppermute | solution.py:19
  118.4 1.7 %collective-permute-start.31 = (f16[64,1280]{1,0:T(8,128)(2,1)S(1)}, f16[64,1280]{1,0:T(8,128)(2,1)S(1)}, u32[]{:S(2)}, u32[]{:S(2)}) collective-permute-start(f16[64,1280]{1,0:T(8,128)(2,1)S(1)} %collective-permute-done.29), channel_id=1, source_target_pairs={{0,4},{4,0},{8,12},{12,8},{16,20},{20,16},{24,28},{28,24},{1,5},{5... | collective-permute-start | bytes 491528 | tf_op jit(solution)/shard_map/ppermute | solution.py:19
  120.1 0.3 collective-permute-start.32
  120.6 0.1 exponential_reduce_fusion.5
  120.9 0.1 exponential_reduce_fusion.4
  121.0 0.1 exponential_reduce_fusion.3
  121.3 0.1 exponential_reduce_fusion.2
  121.5 4.0 %collective-permute-done.31 = f16[64,1280]{1,0:T(8,128)(2,1)S(1)} collective-permute-done((f16[64,1280]{1,0:T(8,128)(2,1)S(1)}, f16[64,1280]{1,0:T(8,128)(2,1)S(1)}, u32[]{:S(2)}, u32[]{:S(2)}) %collective-permute-start.31) | collective-permute-done | bytes 163872 | tf_op jit(solution)/shard_map/ppermute | solution.py:19
  125.6 2.3 %collective-permute-done.32 = f16[64,1280]{1,0:T(8,128)(2,1)S(1)} collective-permute-done((f16[64,1280]{1,0:T(8,128)(2,1)S(1)}, f16[64,1280]{1,0:T(8,128)(2,1)S(1)}, u32[]{:S(2)}, u32[]{:S(2)}) %collective-permute-start.32) | collective-permute-done | bytes 163872 | tf_op jit(solution)/shard_map/ppermute | solution.py:19
  128.0 0.1 exponential_reduce_fusion
  128.5 5.7 %shard_map.105 = (f32[576,256]{1,0:T(8,128)S(1)}, f32[576,256]{1,0:T(8,128)S(1)}) custom-call(f32[576,1152]{1,0:T(8,128)S(1)} %copy-done.3, f32[512,512]{1,0:T(8,128)S(1)} %copy-done.4, f32[64,1152]{1,0:T(8,128)S(1)} %convert_multiply_fusion.7.refs_2_, f32[64,1152]{1,0:T(8,128)S(1)} %convert_multiply_fusion.6.refs_3_, ...), custom_call_target="tpu_custom_call" | custom-call | flops 2944401408 | bytes 3833856 | tf_op jit(solution)/shard_map/pallas_call | solution.py:272
  134.3 1.6 %collective-permute-start.33 = (bf16[1,16,16,128]{3,2,1,0:T(8,128)(2,1)S(1)}, bf16[1,16,16,128]{3,2,1,0:T(8,128)(2,1)S(1)}, u32[]{:S(2)}, u32[]{:S(2)}) collective-permute-start(bf16[1,16,16,128]{3,2,1,0:T(8,128)(2,1)S(1)} %copy-done.23), channel_id=1, source_target_pairs={{0,2},{1,3},{2,0},{3,1},{4,6},{5,7},{6,4},{7,5},{8,10},{9,11},{10,... | collective-permute-start | bytes 196616 | tf_op jit(solution)/shard_map/ppermute | solution.py:19
  135.9 0.2 collective-permute-start.34
  136.1 0.4 collective-permute-start.35
  136.5 1.7 %collective-permute-start.38 = (f32[128,512]{1,0:T(8,128)S(1)}, f32[128,512]{1,0:T(8,128)S(1)}, u32[]{:S(2)}, u32[]{:S(2)}) collective-permute-start(f32[128,512]{1,0:T(8,128)S(1)} %add.71), channel_id=1, source_target_pairs={{0,4},{4,0},{8,12},{12,8},{16,20},{20,16},{24,28},{28,24},{1,5},{5... | collective-permute-start | bytes 786440 | tf_op jit(solution)/shard_map/ppermute | solution.py:19
  138.3 1.6 %collective-permute-start.39 = (f32[576,128]{1,0:T(8,128)S(1)}, f32[576,128]{1,0:T(8,128)S(1)}, u32[]{:S(2)}, u32[]{:S(2)}) collective-permute-start(f32[576,128]{1,0:T(8,128)S(1)} %slice.91), channel_id=1, source_target_pairs={{0,2},{1,3},{2,0},{3,1},{4,6},{5,7},{6,4},{7,5},{8,10},{9,11},{10,... | collective-permute-start | bytes 884744 | tf_op jit(solution)/shard_map/ppermute | solution.py:19
  139.9 1.9 %bitcast_add_fusion = f32[1152,576]{0,1:T(8,128)} fusion(f32[576,1152]{1,0:T(8,128)S(1)} %copy-done.6, f32[576,1152]{1,0:T(8,128)S(1)} %collective-permute-done.36, f32[1152,576]{0,1:T(8,128)S(1)} %copy-done.5), kind=kLoop, calls=%fused_computation | loop fusion | flops 2654208 | bytes 10616832 | tf_op jit(solution)/shard_map/add | solution.py:608
  141.8 0.8 shard_map.106
  142.6 2.3 %collective-permute-done.38 = f32[128,512]{1,0:T(8,128)S(1)} collective-permute-done((f32[128,512]{1,0:T(8,128)S(1)}, f32[128,512]{1,0:T(8,128)S(1)}, u32[]{:S(2)}, u32[]{:S(2)}) %collective-permute-start.38) | collective-permute-done | bytes 262176 | tf_op jit(solution)/shard_map/ppermute | solution.py:19
  144.9 2.3 %collective-permute-done.39 = f32[576,128]{1,0:T(8,128)S(1)} collective-permute-done((f32[576,128]{1,0:T(8,128)S(1)}, f32[576,128]{1,0:T(8,128)S(1)}, u32[]{:S(2)}, u32[]{:S(2)}) %collective-permute-start.39) | collective-permute-done | bytes 294944 | tf_op jit(solution)/shard_map/ppermute | solution.py:19
  147.2 0.7 fusion
  147.9 0.8 add_multiply_fusion
  (104 shorter events, 2.2 us)
Async XLA Ops:
  0.6 43.9 %copy-start = (bf16[576,512]{1,0:T(8,128)(2,1)S(1)}, bf16[576,512]{1,0:T(8,128)(2,1)}, u32[]{:S(2)}) copy-start(bf16[576,512]{1,0:T(8,128)(2,1)} %param.9) | copy-start | bytes 1769476
  0.6 19.0 %copy-start.11 = (bf16[1,16,16,512]{3,2,1,0:T(8,128)(2,1)S(1)}, bf16[1,16,16,512]{3,2,1,0:T(8,128)(2,1)}, u32[]{:S(2)}) copy-start(bf16[1,16,16,512]{3,2,1,0:T(8,128)(2,1)} %refs_0_.2) | copy-start | bytes 786436
  0.7 9.5 %collective-permute-start.7 = (bf16[1,16,16,512]{3,2,1,0:T(8,128)(2,1)}, bf16[1,16,16,512]{3,2,1,0:T(8,128)(2,1)S(1)}, u32[]{:S(2)}, u32[]{:S(2)}) collective-permute-start(bf16[1,16,16,512]{3,2,1,0:T(8,128)(2,1)} %refs_0_.2), channel_id=1, source_target_pairs={{0,4},{4,0},{8,12},{12,8},{16,20},{20,16},{24,28},{28,24},{1,5},{5... | collective-permute-start | bytes 786440 | tf_op jit(solution)/shard_map/ppermute | solution.py:19
  3.7 18.9 %collective-permute-start = (bf16[1,16,16,512]{3,2,1,0:T(8,128)(2,1)}, bf16[1,16,16,512]{3,2,1,0:T(8,128)(2,1)S(1)}, u32[]{:S(2)}, u32[]{:S(2)}) collective-permute-start(bf16[1,16,16,512]{3,2,1,0:T(8,128)(2,1)} %refs_0_.2), channel_id=1, source_target_pairs={{0,2},{1,3},{2,0},{3,1},{4,6},{5,7},{6,4},{7,5},{8,10},{9,11},{10,... | collective-permute-start | bytes 786440 | tf_op jit(solution)/shard_map/ppermute | solution.py:19
  5.2 14.4 %collective-permute-start.1 = (bf16[1,16,16,512]{3,2,1,0:T(8,128)(2,1)}, bf16[1,16,16,512]{3,2,1,0:T(8,128)(2,1)}, u32[]{:S(2)}, u32[]{:S(2)}) collective-permute-start(bf16[1,16,16,512]{3,2,1,0:T(8,128)(2,1)} %refs_0_.2), channel_id=1, source_target_pairs={{0,8},{4,12},{8,16},{12,20},{16,24},{20,28},{24,0},{28,4},{1,9},{5... | collective-permute-start | bytes 786440 | tf_op jit(solution)/shard_map/ppermute | solution.py:19
  6.8 17.9 %collective-permute-start.8 = (bf16[1,16,16,512]{3,2,1,0:T(8,128)(2,1)}, bf16[1,16,16,512]{3,2,1,0:T(8,128)(2,1)}, u32[]{:S(2)}, u32[]{:S(2)}) collective-permute-start(bf16[1,16,16,512]{3,2,1,0:T(8,128)(2,1)} %refs_0_.2), channel_id=1, source_target_pairs={{0,24},{4,28},{8,0},{12,4},{16,8},{20,12},{24,16},{28,20},{1,25},{... | collective-permute-start | bytes 786440 | tf_op jit(solution)/shard_map/ppermute | solution.py:19
  10.2 3.2 %copy-start.14 = (bf16[1,16,16,512]{3,2,1,0:T(8,128)(2,1)}, bf16[1,16,16,512]{3,2,1,0:T(8,128)(2,1)S(1)}, u32[]{:S(2)}) copy-start(bf16[1,16,16,512]{3,2,1,0:T(8,128)(2,1)S(1)} %collective-permute-done.7.refs_1_) | copy-start | bytes 786436
  13.4 31.1 %collective-permute-start.21 = (f32[2,128,512]{2,1,0:T(8,128)S(1)}, f32[2,128,512]{2,1,0:T(8,128)S(1)}, u32[]{:S(2)}, u32[]{:S(2)}) collective-permute-start(f32[2,128,512]{2,1,0:T(8,128)S(1)} %dynamic-slice_bitcast_fusion), channel_id=1, source_target_pairs={{0,1},{1,0},{2,3},{3,2},{4,5},{5,4},{6,7},{7,6},{8,9},{9,8},{10,11... | collective-permute-start | bytes 1572872 | tf_op jit(solution)/shard_map/ppermute | solution.py:19
  13.5 31.0 %all-to-all-start = ((bf16[8,64,256]{2,1,0:T(8,128)(2,1)}), bf16[8,64,256]{2,1,0:T(8,128)(2,1)S(1)}, u32[]{:S(2)}, u32[]{:S(2)}) async-start(bf16[8,64,256]{2,1,0:T(8,128)(2,1)} %bitcast.2), calls=%async_computation | async-start | bytes 524288 | tf_op jit(solution)/shard_map/all_to_all | solution.py:446
  19.6 20.8 %collective-permute-start.2 = (bf16[1,16,16,512]{3,2,1,0:T(8,128)(2,1)S(1)}, bf16[1,16,16,512]{3,2,1,0:T(8,128)(2,1)}, u32[]{:S(2)}, u32[]{:S(2)}) collective-permute-start(bf16[1,16,16,512]{3,2,1,0:T(8,128)(2,1)S(1)} %copy-done.11), channel_id=1, source_target_pairs={{0,16},{4,20},{8,24},{12,28},{16,0},{20,4},{24,8},{28,12},{1,17},{... | collective-permute-start | bytes 786440 | tf_op jit(solution)/shard_map/ppermute | solution.py:19
  22.6 21.4 %copy-start.12 = (bf16[1,16,16,512]{3,2,1,0:T(8,128)(2,1)}, bf16[1,16,16,512]{3,2,1,0:T(8,128)(2,1)S(1)}, u32[]{:S(2)}) copy-start(bf16[1,16,16,512]{3,2,1,0:T(8,128)(2,1)S(1)} %collective-permute-done.refs_2_.refs_1_) | copy-start | bytes 786436
  22.6 19.3 %collective-permute-start.3 = (bf16[1,16,16,512]{3,2,1,0:T(8,128)(2,1)}, bf16[1,16,16,512]{3,2,1,0:T(8,128)(2,1)}, u32[]{:S(2)}, u32[]{:S(2)}) collective-permute-start(bf16[1,16,16,512]{3,2,1,0:T(8,128)(2,1)} %collective-permute-done.1.refs_3_), channel_id=1, source_target_pairs={{0,2},{1,3},{2,0},{3,1},{4,6},{5,7},{6,4},{7,5},{8,10},{9,11},{10,... | collective-permute-start | bytes 786440 | tf_op jit(solution)/shard_map/ppermute | solution.py:19
  24.1 19.3 %collective-permute-start.9 = (bf16[1,16,16,512]{3,2,1,0:T(8,128)(2,1)}, bf16[1,16,16,512]{3,2,1,0:T(8,128)(2,1)}, u32[]{:S(2)}, u32[]{:S(2)}) collective-permute-start(bf16[1,16,16,512]{3,2,1,0:T(8,128)(2,1)} %copy-done.14), channel_id=1, source_target_pairs={{0,2},{1,3},{2,0},{3,1},{4,6},{5,7},{6,4},{7,5},{8,10},{9,11},{10,... | collective-permute-start | bytes 786440 | tf_op jit(solution)/shard_map/ppermute | solution.py:19
  24.6 19.3 %collective-permute-start.10 = (bf16[1,16,16,512]{3,2,1,0:T(8,128)(2,1)}, bf16[1,16,16,512]{3,2,1,0:T(8,128)(2,1)}, u32[]{:S(2)}, u32[]{:S(2)}) collective-permute-start(bf16[1,16,16,512]{3,2,1,0:T(8,128)(2,1)} %collective-permute-done.1.refs_3_), channel_id=1, source_target_pairs={{0,4},{4,0},{8,12},{12,8},{16,20},{20,16},{24,28},{28,24},{1,5},{5... | collective-permute-start | bytes 786440 | tf_op jit(solution)/shard_map/ppermute | solution.py:19
  40.5 13.5 %collective-permute-start.11 = (bf16[1,16,16,512]{3,2,1,0:T(8,128)(2,1)}, bf16[1,16,16,512]{3,2,1,0:T(8,128)(2,1)}, u32[]{:S(2)}, u32[]{:S(2)}) collective-permute-start(bf16[1,16,16,512]{3,2,1,0:T(8,128)(2,1)} %collective-permute-done.8.refs_4_), channel_id=1, source_target_pairs={{0,4},{4,0},{8,12},{12,8},{16,20},{20,16},{24,28},{28,24},{1,5},{5... | collective-permute-start | bytes 786440 | tf_op jit(solution)/shard_map/ppermute | solution.py:19
  41.9 9.6 %collective-permute-start.4 = (bf16[1,16,16,512]{3,2,1,0:T(8,128)(2,1)}, bf16[1,16,16,512]{3,2,1,0:T(8,128)(2,1)}, u32[]{:S(2)}, u32[]{:S(2)}) collective-permute-start(bf16[1,16,16,512]{3,2,1,0:T(8,128)(2,1)} %collective-permute-done.2.refs_8_), channel_id=1, source_target_pairs={{0,2},{1,3},{2,0},{3,1},{4,6},{5,7},{6,4},{7,5},{8,10},{9,11},{10,... | collective-permute-start | bytes 786440 | tf_op jit(solution)/shard_map/ppermute | solution.py:19
  43.5 13.7 %collective-permute-start.12 = (bf16[1,16,16,512]{3,2,1,0:T(8,128)(2,1)}, bf16[1,16,16,512]{3,2,1,0:T(8,128)(2,1)}, u32[]{:S(2)}, u32[]{:S(2)}) collective-permute-start(bf16[1,16,16,512]{3,2,1,0:T(8,128)(2,1)} %collective-permute-done.8.refs_4_), channel_id=1, source_target_pairs={{0,2},{1,3},{2,0},{3,1},{4,6},{5,7},{6,4},{7,5},{8,10},{9,11},{10,... | collective-permute-start | bytes 786440 | tf_op jit(solution)/shard_map/ppermute | solution.py:19
  44.0 10.0 %collective-permute-start.13 = (bf16[1,16,16,512]{3,2,1,0:T(8,128)(2,1)}, bf16[1,16,16,512]{3,2,1,0:T(8,128)(2,1)}, u32[]{:S(2)}, u32[]{:S(2)}) collective-permute-start(bf16[1,16,16,512]{3,2,1,0:T(8,128)(2,1)} %collective-permute-done.2.refs_8_), channel_id=1, source_target_pairs={{0,4},{4,0},{8,12},{12,8},{16,20},{20,16},{24,28},{28,24},{1,5},{5... | collective-permute-start | bytes 786440 | tf_op jit(solution)/shard_map/ppermute | solution.py:19
  44.6 30.2 %copy-start.8 = (bf16[8,64,256]{2,1,0:T(8,128)(2,1)}, bf16[8,64,256]{2,1,0:T(8,128)(2,1)S(1)}, u32[]{:S(2)}) copy-start(bf16[8,64,256]{2,1,0:T(8,128)(2,1)S(1)} %all-to-all-done.refs_16_) | copy-start | bytes 786436
  44.6 8.4 %collective-permute-start.18 = (bf16[1,576,128]{2,1,0:T(8,128)(2,1)S(1)}, bf16[1,576,128]{2,1,0:T(8,128)(2,1)S(1)}, u32[]{:S(2)}, u32[]{:S(2)}) collective-permute-start(bf16[1,576,128]{2,1,0:T(8,128)(2,1)S(1)} %dynamic-slice_bitcast_fusion.2), channel_id=1, source_target_pairs={{0,8},{4,12},{8,0},{12,4},{16,24},{20,28},{24,16},{28,20},{1,9},{5... | collective-permute-start | bytes 442376 | tf_op jit(solution)/shard_map/ppermute | solution.py:19
  44.8 24.3 %copy-start.13 = (bf16[1,16,16,512]{3,2,1,0:T(8,128)(2,1)S(1)}, bf16[1,16,16,512]{3,2,1,0:T(8,128)(2,1)}, u32[]{:S(2)}) copy-start(bf16[1,16,16,512]{3,2,1,0:T(8,128)(2,1)} %copy-done.12) | copy-start | bytes 786436
  51.5 11.1 %collective-permute-start.15 = (bf16[8,64,256]{2,1,0:T(8,128)(2,1)S(1)}, bf16[8,64,256]{2,1,0:T(8,128)(2,1)S(1)}, u32[]{:S(2)}, u32[]{:S(2)}) collective-permute-start(bf16[8,64,256]{2,1,0:T(8,128)(2,1)S(1)} %all-to-all-done.refs_16_), channel_id=1, source_target_pairs={{0,2},{1,3},{2,0},{3,1},{4,6},{5,7},{6,4},{7,5},{8,10},{9,11},{10,... | collective-permute-start | bytes 786440 | tf_op jit(solution)/shard_map/ppermute | solution.py:19
  53.0 15.2 %collective-permute-start.22 = (f32[128,512]{1,0:T(8,128)S(1)}, f32[128,512]{1,0:T(8,128)S(1)}, u32[]{:S(2)}, u32[]{:S(2)}) collective-permute-start(f32[128,512]{1,0:T(8,128)S(1)} %dynamic-slice_bitcast_fusion.1), channel_id=1, source_target_pairs={{0,2},{1,3},{2,0},{3,1},{4,6},{5,7},{6,4},{7,5},{8,10},{9,11},{10,... | collective-permute-start | bytes 786440 | tf_op jit(solution)/shard_map/ppermute | solution.py:19
  54.0 15.0 %collective-permute-start.19 = (bf16[2,576,128]{2,1,0:T(8,128)(2,1)S(1)}, bf16[2,576,128]{2,1,0:T(8,128)(2,1)S(1)}, u32[]{:S(2)}, u32[]{:S(2)}) collective-permute-start(bf16[2,576,128]{2,1,0:T(8,128)(2,1)S(1)} %pad_maximum_fusion.1), channel_id=1, source_target_pairs={{0,16},{4,20},{8,24},{12,28},{16,0},{20,4},{24,8},{28,12},{1,17},{... | collective-permute-start | bytes 884744 | tf_op jit(solution)/shard_map/ppermute | solution.py:19
  54.0 15.1 %collective-permute-start.17 = (bf16[1,16,16,512]{3,2,1,0:T(8,128)(2,1)}, bf16[1,16,16,512]{3,2,1,0:T(8,128)(2,1)S(1)}, u32[]{:S(2)}, u32[]{:S(2)}) collective-permute-start(bf16[1,16,16,512]{3,2,1,0:T(8,128)(2,1)} %collective-permute-done.4.refs_12_), channel_id=1, source_target_pairs={{0,4},{4,0},{8,12},{12,8},{16,20},{20,16},{24,28},{28,24},{1,5},{5... | collective-permute-start | bytes 786440 | tf_op jit(solution)/shard_map/ppermute | solution.py:19
  62.6 14.8 %copy-start.15 = (bf16[8,64,256]{2,1,0:T(8,128)(2,1)}, bf16[8,64,256]{2,1,0:T(8,128)(2,1)S(1)}, u32[]{:S(2)}) copy-start(bf16[8,64,256]{2,1,0:T(8,128)(2,1)S(1)} %collective-permute-done.15.refs_17_) | copy-start | bytes 786436
  62.6 9.3 %collective-permute-start.16 = (bf16[1,16,16,512]{3,2,1,0:T(8,128)(2,1)}, bf16[1,16,16,512]{3,2,1,0:T(8,128)(2,1)S(1)}, u32[]{:S(2)}, u32[]{:S(2)}) collective-permute-start(bf16[1,16,16,512]{3,2,1,0:T(8,128)(2,1)} %collective-permute-done.11.refs_9_), channel_id=1, source_target_pairs={{0,2},{1,3},{2,0},{3,1},{4,6},{5,7},{6,4},{7,5},{8,10},{9,11},{10,... | collective-permute-start | bytes 786440 | tf_op jit(solution)/shard_map/ppermute | solution.py:19
  68.3 6.4 %collective-permute-start.23 = (f32[128,512]{1,0:T(8,128)S(1)}, f32[128,512]{1,0:T(8,128)S(1)}, u32[]{:S(2)}, u32[]{:S(2)}) collective-permute-start(f32[128,512]{1,0:T(8,128)S(1)} %bitcast_add_fusion.2), channel_id=1, source_target_pairs={{0,8},{4,12},{8,0},{12,4},{16,24},{20,28},{24,16},{28,20},{1,9},{5... | collective-permute-start | bytes 786440 | tf_op jit(solution)/shard_map/ppermute | solution.py:19
  68.4 9.0 %collective-permute-start.14 = (bf16[1,16,16,512]{3,2,1,0:T(8,128)(2,1)}, bf16[1,16,16,512]{3,2,1,0:T(8,128)(2,1)S(1)}, u32[]{:S(2)}, u32[]{:S(2)}) collective-permute-start(bf16[1,16,16,512]{3,2,1,0:T(8,128)(2,1)} %collective-permute-done.3.refs_7_), channel_id=1, source_target_pairs={{0,4},{4,0},{8,12},{12,8},{16,20},{20,16},{24,28},{28,24},{1,5},{5... | collective-permute-start | bytes 786440 | tf_op jit(solution)/shard_map/ppermute | solution.py:19
  69.0 31.1 %collective-permute-start.5 = (bf16[1,16,16,512]{3,2,1,0:T(8,128)(2,1)S(1)}, bf16[1,16,16,512]{3,2,1,0:T(8,128)(2,1)S(1)}, u32[]{:S(2)}, u32[]{:S(2)}) collective-permute-start(bf16[1,16,16,512]{3,2,1,0:T(8,128)(2,1)S(1)} %copy-done.11), channel_id=1, source_target_pairs={{0,1},{1,0},{2,3},{3,2},{4,5},{5,4},{6,7},{7,6},{8,9},{9,8},{10,11... | collective-permute-start | bytes 786440 | tf_op jit(solution)/shard_map/ppermute | solution.py:19
  69.0 31.0 %copy-start.7 = (bf16[4,576,128]{2,1,0:T(8,128)(2,1)}, bf16[4,576,128]{2,1,0:T(8,128)(2,1)S(1)}, u32[]{:S(2)}) copy-start(bf16[4,576,128]{2,1,0:T(8,128)(2,1)S(1)} %pad_maximum_fusion.refs_4_) | copy-start | bytes 1769476
  69.1 8.3 %copy-start.18 = (bf16[1,16,16,512]{3,2,1,0:T(8,128)(2,1)}, bf16[1,16,16,512]{3,2,1,0:T(8,128)(2,1)S(1)}, u32[]{:S(2)}) copy-start(bf16[1,16,16,512]{3,2,1,0:T(8,128)(2,1)S(1)} %collective-permute-done.17.refs_15_) | copy-start | bytes 786436
  69.1 31.0 %collective-permute-start.6 = (bf16[1,16,16,512]{3,2,1,0:T(8,128)(2,1)S(1)}, bf16[1,16,16,512]{3,2,1,0:T(8,128)(2,1)S(1)}, u32[]{:S(2)}, u32[]{:S(2)}) collective-permute-start(bf16[1,16,16,512]{3,2,1,0:T(8,128)(2,1)S(1)} %copy-done.13), channel_id=1, source_target_pairs={{0,1},{1,0},{2,3},{3,2},{4,5},{5,4},{6,7},{7,6},{8,9},{9,8},{10,11... | collective-permute-start | bytes 786440 | tf_op jit(solution)/shard_map/ppermute | solution.py:19
  71.9 5.5 %copy-start.19 = (bf16[1,16,16,512]{3,2,1,0:T(8,128)(2,1)}, bf16[1,16,16,512]{3,2,1,0:T(8,128)(2,1)S(1)}, u32[]{:S(2)}) copy-start(bf16[1,16,16,512]{3,2,1,0:T(8,128)(2,1)S(1)} %collective-permute-done.16.refs_14_) | copy-start | bytes 786436
  71.9 28.2 %collective-permute-start.20 = (bf16[4,576,128]{2,1,0:T(8,128)(2,1)S(1)}, bf16[4,576,128]{2,1,0:T(8,128)(2,1)S(1)}, u32[]{:S(2)}, u32[]{:S(2)}) collective-permute-start(bf16[4,576,128]{2,1,0:T(8,128)(2,1)S(1)} %pad_maximum_fusion.refs_4_), channel_id=1, source_target_pairs={{0,4},{4,0},{8,12},{12,8},{16,20},{20,16},{24,28},{28,24},{1,5},{5... | collective-permute-start | bytes 1769480 | tf_op jit(solution)/shard_map/ppermute | solution.py:19
  74.8 25.3 %collective-permute-start.24 = (f32[128,512]{1,0:T(8,128)S(1)}, f32[128,512]{1,0:T(8,128)S(1)}, u32[]{:S(2)}, u32[]{:S(2)}) collective-permute-start(f32[128,512]{1,0:T(8,128)S(1)} %add.70), channel_id=1, source_target_pairs={{0,16},{4,20},{8,24},{12,28},{16,0},{20,4},{24,8},{28,12},{1,17},{... | collective-permute-start | bytes 786440 | tf_op jit(solution)/shard_map/ppermute | solution.py:19
  100.1 8.5 %copy-start.16 = (bf16[1,16,16,512]{3,2,1,0:T(8,128)(2,1)}, bf16[1,16,16,512]{3,2,1,0:T(8,128)(2,1)S(1)}, u32[]{:S(2)}) copy-start(bf16[1,16,16,512]{3,2,1,0:T(8,128)(2,1)S(1)} %collective-permute-done.5.refs_2_) | copy-start | bytes 786436
  100.1 8.6 %copy-start.17 = (bf16[1,16,16,512]{3,2,1,0:T(8,128)(2,1)}, bf16[1,16,16,512]{3,2,1,0:T(8,128)(2,1)S(1)}, u32[]{:S(2)}) copy-start(bf16[1,16,16,512]{3,2,1,0:T(8,128)(2,1)S(1)} %collective-permute-done.6.refs_3_) | copy-start | bytes 786436
  100.1 8.5 %copy-start.10 = (bf16[4,576,128]{2,1,0:T(8,128)(2,1)}, bf16[4,576,128]{2,1,0:T(8,128)(2,1)S(1)}, u32[]{:S(2)}) copy-start(bf16[4,576,128]{2,1,0:T(8,128)(2,1)S(1)} %collective-permute-done.20.refs_5_) | copy-start | bytes 1769476
  100.1 1.9 %collective-permute-start.25 = (f32[64,1280]{1,0:T(8,128)}, f32[64,1280]{1,0:T(8,128)S(1)}, u32[]{:S(2)}, u32[]{:S(2)}) collective-permute-start(f32[64,1280]{1,0:T(8,128)} %get-tuple-element.72), channel_id=1, source_target_pairs={{0,1},{1,0},{2,3},{3,2},{4,5},{5,4},{6,7},{7,6},{8,9},{9,8},{10,11... | collective-permute-start | bytes 983048 | tf_op jit(solution)/shard_map/ppermute | solution.py:19
  102.0 1.0 copy-start.1
  103.1 17.9 %collective-permute-start.26 = (f16[64,1280]{1,0:T(8,128)(2,1)S(1)}, f16[64,1280]{1,0:T(8,128)(2,1)S(1)}, u32[]{:S(2)}, u32[]{:S(2)}) collective-permute-start(f16[64,1280]{1,0:T(8,128)(2,1)S(1)} %convert_element_type.54), channel_id=1, source_target_pairs={{0,4},{4,0},{8,12},{12,8},{16,20},{20,16},{24,28},{28,24},{1,5},{5... | collective-permute-start | bytes 491528 | tf_op jit(solution)/shard_map/ppermute | solution.py:19
  103.2 10.8 %collective-permute-start.27 = (f16[64,1280]{1,0:T(8,128)(2,1)S(1)}, f16[64,1280]{1,0:T(8,128)(2,1)S(1)}, u32[]{:S(2)}, u32[]{:S(2)}) collective-permute-start(f16[64,1280]{1,0:T(8,128)(2,1)S(1)} %convert_element_type.54), channel_id=1, source_target_pairs={{0,8},{4,12},{8,16},{12,20},{16,24},{20,28},{24,0},{28,4},{1,9},{5... | collective-permute-start | bytes 491528 | tf_op jit(solution)/shard_map/ppermute | solution.py:19
  105.4 13.0 %collective-permute-start.29 = (f16[64,1280]{1,0:T(8,128)(2,1)S(1)}, f16[64,1280]{1,0:T(8,128)(2,1)S(1)}, u32[]{:S(2)}, u32[]{:S(2)}) collective-permute-start(f16[64,1280]{1,0:T(8,128)(2,1)S(1)} %convert_element_type.54), channel_id=1, source_target_pairs={{0,16},{4,20},{8,24},{12,28},{16,0},{20,4},{24,8},{28,12},{1,17},{... | collective-permute-start | bytes 491528 | tf_op jit(solution)/shard_map/ppermute | solution.py:19
  105.6 12.8 %collective-permute-start.30 = (f16[64,1280]{1,0:T(8,128)(2,1)S(1)}, f16[64,1280]{1,0:T(8,128)(2,1)S(1)}, u32[]{:S(2)}, u32[]{:S(2)}) collective-permute-start(f16[64,1280]{1,0:T(8,128)(2,1)S(1)} %convert_element_type.54), channel_id=1, source_target_pairs={{0,24},{4,28},{8,0},{12,4},{16,8},{20,12},{24,16},{28,20},{1,25},{... | collective-permute-start | bytes 491528 | tf_op jit(solution)/shard_map/ppermute | solution.py:19
  108.6 19.8 %collective-permute-start.36 = (f32[576,1152]{1,0:T(8,128)}, f32[576,1152]{1,0:T(8,128)S(1)}, u32[]{:S(2)}, u32[]{:S(2)}) collective-permute-start(f32[576,1152]{1,0:T(8,128)} %get-tuple-element.89), channel_id=1, source_target_pairs={{0,1},{1,0},{2,3},{3,2},{4,5},{5,4},{6,7},{7,6},{8,9},{9,8},{10,11... | collective-permute-start | bytes 7962632 | tf_op jit(solution)/shard_map/ppermute | solution.py:19
  108.8 19.6 %copy-start.4 = (f32[512,512]{1,0:T(8,128)S(1)}, f32[512,512]{1,0:T(8,128)}, u32[]{:S(2)}) copy-start(f32[512,512]{1,0:T(8,128)} %refs_1_.1) | copy-start | bytes 3145732
  113.9 14.5 %copy-start.3 = (f32[576,1152]{1,0:T(8,128)S(1)}, f32[576,1152]{1,0:T(8,128)}, u32[]{:S(2)}) copy-start(f32[576,1152]{1,0:T(8,128)} %refs_0_.3) | copy-start | bytes 7962628
  113.9 7.4 %collective-permute-start.28 = (f16[64,1280]{1,0:T(8,128)(2,1)S(1)}, f16[64,1280]{1,0:T(8,128)(2,1)S(1)}, u32[]{:S(2)}, u32[]{:S(2)}) collective-permute-start(f16[64,1280]{1,0:T(8,128)(2,1)S(1)} %collective-permute-done.27), channel_id=1, source_target_pairs={{0,4},{4,0},{8,12},{12,8},{16,20},{20,16},{24,28},{28,24},{1,5},{5... | collective-permute-start | bytes 491528 | tf_op jit(solution)/shard_map/ppermute | solution.py:19
  118.4 7.1 %collective-permute-start.31 = (f16[64,1280]{1,0:T(8,128)(2,1)S(1)}, f16[64,1280]{1,0:T(8,128)(2,1)S(1)}, u32[]{:S(2)}, u32[]{:S(2)}) collective-permute-start(f16[64,1280]{1,0:T(8,128)(2,1)S(1)} %collective-permute-done.29), channel_id=1, source_target_pairs={{0,4},{4,0},{8,12},{12,8},{16,20},{20,16},{24,28},{28,24},{1,5},{5... | collective-permute-start | bytes 491528 | tf_op jit(solution)/shard_map/ppermute | solution.py:19
  120.1 7.9 %collective-permute-start.32 = (f16[64,1280]{1,0:T(8,128)(2,1)S(1)}, f16[64,1280]{1,0:T(8,128)(2,1)S(1)}, u32[]{:S(2)}, u32[]{:S(2)}) collective-permute-start(f16[64,1280]{1,0:T(8,128)(2,1)S(1)} %collective-permute-done.30), channel_id=1, source_target_pairs={{0,4},{4,0},{8,12},{12,8},{16,20},{20,16},{24,28},{28,24},{1,5},{5... | collective-permute-start | bytes 491528 | tf_op jit(solution)/shard_map/ppermute | solution.py:19
  128.4 5.9 %copy-start.23 = (bf16[1,16,16,128]{3,2,1,0:T(8,128)(2,1)S(1)}, bf16[1,16,16,128]{3,2,1,0:T(8,128)(2,1)}, u32[]{:S(2)}) copy-start(bf16[1,16,16,128]{3,2,1,0:T(8,128)(2,1)} %get-tuple-element.85) | copy-start | bytes 196612
  128.4 7.5 %copy-start.22 = (bf16[1,16,16,128]{3,2,1,0:T(8,128)(2,1)S(1)}, bf16[1,16,16,128]{3,2,1,0:T(8,128)(2,1)}, u32[]{:S(2)}) copy-start(bf16[1,16,16,128]{3,2,1,0:T(8,128)(2,1)} %get-tuple-element.86) | copy-start | bytes 196612
  128.4 7.7 %copy-start.21 = (bf16[1,16,16,128]{3,2,1,0:T(8,128)(2,1)S(1)}, bf16[1,16,16,128]{3,2,1,0:T(8,128)(2,1)}, u32[]{:S(2)}) copy-start(bf16[1,16,16,128]{3,2,1,0:T(8,128)(2,1)} %get-tuple-element.87) | copy-start | bytes 196612
  128.4 11.5 %copy-start.5 = (f32[1152,576]{0,1:T(8,128)S(1)}, f32[1152,576]{0,1:T(8,128)}, u32[]{:S(2)}) copy-start(f32[1152,576]{0,1:T(8,128)} %param.10) | copy-start | bytes 7962628
  128.4 11.5 %copy-start.6 = (f32[576,1152]{1,0:T(8,128)S(1)}, f32[576,1152]{1,0:T(8,128)}, u32[]{:S(2)}) copy-start(f32[576,1152]{1,0:T(8,128)} %get-tuple-element.97) | copy-start | bytes 7962628
  134.2 4.0 %collective-permute-start.37 = (f32[576,256]{1,0:T(8,128)S(1)}, f32[576,256]{1,0:T(8,128)S(1)}, u32[]{:S(2)}, u32[]{:S(2)}) collective-permute-start(f32[576,256]{1,0:T(8,128)S(1)} %get-tuple-element.92), channel_id=1, source_target_pairs={{0,1},{1,0},{2,3},{3,2},{4,5},{5,4},{6,7},{7,6},{8,9},{9,8},{10,11... | collective-permute-start | bytes 1769480 | tf_op jit(solution)/shard_map/ppermute | solution.py:19
  134.3 7.5 %collective-permute-start.33 = (bf16[1,16,16,128]{3,2,1,0:T(8,128)(2,1)S(1)}, bf16[1,16,16,128]{3,2,1,0:T(8,128)(2,1)S(1)}, u32[]{:S(2)}, u32[]{:S(2)}) collective-permute-start(bf16[1,16,16,128]{3,2,1,0:T(8,128)(2,1)S(1)} %copy-done.23), channel_id=1, source_target_pairs={{0,2},{1,3},{2,0},{3,1},{4,6},{5,7},{6,4},{7,5},{8,10},{9,11},{10,... | collective-permute-start | bytes 196616 | tf_op jit(solution)/shard_map/ppermute | solution.py:19
  135.9 5.9 %collective-permute-start.34 = (bf16[1,16,16,128]{3,2,1,0:T(8,128)(2,1)S(1)}, bf16[1,16,16,128]{3,2,1,0:T(8,128)(2,1)S(1)}, u32[]{:S(2)}, u32[]{:S(2)}) collective-permute-start(bf16[1,16,16,128]{3,2,1,0:T(8,128)(2,1)S(1)} %copy-done.22), channel_id=1, source_target_pairs={{0,1},{1,0},{2,3},{3,2},{4,5},{5,4},{6,7},{7,6},{8,9},{9,8},{10,11... | collective-permute-start | bytes 196616 | tf_op jit(solution)/shard_map/ppermute | solution.py:19
  136.1 5.7 %collective-permute-start.35 = (bf16[1,16,16,128]{3,2,1,0:T(8,128)(2,1)S(1)}, bf16[1,16,16,128]{3,2,1,0:T(8,128)(2,1)S(1)}, u32[]{:S(2)}, u32[]{:S(2)}) collective-permute-start(bf16[1,16,16,128]{3,2,1,0:T(8,128)(2,1)S(1)} %copy-done.21), channel_id=1, source_target_pairs={{0,3},{1,2},{2,1},{3,0},{4,7},{5,6},{6,5},{7,4},{8,11},{9,10},{10,... | collective-permute-start | bytes 196616 | tf_op jit(solution)/shard_map/ppermute | solution.py:19
  136.5 8.4 %collective-permute-start.38 = (f32[128,512]{1,0:T(8,128)S(1)}, f32[128,512]{1,0:T(8,128)S(1)}, u32[]{:S(2)}, u32[]{:S(2)}) collective-permute-start(f32[128,512]{1,0:T(8,128)S(1)} %add.71), channel_id=1, source_target_pairs={{0,4},{4,0},{8,12},{12,8},{16,20},{20,16},{24,28},{28,24},{1,5},{5... | collective-permute-start | bytes 786440 | tf_op jit(solution)/shard_map/ppermute | solution.py:19
  138.3 8.9 %collective-permute-start.39 = (f32[576,128]{1,0:T(8,128)S(1)}, f32[576,128]{1,0:T(8,128)S(1)}, u32[]{:S(2)}, u32[]{:S(2)}) collective-permute-start(f32[576,128]{1,0:T(8,128)S(1)} %slice.91), channel_id=1, source_target_pairs={{0,2},{1,3},{2,0},{3,1},{4,6},{5,7},{6,4},{7,5},{8,10},{9,11},{10,... | collective-permute-start | bytes 884744 | tf_op jit(solution)/shard_map/ppermute | solution.py:19
  139.9 1.9 %copy-start.2 = (bf16[1,16,16,128]{3,2,1,0:T(8,128)(2,1)S(1)}, bf16[1,16,16,128]{3,2,1,0:T(8,128)(2,1)}, u32[]{:S(2)}) copy-start(bf16[1,16,16,128]{3,2,1,0:T(8,128)(2,1)} %get-tuple-element.93.refs_0_) | copy-start | bytes 196612
  139.9 7.9 %copy-start.9 = (f32[128,512]{1,0:T(8,128)S(1)}, f32[128,512]{1,0:T(8,128)}, u32[]{:S(2)}) copy-start(f32[128,512]{1,0:T(8,128)} %param.11) | copy-start | bytes 786436
  (1 other events, 0.7 us)

commit v13 on v12

--- a/solution.py
+++ b/solution.py
@@ -506,7 +506,6 @@
     near_stack = jnp.stack(near_parts)
     far_parts = over_side(after(near_stack, at_end))
     distance = n_fsdp // 2
-    g_sum = g_sum + moved(g_sum, "fsdp", lambda to: to ^ 2)
     g_sum = after(g_sum, at_end)
     while distance > 2:
         g_sum = g_sum + moved(g_sum, "fsdp", lambda to, d=distance: to ^ d)
@@ -565,7 +564,9 @@
                 out = moved(out, "factor", lambda at, o=other, p=pair: (at ^ o) - 2 * p)
             own_maps.append(out)
             block_order.append(2 * ((pair_at + pair) % n_pair) + (core_at + other) % 2)
-    g_side = over_side(after(g_sum, far_packed))
+    g_near = moved(after(g_sum, near_packed), "fsdp", lambda to: to ^ 2)
+    g_sum = g_sum + after(g_near, far_packed)
+    g_side = over_side(g_sum)
     strips_of_grad = [
         array[:, :rows].astype(jnp.float32) * jnp.exp2(array[:, rows : rows + 1].astype(jnp.float32))
         for array in near_packed + far_packed

time: 150 us -> 151 us (level)
  starting transfers between devices: 47.2 us -> 59.1 us
  waiting for transfers between devices: 56.2 us -> 45.2 us
    ppermute x40, starting transfers between devices: 41.1 us -> 55.7 us  [moved(): lax.ppermute(array, axis, [(at, target(at) % count) for at in range(count)])]
    ppermute x40, waiting for transfers between devices: 56.2 us -> 45.2 us  [moved(): lax.ppermute(array, axis, [(at, target(at) % count) for at in range(count)])]
    all_to_all x1, starting transfers between devices: 6.08 us -> 3.42 us  [per_device(): strips = lax.all_to_all(strips, 'fsdp', split_axis=0, concat_axis=0)]
  transfers between devices with their start and end apart: 41 -> 41, of which waited for: 16 -> 17; matrix products, arithmetic and copies ran while one was open for 5% -> 5% of each run, Pallas kernels for 19% -> 18%
where the time goes in v13:
time: 151 us; the launch traced here: 150 us
  starting transfers between devices  59.1 us (39%)
  waiting for transfers between devices  45.2 us (30%)
  Pallas kernels  33.5 us (22%)
  other arithmetic  6.48 us (4%)
  local copies, waits for them, and re-layouts  3.65 us (2%)
    ppermute x40, starting transfers between devices, moved(): lax.ppermute(array, axis, [(at, target(at) % count) for at in range(count)])  55.7 us
    ppermute x40, waiting for transfers between devices, moved(): lax.ppermute(array, axis, [(at, target(at) % count) for at in range(count)])  45.2 us
    pallas_call x1, Pallas kernels, add_products(): pl.pallas_call(lambda *refs: products_kernel(owners, pairs, len(strips),...  21.9 us
    pallas_call x1, Pallas kernels, tail_products(): pl.pallas_call(lambda *refs: tail_kernel(strip, block, layers, *refs), ou...  5.74 us
    pallas_call x1, Pallas kernels, convolve(): pl.pallas_call(lambda *refs: conv_kernel(n_images, *refs), out_shape=[jax...  5.09 us
    all_to_all x1, starting transfers between devices, per_device(): strips = lax.all_to_all(strips, 'fsdp', split_axis=0, concat_axis=0)  3.42 us
  transfers between devices with their start and end apart: 41, of which 17 were waited for; matrix products, arithmetic and copies ran while one was open for 5% of the time, Pallas kernels for 18%

profile of v13, /device:TPU:0, one launch (start us, length us, event | category | flops | bytes accessed | tf_op | source)
XLA Modules:
  0.0 150.4 jit_solution(2637690992649978741)
XLA Ops:
  0.6 3.1 %collective-permute-start.1 = (bf16[1,16,16,512]{3,2,1,0:T(8,128)(2,1)}, bf16[1,16,16,512]{3,2,1,0:T(8,128)(2,1)S(1)}, u32[]{:S(2)}, u32[]{:S(2)}) collective-permute-start(bf16[1,16,16,512]{3,2,1,0:T(8,128)(2,1)} %refs_0_.2), channel_id=1, source_target_pairs={{0,8},{4,12},{8,16},{12,20},{16,24},{20,28},{24,0},{28,4},{1,9},{5... | collective-permute-start | bytes 786440 | tf_op jit(solution)/shard_map/ppermute | solution.py:19
  3.7 1.5 %collective-permute-start = (bf16[1,16,16,512]{3,2,1,0:T(8,128)(2,1)}, bf16[1,16,16,512]{3,2,1,0:T(8,128)(2,1)S(1)}, u32[]{:S(2)}, u32[]{:S(2)}) collective-permute-start(bf16[1,16,16,512]{3,2,1,0:T(8,128)(2,1)} %refs_0_.2), channel_id=1, source_target_pairs={{0,2},{1,3},{2,0},{3,1},{4,6},{5,7},{6,4},{7,5},{8,10},{9,11},{10,... | collective-permute-start | bytes 786440 | tf_op jit(solution)/shard_map/ppermute | solution.py:19
  5.2 1.5 collective-permute-start.7
  6.7 2.2 %collective-permute-start.8 = (bf16[1,16,16,512]{3,2,1,0:T(8,128)(2,1)}, bf16[1,16,16,512]{3,2,1,0:T(8,128)(2,1)}, u32[]{:S(2)}, u32[]{:S(2)}) collective-permute-start(bf16[1,16,16,512]{3,2,1,0:T(8,128)(2,1)} %refs_0_.2), channel_id=1, source_target_pairs={{0,24},{4,28},{8,0},{12,4},{16,8},{20,12},{24,16},{28,20},{1,25},{... | collective-permute-start | bytes 786440 | tf_op jit(solution)/shard_map/ppermute | solution.py:19
  9.0 4.2 %collective-permute-done.1.refs_3_ = bf16[1,16,16,512]{3,2,1,0:T(8,128)(2,1)S(1)} collective-permute-done((bf16[1,16,16,512]{3,2,1,0:T(8,128)(2,1)}, bf16[1,16,16,512]{3,2,1,0:T(8,128)(2,1)S(1)}, u32[]{:S(2)}, u32[]{:S(2)}) %collective-permute-start.1) | collective-permute-done | bytes 262176 | tf_op jit(solution)/shard_map/ppermute | solution.py:19
  13.1 8.3 %collective-permute-start.2 = (bf16[1,16,16,512]{3,2,1,0:T(8,128)(2,1)}, bf16[1,16,16,512]{3,2,1,0:T(8,128)(2,1)}, u32[]{:S(2)}, u32[]{:S(2)}) collective-permute-start(bf16[1,16,16,512]{3,2,1,0:T(8,128)(2,1)} %refs_0_.2), channel_id=1, source_target_pairs={{0,16},{4,20},{8,24},{12,28},{16,0},{20,4},{24,8},{28,12},{1,17},{... | collective-permute-start | bytes 786440 | tf_op jit(solution)/shard_map/ppermute | solution.py:19
  21.4 1.5 %collective-permute-start.3 = (bf16[1,16,16,512]{3,2,1,0:T(8,128)(2,1)S(1)}, bf16[1,16,16,512]{3,2,1,0:T(8,128)(2,1)}, u32[]{:S(2)}, u32[]{:S(2)}) collective-permute-start(bf16[1,16,16,512]{3,2,1,0:T(8,128)(2,1)S(1)} %collective-permute-done.1.refs_3_), channel_id=1, source_target_pairs={{0,2},{1,3},{2,0},{3,1},{4,6},{5,7},{6,4},{7,5},{8,10},{9,11},{10,... | collective-permute-start | bytes 786440 | tf_op jit(solution)/shard_map/ppermute | solution.py:19
  22.9 1.8 %copy.13 = bf16[512,256]{1,0:T(8,128)(2,1)} copy(bf16[512,256]{0,1:T(8,128)(2,1)} %bitcast.22) | data formatting | bytes 524288 | tf_op jit(solution)/shard_map/transpose | solution.py:445
  24.7 1.3 fusion.1
  26.2 3.4 %all-to-all-start = ((bf16[8,64,256]{2,1,0:T(8,128)(2,1)}), bf16[8,64,256]{2,1,0:T(8,128)(2,1)S(1)}, u32[]{:S(2)}, u32[]{:S(2)}) async-start(bf16[8,64,256]{2,1,0:T(8,128)(2,1)} %bitcast.2), calls=%async_computation | async-start | bytes 524288 | tf_op jit(solution)/shard_map/all_to_all | solution.py:446
  29.6 0.6 collective-permute-start.9
  30.2 1.9 %collective-permute-start.10 = (bf16[1,16,16,512]{3,2,1,0:T(8,128)(2,1)S(1)}, bf16[1,16,16,512]{3,2,1,0:T(8,128)(2,1)}, u32[]{:S(2)}, u32[]{:S(2)}) collective-permute-start(bf16[1,16,16,512]{3,2,1,0:T(8,128)(2,1)S(1)} %collective-permute-done.1.refs_3_), channel_id=1, source_target_pairs={{0,4},{4,0},{8,12},{12,8},{16,20},{20,16},{24,28},{28,24},{1,5},{5... | collective-permute-start | bytes 786440 | tf_op jit(solution)/shard_map/ppermute | solution.py:19
  32.1 1.5 %collective-permute-start.18 = (bf16[1,576,128]{2,1,0:T(8,128)(2,1)S(1)}, bf16[1,576,128]{2,1,0:T(8,128)(2,1)S(1)}, u32[]{:S(2)}, u32[]{:S(2)}) collective-permute-start(bf16[1,576,128]{2,1,0:T(8,128)(2,1)S(1)} %dynamic-slice_bitcast_fusion.2), channel_id=1, source_target_pairs={{0,8},{4,12},{8,0},{12,4},{16,24},{20,28},{24,16},{28,20},{1,9},{5... | collective-permute-start | bytes 442376 | tf_op jit(solution)/shard_map/ppermute | solution.py:19
  33.6 1.5 %collective-permute-start.4 = (bf16[1,16,16,512]{3,2,1,0:T(8,128)(2,1)}, bf16[1,16,16,512]{3,2,1,0:T(8,128)(2,1)}, u32[]{:S(2)}, u32[]{:S(2)}) collective-permute-start(bf16[1,16,16,512]{3,2,1,0:T(8,128)(2,1)} %collective-permute-done.2.refs_8_), channel_id=1, source_target_pairs={{0,2},{1,3},{2,0},{3,1},{4,6},{5,7},{6,4},{7,5},{8,10},{9,11},{10,... | collective-permute-start | bytes 786440 | tf_op jit(solution)/shard_map/ppermute | solution.py:19
  35.2 4.0 %collective-permute-done.9.refs_5_ = bf16[1,16,16,512]{3,2,1,0:T(8,128)(2,1)} collective-permute-done((bf16[1,16,16,512]{3,2,1,0:T(8,128)(2,1)}, bf16[1,16,16,512]{3,2,1,0:T(8,128)(2,1)}, u32[]{:S(2)}, u32[]{:S(2)}) %collective-permute-start.9) | collective-permute-done | bytes 262176 | tf_op jit(solution)/shard_map/ppermute | solution.py:19
  39.1 1.9 %collective-permute-start.11 = (bf16[1,16,16,512]{3,2,1,0:T(8,128)(2,1)}, bf16[1,16,16,512]{3,2,1,0:T(8,128)(2,1)}, u32[]{:S(2)}, u32[]{:S(2)}) collective-permute-start(bf16[1,16,16,512]{3,2,1,0:T(8,128)(2,1)} %collective-permute-done.8.refs_4_), channel_id=1, source_target_pairs={{0,4},{4,0},{8,12},{12,8},{16,20},{20,16},{24,28},{28,24},{1,5},{5... | collective-permute-start | bytes 786440 | tf_op jit(solution)/shard_map/ppermute | solution.py:19
  41.0 0.3 collective-permute-done.10.refs_6_
  41.3 1.3 collective-permute-start.12
  42.7 0.6 collective-permute-start.13
  43.4 1.3 collective-permute-done.4.refs_12_
  44.6 2.4 %collective-permute-start.19 = (bf16[2,576,128]{2,1,0:T(8,128)(2,1)S(1)}, bf16[2,576,128]{2,1,0:T(8,128)(2,1)}, u32[]{:S(2)}, u32[]{:S(2)}) collective-permute-start(bf16[2,576,128]{2,1,0:T(8,128)(2,1)S(1)} %pad_maximum_fusion.1), channel_id=1, source_target_pairs={{0,16},{4,20},{8,24},{12,28},{16,0},{20,4},{24,8},{28,12},{1,17},{... | collective-permute-start | bytes 884744 | tf_op jit(solution)/shard_map/ppermute | solution.py:19
  47.0 0.7 collective-permute-start.15
  47.9 0.8 collective-permute-done.11.refs_9_
  48.7 0.6 collective-permute-start.22
  49.2 3.3 %collective-permute-done.13.refs_11_ = bf16[1,16,16,512]{3,2,1,0:T(8,128)(2,1)} collective-permute-done((bf16[1,16,16,512]{3,2,1,0:T(8,128)(2,1)}, bf16[1,16,16,512]{3,2,1,0:T(8,128)(2,1)}, u32[]{:S(2)}, u32[]{:S(2)}) %collective-permute-start.13) | collective-permute-done | bytes 262176 | tf_op jit(solution)/shard_map/ppermute | solution.py:19
  52.6 1.2 collective-permute-start.14
  53.8 2.7 %collective-permute-done.15.refs_17_ = bf16[8,64,256]{2,1,0:T(8,128)(2,1)} collective-permute-done((bf16[8,64,256]{2,1,0:T(8,128)(2,1)S(1)}, bf16[8,64,256]{2,1,0:T(8,128)(2,1)}, u32[]{:S(2)}, u32[]{:S(2)}) %collective-permute-start.15) | collective-permute-done | bytes 262176 | tf_op jit(solution)/shard_map/ppermute | solution.py:19
  56.5 1.9 %collective-permute-start.17 = (bf16[1,16,16,512]{3,2,1,0:T(8,128)(2,1)}, bf16[1,16,16,512]{3,2,1,0:T(8,128)(2,1)S(1)}, u32[]{:S(2)}, u32[]{:S(2)}) collective-permute-start(bf16[1,16,16,512]{3,2,1,0:T(8,128)(2,1)} %collective-permute-done.4.refs_12_), channel_id=1, source_target_pairs={{0,4},{4,0},{8,12},{12,8},{16,20},{20,16},{24,28},{28,24},{1,5},{5... | collective-permute-start | bytes 786440 | tf_op jit(solution)/shard_map/ppermute | solution.py:19
  58.4 1.9 %collective-permute-done.19 = bf16[2,576,128]{2,1,0:T(8,128)(2,1)} collective-permute-done((bf16[2,576,128]{2,1,0:T(8,128)(2,1)S(1)}, bf16[2,576,128]{2,1,0:T(8,128)(2,1)}, u32[]{:S(2)}, u32[]{:S(2)}) %collective-permute-start.19) | collective-permute-done | bytes 294944 | tf_op jit(solution)/shard_map/ppermute | solution.py:19
  60.3 0.5 collective-permute-start.16
  60.8 1.0 pad_maximum_fusion.refs_4_
  61.9 3.1 %collective-permute-done.17.refs_15_ = bf16[1,16,16,512]{3,2,1,0:T(8,128)(2,1)S(1)} collective-permute-done((bf16[1,16,16,512]{3,2,1,0:T(8,128)(2,1)}, bf16[1,16,16,512]{3,2,1,0:T(8,128)(2,1)S(1)}, u32[]{:S(2)}, u32[]{:S(2)}) %collective-permute-start.17) | collective-permute-done | bytes 262176 | tf_op jit(solution)/shard_map/ppermute | solution.py:19
  65.0 2.9 %collective-permute-done.16.refs_14_ = bf16[1,16,16,512]{3,2,1,0:T(8,128)(2,1)S(1)} collective-permute-done((bf16[1,16,16,512]{3,2,1,0:T(8,128)(2,1)}, bf16[1,16,16,512]{3,2,1,0:T(8,128)(2,1)S(1)}, u32[]{:S(2)}, u32[]{:S(2)}) %collective-permute-start.16) | collective-permute-done | bytes 262176 | tf_op jit(solution)/shard_map/ppermute | solution.py:19
  67.9 1.0 collective-permute-start.20
  69.0 1.7 %collective-permute-start.23 = (f32[128,512]{1,0:T(8,128)S(1)}, f32[128,512]{1,0:T(8,128)S(1)}, u32[]{:S(2)}, u32[]{:S(2)}) collective-permute-start(f32[128,512]{1,0:T(8,128)S(1)} %bitcast_add_fusion.2), channel_id=1, source_target_pairs={{0,16},{4,20},{8,24},{12,28},{16,0},{20,4},{24,8},{28,12},{1,17},{... | collective-permute-start | bytes 786440 | tf_op jit(solution)/shard_map/ppermute | solution.py:19
  70.7 0.7 copy-done.15
  71.4 21.9 %shard_map.102 = (f32[576,1152]{1,0:T(8,128)}, f32[64,1280]{1,0:T(8,128)}, f32[576,1152]{1,0:T(8,128)}, f32[64,1280]{1,0:T(8,128)}) custom-call(bf16[1,16,16,512]{3,2,1,0:T(8,128)(2,1)} %refs_0_.2, bf16[1,16,16,512]{3,2,1,0:T(8,128)(2,1)} %collective-permute-done.7.refs_1_, bf16[1,16,16,512]{3,2,1,0:T(8,128)(2,1)} %copy-done.11, ...), custom_call_target="tpu_custom_call" | custom-call | flops 12079595520 | bytes 11796480 | tf_op jit(solution)/shard_map/pallas_call | solution.py:174
  93.4 1.8 %collective-permute-done.24.theirs_ref = f32[64,1280]{1,0:T(8,128)S(1)} collective-permute-done((f32[64,1280]{1,0:T(8,128)}, f32[64,1280]{1,0:T(8,128)S(1)}, u32[]{:S(2)}, u32[]{:S(2)}) %collective-permute-start.24) | collective-permute-done | bytes 327712 | tf_op jit(solution)/shard_map/ppermute | solution.py:19
  95.3 1.0 copy-done.1
  96.3 0.6 collective-permute-start.25
  97.0 3.1 %collective-permute-start.26 = (f16[64,1280]{1,0:T(8,128)(2,1)S(1)}, f16[64,1280]{1,0:T(8,128)(2,1)S(1)}, u32[]{:S(2)}, u32[]{:S(2)}) collective-permute-start(f16[64,1280]{1,0:T(8,128)(2,1)S(1)} %convert_element_type.54), channel_id=1, source_target_pairs={{0,8},{4,12},{8,16},{12,20},{16,24},{20,28},{24,0},{28,4},{1,9},{5... | collective-permute-start | bytes 491528 | tf_op jit(solution)/shard_map/ppermute | solution.py:19
  100.1 0.1 collective-permute-start.28
  100.2 2.2 %collective-permute-start.29 = (f16[64,1280]{1,0:T(8,128)(2,1)S(1)}, f16[64,1280]{1,0:T(8,128)(2,1)S(1)}, u32[]{:S(2)}, u32[]{:S(2)}) collective-permute-start(f16[64,1280]{1,0:T(8,128)(2,1)S(1)} %convert_element_type.54), channel_id=1, source_target_pairs={{0,24},{4,28},{8,0},{12,4},{16,8},{20,12},{24,16},{28,20},{1,25},{... | collective-permute-start | bytes 491528 | tf_op jit(solution)/shard_map/ppermute | solution.py:19
  102.8 5.1 %shard_map.104 = (bf16[1,16,16,128]{3,2,1,0:T(8,128)(2,1)}, bf16[1,16,16,128]{3,2,1,0:T(8,128)(2,1)}, bf16[1,16,16,128]{3,2,1,0:T(8,128)(2,1)}, bf16[1,16,16,128]{3,2,1,0:T(8,128)(2,1)}) custom-call(bf16[1,16,16,512]{3,2,1,0:T(8,128)(2,1)} %refs_0_.2, bf16[1,16,16,512]{3,2,1,0:T(8,128)(2,1)} %copy-done.11, bf16[1,16,16,512]{3,2,1,0:T(8,128)(2,1)} %copy-done.13, ...), custom_call_target="tpu_custom_call" | custom-call | flops 2415919104 | bytes 2228224 | tf_op jit(solution)/shard_map/pallas_call | solution.py:328
  107.9 1.5 %collective-permute-start.27 = (f16[64,1280]{1,0:T(8,128)(2,1)S(1)}, f16[64,1280]{1,0:T(8,128)(2,1)S(1)}, u32[]{:S(2)}, u32[]{:S(2)}) collective-permute-start(f16[64,1280]{1,0:T(8,128)(2,1)S(1)} %collective-permute-done.26), channel_id=1, source_target_pairs={{0,4},{4,0},{8,12},{12,8},{16,20},{20,16},{24,28},{28,24},{1,5},{5... | collective-permute-start | bytes 491528 | tf_op jit(solution)/shard_map/ppermute | solution.py:19
  109.4 2.4 %collective-permute-done.28 = f16[64,1280]{1,0:T(8,128)(2,1)S(1)} collective-permute-done((f16[64,1280]{1,0:T(8,128)(2,1)S(1)}, f16[64,1280]{1,0:T(8,128)(2,1)S(1)}, u32[]{:S(2)}, u32[]{:S(2)}) %collective-permute-start.28) | collective-permute-done | bytes 163872 | tf_op jit(solution)/shard_map/ppermute | solution.py:19
  111.8 1.5 collective-permute-start.30
  113.3 0.6 collective-permute-start.31
  114.0 0.1 exponential_reduce_fusion.5
  114.9 4.1 %collective-permute-done.30 = f16[64,1280]{1,0:T(8,128)(2,1)S(1)} collective-permute-done((f16[64,1280]{1,0:T(8,128)(2,1)S(1)}, f16[64,1280]{1,0:T(8,128)(2,1)S(1)}, u32[]{:S(2)}, u32[]{:S(2)}) %collective-permute-start.30) | collective-permute-done | bytes 163872 | tf_op jit(solution)/shard_map/ppermute | solution.py:19
  119.0 2.6 %collective-permute-done.31 = f16[64,1280]{1,0:T(8,128)(2,1)S(1)} collective-permute-done((f16[64,1280]{1,0:T(8,128)(2,1)S(1)}, f16[64,1280]{1,0:T(8,128)(2,1)S(1)}, u32[]{:S(2)}, u32[]{:S(2)}) %collective-permute-start.31) | collective-permute-done | bytes 163872 | tf_op jit(solution)/shard_map/ppermute | solution.py:19
  122.1 5.7 %shard_map.105 = (f32[576,256]{1,0:T(8,128)S(1)}, f32[576,256]{1,0:T(8,128)S(1)}) custom-call(f32[576,1152]{1,0:T(8,128)S(1)} %copy-done.3, f32[512,512]{1,0:T(8,128)S(1)} %copy-done.4, f32[64,1152]{1,0:T(8,128)S(1)} %convert_multiply_fusion.7.refs_2_, f32[64,1152]{1,0:T(8,128)S(1)} %convert_multiply_fusion.6.refs_3_, ...), custom_call_target="tpu_custom_call" | custom-call | flops 2944401408 | bytes 3833856 | tf_op jit(solution)/shard_map/pallas_call | solution.py:272
  127.9 3.9 %collective-permute-start.37 = (f32[128,512]{1,0:T(8,128)S(1)}, f32[128,512]{1,0:T(8,128)S(1)}, u32[]{:S(2)}, u32[]{:S(2)}) collective-permute-start(f32[128,512]{1,0:T(8,128)S(1)} %add.70), channel_id=1, source_target_pairs={{0,8},{4,12},{8,0},{12,4},{16,24},{20,28},{24,16},{28,20},{1,9},{5... | collective-permute-start | bytes 786440 | tf_op jit(solution)/shard_map/ppermute | solution.py:19
  131.8 0.5 collective-permute-start.32
  132.4 1.6 %collective-permute-start.34 = (bf16[1,16,16,128]{3,2,1,0:T(8,128)(2,1)S(1)}, bf16[1,16,16,128]{3,2,1,0:T(8,128)(2,1)S(1)}, u32[]{:S(2)}, u32[]{:S(2)}) collective-permute-start(bf16[1,16,16,128]{3,2,1,0:T(8,128)(2,1)S(1)} %copy-done.18), channel_id=1, source_target_pairs={{0,3},{1,2},{2,1},{3,0},{4,7},{5,6},{6,5},{7,4},{8,11},{9,10},{10,... | collective-permute-start | bytes 196616 | tf_op jit(solution)/shard_map/ppermute | solution.py:19
  134.0 4.7 %collective-permute-done.37 = f32[128,512]{1,0:T(8,128)S(1)} collective-permute-done((f32[128,512]{1,0:T(8,128)S(1)}, f32[128,512]{1,0:T(8,128)S(1)}, u32[]{:S(2)}, u32[]{:S(2)}) %collective-permute-start.37) | collective-permute-done | bytes 262176 | tf_op jit(solution)/shard_map/ppermute | solution.py:19
  138.8 1.5 %collective-permute-start.38 = (f32[128,512]{1,0:T(8,128)S(1)}, f32[128,512]{1,0:T(8,128)S(1)}, u32[]{:S(2)}, u32[]{:S(2)}) collective-permute-start(f32[128,512]{1,0:T(8,128)S(1)} %add.74), channel_id=1, source_target_pairs={{0,4},{4,0},{8,12},{12,8},{16,20},{20,16},{24,28},{28,24},{1,5},{5... | collective-permute-start | bytes 786440 | tf_op jit(solution)/shard_map/ppermute | solution.py:19
  140.4 0.6 collective-permute-start.39
  141.0 2.0 %bitcast_add_fusion = f32[1152,576]{0,1:T(8,128)} fusion(f32[576,1152]{1,0:T(8,128)S(1)} %copy-done.6, f32[576,1152]{1,0:T(8,128)S(1)} %collective-permute-done.35, f32[1152,576]{0,1:T(8,128)S(1)} %copy-done.5), kind=kLoop, calls=%fused_computation | loop fusion | flops 2654208 | bytes 10616832 | tf_op jit(solution)/shard_map/add | solution.py:609
  143.1 0.8 shard_map.106
  143.8 3.1 %collective-permute-done.38 = f32[128,512]{1,0:T(8,128)S(1)} collective-permute-done((f32[128,512]{1,0:T(8,128)S(1)}, f32[128,512]{1,0:T(8,128)S(1)}, u32[]{:S(2)}, u32[]{:S(2)}) %collective-permute-start.38) | collective-permute-done | bytes 262176 | tf_op jit(solution)/shard_map/ppermute | solution.py:19
  146.9 2.1 %collective-permute-done.39 = f32[576,128]{1,0:T(8,128)S(1)} collective-permute-done((f32[576,128]{1,0:T(8,128)S(1)}, f32[576,128]{1,0:T(8,128)S(1)}, u32[]{:S(2)}, u32[]{:S(2)}) %collective-permute-start.39) | collective-permute-done | bytes 294944 | tf_op jit(solution)/shard_map/ppermute | solution.py:19
  149.0 0.7 fusion
  149.7 0.8 add_multiply_fusion
  (98 shorter events, 2.5 us)
Async XLA Ops:
  0.6 31.4 %copy-start = (bf16[576,512]{1,0:T(8,128)(2,1)S(1)}, bf16[576,512]{1,0:T(8,128)(2,1)}, u32[]{:S(2)}) copy-start(bf16[576,512]{1,0:T(8,128)(2,1)} %param.9) | copy-start | bytes 1769476
  0.6 12.5 %collective-permute-start.1 = (bf16[1,16,16,512]{3,2,1,0:T(8,128)(2,1)}, bf16[1,16,16,512]{3,2,1,0:T(8,128)(2,1)S(1)}, u32[]{:S(2)}, u32[]{:S(2)}) collective-permute-start(bf16[1,16,16,512]{3,2,1,0:T(8,128)(2,1)} %refs_0_.2), channel_id=1, source_target_pairs={{0,8},{4,12},{8,16},{12,20},{16,24},{20,28},{24,0},{28,4},{1,9},{5... | collective-permute-start | bytes 786440 | tf_op jit(solution)/shard_map/ppermute | solution.py:19
  3.7 17.7 %collective-permute-start = (bf16[1,16,16,512]{3,2,1,0:T(8,128)(2,1)}, bf16[1,16,16,512]{3,2,1,0:T(8,128)(2,1)S(1)}, u32[]{:S(2)}, u32[]{:S(2)}) collective-permute-start(bf16[1,16,16,512]{3,2,1,0:T(8,128)(2,1)} %refs_0_.2), channel_id=1, source_target_pairs={{0,2},{1,3},{2,0},{3,1},{4,6},{5,7},{6,4},{7,5},{8,10},{9,11},{10,... | collective-permute-start | bytes 786440 | tf_op jit(solution)/shard_map/ppermute | solution.py:19
  5.2 17.7 %collective-permute-start.7 = (bf16[1,16,16,512]{3,2,1,0:T(8,128)(2,1)}, bf16[1,16,16,512]{3,2,1,0:T(8,128)(2,1)}, u32[]{:S(2)}, u32[]{:S(2)}) collective-permute-start(bf16[1,16,16,512]{3,2,1,0:T(8,128)(2,1)} %refs_0_.2), channel_id=1, source_target_pairs={{0,4},{4,0},{8,12},{12,8},{16,20},{20,16},{24,28},{28,24},{1,5},{5... | collective-permute-start | bytes 786440 | tf_op jit(solution)/shard_map/ppermute | solution.py:19
  6.7 26.9 %collective-permute-start.8 = (bf16[1,16,16,512]{3,2,1,0:T(8,128)(2,1)}, bf16[1,16,16,512]{3,2,1,0:T(8,128)(2,1)}, u32[]{:S(2)}, u32[]{:S(2)}) collective-permute-start(bf16[1,16,16,512]{3,2,1,0:T(8,128)(2,1)} %refs_0_.2), channel_id=1, source_target_pairs={{0,24},{4,28},{8,0},{12,4},{16,8},{20,12},{24,16},{28,20},{1,25},{... | collective-permute-start | bytes 786440 | tf_op jit(solution)/shard_map/ppermute | solution.py:19
  13.1 29.5 %copy-start.12 = (bf16[1,16,16,512]{3,2,1,0:T(8,128)(2,1)}, bf16[1,16,16,512]{3,2,1,0:T(8,128)(2,1)S(1)}, u32[]{:S(2)}) copy-start(bf16[1,16,16,512]{3,2,1,0:T(8,128)(2,1)S(1)} %collective-permute-done.1.refs_3_) | copy-start | bytes 786436
  13.1 17.1 %collective-permute-start.2 = (bf16[1,16,16,512]{3,2,1,0:T(8,128)(2,1)}, bf16[1,16,16,512]{3,2,1,0:T(8,128)(2,1)}, u32[]{:S(2)}, u32[]{:S(2)}) collective-permute-start(bf16[1,16,16,512]{3,2,1,0:T(8,128)(2,1)} %refs_0_.2), channel_id=1, source_target_pairs={{0,16},{4,20},{8,24},{12,28},{16,0},{20,4},{24,8},{28,12},{1,17},{... | collective-permute-start | bytes 786440 | tf_op jit(solution)/shard_map/ppermute | solution.py:19
  21.4 4.8 %copy-start.11 = (bf16[1,16,16,512]{3,2,1,0:T(8,128)(2,1)}, bf16[1,16,16,512]{3,2,1,0:T(8,128)(2,1)S(1)}, u32[]{:S(2)}) copy-start(bf16[1,16,16,512]{3,2,1,0:T(8,128)(2,1)S(1)} %collective-permute-done.refs_2_.refs_1_) | copy-start | bytes 786436
  21.4 10.7 %collective-permute-start.3 = (bf16[1,16,16,512]{3,2,1,0:T(8,128)(2,1)S(1)}, bf16[1,16,16,512]{3,2,1,0:T(8,128)(2,1)}, u32[]{:S(2)}, u32[]{:S(2)}) collective-permute-start(bf16[1,16,16,512]{3,2,1,0:T(8,128)(2,1)S(1)} %collective-permute-done.1.refs_3_), channel_id=1, source_target_pairs={{0,2},{1,3},{2,0},{3,1},{4,6},{5,7},{6,4},{7,5},{8,10},{9,11},{10,... | collective-permute-start | bytes 786440 | tf_op jit(solution)/shard_map/ppermute | solution.py:19
  26.1 20.9 %collective-permute-start.21 = (f32[2,128,512]{2,1,0:T(8,128)S(1)}, f32[2,128,512]{2,1,0:T(8,128)S(1)}, u32[]{:S(2)}, u32[]{:S(2)}) collective-permute-start(f32[2,128,512]{2,1,0:T(8,128)S(1)} %dynamic-slice_bitcast_fusion), channel_id=1, source_target_pairs={{0,1},{1,0},{2,3},{3,2},{4,5},{5,4},{6,7},{7,6},{8,9},{9,8},{10,11... | collective-permute-start | bytes 1572872 | tf_op jit(solution)/shard_map/ppermute | solution.py:19
  26.2 17.2 %all-to-all-start = ((bf16[8,64,256]{2,1,0:T(8,128)(2,1)}), bf16[8,64,256]{2,1,0:T(8,128)(2,1)S(1)}, u32[]{:S(2)}, u32[]{:S(2)}) async-start(bf16[8,64,256]{2,1,0:T(8,128)(2,1)} %bitcast.2), calls=%async_computation | async-start | bytes 524288 | tf_op jit(solution)/shard_map/all_to_all | solution.py:446
  29.6 9.5 %collective-permute-start.9 = (bf16[1,16,16,512]{3,2,1,0:T(8,128)(2,1)}, bf16[1,16,16,512]{3,2,1,0:T(8,128)(2,1)}, u32[]{:S(2)}, u32[]{:S(2)}) collective-permute-start(bf16[1,16,16,512]{3,2,1,0:T(8,128)(2,1)} %collective-permute-done.7.refs_1_), channel_id=1, source_target_pairs={{0,2},{1,3},{2,0},{3,1},{4,6},{5,7},{6,4},{7,5},{8,10},{9,11},{10,... | collective-permute-start | bytes 786440 | tf_op jit(solution)/shard_map/ppermute | solution.py:19
  30.2 11.1 %collective-permute-start.10 = (bf16[1,16,16,512]{3,2,1,0:T(8,128)(2,1)S(1)}, bf16[1,16,16,512]{3,2,1,0:T(8,128)(2,1)}, u32[]{:S(2)}, u32[]{:S(2)}) collective-permute-start(bf16[1,16,16,512]{3,2,1,0:T(8,128)(2,1)S(1)} %collective-permute-done.1.refs_3_), channel_id=1, source_target_pairs={{0,4},{4,0},{8,12},{12,8},{16,20},{20,16},{24,28},{28,24},{1,5},{5... | collective-permute-start | bytes 786440 | tf_op jit(solution)/shard_map/ppermute | solution.py:19
  32.1 10.6 %collective-permute-start.18 = (bf16[1,576,128]{2,1,0:T(8,128)(2,1)S(1)}, bf16[1,576,128]{2,1,0:T(8,128)(2,1)S(1)}, u32[]{:S(2)}, u32[]{:S(2)}) collective-permute-start(bf16[1,576,128]{2,1,0:T(8,128)(2,1)S(1)} %dynamic-slice_bitcast_fusion.2), channel_id=1, source_target_pairs={{0,8},{4,12},{8,0},{12,4},{16,24},{20,28},{24,16},{28,20},{1,9},{5... | collective-permute-start | bytes 442376 | tf_op jit(solution)/shard_map/ppermute | solution.py:19
  33.6 11.0 %collective-permute-start.4 = (bf16[1,16,16,512]{3,2,1,0:T(8,128)(2,1)}, bf16[1,16,16,512]{3,2,1,0:T(8,128)(2,1)}, u32[]{:S(2)}, u32[]{:S(2)}) collective-permute-start(bf16[1,16,16,512]{3,2,1,0:T(8,128)(2,1)} %collective-permute-done.2.refs_8_), channel_id=1, source_target_pairs={{0,2},{1,3},{2,0},{3,1},{4,6},{5,7},{6,4},{7,5},{8,10},{9,11},{10,... | collective-permute-start | bytes 786440 | tf_op jit(solution)/shard_map/ppermute | solution.py:19
  39.1 9.6 %collective-permute-start.11 = (bf16[1,16,16,512]{3,2,1,0:T(8,128)(2,1)}, bf16[1,16,16,512]{3,2,1,0:T(8,128)(2,1)}, u32[]{:S(2)}, u32[]{:S(2)}) collective-permute-start(bf16[1,16,16,512]{3,2,1,0:T(8,128)(2,1)} %collective-permute-done.8.refs_4_), channel_id=1, source_target_pairs={{0,4},{4,0},{8,12},{12,8},{16,20},{20,16},{24,28},{28,24},{1,5},{5... | collective-permute-start | bytes 786440 | tf_op jit(solution)/shard_map/ppermute | solution.py:19
  41.3 12.5 %collective-permute-start.12 = (bf16[1,16,16,512]{3,2,1,0:T(8,128)(2,1)}, bf16[1,16,16,512]{3,2,1,0:T(8,128)(2,1)}, u32[]{:S(2)}, u32[]{:S(2)}) collective-permute-start(bf16[1,16,16,512]{3,2,1,0:T(8,128)(2,1)} %collective-permute-done.8.refs_4_), channel_id=1, source_target_pairs={{0,2},{1,3},{2,0},{3,1},{4,6},{5,7},{6,4},{7,5},{8,10},{9,11},{10,... | collective-permute-start | bytes 786440 | tf_op jit(solution)/shard_map/ppermute | solution.py:19
  42.7 9.9 %collective-permute-start.13 = (bf16[1,16,16,512]{3,2,1,0:T(8,128)(2,1)}, bf16[1,16,16,512]{3,2,1,0:T(8,128)(2,1)}, u32[]{:S(2)}, u32[]{:S(2)}) collective-permute-start(bf16[1,16,16,512]{3,2,1,0:T(8,128)(2,1)} %collective-permute-done.2.refs_8_), channel_id=1, source_target_pairs={{0,4},{4,0},{8,12},{12,8},{16,20},{20,16},{24,28},{28,24},{1,5},{5... | collective-permute-start | bytes 786440 | tf_op jit(solution)/shard_map/ppermute | solution.py:19
  43.4 27.3 %copy-start.8 = (bf16[8,64,256]{2,1,0:T(8,128)(2,1)}, bf16[8,64,256]{2,1,0:T(8,128)(2,1)S(1)}, u32[]{:S(2)}) copy-start(bf16[8,64,256]{2,1,0:T(8,128)(2,1)S(1)} %all-to-all-done.refs_16_) | copy-start | bytes 786436
  44.6 15.6 %collective-permute-start.19 = (bf16[2,576,128]{2,1,0:T(8,128)(2,1)S(1)}, bf16[2,576,128]{2,1,0:T(8,128)(2,1)}, u32[]{:S(2)}, u32[]{:S(2)}) collective-permute-start(bf16[2,576,128]{2,1,0:T(8,128)(2,1)S(1)} %pad_maximum_fusion.1), channel_id=1, source_target_pairs={{0,16},{4,20},{8,24},{12,28},{16,0},{20,4},{24,8},{28,12},{1,17},{... | collective-permute-start | bytes 884744 | tf_op jit(solution)/shard_map/ppermute | solution.py:19
  47.0 9.5 %collective-permute-start.15 = (bf16[8,64,256]{2,1,0:T(8,128)(2,1)S(1)}, bf16[8,64,256]{2,1,0:T(8,128)(2,1)}, u32[]{:S(2)}, u32[]{:S(2)}) collective-permute-start(bf16[8,64,256]{2,1,0:T(8,128)(2,1)S(1)} %all-to-all-done.refs_16_), channel_id=1, source_target_pairs={{0,2},{1,3},{2,0},{3,1},{4,6},{5,7},{6,4},{7,5},{8,10},{9,11},{10,... | collective-permute-start | bytes 786440 | tf_op jit(solution)/shard_map/ppermute | solution.py:19
  48.7 13.1 %collective-permute-start.22 = (f32[128,512]{1,0:T(8,128)S(1)}, f32[128,512]{1,0:T(8,128)S(1)}, u32[]{:S(2)}, u32[]{:S(2)}) collective-permute-start(f32[128,512]{1,0:T(8,128)S(1)} %dynamic-slice_bitcast_fusion.1), channel_id=1, source_target_pairs={{0,2},{1,3},{2,0},{3,1},{4,6},{5,7},{6,4},{7,5},{8,10},{9,11},{10,... | collective-permute-start | bytes 786440 | tf_op jit(solution)/shard_map/ppermute | solution.py:19
  52.6 18.1 %collective-permute-start.14 = (bf16[1,16,16,512]{3,2,1,0:T(8,128)(2,1)}, bf16[1,16,16,512]{3,2,1,0:T(8,128)(2,1)S(1)}, u32[]{:S(2)}, u32[]{:S(2)}) collective-permute-start(bf16[1,16,16,512]{3,2,1,0:T(8,128)(2,1)} %collective-permute-done.3.refs_7_), channel_id=1, source_target_pairs={{0,4},{4,0},{8,12},{12,8},{16,20},{20,16},{24,28},{28,24},{1,5},{5... | collective-permute-start | bytes 786440 | tf_op jit(solution)/shard_map/ppermute | solution.py:19
  53.8 39.5 %collective-permute-start.5 = (bf16[1,16,16,512]{3,2,1,0:T(8,128)(2,1)}, bf16[1,16,16,512]{3,2,1,0:T(8,128)(2,1)S(1)}, u32[]{:S(2)}, u32[]{:S(2)}) collective-permute-start(bf16[1,16,16,512]{3,2,1,0:T(8,128)(2,1)} %refs_0_.2), channel_id=1, source_target_pairs={{0,1},{1,0},{2,3},{3,2},{4,5},{5,4},{6,7},{7,6},{8,9},{9,8},{10,11... | collective-permute-start | bytes 786440 | tf_op jit(solution)/shard_map/ppermute | solution.py:19
  56.5 8.5 %collective-permute-start.17 = (bf16[1,16,16,512]{3,2,1,0:T(8,128)(2,1)}, bf16[1,16,16,512]{3,2,1,0:T(8,128)(2,1)S(1)}, u32[]{:S(2)}, u32[]{:S(2)}) collective-permute-start(bf16[1,16,16,512]{3,2,1,0:T(8,128)(2,1)} %collective-permute-done.4.refs_12_), channel_id=1, source_target_pairs={{0,4},{4,0},{8,12},{12,8},{16,20},{20,16},{24,28},{28,24},{1,5},{5... | collective-permute-start | bytes 786440 | tf_op jit(solution)/shard_map/ppermute | solution.py:19
  60.3 7.7 %collective-permute-start.16 = (bf16[1,16,16,512]{3,2,1,0:T(8,128)(2,1)}, bf16[1,16,16,512]{3,2,1,0:T(8,128)(2,1)S(1)}, u32[]{:S(2)}, u32[]{:S(2)}) collective-permute-start(bf16[1,16,16,512]{3,2,1,0:T(8,128)(2,1)} %collective-permute-done.11.refs_9_), channel_id=1, source_target_pairs={{0,2},{1,3},{2,0},{3,1},{4,6},{5,7},{6,4},{7,5},{8,10},{9,11},{10,... | collective-permute-start | bytes 786440 | tf_op jit(solution)/shard_map/ppermute | solution.py:19
  61.8 31.5 %copy-start.7 = (bf16[4,576,128]{2,1,0:T(8,128)(2,1)}, bf16[4,576,128]{2,1,0:T(8,128)(2,1)S(1)}, u32[]{:S(2)}) copy-start(bf16[4,576,128]{2,1,0:T(8,128)(2,1)S(1)} %pad_maximum_fusion.refs_4_) | copy-start | bytes 1769476
  61.8 31.5 %collective-permute-start.6 = (bf16[1,16,16,512]{3,2,1,0:T(8,128)(2,1)}, bf16[1,16,16,512]{3,2,1,0:T(8,128)(2,1)S(1)}, u32[]{:S(2)}, u32[]{:S(2)}) collective-permute-start(bf16[1,16,16,512]{3,2,1,0:T(8,128)(2,1)} %copy-done.11), channel_id=1, source_target_pairs={{0,1},{1,0},{2,3},{3,2},{4,5},{5,4},{6,7},{7,6},{8,9},{9,8},{10,11... | collective-permute-start | bytes 786440 | tf_op jit(solution)/shard_map/ppermute | solution.py:19
  65.0 5.7 %copy-start.16 = (bf16[1,16,16,512]{3,2,1,0:T(8,128)(2,1)}, bf16[1,16,16,512]{3,2,1,0:T(8,128)(2,1)S(1)}, u32[]{:S(2)}) copy-start(bf16[1,16,16,512]{3,2,1,0:T(8,128)(2,1)S(1)} %collective-permute-done.17.refs_15_) | copy-start | bytes 786436
  67.9 2.7 %copy-start.17 = (bf16[1,16,16,512]{3,2,1,0:T(8,128)(2,1)}, bf16[1,16,16,512]{3,2,1,0:T(8,128)(2,1)S(1)}, u32[]{:S(2)}) copy-start(bf16[1,16,16,512]{3,2,1,0:T(8,128)(2,1)S(1)} %collective-permute-done.16.refs_14_) | copy-start | bytes 786436
  67.9 25.4 %collective-permute-start.20 = (bf16[4,576,128]{2,1,0:T(8,128)(2,1)S(1)}, bf16[4,576,128]{2,1,0:T(8,128)(2,1)S(1)}, u32[]{:S(2)}, u32[]{:S(2)}) collective-permute-start(bf16[4,576,128]{2,1,0:T(8,128)(2,1)S(1)} %pad_maximum_fusion.refs_4_), channel_id=1, source_target_pairs={{0,4},{4,0},{8,12},{12,8},{16,20},{20,16},{24,28},{28,24},{1,5},{5... | collective-permute-start | bytes 1769480 | tf_op jit(solution)/shard_map/ppermute | solution.py:19
  69.0 24.3 %collective-permute-start.23 = (f32[128,512]{1,0:T(8,128)S(1)}, f32[128,512]{1,0:T(8,128)S(1)}, u32[]{:S(2)}, u32[]{:S(2)}) collective-permute-start(f32[128,512]{1,0:T(8,128)S(1)} %bitcast_add_fusion.2), channel_id=1, source_target_pairs={{0,16},{4,20},{8,24},{12,28},{16,0},{20,4},{24,8},{28,12},{1,17},{... | collective-permute-start | bytes 786440 | tf_op jit(solution)/shard_map/ppermute | solution.py:19
  70.7 0.7 copy-start.15
  93.3 9.3 %copy-start.13 = (bf16[1,16,16,512]{3,2,1,0:T(8,128)(2,1)}, bf16[1,16,16,512]{3,2,1,0:T(8,128)(2,1)S(1)}, u32[]{:S(2)}) copy-start(bf16[1,16,16,512]{3,2,1,0:T(8,128)(2,1)S(1)} %collective-permute-done.5.refs_2_) | copy-start | bytes 786436
  93.3 9.4 %copy-start.14 = (bf16[1,16,16,512]{3,2,1,0:T(8,128)(2,1)}, bf16[1,16,16,512]{3,2,1,0:T(8,128)(2,1)S(1)}, u32[]{:S(2)}) copy-start(bf16[1,16,16,512]{3,2,1,0:T(8,128)(2,1)S(1)} %collective-permute-done.6.refs_3_) | copy-start | bytes 786436
  93.4 1.9 %copy-start.10 = (bf16[4,576,128]{2,1,0:T(8,128)(2,1)}, bf16[4,576,128]{2,1,0:T(8,128)(2,1)S(1)}, u32[]{:S(2)}) copy-start(bf16[4,576,128]{2,1,0:T(8,128)(2,1)S(1)} %collective-permute-done.20.refs_5_) | copy-start | bytes 1769476
  93.4 1.9 %collective-permute-start.24 = (f32[64,1280]{1,0:T(8,128)}, f32[64,1280]{1,0:T(8,128)S(1)}, u32[]{:S(2)}, u32[]{:S(2)}) collective-permute-start(f32[64,1280]{1,0:T(8,128)} %get-tuple-element.73), channel_id=1, source_target_pairs={{0,1},{1,0},{2,3},{3,2},{4,5},{5,4},{6,7},{7,6},{8,9},{9,8},{10,11... | collective-permute-start | bytes 983048 | tf_op jit(solution)/shard_map/ppermute | solution.py:19
  95.3 1.0 copy-start.1
  96.3 18.1 %collective-permute-start.25 = (f16[64,1280]{1,0:T(8,128)(2,1)S(1)}, f16[64,1280]{1,0:T(8,128)(2,1)S(1)}, u32[]{:S(2)}, u32[]{:S(2)}) collective-permute-start(f16[64,1280]{1,0:T(8,128)(2,1)S(1)} %convert_element_type.54), channel_id=1, source_target_pairs={{0,4},{4,0},{8,12},{12,8},{16,20},{20,16},{24,28},{28,24},{1,5},{5... | collective-permute-start | bytes 491528 | tf_op jit(solution)/shard_map/ppermute | solution.py:19
  97.0 10.9 %collective-permute-start.26 = (f16[64,1280]{1,0:T(8,128)(2,1)S(1)}, f16[64,1280]{1,0:T(8,128)(2,1)S(1)}, u32[]{:S(2)}, u32[]{:S(2)}) collective-permute-start(f16[64,1280]{1,0:T(8,128)(2,1)S(1)} %convert_element_type.54), channel_id=1, source_target_pairs={{0,8},{4,12},{8,16},{12,20},{16,24},{20,28},{24,0},{28,4},{1,9},{5... | collective-permute-start | bytes 491528 | tf_op jit(solution)/shard_map/ppermute | solution.py:19
  100.1 11.7 %collective-permute-start.28 = (f16[64,1280]{1,0:T(8,128)(2,1)S(1)}, f16[64,1280]{1,0:T(8,128)(2,1)S(1)}, u32[]{:S(2)}, u32[]{:S(2)}) collective-permute-start(f16[64,1280]{1,0:T(8,128)(2,1)S(1)} %convert_element_type.54), channel_id=1, source_target_pairs={{0,16},{4,20},{8,24},{12,28},{16,0},{20,4},{24,8},{28,12},{1,17},{... | collective-permute-start | bytes 491528 | tf_op jit(solution)/shard_map/ppermute | solution.py:19
  100.2 11.6 %collective-permute-start.29 = (f16[64,1280]{1,0:T(8,128)(2,1)S(1)}, f16[64,1280]{1,0:T(8,128)(2,1)S(1)}, u32[]{:S(2)}, u32[]{:S(2)}) collective-permute-start(f16[64,1280]{1,0:T(8,128)(2,1)S(1)} %convert_element_type.54), channel_id=1, source_target_pairs={{0,24},{4,28},{8,0},{12,4},{16,8},{20,12},{24,16},{28,20},{1,25},{... | collective-permute-start | bytes 491528 | tf_op jit(solution)/shard_map/ppermute | solution.py:19
  102.6 19.4 %collective-permute-start.35 = (f32[576,1152]{1,0:T(8,128)}, f32[576,1152]{1,0:T(8,128)S(1)}, u32[]{:S(2)}, u32[]{:S(2)}) collective-permute-start(f32[576,1152]{1,0:T(8,128)} %get-tuple-element.90), channel_id=1, source_target_pairs={{0,1},{1,0},{2,3},{3,2},{4,5},{5,4},{6,7},{7,6},{8,9},{9,8},{10,11... | collective-permute-start | bytes 7962632 | tf_op jit(solution)/shard_map/ppermute | solution.py:19
  102.8 19.3 %copy-start.4 = (f32[512,512]{1,0:T(8,128)S(1)}, f32[512,512]{1,0:T(8,128)}, u32[]{:S(2)}) copy-start(f32[512,512]{1,0:T(8,128)} %refs_1_.1) | copy-start | bytes 3145732
  107.9 14.2 %copy-start.3 = (f32[576,1152]{1,0:T(8,128)S(1)}, f32[576,1152]{1,0:T(8,128)}, u32[]{:S(2)}) copy-start(f32[576,1152]{1,0:T(8,128)} %refs_0_.3) | copy-start | bytes 7962628
  107.9 6.8 %collective-permute-start.27 = (f16[64,1280]{1,0:T(8,128)(2,1)S(1)}, f16[64,1280]{1,0:T(8,128)(2,1)S(1)}, u32[]{:S(2)}, u32[]{:S(2)}) collective-permute-start(f16[64,1280]{1,0:T(8,128)(2,1)S(1)} %collective-permute-done.26), channel_id=1, source_target_pairs={{0,4},{4,0},{8,12},{12,8},{16,20},{20,16},{24,28},{28,24},{1,5},{5... | collective-permute-start | bytes 491528 | tf_op jit(solution)/shard_map/ppermute | solution.py:19
  111.8 7.1 %collective-permute-start.30 = (f16[64,1280]{1,0:T(8,128)(2,1)S(1)}, f16[64,1280]{1,0:T(8,128)(2,1)S(1)}, u32[]{:S(2)}, u32[]{:S(2)}) collective-permute-start(f16[64,1280]{1,0:T(8,128)(2,1)S(1)} %collective-permute-done.28), channel_id=1, source_target_pairs={{0,4},{4,0},{8,12},{12,8},{16,20},{20,16},{24,28},{28,24},{1,5},{5... | collective-permute-start | bytes 491528 | tf_op jit(solution)/shard_map/ppermute | solution.py:19
  113.3 8.3 %collective-permute-start.31 = (f16[64,1280]{1,0:T(8,128)(2,1)S(1)}, f16[64,1280]{1,0:T(8,128)(2,1)S(1)}, u32[]{:S(2)}, u32[]{:S(2)}) collective-permute-start(f16[64,1280]{1,0:T(8,128)(2,1)S(1)} %collective-permute-done.29), channel_id=1, source_target_pairs={{0,4},{4,0},{8,12},{12,8},{16,20},{20,16},{24,28},{28,24},{1,5},{5... | collective-permute-start | bytes 491528 | tf_op jit(solution)/shard_map/ppermute | solution.py:19
  122.0 9.8 %copy-start.20 = (bf16[1,16,16,128]{3,2,1,0:T(8,128)(2,1)S(1)}, bf16[1,16,16,128]{3,2,1,0:T(8,128)(2,1)}, u32[]{:S(2)}) copy-start(bf16[1,16,16,128]{3,2,1,0:T(8,128)(2,1)} %get-tuple-element.86) | copy-start | bytes 196612
  122.0 10.3 %copy-start.19 = (bf16[1,16,16,128]{3,2,1,0:T(8,128)(2,1)S(1)}, bf16[1,16,16,128]{3,2,1,0:T(8,128)(2,1)}, u32[]{:S(2)}) copy-start(bf16[1,16,16,128]{3,2,1,0:T(8,128)(2,1)} %get-tuple-element.87) | copy-start | bytes 196612
  122.0 10.3 %copy-start.18 = (bf16[1,16,16,128]{3,2,1,0:T(8,128)(2,1)S(1)}, bf16[1,16,16,128]{3,2,1,0:T(8,128)(2,1)}, u32[]{:S(2)}) copy-start(bf16[1,16,16,128]{3,2,1,0:T(8,128)(2,1)} %get-tuple-element.88) | copy-start | bytes 196612
  122.1 18.9 %copy-start.6 = (f32[576,1152]{1,0:T(8,128)S(1)}, f32[576,1152]{1,0:T(8,128)}, u32[]{:S(2)}) copy-start(f32[576,1152]{1,0:T(8,128)} %get-tuple-element.98) | copy-start | bytes 7962628
  127.8 13.2 %copy-start.5 = (f32[1152,576]{0,1:T(8,128)S(1)}, f32[1152,576]{0,1:T(8,128)}, u32[]{:S(2)}) copy-start(f32[1152,576]{0,1:T(8,128)} %param.10) | copy-start | bytes 7962628
  127.8 12.5 %collective-permute-start.36 = (f32[576,256]{1,0:T(8,128)S(1)}, f32[576,256]{1,0:T(8,128)S(1)}, u32[]{:S(2)}, u32[]{:S(2)}) collective-permute-start(f32[576,256]{1,0:T(8,128)S(1)} %get-tuple-element.93), channel_id=1, source_target_pairs={{0,1},{1,0},{2,3},{3,2},{4,5},{5,4},{6,7},{7,6},{8,9},{9,8},{10,11... | collective-permute-start | bytes 1769480 | tf_op jit(solution)/shard_map/ppermute | solution.py:19
  127.9 10.8 %collective-permute-start.37 = (f32[128,512]{1,0:T(8,128)S(1)}, f32[128,512]{1,0:T(8,128)S(1)}, u32[]{:S(2)}, u32[]{:S(2)}) collective-permute-start(f32[128,512]{1,0:T(8,128)S(1)} %add.70), channel_id=1, source_target_pairs={{0,8},{4,12},{8,0},{12,4},{16,24},{20,28},{24,16},{28,20},{1,9},{5... | collective-permute-start | bytes 786440 | tf_op jit(solution)/shard_map/ppermute | solution.py:19
  131.8 11.2 %collective-permute-start.32 = (bf16[1,16,16,128]{3,2,1,0:T(8,128)(2,1)S(1)}, bf16[1,16,16,128]{3,2,1,0:T(8,128)(2,1)S(1)}, u32[]{:S(2)}, u32[]{:S(2)}) collective-permute-start(bf16[1,16,16,128]{3,2,1,0:T(8,128)(2,1)S(1)} %copy-done.20), channel_id=1, source_target_pairs={{0,2},{1,3},{2,0},{3,1},{4,6},{5,7},{6,4},{7,5},{8,10},{9,11},{10,... | collective-permute-start | bytes 196616 | tf_op jit(solution)/shard_map/ppermute | solution.py:19
  132.4 10.7 %collective-permute-start.33 = (bf16[1,16,16,128]{3,2,1,0:T(8,128)(2,1)S(1)}, bf16[1,16,16,128]{3,2,1,0:T(8,128)(2,1)S(1)}, u32[]{:S(2)}, u32[]{:S(2)}) collective-permute-start(bf16[1,16,16,128]{3,2,1,0:T(8,128)(2,1)S(1)} %copy-done.19), channel_id=1, source_target_pairs={{0,1},{1,0},{2,3},{3,2},{4,5},{5,4},{6,7},{7,6},{8,9},{9,8},{10,11... | collective-permute-start | bytes 196616 | tf_op jit(solution)/shard_map/ppermute | solution.py:19
  132.4 10.7 %collective-permute-start.34 = (bf16[1,16,16,128]{3,2,1,0:T(8,128)(2,1)S(1)}, bf16[1,16,16,128]{3,2,1,0:T(8,128)(2,1)S(1)}, u32[]{:S(2)}, u32[]{:S(2)}) collective-permute-start(bf16[1,16,16,128]{3,2,1,0:T(8,128)(2,1)S(1)} %copy-done.18), channel_id=1, source_target_pairs={{0,3},{1,2},{2,1},{3,0},{4,7},{5,6},{6,5},{7,4},{8,11},{9,10},{10,... | collective-permute-start | bytes 196616 | tf_op jit(solution)/shard_map/ppermute | solution.py:19
  138.8 8.1 %collective-permute-start.38 = (f32[128,512]{1,0:T(8,128)S(1)}, f32[128,512]{1,0:T(8,128)S(1)}, u32[]{:S(2)}, u32[]{:S(2)}) collective-permute-start(f32[128,512]{1,0:T(8,128)S(1)} %add.74), channel_id=1, source_target_pairs={{0,4},{4,0},{8,12},{12,8},{16,20},{20,16},{24,28},{28,24},{1,5},{5... | collective-permute-start | bytes 786440 | tf_op jit(solution)/shard_map/ppermute | solution.py:19
  140.4 8.6 %collective-permute-start.39 = (f32[576,128]{1,0:T(8,128)S(1)}, f32[576,128]{1,0:T(8,128)S(1)}, u32[]{:S(2)}, u32[]{:S(2)}) collective-permute-start(f32[576,128]{1,0:T(8,128)S(1)} %slice.91), channel_id=1, source_target_pairs={{0,2},{1,3},{2,0},{3,1},{4,6},{5,7},{6,4},{7,5},{8,10},{9,11},{10,... | collective-permute-start | bytes 884744 | tf_op jit(solution)/shard_map/ppermute | solution.py:19
  141.0 2.1 %copy-start.2 = (bf16[1,16,16,128]{3,2,1,0:T(8,128)(2,1)S(1)}, bf16[1,16,16,128]{3,2,1,0:T(8,128)(2,1)}, u32[]{:S(2)}) copy-start(bf16[1,16,16,128]{3,2,1,0:T(8,128)(2,1)} %get-tuple-element.94.refs_0_) | copy-start | bytes 196612
  141.0 8.7 %copy-start.9 = (f32[128,512]{1,0:T(8,128)S(1)}, f32[128,512]{1,0:T(8,128)}, u32[]{:S(2)}) copy-start(f32[128,512]{1,0:T(8,128)} %param.11) | copy-start | bytes 786436
